TPU v7x, 32 devices: a whole 2x2x4 slice. The times are simulated.
32 devices in a mesh: grp: 2 (over y), adp: 4 (over z), tp: 4 (over x, core).
Axes of the slice: x: 2, y: 2, z: 4, core: 2. Of those that a mesh axis runs over, the one named last changes fastest.
Arguments:
- tokens: bfloat16 [6144, 8192], P(('grp', 'adp'), 'tp'), parts along dimension 0, may hold values from -6 to 6
- adapter_ids: int32 [6144, 1], P(('grp', 'adp')), parts along dimension 0, may hold values from 0 to 7; in each aligned block of 768 rows (0 to 767, 768 to 1535, ...) at most 192 rows name the same one
- base_weight: bfloat16 [8192, 1024], P('tp'), may hold values from -0.0625 to 0.0625
- channel_scale: float32 [1024], P('tp'), may hold values from 0.5 to 2
- adapter_down: bfloat16 [8, 8192, 64], P('adp', 'tp'), may hold values from -0.0625 to 0.0625
- adapter_up: bfloat16 [8, 64, 1024], P('adp', None, 'tp'), may hold values from -0.75 to 0.75
- sign_bits: int32 [128], replicated, may hold values from 0 to 1
Outputs:
- rotated_values: bfloat16 [6144, 1024], P(('grp', 'adp'), 'tp'), parts along dimension 0
There are 2 independent parts, one for each index of `grp`. A program takes and returns all parts, laid end to end along the dimension named above; an argument that names none is the same for every part. Nothing has to cross between parts.
Inputs may be any that keep to these rules, and one draw needn't show every extreme that they name: `adapter_ids`: within each aligned block of 768 rows no adapter is named by more than 192 rows, a bound that some block reaches.
All inputs are finite; a program needn't handle non-finite values.
Results may differ from a plain program's by a relative error of at most 0.013.
Values may be sent and summed in bfloat16 or wider, within the bound.
No kernel may reach another device: no remote copies, remote signals or barrier semaphores. Data moves between devices by JAX's collectives and lax.ppermute only.
A program may use at most 64 MiB of HBM per device.

v0:
```python
import jax
import jax.numpy as jnp
from jax import lax
from jax.sharding import PartitionSpec as P


def hadamard(size):
    first = jnp.arange(size, dtype=jnp.int32)[:, None]
    second = jnp.arange(size, dtype=jnp.int32)[None, :]
    shared = jnp.zeros((size, size), jnp.int32)
    for place in range(size.bit_length() - 1):
        shared = shared + jnp.bitwise_and(jnp.right_shift(first, place), 1) * jnp.bitwise_and(
            jnp.right_shift(second, place), 1
        )
    return (1 - 2 * (shared % 2)).astype(jnp.float32)


def local(tokens, adapter_ids, base_weight, channel_scale, adapter_down, adapter_up, sign_bits):
    owners = lax.axis_size("adp")
    row_count = tokens.shape[0]
    feature_share = tokens.shape[1]
    head_share = adapter_up.shape[2]
    local_adapters = adapter_down.shape[0]
    adapters_all = local_adapters * owners
    slots_each = 2 * row_count // adapters_all
    head_size = sign_bits.shape[0]
    base = (
        lax.psum_scatter(
            jnp.einsum("dk,rd->kr", base_weight, tokens, preferred_element_type=jnp.float32).astype(
                jnp.bfloat16
            ),
            "tp",
            scatter_dimension=0,
            tiled=True,
        )
        .astype(jnp.float32)
        .T
    )
    ids_flat = adapter_ids[:, 0]
    onehot = (ids_flat[:, None] == jnp.arange(adapters_all, dtype=jnp.int32)[None, :]).astype(
        jnp.int32
    )
    before = jnp.cumsum(onehot, axis=0, dtype=jnp.int32) - 1
    rank = jnp.sum(onehot * before, axis=1, dtype=jnp.int32)
    slot = ids_flat * slots_each + rank
    outgoing = (
        jnp.zeros((adapters_all * slots_each, feature_share), jnp.bfloat16).at[slot].set(tokens)
    )
    packed = outgoing.reshape(owners, local_adapters, slots_each, feature_share)
    partial_value = jnp.einsum(
        "sacd,adr->sacr",
        lax.all_to_all(packed, "adp", split_axis=0, concat_axis=0, tiled=True),
        adapter_down,
        preferred_element_type=jnp.float32,
    )
    total = lax.psum(partial_value.astype(jnp.bfloat16), "tp")
    delta = jnp.einsum(
        "sacr,are->sace", total, adapter_up, preferred_element_type=jnp.float32
    ).astype(jnp.bfloat16)
    answered = lax.all_to_all(delta, "adp", split_axis=0, concat_axis=0, tiled=True)
    delta_slots = answered.reshape(adapters_all * slots_each, head_share)
    delta_rows = delta_slots[slot]
    value = base * channel_scale[None, :] + delta_rows.astype(jnp.float32)
    signed = (
        value.reshape(row_count, head_share // head_size, head_size)
        * (1 - 2 * sign_bits).astype(jnp.float32)[None, None, :]
    )
    matrix = hadamard(head_size) / jnp.sqrt(jnp.float32(head_size))
    rotated = jnp.einsum("thd,de->the", signed, matrix, precision=lax.Precision.HIGHEST)
    return rotated.reshape(row_count, head_share).astype(jnp.bfloat16)


def solution(mesh):
    return jax.shard_map(
        local,
        mesh=mesh,
        in_specs=(
            P(("grp", "adp"), "tp"),
            P(("grp", "adp"), None),
            P("tp", None),
            P("tp"),
            P("adp", "tp", None),
            P("adp", None, "tp"),
            P(),
        ),
        out_specs=P(("grp", "adp"), "tp"),
        check_vma=False,
    )
```

profile of v0, /device:TPU:0, one launch (start us, length us, event | category | flops | bytes accessed | tf_op | source)
XLA Modules:
  0.0 241.8 jit_solution(14706064257839721371)
XLA Ops:
  6.5 0.0 copy-start
  6.5 0.0 all-reduce.2.cloned.1.call-start
  6.5 0.8 reduce
  7.3 1.7 reduce-window.6
  9.0 0.1 slice.10
  9.1 0.1 copy.32
  9.2 0.2 reduce-window.9
  9.4 0.1 copy.33
  9.5 0.1 fusion.43
  9.6 0.7 fusion.45
  10.3 11.6 %scatter_custom_fusion = bf16[1536,2048]{1,0:T(8,128)(2,1)} fusion(s32[768]{0:T(1024)S(1)} %fusion.45, bf16[768,2048]{1,0:T(8,128)(2,1)} %param.7, bf16[]{:T(256)} %constant.13.clone.1), kind=kCustom, calls=%fused_computation.4 | custom fusion | bytes 6291968 | tf_op jit(solution)/shard_map/scatter | solution.py:47
  21.9 144.4 %all_to_all.10 = bf16[4,2,192,2048]{3,2,1,0:T(8,128)(2,1)S(1)} all-to-all(bf16[4,2,192,2048]{3,2,1,0:T(8,128)(2,1)} %bitcast.35), channel_id=1, replica_groups=mesh['grp'=2,'adp'=4,'tp'=4] {'adp'}, dimensions={0} | all-to-all | bytes 12582912 | tf_op jit(solution)/shard_map/all_to_all | solution.py:52
  166.3 2.8 %fusion.8 = bf16[4,2,192,64]{2,3,0,1:T(8,128)(2,1)} fusion(bf16[4,2,192,2048]{3,2,1,0:T(8,128)(2,1)S(1)} %all_to_all.10, bf16[2,2048,64]{1,2,0:T(8,128)(2,1)S(1)} %copy-done), kind=kOutput, calls=%fused_computation.11 | convolution fusion | flops 402751488 | bytes 7012352 | tf_op jit(solution)/shard_map/sacd,adr->sacr/dot_general | solution.py:50
  169.1 0.0 all-reduce.2.cloned.1.call-update
  169.1 0.0 copy-start.1
  169.1 0.2 reduce-scatter.2.cloned.1.call-start
  169.4 7.8 %convolution_convert_fusion = bf16[1024,768]{1,0:T(8,128)(2,1)} fusion(bf16[2048,1024]{1,0:T(8,128)(2,1)} %param.9, bf16[768,2048]{1,0:T(8,128)(2,1)} %param.7), kind=kOutput, calls=%fused_computation.6 | convolution fusion | flops 3222011904 | bytes 8912896 | tf_op jit(solution)/shard_map/dk,rd->kr/dot_general | solution.py:29
  177.2 0.0 reduce-scatter.2.cloned.1.call-update
  177.2 0.0 copy-start.2
  177.2 23.5 %all-reduce.2.cloned.1.call-done = bf16[4,2,192,64]{2,3,0,1:T(8,128)(2,1)} async-done(((bf16[4,2,192,64]{2,3,0,1:T(8,128)(2,1)}), bf16[4,2,192,64]{2,3,0,1:T(8,128)(2,1)}) %all-reduce.2.cloned.1.call-update) | async-done | bytes 196624 | tf_op jit(solution)/shard_map/psum | solution.py:56
  200.7 1.4 fusion.4
  202.1 0.9 copy.35
  203.1 4.6 %all-to-all-start.1 = ((bf16[4,2,192,256]{3,2,1,0:T(8,128)(2,1)}), bf16[4,2,192,256]{3,2,1,0:T(8,128)(2,1)S(1)}, u32[]{:S(2)}, u32[]{:S(2)}) async-start(bf16[4,2,192,256]{3,2,1,0:T(8,128)(2,1)} %copy.35), calls=%async_computation.2 | async-start | bytes 1572864 | tf_op jit(solution)/shard_map/all_to_all | solution.py:60
  207.7 0.0 copy-done.3
  207.7 18.9 %all-to-all-done.1 = bf16[4,2,192,256]{3,2,1,0:T(8,128)(2,1)S(1)} async-done(((bf16[4,2,192,256]{3,2,1,0:T(8,128)(2,1)}), bf16[4,2,192,256]{3,2,1,0:T(8,128)(2,1)S(1)}, u32[]{:S(2)}, u32[]{:S(2)}) %all-to-all-start.1) | async-done | bytes 786464 | tf_op jit(solution)/shard_map/all_to_all | solution.py:60
  226.6 2.6 %gather_fusion = bf16[768,256]{1,0:T(8,128)(2,1)S(1)} fusion(bf16[1536,256]{1,0:T(8,128)(2,1)S(1)} %bitcast.36, s32[1024]{0:T(1024)S(1)} %pad_clamp_fusion), kind=kCustom, calls=%fused_computation | custom fusion | bytes 789504 | tf_op jit(solution)/shard_map/gather | solution.py:62
  229.3 0.2 copy.36
  229.5 2.2 reduce-scatter.2.cloned.1.call-done
  231.7 1.2 bitcast_add_fusion
  232.8 0.3 copy.37
  233.1 1.0 convolution_convert_fusion.2
  234.1 0.9 copy.38
  (10 shorter events, 0.0 us)
Async XLA Ops:
  6.5 159.7 %copy-start = (bf16[2,2048,64]{1,2,0:T(8,128)(2,1)S(1)}, bf16[2,2048,64]{1,2,0:T(8,128)(2,1)}, u32[]{:S(2)}) copy-start(bf16[2,2048,64]{1,2,0:T(8,128)(2,1)} %param.11) | copy-start | bytes 1572868
  6.5 194.2 %all-reduce.2.cloned.1.call-start = ((), (), s32[]{:S(2)}) async-start(), calls=%async_computation.4 | async-start | bytes 524288 | tf_op jit(solution)/shard_map/psum | solution.py:56
  169.1 31.6 %copy-start.1 = (bf16[2,64,256]{2,1,0:T(8,128)(2,1)S(1)}, bf16[2,64,256]{2,1,0:T(8,128)(2,1)}, u32[]{:S(2)}) copy-start(bf16[2,64,256]{2,1,0:T(8,128)(2,1)} %param.12) | copy-start | bytes 196612
  169.1 62.5 %reduce-scatter.2.cloned.1.call-start = ((), (), s32[]{:S(2)}) async-start(), calls=%async_computation.3 | async-start | bytes 1966080 | tf_op jit(solution)/shard_map/reduce_scatter | solution.py:28
  177.2 30.5 %copy-start.3 = (s32[128]{0:T(128)S(1)}, s32[128]{0:T(128)}, u32[]{:S(2)}) copy-start(s32[128]{0:T(128)} %param.13) | copy-start | bytes 1540
  177.2 54.5 %copy-start.2 = (f32[256]{0:T(256)S(1)}, f32[256]{0:T(256)}, u32[]{:S(2)}) copy-start(f32[256]{0:T(256)} %param.10) | copy-start | bytes 3076
  203.1 23.6 %all-to-all-start.1 = ((bf16[4,2,192,256]{3,2,1,0:T(8,128)(2,1)}), bf16[4,2,192,256]{3,2,1,0:T(8,128)(2,1)S(1)}, u32[]{:S(2)}, u32[]{:S(2)}) async-start(bf16[4,2,192,256]{3,2,1,0:T(8,128)(2,1)} %copy.35), calls=%async_computation.2 | async-start | bytes 1572864 | tf_op jit(solution)/shard_map/all_to_all | solution.py:60
Sparse Core Ops, SparseCore 0:
  169.2 31.4 all-reduce.1
  203.4 28.1 reduce-scatter.1
where the time goes:
time: 242 us
  blocking collectives  144 us (60%)
  waiting for transfers between devices  44.7 us (18%)
  local copies, waits for them, and re-layouts  16.9 us (7%)
  between operations  13.5 us (6%)
  matrix products  13 us (5%)
  starting transfers between devices  4.82 us (2%)
  other arithmetic  4.61 us (2%)
    all_to_all x1, blocking collectives, local(): lax.all_to_all(packed, 'adp', split_axis=0, concat_axis=0, tiled=True)  144 us
    psum x1, waiting for transfers between devices, local(): total = lax.psum(partial_value.astype(jnp.bfloat16), 'tp')  23.5 us
    all_to_all x1, waiting for transfers between devices, local(): lax.all_to_all(delta, 'adp', split_axis=0, concat_axis=0, tiled=True)  18.9 us
    scatter x1, local copies, waits for them, and re-layouts, local(): jnp.zeros((adapters_all * slots_each, feature_share), jnp.bfloat16).at[slot]  11.6 us
    dot_general x1, matrix products, local(): jnp.einsum('dk,rd->kr', base_weight, tokens, preferred_element_type=jnp.f...  7.82 us
  transfers between devices with their start and end apart: 3, of which 3 were waited for; matrix products, arithmetic and copies ran while one was open for 5% of the time, Pallas kernels for 0%

commit v1 on v0

v1 whole, which is shorter than its diff:
```python
import jax
import jax.numpy as jnp
from jax import lax
from jax.sharding import PartitionSpec as P


def hadamard(size):
    first = jnp.arange(size, dtype=jnp.int32)[:, None]
    second = jnp.arange(size, dtype=jnp.int32)[None, :]
    shared = jnp.zeros((size, size), jnp.int32)
    for place in range(size.bit_length() - 1):
        shared = shared + jnp.bitwise_and(jnp.right_shift(first, place), 1) * jnp.bitwise_and(
            jnp.right_shift(second, place), 1
        )
    return (1 - 2 * (shared % 2)).astype(jnp.float32)


def swap(x, axis, bit):
    return lax.ppermute(x, axis, [(i, i ^ bit) for i in range(lax.axis_size(axis))])


def gathered(own, groups, planes):
    held = {0: own}
    bit = planes // 2
    while bit:
        held.update({at | bit: swap(value, "adp", bit) for at, value in held.items()})
        bit //= 2
    every = []
    for at, value in held.items():
        if at:
            every.append((at, 0, value))
            every += [(at, off, swap(value, "grp", off)) for off in range(1, groups)]
    return every


def reduce_scatter(partial, width, parts):
    me = lax.axis_index("tp")
    rows = partial.shape[0]
    blocks = partial.reshape(rows, parts, width)
    bit = 1
    while bit < parts:
        mine = (me // bit) % 2
        pairs = blocks.reshape(rows, -1, 2, width)
        keep = lax.dynamic_index_in_dim(pairs, mine, 2, keepdims=False)
        give = lax.dynamic_index_in_dim(pairs, 1 - mine, 2, keepdims=False)
        blocks = keep + swap(give.astype(jnp.bfloat16), "tp", bit).astype(jnp.float32)
        bit *= 2
    return blocks.reshape(rows, width)


def local(tokens, adapter_ids, base_weight, channel_scale, adapter_down, adapter_up, sign_bits):
    planes, groups, parts = lax.axis_size("adp"), lax.axis_size("grp"), lax.axis_size("tp")
    z, g = lax.axis_index("adp"), lax.axis_index("grp")
    rows, features = tokens.shape
    here, _, rank = adapter_down.shape
    width = adapter_up.shape[2]
    head = sign_bits.shape[0]
    share = here // groups

    pieces = jnp.concatenate([jnp.swapaxes(adapter_down, 1, 2), adapter_up], axis=2)
    own = lax.dynamic_slice_in_dim(pieces, g * share, share, 0)
    every = [(0, off, lax.dynamic_slice_in_dim(pieces, (g ^ off) * share, share, 0)) for off in range(groups)]
    every += gathered(own, groups, planes)

    partial = jnp.dot(tokens, base_weight, preferred_element_type=jnp.float32)
    base = reduce_scatter(partial, width, parts)

    low = jnp.zeros((rank, rows), jnp.float32)
    masks = []
    for plane, off, piece in every:
        first = (z ^ plane) * here + (g ^ off) * share
        for k in range(share):
            mask = (adapter_ids == first + k).T
            product = lax.dot_general(
                piece[k, :, :features], tokens, (((1,), (1,)), ((), ())), preferred_element_type=jnp.float32
            )
            low = low + jnp.where(mask, product, 0.0)
            masks.append((mask, piece[k, :, features:]))
    bit = 1
    while bit < parts:
        sent = low.astype(jnp.bfloat16)
        low = sent.astype(jnp.float32) + swap(sent, "tp", bit).astype(jnp.float32)
        bit *= 2
    low = low.astype(jnp.bfloat16)

    spread = jnp.concatenate([jnp.where(mask, low, jnp.bfloat16(0)) for mask, _ in masks], axis=0)
    ups = jnp.concatenate([up for _, up in masks], axis=0)
    delta = lax.dot_general(spread, ups, (((0,), (0,)), ((), ())), preferred_element_type=jnp.float32)
    value = base * channel_scale[None, :] + delta
    signed = value.reshape(rows, width // head, head) * (1 - 2 * sign_bits).astype(jnp.float32)[None, None, :]
    matrix = hadamard(head) / jnp.sqrt(jnp.float32(head))
    rotated = jnp.einsum("thd,de->the", signed, matrix, precision=lax.Precision.HIGHEST)
    return rotated.reshape(rows, width).astype(jnp.bfloat16)


def solution(mesh):
    return jax.shard_map(
        local,
        mesh=mesh,
        in_specs=(
            P(("grp", "adp"), "tp"),
            P(("grp", "adp"), None),
            P("tp", None),
            P("tp"),
            P("adp", "tp", None),
            P("adp", None, "tp"),
            P(),
        ),
        out_specs=P(("grp", "adp"), "tp"),
        check_vma=False,
    )
```

time: 242 us -> 91.9 us (0.38)
  blocking collectives: 144 us -> 0 us
  waiting for transfers between devices: 44.7 us -> 19.9 us
  local copies, waits for them, and re-layouts: 16.9 us -> 30.8 us
  between operations: 13.5 us -> 0.15 us
  matrix products: 13 us -> 23.9 us
  starting transfers between devices: 4.82 us -> 11.5 us
    all_to_all x1 -> x0, blocking collectives: 144 us -> none  [local(): lax.all_to_all(packed, 'adp', split_axis=0, concat_axis=0, tiled=True)]
    psum x1 -> x0, waiting for transfers between devices: 23.5 us -> none  [local(): total = lax.psum(partial_value.astype(jnp.bfloat16), 'tp')]
    ppermute x0 -> x10, waiting for transfers between devices: none -> 19.9 us  [swap(): lax.ppermute(x, axis, [(i, i ^ bit) for i in range(lax.axis_size(axis))])]
    all_to_all x1 -> x0, waiting for transfers between devices: 18.9 us -> none  [local(): lax.all_to_all(delta, 'adp', split_axis=0, concat_axis=0, tiled=True)]
    dynamic_slice x0 -> x3, local copies, waits for them, and re-layouts: none -> 13.7 us  [the longest x2 9.26 us: reduce_scatter(): keep = lax.dynamic_index_in_dim(pairs, mine, 2, keepdims=False)]
    scatter x1 -> x0, local copies, waits for them, and re-layouts: 11.6 us -> none  [local(): jnp.zeros((adapters_all * slots_each, feature_share), jnp.bfloat16).at[slot]]
    ppermute x0 -> x10, starting transfers between devices: none -> 11.5 us  [swap(): lax.ppermute(x, axis, [(i, i ^ bit) for i in range(lax.axis_size(axis))])]
    dot_general x3 -> x10, matrix products: 12 us -> 21.8 us  [the longest x8 13.2 us: local(): lax.dot_general(piece[k, :, :features], tokens, (((1,), (1,)), ((), ())),...]
  transfers between devices with their start and end apart: 3 -> 10, of which waited for: 3 -> 4; matrix products, arithmetic and copies ran while one was open for 5% -> 55% of each run, Pallas kernels for 0% -> 0%
where the time goes in v1:
time: 91.9 us; the launch traced here: 91 us
  local copies, waits for them, and re-layouts  30.8 us (34%)
  matrix products  23.9 us (26%)
  waiting for transfers between devices  19.9 us (22%)
  starting transfers between devices  11.5 us (13%)
  other arithmetic  4.74 us (5%)
    ppermute x10, waiting for transfers between devices, swap(): lax.ppermute(x, axis, [(i, i ^ bit) for i in range(lax.axis_size(axis))])  19.9 us
    dot_general x8, matrix products, local(): lax.dot_general(piece[k, :, :features], tokens, (((1,), (1,)), ((), ())),...  13.2 us
    ppermute x10, starting transfers between devices, swap(): lax.ppermute(x, axis, [(i, i ^ bit) for i in range(lax.axis_size(axis))])  11.5 us
    dynamic_slice x2, local copies, waits for them, and re-layouts, reduce_scatter(): keep = lax.dynamic_index_in_dim(pairs, mine, 2, keepdims=False)  9.26 us
    unnamed x20, local copies, waits for them, and re-layouts  8.28 us
    dot_general x1, matrix products, local(): partial = jnp.dot(tokens, base_weight, preferred_element_type=jnp.float32)  7.3 us
    another operation x1, local copies, waits for them, and re-layouts, reduce_scatter(): pairs = blocks.reshape(rows, -1, 2, width)  5.59 us
    dynamic_slice x1, local copies, waits for them, and re-layouts, reduce_scatter(): give = lax.dynamic_index_in_dim(pairs, 1 - mine, 2, keepdims=False)  4.44 us
  transfers between devices with their start and end apart: 10, of which 4 were waited for; matrix products, arithmetic and copies ran while one was open for 55% of the time, Pallas kernels for 0%

profile of v1, /device:TPU:0, one launch (start us, length us, event | category | flops | bytes accessed | tf_op | source)
XLA Modules:
  0.0 91.0 jit_solution(13664182126602182696)
XLA Ops:
  0.0 1.9 %fusion.10 = (bf16[1,64,2304]{2,1,0:T(8,128)(2,1)S(1)}, bf16[1,64,2304]{2,1,0:T(8,128)(2,1)}) fusion(s32[]{:T(128)S(6)} %select_n.102, bf16[2,64,2048]{2,1,0:T(8,128)(2,1)} %bitcast.86, bf16[2,64,256]{2,1,0:T(8,128)(2,1)} %param.12, s32[]{:T(128)S(6)} %select_n.100), kind=kLoop, calls=%fused_computation.28 | loop fusion | flops 1179648 | bytes 1179656 | tf_op jit(solution)/shard_map/concatenate | solution.py:60
  1.9 4.0 %collective-permute-start.2 = (bf16[1,64,2304]{2,1,0:T(8,128)(2,1)}, bf16[1,64,2304]{2,1,0:T(8,128)(2,1)}, u32[]{:S(2)}, u32[]{:S(2)}) collective-permute-start(bf16[1,64,2304]{2,1,0:T(8,128)(2,1)} %get-tuple-element.16), channel_id=1, source_target_pairs={{0,8},{4,12},{8,0},{12,4},{1,9},{5,13},{9,1},{13,5},{2,10},{6,14},... | collective-permute-start | bytes 884744 | tf_op jit(solution)/shard_map/ppermute | solution.py:19
  6.0 1.6 %collective-permute-start.4 = (bf16[1,64,2304]{2,1,0:T(8,128)(2,1)}, bf16[1,64,2304]{2,1,0:T(8,128)(2,1)}, u32[]{:S(2)}, u32[]{:S(2)}) collective-permute-start(bf16[1,64,2304]{2,1,0:T(8,128)(2,1)} %get-tuple-element.16), channel_id=1, source_target_pairs={{0,4},{4,0},{8,12},{12,8},{1,5},{5,1},{9,13},{13,9},{2,6},{6,2},{1... | collective-permute-start | bytes 884744 | tf_op jit(solution)/shard_map/ppermute | solution.py:19
  7.6 7.3 %fusion.44 = f32[768,1024]{1,0:T(8,128)} fusion(bf16[768,2048]{1,0:T(8,128)(2,1)S(1)} %copy-done, bf16[2048,1024]{1,0:T(8,128)(2,1)} %param.9), kind=kOutput, calls=%fused_computation.116 | convolution fusion | flops 3221225472 | bytes 10485760 | tf_op jit(solution)/shard_map/dot_general | solution.py:65
  14.9 5.6 %reshape_reshape.3 = f32[768,2,2,256]{3,2,1,0:T(2,128)} reshape(f32[768,1024]{1,0:T(8,128)} %fusion.44) | data formatting | bytes 6291456 | tf_op jit(solution)/shard_map/reshape;reshape | solution.py:43
  20.4 4.4 %constant_dynamic-slice_fusion = bf16[768,2,1,256]{3,2,1,0:T(2,128)(2,1)} fusion(f32[768,2,2,256]{3,2,1,0:T(2,128)} %reshape_reshape.3, s32[]{:T(128)S(6)} %select_n.95), kind=kLoop, calls=%fused_computation.103 | loop fusion | bytes 1572868 | tf_op jit(solution)/shard_map/jit(dynamic_index_in_dim)/dynamic_slice | solution.py:45
  24.9 4.7 %copy.12 = bf16[768,2,1,256]{0,3,1,2:T(8,128)(2,1)} copy(bf16[768,2,1,256]{3,2,1,0:T(2,128)(2,1)} %constant_dynamic-slice_fusion) | data formatting | bytes 1572864
  29.6 1.4 %constant_dynamic-update-slice_fusion.7 = bf16[512,256]{1,0:T(8,128)(2,1)} fusion(bf16[1,64,2304]{2,1,0:T(8,128)(2,1)} %get-tuple-element.16), kind=kLoop, calls=%fused_computation.67 | loop fusion | bytes 65536
  31.6 4.4 %constant_dynamic-slice_fusion.1 = f32[768,2,1,256]{3,2,1,0:T(1,128)} fusion(f32[768,2,2,256]{3,2,1,0:T(2,128)} %reshape_reshape.3, s32[]{:T(128)S(6)} %select_n.94), kind=kLoop, calls=%fused_computation.104 | loop fusion | bytes 3145732 | tf_op jit(solution)/shard_map/jit(dynamic_index_in_dim)/dynamic_slice | solution.py:44
  36.0 4.9 %copy.8 = f32[768,2,1,256]{0,3,1,2:T(8,128)} copy(f32[768,2,1,256]{3,2,1,0:T(1,128)} %constant_dynamic-slice_fusion.1) | data formatting | bytes 3145728 | tf_op jit(solution)/shard_map/jit(dynamic_index_in_dim)/dynamic_slice | solution.py:44
  40.9 2.7 %convolution_select_fusion.7 = f32[64,768]{1,0:T(8,128)} fusion(bf16[768,2048]{1,0:T(8,128)(2,1)S(1)} %copy-done, bf16[1,64,2304]{2,1,0:T(8,128)(2,1)} %get-tuple-element.16, pred[768]{0:T(1024)(128)(4,1)S(1)} %get-tuple-element.11), kind=kOutput, calls=%fused_computation.17 | convolution fusion | flops 201375744 | bytes 3605248 | tf_op jit(solution)/shard_map/dot_general | solution.py:74
  44.8 2.0 %fusion.6 = f32[64,768]{1,0:T(8,128)S(1)} fusion(f32[64,768]{1,0:T(8,128)} %convolution_select_fusion.7, bf16[768,2048]{1,0:T(8,128)(2,1)S(1)} %copy-done, bf16[1,64,2304]{2,1,0:T(8,128)(2,1)S(1)} %get-tuple-element.15, pred[768]{0:T(1024)(128)(4,1)S(1)} %get-tuple-element.10), kind=kOutput, calls=%fused_computation.16 | convolution fusion | flops 201424896 | bytes 3802112 | tf_op jit(solution)/shard_map/dot_general | solution.py:74
  46.8 1.6 %collective-permute-start.3 = (bf16[1,64,2304]{2,1,0:T(8,128)(2,1)}, bf16[1,64,2304]{2,1,0:T(8,128)(2,1)S(1)}, u32[]{:S(2)}, u32[]{:S(2)}) collective-permute-start(bf16[1,64,2304]{2,1,0:T(8,128)(2,1)} %collective-permute-done.2), channel_id=1, source_target_pairs={{0,16},{16,0},{1,17},{17,1},{2,18},{18,2},{3,19},{19,3},{4,20},{20... | collective-permute-start | bytes 884744 | tf_op jit(solution)/shard_map/ppermute | solution.py:19
  49.4 0.8 constant_dynamic-update-slice_fusion.5
  50.2 2.0 %fusion.5 = f32[64,768]{1,0:T(8,128)S(1)} fusion(f32[64,768]{1,0:T(8,128)S(1)} %fusion.6, bf16[768,2048]{1,0:T(8,128)(2,1)S(1)} %copy-done, bf16[1,64,2304]{2,1,0:T(8,128)(2,1)} %collective-permute-done.2, pred[768]{0:T(1024)(128)(4,1)S(1)} %get-tuple-element.9), kind=kOutput, calls=%fused_computation.14 | convolution fusion | flops 201424896 | bytes 3801856 | tf_op jit(solution)/shard_map/dot_general | solution.py:74
  52.2 2.0 %convolution_select_fusion.3 = f32[64,768]{1,0:T(8,128)S(1)} fusion(bf16[768,2048]{1,0:T(8,128)(2,1)S(1)} %copy-done, bf16[1,64,2304]{2,1,0:T(8,128)(2,1)} %collective-permute-done.4, pred[768]{0:T(1024)(128)(4,1)S(1)} %get-tuple-element.7), kind=kOutput, calls=%fused_computation.9 | convolution fusion | flops 201375744 | bytes 3605248 | tf_op jit(solution)/shard_map/dot_general | solution.py:74
  54.2 3.6 %collective-permute-done.6 = bf16[1,64,2304]{2,1,0:T(8,128)(2,1)S(1)} collective-permute-done((bf16[1,64,2304]{2,1,0:T(8,128)(2,1)}, bf16[1,64,2304]{2,1,0:T(8,128)(2,1)S(1)}, u32[]{:S(2)}, u32[]{:S(2)}) %collective-permute-start.6) | collective-permute-done | bytes 294944 | tf_op jit(solution)/shard_map/ppermute | solution.py:19
  58.3 0.8 constant_dynamic-update-slice_fusion.3
  59.1 1.1 %convolution_select_fusion.1 = f32[64,768]{1,0:T(8,128)S(1)} fusion(bf16[768,2048]{1,0:T(8,128)(2,1)S(1)} %copy-done, bf16[1,64,2304]{2,1,0:T(8,128)(2,1)S(1)} %collective-permute-done.6, pred[768]{0:T(1024)(128)(4,1)S(1)} %get-tuple-element.12), kind=kOutput, calls=%fused_computation.5 | convolution fusion | flops 201375744 | bytes 3605504 | tf_op jit(solution)/shard_map/dot_general | solution.py:74
  60.2 3.1 %collective-permute-done.5 = bf16[1,64,2304]{2,1,0:T(8,128)(2,1)S(1)} collective-permute-done((bf16[1,64,2304]{2,1,0:T(8,128)(2,1)}, bf16[1,64,2304]{2,1,0:T(8,128)(2,1)S(1)}, u32[]{:S(2)}, u32[]{:S(2)}) %collective-permute-start.5) | collective-permute-done | bytes 294944 | tf_op jit(solution)/shard_map/ppermute | solution.py:19
  63.3 1.1 %fusion.4 = f32[64,768]{1,0:T(8,128)S(1)} fusion(f32[64,768]{1,0:T(8,128)S(1)} %convolution_select_fusion.3, f32[64,768]{1,0:T(8,128)S(1)} %fusion.5, bf16[768,2048]{1,0:T(8,128)(2,1)S(1)} %copy-done, bf16[1,64,2304]{2,1,0:T(8,128)(2,1)S(1)} %collective-permute-done.3, pred[768]{0:T(1024)(128)(4,1)S(1)} %get-tuple-element.8), kind=kOutput, calls=%fused_computation.12 | convolution fusion | flops 201474048 | bytes 3998720 | tf_op jit(solution)/shard_map/dot_general | solution.py:74
  64.3 1.1 %fusion.2 = f32[64,768]{1,0:T(8,128)S(1)} fusion(f32[64,768]{1,0:T(8,128)S(1)} %convolution_select_fusion.1, f32[64,768]{1,0:T(8,128)S(1)} %fusion.4, bf16[768,2048]{1,0:T(8,128)(2,1)S(1)} %copy-done, bf16[1,64,2304]{2,1,0:T(8,128)(2,1)S(1)} %collective-permute-done.5, pred[768]{0:T(1024)(128)(4,1)S(1)} %get-tuple-element.6), kind=kOutput, calls=%fused_computation.8 | convolution fusion | flops 201474048 | bytes 3998720 | tf_op jit(solution)/shard_map/dot_general | solution.py:74
  65.5 1.3 %bitcast_add_fusion = f32[768,2,256]{0,2,1:T(8,128)S(1)} fusion(f32[768,2,1,256]{0,3,1,2:T(8,128)S(1)} %copy-done.1, bf16[768,2,256]{0,2,1:T(8,128)(2,1)} %collective-permute-done), kind=kLoop, calls=%fused_computation | loop fusion | flops 786432 | bytes 3932160 | tf_op jit(solution)/shard_map/add | solution.py:46
  66.8 2.4 %collective-permute-done.7 = bf16[1,64,2304]{2,1,0:T(8,128)(2,1)S(1)} collective-permute-done((bf16[1,64,2304]{2,1,0:T(8,128)(2,1)S(1)}, bf16[1,64,2304]{2,1,0:T(8,128)(2,1)S(1)}, u32[]{:S(2)}, u32[]{:S(2)}) %collective-permute-start.7) | collective-permute-done | bytes 294944 | tf_op jit(solution)/shard_map/ppermute | solution.py:19
  69.2 1.1 %fusion.7 = bf16[64,768]{1,0:T(8,128)(2,1)S(1)} fusion(f32[64,768]{1,0:T(8,128)S(1)} %fusion.2, bf16[768,2048]{1,0:T(8,128)(2,1)S(1)} %copy-done, bf16[1,64,2304]{2,1,0:T(8,128)(2,1)S(1)} %collective-permute-done.7, pred[768]{0:T(1024)(128)(4,1)S(1)} %get-tuple-element.5), kind=kOutput, calls=%fused_computation.18 | convolution fusion | flops 201474048 | bytes 3703808 | tf_op jit(solution)/shard_map/dot_general | solution.py:74
  70.4 1.6 %collective-permute-start.1 = (bf16[768,1,256]{0,2,1:T(8,128)(2,1)S(1)}, bf16[768,1,256]{0,2,1:T(8,128)(2,1)S(1)}, u32[]{:S(2)}, u32[]{:S(2)}) collective-permute-start(bf16[768,1,256]{0,2,1:T(8,128)(2,1)S(1)} %dynamic-slice_convert_fusion), channel_id=1, source_target_pairs={{0,2},{1,3},{2,0},{3,1},{4,6},{5,7},{6,4},{7,5},{8,10},{9,11},{10,... | collective-permute-start | bytes 1179656 | tf_op jit(solution)/shard_map/ppermute | solution.py:19
  72.0 1.2 %collective-permute-start.9 = (bf16[64,768]{1,0:T(8,128)(2,1)S(1)}, bf16[64,768]{1,0:T(8,128)(2,1)S(1)}, u32[]{:S(2)}, u32[]{:S(2)}) collective-permute-start(bf16[64,768]{1,0:T(8,128)(2,1)S(1)} %add_convert_fusion.1), channel_id=1, source_target_pairs={{0,2},{1,3},{2,0},{3,1},{4,6},{5,7},{6,4},{7,5},{8,10},{9,11},{10,... | collective-permute-start | bytes 294920 | tf_op jit(solution)/shard_map/ppermute | solution.py:19
  73.2 10.9 %collective-permute-done.9 = bf16[64,768]{1,0:T(8,128)(2,1)S(1)} collective-permute-done((bf16[64,768]{1,0:T(8,128)(2,1)S(1)}, bf16[64,768]{1,0:T(8,128)(2,1)S(1)}, u32[]{:S(2)}, u32[]{:S(2)}) %collective-permute-start.9) | collective-permute-done | bytes 98336 | tf_op jit(solution)/shard_map/ppermute | solution.py:19
  84.4 1.4 %convolution_add_fusion = f32[768,256]{0,1:T(8,128)} fusion(bf16[512,768]{1,0:T(8,128)(2,1)S(1)} %select_dynamic-update-slice_fusion, bf16[512,256]{1,0:T(8,128)(2,1)S(1)} %constant_dynamic-update-slice_fusion, bf16[768,1,256]{0,2,1:T(8,128)(2,1)S(1)} %collective-permute-done.1, f32[768,2,256]{0,2,1:T(8,128)S(1)} %bitcast_add_fusion, s32[]{:T(128)S(6)} %select_n.98, ...), kind=kOutput, calls=%fused_computation.1 | convolution fusion | flops 202113024 | bytes 3015684 | tf_op jit(solution)/shard_map/dot_general | solution.py:88
  85.7 2.3 %copy.10 = f32[768,2,128]{2,0,1:T(8,128)} copy(f32[768,2,128]{0,2,1:T(8,128)} %bitcast.83) | data formatting | bytes 1572864 | tf_op jit(solution)/shard_map/reshape | solution.py:90
  88.0 2.1 %convolution_convert_fusion = bf16[768,2,128]{0,2,1:T(8,128)(2,1)S(1)} fusion(f32[768,2,128]{2,0,1:T(8,128)} %copy.10, f32[128]{0:T(128)} %get-tuple-element.24, s32[128]{0:T(128)S(1)} %get-tuple-element.17, s32[128]{0:T(128)S(1)} %get-tuple-element.18, s32[128]{0:T(128)S(1)} %get-tuple-element.19, s32[128]{0:T(128)S(1)} %get-tuple-element.20, ...), kind=kOutput, calls=%fused_computation.2 | convolution fusion | flops 302841856 | bytes 1183744 | tf_op jit(solution)/shard_map/thd,de->the/dot_general | solution.py:92
  90.1 0.9 %copy.11 = bf16[768,256]{1,0:T(8,128)(2,1)} copy(bf16[768,256]{0,1:T(8,128)(2,1)S(1)} %bitcast.84) | data formatting | bytes 786432 | tf_op jit(solution)/shard_map/convert_element_type | solution.py:93
  (43 shorter events, 3.7 us)
Async XLA Ops:
  0.0 7.6 %copy-start = (bf16[768,2048]{1,0:T(8,128)(2,1)S(1)}, bf16[768,2048]{1,0:T(8,128)(2,1)}, u32[]{:S(2)}) copy-start(bf16[768,2048]{1,0:T(8,128)(2,1)} %param.7) | copy-start | bytes 9437188
  1.9 44.9 %collective-permute-start.2 = (bf16[1,64,2304]{2,1,0:T(8,128)(2,1)}, bf16[1,64,2304]{2,1,0:T(8,128)(2,1)}, u32[]{:S(2)}, u32[]{:S(2)}) collective-permute-start(bf16[1,64,2304]{2,1,0:T(8,128)(2,1)} %get-tuple-element.16), channel_id=1, source_target_pairs={{0,8},{4,12},{8,0},{12,4},{1,9},{5,13},{9,1},{13,5},{2,10},{6,14},... | collective-permute-start | bytes 884744 | tf_op jit(solution)/shard_map/ppermute | solution.py:19
  6.0 42.9 %collective-permute-start.4 = (bf16[1,64,2304]{2,1,0:T(8,128)(2,1)}, bf16[1,64,2304]{2,1,0:T(8,128)(2,1)}, u32[]{:S(2)}, u32[]{:S(2)}) collective-permute-start(bf16[1,64,2304]{2,1,0:T(8,128)(2,1)} %get-tuple-element.16), channel_id=1, source_target_pairs={{0,4},{4,0},{8,12},{12,8},{1,5},{5,1},{9,13},{13,9},{2,6},{6,2},{1... | collective-permute-start | bytes 884744 | tf_op jit(solution)/shard_map/ppermute | solution.py:19
  29.6 35.8 %collective-permute-start = (bf16[768,2,256]{0,2,1:T(8,128)(2,1)}, bf16[768,2,256]{0,2,1:T(8,128)(2,1)}, u32[]{:S(2)}, u32[]{:S(2)}) collective-permute-start(bf16[768,2,256]{0,2,1:T(8,128)(2,1)} %bitcast.85), channel_id=1, source_target_pairs={{0,1},{1,0},{2,3},{3,2},{4,5},{5,4},{6,7},{7,6},{8,9},{9,8},{10,11... | collective-permute-start | bytes 2359304 | tf_op jit(solution)/shard_map/ppermute | solution.py:19
  31.6 9.3 %copy-start.3 = (s32[768,1]{0,1:T(1,128)S(1)}, s32[768,1]{0,1:T(1,128)}, u32[]{:S(2)}) copy-start(s32[768,1]{0,1:T(1,128)} %param.8) | copy-start | bytes 9220
  36.0 7.7 %copy-start.5 = (s32[128]{0:T(128)S(1)}, s32[128]{0:T(128)}, u32[]{:S(2)}) copy-start(s32[128]{0:T(128)} %param.13) | copy-start | bytes 1540
  44.8 4.6 %copy-start.2 = (bf16[512,256]{1,0:T(8,128)(2,1)S(1)}, bf16[512,256]{1,0:T(8,128)(2,1)}, u32[]{:S(2)}) copy-start(bf16[512,256]{1,0:T(8,128)(2,1)} %constant_dynamic-update-slice_fusion.6) | copy-start | bytes 786436
  46.8 11.4 %collective-permute-start.3 = (bf16[1,64,2304]{2,1,0:T(8,128)(2,1)}, bf16[1,64,2304]{2,1,0:T(8,128)(2,1)S(1)}, u32[]{:S(2)}, u32[]{:S(2)}) collective-permute-start(bf16[1,64,2304]{2,1,0:T(8,128)(2,1)} %collective-permute-done.2), channel_id=1, source_target_pairs={{0,16},{16,0},{1,17},{17,1},{2,18},{18,2},{3,19},{19,3},{4,20},{20... | collective-permute-start | bytes 884744 | tf_op jit(solution)/shard_map/ppermute | solution.py:19
  48.4 9.4 %collective-permute-start.6 = (bf16[1,64,2304]{2,1,0:T(8,128)(2,1)}, bf16[1,64,2304]{2,1,0:T(8,128)(2,1)S(1)}, u32[]{:S(2)}, u32[]{:S(2)}) collective-permute-start(bf16[1,64,2304]{2,1,0:T(8,128)(2,1)} %collective-permute-done.2), channel_id=1, source_target_pairs={{0,4},{4,0},{8,12},{12,8},{1,5},{5,1},{9,13},{13,9},{2,6},{6,2},{1... | collective-permute-start | bytes 884744 | tf_op jit(solution)/shard_map/ppermute | solution.py:19
  48.9 14.4 %collective-permute-start.5 = (bf16[1,64,2304]{2,1,0:T(8,128)(2,1)}, bf16[1,64,2304]{2,1,0:T(8,128)(2,1)S(1)}, u32[]{:S(2)}, u32[]{:S(2)}) collective-permute-start(bf16[1,64,2304]{2,1,0:T(8,128)(2,1)} %collective-permute-done.4), channel_id=1, source_target_pairs={{0,16},{16,0},{1,17},{17,1},{2,18},{18,2},{3,19},{19,3},{4,20},{20... | collective-permute-start | bytes 884744 | tf_op jit(solution)/shard_map/ppermute | solution.py:19
  57.8 11.4 %collective-permute-start.7 = (bf16[1,64,2304]{2,1,0:T(8,128)(2,1)S(1)}, bf16[1,64,2304]{2,1,0:T(8,128)(2,1)S(1)}, u32[]{:S(2)}, u32[]{:S(2)}) collective-permute-start(bf16[1,64,2304]{2,1,0:T(8,128)(2,1)S(1)} %collective-permute-done.6), channel_id=1, source_target_pairs={{0,16},{16,0},{1,17},{17,1},{2,18},{18,2},{3,19},{19,3},{4,20},{20... | collective-permute-start | bytes 884744 | tf_op jit(solution)/shard_map/ppermute | solution.py:19
  63.3 2.2 %copy-start.1 = (f32[768,2,1,256]{0,3,1,2:T(8,128)S(1)}, f32[768,2,1,256]{0,3,1,2:T(8,128)}, u32[]{:S(2)}) copy-start(f32[768,2,1,256]{0,3,1,2:T(8,128)} %copy.8) | copy-start | bytes 4718596
  69.2 15.2 %copy-start.4 = (f32[256]{0:T(256)S(1)}, f32[256]{0:T(256)}, u32[]{:S(2)}) copy-start(f32[256]{0:T(256)} %param.10) | copy-start | bytes 3076
  70.3 1.7 %collective-permute-start.8 = (bf16[64,768]{1,0:T(8,128)(2,1)S(1)}, bf16[64,768]{1,0:T(8,128)(2,1)S(1)}, u32[]{:S(2)}, u32[]{:S(2)}) collective-permute-start(bf16[64,768]{1,0:T(8,128)(2,1)S(1)} %fusion.7), channel_id=1, source_target_pairs={{0,1},{1,0},{2,3},{3,2},{4,5},{5,4},{6,7},{7,6},{8,9},{9,8},{10,11... | collective-permute-start | bytes 294920 | tf_op jit(solution)/shard_map/ppermute | solution.py:19
  70.4 13.9 %collective-permute-start.1 = (bf16[768,1,256]{0,2,1:T(8,128)(2,1)S(1)}, bf16[768,1,256]{0,2,1:T(8,128)(2,1)S(1)}, u32[]{:S(2)}, u32[]{:S(2)}) collective-permute-start(bf16[768,1,256]{0,2,1:T(8,128)(2,1)S(1)} %dynamic-slice_convert_fusion), channel_id=1, source_target_pairs={{0,2},{1,3},{2,0},{3,1},{4,6},{5,7},{6,4},{7,5},{8,10},{9,11},{10,... | collective-permute-start | bytes 1179656 | tf_op jit(solution)/shard_map/ppermute | solution.py:19
  72.0 12.1 %collective-permute-start.9 = (bf16[64,768]{1,0:T(8,128)(2,1)S(1)}, bf16[64,768]{1,0:T(8,128)(2,1)S(1)}, u32[]{:S(2)}, u32[]{:S(2)}) collective-permute-start(bf16[64,768]{1,0:T(8,128)(2,1)S(1)} %add_convert_fusion.1), channel_id=1, source_target_pairs={{0,2},{1,3},{2,0},{3,1},{4,6},{5,7},{6,4},{7,5},{8,10},{9,11},{10,... | collective-permute-start | bytes 294920 | tf_op jit(solution)/shard_map/ppermute | solution.py:19

commit v2 on v1

v2 whole, which is shorter than its diff:
```python
import functools

import jax
import jax.numpy as jnp
import numpy as np
from jax import lax
from jax.experimental import pallas as pl
from jax.experimental.pallas import tpu as pltpu
from jax.sharding import PartitionSpec as P

VMEM = pl.BlockSpec(memory_space=pltpu.VMEM)
SMEM = pl.BlockSpec(memory_space=pltpu.SMEM)
F32, BF16 = jnp.float32, jnp.bfloat16
LAST = (((1,), (1,)), ((), ()))


def params(mib):
    return pltpu.CompilerParams(vmem_limit_bytes=mib << 20)


def cost(flops, moved):
    return pl.CostEstimate(flops=flops, bytes_accessed=moved, transcendentals=0)


def hadamard(size):
    index = np.arange(size)
    shared = index[:, None] & index[None, :]
    parity = np.zeros_like(shared)
    while shared.any():
        parity, shared = parity ^ (shared & 1), shared >> 1
    return jnp.asarray(1 - 2 * parity, BF16)


def swap(x, axis, bit):
    return lax.ppermute(x, axis, [(i, i ^ bit) for i in range(lax.axis_size(axis))])


def rotate(value, signs, matrix):
    head = matrix.shape[0]
    scale = signs * (1.0 / np.sqrt(head))
    turned = []
    for at in range(0, value.shape[1], head):
        signed = value[:, at : at + head] * scale
        high = signed.astype(BF16)
        rest = (signed - high.astype(F32)).astype(BF16)
        turned.append(
            jnp.dot(high, matrix, preferred_element_type=F32) + jnp.dot(rest, matrix, preferred_element_type=F32)
        )
    return turned


def partial_kernel(me_ref, tokens_ref, weight_ref, give_ref, keep_ref):
    step, half = pl.program_id(0), pl.num_programs(0) // 2
    product = jnp.dot(tokens_ref[...], weight_ref[...], preferred_element_type=F32).astype(BF16)

    @pl.when(step < half)
    def _():
        give_ref[0] = product

    @pl.when(step >= half)
    def _():
        keep_ref[0] = product


def partials(me, tokens, weight, parts):
    rows, features = tokens.shape
    width = weight.shape[1] // parts
    half = parts // 2

    def offset(step):
        return jnp.where(step < half, 2 * step + 1, 2 * (step - half))

    block = jax.ShapeDtypeStruct((half, rows, width), BF16)
    return pl.pallas_call(
        partial_kernel,
        grid_spec=pltpu.PrefetchScalarGridSpec(
            num_scalar_prefetch=1,
            grid=(parts,),
            in_specs=[
                pl.BlockSpec((rows, features), lambda step, me: (0, 0)),
                pl.BlockSpec((features, width), lambda step, me: (0, jnp.bitwise_xor(me[0], offset(step)))),
            ],
            out_specs=[
                pl.BlockSpec((1, rows, width), lambda step, me: (jnp.minimum(step, half - 1), 0, 0)),
                pl.BlockSpec((1, rows, width), lambda step, me: (jnp.maximum(step - half, 0), 0, 0)),
            ],
        ),
        out_shape=[block, block],
        compiler_params=params(24),
        cost_estimate=cost(2 * rows * features * width * parts, 2 * (tokens.size + weight.size + rows * width * parts)),
        name="partials",
    )(me, tokens, weight)


def base_kernel(*refs):
    terms, (scale_ref, bits_ref, matrix_ref, out_ref) = refs[:-4], refs[-4:]
    total = terms[0][0].astype(F32)
    for term in terms[1:]:
        total = total + term[0].astype(F32)
    signs = (1 - 2 * bits_ref[...]).astype(F32)
    turned = rotate(total * scale_ref[...], signs, matrix_ref[...])
    out_ref[...] = jnp.concatenate(turned, axis=1)


def rotated_base(terms, scale, bits, matrix):
    _, rows, width = terms[0].shape
    whole = lambda shape: pl.BlockSpec(shape, lambda: (0,) * len(shape))
    return pl.pallas_call(
        base_kernel,
        in_specs=[whole((1, rows, width))] * len(terms) + [whole(a.shape) for a in (scale, bits, matrix)],
        out_specs=whole((rows, width)),
        out_shape=jax.ShapeDtypeStruct((rows, width), F32),
        compiler_params=params(16),
        cost_estimate=cost(4 * rows * width * matrix.shape[0], 2 * rows * width * (len(terms) + 2)),
        name="rotated_base",
    )(*terms, scale, bits, matrix)


def low_kernel(pieces, share, rank, ids_ref, named_ref, tokens_ref, *refs):
    refs, out_ref = refs[:-1], refs[-1]
    features = tokens_ref.shape[1]
    total = None if len(refs) == pieces else refs[pieces][...]
    rows = [refs[i][k, :, :features] for i in range(pieces) for k in range(share)]
    joined = rows[0] if len(rows) == 1 else jnp.concatenate(rows, axis=0)
    product = lax.dot_general(joined, tokens_ref[...], LAST, preferred_element_type=F32)
    for i in range(len(rows)):
        term = jnp.where(ids_ref[...] == named_ref[i], product[i * rank : (i + 1) * rank], 0.0)
        total = term if total is None else total + term
    out_ref[...] = total.astype(out_ref.dtype)


def low_rows(ids, named, tokens, pieces, before, dtype):
    share, rank, _ = pieces[0].shape
    rows, features = tokens.shape
    more = [] if before is None else [before]
    return pl.pallas_call(
        functools.partial(low_kernel, len(pieces), share, rank),
        in_specs=[VMEM, SMEM] + [VMEM] * (1 + len(pieces) + len(more)),
        out_specs=VMEM,
        out_shape=jax.ShapeDtypeStruct((rank, rows), dtype),
        compiler_params=params(24),
        cost_estimate=cost(2 * rows * features * rank * share * len(pieces), 2 * tokens.size),
        name="low_rows",
    )(ids, named, tokens, *pieces, *more)


def ups_kernel(pieces, share, rank, ids_ref, named_ref, bits_ref, matrix_ref, *refs):
    features = refs[0].shape[2] - refs[-2].shape[1]
    up_ref, mask_ref = refs[-2:]
    signs = (1 - 2 * bits_ref[...]).astype(F32)
    ids = jnp.broadcast_to(ids_ref[...], (rank, ids_ref.shape[1])).T
    for i in range(pieces):
        for k in range(share):
            at = (i * share + k) * rank
            turned = rotate(refs[i][k, :, features:].astype(F32), signs, matrix_ref[...])
            up_ref[at : at + rank, :] = jnp.concatenate(turned, axis=1).astype(BF16)
            mask_ref[:, at : at + rank] = jnp.where(ids == named_ref[i * share + k], 1.0, 0.0).astype(BF16)


def rotated_ups(ids, named, bits, matrix, pieces, width):
    share, rank, _ = pieces[0].shape
    rows = ids.shape[1]
    every = len(pieces) * share * rank
    return pl.pallas_call(
        functools.partial(ups_kernel, len(pieces), share, rank),
        in_specs=[VMEM, SMEM, VMEM, VMEM] + [VMEM] * len(pieces),
        out_specs=[VMEM, VMEM],
        out_shape=[jax.ShapeDtypeStruct((every, width), BF16), jax.ShapeDtypeStruct((rows, every), BF16)],
        compiler_params=params(32),
        cost_estimate=cost(4 * every * width * matrix.shape[0], 2 * every * (rows + width)),
        name="rotated_ups",
    )(ids, named, bits, matrix, *pieces)


def final_kernel(mine_ref, theirs_ref, base_ref, up_ref, mask_ref, out_ref):
    low = (mine_ref[...].astype(F32) + theirs_ref[...].astype(F32)).T.astype(BF16)
    every = mask_ref.shape[1]
    spread = jnp.concatenate([low] * (every // low.shape[1]), axis=1) * mask_ref[...]
    delta = jnp.dot(spread, up_ref[...], preferred_element_type=F32)
    out_ref[...] = (base_ref[...] + delta).astype(BF16)


def final(mine, theirs, base, up, mask):
    rows, width = base.shape
    return pl.pallas_call(
        final_kernel,
        in_specs=[VMEM] * 5,
        out_specs=VMEM,
        out_shape=jax.ShapeDtypeStruct((rows, width), BF16),
        compiler_params=params(32),
        cost_estimate=cost(2 * rows * width * up.shape[0], 6 * rows * width),
        name="final",
    )(mine, theirs, base, up, mask)


def local(tokens, adapter_ids, base_weight, channel_scale, adapter_down, adapter_up, sign_bits):
    planes, groups, parts = lax.axis_size("adp"), lax.axis_size("grp"), lax.axis_size("tp")
    z, g, me = lax.axis_index("adp"), lax.axis_index("grp"), lax.axis_index("tp")
    rows, features = tokens.shape
    here, _, rank = adapter_down.shape
    width = adapter_up.shape[2]
    share = here // groups
    matrix = hadamard(sign_bits.shape[0])
    bits, scale, ids = sign_bits[None, :], channel_scale[None, :], adapter_ids.T

    down = jnp.swapaxes(adapter_down, 1, 2)

    def own(off):
        at = (g ^ off) * share
        cut = [lax.dynamic_slice_in_dim(a, at, share, 0) for a in (down, adapter_up)]
        return jnp.concatenate(cut, axis=2)

    def names(held):
        firsts = [(z ^ plane) * here + (g ^ off) * share for plane, off, _ in held]
        return jnp.stack([first + k for first in firsts for k in range(share)]).astype(jnp.int32)

    home = [(0, off, own(off)) for off in range(groups)]
    mine = [(0, 0, home[0][2])]
    swapped = []
    bit = planes // 2
    while bit:
        new = [(plane | bit, 0, swap(piece, "adp", bit)) for plane, _, piece in mine]
        mine += new
        swapped += [(plane, off, swap(piece, "grp", off)) for plane, _, piece in new for off in range(1, groups)]
        bit //= 2

    give, keep = partials(me[None].astype(jnp.int32), tokens, base_weight, parts)
    come = swap(give, "tp", 1)
    terms = [keep[:1], come[:1]]
    bit, sums = 2, None
    while bit < parts:
        sums = keep.astype(F32) + come.astype(F32) if sums is None else sums[0::2] + come.astype(F32)
        come = swap(sums[1::2].astype(BF16), "tp", bit)
        terms.append(come[:1])
        bit *= 2
    base = rotated_base(terms, scale, bits, matrix)

    early = home + mine[1:-1] + swapped[:0]
    middle = [mine[-1]] + swapped[:-1]
    late = swapped[-1:]
    low = low_rows(ids, names(early), tokens, [p for _, _, p in early], None, F32)
    low = low_rows(ids, names(middle), tokens, [p for _, _, p in middle], low, F32)
    low = low_rows(ids, names(late), tokens, [p for _, _, p in late], low, BF16)
    bit = 1
    while bit < parts // 2:
        low = (low.astype(F32) + swap(low, "tp", bit).astype(F32)).astype(BF16)
        bit *= 2
    theirs = swap(low, "tp", bit)
    every = early + middle + late
    up, mask = rotated_ups(ids, names(every), bits, matrix, [p for _, _, p in every], width)
    return final(low, theirs, base, up, mask)


def solution(mesh):
    return jax.shard_map(
        local,
        mesh=mesh,
        in_specs=(
            P(("grp", "adp"), "tp"),
            P(("grp", "adp"), None),
            P("tp", None),
            P("tp"),
            P("adp", "tp", None),
            P("adp", None, "tp"),
            P(),
        ),
        out_specs=P(("grp", "adp"), "tp"),
        check_vma=False,
    )
```

time: 91.9 us -> 63.9 us (0.70)
  matrix products: 23.9 us -> 0 us
  local copies, waits for them, and re-layouts: 30.8 us -> 11.6 us
  Pallas kernels: 0 us -> 16 us
  starting transfers between devices: 11.5 us -> 13.1 us
  waiting for transfers between devices: 19.9 us -> 18.8 us
  other arithmetic: 4.74 us -> 3.74 us
    dot_general x11 -> x0, matrix products: 23.9 us -> none  [the longest x8 13.2 us: local(): lax.dot_general(piece[k, :, :features], tokens, (((1,), (1,)), ((), ())),...]
    pallas_call x0 -> x7, Pallas kernels: none -> 16 us  [the longest x3 6.46 us: low_rows(): pl.pallas_call(functools.partial(low_kernel, len(pieces), share, rank), i...]
    dynamic_slice x3 -> x2, local copies, waits for them, and re-layouts: 13.7 us -> 2.55 us  [own(): lax.dynamic_slice_in_dim(a, at, share, 0)]
    another operation x1, local copies, waits for them, and re-layouts: 5.59 us -> 0.08 us  [names(): jnp.stack([first + k for first in firsts for k in range(share)])]
    reshape x1 -> x0, local copies, waits for them, and re-layouts: 2.28 us -> none  [local(): value.reshape(rows, width // head, head)]
    slice x0 -> x2, local copies, waits for them, and re-layouts: none -> 2.05 us  [local(): terms = [keep[:1], come[:1]]]
    another operation x0 -> x3, other arithmetic: none -> 2 us
    ppermute x10, starting transfers between devices: 11.5 us -> 13.1 us  [swap(): lax.ppermute(x, axis, [(i, i ^ bit) for i in range(lax.axis_size(axis))])]
  transfers between devices with their start and end apart: 10 -> 10, of which waited for: 4 -> 7; matrix products, arithmetic and copies ran while one was open for 55% -> 9% of each run, Pallas kernels for 0% -> 23%
where the time goes in v2:
time: 63.9 us; the launch traced here: 63.3 us
  waiting for transfers between devices  18.8 us (29%)
  Pallas kernels  16 us (25%)
  starting transfers between devices  13.1 us (21%)
  local copies, waits for them, and re-layouts  11.6 us (18%)
  other arithmetic  3.74 us (6%)
    ppermute x10, waiting for transfers between devices, swap(): lax.ppermute(x, axis, [(i, i ^ bit) for i in range(lax.axis_size(axis))])  18.8 us
    ppermute x10, starting transfers between devices, swap(): lax.ppermute(x, axis, [(i, i ^ bit) for i in range(lax.axis_size(axis))])  13.1 us
    unnamed x22, local copies, waits for them, and re-layouts  6.9 us
    pallas_call x3, Pallas kernels, low_rows(): pl.pallas_call(functools.partial(low_kernel, len(pieces), share, rank), i...  6.46 us
    pallas_call x1, Pallas kernels, partials(): pl.pallas_call(partial_kernel, grid_spec=pltpu.PrefetchScalarGridSpec(num...  5.5 us
    dynamic_slice x2, local copies, waits for them, and re-layouts, own(): lax.dynamic_slice_in_dim(a, at, share, 0)  2.55 us
    pallas_call x1, Pallas kernels, rotated_ups(): pl.pallas_call(functools.partial(ups_kernel, len(pieces), share, rank), i...  2.07 us
    slice x2, local copies, waits for them, and re-layouts, local(): terms = [keep[:1], come[:1]]  2.05 us
  transfers between devices with their start and end apart: 10, of which 7 were waited for; matrix products, arithmetic and copies ran while one was open for 9% of the time, Pallas kernels for 23%

profile of v2, /device:TPU:0, one launch (start us, length us, event | category | flops | bytes accessed | tf_op | source)
XLA Modules:
  0.0 63.3 jit_solution(9078867480733919846)
XLA Ops:
  0.0 1.8 %dynamic-slice_bitcast_fusion = (bf16[1,64,2048]{2,1,0:T(8,128)(2,1)}, bf16[1,64,2048]{2,1,0:T(8,128)(2,1)S(1)}) fusion(bf16[2,2048,64]{1,2,0:T(8,128)(2,1)} %param.12, s32[]{:T(128)S(6)} %select_n.9, s32[]{:T(128)S(6)} %select_n.8), kind=kLoop, calls=%fused_computation.3 | loop fusion | bytes 1048584 | tf_op jit(solution)/shard_map/dynamic_slice | solution.py:210
  1.8 0.8 %constant_dynamic-slice_fusion = (bf16[1,64,256]{2,1,0:T(8,128)(2,1)S(1)}, bf16[1,64,256]{2,1,0:T(8,128)(2,1)S(1)}) fusion(bf16[2,64,256]{2,1,0:T(8,128)(2,1)} %param.13, s32[]{:T(128)S(6)} %select_n.9, s32[]{:T(128)S(6)} %select_n.8), kind=kLoop, calls=%fused_computation.6 | loop fusion | bytes 131080 | tf_op jit(solution)/shard_map/dynamic_slice | solution.py:210
  2.6 4.1 %collective-permute-start = (bf16[1,64,2304]{2,1,0:T(8,128)(2,1)S(1)}, bf16[1,64,2304]{2,1,0:T(8,128)(2,1)}, u32[]{:S(2)}, u32[]{:S(2)}) collective-permute-start(bf16[1,64,2304]{2,1,0:T(8,128)(2,1)S(1)} %pad_maximum_fusion.refs_0_), channel_id=1, source_target_pairs={{0,8},{4,12},{8,0},{12,4},{1,9},{5,13},{9,1},{13,5},{2,10},{6,14},... | collective-permute-start | bytes 884744 | tf_op jit(solution)/shard_map/ppermute | solution.py:35
  6.7 1.9 %copy-done = bf16[768,2048]{1,0:T(8,128)(2,1)S(1)} copy-done((bf16[768,2048]{1,0:T(8,128)(2,1)S(1)}, bf16[768,2048]{1,0:T(8,128)(2,1)}, u32[]{:S(2)}) %copy-start) | copy-done | bytes 3145752
  8.6 2.2 %copy-done.10 = bf16[2048,1024]{1,0:T(8,128)(2,1)S(1)} copy-done((bf16[2048,1024]{1,0:T(8,128)(2,1)S(1)}, bf16[2048,1024]{1,0:T(8,128)(2,1)}, u32[]{:S(2)}) %copy-start.10) | copy-done | bytes 4194328
  10.8 5.5 %partials.1 = (bf16[2,768,256]{2,1,0:T(8,128)(2,1)}, bf16[2,768,256]{2,1,0:T(8,128)(2,1)S(1)}) custom-call(s32[1]{0:T(128)} %bitcast.11.me_ref, bf16[768,2048]{1,0:T(8,128)(2,1)S(1)} %copy-done, bf16[2048,1024]{1,0:T(8,128)(2,1)S(1)} %copy-done.10), custom_call_target="tpu_custom_call" | custom-call | flops 3221225472 | bytes 8912896 | tf_op jit(solution)/shard_map/partials/pallas_call | solution.py:74
  16.3 0.9 %copy-done.4 = bf16[2,768,256]{2,1,0:T(8,128)(2,1)} copy-done((bf16[2,768,256]{2,1,0:T(8,128)(2,1)}, bf16[2,768,256]{2,1,0:T(8,128)(2,1)S(1)}, u32[]{:S(2)}) %copy-start.4) | copy-done | bytes 786456
  17.1 1.6 %collective-permute-start.4 = (bf16[1,64,2304]{2,1,0:T(8,128)(2,1)S(1)}, bf16[1,64,2304]{2,1,0:T(8,128)(2,1)}, u32[]{:S(2)}, u32[]{:S(2)}) collective-permute-start(bf16[1,64,2304]{2,1,0:T(8,128)(2,1)S(1)} %pad_maximum_fusion.refs_0_), channel_id=1, source_target_pairs={{0,4},{4,0},{8,12},{12,8},{1,5},{5,1},{9,13},{13,9},{2,6},{6,2},{1... | collective-permute-start | bytes 884744 | tf_op jit(solution)/shard_map/ppermute | solution.py:35
  18.7 1.4 %collective-permute-done.refs_2_ = bf16[1,64,2304]{2,1,0:T(8,128)(2,1)} collective-permute-done((bf16[1,64,2304]{2,1,0:T(8,128)(2,1)S(1)}, bf16[1,64,2304]{2,1,0:T(8,128)(2,1)}, u32[]{:S(2)}, u32[]{:S(2)}) %collective-permute-start) | collective-permute-done | bytes 294944 | tf_op jit(solution)/shard_map/ppermute | solution.py:35
  20.1 0.7 %collective-permute-start.1 = (bf16[1,64,2304]{2,1,0:T(8,128)(2,1)}, bf16[1,64,2304]{2,1,0:T(8,128)(2,1)}, u32[]{:S(2)}, u32[]{:S(2)}) collective-permute-start(bf16[1,64,2304]{2,1,0:T(8,128)(2,1)} %collective-permute-done.refs_2_), channel_id=1, source_target_pairs={{0,4},{4,0},{8,12},{12,8},{1,5},{5,1},{9,13},{13,9},{2,6},{6,2},{1... | collective-permute-start | bytes 884744 | tf_op jit(solution)/shard_map/ppermute | solution.py:35
  20.8 1.7 %pad_maximum_fusion.1.refs_1_ = bf16[1,64,2304]{2,1,0:T(8,128)(2,1)} fusion(bf16[1,64,256]{2,1,0:T(8,128)(2,1)S(1)} %get-tuple-element.15, bf16[1,64,2048]{2,1,0:T(8,128)(2,1)} %get-tuple-element.13), kind=kLoop, calls=%fused_computation.2 | loop fusion | flops 589824 | bytes 589824 | tf_op jit(solution)/shard_map/concatenate | solution.py:211
  22.5 1.5 %collective-permute-start.3 = (bf16[1,64,2304]{2,1,0:T(8,128)(2,1)}, bf16[1,64,2304]{2,1,0:T(8,128)(2,1)}, u32[]{:S(2)}, u32[]{:S(2)}) collective-permute-start(bf16[1,64,2304]{2,1,0:T(8,128)(2,1)} %collective-permute-done.refs_2_), channel_id=1, source_target_pairs={{0,16},{16,0},{1,17},{17,1},{2,18},{18,2},{3,19},{19,3},{4,20},{20... | collective-permute-start | bytes 884744 | tf_op jit(solution)/shard_map/ppermute | solution.py:35
  24.0 3.1 %collective-permute-done.4.refs_3_ = bf16[1,64,2304]{2,1,0:T(8,128)(2,1)} collective-permute-done((bf16[1,64,2304]{2,1,0:T(8,128)(2,1)S(1)}, bf16[1,64,2304]{2,1,0:T(8,128)(2,1)}, u32[]{:S(2)}, u32[]{:S(2)}) %collective-permute-start.4) | collective-permute-done | bytes 294944 | tf_op jit(solution)/shard_map/ppermute | solution.py:35
  27.1 1.5 %collective-permute-start.5 = (bf16[1,64,2304]{2,1,0:T(8,128)(2,1)}, bf16[1,64,2304]{2,1,0:T(8,128)(2,1)}, u32[]{:S(2)}, u32[]{:S(2)}) collective-permute-start(bf16[1,64,2304]{2,1,0:T(8,128)(2,1)} %collective-permute-done.4.refs_3_), channel_id=1, source_target_pairs={{0,16},{16,0},{1,17},{17,1},{2,18},{18,2},{3,19},{19,3},{4,20},{20... | collective-permute-start | bytes 884744 | tf_op jit(solution)/shard_map/ppermute | solution.py:35
  28.6 4.4 %collective-permute-done.1.refs_0_.refs_4_ = bf16[1,64,2304]{2,1,0:T(8,128)(2,1)} collective-permute-done((bf16[1,64,2304]{2,1,0:T(8,128)(2,1)}, bf16[1,64,2304]{2,1,0:T(8,128)(2,1)}, u32[]{:S(2)}, u32[]{:S(2)}) %collective-permute-start.1) | collective-permute-done | bytes 294944 | tf_op jit(solution)/shard_map/ppermute | solution.py:35
  33.0 1.5 %collective-permute-start.2 = (bf16[1,64,2304]{2,1,0:T(8,128)(2,1)}, bf16[1,64,2304]{2,1,0:T(8,128)(2,1)}, u32[]{:S(2)}, u32[]{:S(2)}) collective-permute-start(bf16[1,64,2304]{2,1,0:T(8,128)(2,1)} %collective-permute-done.1.refs_0_.refs_4_), channel_id=1, source_target_pairs={{0,16},{16,0},{1,17},{17,1},{2,18},{18,2},{3,19},{19,3},{4,20},{20... | collective-permute-start | bytes 884744 | tf_op jit(solution)/shard_map/ppermute | solution.py:35
  34.7 1.0 %copy-done.2 = bf16[1,64,2304]{2,1,0:T(8,128)(2,1)S(1)} copy-done((bf16[1,64,2304]{2,1,0:T(8,128)(2,1)S(1)}, bf16[1,64,2304]{2,1,0:T(8,128)(2,1)}, u32[]{:S(2)}) %copy-start.2) | copy-done | bytes 294936
  35.6 2.1 %low_rows.3.refs_3_ = f32[64,768]{1,0:T(8,128)S(1)} custom-call(s32[1,768]{1,0:T(1,128)S(1)} %bitcast.16, s32[4]{0:T(128)S(1)} %pad_add_fusion.1.named_ref, bf16[768,2048]{1,0:T(8,128)(2,1)S(1)} %copy-done.1, bf16[1,64,2304]{2,1,0:T(8,128)(2,1)S(1)} %pad_maximum_fusion.refs_0_, bf16[1,64,2304]{2,1,0:T(8,128)(2,1)S(1)} %copy-done.2, ...), custom_call_target="tpu_custom_call" | custom-call | flops 805306368 | bytes 3145728 | tf_op jit(solution)/shard_map/low_rows/pallas_call | solution.py:136
  37.7 1.3 %collective-permute-done.5.refs_2_.refs_6_ = bf16[1,64,2304]{2,1,0:T(8,128)(2,1)} collective-permute-done((bf16[1,64,2304]{2,1,0:T(8,128)(2,1)}, bf16[1,64,2304]{2,1,0:T(8,128)(2,1)}, u32[]{:S(2)}, u32[]{:S(2)}) %collective-permute-start.5) | collective-permute-done | bytes 294944 | tf_op jit(solution)/shard_map/ppermute | solution.py:35
  39.0 2.3 %low_rows.4.refs_1_ = f32[64,768]{1,0:T(8,128)S(1)} custom-call(s32[1,768]{1,0:T(1,128)S(1)} %bitcast.17, s32[3]{0:T(128)S(1)} %pad_add_fusion.named_ref, bf16[768,2048]{1,0:T(8,128)(2,1)S(1)} %copy-done.1, bf16[1,64,2304]{2,1,0:T(8,128)(2,1)} %collective-permute-done.1.refs_0_.refs_4_, bf16[1,64,2304]{2,1,0:T(8,128)(2,1)} %collective-permute-done.3.refs_1_.refs_5_, ...), custom_call_target="tpu_custom_call" | custom-call | flops 603979776 | bytes 3145728 | tf_op jit(solution)/shard_map/low_rows/pallas_call | solution.py:136
  41.4 2.7 %collective-permute-done.2.refs_0_.refs_7_ = bf16[1,64,2304]{2,1,0:T(8,128)(2,1)} collective-permute-done((bf16[1,64,2304]{2,1,0:T(8,128)(2,1)}, bf16[1,64,2304]{2,1,0:T(8,128)(2,1)}, u32[]{:S(2)}, u32[]{:S(2)}) %collective-permute-start.2) | collective-permute-done | bytes 294944 | tf_op jit(solution)/shard_map/ppermute | solution.py:35
  44.1 2.1 %low_rows.5 = bf16[64,768]{1,0:T(8,128)(2,1)S(1)} custom-call(s32[1,768]{1,0:T(1,128)S(1)} %bitcast.18, s32[1]{0:T(128)} %bitcast.1.named_ref, bf16[768,2048]{1,0:T(8,128)(2,1)S(1)} %copy-done.1, bf16[1,64,2304]{2,1,0:T(8,128)(2,1)} %collective-permute-done.2.refs_0_.refs_7_, f32[64,768]{1,0:T(8,128)S(1)} %low_rows.4.refs_1_), custom_call_target="tpu_custom_call" | custom-call | flops 201326592 | bytes 3145728 | tf_op jit(solution)/shard_map/low_rows/pallas_call | solution.py:136
  46.2 1.8 %add_convert_fusion = bf16[1,768,256]{2,1,0:T(8,128)(2,1)} fusion(bf16[2,768,256]{2,1,0:T(8,128)(2,1)} %collective-permute-done.8, bf16[2,768,256]{2,1,0:T(8,128)(2,1)S(1)} %copy-done.5), kind=kLoop, calls=%fused_computation | loop fusion | flops 786432 | bytes 1179648 | tf_op jit(solution)/shard_map/convert
  48.0 1.5 %collective-permute-start.9 = (bf16[1,768,256]{2,1,0:T(8,128)(2,1)}, bf16[1,768,256]{2,1,0:T(8,128)(2,1)S(1)}, u32[]{:S(2)}, u32[]{:S(2)}) collective-permute-start(bf16[1,768,256]{2,1,0:T(8,128)(2,1)} %add_convert_fusion), channel_id=1, source_target_pairs={{0,2},{1,3},{2,0},{3,1},{4,6},{5,7},{6,4},{7,5},{8,10},{9,11},{10,... | collective-permute-start | bytes 1179656 | tf_op jit(solution)/shard_map/ppermute | solution.py:35
  49.6 0.6 collective-permute-start.7
  50.3 1.0 %slice.11.refs_0_ = bf16[1,768,256]{2,1,0:T(8,128)(2,1)S(1)} slice(bf16[2,768,256]{2,1,0:T(8,128)(2,1)} %copy-done.4), slice={[0:1], [0:768], [0:256]} | slice | bytes 786432 | tf_op jit(solution)/shard_map/slice | solution.py:229
  51.3 1.0 %slice.14.refs_1_ = bf16[1,768,256]{2,1,0:T(8,128)(2,1)S(1)} slice(bf16[2,768,256]{2,1,0:T(8,128)(2,1)} %collective-permute-done.8), slice={[0:1], [0:768], [0:256]} | slice | bytes 786432 | tf_op jit(solution)/shard_map/slice | solution.py:229
  52.3 1.0 %copy-done.3 = bf16[1,64,2304]{2,1,0:T(8,128)(2,1)S(1)} copy-done((bf16[1,64,2304]{2,1,0:T(8,128)(2,1)S(1)}, bf16[1,64,2304]{2,1,0:T(8,128)(2,1)}, u32[]{:S(2)}) %copy-start.3) | copy-done | bytes 294936
  53.3 2.1 %rotated_ups.1 = (bf16[512,256]{1,0:T(8,128)(2,1)S(1)}, bf16[768,512]{1,0:T(8,128)(2,1)S(1)}) custom-call(s32[1,768]{1,0:T(1,128)S(1)} %bitcast.19, s32[8]{0:T(128)S(1)} %stack.51.named_ref, s32[1,128]{1,0:T(1,128)S(1)} %bitcast.20, bf16[128,128]{1,0:T(8,128)(2,1)S(1)} %copy-done.6, bf16[1,64,2304]{2,1,0:T(8,128)(2,1)S(1)} %pad_maximum_fusion.refs_0_, ...), custom_call_target="tpu_custom_call" | custom-call | flops 67108864 | bytes 1048576 | tf_op jit(solution)/shard_map/rotated_ups/pallas_call | solution.py:164
  55.4 4.8 %collective-permute-done.9.refs_2_ = bf16[1,768,256]{2,1,0:T(8,128)(2,1)S(1)} collective-permute-done((bf16[1,768,256]{2,1,0:T(8,128)(2,1)}, bf16[1,768,256]{2,1,0:T(8,128)(2,1)S(1)}, u32[]{:S(2)}, u32[]{:S(2)}) %collective-permute-start.9) | collective-permute-done | bytes 393248 | tf_op jit(solution)/shard_map/ppermute | solution.py:35
  60.7 1.2 %collective-permute-done.7.theirs_ref = bf16[64,768]{1,0:T(8,128)(2,1)S(1)} collective-permute-done((bf16[64,768]{1,0:T(8,128)(2,1)S(1)}, bf16[64,768]{1,0:T(8,128)(2,1)S(1)}, u32[]{:S(2)}, u32[]{:S(2)}) %collective-permute-start.7) | collective-permute-done | bytes 98336 | tf_op jit(solution)/shard_map/ppermute | solution.py:35
  61.9 1.4 %final.1 = bf16[768,256]{1,0:T(8,128)(2,1)} custom-call(bf16[64,768]{1,0:T(8,128)(2,1)S(1)} %add_convert_fusion.1.mine_ref, bf16[64,768]{1,0:T(8,128)(2,1)S(1)} %collective-permute-done.7.theirs_ref, f32[768,256]{1,0:T(8,128)S(1)} %rotated_base.1.base_ref, bf16[512,256]{1,0:T(8,128)(2,1)S(1)} %get-tuple-element.11.up_ref, ...), custom_call_target="tpu_custom_call" | custom-call | flops 201326592 | bytes 1179648 | tf_op jit(solution)/shard_map/final/pallas_call | solution.py:185
  (28 shorter events, 0.9 us)
Async XLA Ops:
  2.6 17.5 %collective-permute-start = (bf16[1,64,2304]{2,1,0:T(8,128)(2,1)S(1)}, bf16[1,64,2304]{2,1,0:T(8,128)(2,1)}, u32[]{:S(2)}, u32[]{:S(2)}) collective-permute-start(bf16[1,64,2304]{2,1,0:T(8,128)(2,1)S(1)} %pad_maximum_fusion.refs_0_), channel_id=1, source_target_pairs={{0,8},{4,12},{8,0},{12,4},{1,9},{5,13},{9,1},{13,5},{2,10},{6,14},... | collective-permute-start | bytes 884744 | tf_op jit(solution)/shard_map/ppermute | solution.py:35
  6.7 1.9 %copy-start = (bf16[768,2048]{1,0:T(8,128)(2,1)S(1)}, bf16[768,2048]{1,0:T(8,128)(2,1)}, u32[]{:S(2)}) copy-start(bf16[768,2048]{1,0:T(8,128)(2,1)} %tokens_ref.7) | copy-start | bytes 9437188
  8.6 2.2 %copy-start.10 = (bf16[2048,1024]{1,0:T(8,128)(2,1)S(1)}, bf16[2048,1024]{1,0:T(8,128)(2,1)}, u32[]{:S(2)}) copy-start(bf16[2048,1024]{1,0:T(8,128)(2,1)} %weight_ref.1) | copy-start | bytes 12582916
  10.8 23.9 %copy-start.1 = (bf16[768,2048]{1,0:T(8,128)(2,1)S(1)}, bf16[768,2048]{1,0:T(8,128)(2,1)}, u32[]{:S(2)}) copy-start(bf16[768,2048]{1,0:T(8,128)(2,1)} %tokens_ref.7) | copy-start | bytes 9437188
  10.8 23.9 %copy-start.7 = (s32[768,1]{0,1:T(1,128)S(1)}, s32[768,1]{0,1:T(1,128)}, u32[]{:S(2)}) copy-start(s32[768,1]{0,1:T(1,128)} %param.9) | copy-start | bytes 9220
  16.3 0.9 %copy-start.4 = (bf16[2,768,256]{2,1,0:T(8,128)(2,1)}, bf16[2,768,256]{2,1,0:T(8,128)(2,1)S(1)}, u32[]{:S(2)}) copy-start(bf16[2,768,256]{2,1,0:T(8,128)(2,1)S(1)} %get-tuple-element.9) | copy-start | bytes 2359300
  17.1 29.0 %collective-permute-start.8 = (bf16[2,768,256]{2,1,0:T(8,128)(2,1)}, bf16[2,768,256]{2,1,0:T(8,128)(2,1)}, u32[]{:S(2)}, u32[]{:S(2)}) collective-permute-start(bf16[2,768,256]{2,1,0:T(8,128)(2,1)} %get-tuple-element.10), channel_id=1, source_target_pairs={{0,1},{1,0},{2,3},{3,2},{4,5},{5,4},{6,7},{7,6},{8,9},{9,8},{10,11... | collective-permute-start | bytes 2359304 | tf_op jit(solution)/shard_map/ppermute | solution.py:35
  17.1 9.9 %collective-permute-start.4 = (bf16[1,64,2304]{2,1,0:T(8,128)(2,1)S(1)}, bf16[1,64,2304]{2,1,0:T(8,128)(2,1)}, u32[]{:S(2)}, u32[]{:S(2)}) collective-permute-start(bf16[1,64,2304]{2,1,0:T(8,128)(2,1)S(1)} %pad_maximum_fusion.refs_0_), channel_id=1, source_target_pairs={{0,4},{4,0},{8,12},{12,8},{1,5},{5,1},{9,13},{13,9},{2,6},{6,2},{1... | collective-permute-start | bytes 884744 | tf_op jit(solution)/shard_map/ppermute | solution.py:35
  20.1 12.9 %collective-permute-start.1 = (bf16[1,64,2304]{2,1,0:T(8,128)(2,1)}, bf16[1,64,2304]{2,1,0:T(8,128)(2,1)}, u32[]{:S(2)}, u32[]{:S(2)}) collective-permute-start(bf16[1,64,2304]{2,1,0:T(8,128)(2,1)} %collective-permute-done.refs_2_), channel_id=1, source_target_pairs={{0,4},{4,0},{8,12},{12,8},{1,5},{5,1},{9,13},{13,9},{2,6},{6,2},{1... | collective-permute-start | bytes 884744 | tf_op jit(solution)/shard_map/ppermute | solution.py:35
  22.5 15.3 %collective-permute-start.3 = (bf16[1,64,2304]{2,1,0:T(8,128)(2,1)}, bf16[1,64,2304]{2,1,0:T(8,128)(2,1)}, u32[]{:S(2)}, u32[]{:S(2)}) collective-permute-start(bf16[1,64,2304]{2,1,0:T(8,128)(2,1)} %collective-permute-done.refs_2_), channel_id=1, source_target_pairs={{0,16},{16,0},{1,17},{17,1},{2,18},{18,2},{3,19},{19,3},{4,20},{20... | collective-permute-start | bytes 884744 | tf_op jit(solution)/shard_map/ppermute | solution.py:35
  27.1 12.0 %collective-permute-start.5 = (bf16[1,64,2304]{2,1,0:T(8,128)(2,1)}, bf16[1,64,2304]{2,1,0:T(8,128)(2,1)}, u32[]{:S(2)}, u32[]{:S(2)}) collective-permute-start(bf16[1,64,2304]{2,1,0:T(8,128)(2,1)} %collective-permute-done.4.refs_3_), channel_id=1, source_target_pairs={{0,16},{16,0},{1,17},{17,1},{2,18},{18,2},{3,19},{19,3},{4,20},{20... | collective-permute-start | bytes 884744 | tf_op jit(solution)/shard_map/ppermute | solution.py:35
  33.0 11.1 %collective-permute-start.2 = (bf16[1,64,2304]{2,1,0:T(8,128)(2,1)}, bf16[1,64,2304]{2,1,0:T(8,128)(2,1)}, u32[]{:S(2)}, u32[]{:S(2)}) collective-permute-start(bf16[1,64,2304]{2,1,0:T(8,128)(2,1)} %collective-permute-done.1.refs_0_.refs_4_), channel_id=1, source_target_pairs={{0,16},{16,0},{1,17},{17,1},{2,18},{18,2},{3,19},{19,3},{4,20},{20... | collective-permute-start | bytes 884744 | tf_op jit(solution)/shard_map/ppermute | solution.py:35
  34.7 1.0 %copy-start.2 = (bf16[1,64,2304]{2,1,0:T(8,128)(2,1)S(1)}, bf16[1,64,2304]{2,1,0:T(8,128)(2,1)}, u32[]{:S(2)}) copy-start(bf16[1,64,2304]{2,1,0:T(8,128)(2,1)} %pad_maximum_fusion.1.refs_1_) | copy-start | bytes 884740
  37.7 8.5 %copy-start.5 = (bf16[2,768,256]{2,1,0:T(8,128)(2,1)S(1)}, bf16[2,768,256]{2,1,0:T(8,128)(2,1)}, u32[]{:S(2)}) copy-start(bf16[2,768,256]{2,1,0:T(8,128)(2,1)} %copy-done.4) | copy-start | bytes 2359300
  41.4 10.9 %copy-start.6 = (bf16[128,128]{1,0:T(8,128)(2,1)S(1)}, bf16[128,128]{1,0:T(8,128)(2,1)}, u32[]{:S(2)}) copy-start(bf16[128,128]{1,0:T(8,128)(2,1)} %constant.23.clone.refs_5_.matrix_ref) | copy-start | bytes 98308
  41.4 10.9 %copy-start.8 = (s32[128]{0:T(128)S(1)}, s32[128]{0:T(128)}, u32[]{:S(2)}) copy-start(s32[128]{0:T(128)} %param.14) | copy-start | bytes 1540
  44.0 16.1 %copy-start.9 = (f32[256]{0:T(256)S(1)}, f32[256]{0:T(256)}, u32[]{:S(2)}) copy-start(f32[256]{0:T(256)} %param.11) | copy-start | bytes 3076
  46.1 3.4 %collective-permute-start.6 = (bf16[64,768]{1,0:T(8,128)(2,1)S(1)}, bf16[64,768]{1,0:T(8,128)(2,1)S(1)}, u32[]{:S(2)}, u32[]{:S(2)}) collective-permute-start(bf16[64,768]{1,0:T(8,128)(2,1)S(1)} %low_rows.5), channel_id=1, source_target_pairs={{0,1},{1,0},{2,3},{3,2},{4,5},{5,4},{6,7},{7,6},{8,9},{9,8},{10,11... | collective-permute-start | bytes 294920 | tf_op jit(solution)/shard_map/ppermute | solution.py:35
  48.0 12.1 %collective-permute-start.9 = (bf16[1,768,256]{2,1,0:T(8,128)(2,1)}, bf16[1,768,256]{2,1,0:T(8,128)(2,1)S(1)}, u32[]{:S(2)}, u32[]{:S(2)}) collective-permute-start(bf16[1,768,256]{2,1,0:T(8,128)(2,1)} %add_convert_fusion), channel_id=1, source_target_pairs={{0,2},{1,3},{2,0},{3,1},{4,6},{5,7},{6,4},{7,5},{8,10},{9,11},{10,... | collective-permute-start | bytes 1179656 | tf_op jit(solution)/shard_map/ppermute | solution.py:35
  49.6 12.3 %collective-permute-start.7 = (bf16[64,768]{1,0:T(8,128)(2,1)S(1)}, bf16[64,768]{1,0:T(8,128)(2,1)S(1)}, u32[]{:S(2)}, u32[]{:S(2)}) collective-permute-start(bf16[64,768]{1,0:T(8,128)(2,1)S(1)} %add_convert_fusion.1.mine_ref), channel_id=1, source_target_pairs={{0,2},{1,3},{2,0},{3,1},{4,6},{5,7},{6,4},{7,5},{8,10},{9,11},{10,... | collective-permute-start | bytes 294920 | tf_op jit(solution)/shard_map/ppermute | solution.py:35
  52.3 1.0 %copy-start.3 = (bf16[1,64,2304]{2,1,0:T(8,128)(2,1)S(1)}, bf16[1,64,2304]{2,1,0:T(8,128)(2,1)}, u32[]{:S(2)}) copy-start(bf16[1,64,2304]{2,1,0:T(8,128)(2,1)} %pad_maximum_fusion.1.refs_1_) | copy-start | bytes 884740

commit v3 on v2

v3 whole, which is shorter than its diff:
```python
import functools

import jax
import jax.numpy as jnp
import numpy as np
from jax import lax
from jax.experimental import pallas as pl
from jax.experimental.pallas import tpu as pltpu
from jax.sharding import PartitionSpec as P

VMEM = pl.BlockSpec(memory_space=pltpu.VMEM)
SMEM = pl.BlockSpec(memory_space=pltpu.SMEM)
F32, BF16 = jnp.float32, jnp.bfloat16
LAST = (((1,), (1,)), ((), ()))


def params(mib):
    return pltpu.CompilerParams(vmem_limit_bytes=mib << 20)


COST = pl.CostEstimate(flops=1, bytes_accessed=1, transcendentals=0)


def hadamard(size):
    index = np.arange(size)
    shared = index[:, None] & index[None, :]
    parity = np.zeros_like(shared)
    while shared.any():
        parity, shared = parity ^ (shared & 1), shared >> 1
    return jnp.asarray(1 - 2 * parity, BF16)


def swap(x, axis, bit):
    return lax.ppermute(x, axis, [(i, i ^ bit) for i in range(lax.axis_size(axis))])


def after(value, *others):
    return lax.optimization_barrier((value, *others))[0]


def rotate(value, signs, matrix):
    head = matrix.shape[0]
    scale = signs * (1.0 / np.sqrt(head))
    turned = []
    for at in range(0, value.shape[1], head):
        signed = value[:, at : at + head] * scale
        high = signed.astype(BF16)
        rest = (signed - high.astype(F32)).astype(BF16)
        turned.append(
            jnp.dot(high, matrix, preferred_element_type=F32) + jnp.dot(rest, matrix, preferred_element_type=F32)
        )
    return turned


def pack_kernel(g_ref, down_ref, up_ref, out_ref):
    features = down_ref.shape[2]
    out_ref[:, :, :features] = down_ref[...]
    out_ref[:, :, features:] = up_ref[...]


def packed(g, down, up, share):
    _, rank, features = down.shape
    width = up.shape[2]
    return pl.pallas_call(
        pack_kernel,
        grid_spec=pltpu.PrefetchScalarGridSpec(
            num_scalar_prefetch=1,
            grid=(1,),
            in_specs=[
                pl.BlockSpec((share, rank, features), lambda i, g: (g[0], 0, 0)),
                pl.BlockSpec((share, rank, width), lambda i, g: (g[0], 0, 0)),
            ],
            out_specs=pl.BlockSpec((share, rank, features + width), lambda i, g: (0, 0, 0)),
        ),
        out_shape=jax.ShapeDtypeStruct((share, rank, features + width), BF16),
        compiler_params=params(8),
        cost_estimate=COST,
        name="packed",
    )(g, down, up)


def partial_kernel(me_ref, tokens_ref, weight_ref, give_ref, keep_ref):
    parts = 2 * give_ref.shape[0]
    width = give_ref.shape[2]
    for offset in range(parts):
        at = pl.multiple_of(jnp.bitwise_xor(me_ref[0], offset) * width, 128)
        product = jnp.dot(tokens_ref[...], weight_ref[:, pl.ds(at, width)], preferred_element_type=F32)
        (give_ref if offset % 2 else keep_ref)[offset // 2] = product.astype(BF16)


def partials(me, tokens, weight, parts):
    width = weight.shape[1] // parts
    block = jax.ShapeDtypeStruct((parts // 2, tokens.shape[0], width), BF16)
    return pl.pallas_call(
        partial_kernel,
        in_specs=[SMEM, VMEM, VMEM],
        out_specs=[VMEM, VMEM],
        out_shape=[block, block],
        compiler_params=params(24),
        cost_estimate=COST,
        name="partials",
    )(me, tokens, weight)


def add_kernel(*refs):
    total = refs[0][...].astype(F32)
    for term in refs[1:-1]:
        total = total + term[...].astype(F32)
    refs[-1][...] = total.astype(BF16)


def sum_blocks(keep, came):
    stage = len(came)
    _, rows, width = keep.shape
    count = keep.shape[0] >> stage

    def every(power):
        return pl.BlockSpec((1, rows, width), lambda j: ((2 * j + 1) << power, 0, 0))

    return pl.pallas_call(
        add_kernel,
        grid=(count,),
        in_specs=[every(stage - 1)] + [every(stage - 1 - r) for r in range(stage)],
        out_specs=pl.BlockSpec((1, rows, width), lambda j: (j, 0, 0)),
        out_shape=jax.ShapeDtypeStruct((count, rows, width), BF16),
        compiler_params=params(8),
        cost_estimate=COST,
        name="sum_blocks",
    )(keep, *came)


def base_kernel(*refs):
    terms, (scale_ref, bits_ref, matrix_ref, out_ref) = refs[:-4], refs[-4:]
    total = terms[0][0].astype(F32)
    for term in terms[1:]:
        total = total + term[0].astype(F32)
    signs = (1 - 2 * bits_ref[...]).astype(F32)
    turned = rotate(total * scale_ref[...], signs, matrix_ref[...])
    out_ref[...] = jnp.concatenate(turned, axis=1)


def rotated_base(terms, scale, bits, matrix):
    _, rows, width = terms[0].shape
    first = pl.BlockSpec((1, rows, width), lambda i: (0, 0, 0))
    whole = lambda shape: pl.BlockSpec(shape, lambda i: (0,) * len(shape))
    return pl.pallas_call(
        base_kernel,
        grid=(1,),
        in_specs=[first] * len(terms) + [whole(a.shape) for a in (scale, bits, matrix)],
        out_specs=whole((rows, width)),
        out_shape=jax.ShapeDtypeStruct((rows, width), F32),
        compiler_params=params(16),
        cost_estimate=COST,
        name="rotated_base",
    )(*terms, scale, bits, matrix)


def adapter(at_ref, here, share, name):
    if name[0] == "home":
        return at_ref[0] * here + name[1]
    plane, off, k = name
    return jnp.bitwise_xor(at_ref[0], plane) * here + jnp.bitwise_xor(at_ref[1], off) * share + k


def low_kernel(groups, here, share, rank, more, at_ref, ids_ref, tokens_ref, *refs):
    out_ref = refs[-1]
    total = refs[-2][...] if more else None
    for (start, stop), terms in groups:
        rows = [refs[i][k, :, cut : cut + stop - start] for i, k, cut, _ in terms]
        joined = rows[0] if len(rows) == 1 else jnp.concatenate(rows, axis=0)
        product = lax.dot_general(joined, tokens_ref[:, start:stop], LAST, preferred_element_type=F32)
        for n, (_, _, _, name) in enumerate(terms):
            mine = ids_ref[...] == adapter(at_ref, here, share, name)
            term = jnp.where(mine, product[n * rank : (n + 1) * rank], 0.0)
            total = term if total is None else total + term
    out_ref[...] = total.astype(out_ref.dtype)


def low_rows(at, ids, tokens, here, share, groups, arrays, before, dtype):
    rank = arrays[0].shape[1]
    more = [] if before is None else [before]
    return pl.pallas_call(
        functools.partial(low_kernel, groups, here, share, rank, bool(more)),
        in_specs=[SMEM] + [VMEM] * (2 + len(arrays) + len(more)),
        out_specs=VMEM,
        out_shape=jax.ShapeDtypeStruct((rank, tokens.shape[0]), dtype),
        compiler_params=params(24),
        cost_estimate=COST,
        name="low_rows",
    )(at, ids, tokens, *arrays, *more)


def ups_kernel(terms, here, share, rank, at_ref, ids_ref, bits_ref, matrix_ref, *refs):
    up_ref, mask_ref = refs[-2:]
    width = up_ref.shape[1]
    signs = (1 - 2 * bits_ref[...]).astype(F32)
    ids = jnp.broadcast_to(ids_ref[...], (rank, ids_ref.shape[1])).T
    for n, (i, k, cut, name) in enumerate(terms):
        turned = rotate(refs[i][k, :, cut : cut + width].astype(F32), signs, matrix_ref[...])
        up_ref[n * rank : (n + 1) * rank, :] = jnp.concatenate(turned, axis=1).astype(BF16)
        mine = ids == adapter(at_ref, here, share, name)
        mask_ref[:, n * rank : (n + 1) * rank] = jnp.where(mine, 1.0, 0.0).astype(BF16)


def rotated_ups(at, ids, bits, matrix, here, share, terms, arrays, width):
    rank, rows = arrays[0].shape[1], ids.shape[1]
    every = len(terms) * rank
    return pl.pallas_call(
        functools.partial(ups_kernel, terms, here, share, rank),
        in_specs=[SMEM] + [VMEM] * (3 + len(arrays)),
        out_specs=[VMEM, VMEM],
        out_shape=[jax.ShapeDtypeStruct((every, width), BF16), jax.ShapeDtypeStruct((rows, every), BF16)],
        compiler_params=params(32),
        cost_estimate=COST,
        name="rotated_ups",
    )(at, ids, bits, matrix, *arrays)


def final_kernel(mine_ref, theirs_ref, base_ref, up_ref, mask_ref, out_ref):
    low = (mine_ref[...].astype(F32) + theirs_ref[...].astype(F32)).T.astype(BF16)
    every = mask_ref.shape[1]
    spread = jnp.concatenate([low] * (every // low.shape[1]), axis=1) * mask_ref[...]
    delta = jnp.dot(spread, up_ref[...], preferred_element_type=F32)
    out_ref[...] = (base_ref[...] + delta).astype(BF16)


def final(mine, theirs, base, up, mask):
    rows, width = base.shape
    return pl.pallas_call(
        final_kernel,
        in_specs=[VMEM] * 5,
        out_specs=VMEM,
        out_shape=jax.ShapeDtypeStruct((rows, width), BF16),
        compiler_params=params(32),
        cost_estimate=COST,
        name="final",
    )(mine, theirs, base, up, mask)


def local(tokens, adapter_ids, base_weight, channel_scale, adapter_down, adapter_up, sign_bits):
    planes, groups, parts = lax.axis_size("adp"), lax.axis_size("grp"), lax.axis_size("tp")
    z, g, me = (lax.axis_index(axis).astype(jnp.int32) for axis in ("adp", "grp", "tp"))
    features = tokens.shape[1]
    here, _, rank = adapter_down.shape
    width = adapter_up.shape[2]
    share = here // groups
    split = (features + width) * 5 // 9 // 128 * 128
    matrix = hadamard(sign_bits.shape[0])
    bits, scale, ids = sign_bits[None, :], channel_scale[None, :], adapter_ids.T
    at = jnp.stack([z, g])
    down = jnp.swapaxes(adapter_down, 1, 2)

    own = packed(g[None], down, adapter_up, share)
    mine = [(0, own)]
    theirs = []
    bit = planes // 2
    while bit > 1:
        new = [(plane | bit, swap(piece, "adp", bit)) for plane, piece in mine]
        theirs += [(plane, off, swap(piece, "grp", off)) for plane, piece in new for off in range(1, groups)]
        mine += new
        bit //= 2
    new = [(plane | 1, swap(piece, "adp", 1)) for plane, piece in mine[:-1]]
    theirs += [(plane, off, swap(piece, "grp", off)) for plane, piece in new for off in range(1, groups)]
    last, piece = mine[-1]
    mine += new
    first = swap(piece[:, :, :split], "adp", 1)
    others = [p for plane, _, p in theirs if plane == last]
    if last == 0:
        others = [packed((g ^ off)[None], down, adapter_up, share) for off in range(1, groups)]
    rest = swap(jnp.concatenate([p[:, :, split:] for p in [piece] + others], axis=0), "adp", 1)
    firsts = [first] + [swap(first, "grp", off) for off in range(1, groups)]

    give, keep = partials(me[None], tokens, base_weight, parts)
    came = [swap(give, "tp", 1)]
    bit = 2
    while bit < parts:
        came.append(swap(sum_blocks(keep, came), "tp", bit))
        bit *= 2
    base = rotated_base([keep] + came, scale, bits, matrix)

    def terms(pieces, start):
        return [(start + i, k, 0, (plane, off, k)) for i, (plane, off, _) in enumerate(pieces) for k in range(share)]

    whole = (0, features)
    early = [(plane, 0, p) for plane, p in mine[1:]]
    home = [(0, k, 0, (0, 0, k)) for k in range(here)]
    first_call = [(whole, [(i, k, cut, ("home", k)) for i, k, cut, _ in home] + terms(early, 1))]
    low = low_rows(at, ids, tokens, here, share, first_call, [down] + [p for *_, p in early], None, F32)
    second = [(whole, terms(theirs, 0)), ((0, split), terms([(last | 1, 0, first)], len(theirs)))]
    low = low_rows(at, ids, tokens, here, share, second, [p for *_, p in theirs] + [first], low, F32)
    swapped = [(last | 1, off, p) for off, p in enumerate(firsts) if off]
    ends = [(len(swapped), off * share + k, 0, (last | 1, off, k)) for off in range(groups) for k in range(share)]
    third = [((0, split), terms(swapped, 0)), ((split, features), ends)]
    low = low_rows(at, ids, tokens, here, share, third, [p for *_, p in swapped] + [rest], low, BF16)
    bit = 1
    while bit < parts // 2:
        low = (low.astype(F32) + swap(low, "tp", bit).astype(F32)).astype(BF16)
        bit *= 2
    other = swap(low, "tp", bit)

    full = early + theirs
    every = [(0, k, 0, ("home", k)) for k in range(here)]
    every += [(1 + i, k, features, (plane, off, k)) for i, (plane, off, _) in enumerate(full) for k in range(share)]
    every += [(1 + len(full), i, features - split, name) for _, i, _, name in ends]
    up, mask = rotated_ups(
        at, ids, bits, matrix, here, share, every, [adapter_up] + [p for *_, p in full] + [rest], width
    )
    return final(low, other, base, up, mask)


def solution(mesh):
    return jax.shard_map(
        local,
        mesh=mesh,
        in_specs=(
            P(("grp", "adp"), "tp"),
            P(("grp", "adp"), None),
            P("tp", None),
            P("tp"),
            P("adp", "tp", None),
            P("adp", None, "tp"),
            P(),
        ),
        out_specs=P(("grp", "adp"), "tp"),
        check_vma=False,
    )
```

time: 63.9 us -> 58.6 us (0.917)
  waiting for transfers between devices: 18.8 us -> 15.6 us
  local copies, waits for them, and re-layouts: 11.6 us -> 8.67 us
  other arithmetic: 3.74 us -> 0.82 us
  starting transfers between devices: 13.1 us -> 15 us
  Pallas kernels: 16 us -> 17.9 us
    ppermute x10 -> x11, waiting for transfers between devices: 18.8 us -> 15.6 us  [swap(): lax.ppermute(x, axis, [(i, i ^ bit) for i in range(lax.axis_size(axis))])]
    dynamic_slice x2 -> x0, local copies, waits for them, and re-layouts: 2.55 us -> none  [own(): lax.dynamic_slice_in_dim(a, at, share, 0)]
    slice x2 -> x3, local copies, waits for them, and re-layouts: 2.05 us -> 0.03 us  [the longest x2 0.02 us: local(): p[:, :, split:]]
    ppermute x10 -> x11, starting transfers between devices: 13.1 us -> 15 us  [swap(): lax.ppermute(x, axis, [(i, i ^ bit) for i in range(lax.axis_size(axis))])]
    another operation x3 -> x1, other arithmetic: 2 us -> 0.07 us  [local(): at = jnp.stack([z, g])]
    pallas_call x6 -> x8, Pallas kernels: 14.5 us -> 16.4 us  [the longest x3 6.92 us: low_rows(): pl.pallas_call(functools.partial(low_kernel, groups, here, share, rank, b...]
    unnamed x22 -> x30, local copies, waits for them, and re-layouts: 6.9 us -> 8.64 us
    concatenate x2 -> x1, other arithmetic: 1.72 us -> 0.72 us  [local(): jnp.concatenate([p[:, :, split:] for p in [piece] + others], axis=0)]
  transfers between devices with their start and end apart: 10 -> 11, of which waited for: 7 -> 6; matrix products, arithmetic and copies ran while one was open for 9% -> 1% of each run, Pallas kernels for 23% -> 27%
where the time goes in v3:
time: 58.6 us; the launch traced here: 58.1 us
  Pallas kernels  17.9 us (31%)
  waiting for transfers between devices  15.6 us (27%)
  starting transfers between devices  15 us (26%)
  local copies, waits for them, and re-layouts  8.67 us (15%)
  other arithmetic  0.82 us (1%)
    ppermute x11, waiting for transfers between devices, swap(): lax.ppermute(x, axis, [(i, i ^ bit) for i in range(lax.axis_size(axis))])  15.6 us
    ppermute x11, starting transfers between devices, swap(): lax.ppermute(x, axis, [(i, i ^ bit) for i in range(lax.axis_size(axis))])  15 us
    unnamed x30, local copies, waits for them, and re-layouts  8.64 us
    pallas_call x3, Pallas kernels, low_rows(): pl.pallas_call(functools.partial(low_kernel, groups, here, share, rank, b...  6.92 us
    pallas_call x1, Pallas kernels, partials(): pl.pallas_call(partial_kernel, in_specs=[SMEM, VMEM, VMEM], out_specs=[VM...  4.36 us
    pallas_call x1, Pallas kernels, rotated_ups(): pl.pallas_call(functools.partial(ups_kernel, terms, here, share, rank), i...  1.79 us
    pallas_call x1, Pallas kernels, rotated_base(): pl.pallas_call(base_kernel, grid=(1,), in_specs=[first] * len(terms) + [w...  1.49 us
    pallas_call x1, Pallas kernels, final(): pl.pallas_call(final_kernel, in_specs=[VMEM] * 5, out_specs=VMEM, out_sha...  1.47 us
  transfers between devices with their start and end apart: 11, of which 6 were waited for; matrix products, arithmetic and copies ran while one was open for 1% of the time, Pallas kernels for 27%

profile of v3, /device:TPU:0, one launch (start us, length us, event | category | flops | bytes accessed | tf_op | source)
XLA Modules:
  0.0 58.1 jit_solution(5504437144653405939)
XLA Ops:
  0.0 1.0 %copy-done.5 = bf16[2,2048,64]{1,2,0:T(8,128)(2,1)S(1)} copy-done((bf16[2,2048,64]{1,2,0:T(8,128)(2,1)S(1)}, bf16[2,2048,64]{1,2,0:T(8,128)(2,1)}, u32[]{:S(2)}) %copy-start.5) | copy-done | bytes 524312
  1.0 0.8 %copy-done.9 = bf16[2,64,256]{2,1,0:T(8,128)(2,1)S(1)} copy-done((bf16[2,64,256]{2,1,0:T(8,128)(2,1)S(1)}, bf16[2,64,256]{2,1,0:T(8,128)(2,1)}, u32[]{:S(2)}) %copy-start.9) | copy-done | bytes 65560
  1.9 0.7 %packed.1 = bf16[1,64,2304]{2,1,0:T(8,128)(2,1)} custom-call(s32[1]{0:T(128)} %bitcast.1.g_ref, bf16[2,64,2048]{2,1,0:T(8,128)(2,1)S(1)} %bitcast.7, bf16[2,64,256]{2,1,0:T(8,128)(2,1)S(1)} %copy-done.9), custom_call_target="tpu_custom_call" | custom-call | flops 1 | bytes 1 | tf_op jit(solution)/shard_map/packed/pallas_call | solution.py:64
  2.6 4.0 %collective-permute-start = (bf16[1,64,2304]{2,1,0:T(8,128)(2,1)}, bf16[1,64,2304]{2,1,0:T(8,128)(2,1)S(1)}, u32[]{:S(2)}, u32[]{:S(2)}) collective-permute-start(bf16[1,64,2304]{2,1,0:T(8,128)(2,1)} %packed.1), channel_id=1, source_target_pairs={{0,8},{4,12},{8,0},{12,4},{1,9},{5,13},{9,1},{13,5},{2,10},{6,14},... | collective-permute-start | bytes 884744 | tf_op jit(solution)/shard_map/ppermute | solution.py:34
  6.7 1.9 %copy-done = bf16[768,2048]{1,0:T(8,128)(2,1)S(1)} copy-done((bf16[768,2048]{1,0:T(8,128)(2,1)S(1)}, bf16[768,2048]{1,0:T(8,128)(2,1)}, u32[]{:S(2)}) %copy-start) | copy-done | bytes 3145752
  8.5 2.2 %copy-done.2 = bf16[2048,1024]{1,0:T(8,128)(2,1)S(1)} copy-done((bf16[2048,1024]{1,0:T(8,128)(2,1)S(1)}, bf16[2048,1024]{1,0:T(8,128)(2,1)}, u32[]{:S(2)}) %copy-start.2) | copy-done | bytes 4194328
  10.7 4.4 %partials.1 = (bf16[2,768,256]{2,1,0:T(8,128)(2,1)}, bf16[2,768,256]{2,1,0:T(8,128)(2,1)S(1)}) custom-call(s32[1]{0:T(128)} %bitcast.4.me_ref, bf16[768,2048]{1,0:T(8,128)(2,1)S(1)} %copy-done, bf16[2048,1024]{1,0:T(8,128)(2,1)S(1)} %copy-done.2), custom_call_target="tpu_custom_call" | custom-call | flops 1 | bytes 1 | tf_op jit(solution)/shard_map/partials/pallas_call | solution.py:94
  15.1 0.9 %copy-done.3 = bf16[2,768,256]{2,1,0:T(8,128)(2,1)} copy-done((bf16[2,768,256]{2,1,0:T(8,128)(2,1)}, bf16[2,768,256]{2,1,0:T(8,128)(2,1)S(1)}, u32[]{:S(2)}) %copy-start.3) | copy-done | bytes 786456
  16.0 1.6 %collective-permute-start.5 = (bf16[1,64,2304]{2,1,0:T(8,128)(2,1)}, bf16[1,64,2304]{2,1,0:T(8,128)(2,1)}, u32[]{:S(2)}, u32[]{:S(2)}) collective-permute-start(bf16[1,64,2304]{2,1,0:T(8,128)(2,1)} %packed.1), channel_id=1, source_target_pairs={{0,4},{4,0},{8,12},{12,8},{1,5},{5,1},{9,13},{13,9},{2,6},{6,2},{1... | collective-permute-start | bytes 884744 | tf_op jit(solution)/shard_map/ppermute | solution.py:34
  17.6 2.7 %collective-permute-done.refs_1_ = bf16[1,64,2304]{2,1,0:T(8,128)(2,1)S(1)} collective-permute-done((bf16[1,64,2304]{2,1,0:T(8,128)(2,1)}, bf16[1,64,2304]{2,1,0:T(8,128)(2,1)S(1)}, u32[]{:S(2)}, u32[]{:S(2)}) %collective-permute-start) | collective-permute-done | bytes 294944 | tf_op jit(solution)/shard_map/ppermute | solution.py:34
  20.3 1.6 %collective-permute-start.3 = (bf16[1,64,2304]{2,1,0:T(8,128)(2,1)S(1)}, bf16[1,64,2304]{2,1,0:T(8,128)(2,1)S(1)}, u32[]{:S(2)}, u32[]{:S(2)}) collective-permute-start(bf16[1,64,2304]{2,1,0:T(8,128)(2,1)S(1)} %collective-permute-done.refs_1_), channel_id=1, source_target_pairs={{0,16},{16,0},{1,17},{17,1},{2,18},{18,2},{3,19},{19,3},{4,20},{20... | collective-permute-start | bytes 884744 | tf_op jit(solution)/shard_map/ppermute | solution.py:34
  21.9 0.8 %collective-permute-start.1 = (bf16[1,64,1280]{2,1,0:T(8,128)(2,1)S(1)}, bf16[1,64,1280]{2,1,0:T(8,128)(2,1)}, u32[]{:S(2)}, u32[]{:S(2)}) collective-permute-start(bf16[1,64,1280]{2,1,0:T(8,128)(2,1)S(1)} %slice.12), channel_id=1, source_target_pairs={{0,4},{4,0},{8,12},{12,8},{1,5},{5,1},{9,13},{13,9},{2,6},{6,2},{1... | collective-permute-start | bytes 491528 | tf_op jit(solution)/shard_map/ppermute | solution.py:34
  22.7 4.0 %collective-permute-done.5.refs_2_ = bf16[1,64,2304]{2,1,0:T(8,128)(2,1)} collective-permute-done((bf16[1,64,2304]{2,1,0:T(8,128)(2,1)}, bf16[1,64,2304]{2,1,0:T(8,128)(2,1)}, u32[]{:S(2)}, u32[]{:S(2)}) %collective-permute-start.5) | collective-permute-done | bytes 294944 | tf_op jit(solution)/shard_map/ppermute | solution.py:34
  26.7 1.6 %collective-permute-start.6 = (bf16[1,64,2304]{2,1,0:T(8,128)(2,1)}, bf16[1,64,2304]{2,1,0:T(8,128)(2,1)}, u32[]{:S(2)}, u32[]{:S(2)}) collective-permute-start(bf16[1,64,2304]{2,1,0:T(8,128)(2,1)} %collective-permute-done.5.refs_2_), channel_id=1, source_target_pairs={{0,16},{16,0},{1,17},{17,1},{2,18},{18,2},{3,19},{19,3},{4,20},{20... | collective-permute-start | bytes 884744 | tf_op jit(solution)/shard_map/ppermute | solution.py:34
  28.2 0.2 collective-permute-done.3.refs_0_.refs_3_
  28.4 0.7 %copy-done.7 = bf16[1,64,2304]{2,1,0:T(8,128)(2,1)} copy-done((bf16[1,64,2304]{2,1,0:T(8,128)(2,1)}, bf16[1,64,2304]{2,1,0:T(8,128)(2,1)S(1)}, u32[]{:S(2)}) %copy-start.7) | copy-done | bytes 294936
  29.1 0.7 %pad_maximum_fusion = bf16[2,64,1024]{2,1,0:T(8,128)(2,1)} fusion(bf16[1,64,1024]{2,1,0:T(8,128)(2,1)S(1)} %slice.14, bf16[1,64,1024]{2,1,0:T(8,128)(2,1)S(1)} %slice.13), kind=kLoop, calls=%fused_computation | loop fusion | flops 131072 | bytes 524288 | tf_op jit(solution)/shard_map/concatenate | solution.py:270
  29.8 1.7 %collective-permute-start.4 = (bf16[2,64,1024]{2,1,0:T(8,128)(2,1)}, bf16[2,64,1024]{2,1,0:T(8,128)(2,1)}, u32[]{:S(2)}, u32[]{:S(2)}) collective-permute-start(bf16[2,64,1024]{2,1,0:T(8,128)(2,1)} %pad_maximum_fusion), channel_id=1, source_target_pairs={{0,4},{4,0},{8,12},{12,8},{1,5},{5,1},{9,13},{13,9},{2,6},{6,2},{1... | collective-permute-start | bytes 786440 | tf_op jit(solution)/shard_map/ppermute | solution.py:34
  31.5 1.5 %collective-permute-start.2 = (bf16[1,64,1280]{2,1,0:T(8,128)(2,1)}, bf16[1,64,1280]{2,1,0:T(8,128)(2,1)}, u32[]{:S(2)}, u32[]{:S(2)}) collective-permute-start(bf16[1,64,1280]{2,1,0:T(8,128)(2,1)} %collective-permute-done.1.refs_2_), channel_id=1, source_target_pairs={{0,16},{16,0},{1,17},{17,1},{2,18},{18,2},{3,19},{19,3},{4,20},{20... | collective-permute-start | bytes 491528 | tf_op jit(solution)/shard_map/ppermute | solution.py:34
  33.1 1.0 %copy-done.6 = bf16[2,2048,64]{1,2,0:T(8,128)(2,1)S(1)} copy-done((bf16[2,2048,64]{1,2,0:T(8,128)(2,1)S(1)}, bf16[2,2048,64]{1,2,0:T(8,128)(2,1)}, u32[]{:S(2)}) %copy-start.6) | copy-done | bytes 524312
  34.2 2.0 %low_rows.3.refs_3_ = f32[64,768]{1,0:T(8,128)S(1)} custom-call(s32[2]{0:T(128)S(1)} %pad_add_fusion.at_ref, s32[1,768]{1,0:T(1,128)S(1)} %bitcast.9, bf16[768,2048]{1,0:T(8,128)(2,1)S(1)} %copy-done.1, bf16[2,64,2048]{2,1,0:T(8,128)(2,1)S(1)} %bitcast.8, bf16[1,64,2304]{2,1,0:T(8,128)(2,1)S(1)} %collective-permute-done.refs_1_, ...), custom_call_target="tpu_custom_call" | custom-call | flops 1 | bytes 1 | tf_op jit(solution)/shard_map/low_rows/pallas_call | solution.py:182
  36.3 0.6 %collective-permute-done.6.refs_1_.refs_4_ = bf16[1,64,2304]{2,1,0:T(8,128)(2,1)} collective-permute-done((bf16[1,64,2304]{2,1,0:T(8,128)(2,1)}, bf16[1,64,2304]{2,1,0:T(8,128)(2,1)}, u32[]{:S(2)}, u32[]{:S(2)}) %collective-permute-start.6) | collective-permute-done | bytes 294944 | tf_op jit(solution)/shard_map/ppermute | solution.py:34
  36.8 2.7 %low_rows.4.refs_2_ = f32[64,768]{1,0:T(8,128)S(1)} custom-call(s32[2]{0:T(128)S(1)} %pad_add_fusion.at_ref, s32[1,768]{1,0:T(1,128)S(1)} %bitcast.10, bf16[768,2048]{1,0:T(8,128)(2,1)S(1)} %copy-done.1, bf16[1,64,2304]{2,1,0:T(8,128)(2,1)S(1)} %copy-done.8, bf16[1,64,2304]{2,1,0:T(8,128)(2,1)} %collective-permute-done.6.refs_1_.refs_4_, ...), custom_call_target="tpu_custom_call" | custom-call | flops 1 | bytes 1 | tf_op jit(solution)/shard_map/low_rows/pallas_call | solution.py:182
  39.6 2.2 %low_rows.5 = bf16[64,768]{1,0:T(8,128)(2,1)S(1)} custom-call(s32[2]{0:T(128)S(1)} %pad_add_fusion.at_ref, s32[1,768]{1,0:T(1,128)S(1)} %bitcast.11, bf16[768,2048]{1,0:T(8,128)(2,1)S(1)} %copy-done.1, bf16[1,64,1280]{2,1,0:T(8,128)(2,1)} %collective-permute-done.2.refs_0_, bf16[2,64,1024]{2,1,0:T(8,128)(2,1)} %collective-permute-done.4.refs_1_.refs_5_, ...), custom_call_target="tpu_custom_call" | custom-call | flops 1 | bytes 1 | tf_op jit(solution)/shard_map/low_rows/pallas_call | solution.py:182
  41.9 1.1 %sum_blocks.1 = bf16[1,768,256]{2,1,0:T(8,128)(2,1)S(1)} custom-call(bf16[2,768,256]{2,1,0:T(8,128)(2,1)S(1)} %copy-done.4, bf16[2,768,256]{2,1,0:T(8,128)(2,1)} %collective-permute-done.9.refs_1_), custom_call_target="tpu_custom_call" | custom-call | flops 1 | bytes 1 | tf_op jit(solution)/shard_map/sum_blocks/pallas_call | solution.py:120
  43.0 1.6 %collective-permute-start.10 = (bf16[1,768,256]{2,1,0:T(8,128)(2,1)S(1)}, bf16[1,768,256]{2,1,0:T(8,128)(2,1)S(1)}, u32[]{:S(2)}, u32[]{:S(2)}) collective-permute-start(bf16[1,768,256]{2,1,0:T(8,128)(2,1)S(1)} %sum_blocks.1), channel_id=1, source_target_pairs={{0,2},{1,3},{2,0},{3,1},{4,6},{5,7},{6,4},{7,5},{8,10},{9,11},{10,... | collective-permute-start | bytes 1179656 | tf_op jit(solution)/shard_map/ppermute | solution.py:34
  44.6 0.6 collective-permute-start.8
  45.2 1.8 %rotated_ups.1 = (bf16[512,256]{1,0:T(8,128)(2,1)S(1)}, bf16[768,512]{1,0:T(8,128)(2,1)S(1)}) custom-call(s32[2]{0:T(128)S(1)} %pad_add_fusion.at_ref, s32[1,768]{1,0:T(1,128)S(1)} %bitcast.12, s32[1,128]{1,0:T(1,128)S(1)} %bitcast.13, bf16[128,128]{1,0:T(8,128)(2,1)S(1)} %copy-done.11, bf16[2,64,256]{2,1,0:T(8,128)(2,1)S(1)} %copy-done.10, ...), custom_call_target="tpu_custom_call" | custom-call | flops 1 | bytes 1 | tf_op jit(solution)/shard_map/rotated_ups/pallas_call | solution.py:208
  47.0 8.0 %collective-permute-done.10.refs_2_ = bf16[1,768,256]{2,1,0:T(8,128)(2,1)S(1)} collective-permute-done((bf16[1,768,256]{2,1,0:T(8,128)(2,1)S(1)}, bf16[1,768,256]{2,1,0:T(8,128)(2,1)S(1)}, u32[]{:S(2)}, u32[]{:S(2)}) %collective-permute-start.10) | collective-permute-done | bytes 393248 | tf_op jit(solution)/shard_map/ppermute | solution.py:34
  55.0 1.5 %rotated_base.1.base_ref = f32[768,256]{1,0:T(8,128)S(1)} custom-call(bf16[2,768,256]{2,1,0:T(8,128)(2,1)S(1)} %copy-done.4, bf16[2,768,256]{2,1,0:T(8,128)(2,1)} %collective-permute-done.9.refs_1_, bf16[1,768,256]{2,1,0:T(8,128)(2,1)S(1)} %collective-permute-done.10.refs_2_, f32[1,256]{1,0:T(1,128)S(1)} %bitcast.15, s32[1,128]{1,0:T(1,128)S(1)} %bitcast.14, ...), custom_call_target="tpu_custom_call" | custom-call | flops 1 | bytes 1 | tf_op jit(solution)/shard_map/rotated_base/pallas_call | solution.py:146
  56.5 0.2 collective-permute-done.8.theirs_ref
  56.7 1.5 %final.1 = bf16[768,256]{1,0:T(8,128)(2,1)} custom-call(bf16[64,768]{1,0:T(8,128)(2,1)S(1)} %add_convert_fusion.mine_ref, bf16[64,768]{1,0:T(8,128)(2,1)S(1)} %collective-permute-done.8.theirs_ref, f32[768,256]{1,0:T(8,128)S(1)} %rotated_base.1.base_ref, bf16[512,256]{1,0:T(8,128)(2,1)S(1)} %get-tuple-element.11.up_ref, ...), custom_call_target="tpu_custom_call" | custom-call | flops 1 | bytes 1 | tf_op jit(solution)/shard_map/final/pallas_call | solution.py:229
  (35 shorter events, 0.3 us)
Async XLA Ops:
  0.0 1.0 %copy-start.5 = (bf16[2,2048,64]{1,2,0:T(8,128)(2,1)S(1)}, bf16[2,2048,64]{1,2,0:T(8,128)(2,1)}, u32[]{:S(2)}) copy-start(bf16[2,2048,64]{1,2,0:T(8,128)(2,1)} %param.12) | copy-start | bytes 1572868
  1.0 0.8 %copy-start.9 = (bf16[2,64,256]{2,1,0:T(8,128)(2,1)S(1)}, bf16[2,64,256]{2,1,0:T(8,128)(2,1)}, u32[]{:S(2)}) copy-start(bf16[2,64,256]{2,1,0:T(8,128)(2,1)} %refs_0_.1) | copy-start | bytes 196612
  2.6 17.7 %collective-permute-start = (bf16[1,64,2304]{2,1,0:T(8,128)(2,1)}, bf16[1,64,2304]{2,1,0:T(8,128)(2,1)S(1)}, u32[]{:S(2)}, u32[]{:S(2)}) collective-permute-start(bf16[1,64,2304]{2,1,0:T(8,128)(2,1)} %packed.1), channel_id=1, source_target_pairs={{0,8},{4,12},{8,0},{12,4},{1,9},{5,13},{9,1},{13,5},{2,10},{6,14},... | collective-permute-start | bytes 884744 | tf_op jit(solution)/shard_map/ppermute | solution.py:34
  6.7 1.9 %copy-start = (bf16[768,2048]{1,0:T(8,128)(2,1)S(1)}, bf16[768,2048]{1,0:T(8,128)(2,1)}, u32[]{:S(2)}) copy-start(bf16[768,2048]{1,0:T(8,128)(2,1)} %tokens_ref.7) | copy-start | bytes 9437188
  8.5 2.2 %copy-start.2 = (bf16[2048,1024]{1,0:T(8,128)(2,1)S(1)}, bf16[2048,1024]{1,0:T(8,128)(2,1)}, u32[]{:S(2)}) copy-start(bf16[2048,1024]{1,0:T(8,128)(2,1)} %weight_ref.1) | copy-start | bytes 12582916
  10.7 22.4 %copy-start.1 = (bf16[768,2048]{1,0:T(8,128)(2,1)S(1)}, bf16[768,2048]{1,0:T(8,128)(2,1)}, u32[]{:S(2)}) copy-start(bf16[768,2048]{1,0:T(8,128)(2,1)} %tokens_ref.7) | copy-start | bytes 9437188
  10.7 22.4 %copy-start.12 = (s32[768,1]{0,1:T(1,128)S(1)}, s32[768,1]{0,1:T(1,128)}, u32[]{:S(2)}) copy-start(s32[768,1]{0,1:T(1,128)} %param.9) | copy-start | bytes 9220
  15.1 0.9 %copy-start.3 = (bf16[2,768,256]{2,1,0:T(8,128)(2,1)}, bf16[2,768,256]{2,1,0:T(8,128)(2,1)S(1)}, u32[]{:S(2)}) copy-start(bf16[2,768,256]{2,1,0:T(8,128)(2,1)S(1)} %get-tuple-element.9.refs_0_) | copy-start | bytes 2359300
  16.0 25.9 %collective-permute-start.9 = (bf16[2,768,256]{2,1,0:T(8,128)(2,1)}, bf16[2,768,256]{2,1,0:T(8,128)(2,1)}, u32[]{:S(2)}, u32[]{:S(2)}) collective-permute-start(bf16[2,768,256]{2,1,0:T(8,128)(2,1)} %get-tuple-element.10), channel_id=1, source_target_pairs={{0,1},{1,0},{2,3},{3,2},{4,5},{5,4},{6,7},{7,6},{8,9},{9,8},{10,11... | collective-permute-start | bytes 2359304 | tf_op jit(solution)/shard_map/ppermute | solution.py:34
  16.0 10.7 %collective-permute-start.5 = (bf16[1,64,2304]{2,1,0:T(8,128)(2,1)}, bf16[1,64,2304]{2,1,0:T(8,128)(2,1)}, u32[]{:S(2)}, u32[]{:S(2)}) collective-permute-start(bf16[1,64,2304]{2,1,0:T(8,128)(2,1)} %packed.1), channel_id=1, source_target_pairs={{0,4},{4,0},{8,12},{12,8},{1,5},{5,1},{9,13},{13,9},{2,6},{6,2},{1... | collective-permute-start | bytes 884744 | tf_op jit(solution)/shard_map/ppermute | solution.py:34
  20.3 8.1 %collective-permute-start.3 = (bf16[1,64,2304]{2,1,0:T(8,128)(2,1)S(1)}, bf16[1,64,2304]{2,1,0:T(8,128)(2,1)S(1)}, u32[]{:S(2)}, u32[]{:S(2)}) collective-permute-start(bf16[1,64,2304]{2,1,0:T(8,128)(2,1)S(1)} %collective-permute-done.refs_1_), channel_id=1, source_target_pairs={{0,16},{16,0},{1,17},{17,1},{2,18},{18,2},{3,19},{19,3},{4,20},{20... | collective-permute-start | bytes 884744 | tf_op jit(solution)/shard_map/ppermute | solution.py:34
  21.9 9.7 %collective-permute-start.1 = (bf16[1,64,1280]{2,1,0:T(8,128)(2,1)S(1)}, bf16[1,64,1280]{2,1,0:T(8,128)(2,1)}, u32[]{:S(2)}, u32[]{:S(2)}) collective-permute-start(bf16[1,64,1280]{2,1,0:T(8,128)(2,1)S(1)} %slice.12), channel_id=1, source_target_pairs={{0,4},{4,0},{8,12},{12,8},{1,5},{5,1},{9,13},{13,9},{2,6},{6,2},{1... | collective-permute-start | bytes 491528 | tf_op jit(solution)/shard_map/ppermute | solution.py:34
  26.7 10.2 %collective-permute-start.6 = (bf16[1,64,2304]{2,1,0:T(8,128)(2,1)}, bf16[1,64,2304]{2,1,0:T(8,128)(2,1)}, u32[]{:S(2)}, u32[]{:S(2)}) collective-permute-start(bf16[1,64,2304]{2,1,0:T(8,128)(2,1)} %collective-permute-done.5.refs_2_), channel_id=1, source_target_pairs={{0,16},{16,0},{1,17},{17,1},{2,18},{18,2},{3,19},{19,3},{4,20},{20... | collective-permute-start | bytes 884744 | tf_op jit(solution)/shard_map/ppermute | solution.py:34
  28.4 0.7 %copy-start.7 = (bf16[1,64,2304]{2,1,0:T(8,128)(2,1)}, bf16[1,64,2304]{2,1,0:T(8,128)(2,1)S(1)}, u32[]{:S(2)}) copy-start(bf16[1,64,2304]{2,1,0:T(8,128)(2,1)S(1)} %collective-permute-done.3.refs_0_.refs_3_) | copy-start | bytes 884740
  29.8 9.8 %collective-permute-start.4 = (bf16[2,64,1024]{2,1,0:T(8,128)(2,1)}, bf16[2,64,1024]{2,1,0:T(8,128)(2,1)}, u32[]{:S(2)}, u32[]{:S(2)}) collective-permute-start(bf16[2,64,1024]{2,1,0:T(8,128)(2,1)} %pad_maximum_fusion), channel_id=1, source_target_pairs={{0,4},{4,0},{8,12},{12,8},{1,5},{5,1},{9,13},{13,9},{2,6},{6,2},{1... | collective-permute-start | bytes 786440 | tf_op jit(solution)/shard_map/ppermute | solution.py:34
  31.5 8.1 %collective-permute-start.2 = (bf16[1,64,1280]{2,1,0:T(8,128)(2,1)}, bf16[1,64,1280]{2,1,0:T(8,128)(2,1)}, u32[]{:S(2)}, u32[]{:S(2)}) collective-permute-start(bf16[1,64,1280]{2,1,0:T(8,128)(2,1)} %collective-permute-done.1.refs_2_), channel_id=1, source_target_pairs={{0,16},{16,0},{1,17},{17,1},{2,18},{18,2},{3,19},{19,3},{4,20},{20... | collective-permute-start | bytes 491528 | tf_op jit(solution)/shard_map/ppermute | solution.py:34
  33.1 1.0 %copy-start.6 = (bf16[2,2048,64]{1,2,0:T(8,128)(2,1)S(1)}, bf16[2,2048,64]{1,2,0:T(8,128)(2,1)}, u32[]{:S(2)}) copy-start(bf16[2,2048,64]{1,2,0:T(8,128)(2,1)} %param.12) | copy-start | bytes 1572868
  34.2 2.7 %copy-start.8 = (bf16[1,64,2304]{2,1,0:T(8,128)(2,1)S(1)}, bf16[1,64,2304]{2,1,0:T(8,128)(2,1)}, u32[]{:S(2)}) copy-start(bf16[1,64,2304]{2,1,0:T(8,128)(2,1)} %copy-done.7) | copy-start | bytes 884740
  36.2 5.7 %copy-start.4 = (bf16[2,768,256]{2,1,0:T(8,128)(2,1)S(1)}, bf16[2,768,256]{2,1,0:T(8,128)(2,1)}, u32[]{:S(2)}) copy-start(bf16[2,768,256]{2,1,0:T(8,128)(2,1)} %copy-done.3) | copy-start | bytes 2359300
  36.2 9.0 %copy-start.10 = (bf16[2,64,256]{2,1,0:T(8,128)(2,1)S(1)}, bf16[2,64,256]{2,1,0:T(8,128)(2,1)}, u32[]{:S(2)}) copy-start(bf16[2,64,256]{2,1,0:T(8,128)(2,1)} %refs_0_.1) | copy-start | bytes 196612
  36.2 9.0 %copy-start.11 = (bf16[128,128]{1,0:T(8,128)(2,1)S(1)}, bf16[128,128]{1,0:T(8,128)(2,1)}, u32[]{:S(2)}) copy-start(bf16[128,128]{1,0:T(8,128)(2,1)} %constant.15.clone.refs_5_.matrix_ref) | copy-start | bytes 98308
  36.2 8.9 %copy-start.13 = (s32[128]{0:T(128)S(1)}, s32[128]{0:T(128)}, u32[]{:S(2)}) copy-start(s32[128]{0:T(128)} %param.14) | copy-start | bytes 1540
  39.6 15.4 %copy-start.14 = (f32[256]{0:T(256)S(1)}, f32[256]{0:T(256)}, u32[]{:S(2)}) copy-start(f32[256]{0:T(256)} %param.11) | copy-start | bytes 3076
  41.8 2.8 %collective-permute-start.7 = (bf16[64,768]{1,0:T(8,128)(2,1)S(1)}, bf16[64,768]{1,0:T(8,128)(2,1)S(1)}, u32[]{:S(2)}, u32[]{:S(2)}) collective-permute-start(bf16[64,768]{1,0:T(8,128)(2,1)S(1)} %low_rows.5), channel_id=1, source_target_pairs={{0,1},{1,0},{2,3},{3,2},{4,5},{5,4},{6,7},{7,6},{8,9},{9,8},{10,11... | collective-permute-start | bytes 294920 | tf_op jit(solution)/shard_map/ppermute | solution.py:34
  43.0 12.0 %collective-permute-start.10 = (bf16[1,768,256]{2,1,0:T(8,128)(2,1)S(1)}, bf16[1,768,256]{2,1,0:T(8,128)(2,1)S(1)}, u32[]{:S(2)}, u32[]{:S(2)}) collective-permute-start(bf16[1,768,256]{2,1,0:T(8,128)(2,1)S(1)} %sum_blocks.1), channel_id=1, source_target_pairs={{0,2},{1,3},{2,0},{3,1},{4,6},{5,7},{6,4},{7,5},{8,10},{9,11},{10,... | collective-permute-start | bytes 1179656 | tf_op jit(solution)/shard_map/ppermute | solution.py:34
  44.6 12.0 %collective-permute-start.8 = (bf16[64,768]{1,0:T(8,128)(2,1)S(1)}, bf16[64,768]{1,0:T(8,128)(2,1)S(1)}, u32[]{:S(2)}, u32[]{:S(2)}) collective-permute-start(bf16[64,768]{1,0:T(8,128)(2,1)S(1)} %add_convert_fusion.mine_ref), channel_id=1, source_target_pairs={{0,2},{1,3},{2,0},{3,1},{4,6},{5,7},{6,4},{7,5},{8,10},{9,11},{10,... | collective-permute-start | bytes 294920 | tf_op jit(solution)/shard_map/ppermute | solution.py:34

commit v4 on v3

v4 whole, which is shorter than its diff:
```python
import functools

import jax
import jax.numpy as jnp
import numpy as np
from jax import lax
from jax.experimental import pallas as pl
from jax.experimental.pallas import tpu as pltpu
from jax.sharding import PartitionSpec as P

VMEM = pl.BlockSpec(memory_space=pltpu.VMEM)
SMEM = pl.BlockSpec(memory_space=pltpu.SMEM)
F32, BF16 = jnp.float32, jnp.bfloat16
LAST = (((1,), (1,)), ((), ()))


def params(mib):
    return pltpu.CompilerParams(vmem_limit_bytes=mib << 20)


COST = pl.CostEstimate(flops=1, bytes_accessed=1, transcendentals=0)


def hadamard(size):
    index = np.arange(size)
    shared = index[:, None] & index[None, :]
    parity = np.zeros_like(shared)
    while shared.any():
        parity, shared = parity ^ (shared & 1), shared >> 1
    return jnp.asarray(1 - 2 * parity, BF16)


def swap(x, axis, bit):
    return lax.ppermute(x, axis, [(i, i ^ bit) for i in range(lax.axis_size(axis))])


def after(value, *others):
    return lax.optimization_barrier((value, *others))[0]


def rotate(value, signs, matrix):
    head = matrix.shape[0]
    scale = signs * (1.0 / np.sqrt(head))
    turned = []
    for at in range(0, value.shape[1], head):
        signed = value[:, at : at + head] * scale
        high = signed.astype(BF16)
        rest = (signed - high.astype(F32)).astype(BF16)
        turned.append(
            jnp.dot(high, matrix, preferred_element_type=F32) + jnp.dot(rest, matrix, preferred_element_type=F32)
        )
    return turned


def block(ref, index, width):
    return ref[:, pl.ds(pl.multiple_of(index * width, width), width)].astype(F32)


def add_kernel(stage, parts, me_ref, part_ref, pair_ref, *refs):
    out_ref = refs[-1]
    width = part_ref.shape[1] // parts
    for j in range(out_ref.shape[1] // width):
        offset = (2 * j + 1) << stage
        owner = jnp.bitwise_xor(me_ref[0], offset)
        total = block(part_ref, owner, width) + block(pair_ref, owner, width)
        for r, ref in enumerate(refs[:-1], 1):
            total = total + block(ref, offset >> (r + 1), width)
        out_ref[:, j * width : (j + 1) * width] = total.astype(BF16)


def sum_blocks(me, part, pair, came, parts):
    rows, columns = part.shape
    stage = 1 + len(came)
    return pl.pallas_call(
        functools.partial(add_kernel, stage, parts),
        in_specs=[SMEM] + [VMEM] * (2 + len(came)),
        out_specs=VMEM,
        out_shape=jax.ShapeDtypeStruct((rows, columns >> (stage + 1)), BF16),
        compiler_params=params(16),
        cost_estimate=COST,
        name="sum_blocks",
    )(me, part, pair, *came)


def base_kernel(parts, me_ref, part_ref, pair_ref, scale_ref, bits_ref, matrix_ref, *refs):
    out_ref = refs[-1]
    width = out_ref.shape[1]
    total = block(part_ref, me_ref[0], width) + block(pair_ref, me_ref[0], width)
    for ref in refs[:-1]:
        total = total + ref[:, :width].astype(F32)
    signs = (1 - 2 * bits_ref[...]).astype(F32)
    out_ref[...] = jnp.concatenate(rotate(total * scale_ref[...], signs, matrix_ref[...]), axis=1)


def rotated_base(me, part, pair, came, scale, bits, matrix, parts):
    rows, columns = part.shape
    return pl.pallas_call(
        functools.partial(base_kernel, parts),
        in_specs=[SMEM] + [VMEM] * (5 + len(came)),
        out_specs=VMEM,
        out_shape=jax.ShapeDtypeStruct((rows, columns // parts), F32),
        compiler_params=params(16),
        cost_estimate=COST,
        name="rotated_base",
    )(me, part, pair, scale, bits, matrix, *came)


def adapter(at_ref, here, share, name):
    if name[0] == "home":
        return at_ref[0] * here + name[1]
    if name[0] == "plane":
        return jnp.bitwise_xor(at_ref[0], name[1]) * here + name[2]
    plane, off, k = name
    return jnp.bitwise_xor(at_ref[0], plane) * here + jnp.bitwise_xor(at_ref[1], off) * share + k


def low_kernel(groups, here, share, rank, more, at_ref, ids_ref, tokens_ref, *refs):
    out_ref = refs[-1]
    total = refs[-2][...] if more else None
    for (start, stop), terms in groups:
        rows = [refs[i][k, :, cut : cut + stop - start] for i, k, cut, _ in terms]
        joined = rows[0] if len(rows) == 1 else jnp.concatenate(rows, axis=0)
        product = lax.dot_general(joined, tokens_ref[:, start:stop], LAST, preferred_element_type=F32)
        for n, (_, _, _, name) in enumerate(terms):
            mine = ids_ref[...] == adapter(at_ref, here, share, name)
            term = jnp.where(mine, product[n * rank : (n + 1) * rank], 0.0)
            total = term if total is None else total + term
    out_ref[...] = total.astype(out_ref.dtype)


def low_rows(at, ids, tokens, here, share, groups, arrays, before, dtype):
    rank = arrays[0].shape[1]
    more = [] if before is None else [before]
    return pl.pallas_call(
        functools.partial(low_kernel, groups, here, share, rank, bool(more)),
        in_specs=[SMEM] + [VMEM] * (2 + len(arrays) + len(more)),
        out_specs=VMEM,
        out_shape=jax.ShapeDtypeStruct((rank, tokens.shape[0]), dtype),
        compiler_params=params(24),
        cost_estimate=COST,
        name="low_rows",
    )(at, ids, tokens, *arrays, *more)


def ups_kernel(terms, here, share, rank, at_ref, ids_ref, bits_ref, matrix_ref, *refs):
    up_ref, mask_ref = refs[-2:]
    width = up_ref.shape[1]
    signs = (1 - 2 * bits_ref[...]).astype(F32)
    ids = jnp.broadcast_to(ids_ref[...], (rank, ids_ref.shape[1])).T
    for n, (i, k, cut, name) in enumerate(terms):
        turned = rotate(refs[i][k, :, cut : cut + width].astype(F32), signs, matrix_ref[...])
        up_ref[n * rank : (n + 1) * rank, :] = jnp.concatenate(turned, axis=1).astype(BF16)
        mine = ids == adapter(at_ref, here, share, name)
        mask_ref[:, n * rank : (n + 1) * rank] = jnp.where(mine, 1.0, 0.0).astype(BF16)


def rotated_ups(at, ids, bits, matrix, here, share, terms, arrays, width):
    rank, rows = arrays[0].shape[1], ids.shape[1]
    every = len(terms) * rank
    return pl.pallas_call(
        functools.partial(ups_kernel, terms, here, share, rank),
        in_specs=[SMEM] + [VMEM] * (3 + len(arrays)),
        out_specs=[VMEM, VMEM],
        out_shape=[jax.ShapeDtypeStruct((every, width), BF16), jax.ShapeDtypeStruct((rows, every), BF16)],
        compiler_params=params(32),
        cost_estimate=COST,
        name="rotated_ups",
    )(at, ids, bits, matrix, *arrays)


def final_kernel(mine_ref, theirs_ref, base_ref, up_ref, mask_ref, out_ref):
    low = (mine_ref[...].astype(F32) + theirs_ref[...].astype(F32)).T.astype(BF16)
    every = mask_ref.shape[1]
    spread = jnp.concatenate([low] * (every // low.shape[1]), axis=1) * mask_ref[...]
    delta = jnp.dot(spread, up_ref[...], preferred_element_type=F32)
    out_ref[...] = (base_ref[...] + delta).astype(BF16)


def final(mine, theirs, base, up, mask):
    rows, width = base.shape
    return pl.pallas_call(
        final_kernel,
        in_specs=[VMEM] * 5,
        out_specs=VMEM,
        out_shape=jax.ShapeDtypeStruct((rows, width), BF16),
        compiler_params=params(32),
        cost_estimate=COST,
        name="final",
    )(mine, theirs, base, up, mask)


def local(tokens, adapter_ids, base_weight, channel_scale, adapter_down, adapter_up, sign_bits):
    planes, groups, parts = lax.axis_size("adp"), lax.axis_size("grp"), lax.axis_size("tp")
    z, g, me = (lax.axis_index(axis).astype(jnp.int32) for axis in ("adp", "grp", "tp"))
    features = tokens.shape[1]
    here, _, rank = adapter_down.shape
    width = adapter_up.shape[2]
    share = here // groups
    matrix = hadamard(sign_bits.shape[0])
    bits, scale, ids, me = sign_bits[None, :], channel_scale[None, :], adapter_ids.T, me[None]
    at = jnp.stack([z, g])
    down = jnp.swapaxes(adapter_down, 1, 2)

    own = lax.dynamic_slice_in_dim(down, g * share, share, 0)
    part = jnp.dot(tokens, base_weight, preferred_element_type=F32).astype(BF16)
    pair = swap(part, "tp", 1)
    near = swap(own, "adp", 1)
    mine = [(0, own)]
    bit = planes // 2
    while bit > 1:
        mine += [(plane | bit, swap(piece, "adp", bit)) for plane, piece in mine]
        bit //= 2
    came = []
    pair = after(pair, near)
    bit = 2
    while bit < parts:
        came.append(swap(sum_blocks(me, part, pair, came, parts), "tp", bit))
        bit *= 2
    mine = mine[:1] + [(plane, after(piece, pair)) for plane, piece in mine[1:]]
    odd = [(1, after(near, part))] + [(plane | 1, swap(piece, "adp", 1)) for plane, piece in mine[1:]]

    def others(pieces):
        return [(plane, off, swap(piece, "grp", off)) for plane, piece in pieces for off in range(1, groups)]

    swapped = others(odd[:1]) + others(mine[1:]) + others(odd[1:])
    held = [(plane, 0, piece) for plane, piece in odd[:1] + mine[1:] + odd[1:]]

    ups = [(0, adapter_up)]
    bit = planes // 2
    while bit:
        ups += [(plane | bit, swap(after(up, mine[-1][1]), "adp", bit)) for plane, up in ups]
        bit //= 2

    base = rotated_base(me, part, pair, came, scale, bits, matrix, parts)

    def terms(pieces, start):
        return [(start + i, k, 0, (plane, off, k)) for i, (plane, off, _) in enumerate(pieces) for k in range(share)]

    whole = (0, features)
    early = held[: len(mine)] + swapped[:1]
    middle = held[len(mine) :] + swapped[1:-1]
    late = swapped[-1:]
    home = [(0, k, 0, ("home", k)) for k in range(here)]
    low = low_rows(at, ids, tokens, here, share, [(whole, home + terms(early, 1))], [down] + [p for *_, p in early], None, F32)
    low = low_rows(at, ids, tokens, here, share, [(whole, terms(middle, 0))], [p for *_, p in middle], low, F32)
    low = after(low, base)
    low = low_rows(at, ids, tokens, here, share, [(whole, terms(late, 0))], [p for *_, p in late], low, BF16)
    bit = 1
    while bit < parts // 2:
        low = (low.astype(F32) + swap(low, "tp", bit).astype(F32)).astype(BF16)
        bit *= 2
    other = swap(low, "tp", bit)

    every = [(i, k, 0, ("plane", plane, k)) for i, (plane, _) in enumerate(ups) for k in range(here)]
    up, mask = rotated_ups(at, ids, bits, matrix, here, share, every, [up for _, up in ups], width)
    return final(low, other, base, up, mask)


def solution(mesh):
    return jax.shard_map(
        local,
        mesh=mesh,
        in_specs=(
            P(("grp", "adp"), "tp"),
            P(("grp", "adp"), None),
            P("tp", None),
            P("tp"),
            P("adp", "tp", None),
            P("adp", None, "tp"),
            P(),
        ),
        out_specs=P(("grp", "adp"), "tp"),
        check_vma=False,
    )
```

time: 58.6 us -> 67.3 us (1.15)
  waiting for transfers between devices: 15.6 us -> 28.7 us
  matrix products: 0 us -> 7.73 us
  local copies, waits for them, and re-layouts: 8.67 us -> 2.27 us
  Pallas kernels: 17.9 us -> 13.7 us
  other arithmetic: 0.82 us -> 0.1 us
    ppermute x11 -> x13, waiting for transfers between devices: 15.6 us -> 28.7 us  [swap(): lax.ppermute(x, axis, [(i, i ^ bit) for i in range(lax.axis_size(axis))])]
    dot_general x0 -> x1, matrix products: none -> 7.73 us  [local(): part = jnp.dot(tokens, base_weight, preferred_element_type=F32).astype(BF16)]
    unnamed x30 -> x14, local copies, waits for them, and re-layouts: 8.64 us -> 1.08 us
    pallas_call x4 -> x2, Pallas kernels: 7.69 us -> 4.45 us  [the longest x1 2.46 us: rotated_base(): pl.pallas_call(functools.partial(base_kernel, parts), in_specs=[SMEM] + [...]
    dynamic_slice x0 -> x1, local copies, waits for them, and re-layouts: none -> 1.19 us  [local(): own = lax.dynamic_slice_in_dim(down, g * share, share, 0)]
    concatenate x1 -> x0, other arithmetic: 0.72 us -> none  [local(): jnp.concatenate([p[:, :, split:] for p in [piece] + others], axis=0)]
    ppermute x11 -> x13, starting transfers between devices: 15 us -> 14.5 us  [swap(): lax.ppermute(x, axis, [(i, i ^ bit) for i in range(lax.axis_size(axis))])]
  transfers between devices with their start and end apart: 11 -> 13, of which waited for: 6 -> 8; matrix products, arithmetic and copies ran while one was open for 1% -> 2% of each run, Pallas kernels for 27% -> 15%
where the time goes in v4:
time: 67.3 us; the launch traced here: 67.1 us
  waiting for transfers between devices  28.7 us (43%)
  starting transfers between devices  14.5 us (22%)
  Pallas kernels  13.7 us (20%)
  matrix products  7.73 us (11%)
  local copies, waits for them, and re-layouts  2.27 us (3%)
    ppermute x13, waiting for transfers between devices, swap(): lax.ppermute(x, axis, [(i, i ^ bit) for i in range(lax.axis_size(axis))])  28.7 us
    ppermute x13, starting transfers between devices, swap(): lax.ppermute(x, axis, [(i, i ^ bit) for i in range(lax.axis_size(axis))])  14.5 us
    dot_general x1, matrix products, local(): part = jnp.dot(tokens, base_weight, preferred_element_type=F32).astype(BF16)  7.73 us
    pallas_call x3, Pallas kernels, low_rows(): pl.pallas_call(functools.partial(low_kernel, groups, here, share, rank, b...  6.56 us
    pallas_call x1, Pallas kernels, rotated_base(): pl.pallas_call(functools.partial(base_kernel, parts), in_specs=[SMEM] + [...  2.46 us
    pallas_call x1, Pallas kernels, sum_blocks(): pl.pallas_call(functools.partial(add_kernel, stage, parts), in_specs=[SME...  1.99 us
    pallas_call x1, Pallas kernels, final(): pl.pallas_call(final_kernel, in_specs=[VMEM] * 5, out_specs=VMEM, out_sha...  1.45 us
  transfers between devices with their start and end apart: 13, of which 8 were waited for; matrix products, arithmetic and copies ran while one was open for 2% of the time, Pallas kernels for 15%

profile of v4, /device:TPU:0, one launch (start us, length us, event | category | flops | bytes accessed | tf_op | source)
XLA Modules:
  0.0 67.1 jit_solution(18074124678544171051)
XLA Ops:
  0.0 7.7 %convolution_convert_fusion.part_ref = bf16[768,1024]{1,0:T(8,128)(2,1)} fusion(bf16[768,2048]{1,0:T(8,128)(2,1)} %tokens_ref.5, bf16[2048,1024]{1,0:T(8,128)(2,1)} %param.10), kind=kOutput, calls=%fused_computation | convolution fusion | flops 3222011904 | bytes 8912896 | tf_op jit(solution)/shard_map/dot_general | solution.py:205
  7.7 0.5 collective-permute-start.1
  8.2 1.2 %dynamic-slice_bitcast_fusion = bf16[1,64,2048]{2,1,0:T(8,128)(2,1)S(1)} fusion(bf16[2,2048,64]{1,2,0:T(8,128)(2,1)} %param.12, s32[]{:T(128)S(6)} %select_n.3), kind=kLoop, calls=%fused_computation.1 | loop fusion | bytes 524292 | tf_op jit(solution)/shard_map/dynamic_slice | solution.py:204
  9.4 2.6 %collective-permute-start.2 = (bf16[1,64,2048]{2,1,0:T(8,128)(2,1)S(1)}, bf16[1,64,2048]{2,1,0:T(8,128)(2,1)}, u32[]{:S(2)}, u32[]{:S(2)}) collective-permute-start(bf16[1,64,2048]{2,1,0:T(8,128)(2,1)S(1)} %dynamic-slice_bitcast_fusion), channel_id=1, source_target_pairs={{0,4},{4,0},{8,12},{12,8},{1,5},{5,1},{9,13},{13,9},{2,6},{6,2},{1... | collective-permute-start | bytes 786440 | tf_op jit(solution)/shard_map/ppermute | solution.py:34
  12.0 2.6 %collective-permute-start = (bf16[1,64,2048]{2,1,0:T(8,128)(2,1)S(1)}, bf16[1,64,2048]{2,1,0:T(8,128)(2,1)}, u32[]{:S(2)}, u32[]{:S(2)}) collective-permute-start(bf16[1,64,2048]{2,1,0:T(8,128)(2,1)S(1)} %dynamic-slice_bitcast_fusion), channel_id=1, source_target_pairs={{0,8},{4,12},{8,0},{12,4},{1,9},{5,13},{9,1},{13,5},{2,10},{6,14},... | collective-permute-start | bytes 786440 | tf_op jit(solution)/shard_map/ppermute | solution.py:34
  14.5 10.1 %collective-permute-done.2.refs_1_ = bf16[1,64,2048]{2,1,0:T(8,128)(2,1)} collective-permute-done((bf16[1,64,2048]{2,1,0:T(8,128)(2,1)S(1)}, bf16[1,64,2048]{2,1,0:T(8,128)(2,1)}, u32[]{:S(2)}, u32[]{:S(2)}) %collective-permute-start.2) | collective-permute-done | bytes 262176 | tf_op jit(solution)/shard_map/ppermute | solution.py:34
  24.7 2.5 %collective-permute-done.refs_2_ = bf16[1,64,2048]{2,1,0:T(8,128)(2,1)} collective-permute-done((bf16[1,64,2048]{2,1,0:T(8,128)(2,1)S(1)}, bf16[1,64,2048]{2,1,0:T(8,128)(2,1)}, u32[]{:S(2)}, u32[]{:S(2)}) %collective-permute-start) | collective-permute-done | bytes 262176 | tf_op jit(solution)/shard_map/ppermute | solution.py:34
  27.2 0.5 collective-permute-start.3
  27.6 2.0 %sum_blocks.1 = bf16[768,256]{1,0:T(8,128)(2,1)S(1)} custom-call(s32[1]{0:T(128)} %bitcast.5.me_ref, bf16[768,1024]{1,0:T(8,128)(2,1)} %convolution_convert_fusion.part_ref, bf16[768,1024]{1,0:T(8,128)(2,1)} %collective-permute-done.1.pair_ref), custom_call_target="tpu_custom_call" | custom-call | flops 1 | bytes 1 | tf_op jit(solution)/shard_map/sum_blocks/pallas_call | solution.py:74
  29.6 1.6 %collective-permute-start.7 = (bf16[768,256]{1,0:T(8,128)(2,1)S(1)}, bf16[768,256]{1,0:T(8,128)(2,1)}, u32[]{:S(2)}, u32[]{:S(2)}) collective-permute-start(bf16[768,256]{1,0:T(8,128)(2,1)S(1)} %sum_blocks.1), channel_id=1, source_target_pairs={{0,2},{1,3},{2,0},{3,1},{4,6},{5,7},{6,4},{7,5},{8,10},{9,11},{10,... | collective-permute-start | bytes 1179656 | tf_op jit(solution)/shard_map/ppermute | solution.py:34
  31.2 1.5 %collective-permute-start.6 = (bf16[1,64,2048]{2,1,0:T(8,128)(2,1)}, bf16[1,64,2048]{2,1,0:T(8,128)(2,1)}, u32[]{:S(2)}, u32[]{:S(2)}) collective-permute-start(bf16[1,64,2048]{2,1,0:T(8,128)(2,1)} %collective-permute-done.2.refs_1_), channel_id=1, source_target_pairs={{0,16},{16,0},{1,17},{17,1},{2,18},{18,2},{3,19},{19,3},{4,20},{20... | collective-permute-start | bytes 786440 | tf_op jit(solution)/shard_map/ppermute | solution.py:34
  32.7 0.5 collective-permute-start.5
  33.2 0.9 %collective-permute-done.3.refs_0_ = bf16[1,64,2048]{2,1,0:T(8,128)(2,1)} collective-permute-done((bf16[1,64,2048]{2,1,0:T(8,128)(2,1)}, bf16[1,64,2048]{2,1,0:T(8,128)(2,1)}, u32[]{:S(2)}, u32[]{:S(2)}) %collective-permute-start.3) | collective-permute-done | bytes 262176 | tf_op jit(solution)/shard_map/ppermute | solution.py:34
  34.1 1.5 %collective-permute-start.4 = (bf16[1,64,2048]{2,1,0:T(8,128)(2,1)}, bf16[1,64,2048]{2,1,0:T(8,128)(2,1)}, u32[]{:S(2)}, u32[]{:S(2)}) collective-permute-start(bf16[1,64,2048]{2,1,0:T(8,128)(2,1)} %collective-permute-done.3.refs_0_), channel_id=1, source_target_pairs={{0,16},{16,0},{1,17},{17,1},{2,18},{18,2},{3,19},{19,3},{4,20},{20... | collective-permute-start | bytes 786440 | tf_op jit(solution)/shard_map/ppermute | solution.py:34
  35.7 0.1 pad_add_fusion.at_ref
  35.7 5.0 %collective-permute-done.6.refs_3_ = bf16[1,64,2048]{2,1,0:T(8,128)(2,1)} collective-permute-done((bf16[1,64,2048]{2,1,0:T(8,128)(2,1)}, bf16[1,64,2048]{2,1,0:T(8,128)(2,1)}, u32[]{:S(2)}, u32[]{:S(2)}) %collective-permute-start.6) | collective-permute-done | bytes 262176 | tf_op jit(solution)/shard_map/ppermute | solution.py:34
  40.8 1.0 %copy-done.1 = bf16[2,2048,64]{1,2,0:T(8,128)(2,1)S(1)} copy-done((bf16[2,2048,64]{1,2,0:T(8,128)(2,1)S(1)}, bf16[2,2048,64]{1,2,0:T(8,128)(2,1)}, u32[]{:S(2)}) %copy-start.1) | copy-done | bytes 524312
  41.8 2.3 %low_rows.3.refs_2_ = f32[64,768]{1,0:T(8,128)S(1)} custom-call(s32[2]{0:T(128)S(1)} %pad_add_fusion.at_ref, s32[1,768]{1,0:T(1,128)S(1)} %bitcast.12, bf16[768,2048]{1,0:T(8,128)(2,1)S(1)} %copy-done, bf16[2,64,2048]{2,1,0:T(8,128)(2,1)S(1)} %bitcast.11, bf16[1,64,2048]{2,1,0:T(8,128)(2,1)} %collective-permute-done.2.refs_1_, ...), custom_call_target="tpu_custom_call" | custom-call | flops 1 | bytes 1 | tf_op jit(solution)/shard_map/low_rows/pallas_call | solution.py:134
  44.2 0.0 copy-start.2
  44.2 0.0 copy-start.6
  44.2 2.2 %collective-permute-done.5.refs_1_ = bf16[1,64,2048]{2,1,0:T(8,128)(2,1)} collective-permute-done((bf16[1,64,2048]{2,1,0:T(8,128)(2,1)}, bf16[1,64,2048]{2,1,0:T(8,128)(2,1)}, u32[]{:S(2)}, u32[]{:S(2)}) %collective-permute-start.5) | collective-permute-done | bytes 262176 | tf_op jit(solution)/shard_map/ppermute | solution.py:34
  46.4 2.2 %low_rows.4.refs_1_ = f32[64,768]{1,0:T(8,128)S(1)} custom-call(s32[2]{0:T(128)S(1)} %pad_add_fusion.at_ref, s32[1,768]{1,0:T(1,128)S(1)} %bitcast.13, bf16[768,2048]{1,0:T(8,128)(2,1)S(1)} %copy-done, bf16[1,64,2048]{2,1,0:T(8,128)(2,1)} %collective-permute-done.3.refs_0_, bf16[1,64,2048]{2,1,0:T(8,128)(2,1)} %collective-permute-done.5.refs_1_, ...), custom_call_target="tpu_custom_call" | custom-call | flops 1 | bytes 1 | tf_op jit(solution)/shard_map/low_rows/pallas_call | solution.py:134
  48.7 2.5 %rotated_base.1.base_ref = f32[768,256]{1,0:T(8,128)S(1)} custom-call(s32[1]{0:T(128)} %bitcast.5.me_ref, bf16[768,1024]{1,0:T(8,128)(2,1)} %convolution_convert_fusion.part_ref, bf16[768,1024]{1,0:T(8,128)(2,1)} %collective-permute-done.1.pair_ref, f32[1,256]{1,0:T(1,128)S(1)} %bitcast.18, s32[1,128]{1,0:T(1,128)S(1)} %bitcast.16, ...), custom_call_target="tpu_custom_call" | custom-call | flops 1 | bytes 1 | tf_op jit(solution)/shard_map/rotated_base/pallas_call | solution.py:97
  51.1 2.0 %low_rows.5 = bf16[64,768]{1,0:T(8,128)(2,1)S(1)} custom-call(s32[2]{0:T(128)S(1)} %pad_add_fusion.at_ref, s32[1,768]{1,0:T(1,128)S(1)} %bitcast.14, bf16[768,2048]{1,0:T(8,128)(2,1)S(1)} %copy-done, bf16[1,64,2048]{2,1,0:T(8,128)(2,1)} %collective-permute-done.4.refs_0_, f32[64,768]{1,0:T(8,128)S(1)} %low_rows.4.refs_1_), custom_call_target="tpu_custom_call" | custom-call | flops 1 | bytes 1 | tf_op jit(solution)/shard_map/low_rows/pallas_call | solution.py:134
  53.2 0.1 collective-permute-start.8
  53.3 2.6 %collective-permute-start.10 = (bf16[2,64,256]{2,1,0:T(8,128)(2,1)S(1)}, bf16[2,64,256]{2,1,0:T(8,128)(2,1)S(1)}, u32[]{:S(2)}, u32[]{:S(2)}) collective-permute-start(bf16[2,64,256]{2,1,0:T(8,128)(2,1)S(1)} %copy-done.3), channel_id=1, source_target_pairs={{0,8},{4,12},{8,0},{12,4},{1,9},{5,13},{9,1},{13,5},{2,10},{6,14},... | collective-permute-start | bytes 196616 | tf_op jit(solution)/shard_map/ppermute | solution.py:34
  55.9 0.6 collective-permute-start.9
  56.5 3.6 %collective-permute-done.10.refs_1_ = bf16[2,64,256]{2,1,0:T(8,128)(2,1)S(1)} collective-permute-done((bf16[2,64,256]{2,1,0:T(8,128)(2,1)S(1)}, bf16[2,64,256]{2,1,0:T(8,128)(2,1)S(1)}, u32[]{:S(2)}, u32[]{:S(2)}) %collective-permute-start.10) | collective-permute-done | bytes 65568 | tf_op jit(solution)/shard_map/ppermute | solution.py:34
  60.2 0.9 %collective-permute-done.11.refs_2_ = bf16[2,64,256]{2,1,0:T(8,128)(2,1)S(1)} collective-permute-done((bf16[2,64,256]{2,1,0:T(8,128)(2,1)S(1)}, bf16[2,64,256]{2,1,0:T(8,128)(2,1)S(1)}, u32[]{:S(2)}, u32[]{:S(2)}) %collective-permute-start.11) | collective-permute-done | bytes 65568 | tf_op jit(solution)/shard_map/ppermute | solution.py:34
  61.1 3.3 %collective-permute-done.12.refs_3_ = bf16[2,64,256]{2,1,0:T(8,128)(2,1)S(1)} collective-permute-done((bf16[2,64,256]{2,1,0:T(8,128)(2,1)S(1)}, bf16[2,64,256]{2,1,0:T(8,128)(2,1)S(1)}, u32[]{:S(2)}, u32[]{:S(2)}) %collective-permute-start.12) | collective-permute-done | bytes 65568 | tf_op jit(solution)/shard_map/ppermute | solution.py:34
  64.4 1.2 %rotated_ups.1 = (bf16[512,256]{1,0:T(8,128)(2,1)S(1)}, bf16[768,512]{1,0:T(8,128)(2,1)S(1)}) custom-call(s32[2]{0:T(128)S(1)} %pad_add_fusion.at_ref, s32[1,768]{1,0:T(1,128)S(1)} %bitcast.15, s32[1,128]{1,0:T(1,128)S(1)} %bitcast.17, bf16[128,128]{1,0:T(8,128)(2,1)S(1)} %copy-done.2, bf16[2,64,256]{2,1,0:T(8,128)(2,1)S(1)} %copy-done.3, ...), custom_call_target="tpu_custom_call" | custom-call | flops 1 | bytes 1 | tf_op jit(solution)/shard_map/rotated_ups/pallas_call | solution.py:160
  65.6 1.5 %final.1 = bf16[768,256]{1,0:T(8,128)(2,1)} custom-call(bf16[64,768]{1,0:T(8,128)(2,1)S(1)} %add_convert_fusion.mine_ref, bf16[64,768]{1,0:T(8,128)(2,1)S(1)} %collective-permute-done.9.theirs_ref, f32[768,256]{1,0:T(8,128)S(1)} %rotated_base.1.base_ref, bf16[512,256]{1,0:T(8,128)(2,1)S(1)} %get-tuple-element.19.up_ref, ...), custom_call_target="tpu_custom_call" | custom-call | flops 1 | bytes 1 | tf_op jit(solution)/shard_map/final/pallas_call | solution.py:181
  (19 shorter events, 0.1 us)
Async XLA Ops:
  7.7 33.1 %copy-start = (bf16[768,2048]{1,0:T(8,128)(2,1)S(1)}, bf16[768,2048]{1,0:T(8,128)(2,1)}, u32[]{:S(2)}) copy-start(bf16[768,2048]{1,0:T(8,128)(2,1)} %tokens_ref.5) | copy-start | bytes 9437188
  7.7 33.1 %copy-start.4 = (s32[768,1]{0,1:T(1,128)S(1)}, s32[768,1]{0,1:T(1,128)}, u32[]{:S(2)}) copy-start(s32[768,1]{0,1:T(1,128)} %param.9) | copy-start | bytes 9220
  7.7 16.9 %collective-permute-start.1 = (bf16[768,1024]{1,0:T(8,128)(2,1)}, bf16[768,1024]{1,0:T(8,128)(2,1)}, u32[]{:S(2)}, u32[]{:S(2)}) collective-permute-start(bf16[768,1024]{1,0:T(8,128)(2,1)} %convolution_convert_fusion.part_ref), channel_id=1, source_target_pairs={{0,1},{1,0},{2,3},{3,2},{4,5},{5,4},{6,7},{7,6},{8,9},{9,8},{10,11... | collective-permute-start | bytes 4718600 | tf_op jit(solution)/shard_map/ppermute | solution.py:34
  9.4 15.3 %collective-permute-start.2 = (bf16[1,64,2048]{2,1,0:T(8,128)(2,1)S(1)}, bf16[1,64,2048]{2,1,0:T(8,128)(2,1)}, u32[]{:S(2)}, u32[]{:S(2)}) collective-permute-start(bf16[1,64,2048]{2,1,0:T(8,128)(2,1)S(1)} %dynamic-slice_bitcast_fusion), channel_id=1, source_target_pairs={{0,4},{4,0},{8,12},{12,8},{1,5},{5,1},{9,13},{13,9},{2,6},{6,2},{1... | collective-permute-start | bytes 786440 | tf_op jit(solution)/shard_map/ppermute | solution.py:34
  12.0 15.2 %collective-permute-start = (bf16[1,64,2048]{2,1,0:T(8,128)(2,1)S(1)}, bf16[1,64,2048]{2,1,0:T(8,128)(2,1)}, u32[]{:S(2)}, u32[]{:S(2)}) collective-permute-start(bf16[1,64,2048]{2,1,0:T(8,128)(2,1)S(1)} %dynamic-slice_bitcast_fusion), channel_id=1, source_target_pairs={{0,8},{4,12},{8,0},{12,4},{1,9},{5,13},{9,1},{13,5},{2,10},{6,14},... | collective-permute-start | bytes 786440 | tf_op jit(solution)/shard_map/ppermute | solution.py:34
  27.2 7.0 %collective-permute-start.3 = (bf16[1,64,2048]{2,1,0:T(8,128)(2,1)}, bf16[1,64,2048]{2,1,0:T(8,128)(2,1)}, u32[]{:S(2)}, u32[]{:S(2)}) collective-permute-start(bf16[1,64,2048]{2,1,0:T(8,128)(2,1)} %collective-permute-done.refs_2_), channel_id=1, source_target_pairs={{0,4},{4,0},{8,12},{12,8},{1,5},{5,1},{9,13},{13,9},{2,6},{6,2},{1... | collective-permute-start | bytes 786440 | tf_op jit(solution)/shard_map/ppermute | solution.py:34
  29.6 19.0 %collective-permute-start.7 = (bf16[768,256]{1,0:T(8,128)(2,1)S(1)}, bf16[768,256]{1,0:T(8,128)(2,1)}, u32[]{:S(2)}, u32[]{:S(2)}) collective-permute-start(bf16[768,256]{1,0:T(8,128)(2,1)S(1)} %sum_blocks.1), channel_id=1, source_target_pairs={{0,2},{1,3},{2,0},{3,1},{4,6},{5,7},{6,4},{7,5},{8,10},{9,11},{10,... | collective-permute-start | bytes 1179656 | tf_op jit(solution)/shard_map/ppermute | solution.py:34
  31.2 9.6 %collective-permute-start.6 = (bf16[1,64,2048]{2,1,0:T(8,128)(2,1)}, bf16[1,64,2048]{2,1,0:T(8,128)(2,1)}, u32[]{:S(2)}, u32[]{:S(2)}) collective-permute-start(bf16[1,64,2048]{2,1,0:T(8,128)(2,1)} %collective-permute-done.2.refs_1_), channel_id=1, source_target_pairs={{0,16},{16,0},{1,17},{17,1},{2,18},{18,2},{3,19},{19,3},{4,20},{20... | collective-permute-start | bytes 786440 | tf_op jit(solution)/shard_map/ppermute | solution.py:34
  32.7 13.7 %collective-permute-start.5 = (bf16[1,64,2048]{2,1,0:T(8,128)(2,1)}, bf16[1,64,2048]{2,1,0:T(8,128)(2,1)}, u32[]{:S(2)}, u32[]{:S(2)}) collective-permute-start(bf16[1,64,2048]{2,1,0:T(8,128)(2,1)} %collective-permute-done.refs_2_), channel_id=1, source_target_pairs={{0,16},{16,0},{1,17},{17,1},{2,18},{18,2},{3,19},{19,3},{4,20},{20... | collective-permute-start | bytes 786440 | tf_op jit(solution)/shard_map/ppermute | solution.py:34
  34.1 17.0 %collective-permute-start.4 = (bf16[1,64,2048]{2,1,0:T(8,128)(2,1)}, bf16[1,64,2048]{2,1,0:T(8,128)(2,1)}, u32[]{:S(2)}, u32[]{:S(2)}) collective-permute-start(bf16[1,64,2048]{2,1,0:T(8,128)(2,1)} %collective-permute-done.3.refs_0_), channel_id=1, source_target_pairs={{0,16},{16,0},{1,17},{17,1},{2,18},{18,2},{3,19},{19,3},{4,20},{20... | collective-permute-start | bytes 786440 | tf_op jit(solution)/shard_map/ppermute | solution.py:34
  40.8 1.0 %copy-start.1 = (bf16[2,2048,64]{1,2,0:T(8,128)(2,1)S(1)}, bf16[2,2048,64]{1,2,0:T(8,128)(2,1)}, u32[]{:S(2)}) copy-start(bf16[2,2048,64]{1,2,0:T(8,128)(2,1)} %param.12) | copy-start | bytes 1572868
  44.2 4.5 %copy-start.2 = (bf16[128,128]{1,0:T(8,128)(2,1)S(1)}, bf16[128,128]{1,0:T(8,128)(2,1)}, u32[]{:S(2)}) copy-start(bf16[128,128]{1,0:T(8,128)(2,1)} %constant.19.clone.matrix_ref) | copy-start | bytes 98308
  44.2 4.5 %copy-start.5 = (s32[128]{0:T(128)S(1)}, s32[128]{0:T(128)}, u32[]{:S(2)}) copy-start(s32[128]{0:T(128)} %param.14) | copy-start | bytes 1540
  44.2 4.4 %copy-start.6 = (f32[256]{0:T(256)S(1)}, f32[256]{0:T(256)}, u32[]{:S(2)}) copy-start(f32[256]{0:T(256)} %param.11) | copy-start | bytes 3076
  48.6 4.6 %copy-start.3 = (bf16[2,64,256]{2,1,0:T(8,128)(2,1)S(1)}, bf16[2,64,256]{2,1,0:T(8,128)(2,1)}, u32[]{:S(2)}) copy-start(bf16[2,64,256]{2,1,0:T(8,128)(2,1)} %refs_0_.1) | copy-start | bytes 196612
  53.2 2.7 %collective-permute-start.8 = (bf16[64,768]{1,0:T(8,128)(2,1)S(1)}, bf16[64,768]{1,0:T(8,128)(2,1)S(1)}, u32[]{:S(2)}, u32[]{:S(2)}) collective-permute-start(bf16[64,768]{1,0:T(8,128)(2,1)S(1)} %low_rows.5), channel_id=1, source_target_pairs={{0,1},{1,0},{2,3},{3,2},{4,5},{5,4},{6,7},{7,6},{8,9},{9,8},{10,11... | collective-permute-start | bytes 294920 | tf_op jit(solution)/shard_map/ppermute | solution.py:34
  53.3 6.9 %collective-permute-start.10 = (bf16[2,64,256]{2,1,0:T(8,128)(2,1)S(1)}, bf16[2,64,256]{2,1,0:T(8,128)(2,1)S(1)}, u32[]{:S(2)}, u32[]{:S(2)}) collective-permute-start(bf16[2,64,256]{2,1,0:T(8,128)(2,1)S(1)} %copy-done.3), channel_id=1, source_target_pairs={{0,8},{4,12},{8,0},{12,4},{1,9},{5,13},{9,1},{13,5},{2,10},{6,14},... | collective-permute-start | bytes 196616 | tf_op jit(solution)/shard_map/ppermute | solution.py:34
  55.9 9.7 %collective-permute-start.9 = (bf16[64,768]{1,0:T(8,128)(2,1)S(1)}, bf16[64,768]{1,0:T(8,128)(2,1)S(1)}, u32[]{:S(2)}, u32[]{:S(2)}) collective-permute-start(bf16[64,768]{1,0:T(8,128)(2,1)S(1)} %add_convert_fusion.mine_ref), channel_id=1, source_target_pairs={{0,2},{1,3},{2,0},{3,1},{4,6},{5,7},{6,4},{7,5},{8,10},{9,11},{10,... | collective-permute-start | bytes 294920 | tf_op jit(solution)/shard_map/ppermute | solution.py:34
  56.5 4.6 %collective-permute-start.11 = (bf16[2,64,256]{2,1,0:T(8,128)(2,1)S(1)}, bf16[2,64,256]{2,1,0:T(8,128)(2,1)S(1)}, u32[]{:S(2)}, u32[]{:S(2)}) collective-permute-start(bf16[2,64,256]{2,1,0:T(8,128)(2,1)S(1)} %copy-done.3), channel_id=1, source_target_pairs={{0,4},{4,0},{8,12},{12,8},{1,5},{5,1},{9,13},{13,9},{2,6},{6,2},{1... | collective-permute-start | bytes 196616 | tf_op jit(solution)/shard_map/ppermute | solution.py:34
  60.2 4.3 %collective-permute-start.12 = (bf16[2,64,256]{2,1,0:T(8,128)(2,1)S(1)}, bf16[2,64,256]{2,1,0:T(8,128)(2,1)S(1)}, u32[]{:S(2)}, u32[]{:S(2)}) collective-permute-start(bf16[2,64,256]{2,1,0:T(8,128)(2,1)S(1)} %collective-permute-done.10.refs_1_), channel_id=1, source_target_pairs={{0,4},{4,0},{8,12},{12,8},{1,5},{5,1},{9,13},{13,9},{2,6},{6,2},{1... | collective-permute-start | bytes 196616 | tf_op jit(solution)/shard_map/ppermute | solution.py:34

commit v5 on v4

--- a/solution.py
+++ b/solution.py
@@ -52,57 +52,65 @@
     return turned
 
 
-def block(ref, index, width):
-    return ref[:, pl.ds(pl.multiple_of(index * width, width), width)].astype(F32)
-
-
-def add_kernel(stage, parts, me_ref, part_ref, pair_ref, *refs):
-    out_ref = refs[-1]
-    width = part_ref.shape[1] // parts
-    for j in range(out_ref.shape[1] // width):
-        offset = (2 * j + 1) << stage
-        owner = jnp.bitwise_xor(me_ref[0], offset)
-        total = block(part_ref, owner, width) + block(pair_ref, owner, width)
-        for r, ref in enumerate(refs[:-1], 1):
-            total = total + block(ref, offset >> (r + 1), width)
-        out_ref[:, j * width : (j + 1) * width] = total.astype(BF16)
-
-
-def sum_blocks(me, part, pair, came, parts):
-    rows, columns = part.shape
-    stage = 1 + len(came)
-    return pl.pallas_call(
-        functools.partial(add_kernel, stage, parts),
-        in_specs=[SMEM] + [VMEM] * (2 + len(came)),
-        out_specs=VMEM,
-        out_shape=jax.ShapeDtypeStruct((rows, columns >> (stage + 1)), BF16),
+def partial_kernel(me_ref, tokens_ref, weight_ref, *outs):
+    width = outs[0].shape[1]
+    for n, out_ref in enumerate(outs):
+        offset = (2 * n + 1) % len(outs) if n < len(outs) // 2 else 2 * n - len(outs)
+        at = pl.multiple_of(jnp.bitwise_xor(me_ref[0], offset) * width, width)
+        product = jnp.dot(tokens_ref[...], weight_ref[:, pl.ds(at, width)], preferred_element_type=F32)
+        out_ref[...] = product.astype(BF16)
+
+
+def partials(me, tokens, weight, parts):
+    block = jax.ShapeDtypeStruct((tokens.shape[0], weight.shape[1] // parts), BF16)
+    return pl.pallas_call(
+        partial_kernel,
+        in_specs=[SMEM, VMEM, VMEM],
+        out_specs=[VMEM] * parts,
+        out_shape=[block] * parts,
+        compiler_params=params(24),
+        cost_estimate=COST,
+        name="partials",
+    )(me, tokens, weight)
+
+
+def add_kernel(*refs):
+    total = refs[0][...].astype(F32)
+    for ref in refs[1:-1]:
+        total = total + ref[...].astype(F32)
+    refs[-1][...] = total.astype(BF16)
+
+
+def add(*terms):
+    return pl.pallas_call(
+        add_kernel,
+        in_specs=[VMEM] * len(terms),
+        out_specs=VMEM,
+        out_shape=jax.ShapeDtypeStruct(terms[0].shape, BF16),
         compiler_params=params(16),
         cost_estimate=COST,
-        name="sum_blocks",
-    )(me, part, pair, *came)
-
-
-def base_kernel(parts, me_ref, part_ref, pair_ref, scale_ref, bits_ref, matrix_ref, *refs):
-    out_ref = refs[-1]
-    width = out_ref.shape[1]
-    total = block(part_ref, me_ref[0], width) + block(pair_ref, me_ref[0], width)
-    for ref in refs[:-1]:
-        total = total + ref[:, :width].astype(F32)
+        name="add",
+    )(*terms)
+
+
+def base_kernel(scale_ref, bits_ref, matrix_ref, *refs):
+    total = refs[0][...].astype(F32)
+    for ref in refs[1:-1]:
+        total = total + ref[...].astype(F32)
     signs = (1 - 2 * bits_ref[...]).astype(F32)
-    out_ref[...] = jnp.concatenate(rotate(total * scale_ref[...], signs, matrix_ref[...]), axis=1)
-
-
-def rotated_base(me, part, pair, came, scale, bits, matrix, parts):
-    rows, columns = part.shape
-    return pl.pallas_call(
-        functools.partial(base_kernel, parts),
-        in_specs=[SMEM] + [VMEM] * (5 + len(came)),
-        out_specs=VMEM,
-        out_shape=jax.ShapeDtypeStruct((rows, columns // parts), F32),
+    refs[-1][...] = jnp.concatenate(rotate(total * scale_ref[...], signs, matrix_ref[...]), axis=1)
+
+
+def rotated_base(terms, scale, bits, matrix):
+    return pl.pallas_call(
+        base_kernel,
+        in_specs=[VMEM] * (3 + len(terms)),
+        out_specs=VMEM,
+        out_shape=jax.ShapeDtypeStruct(terms[0].shape, F32),
         compiler_params=params(16),
         cost_estimate=COST,
         name="rotated_base",
-    )(me, part, pair, scale, bits, matrix, *came)
+    )(scale, bits, matrix, *terms)
 
 
 def adapter(at_ref, here, share, name):
@@ -202,48 +210,53 @@
     down = jnp.swapaxes(adapter_down, 1, 2)
 
     own = lax.dynamic_slice_in_dim(down, g * share, share, 0)
-    part = jnp.dot(tokens, base_weight, preferred_element_type=F32).astype(BF16)
-    pair = swap(part, "tp", 1)
     near = swap(own, "adp", 1)
     mine = [(0, own)]
     bit = planes // 2
     while bit > 1:
         mine += [(plane | bit, swap(piece, "adp", bit)) for plane, piece in mine]
         bit //= 2
-    came = []
-    pair = after(pair, near)
+    blocks = partials(me, tokens, base_weight, parts)
+    half = parts // 2
+    near = after(near, *blocks)
+    mine = mine[:1] + [(plane, after(piece, near)) for plane, piece in mine[1:]]
+    odd = [(1, near)] + [(plane | 1, swap(piece, "adp", 1)) for plane, piece in mine[1:]]
+
+    def others(pieces):
+        return [(plane, off, swap(piece, "grp", off)) for plane, piece in pieces for off in range(1, groups)]
+
+    swapped = others(odd[:1]) + others(mine[1:]) + others(odd[1:])
+    held = [(plane, 0, piece) for plane, piece in odd[:1] + mine[1:] + odd[1:]]
+
+    last = mine[-1][1]
+    came = [swap(block, "tp", 1) for block in blocks[:half]]
+    sums = [[block, after(pair, last)] for block, pair in zip(blocks[half:], came)]
     bit = 2
     while bit < parts:
-        came.append(swap(sum_blocks(me, part, pair, came, parts), "tp", bit))
+        came = [swap(add(*terms), "tp", bit) for terms in sums[1::2]]
+        sums = [terms + [pair] for terms, pair in zip(sums[0::2], came)]
         bit *= 2
-    mine = mine[:1] + [(plane, after(piece, pair)) for plane, piece in mine[1:]]
-    odd = [(1, after(near, part))] + [(plane | 1, swap(piece, "adp", 1)) for plane, piece in mine[1:]]
-
-    def others(pieces):
-        return [(plane, off, swap(piece, "grp", off)) for plane, piece in pieces for off in range(1, groups)]
-
-    swapped = others(odd[:1]) + others(mine[1:]) + others(odd[1:])
-    held = [(plane, 0, piece) for plane, piece in odd[:1] + mine[1:] + odd[1:]]
-
-    ups = [(0, adapter_up)]
+    base = rotated_base(sums[0], scale, bits, matrix)
+
+    ups = [(0, after(adapter_up, held[-1][2]))]
     bit = planes // 2
     while bit:
-        ups += [(plane | bit, swap(after(up, mine[-1][1]), "adp", bit)) for plane, up in ups]
+        ups += [(plane | bit, swap(up, "adp", bit)) for plane, up in ups]
         bit //= 2
-
-    base = rotated_base(me, part, pair, came, scale, bits, matrix, parts)
+    every = [(i, k, 0, ("plane", plane, k)) for i, (plane, _) in enumerate(ups) for k in range(here)]
+    up, mask = rotated_ups(at, ids, bits, matrix, here, share, every, [up for _, up in ups], width)
 
     def terms(pieces, start):
         return [(start + i, k, 0, (plane, off, k)) for i, (plane, off, _) in enumerate(pieces) for k in range(share)]
 
     whole = (0, features)
-    early = held[: len(mine)] + swapped[:1]
-    middle = held[len(mine) :] + swapped[1:-1]
+    early = held[: len(mine)]
+    middle = held[len(mine) :] + swapped[:-1]
     late = swapped[-1:]
     home = [(0, k, 0, ("home", k)) for k in range(here)]
     low = low_rows(at, ids, tokens, here, share, [(whole, home + terms(early, 1))], [down] + [p for *_, p in early], None, F32)
     low = low_rows(at, ids, tokens, here, share, [(whole, terms(middle, 0))], [p for *_, p in middle], low, F32)
-    low = after(low, base)
+    low = after(low, base, up)
     low = low_rows(at, ids, tokens, here, share, [(whole, terms(late, 0))], [p for *_, p in late], low, BF16)
     bit = 1
     while bit < parts // 2:
@@ -251,8 +264,6 @@
         bit *= 2
     other = swap(low, "tp", bit)
 
-    every = [(i, k, 0, ("plane", plane, k)) for i, (plane, _) in enumerate(ups) for k in range(here)]
-    up, mask = rotated_ups(at, ids, bits, matrix, here, share, every, [up for _, up in ups], width)
     return final(low, other, base, up, mask)
 
 

time: 67.3 us -> 65 us (0.966)
  local copies, waits for them, and re-layouts: 2.27 us -> 11.9 us
  waiting for transfers between devices: 28.7 us -> 20.5 us
  matrix products: 7.73 us -> 0 us
  starting transfers between devices: 14.5 us -> 17.4 us
  Pallas kernels: 13.7 us -> 14.4 us
    unnamed x14 -> x36, local copies, waits for them, and re-layouts: 1.08 us -> 10.9 us
    ppermute x13 -> x14, waiting for transfers between devices: 28.7 us -> 20.5 us  [swap(): lax.ppermute(x, axis, [(i, i ^ bit) for i in range(lax.axis_size(axis))])]
    dot_general x1 -> x0, matrix products: 7.73 us -> none  [local(): part = jnp.dot(tokens, base_weight, preferred_element_type=F32).astype(BF16)]
    ppermute x13 -> x14, starting transfers between devices: 14.5 us -> 17.4 us  [swap(): lax.ppermute(x, axis, [(i, i ^ bit) for i in range(lax.axis_size(axis))])]
    pallas_call x2 -> x3, Pallas kernels: 4.45 us -> 5.01 us  [the longest x1 3.43 us: partials(): pl.pallas_call(partial_kernel, in_specs=[SMEM, VMEM, VMEM], out_specs=[VM...]
  transfers between devices with their start and end apart: 13 -> 14, of which waited for: 8 -> 5; matrix products, arithmetic and copies ran while one was open for 2% -> 2% of each run, Pallas kernels for 15% -> 12%
where the time goes in v5:
time: 65 us; the launch traced here: 64.5 us
  waiting for transfers between devices  20.5 us (32%)
  starting transfers between devices  17.4 us (27%)
  Pallas kernels  14.4 us (22%)
  local copies, waits for them, and re-layouts  11.9 us (18%)
    ppermute x14, waiting for transfers between devices, swap(): lax.ppermute(x, axis, [(i, i ^ bit) for i in range(lax.axis_size(axis))])  20.5 us
    ppermute x14, starting transfers between devices, swap(): lax.ppermute(x, axis, [(i, i ^ bit) for i in range(lax.axis_size(axis))])  17.4 us
    unnamed x36, local copies, waits for them, and re-layouts  10.9 us
    pallas_call x3, Pallas kernels, low_rows(): pl.pallas_call(functools.partial(low_kernel, groups, here, share, rank, b...  6.46 us
    pallas_call x1, Pallas kernels, partials(): pl.pallas_call(partial_kernel, in_specs=[SMEM, VMEM, VMEM], out_specs=[VM...  3.43 us
    pallas_call x1, Pallas kernels, rotated_ups(): pl.pallas_call(functools.partial(ups_kernel, terms, here, share, rank), i...  1.51 us
    pallas_call x1, Pallas kernels, rotated_base(): pl.pallas_call(base_kernel, in_specs=[VMEM] * (3 + len(terms)), out_specs...  1.49 us
    pallas_call x1, Pallas kernels, final(): pl.pallas_call(final_kernel, in_specs=[VMEM] * 5, out_specs=VMEM, out_sha...  1.45 us
  transfers between devices with their start and end apart: 14, of which 5 were waited for; matrix products, arithmetic and copies ran while one was open for 2% of the time, Pallas kernels for 12%

profile of v5, /device:TPU:0, one launch (start us, length us, event | category | flops | bytes accessed | tf_op | source)
XLA Modules:
  0.0 64.5 jit_solution(1506194337042004543)
XLA Ops:
  0.0 1.9 %copy-done = bf16[768,2048]{1,0:T(8,128)(2,1)S(1)} copy-done((bf16[768,2048]{1,0:T(8,128)(2,1)S(1)}, bf16[768,2048]{1,0:T(8,128)(2,1)}, u32[]{:S(2)}) %copy-start) | copy-done | bytes 3145752
  1.9 2.2 %copy-done.2 = bf16[2048,1024]{1,0:T(8,128)(2,1)S(1)} copy-done((bf16[2048,1024]{1,0:T(8,128)(2,1)S(1)}, bf16[2048,1024]{1,0:T(8,128)(2,1)}, u32[]{:S(2)}) %copy-start.2) | copy-done | bytes 4194328
  4.1 3.4 %partials.1 = (bf16[768,256]{1,0:T(8,128)(2,1)S(1)}, bf16[768,256]{1,0:T(8,128)(2,1)}, bf16[768,256]{1,0:T(8,128)(2,1)S(1)}, bf16[768,256]{1,0:T(8,128)(2,1)S(1)}) custom-call(s32[1]{0:T(128)} %bitcast.4.me_ref, bf16[768,2048]{1,0:T(8,128)(2,1)S(1)} %copy-done, bf16[2048,1024]{1,0:T(8,128)(2,1)S(1)} %copy-done.2), custom_call_target="tpu_custom_call" | custom-call | flops 1 | bytes 1 | tf_op jit(solution)/shard_map/partials/pallas_call | solution.py:66
  7.5 0.8 %copy-done.4 = bf16[768,256]{1,0:T(8,128)(2,1)} copy-done((bf16[768,256]{1,0:T(8,128)(2,1)}, bf16[768,256]{1,0:T(8,128)(2,1)S(1)}, u32[]{:S(2)}) %copy-start.4) | copy-done | bytes 393240
  8.3 0.7 %copy-done.8 = bf16[768,256]{1,0:T(8,128)(2,1)} copy-done((bf16[768,256]{1,0:T(8,128)(2,1)}, bf16[768,256]{1,0:T(8,128)(2,1)S(1)}, u32[]{:S(2)}) %copy-start.8) | copy-done | bytes 393240
  9.0 0.8 %copy-done.17 = bf16[768,256]{1,0:T(8,128)(2,1)} copy-done((bf16[768,256]{1,0:T(8,128)(2,1)}, bf16[768,256]{1,0:T(8,128)(2,1)S(1)}, u32[]{:S(2)}) %copy-start.17) | copy-done | bytes 393240
  10.3 1.0 %dynamic-slice_bitcast_fusion = bf16[1,64,2048]{2,1,0:T(8,128)(2,1)S(1)} fusion(bf16[2,2048,64]{1,2,0:T(8,128)(2,1)} %param.12, s32[]{:T(128)S(6)} %select_n.3), kind=kLoop, calls=%fused_computation | loop fusion | bytes 524292 | tf_op jit(solution)/shard_map/dynamic_slice | solution.py:212
  11.2 2.6 %collective-permute-start.1 = (bf16[1,64,2048]{2,1,0:T(8,128)(2,1)S(1)}, bf16[1,64,2048]{2,1,0:T(8,128)(2,1)}, u32[]{:S(2)}, u32[]{:S(2)}) collective-permute-start(bf16[1,64,2048]{2,1,0:T(8,128)(2,1)S(1)} %dynamic-slice_bitcast_fusion), channel_id=1, source_target_pairs={{0,4},{4,0},{8,12},{12,8},{1,5},{5,1},{9,13},{13,9},{2,6},{6,2},{1... | collective-permute-start | bytes 786440 | tf_op jit(solution)/shard_map/ppermute | solution.py:34
  13.9 2.6 %collective-permute-start = (bf16[1,64,2048]{2,1,0:T(8,128)(2,1)S(1)}, bf16[1,64,2048]{2,1,0:T(8,128)(2,1)}, u32[]{:S(2)}, u32[]{:S(2)}) collective-permute-start(bf16[1,64,2048]{2,1,0:T(8,128)(2,1)S(1)} %dynamic-slice_bitcast_fusion), channel_id=1, source_target_pairs={{0,8},{4,12},{8,0},{12,4},{1,9},{5,13},{9,1},{13,5},{2,10},{6,14},... | collective-permute-start | bytes 786440 | tf_op jit(solution)/shard_map/ppermute | solution.py:34
  16.5 10.0 %collective-permute-done.1.refs_1_ = bf16[1,64,2048]{2,1,0:T(8,128)(2,1)} collective-permute-done((bf16[1,64,2048]{2,1,0:T(8,128)(2,1)S(1)}, bf16[1,64,2048]{2,1,0:T(8,128)(2,1)}, u32[]{:S(2)}, u32[]{:S(2)}) %collective-permute-start.1) | collective-permute-done | bytes 262176 | tf_op jit(solution)/shard_map/ppermute | solution.py:34
  26.5 2.5 %collective-permute-done.refs_2_ = bf16[1,64,2048]{2,1,0:T(8,128)(2,1)} collective-permute-done((bf16[1,64,2048]{2,1,0:T(8,128)(2,1)S(1)}, bf16[1,64,2048]{2,1,0:T(8,128)(2,1)}, u32[]{:S(2)}, u32[]{:S(2)}) %collective-permute-start) | collective-permute-done | bytes 262176 | tf_op jit(solution)/shard_map/ppermute | solution.py:34
  29.4 0.7 %copy-done.6 = bf16[768,256]{1,0:T(8,128)(2,1)} copy-done((bf16[768,256]{1,0:T(8,128)(2,1)}, bf16[768,256]{1,0:T(8,128)(2,1)S(1)}, u32[]{:S(2)}) %copy-start.6) | copy-done | bytes 393240
  30.2 1.0 %copy-done.5 = bf16[768,256]{1,0:T(8,128)(2,1)S(1)} copy-done((bf16[768,256]{1,0:T(8,128)(2,1)S(1)}, bf16[768,256]{1,0:T(8,128)(2,1)}, u32[]{:S(2)}) %copy-start.5) | copy-done | bytes 393240
  31.2 1.0 %copy-done.7 = bf16[768,256]{1,0:T(8,128)(2,1)S(1)} copy-done((bf16[768,256]{1,0:T(8,128)(2,1)S(1)}, bf16[768,256]{1,0:T(8,128)(2,1)}, u32[]{:S(2)}) %copy-start.7) | copy-done | bytes 393240
  32.3 1.6 %collective-permute-start.8 = (bf16[768,256]{1,0:T(8,128)(2,1)S(1)}, bf16[768,256]{1,0:T(8,128)(2,1)}, u32[]{:S(2)}, u32[]{:S(2)}) collective-permute-start(bf16[768,256]{1,0:T(8,128)(2,1)S(1)} %add.12), channel_id=1, source_target_pairs={{0,2},{1,3},{2,0},{3,1},{4,6},{5,7},{6,4},{7,5},{8,10},{9,11},{10,... | collective-permute-start | bytes 1179656 | tf_op jit(solution)/shard_map/ppermute | solution.py:34
  33.8 1.5 %collective-permute-start.4 = (bf16[1,64,2048]{2,1,0:T(8,128)(2,1)}, bf16[1,64,2048]{2,1,0:T(8,128)(2,1)}, u32[]{:S(2)}, u32[]{:S(2)}) collective-permute-start(bf16[1,64,2048]{2,1,0:T(8,128)(2,1)} %collective-permute-done.1.refs_1_), channel_id=1, source_target_pairs={{0,16},{16,0},{1,17},{17,1},{2,18},{18,2},{3,19},{19,3},{4,20},{20... | collective-permute-start | bytes 786440 | tf_op jit(solution)/shard_map/ppermute | solution.py:34
  35.9 1.5 %collective-permute-start.3 = (bf16[1,64,2048]{2,1,0:T(8,128)(2,1)}, bf16[1,64,2048]{2,1,0:T(8,128)(2,1)}, u32[]{:S(2)}, u32[]{:S(2)}) collective-permute-start(bf16[1,64,2048]{2,1,0:T(8,128)(2,1)} %collective-permute-done.2.refs_0_), channel_id=1, source_target_pairs={{0,16},{16,0},{1,17},{17,1},{2,18},{18,2},{3,19},{19,3},{4,20},{20... | collective-permute-start | bytes 786440 | tf_op jit(solution)/shard_map/ppermute | solution.py:34
  37.4 0.7 %copy-done.10 = bf16[768,256]{1,0:T(8,128)(2,1)} copy-done((bf16[768,256]{1,0:T(8,128)(2,1)}, bf16[768,256]{1,0:T(8,128)(2,1)S(1)}, u32[]{:S(2)}) %copy-start.10) | copy-done | bytes 393240
  38.1 2.6 %collective-permute-start.9 = (bf16[2,64,256]{2,1,0:T(8,128)(2,1)}, bf16[2,64,256]{2,1,0:T(8,128)(2,1)}, u32[]{:S(2)}, u32[]{:S(2)}) collective-permute-start(bf16[2,64,256]{2,1,0:T(8,128)(2,1)} %refs_0_), channel_id=1, source_target_pairs={{0,8},{4,12},{8,0},{12,4},{1,9},{5,13},{9,1},{13,5},{2,10},{6,14},... | collective-permute-start | bytes 196616 | tf_op jit(solution)/shard_map/ppermute | solution.py:34
  40.7 2.7 %collective-permute-done.4.refs_1_ = bf16[1,64,2048]{2,1,0:T(8,128)(2,1)} collective-permute-done((bf16[1,64,2048]{2,1,0:T(8,128)(2,1)}, bf16[1,64,2048]{2,1,0:T(8,128)(2,1)}, u32[]{:S(2)}, u32[]{:S(2)}) %collective-permute-start.4) | collective-permute-done | bytes 262176 | tf_op jit(solution)/shard_map/ppermute | solution.py:34
  43.4 1.6 %collective-permute-start.10 = (bf16[2,64,256]{2,1,0:T(8,128)(2,1)}, bf16[2,64,256]{2,1,0:T(8,128)(2,1)S(1)}, u32[]{:S(2)}, u32[]{:S(2)}) collective-permute-start(bf16[2,64,256]{2,1,0:T(8,128)(2,1)} %refs_0_), channel_id=1, source_target_pairs={{0,4},{4,0},{8,12},{12,8},{1,5},{5,1},{9,13},{13,9},{2,6},{6,2},{1... | collective-permute-start | bytes 196616 | tf_op jit(solution)/shard_map/ppermute | solution.py:34
  45.0 1.1 %collective-permute-start.11 = (bf16[2,64,256]{2,1,0:T(8,128)(2,1)}, bf16[2,64,256]{2,1,0:T(8,128)(2,1)S(1)}, u32[]{:S(2)}, u32[]{:S(2)}) collective-permute-start(bf16[2,64,256]{2,1,0:T(8,128)(2,1)} %collective-permute-done.9.refs_1_), channel_id=1, source_target_pairs={{0,4},{4,0},{8,12},{12,8},{1,5},{5,1},{9,13},{13,9},{2,6},{6,2},{1... | collective-permute-start | bytes 196616 | tf_op jit(solution)/shard_map/ppermute | solution.py:34
  46.1 1.0 %copy-done.3 = bf16[2,2048,64]{1,2,0:T(8,128)(2,1)S(1)} copy-done((bf16[2,2048,64]{1,2,0:T(8,128)(2,1)S(1)}, bf16[2,2048,64]{1,2,0:T(8,128)(2,1)}, u32[]{:S(2)}) %copy-start.3) | copy-done | bytes 524312
  47.2 2.1 %low_rows.3.refs_3_ = f32[64,768]{1,0:T(8,128)S(1)} custom-call(s32[2]{0:T(128)S(1)} %pad_add_fusion.at_ref, s32[1,768]{1,0:T(1,128)S(1)} %bitcast.10, bf16[768,2048]{1,0:T(8,128)(2,1)S(1)} %copy-done.1, bf16[2,64,2048]{2,1,0:T(8,128)(2,1)S(1)} %bitcast.9, bf16[1,64,2048]{2,1,0:T(8,128)(2,1)} %collective-permute-done.1.refs_1_, ...), custom_call_target="tpu_custom_call" | custom-call | flops 1 | bytes 1 | tf_op jit(solution)/shard_map/low_rows/pallas_call | solution.py:142
  49.3 2.3 %low_rows.4.refs_1_ = f32[64,768]{1,0:T(8,128)S(1)} custom-call(s32[2]{0:T(128)S(1)} %pad_add_fusion.at_ref, s32[1,768]{1,0:T(1,128)S(1)} %bitcast.11, bf16[768,2048]{1,0:T(8,128)(2,1)S(1)} %copy-done.1, bf16[1,64,2048]{2,1,0:T(8,128)(2,1)} %collective-permute-done.2.refs_0_, bf16[1,64,2048]{2,1,0:T(8,128)(2,1)} %collective-permute-done.4.refs_1_, ...), custom_call_target="tpu_custom_call" | custom-call | flops 1 | bytes 1 | tf_op jit(solution)/shard_map/low_rows/pallas_call | solution.py:142
  51.7 1.5 %rotated_ups.1 = (bf16[512,256]{1,0:T(8,128)(2,1)S(1)}, bf16[768,512]{1,0:T(8,128)(2,1)S(1)}) custom-call(s32[2]{0:T(128)S(1)} %pad_add_fusion.at_ref, s32[1,768]{1,0:T(1,128)S(1)} %bitcast.12, s32[1,128]{1,0:T(1,128)S(1)} %bitcast.14, bf16[128,128]{1,0:T(8,128)(2,1)S(1)} %copy-done.12, bf16[2,64,256]{2,1,0:T(8,128)(2,1)S(1)} %copy-done.13, ...), custom_call_target="tpu_custom_call" | custom-call | flops 1 | bytes 1 | tf_op jit(solution)/shard_map/rotated_ups/pallas_call | solution.py:168
  53.2 1.5 %rotated_base.1.base_ref = f32[768,256]{1,0:T(8,128)S(1)} custom-call(f32[1,256]{1,0:T(1,128)S(1)} %bitcast.16, s32[1,128]{1,0:T(1,128)S(1)} %bitcast.15, bf16[128,128]{1,0:T(8,128)(2,1)S(1)} %copy-done.12, bf16[768,256]{1,0:T(8,128)(2,1)S(1)} %copy-done.9, bf16[768,256]{1,0:T(8,128)(2,1)S(1)} %copy-done.11, bf16[768,256]{1,0:T(8,128)(2,1)} %collective-permute-done.8.refs_2_), custom_call_target="tpu_custom_call" | custom-call | flops 1 | bytes 1 | tf_op jit(solution)/shard_map/rotated_base/pallas_call | solution.py:105
  54.7 2.0 %low_rows.5 = bf16[64,768]{1,0:T(8,128)(2,1)S(1)} custom-call(s32[2]{0:T(128)S(1)} %pad_add_fusion.at_ref, s32[1,768]{1,0:T(1,128)S(1)} %bitcast.13, bf16[768,2048]{1,0:T(8,128)(2,1)S(1)} %copy-done.1, bf16[1,64,2048]{2,1,0:T(8,128)(2,1)} %collective-permute-done.3.refs_0_, f32[64,768]{1,0:T(8,128)S(1)} %low_rows.4.refs_1_), custom_call_target="tpu_custom_call" | custom-call | flops 1 | bytes 1 | tf_op jit(solution)/shard_map/low_rows/pallas_call | solution.py:142
  56.9 1.3 %collective-permute-done.12 = bf16[64,768]{1,0:T(8,128)(2,1)S(1)} collective-permute-done((bf16[64,768]{1,0:T(8,128)(2,1)S(1)}, bf16[64,768]{1,0:T(8,128)(2,1)S(1)}, u32[]{:S(2)}, u32[]{:S(2)}) %collective-permute-start.12) | collective-permute-done | bytes 98336 | tf_op jit(solution)/shard_map/ppermute | solution.py:34
  58.2 0.9 %collective-permute-start.13 = (bf16[64,768]{1,0:T(8,128)(2,1)S(1)}, bf16[64,768]{1,0:T(8,128)(2,1)S(1)}, u32[]{:S(2)}, u32[]{:S(2)}) collective-permute-start(bf16[64,768]{1,0:T(8,128)(2,1)S(1)} %add_convert_fusion.mine_ref), channel_id=1, source_target_pairs={{0,2},{1,3},{2,0},{3,1},{4,6},{5,7},{6,4},{7,5},{8,10},{9,11},{10,... | collective-permute-start | bytes 294920 | tf_op jit(solution)/shard_map/ppermute | solution.py:34
  59.1 4.0 %collective-permute-done.13.theirs_ref = bf16[64,768]{1,0:T(8,128)(2,1)S(1)} collective-permute-done((bf16[64,768]{1,0:T(8,128)(2,1)S(1)}, bf16[64,768]{1,0:T(8,128)(2,1)S(1)}, u32[]{:S(2)}, u32[]{:S(2)}) %collective-permute-start.13) | collective-permute-done | bytes 98336 | tf_op jit(solution)/shard_map/ppermute | solution.py:34
  63.1 1.4 %final.1 = bf16[768,256]{1,0:T(8,128)(2,1)} custom-call(bf16[64,768]{1,0:T(8,128)(2,1)S(1)} %add_convert_fusion.mine_ref, bf16[64,768]{1,0:T(8,128)(2,1)S(1)} %collective-permute-done.13.theirs_ref, f32[768,256]{1,0:T(8,128)S(1)} %rotated_base.1.base_ref, bf16[512,256]{1,0:T(8,128)(2,1)S(1)} %get-tuple-element.26.up_ref, ...), custom_call_target="tpu_custom_call" | custom-call | flops 1 | bytes 1 | tf_op jit(solution)/shard_map/final/pallas_call | solution.py:189
  (43 shorter events, 1.8 us)
Async XLA Ops:
  0.0 1.9 %copy-start = (bf16[768,2048]{1,0:T(8,128)(2,1)S(1)}, bf16[768,2048]{1,0:T(8,128)(2,1)}, u32[]{:S(2)}) copy-start(bf16[768,2048]{1,0:T(8,128)(2,1)} %tokens_ref.7) | copy-start | bytes 9437188
  1.9 2.2 %copy-start.2 = (bf16[2048,1024]{1,0:T(8,128)(2,1)S(1)}, bf16[2048,1024]{1,0:T(8,128)(2,1)}, u32[]{:S(2)}) copy-start(bf16[2048,1024]{1,0:T(8,128)(2,1)} %weight_ref.1) | copy-start | bytes 12582916
  4.1 42.0 %copy-start.1 = (bf16[768,2048]{1,0:T(8,128)(2,1)S(1)}, bf16[768,2048]{1,0:T(8,128)(2,1)}, u32[]{:S(2)}) copy-start(bf16[768,2048]{1,0:T(8,128)(2,1)} %tokens_ref.7) | copy-start | bytes 9437188
  4.1 42.0 %copy-start.14 = (s32[768,1]{0,1:T(1,128)S(1)}, s32[768,1]{0,1:T(1,128)}, u32[]{:S(2)}) copy-start(s32[768,1]{0,1:T(1,128)} %param.9) | copy-start | bytes 9220
  7.5 0.8 %copy-start.4 = (bf16[768,256]{1,0:T(8,128)(2,1)}, bf16[768,256]{1,0:T(8,128)(2,1)S(1)}, u32[]{:S(2)}) copy-start(bf16[768,256]{1,0:T(8,128)(2,1)S(1)} %get-tuple-element.20.refs_0_) | copy-start | bytes 1179652
  8.3 0.7 %copy-start.8 = (bf16[768,256]{1,0:T(8,128)(2,1)}, bf16[768,256]{1,0:T(8,128)(2,1)S(1)}, u32[]{:S(2)}) copy-start(bf16[768,256]{1,0:T(8,128)(2,1)S(1)} %get-tuple-element.19.refs_0_) | copy-start | bytes 1179652
  9.0 0.8 %copy-start.17 = (bf16[768,256]{1,0:T(8,128)(2,1)}, bf16[768,256]{1,0:T(8,128)(2,1)S(1)}, u32[]{:S(2)}) copy-start(bf16[768,256]{1,0:T(8,128)(2,1)S(1)} %get-tuple-element.17) | copy-start | bytes 1179652
  9.8 19.6 %collective-permute-start.7 = (bf16[768,256]{1,0:T(8,128)(2,1)}, bf16[768,256]{1,0:T(8,128)(2,1)S(1)}, u32[]{:S(2)}, u32[]{:S(2)}) collective-permute-start(bf16[768,256]{1,0:T(8,128)(2,1)} %get-tuple-element.18), channel_id=1, source_target_pairs={{0,1},{1,0},{2,3},{3,2},{4,5},{5,4},{6,7},{7,6},{8,9},{9,8},{10,11... | collective-permute-start | bytes 1179656 | tf_op jit(solution)/shard_map/ppermute | solution.py:34
  11.2 15.2 %collective-permute-start.1 = (bf16[1,64,2048]{2,1,0:T(8,128)(2,1)S(1)}, bf16[1,64,2048]{2,1,0:T(8,128)(2,1)}, u32[]{:S(2)}, u32[]{:S(2)}) collective-permute-start(bf16[1,64,2048]{2,1,0:T(8,128)(2,1)S(1)} %dynamic-slice_bitcast_fusion), channel_id=1, source_target_pairs={{0,4},{4,0},{8,12},{12,8},{1,5},{5,1},{9,13},{13,9},{2,6},{6,2},{1... | collective-permute-start | bytes 786440 | tf_op jit(solution)/shard_map/ppermute | solution.py:34
  13.9 15.1 %collective-permute-start = (bf16[1,64,2048]{2,1,0:T(8,128)(2,1)S(1)}, bf16[1,64,2048]{2,1,0:T(8,128)(2,1)}, u32[]{:S(2)}, u32[]{:S(2)}) collective-permute-start(bf16[1,64,2048]{2,1,0:T(8,128)(2,1)S(1)} %dynamic-slice_bitcast_fusion), channel_id=1, source_target_pairs={{0,8},{4,12},{8,0},{12,4},{1,9},{5,13},{9,1},{13,5},{2,10},{6,14},... | collective-permute-start | bytes 786440 | tf_op jit(solution)/shard_map/ppermute | solution.py:34
  16.5 20.9 %collective-permute-start.6 = (bf16[768,256]{1,0:T(8,128)(2,1)}, bf16[768,256]{1,0:T(8,128)(2,1)S(1)}, u32[]{:S(2)}, u32[]{:S(2)}) collective-permute-start(bf16[768,256]{1,0:T(8,128)(2,1)} %copy-done.17), channel_id=1, source_target_pairs={{0,1},{1,0},{2,3},{3,2},{4,5},{5,4},{6,7},{7,6},{8,9},{9,8},{10,11... | collective-permute-start | bytes 1179656 | tf_op jit(solution)/shard_map/ppermute | solution.py:34
  29.0 6.9 %collective-permute-start.2 = (bf16[1,64,2048]{2,1,0:T(8,128)(2,1)}, bf16[1,64,2048]{2,1,0:T(8,128)(2,1)}, u32[]{:S(2)}, u32[]{:S(2)}) collective-permute-start(bf16[1,64,2048]{2,1,0:T(8,128)(2,1)} %collective-permute-done.refs_2_), channel_id=1, source_target_pairs={{0,4},{4,0},{8,12},{12,8},{1,5},{5,1},{9,13},{13,9},{2,6},{6,2},{1... | collective-permute-start | bytes 786440 | tf_op jit(solution)/shard_map/ppermute | solution.py:34
  29.4 0.7 %copy-start.6 = (bf16[768,256]{1,0:T(8,128)(2,1)}, bf16[768,256]{1,0:T(8,128)(2,1)S(1)}, u32[]{:S(2)}) copy-start(bf16[768,256]{1,0:T(8,128)(2,1)S(1)} %collective-permute-done.7.refs_1_) | copy-start | bytes 1179652
  30.2 1.0 %copy-start.5 = (bf16[768,256]{1,0:T(8,128)(2,1)S(1)}, bf16[768,256]{1,0:T(8,128)(2,1)}, u32[]{:S(2)}) copy-start(bf16[768,256]{1,0:T(8,128)(2,1)} %copy-done.4) | copy-start | bytes 1179652
  31.2 1.0 %copy-start.7 = (bf16[768,256]{1,0:T(8,128)(2,1)S(1)}, bf16[768,256]{1,0:T(8,128)(2,1)}, u32[]{:S(2)}) copy-start(bf16[768,256]{1,0:T(8,128)(2,1)} %copy-done.6) | copy-start | bytes 1179652
  32.3 20.9 %collective-permute-start.8 = (bf16[768,256]{1,0:T(8,128)(2,1)S(1)}, bf16[768,256]{1,0:T(8,128)(2,1)}, u32[]{:S(2)}, u32[]{:S(2)}) collective-permute-start(bf16[768,256]{1,0:T(8,128)(2,1)S(1)} %add.12), channel_id=1, source_target_pairs={{0,2},{1,3},{2,0},{3,1},{4,6},{5,7},{6,4},{7,5},{8,10},{9,11},{10,... | collective-permute-start | bytes 1179656 | tf_op jit(solution)/shard_map/ppermute | solution.py:34
  33.8 9.6 %collective-permute-start.4 = (bf16[1,64,2048]{2,1,0:T(8,128)(2,1)}, bf16[1,64,2048]{2,1,0:T(8,128)(2,1)}, u32[]{:S(2)}, u32[]{:S(2)}) collective-permute-start(bf16[1,64,2048]{2,1,0:T(8,128)(2,1)} %collective-permute-done.1.refs_1_), channel_id=1, source_target_pairs={{0,16},{16,0},{1,17},{17,1},{2,18},{18,2},{3,19},{19,3},{4,20},{20... | collective-permute-start | bytes 786440 | tf_op jit(solution)/shard_map/ppermute | solution.py:34
  35.3 14.0 %collective-permute-start.5 = (bf16[1,64,2048]{2,1,0:T(8,128)(2,1)}, bf16[1,64,2048]{2,1,0:T(8,128)(2,1)}, u32[]{:S(2)}, u32[]{:S(2)}) collective-permute-start(bf16[1,64,2048]{2,1,0:T(8,128)(2,1)} %collective-permute-done.refs_2_), channel_id=1, source_target_pairs={{0,16},{16,0},{1,17},{17,1},{2,18},{18,2},{3,19},{19,3},{4,20},{20... | collective-permute-start | bytes 786440 | tf_op jit(solution)/shard_map/ppermute | solution.py:34
  35.9 18.9 %collective-permute-start.3 = (bf16[1,64,2048]{2,1,0:T(8,128)(2,1)}, bf16[1,64,2048]{2,1,0:T(8,128)(2,1)}, u32[]{:S(2)}, u32[]{:S(2)}) collective-permute-start(bf16[1,64,2048]{2,1,0:T(8,128)(2,1)} %collective-permute-done.2.refs_0_), channel_id=1, source_target_pairs={{0,16},{16,0},{1,17},{17,1},{2,18},{18,2},{3,19},{19,3},{4,20},{20... | collective-permute-start | bytes 786440 | tf_op jit(solution)/shard_map/ppermute | solution.py:34
  37.4 0.7 %copy-start.10 = (bf16[768,256]{1,0:T(8,128)(2,1)}, bf16[768,256]{1,0:T(8,128)(2,1)S(1)}, u32[]{:S(2)}) copy-start(bf16[768,256]{1,0:T(8,128)(2,1)S(1)} %collective-permute-done.6.refs_1_) | copy-start | bytes 1179652
  38.1 6.8 %collective-permute-start.9 = (bf16[2,64,256]{2,1,0:T(8,128)(2,1)}, bf16[2,64,256]{2,1,0:T(8,128)(2,1)}, u32[]{:S(2)}, u32[]{:S(2)}) collective-permute-start(bf16[2,64,256]{2,1,0:T(8,128)(2,1)} %refs_0_), channel_id=1, source_target_pairs={{0,8},{4,12},{8,0},{12,4},{1,9},{5,13},{9,1},{13,5},{2,10},{6,14},... | collective-permute-start | bytes 196616 | tf_op jit(solution)/shard_map/ppermute | solution.py:34
  43.4 8.3 %collective-permute-start.10 = (bf16[2,64,256]{2,1,0:T(8,128)(2,1)}, bf16[2,64,256]{2,1,0:T(8,128)(2,1)S(1)}, u32[]{:S(2)}, u32[]{:S(2)}) collective-permute-start(bf16[2,64,256]{2,1,0:T(8,128)(2,1)} %refs_0_), channel_id=1, source_target_pairs={{0,4},{4,0},{8,12},{12,8},{1,5},{5,1},{9,13},{13,9},{2,6},{6,2},{1... | collective-permute-start | bytes 196616 | tf_op jit(solution)/shard_map/ppermute | solution.py:34
  45.0 6.7 %collective-permute-start.11 = (bf16[2,64,256]{2,1,0:T(8,128)(2,1)}, bf16[2,64,256]{2,1,0:T(8,128)(2,1)S(1)}, u32[]{:S(2)}, u32[]{:S(2)}) collective-permute-start(bf16[2,64,256]{2,1,0:T(8,128)(2,1)} %collective-permute-done.9.refs_1_), channel_id=1, source_target_pairs={{0,4},{4,0},{8,12},{12,8},{1,5},{5,1},{9,13},{13,9},{2,6},{6,2},{1... | collective-permute-start | bytes 196616 | tf_op jit(solution)/shard_map/ppermute | solution.py:34
  46.1 1.0 %copy-start.3 = (bf16[2,2048,64]{1,2,0:T(8,128)(2,1)S(1)}, bf16[2,2048,64]{1,2,0:T(8,128)(2,1)}, u32[]{:S(2)}) copy-start(bf16[2,2048,64]{1,2,0:T(8,128)(2,1)} %param.12) | copy-start | bytes 1572868
  47.1 4.5 %copy-start.12 = (bf16[128,128]{1,0:T(8,128)(2,1)S(1)}, bf16[128,128]{1,0:T(8,128)(2,1)}, u32[]{:S(2)}) copy-start(bf16[128,128]{1,0:T(8,128)(2,1)} %constant.19.clone.matrix_ref) | copy-start | bytes 98308
  47.1 4.5 %copy-start.13 = (bf16[2,64,256]{2,1,0:T(8,128)(2,1)S(1)}, bf16[2,64,256]{2,1,0:T(8,128)(2,1)}, u32[]{:S(2)}) copy-start(bf16[2,64,256]{2,1,0:T(8,128)(2,1)} %refs_0_) | copy-start | bytes 196612
  47.1 4.5 %copy-start.15 = (s32[128]{0:T(128)S(1)}, s32[128]{0:T(128)}, u32[]{:S(2)}) copy-start(s32[128]{0:T(128)} %param.14) | copy-start | bytes 1540
  47.1 6.1 %copy-start.9 = (bf16[768,256]{1,0:T(8,128)(2,1)S(1)}, bf16[768,256]{1,0:T(8,128)(2,1)}, u32[]{:S(2)}) copy-start(bf16[768,256]{1,0:T(8,128)(2,1)} %copy-done.8) | copy-start | bytes 1179652
  47.2 6.1 %copy-start.11 = (bf16[768,256]{1,0:T(8,128)(2,1)S(1)}, bf16[768,256]{1,0:T(8,128)(2,1)}, u32[]{:S(2)}) copy-start(bf16[768,256]{1,0:T(8,128)(2,1)} %copy-done.10) | copy-start | bytes 1179652
  47.2 6.1 %copy-start.16 = (f32[256]{0:T(256)S(1)}, f32[256]{0:T(256)}, u32[]{:S(2)}) copy-start(f32[256]{0:T(256)} %param.11) | copy-start | bytes 3076
  56.8 1.4 %collective-permute-start.12 = (bf16[64,768]{1,0:T(8,128)(2,1)S(1)}, bf16[64,768]{1,0:T(8,128)(2,1)S(1)}, u32[]{:S(2)}, u32[]{:S(2)}) collective-permute-start(bf16[64,768]{1,0:T(8,128)(2,1)S(1)} %low_rows.5), channel_id=1, source_target_pairs={{0,1},{1,0},{2,3},{3,2},{4,5},{5,4},{6,7},{7,6},{8,9},{9,8},{10,11... | collective-permute-start | bytes 294920 | tf_op jit(solution)/shard_map/ppermute | solution.py:34
  58.2 4.9 %collective-permute-start.13 = (bf16[64,768]{1,0:T(8,128)(2,1)S(1)}, bf16[64,768]{1,0:T(8,128)(2,1)S(1)}, u32[]{:S(2)}, u32[]{:S(2)}) collective-permute-start(bf16[64,768]{1,0:T(8,128)(2,1)S(1)} %add_convert_fusion.mine_ref), channel_id=1, source_target_pairs={{0,2},{1,3},{2,0},{3,1},{4,6},{5,7},{6,4},{7,5},{8,10},{9,11},{10,... | collective-permute-start | bytes 294920 | tf_op jit(solution)/shard_map/ppermute | solution.py:34

commit v6 on v5

--- a/solution.py
+++ b/solution.py
@@ -34,8 +34,8 @@
     return lax.ppermute(x, axis, [(i, i ^ bit) for i in range(lax.axis_size(axis))])
 
 
-def after(value, *others):
-    return lax.optimization_barrier((value, *others))[0]
+def together(*values):
+    return lax.optimization_barrier(values)
 
 
 def rotate(value, signs, matrix):
@@ -52,26 +52,27 @@
     return turned
 
 
-def partial_kernel(me_ref, tokens_ref, weight_ref, *outs):
-    width = outs[0].shape[1]
+def partial_kernel(tokens_ref, weight_ref, sign_ref, *outs):
+    me, width = lax.axis_index("tp"), outs[0].shape[1]
+    sign_ref[...] = jnp.zeros_like(sign_ref)
     for n, out_ref in enumerate(outs):
         offset = (2 * n + 1) % len(outs) if n < len(outs) // 2 else 2 * n - len(outs)
-        at = pl.multiple_of(jnp.bitwise_xor(me_ref[0], offset) * width, width)
+        at = pl.multiple_of(jnp.bitwise_xor(me, offset) * width, width)
         product = jnp.dot(tokens_ref[...], weight_ref[:, pl.ds(at, width)], preferred_element_type=F32)
         out_ref[...] = product.astype(BF16)
 
 
-def partials(me, tokens, weight, parts):
+def partials(tokens, weight, parts):
     block = jax.ShapeDtypeStruct((tokens.shape[0], weight.shape[1] // parts), BF16)
     return pl.pallas_call(
         partial_kernel,
-        in_specs=[SMEM, VMEM, VMEM],
-        out_specs=[VMEM] * parts,
-        out_shape=[block] * parts,
+        in_specs=[VMEM, VMEM],
+        out_specs=[VMEM] * (1 + parts),
+        out_shape=[jax.ShapeDtypeStruct((8, 128), F32)] + [block] * parts,
         compiler_params=params(24),
         cost_estimate=COST,
         name="partials",
-    )(me, tokens, weight)
+    )(tokens, weight)
 
 
 def add_kernel(*refs):
@@ -113,16 +114,15 @@
     )(scale, bits, matrix, *terms)
 
 
-def adapter(at_ref, here, share, name):
-    if name[0] == "home":
-        return at_ref[0] * here + name[1]
+def adapter(here, share, name):
+    z = lax.axis_index("adp")
     if name[0] == "plane":
-        return jnp.bitwise_xor(at_ref[0], name[1]) * here + name[2]
+        return jnp.bitwise_xor(z, name[1]) * here + name[2]
     plane, off, k = name
-    return jnp.bitwise_xor(at_ref[0], plane) * here + jnp.bitwise_xor(at_ref[1], off) * share + k
-
-
-def low_kernel(groups, here, share, rank, more, at_ref, ids_ref, tokens_ref, *refs):
+    return jnp.bitwise_xor(z, plane) * here + jnp.bitwise_xor(lax.axis_index("grp"), off) * share + k
+
+
+def low_kernel(groups, here, share, rank, more, ids_ref, tokens_ref, *refs):
     out_ref = refs[-1]
     total = refs[-2][...] if more else None
     for (start, stop), terms in groups:
@@ -130,27 +130,27 @@
         joined = rows[0] if len(rows) == 1 else jnp.concatenate(rows, axis=0)
         product = lax.dot_general(joined, tokens_ref[:, start:stop], LAST, preferred_element_type=F32)
         for n, (_, _, _, name) in enumerate(terms):
-            mine = ids_ref[...] == adapter(at_ref, here, share, name)
+            mine = ids_ref[...] == adapter(here, share, name)
             term = jnp.where(mine, product[n * rank : (n + 1) * rank], 0.0)
             total = term if total is None else total + term
     out_ref[...] = total.astype(out_ref.dtype)
 
 
-def low_rows(at, ids, tokens, here, share, groups, arrays, before, dtype):
+def low_rows(ids, tokens, here, share, groups, arrays, before, dtype):
     rank = arrays[0].shape[1]
     more = [] if before is None else [before]
     return pl.pallas_call(
         functools.partial(low_kernel, groups, here, share, rank, bool(more)),
-        in_specs=[SMEM] + [VMEM] * (2 + len(arrays) + len(more)),
+        in_specs=[VMEM] * (2 + len(arrays) + len(more)),
         out_specs=VMEM,
         out_shape=jax.ShapeDtypeStruct((rank, tokens.shape[0]), dtype),
         compiler_params=params(24),
         cost_estimate=COST,
         name="low_rows",
-    )(at, ids, tokens, *arrays, *more)
-
-
-def ups_kernel(terms, here, share, rank, at_ref, ids_ref, bits_ref, matrix_ref, *refs):
+    )(ids, tokens, *arrays, *more)
+
+
+def ups_kernel(terms, here, share, rank, ids_ref, bits_ref, matrix_ref, *refs):
     up_ref, mask_ref = refs[-2:]
     width = up_ref.shape[1]
     signs = (1 - 2 * bits_ref[...]).astype(F32)
@@ -158,22 +158,22 @@
     for n, (i, k, cut, name) in enumerate(terms):
         turned = rotate(refs[i][k, :, cut : cut + width].astype(F32), signs, matrix_ref[...])
         up_ref[n * rank : (n + 1) * rank, :] = jnp.concatenate(turned, axis=1).astype(BF16)
-        mine = ids == adapter(at_ref, here, share, name)
+        mine = ids == adapter(here, share, name)
         mask_ref[:, n * rank : (n + 1) * rank] = jnp.where(mine, 1.0, 0.0).astype(BF16)
 
 
-def rotated_ups(at, ids, bits, matrix, here, share, terms, arrays, width):
+def rotated_ups(ids, bits, matrix, here, share, terms, arrays, width):
     rank, rows = arrays[0].shape[1], ids.shape[1]
     every = len(terms) * rank
     return pl.pallas_call(
         functools.partial(ups_kernel, terms, here, share, rank),
-        in_specs=[SMEM] + [VMEM] * (3 + len(arrays)),
+        in_specs=[VMEM] * (3 + len(arrays)),
         out_specs=[VMEM, VMEM],
         out_shape=[jax.ShapeDtypeStruct((every, width), BF16), jax.ShapeDtypeStruct((rows, every), BF16)],
         compiler_params=params(32),
         cost_estimate=COST,
         name="rotated_ups",
-    )(at, ids, bits, matrix, *arrays)
+    )(ids, bits, matrix, *arrays)
 
 
 def final_kernel(mine_ref, theirs_ref, base_ref, up_ref, mask_ref, out_ref):
@@ -199,27 +199,25 @@
 
 def local(tokens, adapter_ids, base_weight, channel_scale, adapter_down, adapter_up, sign_bits):
     planes, groups, parts = lax.axis_size("adp"), lax.axis_size("grp"), lax.axis_size("tp")
-    z, g, me = (lax.axis_index(axis).astype(jnp.int32) for axis in ("adp", "grp", "tp"))
     features = tokens.shape[1]
     here, _, rank = adapter_down.shape
     width = adapter_up.shape[2]
     share = here // groups
     matrix = hadamard(sign_bits.shape[0])
-    bits, scale, ids, me = sign_bits[None, :], channel_scale[None, :], adapter_ids.T, me[None]
-    at = jnp.stack([z, g])
+    bits, scale, ids = sign_bits[None, :], channel_scale[None, :], adapter_ids.T
     down = jnp.swapaxes(adapter_down, 1, 2)
 
-    own = lax.dynamic_slice_in_dim(down, g * share, share, 0)
+    own = lax.dynamic_slice_in_dim(down, lax.axis_index("grp") * share, share, 0)
     near = swap(own, "adp", 1)
     mine = [(0, own)]
     bit = planes // 2
     while bit > 1:
         mine += [(plane | bit, swap(piece, "adp", bit)) for plane, piece in mine]
         bit //= 2
-    blocks = partials(me, tokens, base_weight, parts)
+    sign, *blocks = partials(tokens, base_weight, parts)
     half = parts // 2
-    near = after(near, *blocks)
-    mine = mine[:1] + [(plane, after(piece, near)) for plane, piece in mine[1:]]
+    near, _, *far = together(near, sign, *(piece for _, piece in mine[1:]))
+    mine = mine[:1] + [(plane, piece) for (plane, _), piece in zip(mine[1:], far)]
     odd = [(1, near)] + [(plane | 1, swap(piece, "adp", 1)) for plane, piece in mine[1:]]
 
     def others(pieces):
@@ -228,9 +226,10 @@
     swapped = others(odd[:1]) + others(mine[1:]) + others(odd[1:])
     held = [(plane, 0, piece) for plane, piece in odd[:1] + mine[1:] + odd[1:]]
 
-    last = mine[-1][1]
-    came = [swap(block, "tp", 1) for block in blocks[:half]]
-    sums = [[block, after(pair, last)] for block, pair in zip(blocks[half:], came)]
+    plane, off, piece = swapped[0]
+    piece, *came = together(piece, *(swap(block, "tp", 1) for block in blocks[:half]))
+    swapped[0] = plane, off, piece
+    sums = [[block, pair] for block, pair in zip(blocks[half:], came)]
     bit = 2
     while bit < parts:
         came = [swap(add(*terms), "tp", bit) for terms in sums[1::2]]
@@ -238,13 +237,16 @@
         bit *= 2
     base = rotated_base(sums[0], scale, bits, matrix)
 
-    ups = [(0, after(adapter_up, held[-1][2]))]
+    plane, off, piece = held[-1]
+    piece, up = together(piece, adapter_up)
+    held[-1] = plane, off, piece
+    ups = [(0, up)]
     bit = planes // 2
     while bit:
         ups += [(plane | bit, swap(up, "adp", bit)) for plane, up in ups]
         bit //= 2
     every = [(i, k, 0, ("plane", plane, k)) for i, (plane, _) in enumerate(ups) for k in range(here)]
-    up, mask = rotated_ups(at, ids, bits, matrix, here, share, every, [up for _, up in ups], width)
+    up, mask = rotated_ups(ids, bits, matrix, here, share, every, [up for _, up in ups], width)
 
     def terms(pieces, start):
         return [(start + i, k, 0, (plane, off, k)) for i, (plane, off, _) in enumerate(pieces) for k in range(share)]
@@ -253,14 +255,14 @@
     early = held[: len(mine)]
     middle = held[len(mine) :] + swapped[:-1]
     late = swapped[-1:]
-    home = [(0, k, 0, ("home", k)) for k in range(here)]
-    low = low_rows(at, ids, tokens, here, share, [(whole, home + terms(early, 1))], [down] + [p for *_, p in early], None, F32)
-    low = low_rows(at, ids, tokens, here, share, [(whole, terms(middle, 0))], [p for *_, p in middle], low, F32)
-    low = after(low, base, up)
-    low = low_rows(at, ids, tokens, here, share, [(whole, terms(late, 0))], [p for *_, p in late], low, BF16)
+    home = [(0, k, 0, ("plane", 0, k)) for k in range(here)]
+    low = low_rows(ids, tokens, here, share, [(whole, home + terms(early, 1))], [down] + [p for *_, p in early], None, F32)
+    low = low_rows(ids, tokens, here, share, [(whole, terms(middle, 0))], [p for *_, p in middle], low, F32)
+    low, base, up, mask = together(low, base, up, mask)
+    low = low_rows(ids, tokens, here, share, [(whole, terms(late, 0))], [p for *_, p in late], low, BF16)
     bit = 1
     while bit < parts // 2:
-        low = (low.astype(F32) + swap(low, "tp", bit).astype(F32)).astype(BF16)
+        low = add(low, swap(low, "tp", bit))
         bit *= 2
     other = swap(low, "tp", bit)
 

time: 65 us -> 50 us (0.77)
  local copies, waits for them, and re-layouts: 11.9 us -> 5.15 us
  Pallas kernels: 14.4 us -> 9.94 us
  waiting for transfers between devices: 20.5 us -> 18.3 us
  starting transfers between devices: 17.4 us -> 16.3 us
    unnamed x36 -> x18, local copies, waits for them, and re-layouts: 10.9 us -> 4.11 us
    pallas_call x3, Pallas kernels: 6.46 us -> 3.28 us  [low_rows(): pl.pallas_call(functools.partial(low_kernel, groups, here, share, rank, b...]
    ppermute x14, waiting for transfers between devices: 20.5 us -> 18.3 us  [swap(): lax.ppermute(x, axis, [(i, i ^ bit) for i in range(lax.axis_size(axis))])]
    ppermute x14, starting transfers between devices: 17.4 us -> 16.3 us  [swap(): lax.ppermute(x, axis, [(i, i ^ bit) for i in range(lax.axis_size(axis))])]
    pallas_call x1, Pallas kernels: 1.49 us -> 0.49 us  [rotated_base(): pl.pallas_call(base_kernel, in_specs=[VMEM] * (3 + len(terms)), out_specs...]
    pallas_call x1, Pallas kernels: 1.51 us -> 0.66 us  [rotated_ups(): pl.pallas_call(functools.partial(ups_kernel, terms, here, share, rank), i...]
  transfers between devices with their start and end apart: 14 -> 14, of which waited for: 5 -> 7; matrix products, arithmetic and copies ran while one was open for 2% -> 0% of each run, Pallas kernels for 12% -> 15%
where the time goes in v6:
time: 50 us; the launch traced here: 49.8 us
  waiting for transfers between devices  18.3 us (37%)
  starting transfers between devices  16.3 us (33%)
  Pallas kernels  9.94 us (20%)
  local copies, waits for them, and re-layouts  5.15 us (10%)
    ppermute x14, waiting for transfers between devices, swap(): lax.ppermute(x, axis, [(i, i ^ bit) for i in range(lax.axis_size(axis))])  18.3 us
    ppermute x14, starting transfers between devices, swap(): lax.ppermute(x, axis, [(i, i ^ bit) for i in range(lax.axis_size(axis))])  16.3 us
    unnamed x18, local copies, waits for them, and re-layouts  4.11 us
    pallas_call x1, Pallas kernels, partials(): pl.pallas_call(partial_kernel, in_specs=[VMEM, VMEM], out_specs=[VMEM] *...  3.94 us
    pallas_call x3, Pallas kernels, low_rows(): pl.pallas_call(functools.partial(low_kernel, groups, here, share, rank, b...  3.28 us
    pallas_call x1, Pallas kernels, final(): pl.pallas_call(final_kernel, in_specs=[VMEM] * 5, out_specs=VMEM, out_sha...  1.45 us
    dynamic_slice x1, local copies, waits for them, and re-layouts, local(): lax.dynamic_slice_in_dim(down, lax.axis_index('grp') * share, share, 0)  1.04 us
  transfers between devices with their start and end apart: 14, of which 7 were waited for; matrix products, arithmetic and copies ran while one was open for 0% of the time, Pallas kernels for 15%

profile of v6, /device:TPU:0, one launch (start us, length us, event | category | flops | bytes accessed | tf_op | source)
XLA Modules:
  0.0 49.8 jit_solution(15027067248300669647)
XLA Ops:
  0.0 1.0 %dynamic-slice_bitcast_fusion = bf16[1,64,2048]{2,1,0:T(8,128)(2,1)S(1)} fusion(bf16[2,2048,64]{1,2,0:T(8,128)(2,1)} %param.12, s32[]{:T(128)S(6)} %select_n.3), kind=kLoop, calls=%fused_computation | loop fusion | bytes 524292 | tf_op jit(solution)/shard_map/dynamic_slice | solution.py:210
  1.0 3.1 %collective-permute-start = (bf16[1,64,2048]{2,1,0:T(8,128)(2,1)S(1)}, bf16[1,64,2048]{2,1,0:T(8,128)(2,1)S(1)}, u32[]{:S(2)}, u32[]{:S(2)}) collective-permute-start(bf16[1,64,2048]{2,1,0:T(8,128)(2,1)S(1)} %dynamic-slice_bitcast_fusion), channel_id=1, source_target_pairs={{0,4},{4,0},{8,12},{12,8},{1,5},{5,1},{9,13},{13,9},{2,6},{6,2},{1... | collective-permute-start | bytes 786440 | tf_op jit(solution)/shard_map/ppermute | solution.py:34
  4.1 2.6 %collective-permute-start.1 = (bf16[1,64,2048]{2,1,0:T(8,128)(2,1)S(1)}, bf16[1,64,2048]{2,1,0:T(8,128)(2,1)S(1)}, u32[]{:S(2)}, u32[]{:S(2)}) collective-permute-start(bf16[1,64,2048]{2,1,0:T(8,128)(2,1)S(1)} %dynamic-slice_bitcast_fusion), channel_id=1, source_target_pairs={{0,8},{4,12},{8,0},{12,4},{1,9},{5,13},{9,1},{13,5},{2,10},{6,14},... | collective-permute-start | bytes 786440 | tf_op jit(solution)/shard_map/ppermute | solution.py:34
  6.7 1.9 %copy-done = bf16[768,2048]{1,0:T(8,128)(2,1)S(1)} copy-done((bf16[768,2048]{1,0:T(8,128)(2,1)S(1)}, bf16[768,2048]{1,0:T(8,128)(2,1)}, u32[]{:S(2)}) %copy-start) | copy-done | bytes 3145752
  8.6 2.2 %copy-done.2 = bf16[2048,1024]{1,0:T(8,128)(2,1)S(1)} copy-done((bf16[2048,1024]{1,0:T(8,128)(2,1)S(1)}, bf16[2048,1024]{1,0:T(8,128)(2,1)}, u32[]{:S(2)}) %copy-start.2) | copy-done | bytes 4194328
  10.8 3.9 %partials.1 = (f32[8,128]{1,0:T(8,128)}, bf16[768,256]{1,0:T(8,128)(2,1)S(1)}, bf16[768,256]{1,0:T(8,128)(2,1)S(1)}, bf16[768,256]{1,0:T(8,128)(2,1)S(1)}, bf16[768,256]{1,0:T(8,128)(2,1)S(1)}) custom-call(bf16[768,2048]{1,0:T(8,128)(2,1)S(1)} %copy-done, bf16[2048,1024]{1,0:T(8,128)(2,1)S(1)} %copy-done.2), custom_call_target="tpu_custom_call" | custom-call | flops 1 | bytes 1 | tf_op jit(solution)/shard_map/partials/pallas_call | solution.py:67
  14.8 0.5 %collective-permute-start.6 = (bf16[768,256]{1,0:T(8,128)(2,1)S(1)}, bf16[768,256]{1,0:T(8,128)(2,1)S(1)}, u32[]{:S(2)}, u32[]{:S(2)}) collective-permute-start(bf16[768,256]{1,0:T(8,128)(2,1)S(1)} %get-tuple-element.26), channel_id=1, source_target_pairs={{0,1},{1,0},{2,3},{3,2},{4,5},{5,4},{6,7},{7,6},{8,9},{9,8},{10,11... | collective-permute-start | bytes 1179656 | tf_op jit(solution)/shard_map/ppermute | solution.py:34
  15.3 0.7 %collective-permute-done.refs_1_ = bf16[1,64,2048]{2,1,0:T(8,128)(2,1)S(1)} collective-permute-done((bf16[1,64,2048]{2,1,0:T(8,128)(2,1)S(1)}, bf16[1,64,2048]{2,1,0:T(8,128)(2,1)S(1)}, u32[]{:S(2)}, u32[]{:S(2)}) %collective-permute-start) | collective-permute-done | bytes 262176 | tf_op jit(solution)/shard_map/ppermute | solution.py:34
  15.9 2.5 %collective-permute-done.1.refs_2_ = bf16[1,64,2048]{2,1,0:T(8,128)(2,1)S(1)} collective-permute-done((bf16[1,64,2048]{2,1,0:T(8,128)(2,1)S(1)}, bf16[1,64,2048]{2,1,0:T(8,128)(2,1)S(1)}, u32[]{:S(2)}, u32[]{:S(2)}) %collective-permute-start.1) | collective-permute-done | bytes 262176 | tf_op jit(solution)/shard_map/ppermute | solution.py:34
  18.5 1.5 %collective-permute-start.4 = (bf16[1,64,2048]{2,1,0:T(8,128)(2,1)S(1)}, bf16[1,64,2048]{2,1,0:T(8,128)(2,1)S(1)}, u32[]{:S(2)}, u32[]{:S(2)}) collective-permute-start(bf16[1,64,2048]{2,1,0:T(8,128)(2,1)S(1)} %collective-permute-done.refs_1_), channel_id=1, source_target_pairs={{0,16},{16,0},{1,17},{17,1},{2,18},{18,2},{3,19},{19,3},{4,20},{20... | collective-permute-start | bytes 786440 | tf_op jit(solution)/shard_map/ppermute | solution.py:34
  20.0 0.4 collective-permute-start.2
  20.4 4.6 %collective-permute-done.4.refs_1_ = bf16[1,64,2048]{2,1,0:T(8,128)(2,1)S(1)} collective-permute-done((bf16[1,64,2048]{2,1,0:T(8,128)(2,1)S(1)}, bf16[1,64,2048]{2,1,0:T(8,128)(2,1)S(1)}, u32[]{:S(2)}, u32[]{:S(2)}) %collective-permute-start.4) | collective-permute-done | bytes 262176 | tf_op jit(solution)/shard_map/ppermute | solution.py:34
  25.1 0.1 add.6
  25.2 2.5 %collective-permute-start.8 = (bf16[768,256]{1,0:T(8,128)(2,1)S(1)}, bf16[768,256]{1,0:T(8,128)(2,1)S(1)}, u32[]{:S(2)}, u32[]{:S(2)}) collective-permute-start(bf16[768,256]{1,0:T(8,128)(2,1)S(1)} %add.6), channel_id=1, source_target_pairs={{0,2},{1,3},{2,0},{3,1},{4,6},{5,7},{6,4},{7,5},{8,10},{9,11},{10,... | collective-permute-start | bytes 1179656 | tf_op jit(solution)/shard_map/ppermute | solution.py:34
  27.7 1.5 %collective-permute-start.7 = (bf16[1,64,2048]{2,1,0:T(8,128)(2,1)S(1)}, bf16[1,64,2048]{2,1,0:T(8,128)(2,1)S(1)}, u32[]{:S(2)}, u32[]{:S(2)}) collective-permute-start(bf16[1,64,2048]{2,1,0:T(8,128)(2,1)S(1)} %collective-permute-done.1.refs_2_), channel_id=1, source_target_pairs={{0,16},{16,0},{1,17},{17,1},{2,18},{18,2},{3,19},{19,3},{4,20},{20... | collective-permute-start | bytes 786440 | tf_op jit(solution)/shard_map/ppermute | solution.py:34
  29.2 0.5 %collective-permute-start.3 = (bf16[1,64,2048]{2,1,0:T(8,128)(2,1)S(1)}, bf16[1,64,2048]{2,1,0:T(8,128)(2,1)S(1)}, u32[]{:S(2)}, u32[]{:S(2)}) collective-permute-start(bf16[1,64,2048]{2,1,0:T(8,128)(2,1)S(1)} %collective-permute-done.2.refs_0_), channel_id=1, source_target_pairs={{0,16},{16,0},{1,17},{17,1},{2,18},{18,2},{3,19},{19,3},{4,20},{20... | collective-permute-start | bytes 786440 | tf_op jit(solution)/shard_map/ppermute | solution.py:34
  29.7 3.3 %collective-permute-start.10 = (bf16[2,64,256]{2,1,0:T(8,128)(2,1)S(1)}, bf16[2,64,256]{2,1,0:T(8,128)(2,1)S(1)}, u32[]{:S(2)}, u32[]{:S(2)}) collective-permute-start(bf16[2,64,256]{2,1,0:T(8,128)(2,1)S(1)} %copy-done.5), channel_id=1, source_target_pairs={{0,4},{4,0},{8,12},{12,8},{1,5},{5,1},{9,13},{13,9},{2,6},{6,2},{1... | collective-permute-start | bytes 196616 | tf_op jit(solution)/shard_map/ppermute | solution.py:34
  33.0 2.5 %collective-permute-done.9.refs_1_ = bf16[2,64,256]{2,1,0:T(8,128)(2,1)S(1)} collective-permute-done((bf16[2,64,256]{2,1,0:T(8,128)(2,1)S(1)}, bf16[2,64,256]{2,1,0:T(8,128)(2,1)S(1)}, u32[]{:S(2)}, u32[]{:S(2)}) %collective-permute-start.9) | collective-permute-done | bytes 65568 | tf_op jit(solution)/shard_map/ppermute | solution.py:34
  35.5 0.0 copy-start.4
  35.6 0.0 copy-start.7
  35.6 0.0 copy-start.8
  35.6 1.0 %low_rows.3.refs_3_ = f32[64,768]{1,0:T(8,128)S(1)} custom-call(s32[1,768]{1,0:T(1,128)S(1)} %bitcast.7, bf16[768,2048]{1,0:T(8,128)(2,1)S(1)} %copy-done.1, bf16[2,64,2048]{2,1,0:T(8,128)(2,1)S(1)} %bitcast.6, bf16[1,64,2048]{2,1,0:T(8,128)(2,1)S(1)} %collective-permute-done.refs_1_, bf16[1,64,2048]{2,1,0:T(8,128)(2,1)S(1)} %collective-permute-done.1.refs_2_), custom_call_target="tpu_custom_call" | custom-call | flops 1 | bytes 1 | tf_op jit(solution)/shard_map/low_rows/pallas_call | solution.py:142
  36.6 1.2 %low_rows.4.refs_1_ = f32[64,768]{1,0:T(8,128)S(1)} custom-call(s32[1,768]{1,0:T(1,128)S(1)} %bitcast.8, bf16[768,2048]{1,0:T(8,128)(2,1)S(1)} %copy-done.1, bf16[1,64,2048]{2,1,0:T(8,128)(2,1)S(1)} %collective-permute-done.2.refs_0_, bf16[1,64,2048]{2,1,0:T(8,128)(2,1)S(1)} %collective-permute-done.4.refs_1_, ...), custom_call_target="tpu_custom_call" | custom-call | flops 1 | bytes 1 | tf_op jit(solution)/shard_map/low_rows/pallas_call | solution.py:142
  37.8 2.0 %collective-permute-done.11.refs_3_ = bf16[2,64,256]{2,1,0:T(8,128)(2,1)S(1)} collective-permute-done((bf16[2,64,256]{2,1,0:T(8,128)(2,1)S(1)}, bf16[2,64,256]{2,1,0:T(8,128)(2,1)S(1)}, u32[]{:S(2)}, u32[]{:S(2)}) %collective-permute-start.11) | collective-permute-done | bytes 65568 | tf_op jit(solution)/shard_map/ppermute | solution.py:34
  39.8 0.7 %rotated_ups.1 = (bf16[512,256]{1,0:T(8,128)(2,1)S(1)}, bf16[768,512]{1,0:T(8,128)(2,1)S(1)}) custom-call(s32[1,768]{1,0:T(1,128)S(1)} %bitcast.9, s32[1,128]{1,0:T(1,128)S(1)} %bitcast.11, bf16[128,128]{1,0:T(8,128)(2,1)S(1)} %copy-done.4, bf16[2,64,256]{2,1,0:T(8,128)(2,1)S(1)} %copy-done.5, bf16[2,64,256]{2,1,0:T(8,128)(2,1)S(1)} %collective-permute-done.9.refs_1_, ...), custom_call_target="tpu_custom_call" | custom-call | flops 1 | bytes 1 | tf_op jit(solution)/shard_map/rotated_ups/pallas_call | solution.py:168
  40.5 0.5 rotated_base.1.base_ref
  41.0 1.1 %low_rows.5.refs_0_ = bf16[64,768]{1,0:T(8,128)(2,1)S(1)} custom-call(s32[1,768]{1,0:T(1,128)S(1)} %bitcast.10, bf16[768,2048]{1,0:T(8,128)(2,1)S(1)} %copy-done.1, bf16[1,64,2048]{2,1,0:T(8,128)(2,1)S(1)} %collective-permute-done.3.refs_0_, f32[64,768]{1,0:T(8,128)S(1)} %low_rows.4.refs_1_), custom_call_target="tpu_custom_call" | custom-call | flops 1 | bytes 1 | tf_op jit(solution)/shard_map/low_rows/pallas_call | solution.py:142
  42.1 0.1 collective-permute-start.12
  42.1 1.3 %collective-permute-done.12.refs_1_ = bf16[64,768]{1,0:T(8,128)(2,1)S(1)} collective-permute-done((bf16[64,768]{1,0:T(8,128)(2,1)S(1)}, bf16[64,768]{1,0:T(8,128)(2,1)S(1)}, u32[]{:S(2)}, u32[]{:S(2)}) %collective-permute-start.12) | collective-permute-done | bytes 98336 | tf_op jit(solution)/shard_map/ppermute | solution.py:34
  43.5 0.2 collective-permute-start.13
  43.7 4.7 %collective-permute-done.13.theirs_ref = bf16[64,768]{1,0:T(8,128)(2,1)S(1)} collective-permute-done((bf16[64,768]{1,0:T(8,128)(2,1)S(1)}, bf16[64,768]{1,0:T(8,128)(2,1)S(1)}, u32[]{:S(2)}, u32[]{:S(2)}) %collective-permute-start.13) | collective-permute-done | bytes 98336 | tf_op jit(solution)/shard_map/ppermute | solution.py:34
  48.4 1.5 %final.1 = bf16[768,256]{1,0:T(8,128)(2,1)} custom-call(bf16[64,768]{1,0:T(8,128)(2,1)S(1)} %add.7.mine_ref, bf16[64,768]{1,0:T(8,128)(2,1)S(1)} %collective-permute-done.13.theirs_ref, f32[768,256]{1,0:T(8,128)S(1)} %rotated_base.1.base_ref, bf16[512,256]{1,0:T(8,128)(2,1)S(1)} %get-tuple-element.37.up_ref, bf16[768,512]{1,0:T(8,128)(2,1)S(1)} %get-tuple-element.38.mask_ref), custom_call_target="tpu_custom_call" | custom-call | flops 1 | bytes 1 | tf_op jit(solution)/shard_map/final/pallas_call | solution.py:189
  (24 shorter events, 0.1 us)
Async XLA Ops:
  0.0 35.5 %copy-start.3 = (bf16[2,2048,64]{1,2,0:T(8,128)(2,1)S(1)}, bf16[2,2048,64]{1,2,0:T(8,128)(2,1)}, u32[]{:S(2)}) copy-start(bf16[2,2048,64]{1,2,0:T(8,128)(2,1)} %param.12) | copy-start | bytes 1572868
  1.0 14.9 %collective-permute-start = (bf16[1,64,2048]{2,1,0:T(8,128)(2,1)S(1)}, bf16[1,64,2048]{2,1,0:T(8,128)(2,1)S(1)}, u32[]{:S(2)}, u32[]{:S(2)}) collective-permute-start(bf16[1,64,2048]{2,1,0:T(8,128)(2,1)S(1)} %dynamic-slice_bitcast_fusion), channel_id=1, source_target_pairs={{0,4},{4,0},{8,12},{12,8},{1,5},{5,1},{9,13},{13,9},{2,6},{6,2},{1... | collective-permute-start | bytes 786440 | tf_op jit(solution)/shard_map/ppermute | solution.py:34
  4.1 14.3 %collective-permute-start.1 = (bf16[1,64,2048]{2,1,0:T(8,128)(2,1)S(1)}, bf16[1,64,2048]{2,1,0:T(8,128)(2,1)S(1)}, u32[]{:S(2)}, u32[]{:S(2)}) collective-permute-start(bf16[1,64,2048]{2,1,0:T(8,128)(2,1)S(1)} %dynamic-slice_bitcast_fusion), channel_id=1, source_target_pairs={{0,8},{4,12},{8,0},{12,4},{1,9},{5,13},{9,1},{13,5},{2,10},{6,14},... | collective-permute-start | bytes 786440 | tf_op jit(solution)/shard_map/ppermute | solution.py:34
  6.7 1.9 %copy-start = (bf16[768,2048]{1,0:T(8,128)(2,1)S(1)}, bf16[768,2048]{1,0:T(8,128)(2,1)}, u32[]{:S(2)}) copy-start(bf16[768,2048]{1,0:T(8,128)(2,1)} %tokens_ref.7) | copy-start | bytes 9437188
  8.6 2.2 %copy-start.2 = (bf16[2048,1024]{1,0:T(8,128)(2,1)S(1)}, bf16[2048,1024]{1,0:T(8,128)(2,1)}, u32[]{:S(2)}) copy-start(bf16[2048,1024]{1,0:T(8,128)(2,1)} %weight_ref.1) | copy-start | bytes 12582916
  10.8 18.9 %copy-start.5 = (bf16[2,64,256]{2,1,0:T(8,128)(2,1)S(1)}, bf16[2,64,256]{2,1,0:T(8,128)(2,1)}, u32[]{:S(2)}) copy-start(bf16[2,64,256]{2,1,0:T(8,128)(2,1)} %refs_0_) | copy-start | bytes 196612
  10.8 24.7 %copy-start.1 = (bf16[768,2048]{1,0:T(8,128)(2,1)S(1)}, bf16[768,2048]{1,0:T(8,128)(2,1)}, u32[]{:S(2)}) copy-start(bf16[768,2048]{1,0:T(8,128)(2,1)} %tokens_ref.7) | copy-start | bytes 9437188
  10.8 24.7 %copy-start.6 = (s32[768,1]{0,1:T(1,128)S(1)}, s32[768,1]{0,1:T(1,128)}, u32[]{:S(2)}) copy-start(s32[768,1]{0,1:T(1,128)} %param.9) | copy-start | bytes 9220
  14.7 5.7 %collective-permute-start.5 = (bf16[768,256]{1,0:T(8,128)(2,1)S(1)}, bf16[768,256]{1,0:T(8,128)(2,1)S(1)}, u32[]{:S(2)}, u32[]{:S(2)}) collective-permute-start(bf16[768,256]{1,0:T(8,128)(2,1)S(1)} %get-tuple-element.25), channel_id=1, source_target_pairs={{0,1},{1,0},{2,3},{3,2},{4,5},{5,4},{6,7},{7,6},{8,9},{9,8},{10,11... | collective-permute-start | bytes 1179656 | tf_op jit(solution)/shard_map/ppermute | solution.py:34
  14.8 5.7 %collective-permute-start.6 = (bf16[768,256]{1,0:T(8,128)(2,1)S(1)}, bf16[768,256]{1,0:T(8,128)(2,1)S(1)}, u32[]{:S(2)}, u32[]{:S(2)}) collective-permute-start(bf16[768,256]{1,0:T(8,128)(2,1)S(1)} %get-tuple-element.26), channel_id=1, source_target_pairs={{0,1},{1,0},{2,3},{3,2},{4,5},{5,4},{6,7},{7,6},{8,9},{9,8},{10,11... | collective-permute-start | bytes 1179656 | tf_op jit(solution)/shard_map/ppermute | solution.py:34
  18.5 6.6 %collective-permute-start.4 = (bf16[1,64,2048]{2,1,0:T(8,128)(2,1)S(1)}, bf16[1,64,2048]{2,1,0:T(8,128)(2,1)S(1)}, u32[]{:S(2)}, u32[]{:S(2)}) collective-permute-start(bf16[1,64,2048]{2,1,0:T(8,128)(2,1)S(1)} %collective-permute-done.refs_1_), channel_id=1, source_target_pairs={{0,16},{16,0},{1,17},{17,1},{2,18},{18,2},{3,19},{19,3},{4,20},{20... | collective-permute-start | bytes 786440 | tf_op jit(solution)/shard_map/ppermute | solution.py:34
  20.0 9.2 %collective-permute-start.2 = (bf16[1,64,2048]{2,1,0:T(8,128)(2,1)S(1)}, bf16[1,64,2048]{2,1,0:T(8,128)(2,1)S(1)}, u32[]{:S(2)}, u32[]{:S(2)}) collective-permute-start(bf16[1,64,2048]{2,1,0:T(8,128)(2,1)S(1)} %collective-permute-done.1.refs_2_), channel_id=1, source_target_pairs={{0,4},{4,0},{8,12},{12,8},{1,5},{5,1},{9,13},{13,9},{2,6},{6,2},{1... | collective-permute-start | bytes 786440 | tf_op jit(solution)/shard_map/ppermute | solution.py:34
  25.2 15.3 %collective-permute-start.8 = (bf16[768,256]{1,0:T(8,128)(2,1)S(1)}, bf16[768,256]{1,0:T(8,128)(2,1)S(1)}, u32[]{:S(2)}, u32[]{:S(2)}) collective-permute-start(bf16[768,256]{1,0:T(8,128)(2,1)S(1)} %add.6), channel_id=1, source_target_pairs={{0,2},{1,3},{2,0},{3,1},{4,6},{5,7},{6,4},{7,5},{8,10},{9,11},{10,... | collective-permute-start | bytes 1179656 | tf_op jit(solution)/shard_map/ppermute | solution.py:34
  27.7 8.9 %collective-permute-start.7 = (bf16[1,64,2048]{2,1,0:T(8,128)(2,1)S(1)}, bf16[1,64,2048]{2,1,0:T(8,128)(2,1)S(1)}, u32[]{:S(2)}, u32[]{:S(2)}) collective-permute-start(bf16[1,64,2048]{2,1,0:T(8,128)(2,1)S(1)} %collective-permute-done.1.refs_2_), channel_id=1, source_target_pairs={{0,16},{16,0},{1,17},{17,1},{2,18},{18,2},{3,19},{19,3},{4,20},{20... | collective-permute-start | bytes 786440 | tf_op jit(solution)/shard_map/ppermute | solution.py:34
  29.2 11.8 %collective-permute-start.3 = (bf16[1,64,2048]{2,1,0:T(8,128)(2,1)S(1)}, bf16[1,64,2048]{2,1,0:T(8,128)(2,1)S(1)}, u32[]{:S(2)}, u32[]{:S(2)}) collective-permute-start(bf16[1,64,2048]{2,1,0:T(8,128)(2,1)S(1)} %collective-permute-done.2.refs_0_), channel_id=1, source_target_pairs={{0,16},{16,0},{1,17},{17,1},{2,18},{18,2},{3,19},{19,3},{4,20},{20... | collective-permute-start | bytes 786440 | tf_op jit(solution)/shard_map/ppermute | solution.py:34
  29.7 5.8 %collective-permute-start.9 = (bf16[2,64,256]{2,1,0:T(8,128)(2,1)S(1)}, bf16[2,64,256]{2,1,0:T(8,128)(2,1)S(1)}, u32[]{:S(2)}, u32[]{:S(2)}) collective-permute-start(bf16[2,64,256]{2,1,0:T(8,128)(2,1)S(1)} %copy-done.5), channel_id=1, source_target_pairs={{0,8},{4,12},{8,0},{12,4},{1,9},{5,13},{9,1},{13,5},{2,10},{6,14},... | collective-permute-start | bytes 196616 | tf_op jit(solution)/shard_map/ppermute | solution.py:34
  29.7 8.1 %collective-permute-start.10 = (bf16[2,64,256]{2,1,0:T(8,128)(2,1)S(1)}, bf16[2,64,256]{2,1,0:T(8,128)(2,1)S(1)}, u32[]{:S(2)}, u32[]{:S(2)}) collective-permute-start(bf16[2,64,256]{2,1,0:T(8,128)(2,1)S(1)} %copy-done.5), channel_id=1, source_target_pairs={{0,4},{4,0},{8,12},{12,8},{1,5},{5,1},{9,13},{13,9},{2,6},{6,2},{1... | collective-permute-start | bytes 196616 | tf_op jit(solution)/shard_map/ppermute | solution.py:34
  35.5 4.3 %collective-permute-start.11 = (bf16[2,64,256]{2,1,0:T(8,128)(2,1)S(1)}, bf16[2,64,256]{2,1,0:T(8,128)(2,1)S(1)}, u32[]{:S(2)}, u32[]{:S(2)}) collective-permute-start(bf16[2,64,256]{2,1,0:T(8,128)(2,1)S(1)} %collective-permute-done.9.refs_1_), channel_id=1, source_target_pairs={{0,4},{4,0},{8,12},{12,8},{1,5},{5,1},{9,13},{13,9},{2,6},{6,2},{1... | collective-permute-start | bytes 196616 | tf_op jit(solution)/shard_map/ppermute | solution.py:34
  35.5 4.2 %copy-start.4 = (bf16[128,128]{1,0:T(8,128)(2,1)S(1)}, bf16[128,128]{1,0:T(8,128)(2,1)}, u32[]{:S(2)}) copy-start(bf16[128,128]{1,0:T(8,128)(2,1)} %constant.12.clone.matrix_ref) | copy-start | bytes 98308
  35.6 4.2 %copy-start.7 = (s32[128]{0:T(128)S(1)}, s32[128]{0:T(128)}, u32[]{:S(2)}) copy-start(s32[128]{0:T(128)} %param.14) | copy-start | bytes 1540
  35.6 4.9 %copy-start.8 = (f32[256]{0:T(256)S(1)}, f32[256]{0:T(256)}, u32[]{:S(2)}) copy-start(f32[256]{0:T(256)} %param.11) | copy-start | bytes 3076
  42.1 1.4 %collective-permute-start.12 = (bf16[64,768]{1,0:T(8,128)(2,1)S(1)}, bf16[64,768]{1,0:T(8,128)(2,1)S(1)}, u32[]{:S(2)}, u32[]{:S(2)}) collective-permute-start(bf16[64,768]{1,0:T(8,128)(2,1)S(1)} %low_rows.5.refs_0_), channel_id=1, source_target_pairs={{0,1},{1,0},{2,3},{3,2},{4,5},{5,4},{6,7},{7,6},{8,9},{9,8},{10,11... | collective-permute-start | bytes 294920 | tf_op jit(solution)/shard_map/ppermute | solution.py:34
  43.5 4.9 %collective-permute-start.13 = (bf16[64,768]{1,0:T(8,128)(2,1)S(1)}, bf16[64,768]{1,0:T(8,128)(2,1)S(1)}, u32[]{:S(2)}, u32[]{:S(2)}) collective-permute-start(bf16[64,768]{1,0:T(8,128)(2,1)S(1)} %add.7.mine_ref), channel_id=1, source_target_pairs={{0,2},{1,3},{2,0},{3,1},{4,6},{5,7},{6,4},{7,5},{8,10},{9,11},{10,... | collective-permute-start | bytes 294920 | tf_op jit(solution)/shard_map/ppermute | solution.py:34

commit v7 on v6

--- a/solution.py
+++ b/solution.py
@@ -19,6 +19,7 @@
 
 
 COST = pl.CostEstimate(flops=1, bytes_accessed=1, transcendentals=0)
+SOME = pl.CostEstimate(flops=5_000_000_000, bytes_accessed=1, transcendentals=0)
 
 
 def hadamard(size):
@@ -136,7 +137,7 @@
     out_ref[...] = total.astype(out_ref.dtype)
 
 
-def low_rows(ids, tokens, here, share, groups, arrays, before, dtype):
+def low_rows(ids, tokens, here, share, groups, arrays, before, dtype, cost=COST):
     rank = arrays[0].shape[1]
     more = [] if before is None else [before]
     return pl.pallas_call(
@@ -145,7 +146,7 @@
         out_specs=VMEM,
         out_shape=jax.ShapeDtypeStruct((rank, tokens.shape[0]), dtype),
         compiler_params=params(24),
-        cost_estimate=COST,
+        cost_estimate=cost,
         name="low_rows",
     )(ids, tokens, *arrays, *more)
 
@@ -226,9 +227,18 @@
     swapped = others(odd[:1]) + others(mine[1:]) + others(odd[1:])
     held = [(plane, 0, piece) for plane, piece in odd[:1] + mine[1:] + odd[1:]]
 
-    plane, off, piece = swapped[0]
-    piece, *came = together(piece, *(swap(block, "tp", 1) for block in blocks[:half]))
-    swapped[0] = plane, off, piece
+    def terms(pieces, start):
+        return [(start + i, k, 0, (plane, off, k)) for i, (plane, off, _) in enumerate(pieces) for k in range(share)]
+
+    whole = (0, features)
+    early = held[: len(mine)]
+    middle = held[len(mine) :] + swapped[:-1]
+    late = swapped[-1:]
+    home = [(0, k, 0, ("plane", 0, k)) for k in range(here)]
+    first = [(whole, home + terms(early, 1))]
+    low = low_rows(ids, tokens, here, share, first, [down] + [p for *_, p in early], None, F32, SOME)
+
+    low, *came = together(low, *(swap(block, "tp", 1) for block in blocks[:half]))
     sums = [[block, pair] for block, pair in zip(blocks[half:], came)]
     bit = 2
     while bit < parts:
@@ -237,9 +247,9 @@
         bit *= 2
     base = rotated_base(sums[0], scale, bits, matrix)
 
-    plane, off, piece = held[-1]
+    plane, off, piece = middle[-len(swapped) + 1]
     piece, up = together(piece, adapter_up)
-    held[-1] = plane, off, piece
+    middle[-len(swapped) + 1] = plane, off, piece
     ups = [(0, up)]
     bit = planes // 2
     while bit:
@@ -248,15 +258,6 @@
     every = [(i, k, 0, ("plane", plane, k)) for i, (plane, _) in enumerate(ups) for k in range(here)]
     up, mask = rotated_ups(ids, bits, matrix, here, share, every, [up for _, up in ups], width)
 
-    def terms(pieces, start):
-        return [(start + i, k, 0, (plane, off, k)) for i, (plane, off, _) in enumerate(pieces) for k in range(share)]
-
-    whole = (0, features)
-    early = held[: len(mine)]
-    middle = held[len(mine) :] + swapped[:-1]
-    late = swapped[-1:]
-    home = [(0, k, 0, ("plane", 0, k)) for k in range(here)]
-    low = low_rows(ids, tokens, here, share, [(whole, home + terms(early, 1))], [down] + [p for *_, p in early], None, F32)
     low = low_rows(ids, tokens, here, share, [(whole, terms(middle, 0))], [p for *_, p in middle], low, F32)
     low, base, up, mask = together(low, base, up, mask)
     low = low_rows(ids, tokens, here, share, [(whole, terms(late, 0))], [p for *_, p in late], low, BF16)

time: 50 us -> 47.6 us (0.952)
  waiting for transfers between devices: 18.3 us -> 13.6 us
  starting transfers between devices: 16.3 us -> 18.6 us
    ppermute x14, waiting for transfers between devices: 18.3 us -> 13.6 us  [swap(): lax.ppermute(x, axis, [(i, i ^ bit) for i in range(lax.axis_size(axis))])]
    ppermute x14, starting transfers between devices: 16.3 us -> 18.6 us  [swap(): lax.ppermute(x, axis, [(i, i ^ bit) for i in range(lax.axis_size(axis))])]
  transfers between devices with their start and end apart: 14 -> 14, of which waited for: 7 -> 8; matrix products, arithmetic and copies ran while one was open for 0% -> 0% of each run, Pallas kernels for 15% -> 16%
where the time goes in v7:
time: 47.6 us; the launch traced here: 47.4 us
  starting transfers between devices  18.6 us (39%)
  waiting for transfers between devices  13.6 us (29%)
  Pallas kernels  9.93 us (21%)
  local copies, waits for them, and re-layouts  5.15 us (11%)
    ppermute x14, starting transfers between devices, swap(): lax.ppermute(x, axis, [(i, i ^ bit) for i in range(lax.axis_size(axis))])  18.6 us
    ppermute x14, waiting for transfers between devices, swap(): lax.ppermute(x, axis, [(i, i ^ bit) for i in range(lax.axis_size(axis))])  13.6 us
    unnamed x18, local copies, waits for them, and re-layouts  4.11 us
    pallas_call x1, Pallas kernels, partials(): pl.pallas_call(partial_kernel, in_specs=[VMEM, VMEM], out_specs=[VMEM] *...  3.94 us
    pallas_call x3, Pallas kernels, low_rows(): pl.pallas_call(functools.partial(low_kernel, groups, here, share, rank, b...  3.28 us
    pallas_call x1, Pallas kernels, final(): pl.pallas_call(final_kernel, in_specs=[VMEM] * 5, out_specs=VMEM, out_sha...  1.45 us
    dynamic_slice x1, local copies, waits for them, and re-layouts, local(): lax.dynamic_slice_in_dim(down, lax.axis_index('grp') * share, share, 0)  1.04 us
  transfers between devices with their start and end apart: 14, of which 8 were waited for; matrix products, arithmetic and copies ran while one was open for 0% of the time, Pallas kernels for 16%

profile of v7, /device:TPU:0, one launch (start us, length us, event | category | flops | bytes accessed | tf_op | source)
XLA Modules:
  0.0 47.4 jit_solution(738512615617873825)
XLA Ops:
  0.0 1.0 %dynamic-slice_bitcast_fusion = bf16[1,64,2048]{2,1,0:T(8,128)(2,1)S(1)} fusion(bf16[2,2048,64]{1,2,0:T(8,128)(2,1)} %param.12, s32[]{:T(128)S(6)} %select_n.3), kind=kLoop, calls=%fused_computation | loop fusion | bytes 524292 | tf_op jit(solution)/shard_map/dynamic_slice | solution.py:211
  1.0 3.1 %collective-permute-start = (bf16[1,64,2048]{2,1,0:T(8,128)(2,1)S(1)}, bf16[1,64,2048]{2,1,0:T(8,128)(2,1)S(1)}, u32[]{:S(2)}, u32[]{:S(2)}) collective-permute-start(bf16[1,64,2048]{2,1,0:T(8,128)(2,1)S(1)} %dynamic-slice_bitcast_fusion), channel_id=1, source_target_pairs={{0,4},{4,0},{8,12},{12,8},{1,5},{5,1},{9,13},{13,9},{2,6},{6,2},{1... | collective-permute-start | bytes 786440 | tf_op jit(solution)/shard_map/ppermute | solution.py:35
  4.1 2.6 %collective-permute-start.1 = (bf16[1,64,2048]{2,1,0:T(8,128)(2,1)S(1)}, bf16[1,64,2048]{2,1,0:T(8,128)(2,1)S(1)}, u32[]{:S(2)}, u32[]{:S(2)}) collective-permute-start(bf16[1,64,2048]{2,1,0:T(8,128)(2,1)S(1)} %dynamic-slice_bitcast_fusion), channel_id=1, source_target_pairs={{0,8},{4,12},{8,0},{12,4},{1,9},{5,13},{9,1},{13,5},{2,10},{6,14},... | collective-permute-start | bytes 786440 | tf_op jit(solution)/shard_map/ppermute | solution.py:35
  6.7 1.9 %copy-done = bf16[768,2048]{1,0:T(8,128)(2,1)S(1)} copy-done((bf16[768,2048]{1,0:T(8,128)(2,1)S(1)}, bf16[768,2048]{1,0:T(8,128)(2,1)}, u32[]{:S(2)}) %copy-start) | copy-done | bytes 3145752
  8.6 2.2 %copy-done.2 = bf16[2048,1024]{1,0:T(8,128)(2,1)S(1)} copy-done((bf16[2048,1024]{1,0:T(8,128)(2,1)S(1)}, bf16[2048,1024]{1,0:T(8,128)(2,1)}, u32[]{:S(2)}) %copy-start.2) | copy-done | bytes 4194328
  10.8 3.9 %partials.1 = (f32[8,128]{1,0:T(8,128)}, bf16[768,256]{1,0:T(8,128)(2,1)S(1)}, bf16[768,256]{1,0:T(8,128)(2,1)S(1)}, bf16[768,256]{1,0:T(8,128)(2,1)S(1)}, bf16[768,256]{1,0:T(8,128)(2,1)S(1)}) custom-call(bf16[768,2048]{1,0:T(8,128)(2,1)S(1)} %copy-done, bf16[2048,1024]{1,0:T(8,128)(2,1)S(1)} %copy-done.2), custom_call_target="tpu_custom_call" | custom-call | flops 1 | bytes 1 | tf_op jit(solution)/shard_map/partials/pallas_call | solution.py:68
  14.7 0.5 %collective-permute-start.7 = (bf16[768,256]{1,0:T(8,128)(2,1)S(1)}, bf16[768,256]{1,0:T(8,128)(2,1)S(1)}, u32[]{:S(2)}, u32[]{:S(2)}) collective-permute-start(bf16[768,256]{1,0:T(8,128)(2,1)S(1)} %get-tuple-element.26), channel_id=1, source_target_pairs={{0,1},{1,0},{2,3},{3,2},{4,5},{5,4},{6,7},{7,6},{8,9},{9,8},{10,11... | collective-permute-start | bytes 1179656 | tf_op jit(solution)/shard_map/ppermute | solution.py:35
  15.3 0.7 %collective-permute-done.refs_1_ = bf16[1,64,2048]{2,1,0:T(8,128)(2,1)S(1)} collective-permute-done((bf16[1,64,2048]{2,1,0:T(8,128)(2,1)S(1)}, bf16[1,64,2048]{2,1,0:T(8,128)(2,1)S(1)}, u32[]{:S(2)}, u32[]{:S(2)}) %collective-permute-start) | collective-permute-done | bytes 262176 | tf_op jit(solution)/shard_map/ppermute | solution.py:35
  15.9 2.5 %collective-permute-done.1.refs_2_ = bf16[1,64,2048]{2,1,0:T(8,128)(2,1)S(1)} collective-permute-done((bf16[1,64,2048]{2,1,0:T(8,128)(2,1)S(1)}, bf16[1,64,2048]{2,1,0:T(8,128)(2,1)S(1)}, u32[]{:S(2)}, u32[]{:S(2)}) %collective-permute-start.1) | collective-permute-done | bytes 262176 | tf_op jit(solution)/shard_map/ppermute | solution.py:35
  18.5 0.4 collective-permute-start.2
  18.9 1.5 %collective-permute-start.4 = (bf16[1,64,2048]{2,1,0:T(8,128)(2,1)S(1)}, bf16[1,64,2048]{2,1,0:T(8,128)(2,1)S(1)}, u32[]{:S(2)}, u32[]{:S(2)}) collective-permute-start(bf16[1,64,2048]{2,1,0:T(8,128)(2,1)S(1)} %collective-permute-done.refs_1_), channel_id=1, source_target_pairs={{0,16},{16,0},{1,17},{17,1},{2,18},{18,2},{3,19},{19,3},{4,20},{20... | collective-permute-start | bytes 786440 | tf_op jit(solution)/shard_map/ppermute | solution.py:35
  20.4 1.0 %low_rows.3.refs_3_ = f32[64,768]{1,0:T(8,128)S(1)} custom-call(s32[1,768]{1,0:T(1,128)S(1)} %bitcast.7, bf16[768,2048]{1,0:T(8,128)(2,1)S(1)} %copy-done.1, bf16[2,64,2048]{2,1,0:T(8,128)(2,1)S(1)} %bitcast.6, bf16[1,64,2048]{2,1,0:T(8,128)(2,1)S(1)} %collective-permute-done.refs_1_, bf16[1,64,2048]{2,1,0:T(8,128)(2,1)S(1)} %collective-permute-done.1.refs_2_), custom_call_target="tpu_custom_call" | custom-call | flops 5000000000 | bytes 1 | tf_op jit(solution)/shard_map/low_rows/pallas_call | solution.py:143
  21.5 0.0 copy-start.3
  21.5 0.1 add.6
  21.6 1.6 %collective-permute-start.8 = (bf16[768,256]{1,0:T(8,128)(2,1)S(1)}, bf16[768,256]{1,0:T(8,128)(2,1)S(1)}, u32[]{:S(2)}, u32[]{:S(2)}) collective-permute-start(bf16[768,256]{1,0:T(8,128)(2,1)S(1)} %add.6), channel_id=1, source_target_pairs={{0,2},{1,3},{2,0},{3,1},{4,6},{5,7},{6,4},{7,5},{8,10},{9,11},{10,... | collective-permute-start | bytes 1179656 | tf_op jit(solution)/shard_map/ppermute | solution.py:35
  23.2 0.5 %collective-permute-start.5 = (bf16[1,64,2048]{2,1,0:T(8,128)(2,1)S(1)}, bf16[1,64,2048]{2,1,0:T(8,128)(2,1)S(1)}, u32[]{:S(2)}, u32[]{:S(2)}) collective-permute-start(bf16[1,64,2048]{2,1,0:T(8,128)(2,1)S(1)} %collective-permute-done.1.refs_2_), channel_id=1, source_target_pairs={{0,16},{16,0},{1,17},{17,1},{2,18},{18,2},{3,19},{19,3},{4,20},{20... | collective-permute-start | bytes 786440 | tf_op jit(solution)/shard_map/ppermute | solution.py:35
  23.7 1.1 %collective-permute-done.2.refs_0_ = bf16[1,64,2048]{2,1,0:T(8,128)(2,1)S(1)} collective-permute-done((bf16[1,64,2048]{2,1,0:T(8,128)(2,1)S(1)}, bf16[1,64,2048]{2,1,0:T(8,128)(2,1)S(1)}, u32[]{:S(2)}, u32[]{:S(2)}) %collective-permute-start.2) | collective-permute-done | bytes 262176 | tf_op jit(solution)/shard_map/ppermute | solution.py:35
  24.8 1.5 %collective-permute-start.3 = (bf16[1,64,2048]{2,1,0:T(8,128)(2,1)S(1)}, bf16[1,64,2048]{2,1,0:T(8,128)(2,1)S(1)}, u32[]{:S(2)}, u32[]{:S(2)}) collective-permute-start(bf16[1,64,2048]{2,1,0:T(8,128)(2,1)S(1)} %collective-permute-done.2.refs_0_), channel_id=1, source_target_pairs={{0,16},{16,0},{1,17},{17,1},{2,18},{18,2},{3,19},{19,3},{4,20},{20... | collective-permute-start | bytes 786440 | tf_op jit(solution)/shard_map/ppermute | solution.py:35
  26.4 1.3 %collective-permute-done.4.refs_1_ = bf16[1,64,2048]{2,1,0:T(8,128)(2,1)S(1)} collective-permute-done((bf16[1,64,2048]{2,1,0:T(8,128)(2,1)S(1)}, bf16[1,64,2048]{2,1,0:T(8,128)(2,1)S(1)}, u32[]{:S(2)}, u32[]{:S(2)}) %collective-permute-start.4) | collective-permute-done | bytes 262176 | tf_op jit(solution)/shard_map/ppermute | solution.py:35
  27.6 3.1 %collective-permute-start.9 = (bf16[2,64,256]{2,1,0:T(8,128)(2,1)S(1)}, bf16[2,64,256]{2,1,0:T(8,128)(2,1)S(1)}, u32[]{:S(2)}, u32[]{:S(2)}) collective-permute-start(bf16[2,64,256]{2,1,0:T(8,128)(2,1)S(1)} %copy-done.5), channel_id=1, source_target_pairs={{0,8},{4,12},{8,0},{12,4},{1,9},{5,13},{9,1},{13,5},{2,10},{6,14},... | collective-permute-start | bytes 196616 | tf_op jit(solution)/shard_map/ppermute | solution.py:35
  30.8 2.2 %collective-permute-done.9.refs_1_ = bf16[2,64,256]{2,1,0:T(8,128)(2,1)S(1)} collective-permute-done((bf16[2,64,256]{2,1,0:T(8,128)(2,1)S(1)}, bf16[2,64,256]{2,1,0:T(8,128)(2,1)S(1)}, u32[]{:S(2)}, u32[]{:S(2)}) %collective-permute-start.9) | collective-permute-done | bytes 65568 | tf_op jit(solution)/shard_map/ppermute | solution.py:35
  33.0 1.8 %collective-permute-start.11 = (bf16[2,64,256]{2,1,0:T(8,128)(2,1)S(1)}, bf16[2,64,256]{2,1,0:T(8,128)(2,1)S(1)}, u32[]{:S(2)}, u32[]{:S(2)}) collective-permute-start(bf16[2,64,256]{2,1,0:T(8,128)(2,1)S(1)} %collective-permute-done.9.refs_1_), channel_id=1, source_target_pairs={{0,4},{4,0},{8,12},{12,8},{1,5},{5,1},{9,13},{13,9},{2,6},{6,2},{1... | collective-permute-start | bytes 196616 | tf_op jit(solution)/shard_map/ppermute | solution.py:35
  34.8 1.2 %low_rows.4.refs_1_ = f32[64,768]{1,0:T(8,128)S(1)} custom-call(s32[1,768]{1,0:T(1,128)S(1)} %bitcast.8, bf16[768,2048]{1,0:T(8,128)(2,1)S(1)} %copy-done.1, bf16[1,64,2048]{2,1,0:T(8,128)(2,1)S(1)} %collective-permute-done.2.refs_0_, bf16[1,64,2048]{2,1,0:T(8,128)(2,1)S(1)} %collective-permute-done.4.refs_1_, ...), custom_call_target="tpu_custom_call" | custom-call | flops 1 | bytes 1 | tf_op jit(solution)/shard_map/low_rows/pallas_call | solution.py:143
  36.0 1.3 %collective-permute-done.11.refs_3_ = bf16[2,64,256]{2,1,0:T(8,128)(2,1)S(1)} collective-permute-done((bf16[2,64,256]{2,1,0:T(8,128)(2,1)S(1)}, bf16[2,64,256]{2,1,0:T(8,128)(2,1)S(1)}, u32[]{:S(2)}, u32[]{:S(2)}) %collective-permute-start.11) | collective-permute-done | bytes 65568 | tf_op jit(solution)/shard_map/ppermute | solution.py:35
  37.3 0.7 %rotated_ups.1 = (bf16[512,256]{1,0:T(8,128)(2,1)S(1)}, bf16[768,512]{1,0:T(8,128)(2,1)S(1)}) custom-call(s32[1,768]{1,0:T(1,128)S(1)} %bitcast.9, s32[1,128]{1,0:T(1,128)S(1)} %bitcast.11, bf16[128,128]{1,0:T(8,128)(2,1)S(1)} %copy-done.3, bf16[2,64,256]{2,1,0:T(8,128)(2,1)S(1)} %copy-done.5, bf16[2,64,256]{2,1,0:T(8,128)(2,1)S(1)} %collective-permute-done.9.refs_1_, ...), custom_call_target="tpu_custom_call" | custom-call | flops 1 | bytes 1 | tf_op jit(solution)/shard_map/rotated_ups/pallas_call | solution.py:169
  38.0 0.5 %rotated_base.1.base_ref = f32[768,256]{1,0:T(8,128)S(1)} custom-call(f32[1,256]{1,0:T(1,128)S(1)} %bitcast.13, s32[1,128]{1,0:T(1,128)S(1)} %bitcast.12, bf16[128,128]{1,0:T(8,128)(2,1)S(1)} %copy-done.3, bf16[768,256]{1,0:T(8,128)(2,1)S(1)} %get-tuple-element.28.refs_0_, bf16[768,256]{1,0:T(8,128)(2,1)S(1)} %collective-permute-done.6.refs_1_, ...), custom_call_target="tpu_custom_call" | custom-call | flops 1 | bytes 1 | tf_op jit(solution)/shard_map/rotated_base/pallas_call | solution.py:107
  38.5 1.1 %low_rows.5.refs_0_ = bf16[64,768]{1,0:T(8,128)(2,1)S(1)} custom-call(s32[1,768]{1,0:T(1,128)S(1)} %bitcast.10, bf16[768,2048]{1,0:T(8,128)(2,1)S(1)} %copy-done.1, bf16[1,64,2048]{2,1,0:T(8,128)(2,1)S(1)} %collective-permute-done.3.refs_0_, f32[64,768]{1,0:T(8,128)S(1)} %low_rows.4.refs_1_), custom_call_target="tpu_custom_call" | custom-call | flops 1 | bytes 1 | tf_op jit(solution)/shard_map/low_rows/pallas_call | solution.py:143
  39.5 0.1 collective-permute-start.12
  39.6 1.3 %collective-permute-done.12.refs_1_ = bf16[64,768]{1,0:T(8,128)(2,1)S(1)} collective-permute-done((bf16[64,768]{1,0:T(8,128)(2,1)S(1)}, bf16[64,768]{1,0:T(8,128)(2,1)S(1)}, u32[]{:S(2)}, u32[]{:S(2)}) %collective-permute-start.12) | collective-permute-done | bytes 98336 | tf_op jit(solution)/shard_map/ppermute | solution.py:35
  40.9 1.9 %collective-permute-start.13 = (bf16[64,768]{1,0:T(8,128)(2,1)S(1)}, bf16[64,768]{1,0:T(8,128)(2,1)S(1)}, u32[]{:S(2)}, u32[]{:S(2)}) collective-permute-start(bf16[64,768]{1,0:T(8,128)(2,1)S(1)} %add.7.mine_ref), channel_id=1, source_target_pairs={{0,2},{1,3},{2,0},{3,1},{4,6},{5,7},{6,4},{7,5},{8,10},{9,11},{10,... | collective-permute-start | bytes 294920 | tf_op jit(solution)/shard_map/ppermute | solution.py:35
  42.8 3.1 %collective-permute-done.13.theirs_ref = bf16[64,768]{1,0:T(8,128)(2,1)S(1)} collective-permute-done((bf16[64,768]{1,0:T(8,128)(2,1)S(1)}, bf16[64,768]{1,0:T(8,128)(2,1)S(1)}, u32[]{:S(2)}, u32[]{:S(2)}) %collective-permute-start.13) | collective-permute-done | bytes 98336 | tf_op jit(solution)/shard_map/ppermute | solution.py:35
  45.9 1.4 %final.1 = bf16[768,256]{1,0:T(8,128)(2,1)} custom-call(bf16[64,768]{1,0:T(8,128)(2,1)S(1)} %add.7.mine_ref, bf16[64,768]{1,0:T(8,128)(2,1)S(1)} %collective-permute-done.13.theirs_ref, f32[768,256]{1,0:T(8,128)S(1)} %rotated_base.1.base_ref, bf16[512,256]{1,0:T(8,128)(2,1)S(1)} %get-tuple-element.37.up_ref, bf16[768,512]{1,0:T(8,128)(2,1)S(1)} %get-tuple-element.38.mask_ref), custom_call_target="tpu_custom_call" | custom-call | flops 1 | bytes 1 | tf_op jit(solution)/shard_map/final/pallas_call | solution.py:190
  (24 shorter events, 0.1 us)
Async XLA Ops:
  0.0 20.4 %copy-start.4 = (bf16[2,2048,64]{1,2,0:T(8,128)(2,1)S(1)}, bf16[2,2048,64]{1,2,0:T(8,128)(2,1)}, u32[]{:S(2)}) copy-start(bf16[2,2048,64]{1,2,0:T(8,128)(2,1)} %param.12) | copy-start | bytes 1572868
  0.0 20.4 %copy-start.6 = (s32[768,1]{0,1:T(1,128)S(1)}, s32[768,1]{0,1:T(1,128)}, u32[]{:S(2)}) copy-start(s32[768,1]{0,1:T(1,128)} %param.9) | copy-start | bytes 9220
  1.0 14.9 %collective-permute-start = (bf16[1,64,2048]{2,1,0:T(8,128)(2,1)S(1)}, bf16[1,64,2048]{2,1,0:T(8,128)(2,1)S(1)}, u32[]{:S(2)}, u32[]{:S(2)}) collective-permute-start(bf16[1,64,2048]{2,1,0:T(8,128)(2,1)S(1)} %dynamic-slice_bitcast_fusion), channel_id=1, source_target_pairs={{0,4},{4,0},{8,12},{12,8},{1,5},{5,1},{9,13},{13,9},{2,6},{6,2},{1... | collective-permute-start | bytes 786440 | tf_op jit(solution)/shard_map/ppermute | solution.py:35
  4.1 14.3 %collective-permute-start.1 = (bf16[1,64,2048]{2,1,0:T(8,128)(2,1)S(1)}, bf16[1,64,2048]{2,1,0:T(8,128)(2,1)S(1)}, u32[]{:S(2)}, u32[]{:S(2)}) collective-permute-start(bf16[1,64,2048]{2,1,0:T(8,128)(2,1)S(1)} %dynamic-slice_bitcast_fusion), channel_id=1, source_target_pairs={{0,8},{4,12},{8,0},{12,4},{1,9},{5,13},{9,1},{13,5},{2,10},{6,14},... | collective-permute-start | bytes 786440 | tf_op jit(solution)/shard_map/ppermute | solution.py:35
  6.7 1.9 %copy-start = (bf16[768,2048]{1,0:T(8,128)(2,1)S(1)}, bf16[768,2048]{1,0:T(8,128)(2,1)}, u32[]{:S(2)}) copy-start(bf16[768,2048]{1,0:T(8,128)(2,1)} %tokens_ref.7) | copy-start | bytes 9437188
  8.6 2.2 %copy-start.2 = (bf16[2048,1024]{1,0:T(8,128)(2,1)S(1)}, bf16[2048,1024]{1,0:T(8,128)(2,1)}, u32[]{:S(2)}) copy-start(bf16[2048,1024]{1,0:T(8,128)(2,1)} %weight_ref.1) | copy-start | bytes 12582916
  10.8 9.6 %copy-start.1 = (bf16[768,2048]{1,0:T(8,128)(2,1)S(1)}, bf16[768,2048]{1,0:T(8,128)(2,1)}, u32[]{:S(2)}) copy-start(bf16[768,2048]{1,0:T(8,128)(2,1)} %tokens_ref.7) | copy-start | bytes 9437188
  14.7 6.8 %collective-permute-start.6 = (bf16[768,256]{1,0:T(8,128)(2,1)S(1)}, bf16[768,256]{1,0:T(8,128)(2,1)S(1)}, u32[]{:S(2)}, u32[]{:S(2)}) collective-permute-start(bf16[768,256]{1,0:T(8,128)(2,1)S(1)} %get-tuple-element.25), channel_id=1, source_target_pairs={{0,1},{1,0},{2,3},{3,2},{4,5},{5,4},{6,7},{7,6},{8,9},{9,8},{10,11... | collective-permute-start | bytes 1179656 | tf_op jit(solution)/shard_map/ppermute | solution.py:35
  14.7 6.8 %collective-permute-start.7 = (bf16[768,256]{1,0:T(8,128)(2,1)S(1)}, bf16[768,256]{1,0:T(8,128)(2,1)S(1)}, u32[]{:S(2)}, u32[]{:S(2)}) collective-permute-start(bf16[768,256]{1,0:T(8,128)(2,1)S(1)} %get-tuple-element.26), channel_id=1, source_target_pairs={{0,1},{1,0},{2,3},{3,2},{4,5},{5,4},{6,7},{7,6},{8,9},{9,8},{10,11... | collective-permute-start | bytes 1179656 | tf_op jit(solution)/shard_map/ppermute | solution.py:35
  18.5 6.4 %collective-permute-start.2 = (bf16[1,64,2048]{2,1,0:T(8,128)(2,1)S(1)}, bf16[1,64,2048]{2,1,0:T(8,128)(2,1)S(1)}, u32[]{:S(2)}, u32[]{:S(2)}) collective-permute-start(bf16[1,64,2048]{2,1,0:T(8,128)(2,1)S(1)} %collective-permute-done.1.refs_2_), channel_id=1, source_target_pairs={{0,4},{4,0},{8,12},{12,8},{1,5},{5,1},{9,13},{13,9},{2,6},{6,2},{1... | collective-permute-start | bytes 786440 | tf_op jit(solution)/shard_map/ppermute | solution.py:35
  18.9 8.7 %collective-permute-start.4 = (bf16[1,64,2048]{2,1,0:T(8,128)(2,1)S(1)}, bf16[1,64,2048]{2,1,0:T(8,128)(2,1)S(1)}, u32[]{:S(2)}, u32[]{:S(2)}) collective-permute-start(bf16[1,64,2048]{2,1,0:T(8,128)(2,1)S(1)} %collective-permute-done.refs_1_), channel_id=1, source_target_pairs={{0,16},{16,0},{1,17},{17,1},{2,18},{18,2},{3,19},{19,3},{4,20},{20... | collective-permute-start | bytes 786440 | tf_op jit(solution)/shard_map/ppermute | solution.py:35
  20.4 7.2 %copy-start.5 = (bf16[2,64,256]{2,1,0:T(8,128)(2,1)S(1)}, bf16[2,64,256]{2,1,0:T(8,128)(2,1)}, u32[]{:S(2)}) copy-start(bf16[2,64,256]{2,1,0:T(8,128)(2,1)} %refs_0_) | copy-start | bytes 196612
  21.5 15.8 %copy-start.3 = (bf16[128,128]{1,0:T(8,128)(2,1)S(1)}, bf16[128,128]{1,0:T(8,128)(2,1)}, u32[]{:S(2)}) copy-start(bf16[128,128]{1,0:T(8,128)(2,1)} %constant.12.clone.matrix_ref) | copy-start | bytes 98308
  21.5 15.8 %copy-start.7 = (s32[128]{0:T(128)S(1)}, s32[128]{0:T(128)}, u32[]{:S(2)}) copy-start(s32[128]{0:T(128)} %param.14) | copy-start | bytes 1540
  21.5 16.5 %copy-start.8 = (f32[256]{0:T(256)S(1)}, f32[256]{0:T(256)}, u32[]{:S(2)}) copy-start(f32[256]{0:T(256)} %param.11) | copy-start | bytes 3076
  21.6 16.3 %collective-permute-start.8 = (bf16[768,256]{1,0:T(8,128)(2,1)S(1)}, bf16[768,256]{1,0:T(8,128)(2,1)S(1)}, u32[]{:S(2)}, u32[]{:S(2)}) collective-permute-start(bf16[768,256]{1,0:T(8,128)(2,1)S(1)} %add.6), channel_id=1, source_target_pairs={{0,2},{1,3},{2,0},{3,1},{4,6},{5,7},{6,4},{7,5},{8,10},{9,11},{10,... | collective-permute-start | bytes 1179656 | tf_op jit(solution)/shard_map/ppermute | solution.py:35
  23.2 11.6 %collective-permute-start.5 = (bf16[1,64,2048]{2,1,0:T(8,128)(2,1)S(1)}, bf16[1,64,2048]{2,1,0:T(8,128)(2,1)S(1)}, u32[]{:S(2)}, u32[]{:S(2)}) collective-permute-start(bf16[1,64,2048]{2,1,0:T(8,128)(2,1)S(1)} %collective-permute-done.1.refs_2_), channel_id=1, source_target_pairs={{0,16},{16,0},{1,17},{17,1},{2,18},{18,2},{3,19},{19,3},{4,20},{20... | collective-permute-start | bytes 786440 | tf_op jit(solution)/shard_map/ppermute | solution.py:35
  24.8 13.6 %collective-permute-start.3 = (bf16[1,64,2048]{2,1,0:T(8,128)(2,1)S(1)}, bf16[1,64,2048]{2,1,0:T(8,128)(2,1)S(1)}, u32[]{:S(2)}, u32[]{:S(2)}) collective-permute-start(bf16[1,64,2048]{2,1,0:T(8,128)(2,1)S(1)} %collective-permute-done.2.refs_0_), channel_id=1, source_target_pairs={{0,16},{16,0},{1,17},{17,1},{2,18},{18,2},{3,19},{19,3},{4,20},{20... | collective-permute-start | bytes 786440 | tf_op jit(solution)/shard_map/ppermute | solution.py:35
  27.6 5.4 %collective-permute-start.9 = (bf16[2,64,256]{2,1,0:T(8,128)(2,1)S(1)}, bf16[2,64,256]{2,1,0:T(8,128)(2,1)S(1)}, u32[]{:S(2)}, u32[]{:S(2)}) collective-permute-start(bf16[2,64,256]{2,1,0:T(8,128)(2,1)S(1)} %copy-done.5), channel_id=1, source_target_pairs={{0,8},{4,12},{8,0},{12,4},{1,9},{5,13},{9,1},{13,5},{2,10},{6,14},... | collective-permute-start | bytes 196616 | tf_op jit(solution)/shard_map/ppermute | solution.py:35
  30.8 5.2 %collective-permute-start.10 = (bf16[2,64,256]{2,1,0:T(8,128)(2,1)S(1)}, bf16[2,64,256]{2,1,0:T(8,128)(2,1)S(1)}, u32[]{:S(2)}, u32[]{:S(2)}) collective-permute-start(bf16[2,64,256]{2,1,0:T(8,128)(2,1)S(1)} %copy-done.5), channel_id=1, source_target_pairs={{0,4},{4,0},{8,12},{12,8},{1,5},{5,1},{9,13},{13,9},{2,6},{6,2},{1... | collective-permute-start | bytes 196616 | tf_op jit(solution)/shard_map/ppermute | solution.py:35
  33.0 4.3 %collective-permute-start.11 = (bf16[2,64,256]{2,1,0:T(8,128)(2,1)S(1)}, bf16[2,64,256]{2,1,0:T(8,128)(2,1)S(1)}, u32[]{:S(2)}, u32[]{:S(2)}) collective-permute-start(bf16[2,64,256]{2,1,0:T(8,128)(2,1)S(1)} %collective-permute-done.9.refs_1_), channel_id=1, source_target_pairs={{0,4},{4,0},{8,12},{12,8},{1,5},{5,1},{9,13},{13,9},{2,6},{6,2},{1... | collective-permute-start | bytes 196616 | tf_op jit(solution)/shard_map/ppermute | solution.py:35
  39.5 1.4 %collective-permute-start.12 = (bf16[64,768]{1,0:T(8,128)(2,1)S(1)}, bf16[64,768]{1,0:T(8,128)(2,1)S(1)}, u32[]{:S(2)}, u32[]{:S(2)}) collective-permute-start(bf16[64,768]{1,0:T(8,128)(2,1)S(1)} %low_rows.5.refs_0_), channel_id=1, source_target_pairs={{0,1},{1,0},{2,3},{3,2},{4,5},{5,4},{6,7},{7,6},{8,9},{9,8},{10,11... | collective-permute-start | bytes 294920 | tf_op jit(solution)/shard_map/ppermute | solution.py:35
  40.9 5.0 %collective-permute-start.13 = (bf16[64,768]{1,0:T(8,128)(2,1)S(1)}, bf16[64,768]{1,0:T(8,128)(2,1)S(1)}, u32[]{:S(2)}, u32[]{:S(2)}) collective-permute-start(bf16[64,768]{1,0:T(8,128)(2,1)S(1)} %add.7.mine_ref), channel_id=1, source_target_pairs={{0,2},{1,3},{2,0},{3,1},{4,6},{5,7},{6,4},{7,5},{8,10},{9,11},{10,... | collective-permute-start | bytes 294920 | tf_op jit(solution)/shard_map/ppermute | solution.py:35

commit v8 on v7

--- a/solution.py
+++ b/solution.py
@@ -53,27 +53,35 @@
     return turned
 
 
-def partial_kernel(tokens_ref, weight_ref, sign_ref, *outs):
+def partial_kernel(here, ids_ref, tokens_ref, weight_ref, down_ref, low_ref, *outs):
     me, width = lax.axis_index("tp"), outs[0].shape[1]
-    sign_ref[...] = jnp.zeros_like(sign_ref)
     for n, out_ref in enumerate(outs):
-        offset = (2 * n + 1) % len(outs) if n < len(outs) // 2 else 2 * n - len(outs)
+        offset = 2 * n + 1 if n < len(outs) // 2 else 2 * n - len(outs)
         at = pl.multiple_of(jnp.bitwise_xor(me, offset) * width, width)
         product = jnp.dot(tokens_ref[...], weight_ref[:, pl.ds(at, width)], preferred_element_type=F32)
         out_ref[...] = product.astype(BF16)
-
-
-def partials(tokens, weight, parts):
-    block = jax.ShapeDtypeStruct((tokens.shape[0], weight.shape[1] // parts), BF16)
-    return pl.pallas_call(
-        partial_kernel,
-        in_specs=[VMEM, VMEM],
+    rank = down_ref.shape[1]
+    joined = jnp.concatenate([down_ref[k] for k in range(here)], axis=0)
+    product = lax.dot_general(joined, tokens_ref[...], LAST, preferred_element_type=F32)
+    terms = [
+        jnp.where(ids_ref[...] == adapter(here, 0, ("plane", 0, k)), product[k * rank : (k + 1) * rank], 0.0)
+        for k in range(here)
+    ]
+    low_ref[...] = functools.reduce(jnp.add, terms)
+
+
+def partials(ids, tokens, weight, down, parts):
+    rows, width = tokens.shape[0], weight.shape[1] // parts
+    here, rank, _ = down.shape
+    return pl.pallas_call(
+        functools.partial(partial_kernel, here),
+        in_specs=[VMEM] * 4,
         out_specs=[VMEM] * (1 + parts),
-        out_shape=[jax.ShapeDtypeStruct((8, 128), F32)] + [block] * parts,
+        out_shape=[jax.ShapeDtypeStruct((rank, rows), F32)] + [jax.ShapeDtypeStruct((rows, width), BF16)] * parts,
         compiler_params=params(24),
         cost_estimate=COST,
         name="partials",
-    )(tokens, weight)
+    )(ids, tokens, weight, down)
 
 
 def add_kernel(*refs):
@@ -123,9 +131,9 @@
     return jnp.bitwise_xor(z, plane) * here + jnp.bitwise_xor(lax.axis_index("grp"), off) * share + k
 
 
-def low_kernel(groups, here, share, rank, more, ids_ref, tokens_ref, *refs):
+def low_kernel(groups, here, share, rank, ids_ref, tokens_ref, *refs):
     out_ref = refs[-1]
-    total = refs[-2][...] if more else None
+    total = refs[-2][...]
     for (start, stop), terms in groups:
         rows = [refs[i][k, :, cut : cut + stop - start] for i, k, cut, _ in terms]
         joined = rows[0] if len(rows) == 1 else jnp.concatenate(rows, axis=0)
@@ -133,22 +141,38 @@
         for n, (_, _, _, name) in enumerate(terms):
             mine = ids_ref[...] == adapter(here, share, name)
             term = jnp.where(mine, product[n * rank : (n + 1) * rank], 0.0)
-            total = term if total is None else total + term
+            total = total + term
     out_ref[...] = total.astype(out_ref.dtype)
 
 
 def low_rows(ids, tokens, here, share, groups, arrays, before, dtype, cost=COST):
     rank = arrays[0].shape[1]
-    more = [] if before is None else [before]
-    return pl.pallas_call(
-        functools.partial(low_kernel, groups, here, share, rank, bool(more)),
-        in_specs=[VMEM] * (2 + len(arrays) + len(more)),
+    return pl.pallas_call(
+        functools.partial(low_kernel, groups, here, share, rank),
+        in_specs=[VMEM] * (3 + len(arrays)),
         out_specs=VMEM,
         out_shape=jax.ShapeDtypeStruct((rank, tokens.shape[0]), dtype),
         compiler_params=params(24),
         cost_estimate=cost,
         name="low_rows",
-    )(ids, tokens, *arrays, *more)
+    )(ids, tokens, *arrays, before)
+
+
+def join_kernel(first_ref, second_ref, out_ref):
+    out_ref[: first_ref.shape[0]] = first_ref[...]
+    out_ref[first_ref.shape[0] :] = second_ref[...]
+
+
+def joined(first, second):
+    return pl.pallas_call(
+        join_kernel,
+        in_specs=[VMEM] * 2,
+        out_specs=VMEM,
+        out_shape=jax.ShapeDtypeStruct((2 * first.shape[0], *first.shape[1:]), BF16),
+        compiler_params=params(16),
+        cost_estimate=COST,
+        name="joined",
+    )(first, second)
 
 
 def ups_kernel(terms, here, share, rank, ids_ref, bits_ref, matrix_ref, *refs):
@@ -215,9 +239,10 @@
     while bit > 1:
         mine += [(plane | bit, swap(piece, "adp", bit)) for plane, piece in mine]
         bit //= 2
-    sign, *blocks = partials(tokens, base_weight, parts)
+    low, *blocks = partials(ids, tokens, base_weight, down, parts)
     half = parts // 2
-    near, _, *far = together(near, sign, *(piece for _, piece in mine[1:]))
+    near, low = together(near, low)
+    close, up, *far = together(near, adapter_up, *(piece for _, piece in mine[1:]))
     mine = mine[:1] + [(plane, piece) for (plane, _), piece in zip(mine[1:], far)]
     odd = [(1, near)] + [(plane | 1, swap(piece, "adp", 1)) for plane, piece in mine[1:]]
 
@@ -225,20 +250,25 @@
         return [(plane, off, swap(piece, "grp", off)) for plane, piece in pieces for off in range(1, groups)]
 
     swapped = others(odd[:1]) + others(mine[1:]) + others(odd[1:])
-    held = [(plane, 0, piece) for plane, piece in odd[:1] + mine[1:] + odd[1:]]
+    held = [(plane, 0, piece) for plane, piece in [(1, close)] + mine[1:] + odd[1:]]
 
     def terms(pieces, start):
         return [(start + i, k, 0, (plane, off, k)) for i, (plane, off, _) in enumerate(pieces) for k in range(share)]
 
     whole = (0, features)
-    early = held[: len(mine)]
-    middle = held[len(mine) :] + swapped[:-1]
+    early = held[: len(mine)] + swapped[:1]
+    middle = held[len(mine) :] + swapped[1:-1]
     late = swapped[-1:]
-    home = [(0, k, 0, ("plane", 0, k)) for k in range(here)]
-    first = [(whole, home + terms(early, 1))]
-    low = low_rows(ids, tokens, here, share, first, [down] + [p for *_, p in early], None, F32, SOME)
-
-    low, *came = together(low, *(swap(block, "tp", 1) for block in blocks[:half]))
+    low = low_rows(ids, tokens, here, share, [(whole, terms(early, 0))], [p for *_, p in early], low, F32, SOME)
+
+    ups, order = up, [0]
+    bit = planes // 2
+    while bit > 1:
+        ups = joined(ups, swap(ups, "adp", bit))
+        order += [plane | bit for plane in order]
+        bit //= 2
+
+    low, ups, *came = together(low, ups, *(swap(block, "tp", 1) for block in blocks[:half]))
     sums = [[block, pair] for block, pair in zip(blocks[half:], came)]
     bit = 2
     while bit < parts:
@@ -247,18 +277,10 @@
         bit *= 2
     base = rotated_base(sums[0], scale, bits, matrix)
 
-    plane, off, piece = middle[-len(swapped) + 1]
-    piece, up = together(piece, adapter_up)
-    middle[-len(swapped) + 1] = plane, off, piece
-    ups = [(0, up)]
-    bit = planes // 2
-    while bit:
-        ups += [(plane | bit, swap(up, "adp", bit)) for plane, up in ups]
-        bit //= 2
-    every = [(i, k, 0, ("plane", plane, k)) for i, (plane, _) in enumerate(ups) for k in range(here)]
-    up, mask = rotated_ups(ids, bits, matrix, here, share, every, [up for _, up in ups], width)
-
-    low = low_rows(ids, tokens, here, share, [(whole, terms(middle, 0))], [p for *_, p in middle], low, F32)
+    every = [(side, here * i + k, 0, ("plane", plane | side, k)) for side in (0, 1) for i, plane in enumerate(order) for k in range(here)]
+    up, mask = rotated_ups(ids, bits, matrix, here, share, every, [ups, swap(ups, "adp", 1)], width)
+
+    low = low_rows(ids, tokens, here, share, [(whole, terms(middle, 0))], [p for *_, p in middle], low, F32, SOME)
     low, base, up, mask = together(low, base, up, mask)
     low = low_rows(ids, tokens, here, share, [(whole, terms(late, 0))], [p for *_, p in late], low, BF16)
     bit = 1

time: 47.6 us -> 46 us (0.966)
  waiting for transfers between devices: 13.6 us -> 11.1 us
  local copies, waits for them, and re-layouts: 5.15 us -> 6.83 us
  starting transfers between devices: 18.6 us -> 17 us
  Pallas kernels: 9.93 us -> 10.6 us
    ppermute x14 -> x13, waiting for transfers between devices: 13.6 us -> 11.1 us  [swap(): lax.ppermute(x, axis, [(i, i ^ bit) for i in range(lax.axis_size(axis))])]
    unnamed x18 -> x20, local copies, waits for them, and re-layouts: 4.11 us -> 5.83 us
    ppermute x14 -> x13, starting transfers between devices: 18.6 us -> 17 us  [swap(): lax.ppermute(x, axis, [(i, i ^ bit) for i in range(lax.axis_size(axis))])]
    pallas_call x4 -> x5, Pallas kernels: 7.22 us -> 7.83 us  [the longest x1 4.37 us: partials(): pl.pallas_call(functools.partial(partial_kernel, here), in_specs=[VMEM] *...]
  transfers between devices with their start and end apart: 14 -> 13, of which waited for: 8 -> 6; matrix products, arithmetic and copies ran while one was open for 0% -> 0% of each run, Pallas kernels for 16% -> 18%
where the time goes in v8:
time: 46 us; the launch traced here: 45.7 us
  starting transfers between devices  17 us (37%)
  waiting for transfers between devices  11.1 us (24%)
  Pallas kernels  10.6 us (23%)
  local copies, waits for them, and re-layouts  6.83 us (15%)
    ppermute x13, starting transfers between devices, swap(): lax.ppermute(x, axis, [(i, i ^ bit) for i in range(lax.axis_size(axis))])  17 us
    ppermute x13, waiting for transfers between devices, swap(): lax.ppermute(x, axis, [(i, i ^ bit) for i in range(lax.axis_size(axis))])  11.1 us
    unnamed x20, local copies, waits for them, and re-layouts  5.83 us
    pallas_call x1, Pallas kernels, partials(): pl.pallas_call(functools.partial(partial_kernel, here), in_specs=[VMEM] *...  4.37 us
    pallas_call x3, Pallas kernels, low_rows(): pl.pallas_call(functools.partial(low_kernel, groups, here, share, rank),...  3.45 us
    pallas_call x1, Pallas kernels, final(): pl.pallas_call(final_kernel, in_specs=[VMEM] * 5, out_specs=VMEM, out_sha...  1.45 us
    dynamic_slice x1, local copies, waits for them, and re-layouts, local(): lax.dynamic_slice_in_dim(down, lax.axis_index('grp') * share, share, 0)  1 us
  transfers between devices with their start and end apart: 13, of which 6 were waited for; matrix products, arithmetic and copies ran while one was open for 0% of the time, Pallas kernels for 18%

profile of v8, /device:TPU:0, one launch (start us, length us, event | category | flops | bytes accessed | tf_op | source)
XLA Modules:
  0.0 45.7 jit_solution(15626775967850849004)
XLA Ops:
  0.0 1.0 %dynamic-slice_bitcast_fusion = bf16[1,64,2048]{2,1,0:T(8,128)(2,1)S(1)} fusion(bf16[2,2048,64]{1,2,0:T(8,128)(2,1)} %param.12, s32[]{:T(128)S(6)} %select_n.3), kind=kLoop, calls=%fused_computation | loop fusion | bytes 524292 | tf_op jit(solution)/shard_map/dynamic_slice | solution.py:235
  1.0 3.1 %collective-permute-start = (bf16[1,64,2048]{2,1,0:T(8,128)(2,1)S(1)}, bf16[1,64,2048]{2,1,0:T(8,128)(2,1)S(1)}, u32[]{:S(2)}, u32[]{:S(2)}) collective-permute-start(bf16[1,64,2048]{2,1,0:T(8,128)(2,1)S(1)} %dynamic-slice_bitcast_fusion), channel_id=1, source_target_pairs={{0,4},{4,0},{8,12},{12,8},{1,5},{5,1},{9,13},{13,9},{2,6},{6,2},{1... | collective-permute-start | bytes 786440 | tf_op jit(solution)/shard_map/ppermute | solution.py:35
  4.1 2.6 %collective-permute-start.1 = (bf16[1,64,2048]{2,1,0:T(8,128)(2,1)S(1)}, bf16[1,64,2048]{2,1,0:T(8,128)(2,1)S(1)}, u32[]{:S(2)}, u32[]{:S(2)}) collective-permute-start(bf16[1,64,2048]{2,1,0:T(8,128)(2,1)S(1)} %dynamic-slice_bitcast_fusion), channel_id=1, source_target_pairs={{0,8},{4,12},{8,0},{12,4},{1,9},{5,13},{9,1},{13,5},{2,10},{6,14},... | collective-permute-start | bytes 786440 | tf_op jit(solution)/shard_map/ppermute | solution.py:35
  6.7 1.9 %copy-done = bf16[768,2048]{1,0:T(8,128)(2,1)S(1)} copy-done((bf16[768,2048]{1,0:T(8,128)(2,1)S(1)}, bf16[768,2048]{1,0:T(8,128)(2,1)}, u32[]{:S(2)}) %copy-start) | copy-done | bytes 3145752
  8.6 2.2 %copy-done.2 = bf16[2048,1024]{1,0:T(8,128)(2,1)S(1)} copy-done((bf16[2048,1024]{1,0:T(8,128)(2,1)S(1)}, bf16[2048,1024]{1,0:T(8,128)(2,1)}, u32[]{:S(2)}) %copy-start.2) | copy-done | bytes 4194328
  10.8 1.0 %copy-done.3 = bf16[2,2048,64]{1,2,0:T(8,128)(2,1)S(1)} copy-done((bf16[2,2048,64]{1,2,0:T(8,128)(2,1)S(1)}, bf16[2,2048,64]{1,2,0:T(8,128)(2,1)}, u32[]{:S(2)}) %copy-start.3) | copy-done | bytes 524312
  11.8 0.7 %copy-done.6 = s32[768,1]{0,1:T(1,128)S(1)} copy-done((s32[768,1]{0,1:T(1,128)S(1)}, s32[768,1]{0,1:T(1,128)}, u32[]{:S(2)}) %copy-start.6) | copy-done | bytes 3096
  12.5 4.4 %partials.1 = (f32[64,768]{1,0:T(8,128)S(1)}, bf16[768,256]{1,0:T(8,128)(2,1)S(1)}, bf16[768,256]{1,0:T(8,128)(2,1)S(1)}, bf16[768,256]{1,0:T(8,128)(2,1)S(1)}, bf16[768,256]{1,0:T(8,128)(2,1)S(1)}) custom-call(s32[1,768]{1,0:T(1,128)S(1)} %bitcast.7, bf16[768,2048]{1,0:T(8,128)(2,1)S(1)} %copy-done, bf16[2048,1024]{1,0:T(8,128)(2,1)S(1)} %copy-done.2, ...), custom_call_target="tpu_custom_call" | custom-call | flops 1 | bytes 1 | tf_op jit(solution)/shard_map/partials/pallas_call | solution.py:76
  16.9 1.6 %collective-permute-start.5 = (bf16[1,64,2048]{2,1,0:T(8,128)(2,1)S(1)}, bf16[1,64,2048]{2,1,0:T(8,128)(2,1)S(1)}, u32[]{:S(2)}, u32[]{:S(2)}) collective-permute-start(bf16[1,64,2048]{2,1,0:T(8,128)(2,1)S(1)} %collective-permute-done.refs_0_), channel_id=1, source_target_pairs={{0,16},{16,0},{1,17},{17,1},{2,18},{18,2},{3,19},{19,3},{4,20},{20... | collective-permute-start | bytes 786440 | tf_op jit(solution)/shard_map/ppermute | solution.py:35
  18.5 0.3 collective-permute-start.6
  18.8 0.5 %collective-permute-start.8 = (bf16[768,256]{1,0:T(8,128)(2,1)S(1)}, bf16[768,256]{1,0:T(8,128)(2,1)S(1)}, u32[]{:S(2)}, u32[]{:S(2)}) collective-permute-start(bf16[768,256]{1,0:T(8,128)(2,1)S(1)} %get-tuple-element.32), channel_id=1, source_target_pairs={{0,1},{1,0},{2,3},{3,2},{4,5},{5,4},{6,7},{7,6},{8,9},{9,8},{10,11... | collective-permute-start | bytes 1179656 | tf_op jit(solution)/shard_map/ppermute | solution.py:35
  19.3 2.7 %collective-permute-start.2 = (bf16[1,64,2048]{2,1,0:T(8,128)(2,1)S(1)}, bf16[1,64,2048]{2,1,0:T(8,128)(2,1)S(1)}, u32[]{:S(2)}, u32[]{:S(2)}) collective-permute-start(bf16[1,64,2048]{2,1,0:T(8,128)(2,1)S(1)} %collective-permute-done.1.refs_1_), channel_id=1, source_target_pairs={{0,4},{4,0},{8,12},{12,8},{1,5},{5,1},{9,13},{13,9},{2,6},{6,2},{1... | collective-permute-start | bytes 786440 | tf_op jit(solution)/shard_map/ppermute | solution.py:35
  22.0 2.4 %collective-permute-done.6.second_ref = bf16[2,64,256]{2,1,0:T(8,128)(2,1)S(1)} collective-permute-done((bf16[2,64,256]{2,1,0:T(8,128)(2,1)S(1)}, bf16[2,64,256]{2,1,0:T(8,128)(2,1)S(1)}, u32[]{:S(2)}, u32[]{:S(2)}) %collective-permute-start.6) | collective-permute-done | bytes 65568 | tf_op jit(solution)/shard_map/ppermute | solution.py:35
  24.3 1.5 %collective-permute-start.4 = (bf16[1,64,2048]{2,1,0:T(8,128)(2,1)S(1)}, bf16[1,64,2048]{2,1,0:T(8,128)(2,1)S(1)}, u32[]{:S(2)}, u32[]{:S(2)}) collective-permute-start(bf16[1,64,2048]{2,1,0:T(8,128)(2,1)S(1)} %collective-permute-done.1.refs_1_), channel_id=1, source_target_pairs={{0,16},{16,0},{1,17},{17,1},{2,18},{18,2},{3,19},{19,3},{4,20},{20... | collective-permute-start | bytes 786440 | tf_op jit(solution)/shard_map/ppermute | solution.py:35
  25.8 1.2 %low_rows.3.refs_2_ = f32[64,768]{1,0:T(8,128)S(1)} custom-call(s32[1,768]{1,0:T(1,128)S(1)} %bitcast.8, bf16[768,2048]{1,0:T(8,128)(2,1)S(1)} %copy-done, bf16[1,64,2048]{2,1,0:T(8,128)(2,1)S(1)} %collective-permute-done.refs_0_, bf16[1,64,2048]{2,1,0:T(8,128)(2,1)S(1)} %collective-permute-done.1.refs_1_, ...), custom_call_target="tpu_custom_call" | custom-call | flops 5000000000 | bytes 1 | tf_op jit(solution)/shard_map/low_rows/pallas_call | solution.py:150
  27.1 0.1 collective-permute-start.10
  27.1 0.1 add.6
  27.2 0.0 copy-start.4
  27.3 1.6 %collective-permute-start.9 = (bf16[768,256]{1,0:T(8,128)(2,1)S(1)}, bf16[768,256]{1,0:T(8,128)(2,1)S(1)}, u32[]{:S(2)}, u32[]{:S(2)}) collective-permute-start(bf16[768,256]{1,0:T(8,128)(2,1)S(1)} %add.6), channel_id=1, source_target_pairs={{0,2},{1,3},{2,0},{3,1},{4,6},{5,7},{6,4},{7,5},{8,10},{9,11},{10,... | collective-permute-start | bytes 1179656 | tf_op jit(solution)/shard_map/ppermute | solution.py:35
  28.8 0.9 %collective-permute-done.2.refs_0_ = bf16[1,64,2048]{2,1,0:T(8,128)(2,1)S(1)} collective-permute-done((bf16[1,64,2048]{2,1,0:T(8,128)(2,1)S(1)}, bf16[1,64,2048]{2,1,0:T(8,128)(2,1)S(1)}, u32[]{:S(2)}, u32[]{:S(2)}) %collective-permute-start.2) | collective-permute-done | bytes 262176 | tf_op jit(solution)/shard_map/ppermute | solution.py:35
  29.7 1.5 %collective-permute-start.3 = (bf16[1,64,2048]{2,1,0:T(8,128)(2,1)S(1)}, bf16[1,64,2048]{2,1,0:T(8,128)(2,1)S(1)}, u32[]{:S(2)}, u32[]{:S(2)}) collective-permute-start(bf16[1,64,2048]{2,1,0:T(8,128)(2,1)S(1)} %collective-permute-done.2.refs_0_), channel_id=1, source_target_pairs={{0,16},{16,0},{1,17},{17,1},{2,18},{18,2},{3,19},{19,3},{4,20},{20... | collective-permute-start | bytes 786440 | tf_op jit(solution)/shard_map/ppermute | solution.py:35
  31.3 1.2 %low_rows.4.refs_1_ = f32[64,768]{1,0:T(8,128)S(1)} custom-call(s32[1,768]{1,0:T(1,128)S(1)} %bitcast.9, bf16[768,2048]{1,0:T(8,128)(2,1)S(1)} %copy-done, bf16[1,64,2048]{2,1,0:T(8,128)(2,1)S(1)} %collective-permute-done.2.refs_0_, bf16[1,64,2048]{2,1,0:T(8,128)(2,1)S(1)} %collective-permute-done.4.refs_1_, f32[64,768]{1,0:T(8,128)S(1)} %low_rows.3.refs_2_), custom_call_target="tpu_custom_call" | custom-call | flops 5000000000 | bytes 1 | tf_op jit(solution)/shard_map/low_rows/pallas_call | solution.py:150
  32.5 0.7 %rotated_ups.1 = (bf16[512,256]{1,0:T(8,128)(2,1)S(1)}, bf16[768,512]{1,0:T(8,128)(2,1)S(1)}) custom-call(s32[1,768]{1,0:T(1,128)S(1)} %bitcast.10, s32[1,128]{1,0:T(1,128)S(1)} %bitcast.12, bf16[128,128]{1,0:T(8,128)(2,1)S(1)} %copy-done.4, bf16[4,64,256]{2,1,0:T(8,128)(2,1)S(1)} %joined.1.refs_0_, bf16[4,64,256]{2,1,0:T(8,128)(2,1)S(1)} %collective-permute-done.10.refs_1_), custom_call_target="tpu_custom_call" | custom-call | flops 1 | bytes 1 | tf_op jit(solution)/shard_map/rotated_ups/pallas_call | solution.py:193
  33.1 2.4 %collective-permute-done.9.refs_2_ = bf16[768,256]{1,0:T(8,128)(2,1)S(1)} collective-permute-done((bf16[768,256]{1,0:T(8,128)(2,1)S(1)}, bf16[768,256]{1,0:T(8,128)(2,1)S(1)}, u32[]{:S(2)}, u32[]{:S(2)}) %collective-permute-start.9) | collective-permute-done | bytes 393248 | tf_op jit(solution)/shard_map/ppermute | solution.py:35
  35.6 0.5 %rotated_base.1.base_ref = f32[768,256]{1,0:T(8,128)S(1)} custom-call(f32[1,256]{1,0:T(1,128)S(1)} %bitcast.14, s32[1,128]{1,0:T(1,128)S(1)} %bitcast.13, bf16[128,128]{1,0:T(8,128)(2,1)S(1)} %copy-done.4, bf16[768,256]{1,0:T(8,128)(2,1)S(1)} %get-tuple-element.34.refs_0_, bf16[768,256]{1,0:T(8,128)(2,1)S(1)} %collective-permute-done.7.refs_1_, ...), custom_call_target="tpu_custom_call" | custom-call | flops 1 | bytes 1 | tf_op jit(solution)/shard_map/rotated_base/pallas_call | solution.py:115
  36.1 0.8 %collective-permute-done.3.refs_0_ = bf16[1,64,2048]{2,1,0:T(8,128)(2,1)S(1)} collective-permute-done((bf16[1,64,2048]{2,1,0:T(8,128)(2,1)S(1)}, bf16[1,64,2048]{2,1,0:T(8,128)(2,1)S(1)}, u32[]{:S(2)}, u32[]{:S(2)}) %collective-permute-start.3) | collective-permute-done | bytes 262176 | tf_op jit(solution)/shard_map/ppermute | solution.py:35
  36.9 1.1 %low_rows.5.refs_0_ = bf16[64,768]{1,0:T(8,128)(2,1)S(1)} custom-call(s32[1,768]{1,0:T(1,128)S(1)} %bitcast.11, bf16[768,2048]{1,0:T(8,128)(2,1)S(1)} %copy-done.1, bf16[1,64,2048]{2,1,0:T(8,128)(2,1)S(1)} %collective-permute-done.3.refs_0_, f32[64,768]{1,0:T(8,128)S(1)} %low_rows.4.refs_1_), custom_call_target="tpu_custom_call" | custom-call | flops 1 | bytes 1 | tf_op jit(solution)/shard_map/low_rows/pallas_call | solution.py:150
  38.0 0.1 collective-permute-start.11
  38.0 1.3 %collective-permute-done.11.refs_1_ = bf16[64,768]{1,0:T(8,128)(2,1)S(1)} collective-permute-done((bf16[64,768]{1,0:T(8,128)(2,1)S(1)}, bf16[64,768]{1,0:T(8,128)(2,1)S(1)}, u32[]{:S(2)}, u32[]{:S(2)}) %collective-permute-start.11) | collective-permute-done | bytes 98336 | tf_op jit(solution)/shard_map/ppermute | solution.py:35
  39.4 1.6 %collective-permute-start.12 = (bf16[64,768]{1,0:T(8,128)(2,1)S(1)}, bf16[64,768]{1,0:T(8,128)(2,1)S(1)}, u32[]{:S(2)}, u32[]{:S(2)}) collective-permute-start(bf16[64,768]{1,0:T(8,128)(2,1)S(1)} %add.7.mine_ref), channel_id=1, source_target_pairs={{0,2},{1,3},{2,0},{3,1},{4,6},{5,7},{6,4},{7,5},{8,10},{9,11},{10,... | collective-permute-start | bytes 294920 | tf_op jit(solution)/shard_map/ppermute | solution.py:35
  40.9 3.4 %collective-permute-done.12.theirs_ref = bf16[64,768]{1,0:T(8,128)(2,1)S(1)} collective-permute-done((bf16[64,768]{1,0:T(8,128)(2,1)S(1)}, bf16[64,768]{1,0:T(8,128)(2,1)S(1)}, u32[]{:S(2)}, u32[]{:S(2)}) %collective-permute-start.12) | collective-permute-done | bytes 98336 | tf_op jit(solution)/shard_map/ppermute | solution.py:35
  44.3 1.4 %final.1 = bf16[768,256]{1,0:T(8,128)(2,1)} custom-call(bf16[64,768]{1,0:T(8,128)(2,1)S(1)} %add.7.mine_ref, bf16[64,768]{1,0:T(8,128)(2,1)S(1)} %collective-permute-done.12.theirs_ref, f32[768,256]{1,0:T(8,128)S(1)} %rotated_base.1.base_ref, bf16[512,256]{1,0:T(8,128)(2,1)S(1)} %get-tuple-element.43.up_ref, bf16[768,512]{1,0:T(8,128)(2,1)S(1)} %get-tuple-element.44.mask_ref), custom_call_target="tpu_custom_call" | custom-call | flops 1 | bytes 1 | tf_op jit(solution)/shard_map/final/pallas_call | solution.py:214
  (25 shorter events, 0.1 us)
Async XLA Ops:
  0.0 18.5 %copy-start.5 = (bf16[2,64,256]{2,1,0:T(8,128)(2,1)S(1)}, bf16[2,64,256]{2,1,0:T(8,128)(2,1)}, u32[]{:S(2)}) copy-start(bf16[2,64,256]{2,1,0:T(8,128)(2,1)} %first_ref) | copy-start | bytes 196612
  1.0 15.9 %collective-permute-start = (bf16[1,64,2048]{2,1,0:T(8,128)(2,1)S(1)}, bf16[1,64,2048]{2,1,0:T(8,128)(2,1)S(1)}, u32[]{:S(2)}, u32[]{:S(2)}) collective-permute-start(bf16[1,64,2048]{2,1,0:T(8,128)(2,1)S(1)} %dynamic-slice_bitcast_fusion), channel_id=1, source_target_pairs={{0,4},{4,0},{8,12},{12,8},{1,5},{5,1},{9,13},{13,9},{2,6},{6,2},{1... | collective-permute-start | bytes 786440 | tf_op jit(solution)/shard_map/ppermute | solution.py:35
  4.1 14.4 %collective-permute-start.1 = (bf16[1,64,2048]{2,1,0:T(8,128)(2,1)S(1)}, bf16[1,64,2048]{2,1,0:T(8,128)(2,1)S(1)}, u32[]{:S(2)}, u32[]{:S(2)}) collective-permute-start(bf16[1,64,2048]{2,1,0:T(8,128)(2,1)S(1)} %dynamic-slice_bitcast_fusion), channel_id=1, source_target_pairs={{0,8},{4,12},{8,0},{12,4},{1,9},{5,13},{9,1},{13,5},{2,10},{6,14},... | collective-permute-start | bytes 786440 | tf_op jit(solution)/shard_map/ppermute | solution.py:35
  6.7 1.9 %copy-start = (bf16[768,2048]{1,0:T(8,128)(2,1)S(1)}, bf16[768,2048]{1,0:T(8,128)(2,1)}, u32[]{:S(2)}) copy-start(bf16[768,2048]{1,0:T(8,128)(2,1)} %tokens_ref.7) | copy-start | bytes 9437188
  8.6 2.2 %copy-start.2 = (bf16[2048,1024]{1,0:T(8,128)(2,1)S(1)}, bf16[2048,1024]{1,0:T(8,128)(2,1)}, u32[]{:S(2)}) copy-start(bf16[2048,1024]{1,0:T(8,128)(2,1)} %weight_ref.1) | copy-start | bytes 12582916
  10.8 1.0 %copy-start.3 = (bf16[2,2048,64]{1,2,0:T(8,128)(2,1)S(1)}, bf16[2,2048,64]{1,2,0:T(8,128)(2,1)}, u32[]{:S(2)}) copy-start(bf16[2,2048,64]{1,2,0:T(8,128)(2,1)} %param.12) | copy-start | bytes 1572868
  11.8 0.7 %copy-start.6 = (s32[768,1]{0,1:T(1,128)S(1)}, s32[768,1]{0,1:T(1,128)}, u32[]{:S(2)}) copy-start(s32[768,1]{0,1:T(1,128)} %param.9) | copy-start | bytes 9220
  16.9 8.9 %collective-permute-start.5 = (bf16[1,64,2048]{2,1,0:T(8,128)(2,1)S(1)}, bf16[1,64,2048]{2,1,0:T(8,128)(2,1)S(1)}, u32[]{:S(2)}, u32[]{:S(2)}) collective-permute-start(bf16[1,64,2048]{2,1,0:T(8,128)(2,1)S(1)} %collective-permute-done.refs_0_), channel_id=1, source_target_pairs={{0,16},{16,0},{1,17},{17,1},{2,18},{18,2},{3,19},{19,3},{4,20},{20... | collective-permute-start | bytes 786440 | tf_op jit(solution)/shard_map/ppermute | solution.py:35
  18.5 5.9 %collective-permute-start.6 = (bf16[2,64,256]{2,1,0:T(8,128)(2,1)S(1)}, bf16[2,64,256]{2,1,0:T(8,128)(2,1)S(1)}, u32[]{:S(2)}, u32[]{:S(2)}) collective-permute-start(bf16[2,64,256]{2,1,0:T(8,128)(2,1)S(1)} %copy-done.5), channel_id=1, source_target_pairs={{0,8},{4,12},{8,0},{12,4},{1,9},{5,13},{9,1},{13,5},{2,10},{6,14},... | collective-permute-start | bytes 196616 | tf_op jit(solution)/shard_map/ppermute | solution.py:35
  18.8 8.2 %collective-permute-start.7 = (bf16[768,256]{1,0:T(8,128)(2,1)S(1)}, bf16[768,256]{1,0:T(8,128)(2,1)S(1)}, u32[]{:S(2)}, u32[]{:S(2)}) collective-permute-start(bf16[768,256]{1,0:T(8,128)(2,1)S(1)} %get-tuple-element.31), channel_id=1, source_target_pairs={{0,1},{1,0},{2,3},{3,2},{4,5},{5,4},{6,7},{7,6},{8,9},{9,8},{10,11... | collective-permute-start | bytes 1179656 | tf_op jit(solution)/shard_map/ppermute | solution.py:35
  18.8 8.2 %collective-permute-start.8 = (bf16[768,256]{1,0:T(8,128)(2,1)S(1)}, bf16[768,256]{1,0:T(8,128)(2,1)S(1)}, u32[]{:S(2)}, u32[]{:S(2)}) collective-permute-start(bf16[768,256]{1,0:T(8,128)(2,1)S(1)} %get-tuple-element.32), channel_id=1, source_target_pairs={{0,1},{1,0},{2,3},{3,2},{4,5},{5,4},{6,7},{7,6},{8,9},{9,8},{10,11... | collective-permute-start | bytes 1179656 | tf_op jit(solution)/shard_map/ppermute | solution.py:35
  19.3 10.4 %collective-permute-start.2 = (bf16[1,64,2048]{2,1,0:T(8,128)(2,1)S(1)}, bf16[1,64,2048]{2,1,0:T(8,128)(2,1)S(1)}, u32[]{:S(2)}, u32[]{:S(2)}) collective-permute-start(bf16[1,64,2048]{2,1,0:T(8,128)(2,1)S(1)} %collective-permute-done.1.refs_1_), channel_id=1, source_target_pairs={{0,4},{4,0},{8,12},{12,8},{1,5},{5,1},{9,13},{13,9},{2,6},{6,2},{1... | collective-permute-start | bytes 786440 | tf_op jit(solution)/shard_map/ppermute | solution.py:35
  24.3 6.9 %collective-permute-start.4 = (bf16[1,64,2048]{2,1,0:T(8,128)(2,1)S(1)}, bf16[1,64,2048]{2,1,0:T(8,128)(2,1)S(1)}, u32[]{:S(2)}, u32[]{:S(2)}) collective-permute-start(bf16[1,64,2048]{2,1,0:T(8,128)(2,1)S(1)} %collective-permute-done.1.refs_1_), channel_id=1, source_target_pairs={{0,16},{16,0},{1,17},{17,1},{2,18},{18,2},{3,19},{19,3},{4,20},{20... | collective-permute-start | bytes 786440 | tf_op jit(solution)/shard_map/ppermute | solution.py:35
  27.1 5.4 %collective-permute-start.10 = (bf16[4,64,256]{2,1,0:T(8,128)(2,1)S(1)}, bf16[4,64,256]{2,1,0:T(8,128)(2,1)S(1)}, u32[]{:S(2)}, u32[]{:S(2)}) collective-permute-start(bf16[4,64,256]{2,1,0:T(8,128)(2,1)S(1)} %joined.1.refs_0_), channel_id=1, source_target_pairs={{0,4},{4,0},{8,12},{12,8},{1,5},{5,1},{9,13},{13,9},{2,6},{6,2},{1... | collective-permute-start | bytes 393224 | tf_op jit(solution)/shard_map/ppermute | solution.py:35
  27.2 5.2 %copy-start.4 = (bf16[128,128]{1,0:T(8,128)(2,1)S(1)}, bf16[128,128]{1,0:T(8,128)(2,1)}, u32[]{:S(2)}) copy-start(bf16[128,128]{1,0:T(8,128)(2,1)} %constant.12.clone.matrix_ref) | copy-start | bytes 98308
  27.3 5.2 %copy-start.7 = (s32[768,1]{0,1:T(1,128)S(1)}, s32[768,1]{0,1:T(1,128)}, u32[]{:S(2)}) copy-start(s32[768,1]{0,1:T(1,128)} %param.9) | copy-start | bytes 9220
  27.3 5.2 %copy-start.8 = (s32[128]{0:T(128)S(1)}, s32[128]{0:T(128)}, u32[]{:S(2)}) copy-start(s32[128]{0:T(128)} %param.14) | copy-start | bytes 1540
  27.3 8.3 %copy-start.9 = (f32[256]{0:T(256)S(1)}, f32[256]{0:T(256)}, u32[]{:S(2)}) copy-start(f32[256]{0:T(256)} %param.11) | copy-start | bytes 3076
  27.3 8.3 %collective-permute-start.9 = (bf16[768,256]{1,0:T(8,128)(2,1)S(1)}, bf16[768,256]{1,0:T(8,128)(2,1)S(1)}, u32[]{:S(2)}, u32[]{:S(2)}) collective-permute-start(bf16[768,256]{1,0:T(8,128)(2,1)S(1)} %add.6), channel_id=1, source_target_pairs={{0,2},{1,3},{2,0},{3,1},{4,6},{5,7},{6,4},{7,5},{8,10},{9,11},{10,... | collective-permute-start | bytes 1179656 | tf_op jit(solution)/shard_map/ppermute | solution.py:35
  29.7 7.1 %collective-permute-start.3 = (bf16[1,64,2048]{2,1,0:T(8,128)(2,1)S(1)}, bf16[1,64,2048]{2,1,0:T(8,128)(2,1)S(1)}, u32[]{:S(2)}, u32[]{:S(2)}) collective-permute-start(bf16[1,64,2048]{2,1,0:T(8,128)(2,1)S(1)} %collective-permute-done.2.refs_0_), channel_id=1, source_target_pairs={{0,16},{16,0},{1,17},{17,1},{2,18},{18,2},{3,19},{19,3},{4,20},{20... | collective-permute-start | bytes 786440 | tf_op jit(solution)/shard_map/ppermute | solution.py:35
  31.3 5.6 %copy-start.1 = (bf16[768,2048]{1,0:T(8,128)(2,1)S(1)}, bf16[768,2048]{1,0:T(8,128)(2,1)}, u32[]{:S(2)}) copy-start(bf16[768,2048]{1,0:T(8,128)(2,1)} %tokens_ref.7) | copy-start | bytes 9437188
  38.0 1.4 %collective-permute-start.11 = (bf16[64,768]{1,0:T(8,128)(2,1)S(1)}, bf16[64,768]{1,0:T(8,128)(2,1)S(1)}, u32[]{:S(2)}, u32[]{:S(2)}) collective-permute-start(bf16[64,768]{1,0:T(8,128)(2,1)S(1)} %low_rows.5.refs_0_), channel_id=1, source_target_pairs={{0,1},{1,0},{2,3},{3,2},{4,5},{5,4},{6,7},{7,6},{8,9},{9,8},{10,11... | collective-permute-start | bytes 294920 | tf_op jit(solution)/shard_map/ppermute | solution.py:35
  39.4 4.9 %collective-permute-start.12 = (bf16[64,768]{1,0:T(8,128)(2,1)S(1)}, bf16[64,768]{1,0:T(8,128)(2,1)S(1)}, u32[]{:S(2)}, u32[]{:S(2)}) collective-permute-start(bf16[64,768]{1,0:T(8,128)(2,1)S(1)} %add.7.mine_ref), channel_id=1, source_target_pairs={{0,2},{1,3},{2,0},{3,1},{4,6},{5,7},{6,4},{7,5},{8,10},{9,11},{10,... | collective-permute-start | bytes 294920 | tf_op jit(solution)/shard_map/ppermute | solution.py:35

commit v9 on v8

--- a/solution.py
+++ b/solution.py
@@ -242,7 +242,7 @@
     low, *blocks = partials(ids, tokens, base_weight, down, parts)
     half = parts // 2
     near, low = together(near, low)
-    close, up, *far = together(near, adapter_up, *(piece for _, piece in mine[1:]))
+    close, *far = together(near, *(piece for _, piece in mine[1:]))
     mine = mine[:1] + [(plane, piece) for (plane, _), piece in zip(mine[1:], far)]
     odd = [(1, near)] + [(plane | 1, swap(piece, "adp", 1)) for plane, piece in mine[1:]]
 
@@ -259,16 +259,17 @@
     early = held[: len(mine)] + swapped[:1]
     middle = held[len(mine) :] + swapped[1:-1]
     late = swapped[-1:]
-    low = low_rows(ids, tokens, here, share, [(whole, terms(early, 0))], [p for *_, p in early], low, F32, SOME)
-
-    ups, order = up, [0]
+    plane, off, piece = early[-1]
+    piece, ups = together(piece, adapter_up)
+    early[-1], order = (plane, off, piece), [0]
     bit = planes // 2
     while bit > 1:
         ups = joined(ups, swap(ups, "adp", bit))
         order += [plane | bit for plane in order]
         bit //= 2
-
-    low, ups, *came = together(low, ups, *(swap(block, "tp", 1) for block in blocks[:half]))
+    low = low_rows(ids, tokens, here, share, [(whole, terms(early, 0))], [p for *_, p in early], low, F32, SOME)
+
+    low, *came = together(low, *(swap(block, "tp", 1) for block in blocks[:half]))
     sums = [[block, pair] for block, pair in zip(blocks[half:], came)]
     bit = 2
     while bit < parts:

time: 46 us -> 47.3 us (1.028)
  waiting for transfers between devices: 11.1 us -> 14.2 us
  starting transfers between devices: 17 us -> 15.2 us
    ppermute x13, waiting for transfers between devices: 11.1 us -> 14.2 us  [swap(): lax.ppermute(x, axis, [(i, i ^ bit) for i in range(lax.axis_size(axis))])]
    ppermute x13, starting transfers between devices: 17 us -> 15.2 us  [swap(): lax.ppermute(x, axis, [(i, i ^ bit) for i in range(lax.axis_size(axis))])]
  transfers between devices with their start and end apart: 13 -> 13, of which waited for: 6 -> 5; matrix products, arithmetic and copies ran while one was open for 0% -> 0% of each run, Pallas kernels for 18% -> 17%
where the time goes in v9:
time: 47.3 us; the launch traced here: 47 us
  starting transfers between devices  15.2 us (32%)
  waiting for transfers between devices  14.2 us (30%)
  Pallas kernels  10.6 us (22%)
  local copies, waits for them, and re-layouts  6.83 us (14%)
    ppermute x13, starting transfers between devices, swap(): lax.ppermute(x, axis, [(i, i ^ bit) for i in range(lax.axis_size(axis))])  15.2 us
    ppermute x13, waiting for transfers between devices, swap(): lax.ppermute(x, axis, [(i, i ^ bit) for i in range(lax.axis_size(axis))])  14.2 us
    unnamed x20, local copies, waits for them, and re-layouts  5.83 us
    pallas_call x1, Pallas kernels, partials(): pl.pallas_call(functools.partial(partial_kernel, here), in_specs=[VMEM] *...  4.37 us
    pallas_call x3, Pallas kernels, low_rows(): pl.pallas_call(functools.partial(low_kernel, groups, here, share, rank),...  3.45 us
    pallas_call x1, Pallas kernels, final(): pl.pallas_call(final_kernel, in_specs=[VMEM] * 5, out_specs=VMEM, out_sha...  1.45 us
    dynamic_slice x1, local copies, waits for them, and re-layouts, local(): lax.dynamic_slice_in_dim(down, lax.axis_index('grp') * share, share, 0)  1 us
  transfers between devices with their start and end apart: 13, of which 5 were waited for; matrix products, arithmetic and copies ran while one was open for 0% of the time, Pallas kernels for 17%

profile of v9, /device:TPU:0, one launch (start us, length us, event | category | flops | bytes accessed | tf_op | source)
XLA Modules:
  0.0 47.0 jit_solution(18198043372052837638)
XLA Ops:
  0.0 1.0 %dynamic-slice_bitcast_fusion = bf16[1,64,2048]{2,1,0:T(8,128)(2,1)S(1)} fusion(bf16[2,2048,64]{1,2,0:T(8,128)(2,1)} %param.12, s32[]{:T(128)S(6)} %select_n.3), kind=kLoop, calls=%fused_computation | loop fusion | bytes 524292 | tf_op jit(solution)/shard_map/dynamic_slice | solution.py:235
  1.0 3.1 %collective-permute-start = (bf16[1,64,2048]{2,1,0:T(8,128)(2,1)S(1)}, bf16[1,64,2048]{2,1,0:T(8,128)(2,1)S(1)}, u32[]{:S(2)}, u32[]{:S(2)}) collective-permute-start(bf16[1,64,2048]{2,1,0:T(8,128)(2,1)S(1)} %dynamic-slice_bitcast_fusion), channel_id=1, source_target_pairs={{0,4},{4,0},{8,12},{12,8},{1,5},{5,1},{9,13},{13,9},{2,6},{6,2},{1... | collective-permute-start | bytes 786440 | tf_op jit(solution)/shard_map/ppermute | solution.py:35
  4.1 2.6 %collective-permute-start.1 = (bf16[1,64,2048]{2,1,0:T(8,128)(2,1)S(1)}, bf16[1,64,2048]{2,1,0:T(8,128)(2,1)S(1)}, u32[]{:S(2)}, u32[]{:S(2)}) collective-permute-start(bf16[1,64,2048]{2,1,0:T(8,128)(2,1)S(1)} %dynamic-slice_bitcast_fusion), channel_id=1, source_target_pairs={{0,8},{4,12},{8,0},{12,4},{1,9},{5,13},{9,1},{13,5},{2,10},{6,14},... | collective-permute-start | bytes 786440 | tf_op jit(solution)/shard_map/ppermute | solution.py:35
  6.7 1.9 %copy-done = bf16[768,2048]{1,0:T(8,128)(2,1)S(1)} copy-done((bf16[768,2048]{1,0:T(8,128)(2,1)S(1)}, bf16[768,2048]{1,0:T(8,128)(2,1)}, u32[]{:S(2)}) %copy-start) | copy-done | bytes 3145752
  8.6 2.2 %copy-done.2 = bf16[2048,1024]{1,0:T(8,128)(2,1)S(1)} copy-done((bf16[2048,1024]{1,0:T(8,128)(2,1)S(1)}, bf16[2048,1024]{1,0:T(8,128)(2,1)}, u32[]{:S(2)}) %copy-start.2) | copy-done | bytes 4194328
  10.8 1.0 %copy-done.3 = bf16[2,2048,64]{1,2,0:T(8,128)(2,1)S(1)} copy-done((bf16[2,2048,64]{1,2,0:T(8,128)(2,1)S(1)}, bf16[2,2048,64]{1,2,0:T(8,128)(2,1)}, u32[]{:S(2)}) %copy-start.3) | copy-done | bytes 524312
  11.8 0.7 %copy-done.6 = s32[768,1]{0,1:T(1,128)S(1)} copy-done((s32[768,1]{0,1:T(1,128)S(1)}, s32[768,1]{0,1:T(1,128)}, u32[]{:S(2)}) %copy-start.6) | copy-done | bytes 3096
  12.5 4.4 %partials.1 = (f32[64,768]{1,0:T(8,128)S(1)}, bf16[768,256]{1,0:T(8,128)(2,1)S(1)}, bf16[768,256]{1,0:T(8,128)(2,1)S(1)}, bf16[768,256]{1,0:T(8,128)(2,1)S(1)}, bf16[768,256]{1,0:T(8,128)(2,1)S(1)}) custom-call(s32[1,768]{1,0:T(1,128)S(1)} %bitcast.7, bf16[768,2048]{1,0:T(8,128)(2,1)S(1)} %copy-done, bf16[2048,1024]{1,0:T(8,128)(2,1)S(1)} %copy-done.2, ...), custom_call_target="tpu_custom_call" | custom-call | flops 1 | bytes 1 | tf_op jit(solution)/shard_map/partials/pallas_call | solution.py:76
  16.9 1.6 %collective-permute-start.5 = (bf16[1,64,2048]{2,1,0:T(8,128)(2,1)S(1)}, bf16[1,64,2048]{2,1,0:T(8,128)(2,1)S(1)}, u32[]{:S(2)}, u32[]{:S(2)}) collective-permute-start(bf16[1,64,2048]{2,1,0:T(8,128)(2,1)S(1)} %collective-permute-done.refs_0_), channel_id=1, source_target_pairs={{0,16},{16,0},{1,17},{17,1},{2,18},{18,2},{3,19},{19,3},{4,20},{20... | collective-permute-start | bytes 786440 | tf_op jit(solution)/shard_map/ppermute | solution.py:35
  18.5 0.5 %collective-permute-start.7 = (bf16[768,256]{1,0:T(8,128)(2,1)S(1)}, bf16[768,256]{1,0:T(8,128)(2,1)S(1)}, u32[]{:S(2)}, u32[]{:S(2)}) collective-permute-start(bf16[768,256]{1,0:T(8,128)(2,1)S(1)} %get-tuple-element.32), channel_id=1, source_target_pairs={{0,1},{1,0},{2,3},{3,2},{4,5},{5,4},{6,7},{7,6},{8,9},{9,8},{10,11... | collective-permute-start | bytes 1179656 | tf_op jit(solution)/shard_map/ppermute | solution.py:35
  19.0 0.5 collective-permute-start.2
  19.4 1.0 %collective-permute-start.4 = (bf16[1,64,2048]{2,1,0:T(8,128)(2,1)S(1)}, bf16[1,64,2048]{2,1,0:T(8,128)(2,1)S(1)}, u32[]{:S(2)}, u32[]{:S(2)}) collective-permute-start(bf16[1,64,2048]{2,1,0:T(8,128)(2,1)S(1)} %collective-permute-done.1.refs_1_), channel_id=1, source_target_pairs={{0,16},{16,0},{1,17},{17,1},{2,18},{18,2},{3,19},{19,3},{4,20},{20... | collective-permute-start | bytes 786440 | tf_op jit(solution)/shard_map/ppermute | solution.py:35
  20.4 5.8 %collective-permute-done.5.refs_2_ = bf16[1,64,2048]{2,1,0:T(8,128)(2,1)S(1)} collective-permute-done((bf16[1,64,2048]{2,1,0:T(8,128)(2,1)S(1)}, bf16[1,64,2048]{2,1,0:T(8,128)(2,1)S(1)}, u32[]{:S(2)}, u32[]{:S(2)}) %collective-permute-start.5) | collective-permute-done | bytes 262176 | tf_op jit(solution)/shard_map/ppermute | solution.py:35
  26.2 1.2 %low_rows.3.refs_2_ = f32[64,768]{1,0:T(8,128)S(1)} custom-call(s32[1,768]{1,0:T(1,128)S(1)} %bitcast.8, bf16[768,2048]{1,0:T(8,128)(2,1)S(1)} %copy-done, bf16[1,64,2048]{2,1,0:T(8,128)(2,1)S(1)} %collective-permute-done.refs_0_, bf16[1,64,2048]{2,1,0:T(8,128)(2,1)S(1)} %collective-permute-done.1.refs_1_, ...), custom_call_target="tpu_custom_call" | custom-call | flops 5000000000 | bytes 1 | tf_op jit(solution)/shard_map/low_rows/pallas_call | solution.py:150
  27.4 0.1 add.6
  27.5 1.6 %collective-permute-start.8 = (bf16[768,256]{1,0:T(8,128)(2,1)S(1)}, bf16[768,256]{1,0:T(8,128)(2,1)S(1)}, u32[]{:S(2)}, u32[]{:S(2)}) collective-permute-start(bf16[768,256]{1,0:T(8,128)(2,1)S(1)} %add.6), channel_id=1, source_target_pairs={{0,2},{1,3},{2,0},{3,1},{4,6},{5,7},{6,4},{7,5},{8,10},{9,11},{10,... | collective-permute-start | bytes 1179656 | tf_op jit(solution)/shard_map/ppermute | solution.py:35
  29.1 1.9 %collective-permute-start.3 = (bf16[1,64,2048]{2,1,0:T(8,128)(2,1)S(1)}, bf16[1,64,2048]{2,1,0:T(8,128)(2,1)S(1)}, u32[]{:S(2)}, u32[]{:S(2)}) collective-permute-start(bf16[1,64,2048]{2,1,0:T(8,128)(2,1)S(1)} %collective-permute-done.2.refs_0_), channel_id=1, source_target_pairs={{0,16},{16,0},{1,17},{17,1},{2,18},{18,2},{3,19},{19,3},{4,20},{20... | collective-permute-start | bytes 786440 | tf_op jit(solution)/shard_map/ppermute | solution.py:35
  30.9 0.9 %collective-permute-done.9.second_ref = bf16[2,64,256]{2,1,0:T(8,128)(2,1)S(1)} collective-permute-done((bf16[2,64,256]{2,1,0:T(8,128)(2,1)S(1)}, bf16[2,64,256]{2,1,0:T(8,128)(2,1)S(1)}, u32[]{:S(2)}, u32[]{:S(2)}) %collective-permute-start.9) | collective-permute-done | bytes 65568 | tf_op jit(solution)/shard_map/ppermute | solution.py:35
  31.8 0.0 copy-start.4
  31.9 0.0 copy-start.8
  31.9 0.0 copy-start.9
  31.9 1.0 %collective-permute-start.10 = (bf16[4,64,256]{2,1,0:T(8,128)(2,1)S(1)}, bf16[4,64,256]{2,1,0:T(8,128)(2,1)S(1)}, u32[]{:S(2)}, u32[]{:S(2)}) collective-permute-start(bf16[4,64,256]{2,1,0:T(8,128)(2,1)S(1)} %joined.1.refs_0_), channel_id=1, source_target_pairs={{0,4},{4,0},{8,12},{12,8},{1,5},{5,1},{9,13},{13,9},{2,6},{6,2},{1... | collective-permute-start | bytes 393224 | tf_op jit(solution)/shard_map/ppermute | solution.py:35
  32.9 1.2 %low_rows.4.refs_1_ = f32[64,768]{1,0:T(8,128)S(1)} custom-call(s32[1,768]{1,0:T(1,128)S(1)} %bitcast.9, bf16[768,2048]{1,0:T(8,128)(2,1)S(1)} %copy-done, bf16[1,64,2048]{2,1,0:T(8,128)(2,1)S(1)} %collective-permute-done.2.refs_0_, bf16[1,64,2048]{2,1,0:T(8,128)(2,1)S(1)} %collective-permute-done.4.refs_1_, f32[64,768]{1,0:T(8,128)S(1)} %low_rows.3.refs_2_), custom_call_target="tpu_custom_call" | custom-call | flops 5000000000 | bytes 1 | tf_op jit(solution)/shard_map/low_rows/pallas_call | solution.py:150
  34.1 2.8 %collective-permute-done.10.refs_1_ = bf16[4,64,256]{2,1,0:T(8,128)(2,1)S(1)} collective-permute-done((bf16[4,64,256]{2,1,0:T(8,128)(2,1)S(1)}, bf16[4,64,256]{2,1,0:T(8,128)(2,1)S(1)}, u32[]{:S(2)}, u32[]{:S(2)}) %collective-permute-start.10) | collective-permute-done | bytes 131104 | tf_op jit(solution)/shard_map/ppermute | solution.py:35
  36.9 0.7 %rotated_ups.1 = (bf16[512,256]{1,0:T(8,128)(2,1)S(1)}, bf16[768,512]{1,0:T(8,128)(2,1)S(1)}) custom-call(s32[1,768]{1,0:T(1,128)S(1)} %bitcast.10, s32[1,128]{1,0:T(1,128)S(1)} %bitcast.12, bf16[128,128]{1,0:T(8,128)(2,1)S(1)} %copy-done.4, bf16[4,64,256]{2,1,0:T(8,128)(2,1)S(1)} %joined.1.refs_0_, bf16[4,64,256]{2,1,0:T(8,128)(2,1)S(1)} %collective-permute-done.10.refs_1_), custom_call_target="tpu_custom_call" | custom-call | flops 1 | bytes 1 | tf_op jit(solution)/shard_map/rotated_ups/pallas_call | solution.py:193
  37.6 0.5 %rotated_base.1.base_ref = f32[768,256]{1,0:T(8,128)S(1)} custom-call(f32[1,256]{1,0:T(1,128)S(1)} %bitcast.14, s32[1,128]{1,0:T(1,128)S(1)} %bitcast.13, bf16[128,128]{1,0:T(8,128)(2,1)S(1)} %copy-done.4, bf16[768,256]{1,0:T(8,128)(2,1)S(1)} %get-tuple-element.34.refs_0_, bf16[768,256]{1,0:T(8,128)(2,1)S(1)} %collective-permute-done.6.refs_1_, ...), custom_call_target="tpu_custom_call" | custom-call | flops 1 | bytes 1 | tf_op jit(solution)/shard_map/rotated_base/pallas_call | solution.py:115
  38.1 1.1 %low_rows.5.refs_0_ = bf16[64,768]{1,0:T(8,128)(2,1)S(1)} custom-call(s32[1,768]{1,0:T(1,128)S(1)} %bitcast.11, bf16[768,2048]{1,0:T(8,128)(2,1)S(1)} %copy-done.1, bf16[1,64,2048]{2,1,0:T(8,128)(2,1)S(1)} %collective-permute-done.3.refs_0_, f32[64,768]{1,0:T(8,128)S(1)} %low_rows.4.refs_1_), custom_call_target="tpu_custom_call" | custom-call | flops 1 | bytes 1 | tf_op jit(solution)/shard_map/low_rows/pallas_call | solution.py:150
  39.2 0.1 collective-permute-start.11
  39.3 1.3 %collective-permute-done.11.refs_1_ = bf16[64,768]{1,0:T(8,128)(2,1)S(1)} collective-permute-done((bf16[64,768]{1,0:T(8,128)(2,1)S(1)}, bf16[64,768]{1,0:T(8,128)(2,1)S(1)}, u32[]{:S(2)}, u32[]{:S(2)}) %collective-permute-start.11) | collective-permute-done | bytes 98336 | tf_op jit(solution)/shard_map/ppermute | solution.py:35
  40.6 1.5 %collective-permute-start.12 = (bf16[64,768]{1,0:T(8,128)(2,1)S(1)}, bf16[64,768]{1,0:T(8,128)(2,1)S(1)}, u32[]{:S(2)}, u32[]{:S(2)}) collective-permute-start(bf16[64,768]{1,0:T(8,128)(2,1)S(1)} %add.7.mine_ref), channel_id=1, source_target_pairs={{0,2},{1,3},{2,0},{3,1},{4,6},{5,7},{6,4},{7,5},{8,10},{9,11},{10,... | collective-permute-start | bytes 294920 | tf_op jit(solution)/shard_map/ppermute | solution.py:35
  42.1 3.4 %collective-permute-done.12.theirs_ref = bf16[64,768]{1,0:T(8,128)(2,1)S(1)} collective-permute-done((bf16[64,768]{1,0:T(8,128)(2,1)S(1)}, bf16[64,768]{1,0:T(8,128)(2,1)S(1)}, u32[]{:S(2)}, u32[]{:S(2)}) %collective-permute-start.12) | collective-permute-done | bytes 98336 | tf_op jit(solution)/shard_map/ppermute | solution.py:35
  45.5 1.5 %final.1 = bf16[768,256]{1,0:T(8,128)(2,1)} custom-call(bf16[64,768]{1,0:T(8,128)(2,1)S(1)} %add.7.mine_ref, bf16[64,768]{1,0:T(8,128)(2,1)S(1)} %collective-permute-done.12.theirs_ref, f32[768,256]{1,0:T(8,128)S(1)} %rotated_base.1.base_ref, bf16[512,256]{1,0:T(8,128)(2,1)S(1)} %get-tuple-element.43.up_ref, bf16[768,512]{1,0:T(8,128)(2,1)S(1)} %get-tuple-element.44.mask_ref), custom_call_target="tpu_custom_call" | custom-call | flops 1 | bytes 1 | tf_op jit(solution)/shard_map/final/pallas_call | solution.py:214
  (25 shorter events, 0.1 us)
Async XLA Ops:
  0.0 26.2 %copy-start.5 = (bf16[2,64,256]{2,1,0:T(8,128)(2,1)S(1)}, bf16[2,64,256]{2,1,0:T(8,128)(2,1)}, u32[]{:S(2)}) copy-start(bf16[2,64,256]{2,1,0:T(8,128)(2,1)} %first_ref) | copy-start | bytes 196612
  1.0 15.9 %collective-permute-start = (bf16[1,64,2048]{2,1,0:T(8,128)(2,1)S(1)}, bf16[1,64,2048]{2,1,0:T(8,128)(2,1)S(1)}, u32[]{:S(2)}, u32[]{:S(2)}) collective-permute-start(bf16[1,64,2048]{2,1,0:T(8,128)(2,1)S(1)} %dynamic-slice_bitcast_fusion), channel_id=1, source_target_pairs={{0,4},{4,0},{8,12},{12,8},{1,5},{5,1},{9,13},{13,9},{2,6},{6,2},{1... | collective-permute-start | bytes 786440 | tf_op jit(solution)/shard_map/ppermute | solution.py:35
  4.1 14.9 %collective-permute-start.1 = (bf16[1,64,2048]{2,1,0:T(8,128)(2,1)S(1)}, bf16[1,64,2048]{2,1,0:T(8,128)(2,1)S(1)}, u32[]{:S(2)}, u32[]{:S(2)}) collective-permute-start(bf16[1,64,2048]{2,1,0:T(8,128)(2,1)S(1)} %dynamic-slice_bitcast_fusion), channel_id=1, source_target_pairs={{0,8},{4,12},{8,0},{12,4},{1,9},{5,13},{9,1},{13,5},{2,10},{6,14},... | collective-permute-start | bytes 786440 | tf_op jit(solution)/shard_map/ppermute | solution.py:35
  6.7 1.9 %copy-start = (bf16[768,2048]{1,0:T(8,128)(2,1)S(1)}, bf16[768,2048]{1,0:T(8,128)(2,1)}, u32[]{:S(2)}) copy-start(bf16[768,2048]{1,0:T(8,128)(2,1)} %tokens_ref.7) | copy-start | bytes 9437188
  8.6 2.2 %copy-start.2 = (bf16[2048,1024]{1,0:T(8,128)(2,1)S(1)}, bf16[2048,1024]{1,0:T(8,128)(2,1)}, u32[]{:S(2)}) copy-start(bf16[2048,1024]{1,0:T(8,128)(2,1)} %weight_ref.1) | copy-start | bytes 12582916
  10.8 1.0 %copy-start.3 = (bf16[2,2048,64]{1,2,0:T(8,128)(2,1)S(1)}, bf16[2,2048,64]{1,2,0:T(8,128)(2,1)}, u32[]{:S(2)}) copy-start(bf16[2,2048,64]{1,2,0:T(8,128)(2,1)} %param.12) | copy-start | bytes 1572868
  11.8 0.7 %copy-start.6 = (s32[768,1]{0,1:T(1,128)S(1)}, s32[768,1]{0,1:T(1,128)}, u32[]{:S(2)}) copy-start(s32[768,1]{0,1:T(1,128)} %param.9) | copy-start | bytes 9220
  16.9 9.3 %collective-permute-start.5 = (bf16[1,64,2048]{2,1,0:T(8,128)(2,1)S(1)}, bf16[1,64,2048]{2,1,0:T(8,128)(2,1)S(1)}, u32[]{:S(2)}, u32[]{:S(2)}) collective-permute-start(bf16[1,64,2048]{2,1,0:T(8,128)(2,1)S(1)} %collective-permute-done.refs_0_), channel_id=1, source_target_pairs={{0,16},{16,0},{1,17},{17,1},{2,18},{18,2},{3,19},{19,3},{4,20},{20... | collective-permute-start | bytes 786440 | tf_op jit(solution)/shard_map/ppermute | solution.py:35
  18.5 8.9 %collective-permute-start.6 = (bf16[768,256]{1,0:T(8,128)(2,1)S(1)}, bf16[768,256]{1,0:T(8,128)(2,1)S(1)}, u32[]{:S(2)}, u32[]{:S(2)}) collective-permute-start(bf16[768,256]{1,0:T(8,128)(2,1)S(1)} %get-tuple-element.31), channel_id=1, source_target_pairs={{0,1},{1,0},{2,3},{3,2},{4,5},{5,4},{6,7},{7,6},{8,9},{9,8},{10,11... | collective-permute-start | bytes 1179656 | tf_op jit(solution)/shard_map/ppermute | solution.py:35
  18.5 8.9 %collective-permute-start.7 = (bf16[768,256]{1,0:T(8,128)(2,1)S(1)}, bf16[768,256]{1,0:T(8,128)(2,1)S(1)}, u32[]{:S(2)}, u32[]{:S(2)}) collective-permute-start(bf16[768,256]{1,0:T(8,128)(2,1)S(1)} %get-tuple-element.32), channel_id=1, source_target_pairs={{0,1},{1,0},{2,3},{3,2},{4,5},{5,4},{6,7},{7,6},{8,9},{9,8},{10,11... | collective-permute-start | bytes 1179656 | tf_op jit(solution)/shard_map/ppermute | solution.py:35
  19.0 10.1 %collective-permute-start.2 = (bf16[1,64,2048]{2,1,0:T(8,128)(2,1)S(1)}, bf16[1,64,2048]{2,1,0:T(8,128)(2,1)S(1)}, u32[]{:S(2)}, u32[]{:S(2)}) collective-permute-start(bf16[1,64,2048]{2,1,0:T(8,128)(2,1)S(1)} %collective-permute-done.1.refs_1_), channel_id=1, source_target_pairs={{0,4},{4,0},{8,12},{12,8},{1,5},{5,1},{9,13},{13,9},{2,6},{6,2},{1... | collective-permute-start | bytes 786440 | tf_op jit(solution)/shard_map/ppermute | solution.py:35
  19.4 13.5 %collective-permute-start.4 = (bf16[1,64,2048]{2,1,0:T(8,128)(2,1)S(1)}, bf16[1,64,2048]{2,1,0:T(8,128)(2,1)S(1)}, u32[]{:S(2)}, u32[]{:S(2)}) collective-permute-start(bf16[1,64,2048]{2,1,0:T(8,128)(2,1)S(1)} %collective-permute-done.1.refs_1_), channel_id=1, source_target_pairs={{0,16},{16,0},{1,17},{17,1},{2,18},{18,2},{3,19},{19,3},{4,20},{20... | collective-permute-start | bytes 786440 | tf_op jit(solution)/shard_map/ppermute | solution.py:35
  26.2 5.6 %collective-permute-start.9 = (bf16[2,64,256]{2,1,0:T(8,128)(2,1)S(1)}, bf16[2,64,256]{2,1,0:T(8,128)(2,1)S(1)}, u32[]{:S(2)}, u32[]{:S(2)}) collective-permute-start(bf16[2,64,256]{2,1,0:T(8,128)(2,1)S(1)} %copy-done.5), channel_id=1, source_target_pairs={{0,8},{4,12},{8,0},{12,4},{1,9},{5,13},{9,1},{13,5},{2,10},{6,14},... | collective-permute-start | bytes 196616 | tf_op jit(solution)/shard_map/ppermute | solution.py:35
  27.5 10.1 %collective-permute-start.8 = (bf16[768,256]{1,0:T(8,128)(2,1)S(1)}, bf16[768,256]{1,0:T(8,128)(2,1)S(1)}, u32[]{:S(2)}, u32[]{:S(2)}) collective-permute-start(bf16[768,256]{1,0:T(8,128)(2,1)S(1)} %add.6), channel_id=1, source_target_pairs={{0,2},{1,3},{2,0},{3,1},{4,6},{5,7},{6,4},{7,5},{8,10},{9,11},{10,... | collective-permute-start | bytes 1179656 | tf_op jit(solution)/shard_map/ppermute | solution.py:35
  29.1 9.0 %collective-permute-start.3 = (bf16[1,64,2048]{2,1,0:T(8,128)(2,1)S(1)}, bf16[1,64,2048]{2,1,0:T(8,128)(2,1)S(1)}, u32[]{:S(2)}, u32[]{:S(2)}) collective-permute-start(bf16[1,64,2048]{2,1,0:T(8,128)(2,1)S(1)} %collective-permute-done.2.refs_0_), channel_id=1, source_target_pairs={{0,16},{16,0},{1,17},{17,1},{2,18},{18,2},{3,19},{19,3},{4,20},{20... | collective-permute-start | bytes 786440 | tf_op jit(solution)/shard_map/ppermute | solution.py:35
  31.8 5.1 %copy-start.4 = (bf16[128,128]{1,0:T(8,128)(2,1)S(1)}, bf16[128,128]{1,0:T(8,128)(2,1)}, u32[]{:S(2)}) copy-start(bf16[128,128]{1,0:T(8,128)(2,1)} %constant.12.clone.matrix_ref) | copy-start | bytes 98308
  31.8 5.1 %copy-start.7 = (s32[768,1]{0,1:T(1,128)S(1)}, s32[768,1]{0,1:T(1,128)}, u32[]{:S(2)}) copy-start(s32[768,1]{0,1:T(1,128)} %param.9) | copy-start | bytes 9220
  31.9 5.1 %copy-start.8 = (s32[128]{0:T(128)S(1)}, s32[128]{0:T(128)}, u32[]{:S(2)}) copy-start(s32[128]{0:T(128)} %param.14) | copy-start | bytes 1540
  31.9 5.7 %copy-start.9 = (f32[256]{0:T(256)S(1)}, f32[256]{0:T(256)}, u32[]{:S(2)}) copy-start(f32[256]{0:T(256)} %param.11) | copy-start | bytes 3076
  31.9 5.0 %collective-permute-start.10 = (bf16[4,64,256]{2,1,0:T(8,128)(2,1)S(1)}, bf16[4,64,256]{2,1,0:T(8,128)(2,1)S(1)}, u32[]{:S(2)}, u32[]{:S(2)}) collective-permute-start(bf16[4,64,256]{2,1,0:T(8,128)(2,1)S(1)} %joined.1.refs_0_), channel_id=1, source_target_pairs={{0,4},{4,0},{8,12},{12,8},{1,5},{5,1},{9,13},{13,9},{2,6},{6,2},{1... | collective-permute-start | bytes 393224 | tf_op jit(solution)/shard_map/ppermute | solution.py:35
  32.9 5.2 %copy-start.1 = (bf16[768,2048]{1,0:T(8,128)(2,1)S(1)}, bf16[768,2048]{1,0:T(8,128)(2,1)}, u32[]{:S(2)}) copy-start(bf16[768,2048]{1,0:T(8,128)(2,1)} %tokens_ref.7) | copy-start | bytes 9437188
  39.2 1.4 %collective-permute-start.11 = (bf16[64,768]{1,0:T(8,128)(2,1)S(1)}, bf16[64,768]{1,0:T(8,128)(2,1)S(1)}, u32[]{:S(2)}, u32[]{:S(2)}) collective-permute-start(bf16[64,768]{1,0:T(8,128)(2,1)S(1)} %low_rows.5.refs_0_), channel_id=1, source_target_pairs={{0,1},{1,0},{2,3},{3,2},{4,5},{5,4},{6,7},{7,6},{8,9},{9,8},{10,11... | collective-permute-start | bytes 294920 | tf_op jit(solution)/shard_map/ppermute | solution.py:35
  40.6 4.9 %collective-permute-start.12 = (bf16[64,768]{1,0:T(8,128)(2,1)S(1)}, bf16[64,768]{1,0:T(8,128)(2,1)S(1)}, u32[]{:S(2)}, u32[]{:S(2)}) collective-permute-start(bf16[64,768]{1,0:T(8,128)(2,1)S(1)} %add.7.mine_ref), channel_id=1, source_target_pairs={{0,2},{1,3},{2,0},{3,1},{4,6},{5,7},{6,4},{7,5},{8,10},{9,11},{10,... | collective-permute-start | bytes 294920 | tf_op jit(solution)/shard_map/ppermute | solution.py:35

commit v10 on v8

--- a/solution.py
+++ b/solution.py
@@ -19,7 +19,10 @@
 
 
 COST = pl.CostEstimate(flops=1, bytes_accessed=1, transcendentals=0)
-SOME = pl.CostEstimate(flops=5_000_000_000, bytes_accessed=1, transcendentals=0)
+
+
+def lasting(microseconds):
+    return pl.CostEstimate(flops=int(microseconds * 1e9), bytes_accessed=1, transcendentals=0)
 
 
 def hadamard(size):
@@ -53,35 +56,26 @@
     return turned
 
 
-def partial_kernel(here, ids_ref, tokens_ref, weight_ref, down_ref, low_ref, *outs):
-    me, width = lax.axis_index("tp"), outs[0].shape[1]
-    for n, out_ref in enumerate(outs):
-        offset = 2 * n + 1 if n < len(outs) // 2 else 2 * n - len(outs)
+def partial_kernel(offsets, parts, tokens_ref, weight_ref, before_ref, after_ref, *outs):
+    me, width = lax.axis_index("tp"), weight_ref.shape[1] // parts
+    for offset, out_ref in zip(offsets, outs):
         at = pl.multiple_of(jnp.bitwise_xor(me, offset) * width, width)
         product = jnp.dot(tokens_ref[...], weight_ref[:, pl.ds(at, width)], preferred_element_type=F32)
         out_ref[...] = product.astype(BF16)
-    rank = down_ref.shape[1]
-    joined = jnp.concatenate([down_ref[k] for k in range(here)], axis=0)
-    product = lax.dot_general(joined, tokens_ref[...], LAST, preferred_element_type=F32)
-    terms = [
-        jnp.where(ids_ref[...] == adapter(here, 0, ("plane", 0, k)), product[k * rank : (k + 1) * rank], 0.0)
-        for k in range(here)
-    ]
-    low_ref[...] = functools.reduce(jnp.add, terms)
-
-
-def partials(ids, tokens, weight, down, parts):
-    rows, width = tokens.shape[0], weight.shape[1] // parts
-    here, rank, _ = down.shape
-    return pl.pallas_call(
-        functools.partial(partial_kernel, here),
-        in_specs=[VMEM] * 4,
-        out_specs=[VMEM] * (1 + parts),
-        out_shape=[jax.ShapeDtypeStruct((rank, rows), F32)] + [jax.ShapeDtypeStruct((rows, width), BF16)] * parts,
+    after_ref[...] = before_ref[...]
+
+
+def partials(tokens, weight, parts, offsets, before, cost):
+    block = jax.ShapeDtypeStruct((tokens.shape[0], weight.shape[1] // parts), BF16)
+    return pl.pallas_call(
+        functools.partial(partial_kernel, offsets, parts),
+        in_specs=[VMEM] * 3,
+        out_specs=[VMEM] * (1 + len(offsets)),
+        out_shape=[jax.ShapeDtypeStruct(before.shape, before.dtype)] + [block] * len(offsets),
         compiler_params=params(24),
-        cost_estimate=COST,
+        cost_estimate=cost,
         name="partials",
-    )(ids, tokens, weight, down)
+    )(tokens, weight, before)
 
 
 def add_kernel(*refs):
@@ -131,9 +125,9 @@
     return jnp.bitwise_xor(z, plane) * here + jnp.bitwise_xor(lax.axis_index("grp"), off) * share + k
 
 
-def low_kernel(groups, here, share, rank, ids_ref, tokens_ref, *refs):
+def low_kernel(groups, here, share, rank, more, ids_ref, tokens_ref, *refs):
     out_ref = refs[-1]
-    total = refs[-2][...]
+    total = refs[-2][...] if more else None
     for (start, stop), terms in groups:
         rows = [refs[i][k, :, cut : cut + stop - start] for i, k, cut, _ in terms]
         joined = rows[0] if len(rows) == 1 else jnp.concatenate(rows, axis=0)
@@ -141,21 +135,22 @@
         for n, (_, _, _, name) in enumerate(terms):
             mine = ids_ref[...] == adapter(here, share, name)
             term = jnp.where(mine, product[n * rank : (n + 1) * rank], 0.0)
-            total = total + term
+            total = term if total is None else total + term
     out_ref[...] = total.astype(out_ref.dtype)
 
 
 def low_rows(ids, tokens, here, share, groups, arrays, before, dtype, cost=COST):
     rank = arrays[0].shape[1]
-    return pl.pallas_call(
-        functools.partial(low_kernel, groups, here, share, rank),
-        in_specs=[VMEM] * (3 + len(arrays)),
+    more = [] if before is None else [before]
+    return pl.pallas_call(
+        functools.partial(low_kernel, groups, here, share, rank, bool(more)),
+        in_specs=[VMEM] * (2 + len(arrays) + len(more)),
         out_specs=VMEM,
         out_shape=jax.ShapeDtypeStruct((rank, tokens.shape[0]), dtype),
         compiler_params=params(24),
         cost_estimate=cost,
         name="low_rows",
-    )(ids, tokens, *arrays, before)
+    )(ids, tokens, *arrays, *more)
 
 
 def join_kernel(first_ref, second_ref, out_ref):
@@ -239,10 +234,13 @@
     while bit > 1:
         mine += [(plane | bit, swap(piece, "adp", bit)) for plane, piece in mine]
         bit //= 2
-    low, *blocks = partials(ids, tokens, base_weight, down, parts)
     half = parts // 2
-    near, low = together(near, low)
-    close, up, *far = together(near, adapter_up, *(piece for _, piece in mine[1:]))
+    offsets = (*range(1, parts, 2), *range(2, parts, 2))
+    passed, *blocks = partials(tokens, base_weight, parts, offsets, scale, lasting(4))
+    near, passed = together(near, passed)
+    scale, block = partials(tokens, base_weight, parts, (0,), passed, COST)
+    blocks = blocks[:half] + [block] + blocks[half:]
+    close, scale, *far = together(near, scale, *(piece for _, piece in mine[1:]))
     mine = mine[:1] + [(plane, piece) for (plane, _), piece in zip(mine[1:], far)]
     odd = [(1, near)] + [(plane | 1, swap(piece, "adp", 1)) for plane, piece in mine[1:]]
 
@@ -255,20 +253,27 @@
     def terms(pieces, start):
         return [(start + i, k, 0, (plane, off, k)) for i, (plane, off, _) in enumerate(pieces) for k in range(share)]
 
-    whole = (0, features)
-    early = held[: len(mine)] + swapped[:1]
-    middle = held[len(mine) :] + swapped[1:-1]
-    late = swapped[-1:]
-    low = low_rows(ids, tokens, here, share, [(whole, terms(early, 0))], [p for *_, p in early], low, F32, SOME)
-
-    ups, order = up, [0]
+    def more(low, pieces, dtype, cost=COST):
+        arrays, every = [p for *_, p in pieces], terms(pieces, 0)
+        if low is None:
+            every += [(len(arrays), k, 0, ("plane", 0, k)) for k in range(here)]
+            arrays = arrays + [down]
+        return low_rows(ids, tokens, here, share, [((0, features), every)], arrays, low, dtype, cost)
+
+    low = more(None, held[: len(mine)] + swapped[:1], F32, lasting(2))
+    low, ups, *came = together(low, adapter_up, *(swap(block, "tp", 1) for block in blocks[:half]))
+
+    order = [0]
     bit = planes // 2
+    rest = held[len(mine) :]
     while bit > 1:
-        ups = joined(ups, swap(ups, "adp", bit))
+        (plane, off, piece), other = rest[0], swap(ups, "adp", bit)
+        piece, other = together(piece, other)
+        rest[0], ups = (plane, off, piece), joined(ups, other)
         order += [plane | bit for plane in order]
         bit //= 2
-
-    low, ups, *came = together(low, ups, *(swap(block, "tp", 1) for block in blocks[:half]))
+    low = more(low, swapped[1:-1] + rest, F32, lasting(5))
+
     sums = [[block, pair] for block, pair in zip(blocks[half:], came)]
     bit = 2
     while bit < parts:
@@ -280,9 +285,8 @@
     every = [(side, here * i + k, 0, ("plane", plane | side, k)) for side in (0, 1) for i, plane in enumerate(order) for k in range(here)]
     up, mask = rotated_ups(ids, bits, matrix, here, share, every, [ups, swap(ups, "adp", 1)], width)
 
-    low = low_rows(ids, tokens, here, share, [(whole, terms(middle, 0))], [p for *_, p in middle], low, F32, SOME)
-    low, base, up, mask = together(low, base, up, mask)
-    low = low_rows(ids, tokens, here, share, [(whole, terms(late, 0))], [p for *_, p in late], low, BF16)
+    low, up, mask = together(low, up, mask)
+    low = more(low, swapped[-1:], BF16)
     bit = 1
     while bit < parts // 2:
         low = add(low, swap(low, "tp", bit))

time: 46 us -> 46.2 us (level)
  waiting for transfers between devices: 11.1 us -> 14.9 us
  starting transfers between devices: 17 us -> 15.3 us
  local copies, waits for them, and re-layouts: 6.83 us -> 5.76 us
  Pallas kernels: 10.6 us -> 9.86 us
    ppermute x13, waiting for transfers between devices: 11.1 us -> 14.9 us  [swap(): lax.ppermute(x, axis, [(i, i ^ bit) for i in range(lax.axis_size(axis))])]
    ppermute x13, starting transfers between devices: 17 us -> 15.3 us  [swap(): lax.ppermute(x, axis, [(i, i ^ bit) for i in range(lax.axis_size(axis))])]
    unnamed x20 -> x18, local copies, waits for them, and re-layouts: 5.83 us -> 4.79 us
    pallas_call x4 -> x5, Pallas kernels: 7.82 us -> 7.12 us  [the longest x2 3.66 us: partials(): pl.pallas_call(functools.partial(partial_kernel, offsets, parts), in_spec...]
  transfers between devices with their start and end apart: 13 -> 13, of which waited for: 6 -> 7; matrix products, arithmetic and copies ran while one was open for 0% -> 0% of each run, Pallas kernels for 18% -> 18%
where the time goes in v10:
time: 46.2 us; the launch traced here: 46 us
  starting transfers between devices  15.3 us (33%)
  waiting for transfers between devices  14.9 us (32%)
  Pallas kernels  9.86 us (21%)
  local copies, waits for them, and re-layouts  5.76 us (12%)
    ppermute x13, starting transfers between devices, swap(): lax.ppermute(x, axis, [(i, i ^ bit) for i in range(lax.axis_size(axis))])  15.3 us
    ppermute x13, waiting for transfers between devices, swap(): lax.ppermute(x, axis, [(i, i ^ bit) for i in range(lax.axis_size(axis))])  14.9 us
    unnamed x18, local copies, waits for them, and re-layouts  4.79 us
    pallas_call x2, Pallas kernels, partials(): pl.pallas_call(functools.partial(partial_kernel, offsets, parts), in_spec...  3.66 us
    pallas_call x3, Pallas kernels, low_rows(): pl.pallas_call(functools.partial(low_kernel, groups, here, share, rank, b...  3.46 us
    pallas_call x1, Pallas kernels, final(): pl.pallas_call(final_kernel, in_specs=[VMEM] * 5, out_specs=VMEM, out_sha...  1.45 us
    dynamic_slice x1, local copies, waits for them, and re-layouts, local(): lax.dynamic_slice_in_dim(down, lax.axis_index('grp') * share, share, 0)  0.97 us
  transfers between devices with their start and end apart: 13, of which 7 were waited for; matrix products, arithmetic and copies ran while one was open for 0% of the time, Pallas kernels for 18%

profile of v10, /device:TPU:0, one launch (start us, length us, event | category | flops | bytes accessed | tf_op | source)
XLA Modules:
  0.0 46.0 jit_solution(18093907521137072741)
XLA Ops:
  0.0 1.0 %dynamic-slice_bitcast_fusion = bf16[1,64,2048]{2,1,0:T(8,128)(2,1)S(1)} fusion(bf16[2,2048,64]{1,2,0:T(8,128)(2,1)} %param.12, s32[]{:T(128)S(6)} %select_n.3), kind=kLoop, calls=%fused_computation | loop fusion | bytes 524292 | tf_op jit(solution)/shard_map/dynamic_slice | solution.py:230
  1.0 3.1 %collective-permute-start = (bf16[1,64,2048]{2,1,0:T(8,128)(2,1)S(1)}, bf16[1,64,2048]{2,1,0:T(8,128)(2,1)S(1)}, u32[]{:S(2)}, u32[]{:S(2)}) collective-permute-start(bf16[1,64,2048]{2,1,0:T(8,128)(2,1)S(1)} %dynamic-slice_bitcast_fusion), channel_id=1, source_target_pairs={{0,4},{4,0},{8,12},{12,8},{1,5},{5,1},{9,13},{13,9},{2,6},{6,2},{1... | collective-permute-start | bytes 786440 | tf_op jit(solution)/shard_map/ppermute | solution.py:38
  4.1 2.6 %collective-permute-start.1 = (bf16[1,64,2048]{2,1,0:T(8,128)(2,1)S(1)}, bf16[1,64,2048]{2,1,0:T(8,128)(2,1)S(1)}, u32[]{:S(2)}, u32[]{:S(2)}) collective-permute-start(bf16[1,64,2048]{2,1,0:T(8,128)(2,1)S(1)} %dynamic-slice_bitcast_fusion), channel_id=1, source_target_pairs={{0,8},{4,12},{8,0},{12,4},{1,9},{5,13},{9,1},{13,5},{2,10},{6,14},... | collective-permute-start | bytes 786440 | tf_op jit(solution)/shard_map/ppermute | solution.py:38
  6.7 1.9 %copy-done = bf16[768,2048]{1,0:T(8,128)(2,1)S(1)} copy-done((bf16[768,2048]{1,0:T(8,128)(2,1)S(1)}, bf16[768,2048]{1,0:T(8,128)(2,1)}, u32[]{:S(2)}) %copy-start) | copy-done | bytes 3145752
  8.5 2.2 %copy-done.2 = bf16[2048,1024]{1,0:T(8,128)(2,1)S(1)} copy-done((bf16[2048,1024]{1,0:T(8,128)(2,1)S(1)}, bf16[2048,1024]{1,0:T(8,128)(2,1)}, u32[]{:S(2)}) %copy-start.2) | copy-done | bytes 4194328
  10.7 0.7 %copy-done.8 = f32[256]{0:T(256)S(1)} copy-done((f32[256]{0:T(256)S(1)}, f32[256]{0:T(256)}, u32[]{:S(2)}) %copy-start.8) | copy-done | bytes 1048
  11.4 2.7 %partials.2 = (f32[1,256]{1,0:T(1,128)S(1)}, bf16[768,256]{1,0:T(8,128)(2,1)S(1)}, bf16[768,256]{1,0:T(8,128)(2,1)S(1)}, bf16[768,256]{1,0:T(8,128)(2,1)S(1)}) custom-call(bf16[768,2048]{1,0:T(8,128)(2,1)S(1)} %copy-done, bf16[2048,1024]{1,0:T(8,128)(2,1)S(1)} %copy-done.2, f32[1,256]{1,0:T(1,128)S(1)} %bitcast.13), custom_call_target="tpu_custom_call" | custom-call | flops 4000000000 | bytes 1 | tf_op jit(solution)/shard_map/partials/pallas_call | solution.py:70
  14.1 1.8 %collective-permute-done.refs_0_ = bf16[1,64,2048]{2,1,0:T(8,128)(2,1)S(1)} collective-permute-done((bf16[1,64,2048]{2,1,0:T(8,128)(2,1)S(1)}, bf16[1,64,2048]{2,1,0:T(8,128)(2,1)S(1)}, u32[]{:S(2)}, u32[]{:S(2)}) %collective-permute-start) | collective-permute-done | bytes 262176 | tf_op jit(solution)/shard_map/ppermute | solution.py:38
  15.9 1.7 %collective-permute-start.5 = (bf16[1,64,2048]{2,1,0:T(8,128)(2,1)S(1)}, bf16[1,64,2048]{2,1,0:T(8,128)(2,1)S(1)}, u32[]{:S(2)}, u32[]{:S(2)}) collective-permute-start(bf16[1,64,2048]{2,1,0:T(8,128)(2,1)S(1)} %collective-permute-done.refs_0_), channel_id=1, source_target_pairs={{0,16},{16,0},{1,17},{17,1},{2,18},{18,2},{3,19},{19,3},{4,20},{20... | collective-permute-start | bytes 786440 | tf_op jit(solution)/shard_map/ppermute | solution.py:38
  17.6 0.5 %collective-permute-start.7 = (bf16[768,256]{1,0:T(8,128)(2,1)S(1)}, bf16[768,256]{1,0:T(8,128)(2,1)S(1)}, u32[]{:S(2)}, u32[]{:S(2)}) collective-permute-start(bf16[768,256]{1,0:T(8,128)(2,1)S(1)} %get-tuple-element.34), channel_id=1, source_target_pairs={{0,1},{1,0},{2,3},{3,2},{4,5},{5,4},{6,7},{7,6},{8,9},{9,8},{10,11... | collective-permute-start | bytes 1179656 | tf_op jit(solution)/shard_map/ppermute | solution.py:38
  18.1 1.0 %partials.3 = (f32[1,256]{1,0:T(1,128)S(1)}, bf16[768,256]{1,0:T(8,128)(2,1)S(1)}) custom-call(bf16[768,2048]{1,0:T(8,128)(2,1)S(1)} %copy-done, bf16[2048,1024]{1,0:T(8,128)(2,1)S(1)} %copy-done.2, f32[1,256]{1,0:T(1,128)S(1)} %get-tuple-element.29.before_ref), custom_call_target="tpu_custom_call" | custom-call | flops 1 | bytes 1 | tf_op jit(solution)/shard_map/partials/pallas_call | solution.py:70
  19.1 0.1 collective-permute-start.2
  19.2 1.2 %collective-permute-start.4 = (bf16[1,64,2048]{2,1,0:T(8,128)(2,1)S(1)}, bf16[1,64,2048]{2,1,0:T(8,128)(2,1)S(1)}, u32[]{:S(2)}, u32[]{:S(2)}) collective-permute-start(bf16[1,64,2048]{2,1,0:T(8,128)(2,1)S(1)} %collective-permute-done.1.refs_1_), channel_id=1, source_target_pairs={{0,16},{16,0},{1,17},{17,1},{2,18},{18,2},{3,19},{19,3},{4,20},{20... | collective-permute-start | bytes 786440 | tf_op jit(solution)/shard_map/ppermute | solution.py:38
  20.4 4.4 %collective-permute-done.5.refs_2_ = bf16[1,64,2048]{2,1,0:T(8,128)(2,1)S(1)} collective-permute-done((bf16[1,64,2048]{2,1,0:T(8,128)(2,1)S(1)}, bf16[1,64,2048]{2,1,0:T(8,128)(2,1)S(1)}, u32[]{:S(2)}, u32[]{:S(2)}) %collective-permute-start.5) | collective-permute-done | bytes 262176 | tf_op jit(solution)/shard_map/ppermute | solution.py:38
  24.8 1.2 %low_rows.3.refs_2_ = f32[64,768]{1,0:T(8,128)S(1)} custom-call(s32[1,768]{1,0:T(1,128)S(1)} %bitcast.7, bf16[768,2048]{1,0:T(8,128)(2,1)S(1)} %copy-done.1, bf16[1,64,2048]{2,1,0:T(8,128)(2,1)S(1)} %collective-permute-done.refs_0_, bf16[1,64,2048]{2,1,0:T(8,128)(2,1)S(1)} %collective-permute-done.1.refs_1_, ...), custom_call_target="tpu_custom_call" | custom-call | flops 2000000000 | bytes 1 | tf_op jit(solution)/shard_map/low_rows/pallas_call | solution.py:145
  26.1 0.1 collective-permute-start.8
  26.1 0.1 add.7
  26.2 1.3 %collective-permute-start.12 = (bf16[768,256]{1,0:T(8,128)(2,1)S(1)}, bf16[768,256]{1,0:T(8,128)(2,1)S(1)}, u32[]{:S(2)}, u32[]{:S(2)}) collective-permute-start(bf16[768,256]{1,0:T(8,128)(2,1)S(1)} %add.7), channel_id=1, source_target_pairs={{0,2},{1,3},{2,0},{3,1},{4,6},{5,7},{6,4},{7,5},{8,10},{9,11},{10,... | collective-permute-start | bytes 1179656 | tf_op jit(solution)/shard_map/ppermute | solution.py:38
  27.5 0.6 %collective-permute-done.2.refs_1_ = bf16[1,64,2048]{2,1,0:T(8,128)(2,1)S(1)} collective-permute-done((bf16[1,64,2048]{2,1,0:T(8,128)(2,1)S(1)}, bf16[1,64,2048]{2,1,0:T(8,128)(2,1)S(1)}, u32[]{:S(2)}, u32[]{:S(2)}) %collective-permute-start.2) | collective-permute-done | bytes 262176 | tf_op jit(solution)/shard_map/ppermute | solution.py:38
  28.1 1.7 %collective-permute-start.3 = (bf16[1,64,2048]{2,1,0:T(8,128)(2,1)S(1)}, bf16[1,64,2048]{2,1,0:T(8,128)(2,1)S(1)}, u32[]{:S(2)}, u32[]{:S(2)}) collective-permute-start(bf16[1,64,2048]{2,1,0:T(8,128)(2,1)S(1)} %collective-permute-done.2.refs_1_), channel_id=1, source_target_pairs={{0,16},{16,0},{1,17},{17,1},{2,18},{18,2},{3,19},{19,3},{4,20},{20... | collective-permute-start | bytes 786440 | tf_op jit(solution)/shard_map/ppermute | solution.py:38
  29.8 1.6 %collective-permute-done.8.second_ref = bf16[2,64,256]{2,1,0:T(8,128)(2,1)S(1)} collective-permute-done((bf16[2,64,256]{2,1,0:T(8,128)(2,1)S(1)}, bf16[2,64,256]{2,1,0:T(8,128)(2,1)S(1)}, u32[]{:S(2)}, u32[]{:S(2)}) %collective-permute-start.8) | collective-permute-done | bytes 65568 | tf_op jit(solution)/shard_map/ppermute | solution.py:38
  31.4 1.5 %collective-permute-start.9 = (bf16[4,64,256]{2,1,0:T(8,128)(2,1)S(1)}, bf16[4,64,256]{2,1,0:T(8,128)(2,1)S(1)}, u32[]{:S(2)}, u32[]{:S(2)}) collective-permute-start(bf16[4,64,256]{2,1,0:T(8,128)(2,1)S(1)} %joined.1.refs_0_), channel_id=1, source_target_pairs={{0,4},{4,0},{8,12},{12,8},{1,5},{5,1},{9,13},{13,9},{2,6},{6,2},{1... | collective-permute-start | bytes 393224 | tf_op jit(solution)/shard_map/ppermute | solution.py:38
  32.9 1.2 %low_rows.4.refs_1_ = f32[64,768]{1,0:T(8,128)S(1)} custom-call(s32[1,768]{1,0:T(1,128)S(1)} %bitcast.8, bf16[768,2048]{1,0:T(8,128)(2,1)S(1)} %copy-done.1, bf16[1,64,2048]{2,1,0:T(8,128)(2,1)S(1)} %collective-permute-done.4.refs_0_, bf16[1,64,2048]{2,1,0:T(8,128)(2,1)S(1)} %collective-permute-done.2.refs_1_, f32[64,768]{1,0:T(8,128)S(1)} %low_rows.3.refs_2_), custom_call_target="tpu_custom_call" | custom-call | flops 5000000000 | bytes 1 | tf_op jit(solution)/shard_map/low_rows/pallas_call | solution.py:145
  34.1 2.4 %collective-permute-done.9.refs_1_ = bf16[4,64,256]{2,1,0:T(8,128)(2,1)S(1)} collective-permute-done((bf16[4,64,256]{2,1,0:T(8,128)(2,1)S(1)}, bf16[4,64,256]{2,1,0:T(8,128)(2,1)S(1)}, u32[]{:S(2)}, u32[]{:S(2)}) %collective-permute-start.9) | collective-permute-done | bytes 131104 | tf_op jit(solution)/shard_map/ppermute | solution.py:38
  36.5 0.7 %rotated_ups.1 = (bf16[512,256]{1,0:T(8,128)(2,1)S(1)}, bf16[768,512]{1,0:T(8,128)(2,1)S(1)}) custom-call(s32[1,768]{1,0:T(1,128)S(1)} %bitcast.9, s32[1,128]{1,0:T(1,128)S(1)} %bitcast.11, bf16[128,128]{1,0:T(8,128)(2,1)S(1)} %copy-done.3, bf16[4,64,256]{2,1,0:T(8,128)(2,1)S(1)} %joined.1.refs_0_, bf16[4,64,256]{2,1,0:T(8,128)(2,1)S(1)} %collective-permute-done.9.refs_1_), custom_call_target="tpu_custom_call" | custom-call | flops 1 | bytes 1 | tf_op jit(solution)/shard_map/rotated_ups/pallas_call | solution.py:188
  37.2 1.1 %low_rows.5.refs_0_ = bf16[64,768]{1,0:T(8,128)(2,1)S(1)} custom-call(s32[1,768]{1,0:T(1,128)S(1)} %bitcast.10, bf16[768,2048]{1,0:T(8,128)(2,1)S(1)} %copy-done.1, bf16[1,64,2048]{2,1,0:T(8,128)(2,1)S(1)} %collective-permute-done.3.refs_0_, f32[64,768]{1,0:T(8,128)S(1)} %low_rows.4.refs_1_), custom_call_target="tpu_custom_call" | custom-call | flops 1 | bytes 1 | tf_op jit(solution)/shard_map/low_rows/pallas_call | solution.py:145
  38.3 0.1 collective-permute-start.10
  38.3 1.3 %collective-permute-done.10.refs_1_ = bf16[64,768]{1,0:T(8,128)(2,1)S(1)} collective-permute-done((bf16[64,768]{1,0:T(8,128)(2,1)S(1)}, bf16[64,768]{1,0:T(8,128)(2,1)S(1)}, u32[]{:S(2)}, u32[]{:S(2)}) %collective-permute-start.10) | collective-permute-done | bytes 98336 | tf_op jit(solution)/shard_map/ppermute | solution.py:38
  39.6 1.5 %collective-permute-start.11 = (bf16[64,768]{1,0:T(8,128)(2,1)S(1)}, bf16[64,768]{1,0:T(8,128)(2,1)S(1)}, u32[]{:S(2)}, u32[]{:S(2)}) collective-permute-start(bf16[64,768]{1,0:T(8,128)(2,1)S(1)} %add.6.mine_ref), channel_id=1, source_target_pairs={{0,2},{1,3},{2,0},{3,1},{4,6},{5,7},{6,4},{7,5},{8,10},{9,11},{10,... | collective-permute-start | bytes 294920 | tf_op jit(solution)/shard_map/ppermute | solution.py:38
  41.2 0.5 %rotated_base.1.base_ref = f32[768,256]{1,0:T(8,128)S(1)} custom-call(f32[1,256]{1,0:T(1,128)S(1)} %get-tuple-element.42.scale_ref, s32[1,128]{1,0:T(1,128)S(1)} %bitcast.12, bf16[128,128]{1,0:T(8,128)(2,1)S(1)} %copy-done.3, bf16[768,256]{1,0:T(8,128)(2,1)S(1)} %get-tuple-element.43.refs_0_, bf16[768,256]{1,0:T(8,128)(2,1)S(1)} %collective-permute-done.6.refs_1_, ...), custom_call_target="tpu_custom_call" | custom-call | flops 1 | bytes 1 | tf_op jit(solution)/shard_map/rotated_base/pallas_call | solution.py:109
  41.7 2.9 %collective-permute-done.11.theirs_ref = bf16[64,768]{1,0:T(8,128)(2,1)S(1)} collective-permute-done((bf16[64,768]{1,0:T(8,128)(2,1)S(1)}, bf16[64,768]{1,0:T(8,128)(2,1)S(1)}, u32[]{:S(2)}, u32[]{:S(2)}) %collective-permute-start.11) | collective-permute-done | bytes 98336 | tf_op jit(solution)/shard_map/ppermute | solution.py:38
  44.6 1.4 %final.1 = bf16[768,256]{1,0:T(8,128)(2,1)} custom-call(bf16[64,768]{1,0:T(8,128)(2,1)S(1)} %add.6.mine_ref, bf16[64,768]{1,0:T(8,128)(2,1)S(1)} %collective-permute-done.11.theirs_ref, f32[768,256]{1,0:T(8,128)S(1)} %rotated_base.1.base_ref, bf16[512,256]{1,0:T(8,128)(2,1)S(1)} %get-tuple-element.47.up_ref, bf16[768,512]{1,0:T(8,128)(2,1)S(1)} %get-tuple-element.48.mask_ref), custom_call_target="tpu_custom_call" | custom-call | flops 1 | bytes 1 | tf_op jit(solution)/shard_map/final/pallas_call | solution.py:209
  (24 shorter events, 0.1 us)
Async XLA Ops:
  1.0 14.9 %collective-permute-start = (bf16[1,64,2048]{2,1,0:T(8,128)(2,1)S(1)}, bf16[1,64,2048]{2,1,0:T(8,128)(2,1)S(1)}, u32[]{:S(2)}, u32[]{:S(2)}) collective-permute-start(bf16[1,64,2048]{2,1,0:T(8,128)(2,1)S(1)} %dynamic-slice_bitcast_fusion), channel_id=1, source_target_pairs={{0,4},{4,0},{8,12},{12,8},{1,5},{5,1},{9,13},{13,9},{2,6},{6,2},{1... | collective-permute-start | bytes 786440 | tf_op jit(solution)/shard_map/ppermute | solution.py:38
  4.1 15.0 %collective-permute-start.1 = (bf16[1,64,2048]{2,1,0:T(8,128)(2,1)S(1)}, bf16[1,64,2048]{2,1,0:T(8,128)(2,1)S(1)}, u32[]{:S(2)}, u32[]{:S(2)}) collective-permute-start(bf16[1,64,2048]{2,1,0:T(8,128)(2,1)S(1)} %dynamic-slice_bitcast_fusion), channel_id=1, source_target_pairs={{0,8},{4,12},{8,0},{12,4},{1,9},{5,13},{9,1},{13,5},{2,10},{6,14},... | collective-permute-start | bytes 786440 | tf_op jit(solution)/shard_map/ppermute | solution.py:38
  6.7 1.9 %copy-start = (bf16[768,2048]{1,0:T(8,128)(2,1)S(1)}, bf16[768,2048]{1,0:T(8,128)(2,1)}, u32[]{:S(2)}) copy-start(bf16[768,2048]{1,0:T(8,128)(2,1)} %tokens_ref.9) | copy-start | bytes 9437188
  8.5 2.2 %copy-start.2 = (bf16[2048,1024]{1,0:T(8,128)(2,1)S(1)}, bf16[2048,1024]{1,0:T(8,128)(2,1)}, u32[]{:S(2)}) copy-start(bf16[2048,1024]{1,0:T(8,128)(2,1)} %weight_ref.3) | copy-start | bytes 12582916
  10.7 0.7 %copy-start.8 = (f32[256]{0:T(256)S(1)}, f32[256]{0:T(256)}, u32[]{:S(2)}) copy-start(f32[256]{0:T(256)} %param.11) | copy-start | bytes 3076
  14.1 10.7 %copy-start.1 = (bf16[768,2048]{1,0:T(8,128)(2,1)S(1)}, bf16[768,2048]{1,0:T(8,128)(2,1)}, u32[]{:S(2)}) copy-start(bf16[768,2048]{1,0:T(8,128)(2,1)} %tokens_ref.9) | copy-start | bytes 9437188
  14.1 10.7 %copy-start.4 = (bf16[2,2048,64]{1,2,0:T(8,128)(2,1)S(1)}, bf16[2,2048,64]{1,2,0:T(8,128)(2,1)}, u32[]{:S(2)}) copy-start(bf16[2,2048,64]{1,2,0:T(8,128)(2,1)} %param.12) | copy-start | bytes 1572868
  14.1 10.7 %copy-start.6 = (s32[768,1]{0,1:T(1,128)S(1)}, s32[768,1]{0,1:T(1,128)}, u32[]{:S(2)}) copy-start(s32[768,1]{0,1:T(1,128)} %param.9) | copy-start | bytes 9220
  15.9 8.9 %collective-permute-start.5 = (bf16[1,64,2048]{2,1,0:T(8,128)(2,1)S(1)}, bf16[1,64,2048]{2,1,0:T(8,128)(2,1)S(1)}, u32[]{:S(2)}, u32[]{:S(2)}) collective-permute-start(bf16[1,64,2048]{2,1,0:T(8,128)(2,1)S(1)} %collective-permute-done.refs_0_), channel_id=1, source_target_pairs={{0,16},{16,0},{1,17},{17,1},{2,18},{18,2},{3,19},{19,3},{4,20},{20... | collective-permute-start | bytes 786440 | tf_op jit(solution)/shard_map/ppermute | solution.py:38
  17.6 8.5 %collective-permute-start.6 = (bf16[768,256]{1,0:T(8,128)(2,1)S(1)}, bf16[768,256]{1,0:T(8,128)(2,1)S(1)}, u32[]{:S(2)}, u32[]{:S(2)}) collective-permute-start(bf16[768,256]{1,0:T(8,128)(2,1)S(1)} %get-tuple-element.33), channel_id=1, source_target_pairs={{0,1},{1,0},{2,3},{3,2},{4,5},{5,4},{6,7},{7,6},{8,9},{9,8},{10,11... | collective-permute-start | bytes 1179656 | tf_op jit(solution)/shard_map/ppermute | solution.py:38
  17.6 8.5 %collective-permute-start.7 = (bf16[768,256]{1,0:T(8,128)(2,1)S(1)}, bf16[768,256]{1,0:T(8,128)(2,1)S(1)}, u32[]{:S(2)}, u32[]{:S(2)}) collective-permute-start(bf16[768,256]{1,0:T(8,128)(2,1)S(1)} %get-tuple-element.34), channel_id=1, source_target_pairs={{0,1},{1,0},{2,3},{3,2},{4,5},{5,4},{6,7},{7,6},{8,9},{9,8},{10,11... | collective-permute-start | bytes 1179656 | tf_op jit(solution)/shard_map/ppermute | solution.py:38
  19.1 7.0 %copy-start.5 = (bf16[2,64,256]{2,1,0:T(8,128)(2,1)S(1)}, bf16[2,64,256]{2,1,0:T(8,128)(2,1)}, u32[]{:S(2)}) copy-start(bf16[2,64,256]{2,1,0:T(8,128)(2,1)} %first_ref) | copy-start | bytes 196612
  19.1 9.0 %collective-permute-start.2 = (bf16[1,64,2048]{2,1,0:T(8,128)(2,1)S(1)}, bf16[1,64,2048]{2,1,0:T(8,128)(2,1)S(1)}, u32[]{:S(2)}, u32[]{:S(2)}) collective-permute-start(bf16[1,64,2048]{2,1,0:T(8,128)(2,1)S(1)} %collective-permute-done.1.refs_1_), channel_id=1, source_target_pairs={{0,4},{4,0},{8,12},{12,8},{1,5},{5,1},{9,13},{13,9},{2,6},{6,2},{1... | collective-permute-start | bytes 786440 | tf_op jit(solution)/shard_map/ppermute | solution.py:38
  19.2 13.8 %collective-permute-start.4 = (bf16[1,64,2048]{2,1,0:T(8,128)(2,1)S(1)}, bf16[1,64,2048]{2,1,0:T(8,128)(2,1)S(1)}, u32[]{:S(2)}, u32[]{:S(2)}) collective-permute-start(bf16[1,64,2048]{2,1,0:T(8,128)(2,1)S(1)} %collective-permute-done.1.refs_1_), channel_id=1, source_target_pairs={{0,16},{16,0},{1,17},{17,1},{2,18},{18,2},{3,19},{19,3},{4,20},{20... | collective-permute-start | bytes 786440 | tf_op jit(solution)/shard_map/ppermute | solution.py:38
  26.1 5.3 %collective-permute-start.8 = (bf16[2,64,256]{2,1,0:T(8,128)(2,1)S(1)}, bf16[2,64,256]{2,1,0:T(8,128)(2,1)S(1)}, u32[]{:S(2)}, u32[]{:S(2)}) collective-permute-start(bf16[2,64,256]{2,1,0:T(8,128)(2,1)S(1)} %copy-done.5), channel_id=1, source_target_pairs={{0,8},{4,12},{8,0},{12,4},{1,9},{5,13},{9,1},{13,5},{2,10},{6,14},... | collective-permute-start | bytes 196616 | tf_op jit(solution)/shard_map/ppermute | solution.py:38
  26.2 14.9 %collective-permute-start.12 = (bf16[768,256]{1,0:T(8,128)(2,1)S(1)}, bf16[768,256]{1,0:T(8,128)(2,1)S(1)}, u32[]{:S(2)}, u32[]{:S(2)}) collective-permute-start(bf16[768,256]{1,0:T(8,128)(2,1)S(1)} %add.7), channel_id=1, source_target_pairs={{0,2},{1,3},{2,0},{3,1},{4,6},{5,7},{6,4},{7,5},{8,10},{9,11},{10,... | collective-permute-start | bytes 1179656 | tf_op jit(solution)/shard_map/ppermute | solution.py:38
  28.1 9.1 %collective-permute-start.3 = (bf16[1,64,2048]{2,1,0:T(8,128)(2,1)S(1)}, bf16[1,64,2048]{2,1,0:T(8,128)(2,1)S(1)}, u32[]{:S(2)}, u32[]{:S(2)}) collective-permute-start(bf16[1,64,2048]{2,1,0:T(8,128)(2,1)S(1)} %collective-permute-done.2.refs_1_), channel_id=1, source_target_pairs={{0,16},{16,0},{1,17},{17,1},{2,18},{18,2},{3,19},{19,3},{4,20},{20... | collective-permute-start | bytes 786440 | tf_op jit(solution)/shard_map/ppermute | solution.py:38
  31.4 5.1 %copy-start.3 = (bf16[128,128]{1,0:T(8,128)(2,1)S(1)}, bf16[128,128]{1,0:T(8,128)(2,1)}, u32[]{:S(2)}) copy-start(bf16[128,128]{1,0:T(8,128)(2,1)} %constant.12.clone.matrix_ref) | copy-start | bytes 98308
  31.4 5.1 %copy-start.7 = (s32[128]{0:T(128)S(1)}, s32[128]{0:T(128)}, u32[]{:S(2)}) copy-start(s32[128]{0:T(128)} %param.14) | copy-start | bytes 1540
  31.4 5.0 %collective-permute-start.9 = (bf16[4,64,256]{2,1,0:T(8,128)(2,1)S(1)}, bf16[4,64,256]{2,1,0:T(8,128)(2,1)S(1)}, u32[]{:S(2)}, u32[]{:S(2)}) collective-permute-start(bf16[4,64,256]{2,1,0:T(8,128)(2,1)S(1)} %joined.1.refs_0_), channel_id=1, source_target_pairs={{0,4},{4,0},{8,12},{12,8},{1,5},{5,1},{9,13},{13,9},{2,6},{6,2},{1... | collective-permute-start | bytes 393224 | tf_op jit(solution)/shard_map/ppermute | solution.py:38
  38.3 1.4 %collective-permute-start.10 = (bf16[64,768]{1,0:T(8,128)(2,1)S(1)}, bf16[64,768]{1,0:T(8,128)(2,1)S(1)}, u32[]{:S(2)}, u32[]{:S(2)}) collective-permute-start(bf16[64,768]{1,0:T(8,128)(2,1)S(1)} %low_rows.5.refs_0_), channel_id=1, source_target_pairs={{0,1},{1,0},{2,3},{3,2},{4,5},{5,4},{6,7},{7,6},{8,9},{9,8},{10,11... | collective-permute-start | bytes 294920 | tf_op jit(solution)/shard_map/ppermute | solution.py:38
  39.6 4.9 %collective-permute-start.11 = (bf16[64,768]{1,0:T(8,128)(2,1)S(1)}, bf16[64,768]{1,0:T(8,128)(2,1)S(1)}, u32[]{:S(2)}, u32[]{:S(2)}) collective-permute-start(bf16[64,768]{1,0:T(8,128)(2,1)S(1)} %add.6.mine_ref), channel_id=1, source_target_pairs={{0,2},{1,3},{2,0},{3,1},{4,6},{5,7},{6,4},{7,5},{8,10},{9,11},{10,... | collective-permute-start | bytes 294920 | tf_op jit(solution)/shard_map/ppermute | solution.py:38

commit v11 on v10

--- a/solution.py
+++ b/solution.py
@@ -153,23 +153,6 @@
     )(ids, tokens, *arrays, *more)
 
 
-def join_kernel(first_ref, second_ref, out_ref):
-    out_ref[: first_ref.shape[0]] = first_ref[...]
-    out_ref[first_ref.shape[0] :] = second_ref[...]
-
-
-def joined(first, second):
-    return pl.pallas_call(
-        join_kernel,
-        in_specs=[VMEM] * 2,
-        out_specs=VMEM,
-        out_shape=jax.ShapeDtypeStruct((2 * first.shape[0], *first.shape[1:]), BF16),
-        compiler_params=params(16),
-        cost_estimate=COST,
-        name="joined",
-    )(first, second)
-
-
 def ups_kernel(terms, here, share, rank, ids_ref, bits_ref, matrix_ref, *refs):
     up_ref, mask_ref = refs[-2:]
     width = up_ref.shape[1]
@@ -227,9 +210,10 @@
     bits, scale, ids = sign_bits[None, :], channel_scale[None, :], adapter_ids.T
     down = jnp.swapaxes(adapter_down, 1, 2)
 
-    own = lax.dynamic_slice_in_dim(down, lax.axis_index("grp") * share, share, 0)
+    start = lax.axis_index("grp") * share
+    own = lax.dynamic_slice_in_dim(down, start, share, 0)
     near = swap(own, "adp", 1)
-    mine = [(0, own)]
+    mine = [(0, jnp.concatenate([own, lax.dynamic_slice_in_dim(adapter_up, start, share, 0)], axis=2))]
     bit = planes // 2
     while bit > 1:
         mine += [(plane | bit, swap(piece, "adp", bit)) for plane, piece in mine]
@@ -261,17 +245,13 @@
         return low_rows(ids, tokens, here, share, [((0, features), every)], arrays, low, dtype, cost)
 
     low = more(None, held[: len(mine)] + swapped[:1], F32, lasting(2))
-    low, ups, *came = together(low, adapter_up, *(swap(block, "tp", 1) for block in blocks[:half]))
-
-    order = [0]
-    bit = planes // 2
+    low, *came = together(low, *(swap(block, "tp", 1) for block in blocks[:half]))
+
     rest = held[len(mine) :]
-    while bit > 1:
-        (plane, off, piece), other = rest[0], swap(ups, "adp", bit)
-        piece, other = together(piece, other)
-        rest[0], ups = (plane, off, piece), joined(ups, other)
-        order += [plane | bit for plane in order]
-        bit //= 2
+    plane, off, piece = swapped[-2]
+    piece, up = together(piece, adapter_up)
+    swapped[-2] = plane, off, piece
+    ups = [adapter_up, swap(up, "adp", 1)]
     low = more(low, swapped[1:-1] + rest, F32, lasting(5))
 
     sums = [[block, pair] for block, pair in zip(blocks[half:], came)]
@@ -282,18 +262,20 @@
         bit *= 2
     base = rotated_base(sums[0], scale, bits, matrix)
 
-    every = [(side, here * i + k, 0, ("plane", plane | side, k)) for side in (0, 1) for i, plane in enumerate(order) for k in range(here)]
-    up, mask = rotated_ups(ids, bits, matrix, here, share, every, [ups, swap(ups, "adp", 1)], width)
-
-    low, up, mask = together(low, up, mask)
+    low, ups[1] = together(low, ups[1])
     low = more(low, swapped[-1:], BF16)
     bit = 1
     while bit < parts // 2:
         low = add(low, swap(low, "tp", bit))
         bit *= 2
-    other = swap(low, "tp", bit)
-
-    return final(low, other, base, up, mask)
+    theirs = swap(low, "tp", bit)
+
+
+    far = [one for one in held + swapped if one[0] > 1]
+    every = [(plane, k, 0, ("plane", plane, k)) for plane in (0, 1) for k in range(here)]
+    every += [(2 + i, k, features, (plane, off, k)) for i, (plane, off, _) in enumerate(far) for k in range(share)]
+    up, mask = rotated_ups(ids, bits, matrix, here, share, every, ups + [piece for *_, piece in far], width)
+    return final(low, theirs, base, up, mask)
 
 
 def solution(mesh):

time: 46.2 us -> 45.9 us (level)
  starting transfers between devices: 15.3 us -> 14.4 us
  local copies, waits for them, and re-layouts: 5.76 us -> 6.52 us
    ppermute x13 -> x12, starting transfers between devices: 15.3 us -> 14.4 us  [swap(): lax.ppermute(x, axis, [(i, i ^ bit) for i in range(lax.axis_size(axis))])]
    dynamic_slice x1 -> x2, local copies, waits for them, and re-layouts: 0.97 us -> 1.73 us  [the longest x1 0.97 us: local(): own = lax.dynamic_slice_in_dim(down, start, share, 0)]
    ppermute x13 -> x12, waiting for transfers between devices: 14.9 us -> 14.7 us  [swap(): lax.ppermute(x, axis, [(i, i ^ bit) for i in range(lax.axis_size(axis))])]
  transfers between devices with their start and end apart: 13 -> 12, of which waited for: 7 -> 9; matrix products, arithmetic and copies ran while one was open for 0% -> 2% of each run, Pallas kernels for 18% -> 18%
where the time goes in v11:
time: 45.9 us; the launch traced here: 45.6 us
  waiting for transfers between devices  14.7 us (32%)
  starting transfers between devices  14.4 us (31%)
  Pallas kernels  9.84 us (21%)
  local copies, waits for them, and re-layouts  6.52 us (14%)
    ppermute x12, waiting for transfers between devices, swap(): lax.ppermute(x, axis, [(i, i ^ bit) for i in range(lax.axis_size(axis))])  14.7 us
    ppermute x12, starting transfers between devices, swap(): lax.ppermute(x, axis, [(i, i ^ bit) for i in range(lax.axis_size(axis))])  14.4 us
    unnamed x18, local copies, waits for them, and re-layouts  4.79 us
    pallas_call x2, Pallas kernels, partials(): pl.pallas_call(functools.partial(partial_kernel, offsets, parts), in_spec...  3.66 us
    pallas_call x3, Pallas kernels, low_rows(): pl.pallas_call(functools.partial(low_kernel, groups, here, share, rank, b...  3.46 us
    pallas_call x1, Pallas kernels, final(): pl.pallas_call(final_kernel, in_specs=[VMEM] * 5, out_specs=VMEM, out_sha...  1.45 us
    dynamic_slice x1, local copies, waits for them, and re-layouts, local(): own = lax.dynamic_slice_in_dim(down, start, share, 0)  0.97 us
  transfers between devices with their start and end apart: 12, of which 9 were waited for; matrix products, arithmetic and copies ran while one was open for 2% of the time, Pallas kernels for 18%

profile of v11, /device:TPU:0, one launch (start us, length us, event | category | flops | bytes accessed | tf_op | source)
XLA Modules:
  0.0 45.6 jit_solution(8171321414172187767)
XLA Ops:
  0.0 1.0 %dynamic-slice_bitcast_fusion = bf16[1,64,2048]{2,1,0:T(8,128)(2,1)S(1)} fusion(bf16[2,2048,64]{1,2,0:T(8,128)(2,1)} %param.12, s32[]{:T(128)S(6)} %select_n.4), kind=kLoop, calls=%fused_computation.1 | loop fusion | bytes 524292 | tf_op jit(solution)/shard_map/dynamic_slice | solution.py:214
  1.0 3.1 %collective-permute-start = (bf16[1,64,2048]{2,1,0:T(8,128)(2,1)S(1)}, bf16[1,64,2048]{2,1,0:T(8,128)(2,1)S(1)}, u32[]{:S(2)}, u32[]{:S(2)}) collective-permute-start(bf16[1,64,2048]{2,1,0:T(8,128)(2,1)S(1)} %dynamic-slice_bitcast_fusion), channel_id=1, source_target_pairs={{0,4},{4,0},{8,12},{12,8},{1,5},{5,1},{9,13},{13,9},{2,6},{6,2},{1... | collective-permute-start | bytes 786440 | tf_op jit(solution)/shard_map/ppermute | solution.py:38
  4.1 0.8 %constant_dynamic-slice_fusion = bf16[1,64,256]{2,1,0:T(8,128)(2,1)S(1)} fusion(bf16[2,64,256]{2,1,0:T(8,128)(2,1)} %refs_0_.1, s32[]{:T(128)S(6)} %select_n.4), kind=kLoop, calls=%fused_computation.2 | loop fusion | bytes 65540 | tf_op jit(solution)/shard_map/dynamic_slice | solution.py:216
  4.8 2.7 %collective-permute-start.1 = (bf16[1,64,2304]{2,1,0:T(8,128)(2,1)S(1)}, bf16[1,64,2304]{2,1,0:T(8,128)(2,1)S(1)}, u32[]{:S(2)}, u32[]{:S(2)}) collective-permute-start(bf16[1,64,2304]{2,1,0:T(8,128)(2,1)S(1)} %pad_maximum_fusion), channel_id=1, source_target_pairs={{0,8},{4,12},{8,0},{12,4},{1,9},{5,13},{9,1},{13,5},{2,10},{6,14},... | collective-permute-start | bytes 884744 | tf_op jit(solution)/shard_map/ppermute | solution.py:38
  7.5 1.9 %copy-done = bf16[768,2048]{1,0:T(8,128)(2,1)S(1)} copy-done((bf16[768,2048]{1,0:T(8,128)(2,1)S(1)}, bf16[768,2048]{1,0:T(8,128)(2,1)}, u32[]{:S(2)}) %copy-start) | copy-done | bytes 3145752
  9.4 2.2 %copy-done.2 = bf16[2048,1024]{1,0:T(8,128)(2,1)S(1)} copy-done((bf16[2048,1024]{1,0:T(8,128)(2,1)S(1)}, bf16[2048,1024]{1,0:T(8,128)(2,1)}, u32[]{:S(2)}) %copy-start.2) | copy-done | bytes 4194328
  11.6 0.7 %copy-done.8 = f32[256]{0:T(256)S(1)} copy-done((f32[256]{0:T(256)S(1)}, f32[256]{0:T(256)}, u32[]{:S(2)}) %copy-start.8) | copy-done | bytes 1048
  12.3 2.7 %partials.2 = (f32[1,256]{1,0:T(1,128)S(1)}, bf16[768,256]{1,0:T(8,128)(2,1)S(1)}, bf16[768,256]{1,0:T(8,128)(2,1)S(1)}, bf16[768,256]{1,0:T(8,128)(2,1)S(1)}) custom-call(bf16[768,2048]{1,0:T(8,128)(2,1)S(1)} %copy-done, bf16[2048,1024]{1,0:T(8,128)(2,1)S(1)} %copy-done.2, f32[1,256]{1,0:T(1,128)S(1)} %bitcast.13), custom_call_target="tpu_custom_call" | custom-call | flops 4000000000 | bytes 1 | tf_op jit(solution)/shard_map/partials/pallas_call | solution.py:70
  15.0 1.7 %collective-permute-start.5 = (bf16[1,64,2048]{2,1,0:T(8,128)(2,1)S(1)}, bf16[1,64,2048]{2,1,0:T(8,128)(2,1)S(1)}, u32[]{:S(2)}, u32[]{:S(2)}) collective-permute-start(bf16[1,64,2048]{2,1,0:T(8,128)(2,1)S(1)} %collective-permute-done.refs_0_), channel_id=1, source_target_pairs={{0,16},{16,0},{1,17},{17,1},{2,18},{18,2},{3,19},{19,3},{4,20},{20... | collective-permute-start | bytes 786440 | tf_op jit(solution)/shard_map/ppermute | solution.py:38
  16.7 0.5 %collective-permute-start.7 = (bf16[768,256]{1,0:T(8,128)(2,1)S(1)}, bf16[768,256]{1,0:T(8,128)(2,1)S(1)}, u32[]{:S(2)}, u32[]{:S(2)}) collective-permute-start(bf16[768,256]{1,0:T(8,128)(2,1)S(1)} %get-tuple-element.33), channel_id=1, source_target_pairs={{0,1},{1,0},{2,3},{3,2},{4,5},{5,4},{6,7},{7,6},{8,9},{9,8},{10,11... | collective-permute-start | bytes 1179656 | tf_op jit(solution)/shard_map/ppermute | solution.py:38
  17.2 1.0 %partials.3 = (f32[1,256]{1,0:T(1,128)S(1)}, bf16[768,256]{1,0:T(8,128)(2,1)S(1)}) custom-call(bf16[768,2048]{1,0:T(8,128)(2,1)S(1)} %copy-done, bf16[2048,1024]{1,0:T(8,128)(2,1)S(1)} %copy-done.2, f32[1,256]{1,0:T(1,128)S(1)} %get-tuple-element.27.before_ref), custom_call_target="tpu_custom_call" | custom-call | flops 1 | bytes 1 | tf_op jit(solution)/shard_map/partials/pallas_call | solution.py:70
  18.2 2.4 %collective-permute-done.1.refs_1_.refs_2_ = bf16[1,64,2304]{2,1,0:T(8,128)(2,1)S(1)} collective-permute-done((bf16[1,64,2304]{2,1,0:T(8,128)(2,1)S(1)}, bf16[1,64,2304]{2,1,0:T(8,128)(2,1)S(1)}, u32[]{:S(2)}, u32[]{:S(2)}) %collective-permute-start.1) | collective-permute-done | bytes 294944 | tf_op jit(solution)/shard_map/ppermute | solution.py:38
  20.6 1.5 %collective-permute-start.4 = (bf16[1,64,2304]{2,1,0:T(8,128)(2,1)S(1)}, bf16[1,64,2304]{2,1,0:T(8,128)(2,1)S(1)}, u32[]{:S(2)}, u32[]{:S(2)}) collective-permute-start(bf16[1,64,2304]{2,1,0:T(8,128)(2,1)S(1)} %collective-permute-done.1.refs_1_.refs_2_), channel_id=1, source_target_pairs={{0,16},{16,0},{1,17},{17,1},{2,18},{18,2},{3,19},{19,3},{4,20},{20... | collective-permute-start | bytes 884744 | tf_op jit(solution)/shard_map/ppermute | solution.py:38
  22.2 0.9 %collective-permute-done.5.refs_2_ = bf16[1,64,2048]{2,1,0:T(8,128)(2,1)S(1)} collective-permute-done((bf16[1,64,2048]{2,1,0:T(8,128)(2,1)S(1)}, bf16[1,64,2048]{2,1,0:T(8,128)(2,1)S(1)}, u32[]{:S(2)}, u32[]{:S(2)}) %collective-permute-start.5) | collective-permute-done | bytes 262176 | tf_op jit(solution)/shard_map/ppermute | solution.py:38
  23.1 1.2 %low_rows.3.refs_2_ = f32[64,768]{1,0:T(8,128)S(1)} custom-call(s32[1,768]{1,0:T(1,128)S(1)} %bitcast.7, bf16[768,2048]{1,0:T(8,128)(2,1)S(1)} %copy-done.1, bf16[1,64,2048]{2,1,0:T(8,128)(2,1)S(1)} %collective-permute-done.refs_0_, bf16[1,64,2304]{2,1,0:T(8,128)(2,1)S(1)} %collective-permute-done.1.refs_1_.refs_2_, ...), custom_call_target="tpu_custom_call" | custom-call | flops 2000000000 | bytes 1 | tf_op jit(solution)/shard_map/low_rows/pallas_call | solution.py:145
  24.3 0.1 add.8
  24.5 1.5 %collective-permute-start.11 = (bf16[768,256]{1,0:T(8,128)(2,1)S(1)}, bf16[768,256]{1,0:T(8,128)(2,1)S(1)}, u32[]{:S(2)}, u32[]{:S(2)}) collective-permute-start(bf16[768,256]{1,0:T(8,128)(2,1)S(1)} %add.8), channel_id=1, source_target_pairs={{0,2},{1,3},{2,0},{3,1},{4,6},{5,7},{6,4},{7,5},{8,10},{9,11},{10,... | collective-permute-start | bytes 1179656 | tf_op jit(solution)/shard_map/ppermute | solution.py:38
  26.0 2.9 %collective-permute-done.4.refs_0_.refs_4_ = bf16[1,64,2304]{2,1,0:T(8,128)(2,1)S(1)} collective-permute-done((bf16[1,64,2304]{2,1,0:T(8,128)(2,1)S(1)}, bf16[1,64,2304]{2,1,0:T(8,128)(2,1)S(1)}, u32[]{:S(2)}, u32[]{:S(2)}) %collective-permute-start.4) | collective-permute-done | bytes 294944 | tf_op jit(solution)/shard_map/ppermute | solution.py:38
  28.8 0.4 collective-permute-start.8
  29.3 0.2 collective-permute-done.2.refs_1_.refs_3_
  29.5 1.3 %collective-permute-start.3 = (bf16[1,64,2304]{2,1,0:T(8,128)(2,1)S(1)}, bf16[1,64,2304]{2,1,0:T(8,128)(2,1)S(1)}, u32[]{:S(2)}, u32[]{:S(2)}) collective-permute-start(bf16[1,64,2304]{2,1,0:T(8,128)(2,1)S(1)} %collective-permute-done.2.refs_1_.refs_3_), channel_id=1, source_target_pairs={{0,16},{16,0},{1,17},{17,1},{2,18},{18,2},{3,19},{19,3},{4,20},{20... | collective-permute-start | bytes 884744 | tf_op jit(solution)/shard_map/ppermute | solution.py:38
  30.8 1.2 %low_rows.4.refs_1_ = f32[64,768]{1,0:T(8,128)S(1)} custom-call(s32[1,768]{1,0:T(1,128)S(1)} %bitcast.8, bf16[768,2048]{1,0:T(8,128)(2,1)S(1)} %copy-done.1, bf16[1,64,2304]{2,1,0:T(8,128)(2,1)S(1)} %collective-permute-done.4.refs_0_.refs_4_, bf16[1,64,2304]{2,1,0:T(8,128)(2,1)S(1)} %collective-permute-done.2.refs_1_.refs_3_, f32[64,768]{1,0:T(8,128)S(1)} %low_rows.3.refs_2_), custom_call_target="tpu_custom_call" | custom-call | flops 5000000000 | bytes 1 | tf_op jit(solution)/shard_map/low_rows/pallas_call | solution.py:145
  32.0 1.1 %collective-permute-done.8.refs_1_ = bf16[2,64,256]{2,1,0:T(8,128)(2,1)S(1)} collective-permute-done((bf16[2,64,256]{2,1,0:T(8,128)(2,1)S(1)}, bf16[2,64,256]{2,1,0:T(8,128)(2,1)S(1)}, u32[]{:S(2)}, u32[]{:S(2)}) %collective-permute-start.8) | collective-permute-done | bytes 65568 | tf_op jit(solution)/shard_map/ppermute | solution.py:38
  33.1 3.6 %collective-permute-done.3.refs_0_.refs_5_ = bf16[1,64,2304]{2,1,0:T(8,128)(2,1)S(1)} collective-permute-done((bf16[1,64,2304]{2,1,0:T(8,128)(2,1)S(1)}, bf16[1,64,2304]{2,1,0:T(8,128)(2,1)S(1)}, u32[]{:S(2)}, u32[]{:S(2)}) %collective-permute-start.3) | collective-permute-done | bytes 294944 | tf_op jit(solution)/shard_map/ppermute | solution.py:38
  36.7 1.1 %low_rows.5.refs_0_ = bf16[64,768]{1,0:T(8,128)(2,1)S(1)} custom-call(s32[1,768]{1,0:T(1,128)S(1)} %bitcast.9, bf16[768,2048]{1,0:T(8,128)(2,1)S(1)} %copy-done.1, bf16[1,64,2304]{2,1,0:T(8,128)(2,1)S(1)} %collective-permute-done.3.refs_0_.refs_5_, f32[64,768]{1,0:T(8,128)S(1)} %low_rows.4.refs_1_), custom_call_target="tpu_custom_call" | custom-call | flops 1 | bytes 1 | tf_op jit(solution)/shard_map/low_rows/pallas_call | solution.py:145
  37.8 0.1 collective-permute-start.9
  37.9 1.3 %collective-permute-done.9.refs_1_ = bf16[64,768]{1,0:T(8,128)(2,1)S(1)} collective-permute-done((bf16[64,768]{1,0:T(8,128)(2,1)S(1)}, bf16[64,768]{1,0:T(8,128)(2,1)S(1)}, u32[]{:S(2)}, u32[]{:S(2)}) %collective-permute-start.9) | collective-permute-done | bytes 98336 | tf_op jit(solution)/shard_map/ppermute | solution.py:38
  39.2 1.6 %collective-permute-start.10 = (bf16[64,768]{1,0:T(8,128)(2,1)S(1)}, bf16[64,768]{1,0:T(8,128)(2,1)S(1)}, u32[]{:S(2)}, u32[]{:S(2)}) collective-permute-start(bf16[64,768]{1,0:T(8,128)(2,1)S(1)} %add.7.mine_ref), channel_id=1, source_target_pairs={{0,2},{1,3},{2,0},{3,1},{4,6},{5,7},{6,4},{7,5},{8,10},{9,11},{10,... | collective-permute-start | bytes 294920 | tf_op jit(solution)/shard_map/ppermute | solution.py:38
  40.8 0.7 %rotated_ups.1 = (bf16[512,256]{1,0:T(8,128)(2,1)S(1)}, bf16[768,512]{1,0:T(8,128)(2,1)S(1)}) custom-call(s32[1,768]{1,0:T(1,128)S(1)} %bitcast.10, s32[1,128]{1,0:T(1,128)S(1)} %bitcast.11, bf16[128,128]{1,0:T(8,128)(2,1)S(1)} %copy-done.4, bf16[2,64,256]{2,1,0:T(8,128)(2,1)S(1)} %copy-done.3, bf16[2,64,256]{2,1,0:T(8,128)(2,1)S(1)} %collective-permute-done.8.refs_1_, ...), custom_call_target="tpu_custom_call" | custom-call | flops 1 | bytes 1 | tf_op jit(solution)/shard_map/rotated_ups/pallas_call | solution.py:171
  41.4 0.5 %rotated_base.1.base_ref = f32[768,256]{1,0:T(8,128)S(1)} custom-call(f32[1,256]{1,0:T(1,128)S(1)} %get-tuple-element.37.scale_ref, s32[1,128]{1,0:T(1,128)S(1)} %bitcast.12, bf16[128,128]{1,0:T(8,128)(2,1)S(1)} %copy-done.4, bf16[768,256]{1,0:T(8,128)(2,1)S(1)} %get-tuple-element.38.refs_0_, bf16[768,256]{1,0:T(8,128)(2,1)S(1)} %collective-permute-done.6.refs_1_, ...), custom_call_target="tpu_custom_call" | custom-call | flops 1 | bytes 1 | tf_op jit(solution)/shard_map/rotated_base/pallas_call | solution.py:109
  41.9 2.2 %collective-permute-done.10.theirs_ref = bf16[64,768]{1,0:T(8,128)(2,1)S(1)} collective-permute-done((bf16[64,768]{1,0:T(8,128)(2,1)S(1)}, bf16[64,768]{1,0:T(8,128)(2,1)S(1)}, u32[]{:S(2)}, u32[]{:S(2)}) %collective-permute-start.10) | collective-permute-done | bytes 98336 | tf_op jit(solution)/shard_map/ppermute | solution.py:38
  44.1 1.4 %final.1 = bf16[768,256]{1,0:T(8,128)(2,1)} custom-call(bf16[64,768]{1,0:T(8,128)(2,1)S(1)} %add.7.mine_ref, bf16[64,768]{1,0:T(8,128)(2,1)S(1)} %collective-permute-done.10.theirs_ref, f32[768,256]{1,0:T(8,128)S(1)} %rotated_base.1.base_ref, bf16[512,256]{1,0:T(8,128)(2,1)S(1)} %get-tuple-element.43.up_ref, bf16[768,512]{1,0:T(8,128)(2,1)S(1)} %get-tuple-element.44.mask_ref), custom_call_target="tpu_custom_call" | custom-call | flops 1 | bytes 1 | tf_op jit(solution)/shard_map/final/pallas_call | solution.py:192
  (23 shorter events, 0.2 us)
Async XLA Ops:
  1.0 14.1 %collective-permute-start = (bf16[1,64,2048]{2,1,0:T(8,128)(2,1)S(1)}, bf16[1,64,2048]{2,1,0:T(8,128)(2,1)S(1)}, u32[]{:S(2)}, u32[]{:S(2)}) collective-permute-start(bf16[1,64,2048]{2,1,0:T(8,128)(2,1)S(1)} %dynamic-slice_bitcast_fusion), channel_id=1, source_target_pairs={{0,4},{4,0},{8,12},{12,8},{1,5},{5,1},{9,13},{13,9},{2,6},{6,2},{1... | collective-permute-start | bytes 786440 | tf_op jit(solution)/shard_map/ppermute | solution.py:38
  4.8 15.8 %collective-permute-start.1 = (bf16[1,64,2304]{2,1,0:T(8,128)(2,1)S(1)}, bf16[1,64,2304]{2,1,0:T(8,128)(2,1)S(1)}, u32[]{:S(2)}, u32[]{:S(2)}) collective-permute-start(bf16[1,64,2304]{2,1,0:T(8,128)(2,1)S(1)} %pad_maximum_fusion), channel_id=1, source_target_pairs={{0,8},{4,12},{8,0},{12,4},{1,9},{5,13},{9,1},{13,5},{2,10},{6,14},... | collective-permute-start | bytes 884744 | tf_op jit(solution)/shard_map/ppermute | solution.py:38
  7.5 1.9 %copy-start = (bf16[768,2048]{1,0:T(8,128)(2,1)S(1)}, bf16[768,2048]{1,0:T(8,128)(2,1)}, u32[]{:S(2)}) copy-start(bf16[768,2048]{1,0:T(8,128)(2,1)} %tokens_ref.9) | copy-start | bytes 9437188
  9.4 2.2 %copy-start.2 = (bf16[2048,1024]{1,0:T(8,128)(2,1)S(1)}, bf16[2048,1024]{1,0:T(8,128)(2,1)}, u32[]{:S(2)}) copy-start(bf16[2048,1024]{1,0:T(8,128)(2,1)} %weight_ref.3) | copy-start | bytes 12582916
  11.6 0.7 %copy-start.8 = (f32[256]{0:T(256)S(1)}, f32[256]{0:T(256)}, u32[]{:S(2)}) copy-start(f32[256]{0:T(256)} %param.11) | copy-start | bytes 3076
  14.9 8.1 %copy-start.1 = (bf16[768,2048]{1,0:T(8,128)(2,1)S(1)}, bf16[768,2048]{1,0:T(8,128)(2,1)}, u32[]{:S(2)}) copy-start(bf16[768,2048]{1,0:T(8,128)(2,1)} %tokens_ref.9) | copy-start | bytes 9437188
  14.9 8.1 %copy-start.5 = (bf16[2,2048,64]{1,2,0:T(8,128)(2,1)S(1)}, bf16[2,2048,64]{1,2,0:T(8,128)(2,1)}, u32[]{:S(2)}) copy-start(bf16[2,2048,64]{1,2,0:T(8,128)(2,1)} %param.12) | copy-start | bytes 1572868
  14.9 8.1 %copy-start.6 = (s32[768,1]{0,1:T(1,128)S(1)}, s32[768,1]{0,1:T(1,128)}, u32[]{:S(2)}) copy-start(s32[768,1]{0,1:T(1,128)} %param.9) | copy-start | bytes 9220
  15.0 8.0 %collective-permute-start.5 = (bf16[1,64,2048]{2,1,0:T(8,128)(2,1)S(1)}, bf16[1,64,2048]{2,1,0:T(8,128)(2,1)S(1)}, u32[]{:S(2)}, u32[]{:S(2)}) collective-permute-start(bf16[1,64,2048]{2,1,0:T(8,128)(2,1)S(1)} %collective-permute-done.refs_0_), channel_id=1, source_target_pairs={{0,16},{16,0},{1,17},{17,1},{2,18},{18,2},{3,19},{19,3},{4,20},{20... | collective-permute-start | bytes 786440 | tf_op jit(solution)/shard_map/ppermute | solution.py:38
  16.7 7.6 %collective-permute-start.6 = (bf16[768,256]{1,0:T(8,128)(2,1)S(1)}, bf16[768,256]{1,0:T(8,128)(2,1)S(1)}, u32[]{:S(2)}, u32[]{:S(2)}) collective-permute-start(bf16[768,256]{1,0:T(8,128)(2,1)S(1)} %get-tuple-element.32), channel_id=1, source_target_pairs={{0,1},{1,0},{2,3},{3,2},{4,5},{5,4},{6,7},{7,6},{8,9},{9,8},{10,11... | collective-permute-start | bytes 1179656 | tf_op jit(solution)/shard_map/ppermute | solution.py:38
  16.7 7.6 %collective-permute-start.7 = (bf16[768,256]{1,0:T(8,128)(2,1)S(1)}, bf16[768,256]{1,0:T(8,128)(2,1)S(1)}, u32[]{:S(2)}, u32[]{:S(2)}) collective-permute-start(bf16[768,256]{1,0:T(8,128)(2,1)S(1)} %get-tuple-element.33), channel_id=1, source_target_pairs={{0,1},{1,0},{2,3},{3,2},{4,5},{5,4},{6,7},{7,6},{8,9},{9,8},{10,11... | collective-permute-start | bytes 1179656 | tf_op jit(solution)/shard_map/ppermute | solution.py:38
  20.6 8.2 %collective-permute-start.4 = (bf16[1,64,2304]{2,1,0:T(8,128)(2,1)S(1)}, bf16[1,64,2304]{2,1,0:T(8,128)(2,1)S(1)}, u32[]{:S(2)}, u32[]{:S(2)}) collective-permute-start(bf16[1,64,2304]{2,1,0:T(8,128)(2,1)S(1)} %collective-permute-done.1.refs_1_.refs_2_), channel_id=1, source_target_pairs={{0,16},{16,0},{1,17},{17,1},{2,18},{18,2},{3,19},{19,3},{4,20},{20... | collective-permute-start | bytes 884744 | tf_op jit(solution)/shard_map/ppermute | solution.py:38
  22.2 7.3 %collective-permute-start.2 = (bf16[1,64,2304]{2,1,0:T(8,128)(2,1)S(1)}, bf16[1,64,2304]{2,1,0:T(8,128)(2,1)S(1)}, u32[]{:S(2)}, u32[]{:S(2)}) collective-permute-start(bf16[1,64,2304]{2,1,0:T(8,128)(2,1)S(1)} %collective-permute-done.1.refs_1_.refs_2_), channel_id=1, source_target_pairs={{0,4},{4,0},{8,12},{12,8},{1,5},{5,1},{9,13},{13,9},{2,6},{6,2},{1... | collective-permute-start | bytes 884744 | tf_op jit(solution)/shard_map/ppermute | solution.py:38
  23.1 5.8 %copy-start.3 = (bf16[2,64,256]{2,1,0:T(8,128)(2,1)S(1)}, bf16[2,64,256]{2,1,0:T(8,128)(2,1)}, u32[]{:S(2)}) copy-start(bf16[2,64,256]{2,1,0:T(8,128)(2,1)} %refs_0_.1) | copy-start | bytes 196612
  24.4 16.3 %copy-start.4 = (bf16[128,128]{1,0:T(8,128)(2,1)S(1)}, bf16[128,128]{1,0:T(8,128)(2,1)}, u32[]{:S(2)}) copy-start(bf16[128,128]{1,0:T(8,128)(2,1)} %constant.12.clone.matrix_ref) | copy-start | bytes 98308
  24.4 16.3 %copy-start.7 = (s32[128]{0:T(128)S(1)}, s32[128]{0:T(128)}, u32[]{:S(2)}) copy-start(s32[128]{0:T(128)} %param.14) | copy-start | bytes 1540
  24.5 17.0 %collective-permute-start.11 = (bf16[768,256]{1,0:T(8,128)(2,1)S(1)}, bf16[768,256]{1,0:T(8,128)(2,1)S(1)}, u32[]{:S(2)}, u32[]{:S(2)}) collective-permute-start(bf16[768,256]{1,0:T(8,128)(2,1)S(1)} %add.8), channel_id=1, source_target_pairs={{0,2},{1,3},{2,0},{3,1},{4,6},{5,7},{6,4},{7,5},{8,10},{9,11},{10,... | collective-permute-start | bytes 1179656 | tf_op jit(solution)/shard_map/ppermute | solution.py:38
  28.8 4.3 %collective-permute-start.8 = (bf16[2,64,256]{2,1,0:T(8,128)(2,1)S(1)}, bf16[2,64,256]{2,1,0:T(8,128)(2,1)S(1)}, u32[]{:S(2)}, u32[]{:S(2)}) collective-permute-start(bf16[2,64,256]{2,1,0:T(8,128)(2,1)S(1)} %copy-done.3), channel_id=1, source_target_pairs={{0,4},{4,0},{8,12},{12,8},{1,5},{5,1},{9,13},{13,9},{2,6},{6,2},{1... | collective-permute-start | bytes 196616 | tf_op jit(solution)/shard_map/ppermute | solution.py:38
  29.5 7.2 %collective-permute-start.3 = (bf16[1,64,2304]{2,1,0:T(8,128)(2,1)S(1)}, bf16[1,64,2304]{2,1,0:T(8,128)(2,1)S(1)}, u32[]{:S(2)}, u32[]{:S(2)}) collective-permute-start(bf16[1,64,2304]{2,1,0:T(8,128)(2,1)S(1)} %collective-permute-done.2.refs_1_.refs_3_), channel_id=1, source_target_pairs={{0,16},{16,0},{1,17},{17,1},{2,18},{18,2},{3,19},{19,3},{4,20},{20... | collective-permute-start | bytes 884744 | tf_op jit(solution)/shard_map/ppermute | solution.py:38
  37.8 1.4 %collective-permute-start.9 = (bf16[64,768]{1,0:T(8,128)(2,1)S(1)}, bf16[64,768]{1,0:T(8,128)(2,1)S(1)}, u32[]{:S(2)}, u32[]{:S(2)}) collective-permute-start(bf16[64,768]{1,0:T(8,128)(2,1)S(1)} %low_rows.5.refs_0_), channel_id=1, source_target_pairs={{0,1},{1,0},{2,3},{3,2},{4,5},{5,4},{6,7},{7,6},{8,9},{9,8},{10,11... | collective-permute-start | bytes 294920 | tf_op jit(solution)/shard_map/ppermute | solution.py:38
  39.2 4.9 %collective-permute-start.10 = (bf16[64,768]{1,0:T(8,128)(2,1)S(1)}, bf16[64,768]{1,0:T(8,128)(2,1)S(1)}, u32[]{:S(2)}, u32[]{:S(2)}) collective-permute-start(bf16[64,768]{1,0:T(8,128)(2,1)S(1)} %add.7.mine_ref), channel_id=1, source_target_pairs={{0,2},{1,3},{2,0},{3,1},{4,6},{5,7},{6,4},{7,5},{8,10},{9,11},{10,... | collective-permute-start | bytes 294920 | tf_op jit(solution)/shard_map/ppermute | solution.py:38

commit v12 on v11

--- a/solution.py
+++ b/solution.py
@@ -56,26 +56,25 @@
     return turned
 
 
-def partial_kernel(offsets, parts, tokens_ref, weight_ref, before_ref, after_ref, *outs):
+def partial_kernel(offsets, parts, tokens_ref, weight_ref, *refs):
     me, width = lax.axis_index("tp"), weight_ref.shape[1] // parts
-    for offset, out_ref in zip(offsets, outs):
+    for offset, out_ref in zip(offsets, refs[-len(offsets) :]):
         at = pl.multiple_of(jnp.bitwise_xor(me, offset) * width, width)
         product = jnp.dot(tokens_ref[...], weight_ref[:, pl.ds(at, width)], preferred_element_type=F32)
         out_ref[...] = product.astype(BF16)
-    after_ref[...] = before_ref[...]
-
-
-def partials(tokens, weight, parts, offsets, before, cost):
+
+
+def partials(tokens, weight, parts, offsets, cost, *before):
     block = jax.ShapeDtypeStruct((tokens.shape[0], weight.shape[1] // parts), BF16)
     return pl.pallas_call(
         functools.partial(partial_kernel, offsets, parts),
-        in_specs=[VMEM] * 3,
-        out_specs=[VMEM] * (1 + len(offsets)),
-        out_shape=[jax.ShapeDtypeStruct(before.shape, before.dtype)] + [block] * len(offsets),
+        in_specs=[VMEM] * (2 + len(before)),
+        out_specs=[VMEM] * len(offsets),
+        out_shape=[block] * len(offsets),
         compiler_params=params(24),
         cost_estimate=cost,
         name="partials",
-    )(tokens, weight, before)
+    )(tokens, weight, *before)
 
 
 def add_kernel(*refs):
@@ -220,11 +219,11 @@
         bit //= 2
     half = parts // 2
     offsets = (*range(1, parts, 2), *range(2, parts, 2))
-    passed, *blocks = partials(tokens, base_weight, parts, offsets, scale, lasting(4))
-    near, passed = together(near, passed)
-    scale, block = partials(tokens, base_weight, parts, (0,), passed, COST)
+    blocks = list(partials(tokens, base_weight, parts, offsets, lasting(4)))
+    near, blocks[-1] = together(near, blocks[-1])
+    (block,) = partials(tokens, base_weight, parts, (0,), COST, blocks[-1])
+    close, block, *far = together(near, block, *(piece for _, piece in mine[1:]))
     blocks = blocks[:half] + [block] + blocks[half:]
-    close, scale, *far = together(near, scale, *(piece for _, piece in mine[1:]))
     mine = mine[:1] + [(plane, piece) for (plane, _), piece in zip(mine[1:], far)]
     odd = [(1, near)] + [(plane | 1, swap(piece, "adp", 1)) for plane, piece in mine[1:]]
 
@@ -248,11 +247,9 @@
     low, *came = together(low, *(swap(block, "tp", 1) for block in blocks[:half]))
 
     rest = held[len(mine) :]
-    plane, off, piece = swapped[-2]
-    piece, up = together(piece, adapter_up)
-    swapped[-2] = plane, off, piece
+    low = more(low, swapped[1:-1] + rest, F32, lasting(5))
+    low, up = together(low, adapter_up)
     ups = [adapter_up, swap(up, "adp", 1)]
-    low = more(low, swapped[1:-1] + rest, F32, lasting(5))
 
     sums = [[block, pair] for block, pair in zip(blocks[half:], came)]
     bit = 2

time: 45.9 us -> 44.4 us (0.967)
  waiting for transfers between devices: 14.7 us -> 13.3 us
  local copies, waits for them, and re-layouts: 6.52 us -> 5.85 us
  starting transfers between devices: 14.4 us -> 14.9 us
    ppermute x12, waiting for transfers between devices: 14.7 us -> 13.3 us  [swap(): lax.ppermute(x, axis, [(i, i ^ bit) for i in range(lax.axis_size(axis))])]
    unnamed x18, local copies, waits for them, and re-layouts: 4.79 us -> 4.12 us
    ppermute x12, starting transfers between devices: 14.4 us -> 14.9 us  [swap(): lax.ppermute(x, axis, [(i, i ^ bit) for i in range(lax.axis_size(axis))])]
  transfers between devices with their start and end apart: 12 -> 12, of which waited for: 9 -> 7; matrix products, arithmetic and copies ran while one was open for 2% -> 2% of each run, Pallas kernels for 18% -> 19%
where the time goes in v12:
time: 44.4 us; the launch traced here: 44.1 us
  starting transfers between devices  14.9 us (34%)
  waiting for transfers between devices  13.3 us (30%)
  Pallas kernels  9.84 us (22%)
  local copies, waits for them, and re-layouts  5.85 us (13%)
    ppermute x12, starting transfers between devices, swap(): lax.ppermute(x, axis, [(i, i ^ bit) for i in range(lax.axis_size(axis))])  14.9 us
    ppermute x12, waiting for transfers between devices, swap(): lax.ppermute(x, axis, [(i, i ^ bit) for i in range(lax.axis_size(axis))])  13.3 us
    unnamed x18, local copies, waits for them, and re-layouts  4.12 us
    pallas_call x2, Pallas kernels, partials(): pl.pallas_call(functools.partial(partial_kernel, offsets, parts), in_spec...  3.66 us
    pallas_call x3, Pallas kernels, low_rows(): pl.pallas_call(functools.partial(low_kernel, groups, here, share, rank, b...  3.46 us
    pallas_call x1, Pallas kernels, final(): pl.pallas_call(final_kernel, in_specs=[VMEM] * 5, out_specs=VMEM, out_sha...  1.45 us
    dynamic_slice x1, local copies, waits for them, and re-layouts, local(): own = lax.dynamic_slice_in_dim(down, start, share, 0)  0.97 us
  transfers between devices with their start and end apart: 12, of which 7 were waited for; matrix products, arithmetic and copies ran while one was open for 2% of the time, Pallas kernels for 19%

profile of v12, /device:TPU:0, one launch (start us, length us, event | category | flops | bytes accessed | tf_op | source)
XLA Modules:
  0.0 44.1 jit_solution(18307765346372255906)
XLA Ops:
  0.0 1.0 %dynamic-slice_bitcast_fusion = bf16[1,64,2048]{2,1,0:T(8,128)(2,1)S(1)} fusion(bf16[2,2048,64]{1,2,0:T(8,128)(2,1)} %param.12, s32[]{:T(128)S(6)} %select_n.4), kind=kLoop, calls=%fused_computation.1 | loop fusion | bytes 524292 | tf_op jit(solution)/shard_map/dynamic_slice | solution.py:213
  1.0 3.1 %collective-permute-start = (bf16[1,64,2048]{2,1,0:T(8,128)(2,1)S(1)}, bf16[1,64,2048]{2,1,0:T(8,128)(2,1)S(1)}, u32[]{:S(2)}, u32[]{:S(2)}) collective-permute-start(bf16[1,64,2048]{2,1,0:T(8,128)(2,1)S(1)} %dynamic-slice_bitcast_fusion), channel_id=1, source_target_pairs={{0,4},{4,0},{8,12},{12,8},{1,5},{5,1},{9,13},{13,9},{2,6},{6,2},{1... | collective-permute-start | bytes 786440 | tf_op jit(solution)/shard_map/ppermute | solution.py:38
  4.1 0.8 %constant_dynamic-slice_fusion = bf16[1,64,256]{2,1,0:T(8,128)(2,1)S(1)} fusion(bf16[2,64,256]{2,1,0:T(8,128)(2,1)} %refs_0_.1, s32[]{:T(128)S(6)} %select_n.4), kind=kLoop, calls=%fused_computation.2 | loop fusion | bytes 65540 | tf_op jit(solution)/shard_map/dynamic_slice | solution.py:215
  4.8 2.7 %collective-permute-start.1 = (bf16[1,64,2304]{2,1,0:T(8,128)(2,1)S(1)}, bf16[1,64,2304]{2,1,0:T(8,128)(2,1)S(1)}, u32[]{:S(2)}, u32[]{:S(2)}) collective-permute-start(bf16[1,64,2304]{2,1,0:T(8,128)(2,1)S(1)} %pad_maximum_fusion), channel_id=1, source_target_pairs={{0,8},{4,12},{8,0},{12,4},{1,9},{5,13},{9,1},{13,5},{2,10},{6,14},... | collective-permute-start | bytes 884744 | tf_op jit(solution)/shard_map/ppermute | solution.py:38
  7.5 1.9 %copy-done = bf16[768,2048]{1,0:T(8,128)(2,1)S(1)} copy-done((bf16[768,2048]{1,0:T(8,128)(2,1)S(1)}, bf16[768,2048]{1,0:T(8,128)(2,1)}, u32[]{:S(2)}) %copy-start) | copy-done | bytes 3145752
  9.4 2.2 %copy-done.2 = bf16[2048,1024]{1,0:T(8,128)(2,1)S(1)} copy-done((bf16[2048,1024]{1,0:T(8,128)(2,1)S(1)}, bf16[2048,1024]{1,0:T(8,128)(2,1)}, u32[]{:S(2)}) %copy-start.2) | copy-done | bytes 4194328
  11.6 2.7 %partials.2 = (bf16[768,256]{1,0:T(8,128)(2,1)S(1)}, bf16[768,256]{1,0:T(8,128)(2,1)S(1)}, bf16[768,256]{1,0:T(8,128)(2,1)S(1)}) custom-call(bf16[768,2048]{1,0:T(8,128)(2,1)S(1)} %copy-done, bf16[2048,1024]{1,0:T(8,128)(2,1)S(1)} %copy-done.2), custom_call_target="tpu_custom_call" | custom-call | flops 4000000000 | bytes 1 | tf_op jit(solution)/shard_map/partials/pallas_call | solution.py:69
  14.3 0.0 copy-start.5
  14.3 0.7 %collective-permute-done.refs_0_ = bf16[1,64,2048]{2,1,0:T(8,128)(2,1)S(1)} collective-permute-done((bf16[1,64,2048]{2,1,0:T(8,128)(2,1)S(1)}, bf16[1,64,2048]{2,1,0:T(8,128)(2,1)S(1)}, u32[]{:S(2)}, u32[]{:S(2)}) %collective-permute-start) | collective-permute-done | bytes 262176 | tf_op jit(solution)/shard_map/ppermute | solution.py:38
  15.0 1.7 %collective-permute-start.5 = (bf16[1,64,2048]{2,1,0:T(8,128)(2,1)S(1)}, bf16[1,64,2048]{2,1,0:T(8,128)(2,1)S(1)}, u32[]{:S(2)}, u32[]{:S(2)}) collective-permute-start(bf16[1,64,2048]{2,1,0:T(8,128)(2,1)S(1)} %collective-permute-done.refs_0_), channel_id=1, source_target_pairs={{0,16},{16,0},{1,17},{17,1},{2,18},{18,2},{3,19},{19,3},{4,20},{20... | collective-permute-start | bytes 786440 | tf_op jit(solution)/shard_map/ppermute | solution.py:38
  16.7 0.5 %collective-permute-start.7 = (bf16[768,256]{1,0:T(8,128)(2,1)S(1)}, bf16[768,256]{1,0:T(8,128)(2,1)S(1)}, u32[]{:S(2)}, u32[]{:S(2)}) collective-permute-start(bf16[768,256]{1,0:T(8,128)(2,1)S(1)} %get-tuple-element.28), channel_id=1, source_target_pairs={{0,1},{1,0},{2,3},{3,2},{4,5},{5,4},{6,7},{7,6},{8,9},{9,8},{10,11... | collective-permute-start | bytes 1179656 | tf_op jit(solution)/shard_map/ppermute | solution.py:38
  17.2 1.0 %partials.3.refs_0_ = bf16[768,256]{1,0:T(8,128)(2,1)S(1)} custom-call(bf16[768,2048]{1,0:T(8,128)(2,1)S(1)} %copy-done, bf16[2048,1024]{1,0:T(8,128)(2,1)S(1)} %copy-done.2, bf16[768,256]{1,0:T(8,128)(2,1)S(1)} %get-tuple-element.24.refs_0_), custom_call_target="tpu_custom_call" | custom-call | flops 1 | bytes 1 | tf_op jit(solution)/shard_map/partials/pallas_call | solution.py:69
  18.2 2.4 %collective-permute-done.1.refs_1_.refs_2_ = bf16[1,64,2304]{2,1,0:T(8,128)(2,1)S(1)} collective-permute-done((bf16[1,64,2304]{2,1,0:T(8,128)(2,1)S(1)}, bf16[1,64,2304]{2,1,0:T(8,128)(2,1)S(1)}, u32[]{:S(2)}, u32[]{:S(2)}) %collective-permute-start.1) | collective-permute-done | bytes 294944 | tf_op jit(solution)/shard_map/ppermute | solution.py:38
  20.6 1.5 %collective-permute-start.4 = (bf16[1,64,2304]{2,1,0:T(8,128)(2,1)S(1)}, bf16[1,64,2304]{2,1,0:T(8,128)(2,1)S(1)}, u32[]{:S(2)}, u32[]{:S(2)}) collective-permute-start(bf16[1,64,2304]{2,1,0:T(8,128)(2,1)S(1)} %collective-permute-done.1.refs_1_.refs_2_), channel_id=1, source_target_pairs={{0,16},{16,0},{1,17},{17,1},{2,18},{18,2},{3,19},{19,3},{4,20},{20... | collective-permute-start | bytes 884744 | tf_op jit(solution)/shard_map/ppermute | solution.py:38
  22.2 0.9 %collective-permute-done.5.refs_2_ = bf16[1,64,2048]{2,1,0:T(8,128)(2,1)S(1)} collective-permute-done((bf16[1,64,2048]{2,1,0:T(8,128)(2,1)S(1)}, bf16[1,64,2048]{2,1,0:T(8,128)(2,1)S(1)}, u32[]{:S(2)}, u32[]{:S(2)}) %collective-permute-start.5) | collective-permute-done | bytes 262176 | tf_op jit(solution)/shard_map/ppermute | solution.py:38
  23.0 1.2 %low_rows.3.refs_2_ = f32[64,768]{1,0:T(8,128)S(1)} custom-call(s32[1,768]{1,0:T(1,128)S(1)} %bitcast.7, bf16[768,2048]{1,0:T(8,128)(2,1)S(1)} %copy-done.1, bf16[1,64,2048]{2,1,0:T(8,128)(2,1)S(1)} %collective-permute-done.refs_0_, bf16[1,64,2304]{2,1,0:T(8,128)(2,1)S(1)} %collective-permute-done.1.refs_1_.refs_2_, ...), custom_call_target="tpu_custom_call" | custom-call | flops 2000000000 | bytes 1 | tf_op jit(solution)/shard_map/low_rows/pallas_call | solution.py:144
  24.3 0.1 add.8
  24.4 0.0 copy-start.4
  24.4 1.3 %collective-permute-start.11 = (bf16[768,256]{1,0:T(8,128)(2,1)S(1)}, bf16[768,256]{1,0:T(8,128)(2,1)S(1)}, u32[]{:S(2)}, u32[]{:S(2)}) collective-permute-start(bf16[768,256]{1,0:T(8,128)(2,1)S(1)} %add.8), channel_id=1, source_target_pairs={{0,2},{1,3},{2,0},{3,1},{4,6},{5,7},{6,4},{7,5},{8,10},{9,11},{10,... | collective-permute-start | bytes 1179656 | tf_op jit(solution)/shard_map/ppermute | solution.py:38
  25.7 2.5 %collective-permute-done.2.refs_1_.refs_3_ = bf16[1,64,2304]{2,1,0:T(8,128)(2,1)S(1)} collective-permute-done((bf16[1,64,2304]{2,1,0:T(8,128)(2,1)S(1)}, bf16[1,64,2304]{2,1,0:T(8,128)(2,1)S(1)}, u32[]{:S(2)}, u32[]{:S(2)}) %collective-permute-start.2) | collective-permute-done | bytes 294944 | tf_op jit(solution)/shard_map/ppermute | solution.py:38
  28.2 1.5 %collective-permute-start.3 = (bf16[1,64,2304]{2,1,0:T(8,128)(2,1)S(1)}, bf16[1,64,2304]{2,1,0:T(8,128)(2,1)S(1)}, u32[]{:S(2)}, u32[]{:S(2)}) collective-permute-start(bf16[1,64,2304]{2,1,0:T(8,128)(2,1)S(1)} %collective-permute-done.2.refs_1_.refs_3_), channel_id=1, source_target_pairs={{0,16},{16,0},{1,17},{17,1},{2,18},{18,2},{3,19},{19,3},{4,20},{20... | collective-permute-start | bytes 884744 | tf_op jit(solution)/shard_map/ppermute | solution.py:38
  29.8 1.2 %low_rows.4.refs_1_ = f32[64,768]{1,0:T(8,128)S(1)} custom-call(s32[1,768]{1,0:T(1,128)S(1)} %bitcast.8, bf16[768,2048]{1,0:T(8,128)(2,1)S(1)} %copy-done.1, bf16[1,64,2304]{2,1,0:T(8,128)(2,1)S(1)} %collective-permute-done.4.refs_0_.refs_4_, bf16[1,64,2304]{2,1,0:T(8,128)(2,1)S(1)} %collective-permute-done.2.refs_1_.refs_3_, f32[64,768]{1,0:T(8,128)S(1)} %low_rows.3.refs_2_), custom_call_target="tpu_custom_call" | custom-call | flops 5000000000 | bytes 1 | tf_op jit(solution)/shard_map/low_rows/pallas_call | solution.py:144
  30.9 1.0 %collective-permute-start.8 = (bf16[2,64,256]{2,1,0:T(8,128)(2,1)S(1)}, bf16[2,64,256]{2,1,0:T(8,128)(2,1)S(1)}, u32[]{:S(2)}, u32[]{:S(2)}) collective-permute-start(bf16[2,64,256]{2,1,0:T(8,128)(2,1)S(1)} %copy-done.3), channel_id=1, source_target_pairs={{0,4},{4,0},{8,12},{12,8},{1,5},{5,1},{9,13},{13,9},{2,6},{6,2},{1... | collective-permute-start | bytes 196616 | tf_op jit(solution)/shard_map/ppermute | solution.py:38
  32.0 3.3 %collective-permute-done.8.refs_1_ = bf16[2,64,256]{2,1,0:T(8,128)(2,1)S(1)} collective-permute-done((bf16[2,64,256]{2,1,0:T(8,128)(2,1)S(1)}, bf16[2,64,256]{2,1,0:T(8,128)(2,1)S(1)}, u32[]{:S(2)}, u32[]{:S(2)}) %collective-permute-start.8) | collective-permute-done | bytes 65568 | tf_op jit(solution)/shard_map/ppermute | solution.py:38
  35.3 1.1 %low_rows.5.refs_0_ = bf16[64,768]{1,0:T(8,128)(2,1)S(1)} custom-call(s32[1,768]{1,0:T(1,128)S(1)} %bitcast.9, bf16[768,2048]{1,0:T(8,128)(2,1)S(1)} %copy-done.1, bf16[1,64,2304]{2,1,0:T(8,128)(2,1)S(1)} %collective-permute-done.3.refs_0_.refs_5_, f32[64,768]{1,0:T(8,128)S(1)} %low_rows.4.refs_1_), custom_call_target="tpu_custom_call" | custom-call | flops 1 | bytes 1 | tf_op jit(solution)/shard_map/low_rows/pallas_call | solution.py:144
  36.4 0.1 collective-permute-start.9
  36.4 1.3 %collective-permute-done.9.refs_1_ = bf16[64,768]{1,0:T(8,128)(2,1)S(1)} collective-permute-done((bf16[64,768]{1,0:T(8,128)(2,1)S(1)}, bf16[64,768]{1,0:T(8,128)(2,1)S(1)}, u32[]{:S(2)}, u32[]{:S(2)}) %collective-permute-start.9) | collective-permute-done | bytes 98336 | tf_op jit(solution)/shard_map/ppermute | solution.py:38
  37.8 1.6 %collective-permute-start.10 = (bf16[64,768]{1,0:T(8,128)(2,1)S(1)}, bf16[64,768]{1,0:T(8,128)(2,1)S(1)}, u32[]{:S(2)}, u32[]{:S(2)}) collective-permute-start(bf16[64,768]{1,0:T(8,128)(2,1)S(1)} %add.7.mine_ref), channel_id=1, source_target_pairs={{0,2},{1,3},{2,0},{3,1},{4,6},{5,7},{6,4},{7,5},{8,10},{9,11},{10,... | collective-permute-start | bytes 294920 | tf_op jit(solution)/shard_map/ppermute | solution.py:38
  39.3 0.7 %rotated_ups.1 = (bf16[512,256]{1,0:T(8,128)(2,1)S(1)}, bf16[768,512]{1,0:T(8,128)(2,1)S(1)}) custom-call(s32[1,768]{1,0:T(1,128)S(1)} %bitcast.10, s32[1,128]{1,0:T(1,128)S(1)} %bitcast.11, bf16[128,128]{1,0:T(8,128)(2,1)S(1)} %copy-done.4, bf16[2,64,256]{2,1,0:T(8,128)(2,1)S(1)} %copy-done.3, bf16[2,64,256]{2,1,0:T(8,128)(2,1)S(1)} %collective-permute-done.8.refs_1_, ...), custom_call_target="tpu_custom_call" | custom-call | flops 1 | bytes 1 | tf_op jit(solution)/shard_map/rotated_ups/pallas_call | solution.py:170
  40.0 0.5 %rotated_base.1.base_ref = f32[768,256]{1,0:T(8,128)S(1)} custom-call(f32[1,256]{1,0:T(1,128)S(1)} %bitcast.13, s32[1,128]{1,0:T(1,128)S(1)} %bitcast.12, bf16[128,128]{1,0:T(8,128)(2,1)S(1)} %copy-done.4, bf16[768,256]{1,0:T(8,128)(2,1)S(1)} %partials.3.refs_0_, bf16[768,256]{1,0:T(8,128)(2,1)S(1)} %collective-permute-done.6.refs_1_, ...), custom_call_target="tpu_custom_call" | custom-call | flops 1 | bytes 1 | tf_op jit(solution)/shard_map/rotated_base/pallas_call | solution.py:108
  40.5 2.2 %collective-permute-done.10.theirs_ref = bf16[64,768]{1,0:T(8,128)(2,1)S(1)} collective-permute-done((bf16[64,768]{1,0:T(8,128)(2,1)S(1)}, bf16[64,768]{1,0:T(8,128)(2,1)S(1)}, u32[]{:S(2)}, u32[]{:S(2)}) %collective-permute-start.10) | collective-permute-done | bytes 98336 | tf_op jit(solution)/shard_map/ppermute | solution.py:38
  42.7 1.4 %final.1 = bf16[768,256]{1,0:T(8,128)(2,1)} custom-call(bf16[64,768]{1,0:T(8,128)(2,1)S(1)} %add.7.mine_ref, bf16[64,768]{1,0:T(8,128)(2,1)S(1)} %collective-permute-done.10.theirs_ref, f32[768,256]{1,0:T(8,128)S(1)} %rotated_base.1.base_ref, bf16[512,256]{1,0:T(8,128)(2,1)S(1)} %get-tuple-element.37.up_ref, bf16[768,512]{1,0:T(8,128)(2,1)S(1)} %get-tuple-element.38.mask_ref), custom_call_target="tpu_custom_call" | custom-call | flops 1 | bytes 1 | tf_op jit(solution)/shard_map/final/pallas_call | solution.py:191
  (23 shorter events, 0.1 us)
Async XLA Ops:
  1.0 14.1 %collective-permute-start = (bf16[1,64,2048]{2,1,0:T(8,128)(2,1)S(1)}, bf16[1,64,2048]{2,1,0:T(8,128)(2,1)S(1)}, u32[]{:S(2)}, u32[]{:S(2)}) collective-permute-start(bf16[1,64,2048]{2,1,0:T(8,128)(2,1)S(1)} %dynamic-slice_bitcast_fusion), channel_id=1, source_target_pairs={{0,4},{4,0},{8,12},{12,8},{1,5},{5,1},{9,13},{13,9},{2,6},{6,2},{1... | collective-permute-start | bytes 786440 | tf_op jit(solution)/shard_map/ppermute | solution.py:38
  4.8 15.8 %collective-permute-start.1 = (bf16[1,64,2304]{2,1,0:T(8,128)(2,1)S(1)}, bf16[1,64,2304]{2,1,0:T(8,128)(2,1)S(1)}, u32[]{:S(2)}, u32[]{:S(2)}) collective-permute-start(bf16[1,64,2304]{2,1,0:T(8,128)(2,1)S(1)} %pad_maximum_fusion), channel_id=1, source_target_pairs={{0,8},{4,12},{8,0},{12,4},{1,9},{5,13},{9,1},{13,5},{2,10},{6,14},... | collective-permute-start | bytes 884744 | tf_op jit(solution)/shard_map/ppermute | solution.py:38
  7.5 1.9 %copy-start = (bf16[768,2048]{1,0:T(8,128)(2,1)S(1)}, bf16[768,2048]{1,0:T(8,128)(2,1)}, u32[]{:S(2)}) copy-start(bf16[768,2048]{1,0:T(8,128)(2,1)} %tokens_ref.9) | copy-start | bytes 9437188
  9.4 2.2 %copy-start.2 = (bf16[2048,1024]{1,0:T(8,128)(2,1)S(1)}, bf16[2048,1024]{1,0:T(8,128)(2,1)}, u32[]{:S(2)}) copy-start(bf16[2048,1024]{1,0:T(8,128)(2,1)} %weight_ref.3) | copy-start | bytes 12582916
  14.2 8.8 %copy-start.1 = (bf16[768,2048]{1,0:T(8,128)(2,1)S(1)}, bf16[768,2048]{1,0:T(8,128)(2,1)}, u32[]{:S(2)}) copy-start(bf16[768,2048]{1,0:T(8,128)(2,1)} %tokens_ref.9) | copy-start | bytes 9437188
  14.3 8.8 %copy-start.5 = (bf16[2,2048,64]{1,2,0:T(8,128)(2,1)S(1)}, bf16[2,2048,64]{1,2,0:T(8,128)(2,1)}, u32[]{:S(2)}) copy-start(bf16[2,2048,64]{1,2,0:T(8,128)(2,1)} %param.12) | copy-start | bytes 1572868
  14.3 8.8 %copy-start.6 = (s32[768,1]{0,1:T(1,128)S(1)}, s32[768,1]{0,1:T(1,128)}, u32[]{:S(2)}) copy-start(s32[768,1]{0,1:T(1,128)} %param.9) | copy-start | bytes 9220
  15.0 8.0 %collective-permute-start.5 = (bf16[1,64,2048]{2,1,0:T(8,128)(2,1)S(1)}, bf16[1,64,2048]{2,1,0:T(8,128)(2,1)S(1)}, u32[]{:S(2)}, u32[]{:S(2)}) collective-permute-start(bf16[1,64,2048]{2,1,0:T(8,128)(2,1)S(1)} %collective-permute-done.refs_0_), channel_id=1, source_target_pairs={{0,16},{16,0},{1,17},{17,1},{2,18},{18,2},{3,19},{19,3},{4,20},{20... | collective-permute-start | bytes 786440 | tf_op jit(solution)/shard_map/ppermute | solution.py:38
  16.7 7.6 %collective-permute-start.6 = (bf16[768,256]{1,0:T(8,128)(2,1)S(1)}, bf16[768,256]{1,0:T(8,128)(2,1)S(1)}, u32[]{:S(2)}, u32[]{:S(2)}) collective-permute-start(bf16[768,256]{1,0:T(8,128)(2,1)S(1)} %get-tuple-element.27), channel_id=1, source_target_pairs={{0,1},{1,0},{2,3},{3,2},{4,5},{5,4},{6,7},{7,6},{8,9},{9,8},{10,11... | collective-permute-start | bytes 1179656 | tf_op jit(solution)/shard_map/ppermute | solution.py:38
  16.7 7.6 %collective-permute-start.7 = (bf16[768,256]{1,0:T(8,128)(2,1)S(1)}, bf16[768,256]{1,0:T(8,128)(2,1)S(1)}, u32[]{:S(2)}, u32[]{:S(2)}) collective-permute-start(bf16[768,256]{1,0:T(8,128)(2,1)S(1)} %get-tuple-element.28), channel_id=1, source_target_pairs={{0,1},{1,0},{2,3},{3,2},{4,5},{5,4},{6,7},{7,6},{8,9},{9,8},{10,11... | collective-permute-start | bytes 1179656 | tf_op jit(solution)/shard_map/ppermute | solution.py:38
  20.6 7.6 %collective-permute-start.2 = (bf16[1,64,2304]{2,1,0:T(8,128)(2,1)S(1)}, bf16[1,64,2304]{2,1,0:T(8,128)(2,1)S(1)}, u32[]{:S(2)}, u32[]{:S(2)}) collective-permute-start(bf16[1,64,2304]{2,1,0:T(8,128)(2,1)S(1)} %collective-permute-done.1.refs_1_.refs_2_), channel_id=1, source_target_pairs={{0,4},{4,0},{8,12},{12,8},{1,5},{5,1},{9,13},{13,9},{2,6},{6,2},{1... | collective-permute-start | bytes 884744 | tf_op jit(solution)/shard_map/ppermute | solution.py:38
  20.6 9.1 %collective-permute-start.4 = (bf16[1,64,2304]{2,1,0:T(8,128)(2,1)S(1)}, bf16[1,64,2304]{2,1,0:T(8,128)(2,1)S(1)}, u32[]{:S(2)}, u32[]{:S(2)}) collective-permute-start(bf16[1,64,2304]{2,1,0:T(8,128)(2,1)S(1)} %collective-permute-done.1.refs_1_.refs_2_), channel_id=1, source_target_pairs={{0,16},{16,0},{1,17},{17,1},{2,18},{18,2},{3,19},{19,3},{4,20},{20... | collective-permute-start | bytes 884744 | tf_op jit(solution)/shard_map/ppermute | solution.py:38
  24.4 6.5 %copy-start.3 = (bf16[2,64,256]{2,1,0:T(8,128)(2,1)S(1)}, bf16[2,64,256]{2,1,0:T(8,128)(2,1)}, u32[]{:S(2)}) copy-start(bf16[2,64,256]{2,1,0:T(8,128)(2,1)} %refs_0_.1) | copy-start | bytes 196612
  24.4 14.9 %copy-start.4 = (bf16[128,128]{1,0:T(8,128)(2,1)S(1)}, bf16[128,128]{1,0:T(8,128)(2,1)}, u32[]{:S(2)}) copy-start(bf16[128,128]{1,0:T(8,128)(2,1)} %constant.12.clone.matrix_ref) | copy-start | bytes 98308
  24.4 14.9 %copy-start.7 = (s32[128]{0:T(128)S(1)}, s32[128]{0:T(128)}, u32[]{:S(2)}) copy-start(s32[128]{0:T(128)} %param.14) | copy-start | bytes 1540
  24.4 15.5 %collective-permute-start.11 = (bf16[768,256]{1,0:T(8,128)(2,1)S(1)}, bf16[768,256]{1,0:T(8,128)(2,1)S(1)}, u32[]{:S(2)}, u32[]{:S(2)}) collective-permute-start(bf16[768,256]{1,0:T(8,128)(2,1)S(1)} %add.8), channel_id=1, source_target_pairs={{0,2},{1,3},{2,0},{3,1},{4,6},{5,7},{6,4},{7,5},{8,10},{9,11},{10,... | collective-permute-start | bytes 1179656 | tf_op jit(solution)/shard_map/ppermute | solution.py:38
  28.2 7.0 %collective-permute-start.3 = (bf16[1,64,2304]{2,1,0:T(8,128)(2,1)S(1)}, bf16[1,64,2304]{2,1,0:T(8,128)(2,1)S(1)}, u32[]{:S(2)}, u32[]{:S(2)}) collective-permute-start(bf16[1,64,2304]{2,1,0:T(8,128)(2,1)S(1)} %collective-permute-done.2.refs_1_.refs_3_), channel_id=1, source_target_pairs={{0,16},{16,0},{1,17},{17,1},{2,18},{18,2},{3,19},{19,3},{4,20},{20... | collective-permute-start | bytes 884744 | tf_op jit(solution)/shard_map/ppermute | solution.py:38
  30.9 9.1 %copy-start.8 = (f32[256]{0:T(256)S(1)}, f32[256]{0:T(256)}, u32[]{:S(2)}) copy-start(f32[256]{0:T(256)} %param.11) | copy-start | bytes 3076
  30.9 4.3 %collective-permute-start.8 = (bf16[2,64,256]{2,1,0:T(8,128)(2,1)S(1)}, bf16[2,64,256]{2,1,0:T(8,128)(2,1)S(1)}, u32[]{:S(2)}, u32[]{:S(2)}) collective-permute-start(bf16[2,64,256]{2,1,0:T(8,128)(2,1)S(1)} %copy-done.3), channel_id=1, source_target_pairs={{0,4},{4,0},{8,12},{12,8},{1,5},{5,1},{9,13},{13,9},{2,6},{6,2},{1... | collective-permute-start | bytes 196616 | tf_op jit(solution)/shard_map/ppermute | solution.py:38
  36.4 1.4 %collective-permute-start.9 = (bf16[64,768]{1,0:T(8,128)(2,1)S(1)}, bf16[64,768]{1,0:T(8,128)(2,1)S(1)}, u32[]{:S(2)}, u32[]{:S(2)}) collective-permute-start(bf16[64,768]{1,0:T(8,128)(2,1)S(1)} %low_rows.5.refs_0_), channel_id=1, source_target_pairs={{0,1},{1,0},{2,3},{3,2},{4,5},{5,4},{6,7},{7,6},{8,9},{9,8},{10,11... | collective-permute-start | bytes 294920 | tf_op jit(solution)/shard_map/ppermute | solution.py:38
  37.8 4.9 %collective-permute-start.10 = (bf16[64,768]{1,0:T(8,128)(2,1)S(1)}, bf16[64,768]{1,0:T(8,128)(2,1)S(1)}, u32[]{:S(2)}, u32[]{:S(2)}) collective-permute-start(bf16[64,768]{1,0:T(8,128)(2,1)S(1)} %add.7.mine_ref), channel_id=1, source_target_pairs={{0,2},{1,3},{2,0},{3,1},{4,6},{5,7},{6,4},{7,5},{8,10},{9,11},{10,... | collective-permute-start | bytes 294920 | tf_op jit(solution)/shard_map/ppermute | solution.py:38

commit v13 on v12

--- a/solution.py
+++ b/solution.py
@@ -96,26 +96,6 @@
     )(*terms)
 
 
-def base_kernel(scale_ref, bits_ref, matrix_ref, *refs):
-    total = refs[0][...].astype(F32)
-    for ref in refs[1:-1]:
-        total = total + ref[...].astype(F32)
-    signs = (1 - 2 * bits_ref[...]).astype(F32)
-    refs[-1][...] = jnp.concatenate(rotate(total * scale_ref[...], signs, matrix_ref[...]), axis=1)
-
-
-def rotated_base(terms, scale, bits, matrix):
-    return pl.pallas_call(
-        base_kernel,
-        in_specs=[VMEM] * (3 + len(terms)),
-        out_specs=VMEM,
-        out_shape=jax.ShapeDtypeStruct(terms[0].shape, F32),
-        compiler_params=params(16),
-        cost_estimate=COST,
-        name="rotated_base",
-    )(scale, bits, matrix, *terms)
-
-
 def adapter(here, share, name):
     z = lax.axis_index("adp")
     if name[0] == "plane":
@@ -152,51 +132,137 @@
     )(ids, tokens, *arrays, *more)
 
 
-def ups_kernel(terms, here, share, rank, ids_ref, bits_ref, matrix_ref, *refs):
+def ups_kernel(named, terms, here, share, rank, ids_ref, bits_ref, matrix_ref, *refs):
     up_ref, mask_ref = refs[-2:]
     width = up_ref.shape[1]
     signs = (1 - 2 * bits_ref[...]).astype(F32)
-    ids = jnp.broadcast_to(ids_ref[...], (rank, ids_ref.shape[1])).T
-    for n, (i, k, cut, name) in enumerate(terms):
+    for n, (i, k, cut) in enumerate(terms):
         turned = rotate(refs[i][k, :, cut : cut + width].astype(F32), signs, matrix_ref[...])
         up_ref[n * rank : (n + 1) * rank, :] = jnp.concatenate(turned, axis=1).astype(BF16)
+    ids = jnp.broadcast_to(ids_ref[...], (rank, ids_ref.shape[1])).T
+    mask_ref[...] = jnp.zeros_like(mask_ref)
+    for n, name in enumerate(named):
         mine = ids == adapter(here, share, name)
         mask_ref[:, n * rank : (n + 1) * rank] = jnp.where(mine, 1.0, 0.0).astype(BF16)
 
 
-def rotated_ups(ids, bits, matrix, here, share, terms, arrays, width):
+def rotated_ups(ids, bits, matrix, here, share, named, terms, arrays, width):
     rank, rows = arrays[0].shape[1], ids.shape[1]
-    every = len(terms) * rank
-    return pl.pallas_call(
-        functools.partial(ups_kernel, terms, here, share, rank),
+    columns = -(-len(named) * rank // 128) * 128
+    return pl.pallas_call(
+        functools.partial(ups_kernel, named, terms, here, share, rank),
         in_specs=[VMEM] * (3 + len(arrays)),
         out_specs=[VMEM, VMEM],
-        out_shape=[jax.ShapeDtypeStruct((every, width), BF16), jax.ShapeDtypeStruct((rows, every), BF16)],
+        out_shape=[jax.ShapeDtypeStruct((len(terms) * rank, width), BF16), jax.ShapeDtypeStruct((rows, columns), BF16)],
         compiler_params=params(32),
         cost_estimate=COST,
         name="rotated_ups",
     )(ids, bits, matrix, *arrays)
 
 
-def final_kernel(mine_ref, theirs_ref, base_ref, up_ref, mask_ref, out_ref):
-    low = (mine_ref[...].astype(F32) + theirs_ref[...].astype(F32)).T.astype(BF16)
-    every = mask_ref.shape[1]
-    spread = jnp.concatenate([low] * (every // low.shape[1]), axis=1) * mask_ref[...]
-    delta = jnp.dot(spread, up_ref[...], preferred_element_type=F32)
-    out_ref[...] = (base_ref[...] + delta).astype(BF16)
-
-
-def final(mine, theirs, base, up, mask):
-    rows, width = base.shape
+def pick_kernel(named, here, share, ids_ref, pick_ref):
+    rows, slots = pick_ref.shape[0], pick_ref.shape[1] // len(named)
+    earlier = lax.broadcasted_iota(jnp.int32, (rows, rows), 0) < lax.broadcasted_iota(jnp.int32, (rows, rows), 1)
+    earlier = jnp.where(earlier, 1.0, 0.0).astype(BF16)
+    ids = jnp.broadcast_to(ids_ref[...], (8, rows))
+    for k, name in enumerate(named):
+        mine = ids == adapter(here, share, name)
+        rank = jnp.dot(jnp.where(mine, 1.0, 0.0).astype(BF16), earlier, preferred_element_type=F32)
+        rank = jnp.where(mine, rank, -1.0)
+        rank = jnp.broadcast_to(rank[:1], (128, rows)).T
+        for at in range(0, slots, 128):
+            slot = (lax.broadcasted_iota(jnp.int32, (rows, 128), 1) + at).astype(F32)
+            pick_ref[:, k * slots + at : k * slots + at + 128] = jnp.where(rank == slot, 1.0, 0.0).astype(BF16)
+
+
+def picked(ids, here, share, named, slots):
+    return pl.pallas_call(
+        functools.partial(pick_kernel, named, here, share),
+        in_specs=[VMEM],
+        out_specs=VMEM,
+        out_shape=jax.ShapeDtypeStruct((ids.shape[1], len(named) * slots), BF16),
+        compiler_params=params(24),
+        cost_estimate=COST,
+        name="picked",
+    )(ids)
+
+
+def compact_kernel(tokens_ref, piece_ref, pick_ref, out_ref):
+    share, features = piece_ref.shape[0], tokens_ref.shape[1]
+    slots = pick_ref.shape[1] // share
+    for k in range(share):
+        product = lax.dot_general(piece_ref[k, :, :features], tokens_ref[...], LAST, preferred_element_type=F32)
+        columns = slice(k * slots, (k + 1) * slots)
+        kept = jnp.dot(product.astype(BF16), pick_ref[:, columns], preferred_element_type=F32)
+        out_ref[:, columns] = kept.astype(BF16)
+
+
+def compact(tokens, piece, pick):
+    return pl.pallas_call(
+        compact_kernel,
+        in_specs=[VMEM] * 3,
+        out_specs=VMEM,
+        out_shape=jax.ShapeDtypeStruct((piece.shape[1], pick.shape[1]), BF16),
+        compiler_params=params(24),
+        cost_estimate=COST,
+        name="compact",
+    )(tokens, piece, pick)
+
+
+def most_kernel(mine_ref, theirs_ref, up_ref, mask_ref, near_ref, scale_ref, bits_ref, matrix_ref, *refs):
+    low = (mine_ref[...].astype(F32) + theirs_ref[...].astype(F32)).astype(BF16).T
+    rank, columns = low.shape[1], mask_ref.shape[1]
+    signs = (1 - 2 * bits_ref[...]).astype(F32)
+    ups = [up_ref[...]]
+    for k in range(near_ref.shape[0]):
+        turned = rotate(near_ref[k].astype(F32), signs, matrix_ref[...])
+        ups.append(jnp.concatenate(turned, axis=1).astype(BF16))
+    missing = columns - sum(up.shape[0] for up in ups)
+    if missing:
+        ups.append(jnp.zeros((missing, up_ref.shape[1]), BF16))
+    spread = jnp.concatenate([low] * (columns // rank), axis=1) * mask_ref[...]
+    delta = jnp.dot(spread, jnp.concatenate(ups, axis=0), preferred_element_type=F32)
+    value = functools.reduce(jnp.add, [ref[...].astype(F32) for ref in refs[:-1]]) * scale_ref[...]
+    refs[-1][...] = jnp.concatenate(rotate(value, signs, matrix_ref[...]), axis=1) + delta
+
+
+def most(mine, theirs, up, mask, near, scale, bits, matrix, terms):
+    return pl.pallas_call(
+        most_kernel,
+        in_specs=[VMEM] * (8 + len(terms)),
+        out_specs=VMEM,
+        out_shape=jax.ShapeDtypeStruct(terms[0].shape, F32),
+        compiler_params=params(32),
+        cost_estimate=COST,
+        name="most",
+    )(mine, theirs, up, mask, near, scale, bits, matrix, *terms)
+
+
+def final_kernel(mine_ref, theirs_ref, pick_ref, piece_ref, bits_ref, matrix_ref, most_ref, out_ref):
+    share, width = piece_ref.shape[0], out_ref.shape[1]
+    features, slots = piece_ref.shape[2] - width, pick_ref.shape[1] // share
+    signs = (1 - 2 * bits_ref[...]).astype(F32)
+    low = (mine_ref[...].astype(F32) + theirs_ref[...].astype(F32)).astype(BF16).T
+    deltas = []
+    for k in range(share):
+        turned = rotate(piece_ref[k, :, features:].astype(F32), signs, matrix_ref[...])
+        up = jnp.concatenate(turned, axis=1).astype(BF16)
+        deltas.append(jnp.dot(low[k * slots : (k + 1) * slots], up, preferred_element_type=F32).astype(BF16))
+    delta = deltas[0] if share == 1 else jnp.concatenate(deltas, axis=0)
+    result = most_ref[...] + jnp.dot(pick_ref[...], delta, preferred_element_type=F32)
+    out_ref[...] = result.astype(BF16)
+
+
+def final(mine, theirs, pick, piece, bits, matrix, rest):
     return pl.pallas_call(
         final_kernel,
-        in_specs=[VMEM] * 5,
-        out_specs=VMEM,
-        out_shape=jax.ShapeDtypeStruct((rows, width), BF16),
+        in_specs=[VMEM] * 7,
+        out_specs=VMEM,
+        out_shape=jax.ShapeDtypeStruct(rest.shape, BF16),
         compiler_params=params(32),
         cost_estimate=COST,
         name="final",
-    )(mine, theirs, base, up, mask)
+    )(mine, theirs, pick, piece, bits, matrix, rest)
 
 
 def local(tokens, adapter_ids, base_weight, channel_scale, adapter_down, adapter_up, sign_bits):
@@ -244,12 +310,23 @@
         return low_rows(ids, tokens, here, share, [((0, features), every)], arrays, low, dtype, cost)
 
     low = more(None, held[: len(mine)] + swapped[:1], F32, lasting(2))
-    low, *came = together(low, *(swap(block, "tp", 1) for block in blocks[:half]))
+    slots = -(-2 * tokens.shape[0] // (here * planes) // 128) * 128
+    last = swapped[-1]
+    pick = picked(ids, here, share, [(last[0], last[1], k) for k in range(share)], slots)
+    low, pick, *came = together(low, pick, *(swap(block, "tp", 1) for block in blocks[:half]))
+
+    def both(low):
+        bit = 1
+        while bit < parts // 2:
+            low = add(low, swap(low, "tp", bit))
+            bit *= 2
+        return low, swap(low, "tp", bit)
 
     rest = held[len(mine) :]
-    low = more(low, swapped[1:-1] + rest, F32, lasting(5))
+    low = more(low, swapped[1:-1] + rest, BF16, lasting(5))
     low, up = together(low, adapter_up)
-    ups = [adapter_up, swap(up, "adp", 1)]
+    near_up = swap(up, "adp", 1)
+    low, other = both(low)
 
     sums = [[block, pair] for block, pair in zip(blocks[half:], came)]
     bit = 2
@@ -257,22 +334,19 @@
         came = [swap(add(*terms), "tp", bit) for terms in sums[1::2]]
         sums = [terms + [pair] for terms, pair in zip(sums[0::2], came)]
         bit *= 2
-    base = rotated_base(sums[0], scale, bits, matrix)
-
-    low, ups[1] = together(low, ups[1])
-    low = more(low, swapped[-1:], BF16)
-    bit = 1
-    while bit < parts // 2:
-        low = add(low, swap(low, "tp", bit))
-        bit *= 2
-    theirs = swap(low, "tp", bit)
-
-
-    far = [one for one in held + swapped if one[0] > 1]
-    every = [(plane, k, 0, ("plane", plane, k)) for plane in (0, 1) for k in range(here)]
-    every += [(2 + i, k, features, (plane, off, k)) for i, (plane, off, _) in enumerate(far) for k in range(share)]
-    up, mask = rotated_ups(ids, bits, matrix, here, share, every, ups + [piece for *_, piece in far], width)
-    return final(low, theirs, base, up, mask)
+
+    far = [one for one in held + swapped[:-1] if one[0] > 1]
+    named = [("plane", 0, k) for k in range(here)]
+    named += [(plane, off, k) for plane, off, _ in far for k in range(share)]
+    ups = [(0, k, 0) for k in range(here)] + [(1 + i, k, features) for i in range(len(far)) for k in range(share)]
+    named += [("plane", 1, k) for k in range(here)]
+    arrays = [adapter_up] + [piece for *_, piece in far]
+    up, mask = rotated_ups(ids, bits, matrix, here, share, named, ups, arrays, width)
+
+    piece, up, mask, near_up = together(last[2], up, mask, near_up)
+    kept, more_kept = both(compact(tokens, piece, pick))
+    rest = most(low, other, up, mask, near_up, scale, bits, matrix, sums[0])
+    return final(kept, more_kept, pick, piece, bits, matrix, rest)
 
 
 def solution(mesh):

time: 44.4 us -> 43.7 us (0.984)
  waiting for transfers between devices: 13.3 us -> 10.4 us
  starting transfers between devices: 14.9 us -> 16.5 us
  Pallas kernels: 9.84 us -> 10.5 us
    ppermute x12 -> x14, waiting for transfers between devices: 13.3 us -> 10.4 us  [swap(): lax.ppermute(x, axis, [(i, i ^ bit) for i in range(lax.axis_size(axis))])]
    pallas_call x3 -> x5, Pallas kernels: 2.59 us -> 4.28 us  [the longest x1 1.35 us: final(): pl.pallas_call(final_kernel, in_specs=[VMEM] * 7, out_specs=VMEM, out_sha...]
    ppermute x12 -> x14, starting transfers between devices: 14.9 us -> 16.5 us  [swap(): lax.ppermute(x, axis, [(i, i ^ bit) for i in range(lax.axis_size(axis))])]
    pallas_call x3 -> x2, Pallas kernels: 3.46 us -> 2.39 us  [low_rows(): pl.pallas_call(functools.partial(low_kernel, groups, here, share, rank, b...]
  transfers between devices with their start and end apart: 12 -> 14, of which waited for: 7 -> 8; matrix products, arithmetic and copies ran while one was open for 2% -> 2% of each run, Pallas kernels for 19% -> 21%
where the time goes in v13:
time: 43.7 us; the launch traced here: 43.4 us
  starting transfers between devices  16.5 us (38%)
  Pallas kernels  10.5 us (24%)
  waiting for transfers between devices  10.4 us (24%)
  local copies, waits for them, and re-layouts  5.84 us (13%)
    ppermute x14, starting transfers between devices, swap(): lax.ppermute(x, axis, [(i, i ^ bit) for i in range(lax.axis_size(axis))])  16.5 us
    ppermute x14, waiting for transfers between devices, swap(): lax.ppermute(x, axis, [(i, i ^ bit) for i in range(lax.axis_size(axis))])  10.4 us
    unnamed x18, local copies, waits for them, and re-layouts  4.12 us
    pallas_call x2, Pallas kernels, partials(): pl.pallas_call(functools.partial(partial_kernel, offsets, parts), in_spec...  3.66 us
    pallas_call x2, Pallas kernels, low_rows(): pl.pallas_call(functools.partial(low_kernel, groups, here, share, rank, b...  2.39 us
    pallas_call x1, Pallas kernels, final(): pl.pallas_call(final_kernel, in_specs=[VMEM] * 7, out_specs=VMEM, out_sha...  1.35 us
    pallas_call x1, Pallas kernels, compact(): pl.pallas_call(compact_kernel, in_specs=[VMEM] * 3, out_specs=VMEM, out_s...  1.25 us
    dynamic_slice x1, local copies, waits for them, and re-layouts, local(): own = lax.dynamic_slice_in_dim(down, start, share, 0)  0.97 us
  transfers between devices with their start and end apart: 14, of which 8 were waited for; matrix products, arithmetic and copies ran while one was open for 2% of the time, Pallas kernels for 21%

profile of v13, /device:TPU:0, one launch (start us, length us, event | category | flops | bytes accessed | tf_op | source)
XLA Modules:
  0.0 43.4 jit_solution(16295615875330815663)
XLA Ops:
  0.0 1.0 %dynamic-slice_bitcast_fusion = bf16[1,64,2048]{2,1,0:T(8,128)(2,1)S(1)} fusion(bf16[2,2048,64]{1,2,0:T(8,128)(2,1)} %param.12, s32[]{:T(128)S(6)} %select_n.4), kind=kLoop, calls=%fused_computation.1 | loop fusion | bytes 524292 | tf_op jit(solution)/shard_map/dynamic_slice | solution.py:279
  1.0 3.1 %collective-permute-start = (bf16[1,64,2048]{2,1,0:T(8,128)(2,1)S(1)}, bf16[1,64,2048]{2,1,0:T(8,128)(2,1)S(1)}, u32[]{:S(2)}, u32[]{:S(2)}) collective-permute-start(bf16[1,64,2048]{2,1,0:T(8,128)(2,1)S(1)} %dynamic-slice_bitcast_fusion), channel_id=1, source_target_pairs={{0,4},{4,0},{8,12},{12,8},{1,5},{5,1},{9,13},{13,9},{2,6},{6,2},{1... | collective-permute-start | bytes 786440 | tf_op jit(solution)/shard_map/ppermute | solution.py:38
  4.1 0.8 %constant_dynamic-slice_fusion = bf16[1,64,256]{2,1,0:T(8,128)(2,1)S(1)} fusion(bf16[2,64,256]{2,1,0:T(8,128)(2,1)} %refs_0_.1, s32[]{:T(128)S(6)} %select_n.4), kind=kLoop, calls=%fused_computation.2 | loop fusion | bytes 65540 | tf_op jit(solution)/shard_map/dynamic_slice | solution.py:281
  4.8 2.7 %collective-permute-start.1 = (bf16[1,64,2304]{2,1,0:T(8,128)(2,1)S(1)}, bf16[1,64,2304]{2,1,0:T(8,128)(2,1)S(1)}, u32[]{:S(2)}, u32[]{:S(2)}) collective-permute-start(bf16[1,64,2304]{2,1,0:T(8,128)(2,1)S(1)} %pad_maximum_fusion), channel_id=1, source_target_pairs={{0,8},{4,12},{8,0},{12,4},{1,9},{5,13},{9,1},{13,5},{2,10},{6,14},... | collective-permute-start | bytes 884744 | tf_op jit(solution)/shard_map/ppermute | solution.py:38
  7.5 1.9 %copy-done = bf16[768,2048]{1,0:T(8,128)(2,1)S(1)} copy-done((bf16[768,2048]{1,0:T(8,128)(2,1)S(1)}, bf16[768,2048]{1,0:T(8,128)(2,1)}, u32[]{:S(2)}) %copy-start) | copy-done | bytes 3145752
  9.4 2.2 %copy-done.2 = bf16[2048,1024]{1,0:T(8,128)(2,1)S(1)} copy-done((bf16[2048,1024]{1,0:T(8,128)(2,1)S(1)}, bf16[2048,1024]{1,0:T(8,128)(2,1)}, u32[]{:S(2)}) %copy-start.2) | copy-done | bytes 4194328
  11.6 2.7 %partials.2 = (bf16[768,256]{1,0:T(8,128)(2,1)S(1)}, bf16[768,256]{1,0:T(8,128)(2,1)S(1)}, bf16[768,256]{1,0:T(8,128)(2,1)S(1)}) custom-call(bf16[768,2048]{1,0:T(8,128)(2,1)S(1)} %copy-done, bf16[2048,1024]{1,0:T(8,128)(2,1)S(1)} %copy-done.2), custom_call_target="tpu_custom_call" | custom-call | flops 4000000000 | bytes 1 | tf_op jit(solution)/shard_map/partials/pallas_call | solution.py:69
  14.3 0.8 %collective-permute-done.refs_0_ = bf16[1,64,2048]{2,1,0:T(8,128)(2,1)S(1)} collective-permute-done((bf16[1,64,2048]{2,1,0:T(8,128)(2,1)S(1)}, bf16[1,64,2048]{2,1,0:T(8,128)(2,1)S(1)}, u32[]{:S(2)}, u32[]{:S(2)}) %collective-permute-start) | collective-permute-done | bytes 262176 | tf_op jit(solution)/shard_map/ppermute | solution.py:38
  15.0 1.7 %collective-permute-start.5 = (bf16[1,64,2048]{2,1,0:T(8,128)(2,1)S(1)}, bf16[1,64,2048]{2,1,0:T(8,128)(2,1)S(1)}, u32[]{:S(2)}, u32[]{:S(2)}) collective-permute-start(bf16[1,64,2048]{2,1,0:T(8,128)(2,1)S(1)} %collective-permute-done.refs_0_), channel_id=1, source_target_pairs={{0,16},{16,0},{1,17},{17,1},{2,18},{18,2},{3,19},{19,3},{4,20},{20... | collective-permute-start | bytes 786440 | tf_op jit(solution)/shard_map/ppermute | solution.py:38
  16.7 0.5 %collective-permute-start.7 = (bf16[768,256]{1,0:T(8,128)(2,1)S(1)}, bf16[768,256]{1,0:T(8,128)(2,1)S(1)}, u32[]{:S(2)}, u32[]{:S(2)}) collective-permute-start(bf16[768,256]{1,0:T(8,128)(2,1)S(1)} %get-tuple-element.33), channel_id=1, source_target_pairs={{0,1},{1,0},{2,3},{3,2},{4,5},{5,4},{6,7},{7,6},{8,9},{9,8},{10,11... | collective-permute-start | bytes 1179656 | tf_op jit(solution)/shard_map/ppermute | solution.py:38
  17.2 1.0 %partials.3.refs_0_ = bf16[768,256]{1,0:T(8,128)(2,1)S(1)} custom-call(bf16[768,2048]{1,0:T(8,128)(2,1)S(1)} %copy-done, bf16[2048,1024]{1,0:T(8,128)(2,1)S(1)} %copy-done.2, bf16[768,256]{1,0:T(8,128)(2,1)S(1)} %get-tuple-element.27.refs_0_), custom_call_target="tpu_custom_call" | custom-call | flops 1 | bytes 1 | tf_op jit(solution)/shard_map/partials/pallas_call | solution.py:69
  18.2 2.4 %collective-permute-done.1.refs_1_ = bf16[1,64,2304]{2,1,0:T(8,128)(2,1)S(1)} collective-permute-done((bf16[1,64,2304]{2,1,0:T(8,128)(2,1)S(1)}, bf16[1,64,2304]{2,1,0:T(8,128)(2,1)S(1)}, u32[]{:S(2)}, u32[]{:S(2)}) %collective-permute-start.1) | collective-permute-done | bytes 294944 | tf_op jit(solution)/shard_map/ppermute | solution.py:38
  20.6 1.5 %collective-permute-start.4 = (bf16[1,64,2304]{2,1,0:T(8,128)(2,1)S(1)}, bf16[1,64,2304]{2,1,0:T(8,128)(2,1)S(1)}, u32[]{:S(2)}, u32[]{:S(2)}) collective-permute-start(bf16[1,64,2304]{2,1,0:T(8,128)(2,1)S(1)} %collective-permute-done.1.refs_1_), channel_id=1, source_target_pairs={{0,16},{16,0},{1,17},{17,1},{2,18},{18,2},{3,19},{19,3},{4,20},{20... | collective-permute-start | bytes 884744 | tf_op jit(solution)/shard_map/ppermute | solution.py:38
  22.2 0.4 picked.1.pick_ref
  22.5 0.5 %collective-permute-done.5.refs_2_ = bf16[1,64,2048]{2,1,0:T(8,128)(2,1)S(1)} collective-permute-done((bf16[1,64,2048]{2,1,0:T(8,128)(2,1)S(1)}, bf16[1,64,2048]{2,1,0:T(8,128)(2,1)S(1)}, u32[]{:S(2)}, u32[]{:S(2)}) %collective-permute-start.5) | collective-permute-done | bytes 262176 | tf_op jit(solution)/shard_map/ppermute | solution.py:38
  23.0 1.2 %low_rows.2.refs_2_ = f32[64,768]{1,0:T(8,128)S(1)} custom-call(s32[1,768]{1,0:T(1,128)S(1)} %bitcast.8, bf16[768,2048]{1,0:T(8,128)(2,1)S(1)} %copy-done.1, bf16[1,64,2048]{2,1,0:T(8,128)(2,1)S(1)} %collective-permute-done.refs_0_, bf16[1,64,2304]{2,1,0:T(8,128)(2,1)S(1)} %collective-permute-done.1.refs_1_, ...), custom_call_target="tpu_custom_call" | custom-call | flops 2000000000 | bytes 1 | tf_op jit(solution)/shard_map/low_rows/pallas_call | solution.py:124
  24.3 0.1 add.10
  24.4 1.3 %collective-permute-start.13 = (bf16[768,256]{1,0:T(8,128)(2,1)S(1)}, bf16[768,256]{1,0:T(8,128)(2,1)S(1)}, u32[]{:S(2)}, u32[]{:S(2)}) collective-permute-start(bf16[768,256]{1,0:T(8,128)(2,1)S(1)} %add.10), channel_id=1, source_target_pairs={{0,2},{1,3},{2,0},{3,1},{4,6},{5,7},{6,4},{7,5},{8,10},{9,11},{10,... | collective-permute-start | bytes 1179656 | tf_op jit(solution)/shard_map/ppermute | solution.py:38
  25.7 2.6 %collective-permute-done.2.refs_2_.refs_1_ = bf16[1,64,2304]{2,1,0:T(8,128)(2,1)S(1)} collective-permute-done((bf16[1,64,2304]{2,1,0:T(8,128)(2,1)S(1)}, bf16[1,64,2304]{2,1,0:T(8,128)(2,1)S(1)}, u32[]{:S(2)}, u32[]{:S(2)}) %collective-permute-start.2) | collective-permute-done | bytes 294944 | tf_op jit(solution)/shard_map/ppermute | solution.py:38
  28.2 1.5 %collective-permute-start.3 = (bf16[1,64,2304]{2,1,0:T(8,128)(2,1)S(1)}, bf16[1,64,2304]{2,1,0:T(8,128)(2,1)S(1)}, u32[]{:S(2)}, u32[]{:S(2)}) collective-permute-start(bf16[1,64,2304]{2,1,0:T(8,128)(2,1)S(1)} %collective-permute-done.2.refs_2_.refs_1_), channel_id=1, source_target_pairs={{0,16},{16,0},{1,17},{17,1},{2,18},{18,2},{3,19},{19,3},{4,20},{20... | collective-permute-start | bytes 884744 | tf_op jit(solution)/shard_map/ppermute | solution.py:38
  29.8 1.2 %low_rows.3.refs_0_ = bf16[64,768]{1,0:T(8,128)(2,1)S(1)} custom-call(s32[1,768]{1,0:T(1,128)S(1)} %bitcast.9, bf16[768,2048]{1,0:T(8,128)(2,1)S(1)} %copy-done.1, bf16[1,64,2304]{2,1,0:T(8,128)(2,1)S(1)} %collective-permute-done.4.refs_3_.refs_0_, bf16[1,64,2304]{2,1,0:T(8,128)(2,1)S(1)} %collective-permute-done.2.refs_2_.refs_1_, ...), custom_call_target="tpu_custom_call" | custom-call | flops 5000000000 | bytes 1 | tf_op jit(solution)/shard_map/low_rows/pallas_call | solution.py:124
  31.0 1.0 %collective-permute-start.8 = (bf16[2,64,256]{2,1,0:T(8,128)(2,1)S(1)}, bf16[2,64,256]{2,1,0:T(8,128)(2,1)S(1)}, u32[]{:S(2)}, u32[]{:S(2)}) collective-permute-start(bf16[2,64,256]{2,1,0:T(8,128)(2,1)S(1)} %copy-done.4), channel_id=1, source_target_pairs={{0,4},{4,0},{8,12},{12,8},{1,5},{5,1},{9,13},{13,9},{2,6},{6,2},{1... | collective-permute-start | bytes 196616 | tf_op jit(solution)/shard_map/ppermute | solution.py:38
  32.1 0.2 collective-permute-done.11.refs_1_
  32.3 1.6 %collective-permute-start.12 = (bf16[64,768]{1,0:T(8,128)(2,1)S(1)}, bf16[64,768]{1,0:T(8,128)(2,1)S(1)}, u32[]{:S(2)}, u32[]{:S(2)}) collective-permute-start(bf16[64,768]{1,0:T(8,128)(2,1)S(1)} %add.9.mine_ref), channel_id=1, source_target_pairs={{0,2},{1,3},{2,0},{3,1},{4,6},{5,7},{6,4},{7,5},{8,10},{9,11},{10,... | collective-permute-start | bytes 294920 | tf_op jit(solution)/shard_map/ppermute | solution.py:38
  33.9 0.5 %rotated_ups.1 = (bf16[320,256]{1,0:T(8,128)(2,1)S(1)}, bf16[768,512]{1,0:T(8,128)(2,1)S(1)}) custom-call(s32[1,768]{1,0:T(1,128)S(1)} %bitcast.10, s32[1,128]{1,0:T(1,128)S(1)} %bitcast.11, bf16[128,128]{1,0:T(8,128)(2,1)S(1)} %copy-done.3, bf16[2,64,256]{2,1,0:T(8,128)(2,1)S(1)} %copy-done.4, bf16[1,64,2304]{2,1,0:T(8,128)(2,1)S(1)} %collective-permute-done.1.refs_1_, ...), custom_call_target="tpu_custom_call" | custom-call | flops 1 | bytes 1 | tf_op jit(solution)/shard_map/rotated_ups/pallas_call | solution.py:152
  34.4 1.1 %collective-permute-done.8.near_ref = bf16[2,64,256]{2,1,0:T(8,128)(2,1)S(1)} collective-permute-done((bf16[2,64,256]{2,1,0:T(8,128)(2,1)S(1)}, bf16[2,64,256]{2,1,0:T(8,128)(2,1)S(1)}, u32[]{:S(2)}, u32[]{:S(2)}) %collective-permute-start.8) | collective-permute-done | bytes 65568 | tf_op jit(solution)/shard_map/ppermute | solution.py:38
  35.5 1.3 %compact.1.refs_0_ = bf16[64,256]{1,0:T(8,128)(2,1)S(1)} custom-call(bf16[768,2048]{1,0:T(8,128)(2,1)S(1)} %copy-done.1, bf16[1,64,2304]{2,1,0:T(8,128)(2,1)S(1)} %collective-permute-done.3.piece_ref, bf16[768,256]{1,0:T(8,128)(2,1)S(1)} %picked.1.pick_ref), custom_call_target="tpu_custom_call" | custom-call | flops 1 | bytes 1 | tf_op jit(solution)/shard_map/compact/pallas_call | solution.py:201
  36.9 1.2 %collective-permute-done.9.refs_1_ = bf16[64,256]{1,0:T(8,128)(2,1)S(1)} collective-permute-done((bf16[64,256]{1,0:T(8,128)(2,1)S(1)}, bf16[64,256]{1,0:T(8,128)(2,1)S(1)}, u32[]{:S(2)}, u32[]{:S(2)}) %collective-permute-start.9) | collective-permute-done | bytes 32800 | tf_op jit(solution)/shard_map/ppermute | solution.py:38
  38.1 1.6 %collective-permute-start.10 = (bf16[64,256]{1,0:T(8,128)(2,1)S(1)}, bf16[64,256]{1,0:T(8,128)(2,1)S(1)}, u32[]{:S(2)}, u32[]{:S(2)}) collective-permute-start(bf16[64,256]{1,0:T(8,128)(2,1)S(1)} %add.8.mine_ref), channel_id=1, source_target_pairs={{0,2},{1,3},{2,0},{3,1},{4,6},{5,7},{6,4},{7,5},{8,10},{9,11},{10,... | collective-permute-start | bytes 98312 | tf_op jit(solution)/shard_map/ppermute | solution.py:38
  39.7 0.8 %most.1.most_ref = f32[768,256]{1,0:T(8,128)S(1)} custom-call(bf16[64,768]{1,0:T(8,128)(2,1)S(1)} %add.9.mine_ref, bf16[64,768]{1,0:T(8,128)(2,1)S(1)} %collective-permute-done.12.theirs_ref, bf16[320,256]{1,0:T(8,128)(2,1)S(1)} %get-tuple-element.39.up_ref, bf16[768,512]{1,0:T(8,128)(2,1)S(1)} %get-tuple-element.40.mask_ref, ...), custom_call_target="tpu_custom_call" | custom-call | flops 1 | bytes 1 | tf_op jit(solution)/shard_map/most/pallas_call | solution.py:230
  40.4 1.6 %collective-permute-done.10.theirs_ref = bf16[64,256]{1,0:T(8,128)(2,1)S(1)} collective-permute-done((bf16[64,256]{1,0:T(8,128)(2,1)S(1)}, bf16[64,256]{1,0:T(8,128)(2,1)S(1)}, u32[]{:S(2)}, u32[]{:S(2)}) %collective-permute-start.10) | collective-permute-done | bytes 32800 | tf_op jit(solution)/shard_map/ppermute | solution.py:38
  42.1 1.3 %final.1 = bf16[768,256]{1,0:T(8,128)(2,1)} custom-call(bf16[64,256]{1,0:T(8,128)(2,1)S(1)} %add.8.mine_ref, bf16[64,256]{1,0:T(8,128)(2,1)S(1)} %collective-permute-done.10.theirs_ref, bf16[768,256]{1,0:T(8,128)(2,1)S(1)} %picked.1.pick_ref, bf16[1,64,2304]{2,1,0:T(8,128)(2,1)S(1)} %collective-permute-done.3.piece_ref, s32[1,128]{1,0:T(1,128)S(1)} %bitcast.13, ...), custom_call_target="tpu_custom_call" | custom-call | flops 1 | bytes 1 | tf_op jit(solution)/shard_map/final/pallas_call | solution.py:257
  (29 shorter events, 0.3 us)
Async XLA Ops:
  1.0 14.1 %collective-permute-start = (bf16[1,64,2048]{2,1,0:T(8,128)(2,1)S(1)}, bf16[1,64,2048]{2,1,0:T(8,128)(2,1)S(1)}, u32[]{:S(2)}, u32[]{:S(2)}) collective-permute-start(bf16[1,64,2048]{2,1,0:T(8,128)(2,1)S(1)} %dynamic-slice_bitcast_fusion), channel_id=1, source_target_pairs={{0,4},{4,0},{8,12},{12,8},{1,5},{5,1},{9,13},{13,9},{2,6},{6,2},{1... | collective-permute-start | bytes 786440 | tf_op jit(solution)/shard_map/ppermute | solution.py:38
  4.8 15.8 %collective-permute-start.1 = (bf16[1,64,2304]{2,1,0:T(8,128)(2,1)S(1)}, bf16[1,64,2304]{2,1,0:T(8,128)(2,1)S(1)}, u32[]{:S(2)}, u32[]{:S(2)}) collective-permute-start(bf16[1,64,2304]{2,1,0:T(8,128)(2,1)S(1)} %pad_maximum_fusion), channel_id=1, source_target_pairs={{0,8},{4,12},{8,0},{12,4},{1,9},{5,13},{9,1},{13,5},{2,10},{6,14},... | collective-permute-start | bytes 884744 | tf_op jit(solution)/shard_map/ppermute | solution.py:38
  7.5 1.9 %copy-start = (bf16[768,2048]{1,0:T(8,128)(2,1)S(1)}, bf16[768,2048]{1,0:T(8,128)(2,1)}, u32[]{:S(2)}) copy-start(bf16[768,2048]{1,0:T(8,128)(2,1)} %tokens_ref.9) | copy-start | bytes 9437188
  9.4 2.2 %copy-start.2 = (bf16[2048,1024]{1,0:T(8,128)(2,1)S(1)}, bf16[2048,1024]{1,0:T(8,128)(2,1)}, u32[]{:S(2)}) copy-start(bf16[2048,1024]{1,0:T(8,128)(2,1)} %weight_ref.3) | copy-start | bytes 12582916
  14.2 7.9 %copy-start.6 = (s32[768,1]{0,1:T(1,128)S(1)}, s32[768,1]{0,1:T(1,128)}, u32[]{:S(2)}) copy-start(s32[768,1]{0,1:T(1,128)} %param.9) | copy-start | bytes 9220
  15.0 8.0 %collective-permute-start.5 = (bf16[1,64,2048]{2,1,0:T(8,128)(2,1)S(1)}, bf16[1,64,2048]{2,1,0:T(8,128)(2,1)S(1)}, u32[]{:S(2)}, u32[]{:S(2)}) collective-permute-start(bf16[1,64,2048]{2,1,0:T(8,128)(2,1)S(1)} %collective-permute-done.refs_0_), channel_id=1, source_target_pairs={{0,16},{16,0},{1,17},{17,1},{2,18},{18,2},{3,19},{19,3},{4,20},{20... | collective-permute-start | bytes 786440 | tf_op jit(solution)/shard_map/ppermute | solution.py:38
  16.7 7.6 %collective-permute-start.6 = (bf16[768,256]{1,0:T(8,128)(2,1)S(1)}, bf16[768,256]{1,0:T(8,128)(2,1)S(1)}, u32[]{:S(2)}, u32[]{:S(2)}) collective-permute-start(bf16[768,256]{1,0:T(8,128)(2,1)S(1)} %get-tuple-element.32), channel_id=1, source_target_pairs={{0,1},{1,0},{2,3},{3,2},{4,5},{5,4},{6,7},{7,6},{8,9},{9,8},{10,11... | collective-permute-start | bytes 1179656 | tf_op jit(solution)/shard_map/ppermute | solution.py:38
  16.7 6.3 %copy-start.1 = (bf16[768,2048]{1,0:T(8,128)(2,1)S(1)}, bf16[768,2048]{1,0:T(8,128)(2,1)}, u32[]{:S(2)}) copy-start(bf16[768,2048]{1,0:T(8,128)(2,1)} %tokens_ref.9) | copy-start | bytes 9437188
  16.7 6.3 %copy-start.5 = (bf16[2,2048,64]{1,2,0:T(8,128)(2,1)S(1)}, bf16[2,2048,64]{1,2,0:T(8,128)(2,1)}, u32[]{:S(2)}) copy-start(bf16[2,2048,64]{1,2,0:T(8,128)(2,1)} %param.12) | copy-start | bytes 1572868
  16.7 7.6 %collective-permute-start.7 = (bf16[768,256]{1,0:T(8,128)(2,1)S(1)}, bf16[768,256]{1,0:T(8,128)(2,1)S(1)}, u32[]{:S(2)}, u32[]{:S(2)}) collective-permute-start(bf16[768,256]{1,0:T(8,128)(2,1)S(1)} %get-tuple-element.33), channel_id=1, source_target_pairs={{0,1},{1,0},{2,3},{3,2},{4,5},{5,4},{6,7},{7,6},{8,9},{9,8},{10,11... | collective-permute-start | bytes 1179656 | tf_op jit(solution)/shard_map/ppermute | solution.py:38
  20.6 7.6 %collective-permute-start.2 = (bf16[1,64,2304]{2,1,0:T(8,128)(2,1)S(1)}, bf16[1,64,2304]{2,1,0:T(8,128)(2,1)S(1)}, u32[]{:S(2)}, u32[]{:S(2)}) collective-permute-start(bf16[1,64,2304]{2,1,0:T(8,128)(2,1)S(1)} %collective-permute-done.1.refs_1_), channel_id=1, source_target_pairs={{0,4},{4,0},{8,12},{12,8},{1,5},{5,1},{9,13},{13,9},{2,6},{6,2},{1... | collective-permute-start | bytes 884744 | tf_op jit(solution)/shard_map/ppermute | solution.py:38
  20.6 9.1 %collective-permute-start.4 = (bf16[1,64,2304]{2,1,0:T(8,128)(2,1)S(1)}, bf16[1,64,2304]{2,1,0:T(8,128)(2,1)S(1)}, u32[]{:S(2)}, u32[]{:S(2)}) collective-permute-start(bf16[1,64,2304]{2,1,0:T(8,128)(2,1)S(1)} %collective-permute-done.1.refs_1_), channel_id=1, source_target_pairs={{0,16},{16,0},{1,17},{17,1},{2,18},{18,2},{3,19},{19,3},{4,20},{20... | collective-permute-start | bytes 884744 | tf_op jit(solution)/shard_map/ppermute | solution.py:38
  24.4 6.6 %copy-start.4 = (bf16[2,64,256]{2,1,0:T(8,128)(2,1)S(1)}, bf16[2,64,256]{2,1,0:T(8,128)(2,1)}, u32[]{:S(2)}) copy-start(bf16[2,64,256]{2,1,0:T(8,128)(2,1)} %refs_0_.1) | copy-start | bytes 196612
  24.4 9.5 %copy-start.3 = (bf16[128,128]{1,0:T(8,128)(2,1)S(1)}, bf16[128,128]{1,0:T(8,128)(2,1)}, u32[]{:S(2)}) copy-start(bf16[128,128]{1,0:T(8,128)(2,1)} %constant.12.clone.matrix_ref) | copy-start | bytes 98308
  24.4 9.5 %copy-start.7 = (s32[128]{0:T(128)S(1)}, s32[128]{0:T(128)}, u32[]{:S(2)}) copy-start(s32[128]{0:T(128)} %param.14) | copy-start | bytes 1540
  24.4 15.2 %collective-permute-start.13 = (bf16[768,256]{1,0:T(8,128)(2,1)S(1)}, bf16[768,256]{1,0:T(8,128)(2,1)S(1)}, u32[]{:S(2)}, u32[]{:S(2)}) collective-permute-start(bf16[768,256]{1,0:T(8,128)(2,1)S(1)} %add.10), channel_id=1, source_target_pairs={{0,2},{1,3},{2,0},{3,1},{4,6},{5,7},{6,4},{7,5},{8,10},{9,11},{10,... | collective-permute-start | bytes 1179656 | tf_op jit(solution)/shard_map/ppermute | solution.py:38
  28.2 7.3 %collective-permute-start.3 = (bf16[1,64,2304]{2,1,0:T(8,128)(2,1)S(1)}, bf16[1,64,2304]{2,1,0:T(8,128)(2,1)S(1)}, u32[]{:S(2)}, u32[]{:S(2)}) collective-permute-start(bf16[1,64,2304]{2,1,0:T(8,128)(2,1)S(1)} %collective-permute-done.2.refs_2_.refs_1_), channel_id=1, source_target_pairs={{0,16},{16,0},{1,17},{17,1},{2,18},{18,2},{3,19},{19,3},{4,20},{20... | collective-permute-start | bytes 884744 | tf_op jit(solution)/shard_map/ppermute | solution.py:38
  30.9 8.7 %copy-start.8 = (f32[256]{0:T(256)S(1)}, f32[256]{0:T(256)}, u32[]{:S(2)}) copy-start(f32[256]{0:T(256)} %param.11) | copy-start | bytes 3076
  30.9 1.4 %collective-permute-start.11 = (bf16[64,768]{1,0:T(8,128)(2,1)S(1)}, bf16[64,768]{1,0:T(8,128)(2,1)S(1)}, u32[]{:S(2)}, u32[]{:S(2)}) collective-permute-start(bf16[64,768]{1,0:T(8,128)(2,1)S(1)} %low_rows.3.refs_0_), channel_id=1, source_target_pairs={{0,1},{1,0},{2,3},{3,2},{4,5},{5,4},{6,7},{7,6},{8,9},{9,8},{10,11... | collective-permute-start | bytes 294920 | tf_op jit(solution)/shard_map/ppermute | solution.py:38
  31.0 4.5 %collective-permute-start.8 = (bf16[2,64,256]{2,1,0:T(8,128)(2,1)S(1)}, bf16[2,64,256]{2,1,0:T(8,128)(2,1)S(1)}, u32[]{:S(2)}, u32[]{:S(2)}) collective-permute-start(bf16[2,64,256]{2,1,0:T(8,128)(2,1)S(1)} %copy-done.4), channel_id=1, source_target_pairs={{0,4},{4,0},{8,12},{12,8},{1,5},{5,1},{9,13},{13,9},{2,6},{6,2},{1... | collective-permute-start | bytes 196616 | tf_op jit(solution)/shard_map/ppermute | solution.py:38
  32.3 7.3 %collective-permute-start.12 = (bf16[64,768]{1,0:T(8,128)(2,1)S(1)}, bf16[64,768]{1,0:T(8,128)(2,1)S(1)}, u32[]{:S(2)}, u32[]{:S(2)}) collective-permute-start(bf16[64,768]{1,0:T(8,128)(2,1)S(1)} %add.9.mine_ref), channel_id=1, source_target_pairs={{0,2},{1,3},{2,0},{3,1},{4,6},{5,7},{6,4},{7,5},{8,10},{9,11},{10,... | collective-permute-start | bytes 294920 | tf_op jit(solution)/shard_map/ppermute | solution.py:38
  36.8 1.3 %collective-permute-start.9 = (bf16[64,256]{1,0:T(8,128)(2,1)S(1)}, bf16[64,256]{1,0:T(8,128)(2,1)S(1)}, u32[]{:S(2)}, u32[]{:S(2)}) collective-permute-start(bf16[64,256]{1,0:T(8,128)(2,1)S(1)} %compact.1.refs_0_), channel_id=1, source_target_pairs={{0,1},{1,0},{2,3},{3,2},{4,5},{5,4},{6,7},{7,6},{8,9},{9,8},{10,11... | collective-permute-start | bytes 98312 | tf_op jit(solution)/shard_map/ppermute | solution.py:38
  38.1 4.0 %collective-permute-start.10 = (bf16[64,256]{1,0:T(8,128)(2,1)S(1)}, bf16[64,256]{1,0:T(8,128)(2,1)S(1)}, u32[]{:S(2)}, u32[]{:S(2)}) collective-permute-start(bf16[64,256]{1,0:T(8,128)(2,1)S(1)} %add.8.mine_ref), channel_id=1, source_target_pairs={{0,2},{1,3},{2,0},{3,1},{4,6},{5,7},{6,4},{7,5},{8,10},{9,11},{10,... | collective-permute-start | bytes 98312 | tf_op jit(solution)/shard_map/ppermute | solution.py:38

commit v14 on v13

--- a/solution.py
+++ b/solution.py
@@ -135,6 +135,7 @@
 def ups_kernel(named, terms, here, share, rank, ids_ref, bits_ref, matrix_ref, *refs):
     up_ref, mask_ref = refs[-2:]
     width = up_ref.shape[1]
+    up_ref[...] = jnp.zeros_like(up_ref)
     signs = (1 - 2 * bits_ref[...]).astype(F32)
     for n, (i, k, cut) in enumerate(terms):
         turned = rotate(refs[i][k, :, cut : cut + width].astype(F32), signs, matrix_ref[...])
@@ -153,7 +154,7 @@
         functools.partial(ups_kernel, named, terms, here, share, rank),
         in_specs=[VMEM] * (3 + len(arrays)),
         out_specs=[VMEM, VMEM],
-        out_shape=[jax.ShapeDtypeStruct((len(terms) * rank, width), BF16), jax.ShapeDtypeStruct((rows, columns), BF16)],
+        out_shape=[jax.ShapeDtypeStruct((columns, width), BF16), jax.ShapeDtypeStruct((rows, columns), BF16)],
         compiler_params=params(32),
         cost_estimate=COST,
         name="rotated_ups",
@@ -209,40 +210,34 @@
     )(tokens, piece, pick)
 
 
-def most_kernel(mine_ref, theirs_ref, up_ref, mask_ref, near_ref, scale_ref, bits_ref, matrix_ref, *refs):
+def most_kernel(mine_ref, theirs_ref, up_ref, mask_ref, scale_ref, bits_ref, matrix_ref, *refs):
     low = (mine_ref[...].astype(F32) + theirs_ref[...].astype(F32)).astype(BF16).T
     rank, columns = low.shape[1], mask_ref.shape[1]
     signs = (1 - 2 * bits_ref[...]).astype(F32)
-    ups = [up_ref[...]]
-    for k in range(near_ref.shape[0]):
-        turned = rotate(near_ref[k].astype(F32), signs, matrix_ref[...])
-        ups.append(jnp.concatenate(turned, axis=1).astype(BF16))
-    missing = columns - sum(up.shape[0] for up in ups)
-    if missing:
-        ups.append(jnp.zeros((missing, up_ref.shape[1]), BF16))
     spread = jnp.concatenate([low] * (columns // rank), axis=1) * mask_ref[...]
-    delta = jnp.dot(spread, jnp.concatenate(ups, axis=0), preferred_element_type=F32)
+    delta = jnp.dot(spread, up_ref[...], preferred_element_type=F32)
     value = functools.reduce(jnp.add, [ref[...].astype(F32) for ref in refs[:-1]]) * scale_ref[...]
     refs[-1][...] = jnp.concatenate(rotate(value, signs, matrix_ref[...]), axis=1) + delta
 
 
-def most(mine, theirs, up, mask, near, scale, bits, matrix, terms):
+def most(mine, theirs, up, mask, scale, bits, matrix, terms):
     return pl.pallas_call(
         most_kernel,
-        in_specs=[VMEM] * (8 + len(terms)),
+        in_specs=[VMEM] * (7 + len(terms)),
         out_specs=VMEM,
         out_shape=jax.ShapeDtypeStruct(terms[0].shape, F32),
         compiler_params=params(32),
         cost_estimate=COST,
         name="most",
-    )(mine, theirs, up, mask, near, scale, bits, matrix, *terms)
-
-
-def final_kernel(mine_ref, theirs_ref, pick_ref, piece_ref, bits_ref, matrix_ref, most_ref, out_ref):
+    )(mine, theirs, up, mask, scale, bits, matrix, *terms)
+
+
+def final_kernel(pick_ref, piece_ref, bits_ref, matrix_ref, most_ref, *refs):
+    kept_refs, out_ref = refs[:-1], refs[-1]
     share, width = piece_ref.shape[0], out_ref.shape[1]
     features, slots = piece_ref.shape[2] - width, pick_ref.shape[1] // share
     signs = (1 - 2 * bits_ref[...]).astype(F32)
-    low = (mine_ref[...].astype(F32) + theirs_ref[...].astype(F32)).astype(BF16).T
+    low = functools.reduce(jnp.add, [ref[...].astype(F32) for ref in kept_refs]).astype(BF16).T
     deltas = []
     for k in range(share):
         turned = rotate(piece_ref[k, :, features:].astype(F32), signs, matrix_ref[...])
@@ -253,16 +248,16 @@
     out_ref[...] = result.astype(BF16)
 
 
-def final(mine, theirs, pick, piece, bits, matrix, rest):
+def final(kept, pick, piece, bits, matrix, rest):
     return pl.pallas_call(
         final_kernel,
-        in_specs=[VMEM] * 7,
+        in_specs=[VMEM] * (5 + len(kept)),
         out_specs=VMEM,
         out_shape=jax.ShapeDtypeStruct(rest.shape, BF16),
         compiler_params=params(32),
         cost_estimate=COST,
         name="final",
-    )(mine, theirs, pick, piece, bits, matrix, rest)
+    )(pick, piece, bits, matrix, rest, *kept)
 
 
 def local(tokens, adapter_ids, base_weight, channel_scale, adapter_down, adapter_up, sign_bits):
@@ -276,9 +271,9 @@
     down = jnp.swapaxes(adapter_down, 1, 2)
 
     start = lax.axis_index("grp") * share
-    own = lax.dynamic_slice_in_dim(down, start, share, 0)
+    own = jnp.concatenate([lax.dynamic_slice_in_dim(a, start, share, 0) for a in (down, adapter_up)], axis=2)
     near = swap(own, "adp", 1)
-    mine = [(0, jnp.concatenate([own, lax.dynamic_slice_in_dim(adapter_up, start, share, 0)], axis=2))]
+    mine = [(0, own)]
     bit = planes // 2
     while bit > 1:
         mine += [(plane | bit, swap(piece, "adp", bit)) for plane, piece in mine]
@@ -324,8 +319,6 @@
 
     rest = held[len(mine) :]
     low = more(low, swapped[1:-1] + rest, BF16, lasting(5))
-    low, up = together(low, adapter_up)
-    near_up = swap(up, "adp", 1)
     low, other = both(low)
 
     sums = [[block, pair] for block, pair in zip(blocks[half:], came)]
@@ -335,18 +328,18 @@
         sums = [terms + [pair] for terms, pair in zip(sums[0::2], came)]
         bit *= 2
 
-    far = [one for one in held + swapped[:-1] if one[0] > 1]
+    far = held + swapped[:-1]
     named = [("plane", 0, k) for k in range(here)]
     named += [(plane, off, k) for plane, off, _ in far for k in range(share)]
     ups = [(0, k, 0) for k in range(here)] + [(1 + i, k, features) for i in range(len(far)) for k in range(share)]
-    named += [("plane", 1, k) for k in range(here)]
     arrays = [adapter_up] + [piece for *_, piece in far]
     up, mask = rotated_ups(ids, bits, matrix, here, share, named, ups, arrays, width)
 
-    piece, up, mask, near_up = together(last[2], up, mask, near_up)
-    kept, more_kept = both(compact(tokens, piece, pick))
-    rest = most(low, other, up, mask, near_up, scale, bits, matrix, sums[0])
-    return final(kept, more_kept, pick, piece, bits, matrix, rest)
+    piece, up, mask = together(last[2], up, mask)
+    kept = compact(tokens, piece, pick)
+    kept = [kept] + [swap(kept, "tp", offset) for offset in range(1, parts)]
+    rest = most(low, other, up, mask, scale, bits, matrix, sums[0])
+    return final(kept, pick, piece, bits, matrix, rest)
 
 
 def solution(mesh):

time: 43.7 us -> 46.6 us (1.066)
  waiting for transfers between devices: 10.4 us -> 13.8 us
  starting transfers between devices: 16.5 us -> 16 us
    ppermute x14, waiting for transfers between devices: 10.4 us -> 13.8 us  [swap(): lax.ppermute(x, axis, [(i, i ^ bit) for i in range(lax.axis_size(axis))])]
    ppermute x14, starting transfers between devices: 16.5 us -> 16 us  [swap(): lax.ppermute(x, axis, [(i, i ^ bit) for i in range(lax.axis_size(axis))])]
  transfers between devices with their start and end apart: 14 -> 14, of which waited for: 8 -> 7; matrix products, arithmetic and copies ran while one was open for 2% -> 0% of each run, Pallas kernels for 21% -> 20%
where the time goes in v14:
time: 46.6 us; the launch traced here: 46.3 us
  starting transfers between devices  16 us (34%)
  waiting for transfers between devices  13.8 us (30%)
  Pallas kernels  10.5 us (23%)
  local copies, waits for them, and re-layouts  5.85 us (13%)
    ppermute x14, starting transfers between devices, swap(): lax.ppermute(x, axis, [(i, i ^ bit) for i in range(lax.axis_size(axis))])  16 us
    ppermute x14, waiting for transfers between devices, swap(): lax.ppermute(x, axis, [(i, i ^ bit) for i in range(lax.axis_size(axis))])  13.8 us
    unnamed x18, local copies, waits for them, and re-layouts  4.12 us
    pallas_call x2, Pallas kernels, partials(): pl.pallas_call(functools.partial(partial_kernel, offsets, parts), in_spec...  3.67 us
    pallas_call x2, Pallas kernels, low_rows(): pl.pallas_call(functools.partial(low_kernel, groups, here, share, rank, b...  2.41 us
    dynamic_slice x2, local copies, waits for them, and re-layouts, local(): lax.dynamic_slice_in_dim(a, start, share, 0)  1.73 us
    pallas_call x1, Pallas kernels, final(): pl.pallas_call(final_kernel, in_specs=[VMEM] * (5 + len(kept)), out_specs...  1.35 us
    pallas_call x1, Pallas kernels, compact(): pl.pallas_call(compact_kernel, in_specs=[VMEM] * 3, out_specs=VMEM, out_s...  1.25 us
  transfers between devices with their start and end apart: 14, of which 7 were waited for; matrix products, arithmetic and copies ran while one was open for 0% of the time, Pallas kernels for 20%

profile of v14, /device:TPU:0, one launch (start us, length us, event | category | flops | bytes accessed | tf_op | source)
XLA Modules:
  0.0 46.3 jit_solution(7758899655913640423)
XLA Ops:
  0.0 1.0 %dynamic-slice_bitcast_fusion = bf16[1,64,2048]{2,1,0:T(8,128)(2,1)S(1)} fusion(bf16[2,2048,64]{1,2,0:T(8,128)(2,1)} %param.12, s32[]{:T(128)S(6)} %select_n.4), kind=kLoop, calls=%fused_computation.1 | loop fusion | bytes 524292 | tf_op jit(solution)/shard_map/dynamic_slice | solution.py:274
  1.0 0.8 %constant_dynamic-slice_fusion = bf16[1,64,256]{2,1,0:T(8,128)(2,1)S(1)} fusion(bf16[2,64,256]{2,1,0:T(8,128)(2,1)} %refs_0_.1, s32[]{:T(128)S(6)} %select_n.4), kind=kLoop, calls=%fused_computation.2 | loop fusion | bytes 65540 | tf_op jit(solution)/shard_map/dynamic_slice | solution.py:274
  1.8 3.1 %collective-permute-start = (bf16[1,64,2304]{2,1,0:T(8,128)(2,1)S(1)}, bf16[1,64,2304]{2,1,0:T(8,128)(2,1)S(1)}, u32[]{:S(2)}, u32[]{:S(2)}) collective-permute-start(bf16[1,64,2304]{2,1,0:T(8,128)(2,1)S(1)} %pad_maximum_fusion), channel_id=1, source_target_pairs={{0,4},{4,0},{8,12},{12,8},{1,5},{5,1},{9,13},{13,9},{2,6},{6,2},{1... | collective-permute-start | bytes 884744 | tf_op jit(solution)/shard_map/ppermute | solution.py:38
  4.9 2.6 %collective-permute-start.1 = (bf16[1,64,2304]{2,1,0:T(8,128)(2,1)S(1)}, bf16[1,64,2304]{2,1,0:T(8,128)(2,1)S(1)}, u32[]{:S(2)}, u32[]{:S(2)}) collective-permute-start(bf16[1,64,2304]{2,1,0:T(8,128)(2,1)S(1)} %pad_maximum_fusion), channel_id=1, source_target_pairs={{0,8},{4,12},{8,0},{12,4},{1,9},{5,13},{9,1},{13,5},{2,10},{6,14},... | collective-permute-start | bytes 884744 | tf_op jit(solution)/shard_map/ppermute | solution.py:38
  7.4 1.9 %copy-done = bf16[768,2048]{1,0:T(8,128)(2,1)S(1)} copy-done((bf16[768,2048]{1,0:T(8,128)(2,1)S(1)}, bf16[768,2048]{1,0:T(8,128)(2,1)}, u32[]{:S(2)}) %copy-start) | copy-done | bytes 3145752
  9.3 2.2 %copy-done.2 = bf16[2048,1024]{1,0:T(8,128)(2,1)S(1)} copy-done((bf16[2048,1024]{1,0:T(8,128)(2,1)S(1)}, bf16[2048,1024]{1,0:T(8,128)(2,1)}, u32[]{:S(2)}) %copy-start.2) | copy-done | bytes 4194328
  11.5 2.7 %partials.2 = (bf16[768,256]{1,0:T(8,128)(2,1)S(1)}, bf16[768,256]{1,0:T(8,128)(2,1)S(1)}, bf16[768,256]{1,0:T(8,128)(2,1)S(1)}) custom-call(bf16[768,2048]{1,0:T(8,128)(2,1)S(1)} %copy-done, bf16[2048,1024]{1,0:T(8,128)(2,1)S(1)} %copy-done.2), custom_call_target="tpu_custom_call" | custom-call | flops 4000000000 | bytes 1 | tf_op jit(solution)/shard_map/partials/pallas_call | solution.py:69
  14.2 3.9 %collective-permute-done.refs_0_.refs_1_ = bf16[1,64,2304]{2,1,0:T(8,128)(2,1)S(1)} collective-permute-done((bf16[1,64,2304]{2,1,0:T(8,128)(2,1)S(1)}, bf16[1,64,2304]{2,1,0:T(8,128)(2,1)S(1)}, u32[]{:S(2)}, u32[]{:S(2)}) %collective-permute-start) | collective-permute-done | bytes 294944 | tf_op jit(solution)/shard_map/ppermute | solution.py:38
  18.1 1.7 %collective-permute-start.2 = (bf16[1,64,2304]{2,1,0:T(8,128)(2,1)S(1)}, bf16[1,64,2304]{2,1,0:T(8,128)(2,1)S(1)}, u32[]{:S(2)}, u32[]{:S(2)}) collective-permute-start(bf16[1,64,2304]{2,1,0:T(8,128)(2,1)S(1)} %collective-permute-done.refs_0_.refs_1_), channel_id=1, source_target_pairs={{0,16},{16,0},{1,17},{17,1},{2,18},{18,2},{3,19},{19,3},{4,20},{20... | collective-permute-start | bytes 884744 | tf_op jit(solution)/shard_map/ppermute | solution.py:38
  19.8 0.5 %collective-permute-start.4 = (bf16[768,256]{1,0:T(8,128)(2,1)S(1)}, bf16[768,256]{1,0:T(8,128)(2,1)S(1)}, u32[]{:S(2)}, u32[]{:S(2)}) collective-permute-start(bf16[768,256]{1,0:T(8,128)(2,1)S(1)} %get-tuple-element.28), channel_id=1, source_target_pairs={{0,1},{1,0},{2,3},{3,2},{4,5},{5,4},{6,7},{7,6},{8,9},{9,8},{10,11... | collective-permute-start | bytes 1179656 | tf_op jit(solution)/shard_map/ppermute | solution.py:38
  20.3 1.0 %partials.3.refs_0_ = bf16[768,256]{1,0:T(8,128)(2,1)S(1)} custom-call(bf16[768,2048]{1,0:T(8,128)(2,1)S(1)} %copy-done, bf16[2048,1024]{1,0:T(8,128)(2,1)S(1)} %copy-done.2, bf16[768,256]{1,0:T(8,128)(2,1)S(1)} %get-tuple-element.24.refs_0_), custom_call_target="tpu_custom_call" | custom-call | flops 1 | bytes 1 | tf_op jit(solution)/shard_map/partials/pallas_call | solution.py:69
  21.3 0.1 collective-permute-start.5
  21.4 1.2 %collective-permute-start.7 = (bf16[1,64,2304]{2,1,0:T(8,128)(2,1)S(1)}, bf16[1,64,2304]{2,1,0:T(8,128)(2,1)S(1)}, u32[]{:S(2)}, u32[]{:S(2)}) collective-permute-start(bf16[1,64,2304]{2,1,0:T(8,128)(2,1)S(1)} %collective-permute-done.1.refs_1_.refs_2_), channel_id=1, source_target_pairs={{0,16},{16,0},{1,17},{17,1},{2,18},{18,2},{3,19},{19,3},{4,20},{20... | collective-permute-start | bytes 884744 | tf_op jit(solution)/shard_map/ppermute | solution.py:38
  22.6 0.4 picked.1.pick_ref
  22.9 5.1 %collective-permute-done.2.refs_2_.refs_4_ = bf16[1,64,2304]{2,1,0:T(8,128)(2,1)S(1)} collective-permute-done((bf16[1,64,2304]{2,1,0:T(8,128)(2,1)S(1)}, bf16[1,64,2304]{2,1,0:T(8,128)(2,1)S(1)}, u32[]{:S(2)}, u32[]{:S(2)}) %collective-permute-start.2) | collective-permute-done | bytes 294944 | tf_op jit(solution)/shard_map/ppermute | solution.py:38
  28.0 1.2 %low_rows.2.refs_2_ = f32[64,768]{1,0:T(8,128)S(1)} custom-call(s32[1,768]{1,0:T(1,128)S(1)} %bitcast.8, bf16[768,2048]{1,0:T(8,128)(2,1)S(1)} %copy-done.1, bf16[1,64,2304]{2,1,0:T(8,128)(2,1)S(1)} %collective-permute-done.refs_0_.refs_1_, bf16[1,64,2304]{2,1,0:T(8,128)(2,1)S(1)} %collective-permute-done.1.refs_1_.refs_2_, ...), custom_call_target="tpu_custom_call" | custom-call | flops 2000000000 | bytes 1 | tf_op jit(solution)/shard_map/low_rows/pallas_call | solution.py:124
  29.3 0.1 add.8
  29.4 1.7 %collective-permute-start.10 = (bf16[768,256]{1,0:T(8,128)(2,1)S(1)}, bf16[768,256]{1,0:T(8,128)(2,1)S(1)}, u32[]{:S(2)}, u32[]{:S(2)}) collective-permute-start(bf16[768,256]{1,0:T(8,128)(2,1)S(1)} %add.8), channel_id=1, source_target_pairs={{0,2},{1,3},{2,0},{3,1},{4,6},{5,7},{6,4},{7,5},{8,10},{9,11},{10,... | collective-permute-start | bytes 1179656 | tf_op jit(solution)/shard_map/ppermute | solution.py:38
  31.1 1.5 %collective-permute-start.6 = (bf16[1,64,2304]{2,1,0:T(8,128)(2,1)S(1)}, bf16[1,64,2304]{2,1,0:T(8,128)(2,1)S(1)}, u32[]{:S(2)}, u32[]{:S(2)}) collective-permute-start(bf16[1,64,2304]{2,1,0:T(8,128)(2,1)S(1)} %collective-permute-done.5.refs_3_.refs_1_), channel_id=1, source_target_pairs={{0,16},{16,0},{1,17},{17,1},{2,18},{18,2},{3,19},{19,3},{4,20},{20... | collective-permute-start | bytes 884744 | tf_op jit(solution)/shard_map/ppermute | solution.py:38
  32.6 0.4 collective-permute-done.7.refs_5_.refs_0_
  33.0 1.2 %low_rows.3.refs_0_ = bf16[64,768]{1,0:T(8,128)(2,1)S(1)} custom-call(s32[1,768]{1,0:T(1,128)S(1)} %bitcast.9, bf16[768,2048]{1,0:T(8,128)(2,1)S(1)} %copy-done.1, bf16[1,64,2304]{2,1,0:T(8,128)(2,1)S(1)} %collective-permute-done.7.refs_5_.refs_0_, bf16[1,64,2304]{2,1,0:T(8,128)(2,1)S(1)} %collective-permute-done.5.refs_3_.refs_1_, ...), custom_call_target="tpu_custom_call" | custom-call | flops 5000000000 | bytes 1 | tf_op jit(solution)/shard_map/low_rows/pallas_call | solution.py:124
  34.3 1.3 %collective-permute-done.8.refs_1_ = bf16[64,768]{1,0:T(8,128)(2,1)S(1)} collective-permute-done((bf16[64,768]{1,0:T(8,128)(2,1)S(1)}, bf16[64,768]{1,0:T(8,128)(2,1)S(1)}, u32[]{:S(2)}, u32[]{:S(2)}) %collective-permute-start.8) | collective-permute-done | bytes 98336 | tf_op jit(solution)/shard_map/ppermute | solution.py:38
  35.6 1.6 %collective-permute-start.9 = (bf16[64,768]{1,0:T(8,128)(2,1)S(1)}, bf16[64,768]{1,0:T(8,128)(2,1)S(1)}, u32[]{:S(2)}, u32[]{:S(2)}) collective-permute-start(bf16[64,768]{1,0:T(8,128)(2,1)S(1)} %add.7.mine_ref), channel_id=1, source_target_pairs={{0,2},{1,3},{2,0},{3,1},{4,6},{5,7},{6,4},{7,5},{8,10},{9,11},{10,... | collective-permute-start | bytes 294920 | tf_op jit(solution)/shard_map/ppermute | solution.py:38
  37.2 0.6 %rotated_ups.1 = (bf16[512,256]{1,0:T(8,128)(2,1)S(1)}, bf16[768,512]{1,0:T(8,128)(2,1)S(1)}) custom-call(s32[1,768]{1,0:T(1,128)S(1)} %bitcast.10, s32[1,128]{1,0:T(1,128)S(1)} %bitcast.11, bf16[128,128]{1,0:T(8,128)(2,1)S(1)} %copy-done.3, bf16[2,64,256]{2,1,0:T(8,128)(2,1)S(1)} %copy-done.4, ...), custom_call_target="tpu_custom_call" | custom-call | flops 1 | bytes 1 | tf_op jit(solution)/shard_map/rotated_ups/pallas_call | solution.py:153
  37.8 1.1 %collective-permute-done.6.piece_ref = bf16[1,64,2304]{2,1,0:T(8,128)(2,1)S(1)} collective-permute-done((bf16[1,64,2304]{2,1,0:T(8,128)(2,1)S(1)}, bf16[1,64,2304]{2,1,0:T(8,128)(2,1)S(1)}, u32[]{:S(2)}, u32[]{:S(2)}) %collective-permute-start.6) | collective-permute-done | bytes 294944 | tf_op jit(solution)/shard_map/ppermute | solution.py:38
  38.9 1.2 %compact.1.refs_0_ = bf16[64,256]{1,0:T(8,128)(2,1)S(1)} custom-call(bf16[768,2048]{1,0:T(8,128)(2,1)S(1)} %copy-done.1, bf16[1,64,2304]{2,1,0:T(8,128)(2,1)S(1)} %collective-permute-done.6.piece_ref, bf16[768,256]{1,0:T(8,128)(2,1)S(1)} %picked.1.pick_ref), custom_call_target="tpu_custom_call" | custom-call | flops 1 | bytes 1 | tf_op jit(solution)/shard_map/compact/pallas_call | solution.py:202
  40.2 1.4 %collective-permute-start.12 = (bf16[64,256]{1,0:T(8,128)(2,1)S(1)}, bf16[64,256]{1,0:T(8,128)(2,1)S(1)}, u32[]{:S(2)}, u32[]{:S(2)}) collective-permute-start(bf16[64,256]{1,0:T(8,128)(2,1)S(1)} %compact.1.refs_0_), channel_id=1, source_target_pairs={{0,2},{1,3},{2,0},{3,1},{4,6},{5,7},{6,4},{7,5},{8,10},{9,11},{10,... | collective-permute-start | bytes 98312 | tf_op jit(solution)/shard_map/ppermute | solution.py:38
  41.6 0.5 collective-permute-start.13
  42.1 0.8 %most.1.most_ref = f32[768,256]{1,0:T(8,128)S(1)} custom-call(bf16[64,768]{1,0:T(8,128)(2,1)S(1)} %add.7.mine_ref, bf16[64,768]{1,0:T(8,128)(2,1)S(1)} %collective-permute-done.9.theirs_ref, bf16[512,256]{1,0:T(8,128)(2,1)S(1)} %get-tuple-element.34.up_ref, bf16[768,512]{1,0:T(8,128)(2,1)S(1)} %get-tuple-element.35.mask_ref, f32[1,256]{1,0:T(1,128)S(1)} %bitcast.14, ...), custom_call_target="tpu_custom_call" | custom-call | flops 1 | bytes 1 | tf_op jit(solution)/shard_map/most/pallas_call | solution.py:224
  42.9 1.3 %collective-permute-done.12.refs_2_ = bf16[64,256]{1,0:T(8,128)(2,1)S(1)} collective-permute-done((bf16[64,256]{1,0:T(8,128)(2,1)S(1)}, bf16[64,256]{1,0:T(8,128)(2,1)S(1)}, u32[]{:S(2)}, u32[]{:S(2)}) %collective-permute-start.12) | collective-permute-done | bytes 32800 | tf_op jit(solution)/shard_map/ppermute | solution.py:38
  44.2 0.8 %collective-permute-done.13.refs_3_ = bf16[64,256]{1,0:T(8,128)(2,1)S(1)} collective-permute-done((bf16[64,256]{1,0:T(8,128)(2,1)S(1)}, bf16[64,256]{1,0:T(8,128)(2,1)S(1)}, u32[]{:S(2)}, u32[]{:S(2)}) %collective-permute-start.13) | collective-permute-done | bytes 32800 | tf_op jit(solution)/shard_map/ppermute | solution.py:38
  45.0 1.4 %final.1 = bf16[768,256]{1,0:T(8,128)(2,1)} custom-call(bf16[768,256]{1,0:T(8,128)(2,1)S(1)} %picked.1.pick_ref, bf16[1,64,2304]{2,1,0:T(8,128)(2,1)S(1)} %collective-permute-done.6.piece_ref, s32[1,128]{1,0:T(1,128)S(1)} %bitcast.13, bf16[128,128]{1,0:T(8,128)(2,1)S(1)} %copy-done.3, f32[768,256]{1,0:T(8,128)S(1)} %most.1.most_ref, ...), custom_call_target="tpu_custom_call" | custom-call | flops 1 | bytes 1 | tf_op jit(solution)/shard_map/final/pallas_call | solution.py:252
  (28 shorter events, 0.3 us)
Async XLA Ops:
  1.8 16.3 %collective-permute-start = (bf16[1,64,2304]{2,1,0:T(8,128)(2,1)S(1)}, bf16[1,64,2304]{2,1,0:T(8,128)(2,1)S(1)}, u32[]{:S(2)}, u32[]{:S(2)}) collective-permute-start(bf16[1,64,2304]{2,1,0:T(8,128)(2,1)S(1)} %pad_maximum_fusion), channel_id=1, source_target_pairs={{0,4},{4,0},{8,12},{12,8},{1,5},{5,1},{9,13},{13,9},{2,6},{6,2},{1... | collective-permute-start | bytes 884744 | tf_op jit(solution)/shard_map/ppermute | solution.py:38
  4.9 16.4 %collective-permute-start.1 = (bf16[1,64,2304]{2,1,0:T(8,128)(2,1)S(1)}, bf16[1,64,2304]{2,1,0:T(8,128)(2,1)S(1)}, u32[]{:S(2)}, u32[]{:S(2)}) collective-permute-start(bf16[1,64,2304]{2,1,0:T(8,128)(2,1)S(1)} %pad_maximum_fusion), channel_id=1, source_target_pairs={{0,8},{4,12},{8,0},{12,4},{1,9},{5,13},{9,1},{13,5},{2,10},{6,14},... | collective-permute-start | bytes 884744 | tf_op jit(solution)/shard_map/ppermute | solution.py:38
  7.4 1.9 %copy-start = (bf16[768,2048]{1,0:T(8,128)(2,1)S(1)}, bf16[768,2048]{1,0:T(8,128)(2,1)}, u32[]{:S(2)}) copy-start(bf16[768,2048]{1,0:T(8,128)(2,1)} %tokens_ref.9) | copy-start | bytes 9437188
  9.3 2.2 %copy-start.2 = (bf16[2048,1024]{1,0:T(8,128)(2,1)S(1)}, bf16[2048,1024]{1,0:T(8,128)(2,1)}, u32[]{:S(2)}) copy-start(bf16[2048,1024]{1,0:T(8,128)(2,1)} %weight_ref.3) | copy-start | bytes 12582916
  14.2 8.4 %copy-start.6 = (s32[768,1]{0,1:T(1,128)S(1)}, s32[768,1]{0,1:T(1,128)}, u32[]{:S(2)}) copy-start(s32[768,1]{0,1:T(1,128)} %param.9) | copy-start | bytes 9220
  18.1 9.9 %collective-permute-start.2 = (bf16[1,64,2304]{2,1,0:T(8,128)(2,1)S(1)}, bf16[1,64,2304]{2,1,0:T(8,128)(2,1)S(1)}, u32[]{:S(2)}, u32[]{:S(2)}) collective-permute-start(bf16[1,64,2304]{2,1,0:T(8,128)(2,1)S(1)} %collective-permute-done.refs_0_.refs_1_), channel_id=1, source_target_pairs={{0,16},{16,0},{1,17},{17,1},{2,18},{18,2},{3,19},{19,3},{4,20},{20... | collective-permute-start | bytes 884744 | tf_op jit(solution)/shard_map/ppermute | solution.py:38
  19.7 9.5 %collective-permute-start.3 = (bf16[768,256]{1,0:T(8,128)(2,1)S(1)}, bf16[768,256]{1,0:T(8,128)(2,1)S(1)}, u32[]{:S(2)}, u32[]{:S(2)}) collective-permute-start(bf16[768,256]{1,0:T(8,128)(2,1)S(1)} %get-tuple-element.27), channel_id=1, source_target_pairs={{0,1},{1,0},{2,3},{3,2},{4,5},{5,4},{6,7},{7,6},{8,9},{9,8},{10,11... | collective-permute-start | bytes 1179656 | tf_op jit(solution)/shard_map/ppermute | solution.py:38
  19.8 8.3 %copy-start.1 = (bf16[768,2048]{1,0:T(8,128)(2,1)S(1)}, bf16[768,2048]{1,0:T(8,128)(2,1)}, u32[]{:S(2)}) copy-start(bf16[768,2048]{1,0:T(8,128)(2,1)} %tokens_ref.9) | copy-start | bytes 9437188
  19.8 8.3 %copy-start.5 = (bf16[2,2048,64]{1,2,0:T(8,128)(2,1)S(1)}, bf16[2,2048,64]{1,2,0:T(8,128)(2,1)}, u32[]{:S(2)}) copy-start(bf16[2,2048,64]{1,2,0:T(8,128)(2,1)} %param.12) | copy-start | bytes 1572868
  19.8 9.5 %collective-permute-start.4 = (bf16[768,256]{1,0:T(8,128)(2,1)S(1)}, bf16[768,256]{1,0:T(8,128)(2,1)S(1)}, u32[]{:S(2)}, u32[]{:S(2)}) collective-permute-start(bf16[768,256]{1,0:T(8,128)(2,1)S(1)} %get-tuple-element.28), channel_id=1, source_target_pairs={{0,1},{1,0},{2,3},{3,2},{4,5},{5,4},{6,7},{7,6},{8,9},{9,8},{10,11... | collective-permute-start | bytes 1179656 | tf_op jit(solution)/shard_map/ppermute | solution.py:38
  21.3 9.8 %collective-permute-start.5 = (bf16[1,64,2304]{2,1,0:T(8,128)(2,1)S(1)}, bf16[1,64,2304]{2,1,0:T(8,128)(2,1)S(1)}, u32[]{:S(2)}, u32[]{:S(2)}) collective-permute-start(bf16[1,64,2304]{2,1,0:T(8,128)(2,1)S(1)} %collective-permute-done.1.refs_1_.refs_2_), channel_id=1, source_target_pairs={{0,4},{4,0},{8,12},{12,8},{1,5},{5,1},{9,13},{13,9},{2,6},{6,2},{1... | collective-permute-start | bytes 884744 | tf_op jit(solution)/shard_map/ppermute | solution.py:38
  21.4 11.7 %collective-permute-start.7 = (bf16[1,64,2304]{2,1,0:T(8,128)(2,1)S(1)}, bf16[1,64,2304]{2,1,0:T(8,128)(2,1)S(1)}, u32[]{:S(2)}, u32[]{:S(2)}) collective-permute-start(bf16[1,64,2304]{2,1,0:T(8,128)(2,1)S(1)} %collective-permute-done.1.refs_1_.refs_2_), channel_id=1, source_target_pairs={{0,16},{16,0},{1,17},{17,1},{2,18},{18,2},{3,19},{19,3},{4,20},{20... | collective-permute-start | bytes 884744 | tf_op jit(solution)/shard_map/ppermute | solution.py:38
  29.4 7.9 %copy-start.3 = (bf16[128,128]{1,0:T(8,128)(2,1)S(1)}, bf16[128,128]{1,0:T(8,128)(2,1)}, u32[]{:S(2)}) copy-start(bf16[128,128]{1,0:T(8,128)(2,1)} %constant.12.clone.matrix_ref) | copy-start | bytes 98308
  29.4 7.9 %copy-start.4 = (bf16[2,64,256]{2,1,0:T(8,128)(2,1)S(1)}, bf16[2,64,256]{2,1,0:T(8,128)(2,1)}, u32[]{:S(2)}) copy-start(bf16[2,64,256]{2,1,0:T(8,128)(2,1)} %refs_0_.1) | copy-start | bytes 196612
  29.4 7.9 %copy-start.7 = (s32[128]{0:T(128)S(1)}, s32[128]{0:T(128)}, u32[]{:S(2)}) copy-start(s32[128]{0:T(128)} %param.14) | copy-start | bytes 1540
  29.4 12.7 %collective-permute-start.10 = (bf16[768,256]{1,0:T(8,128)(2,1)S(1)}, bf16[768,256]{1,0:T(8,128)(2,1)S(1)}, u32[]{:S(2)}, u32[]{:S(2)}) collective-permute-start(bf16[768,256]{1,0:T(8,128)(2,1)S(1)} %add.8), channel_id=1, source_target_pairs={{0,2},{1,3},{2,0},{3,1},{4,6},{5,7},{6,4},{7,5},{8,10},{9,11},{10,... | collective-permute-start | bytes 1179656 | tf_op jit(solution)/shard_map/ppermute | solution.py:38
  31.1 7.8 %collective-permute-start.6 = (bf16[1,64,2304]{2,1,0:T(8,128)(2,1)S(1)}, bf16[1,64,2304]{2,1,0:T(8,128)(2,1)S(1)}, u32[]{:S(2)}, u32[]{:S(2)}) collective-permute-start(bf16[1,64,2304]{2,1,0:T(8,128)(2,1)S(1)} %collective-permute-done.5.refs_3_.refs_1_), channel_id=1, source_target_pairs={{0,16},{16,0},{1,17},{17,1},{2,18},{18,2},{3,19},{19,3},{4,20},{20... | collective-permute-start | bytes 884744 | tf_op jit(solution)/shard_map/ppermute | solution.py:38
  34.2 7.9 %copy-start.8 = (f32[256]{0:T(256)S(1)}, f32[256]{0:T(256)}, u32[]{:S(2)}) copy-start(f32[256]{0:T(256)} %param.11) | copy-start | bytes 3076
  34.3 1.4 %collective-permute-start.8 = (bf16[64,768]{1,0:T(8,128)(2,1)S(1)}, bf16[64,768]{1,0:T(8,128)(2,1)S(1)}, u32[]{:S(2)}, u32[]{:S(2)}) collective-permute-start(bf16[64,768]{1,0:T(8,128)(2,1)S(1)} %low_rows.3.refs_0_), channel_id=1, source_target_pairs={{0,1},{1,0},{2,3},{3,2},{4,5},{5,4},{6,7},{7,6},{8,9},{9,8},{10,11... | collective-permute-start | bytes 294920 | tf_op jit(solution)/shard_map/ppermute | solution.py:38
  35.6 6.4 %collective-permute-start.9 = (bf16[64,768]{1,0:T(8,128)(2,1)S(1)}, bf16[64,768]{1,0:T(8,128)(2,1)S(1)}, u32[]{:S(2)}, u32[]{:S(2)}) collective-permute-start(bf16[64,768]{1,0:T(8,128)(2,1)S(1)} %add.7.mine_ref), channel_id=1, source_target_pairs={{0,2},{1,3},{2,0},{3,1},{4,6},{5,7},{6,4},{7,5},{8,10},{9,11},{10,... | collective-permute-start | bytes 294920 | tf_op jit(solution)/shard_map/ppermute | solution.py:38
  40.2 2.7 %collective-permute-start.11 = (bf16[64,256]{1,0:T(8,128)(2,1)S(1)}, bf16[64,256]{1,0:T(8,128)(2,1)S(1)}, u32[]{:S(2)}, u32[]{:S(2)}) collective-permute-start(bf16[64,256]{1,0:T(8,128)(2,1)S(1)} %compact.1.refs_0_), channel_id=1, source_target_pairs={{0,1},{1,0},{2,3},{3,2},{4,5},{5,4},{6,7},{7,6},{8,9},{9,8},{10,11... | collective-permute-start | bytes 98312 | tf_op jit(solution)/shard_map/ppermute | solution.py:38
  40.2 4.0 %collective-permute-start.12 = (bf16[64,256]{1,0:T(8,128)(2,1)S(1)}, bf16[64,256]{1,0:T(8,128)(2,1)S(1)}, u32[]{:S(2)}, u32[]{:S(2)}) collective-permute-start(bf16[64,256]{1,0:T(8,128)(2,1)S(1)} %compact.1.refs_0_), channel_id=1, source_target_pairs={{0,2},{1,3},{2,0},{3,1},{4,6},{5,7},{6,4},{7,5},{8,10},{9,11},{10,... | collective-permute-start | bytes 98312 | tf_op jit(solution)/shard_map/ppermute | solution.py:38
  41.6 3.3 %collective-permute-start.13 = (bf16[64,256]{1,0:T(8,128)(2,1)S(1)}, bf16[64,256]{1,0:T(8,128)(2,1)S(1)}, u32[]{:S(2)}, u32[]{:S(2)}) collective-permute-start(bf16[64,256]{1,0:T(8,128)(2,1)S(1)} %compact.1.refs_0_), channel_id=1, source_target_pairs={{0,3},{1,2},{2,1},{3,0},{4,7},{5,6},{6,5},{7,4},{8,11},{9,10},{10,... | collective-permute-start | bytes 98312 | tf_op jit(solution)/shard_map/ppermute | solution.py:38

commit v15 on v14

--- a/solution.py
+++ b/solution.py
@@ -271,9 +271,9 @@
     down = jnp.swapaxes(adapter_down, 1, 2)
 
     start = lax.axis_index("grp") * share
-    own = jnp.concatenate([lax.dynamic_slice_in_dim(a, start, share, 0) for a in (down, adapter_up)], axis=2)
+    own = lax.dynamic_slice_in_dim(down, start, share, 0)
     near = swap(own, "adp", 1)
-    mine = [(0, own)]
+    mine = [(0, jnp.concatenate([own, lax.dynamic_slice_in_dim(adapter_up, start, share, 0)], axis=2))]
     bit = planes // 2
     while bit > 1:
         mine += [(plane | bit, swap(piece, "adp", bit)) for plane, piece in mine]
@@ -281,9 +281,9 @@
     half = parts // 2
     offsets = (*range(1, parts, 2), *range(2, parts, 2))
     blocks = list(partials(tokens, base_weight, parts, offsets, lasting(4)))
-    near, blocks[-1] = together(near, blocks[-1])
+    near, blocks[-1], up = together(near, blocks[-1], adapter_up)
     (block,) = partials(tokens, base_weight, parts, (0,), COST, blocks[-1])
-    close, block, *far = together(near, block, *(piece for _, piece in mine[1:]))
+    close, block, near_up, *far = together(near, block, swap(up, "adp", 1), *(piece for _, piece in mine[1:]))
     blocks = blocks[:half] + [block] + blocks[half:]
     mine = mine[:1] + [(plane, piece) for (plane, _), piece in zip(mine[1:], far)]
     odd = [(1, near)] + [(plane | 1, swap(piece, "adp", 1)) for plane, piece in mine[1:]]
@@ -328,11 +328,13 @@
         sums = [terms + [pair] for terms, pair in zip(sums[0::2], came)]
         bit *= 2
 
-    far = held + swapped[:-1]
+    far = [one for one in held + swapped[:-1] if one[0] > 1]
     named = [("plane", 0, k) for k in range(here)]
     named += [(plane, off, k) for plane, off, _ in far for k in range(share)]
     ups = [(0, k, 0) for k in range(here)] + [(1 + i, k, features) for i in range(len(far)) for k in range(share)]
-    arrays = [adapter_up] + [piece for *_, piece in far]
+    named += [("plane", 1, k) for k in range(here)]
+    ups += [(1 + len(far), k, 0) for k in range(here)]
+    arrays = [adapter_up] + [piece for *_, piece in far] + [near_up]
     up, mask = rotated_ups(ids, bits, matrix, here, share, named, ups, arrays, width)
 
     piece, up, mask = together(last[2], up, mask)

time: 46.6 us -> 45.9 us (0.985)
  waiting for transfers between devices: 13.8 us -> 13.3 us
    ppermute x14 -> x15, waiting for transfers between devices: 13.8 us -> 13.3 us  [swap(): lax.ppermute(x, axis, [(i, i ^ bit) for i in range(lax.axis_size(axis))])]
    ppermute x14 -> x15, starting transfers between devices: 16 us -> 15.8 us  [swap(): lax.ppermute(x, axis, [(i, i ^ bit) for i in range(lax.axis_size(axis))])]
  transfers between devices with their start and end apart: 14 -> 15, of which waited for: 7 -> 8; matrix products, arithmetic and copies ran while one was open for 0% -> 2% of each run, Pallas kernels for 20% -> 20%
where the time goes in v15:
time: 45.9 us; the launch traced here: 45.7 us
  starting transfers between devices  15.8 us (34%)
  waiting for transfers between devices  13.3 us (29%)
  Pallas kernels  10.5 us (23%)
  local copies, waits for them, and re-layouts  5.84 us (13%)
    ppermute x15, starting transfers between devices, swap(): lax.ppermute(x, axis, [(i, i ^ bit) for i in range(lax.axis_size(axis))])  15.8 us
    ppermute x15, waiting for transfers between devices, swap(): lax.ppermute(x, axis, [(i, i ^ bit) for i in range(lax.axis_size(axis))])  13.3 us
    unnamed x18, local copies, waits for them, and re-layouts  4.11 us
    pallas_call x2, Pallas kernels, partials(): pl.pallas_call(functools.partial(partial_kernel, offsets, parts), in_spec...  3.66 us
    pallas_call x2, Pallas kernels, low_rows(): pl.pallas_call(functools.partial(low_kernel, groups, here, share, rank, b...  2.4 us
    pallas_call x1, Pallas kernels, final(): pl.pallas_call(final_kernel, in_specs=[VMEM] * (5 + len(kept)), out_specs...  1.35 us
    pallas_call x1, Pallas kernels, compact(): pl.pallas_call(compact_kernel, in_specs=[VMEM] * 3, out_specs=VMEM, out_s...  1.25 us
    dynamic_slice x1, local copies, waits for them, and re-layouts, local(): own = lax.dynamic_slice_in_dim(down, start, share, 0)  0.97 us
  transfers between devices with their start and end apart: 15, of which 8 were waited for; matrix products, arithmetic and copies ran while one was open for 2% of the time, Pallas kernels for 20%

profile of v15, /device:TPU:0, one launch (start us, length us, event | category | flops | bytes accessed | tf_op | source)
XLA Modules:
  0.0 45.7 jit_solution(14699972465447187912)
XLA Ops:
  0.0 1.0 %dynamic-slice_bitcast_fusion = bf16[1,64,2048]{2,1,0:T(8,128)(2,1)S(1)} fusion(bf16[2,2048,64]{1,2,0:T(8,128)(2,1)} %param.12, s32[]{:T(128)S(6)} %select_n.4), kind=kLoop, calls=%fused_computation.1 | loop fusion | bytes 524292 | tf_op jit(solution)/shard_map/dynamic_slice | solution.py:274
  1.0 3.1 %collective-permute-start = (bf16[1,64,2048]{2,1,0:T(8,128)(2,1)S(1)}, bf16[1,64,2048]{2,1,0:T(8,128)(2,1)S(1)}, u32[]{:S(2)}, u32[]{:S(2)}) collective-permute-start(bf16[1,64,2048]{2,1,0:T(8,128)(2,1)S(1)} %dynamic-slice_bitcast_fusion), channel_id=1, source_target_pairs={{0,4},{4,0},{8,12},{12,8},{1,5},{5,1},{9,13},{13,9},{2,6},{6,2},{1... | collective-permute-start | bytes 786440 | tf_op jit(solution)/shard_map/ppermute | solution.py:38
  4.1 0.8 %constant_dynamic-slice_fusion = bf16[1,64,256]{2,1,0:T(8,128)(2,1)S(1)} fusion(bf16[2,64,256]{2,1,0:T(8,128)(2,1)} %refs_0_.1, s32[]{:T(128)S(6)} %select_n.4), kind=kLoop, calls=%fused_computation.2 | loop fusion | bytes 65540 | tf_op jit(solution)/shard_map/dynamic_slice | solution.py:276
  4.8 2.7 %collective-permute-start.2 = (bf16[1,64,2304]{2,1,0:T(8,128)(2,1)S(1)}, bf16[1,64,2304]{2,1,0:T(8,128)(2,1)S(1)}, u32[]{:S(2)}, u32[]{:S(2)}) collective-permute-start(bf16[1,64,2304]{2,1,0:T(8,128)(2,1)S(1)} %pad_maximum_fusion), channel_id=1, source_target_pairs={{0,8},{4,12},{8,0},{12,4},{1,9},{5,13},{9,1},{13,5},{2,10},{6,14},... | collective-permute-start | bytes 884744 | tf_op jit(solution)/shard_map/ppermute | solution.py:38
  7.5 1.9 %copy-done = bf16[768,2048]{1,0:T(8,128)(2,1)S(1)} copy-done((bf16[768,2048]{1,0:T(8,128)(2,1)S(1)}, bf16[768,2048]{1,0:T(8,128)(2,1)}, u32[]{:S(2)}) %copy-start) | copy-done | bytes 3145752
  9.4 2.2 %copy-done.2 = bf16[2048,1024]{1,0:T(8,128)(2,1)S(1)} copy-done((bf16[2048,1024]{1,0:T(8,128)(2,1)S(1)}, bf16[2048,1024]{1,0:T(8,128)(2,1)}, u32[]{:S(2)}) %copy-start.2) | copy-done | bytes 4194328
  11.6 2.7 %partials.2 = (bf16[768,256]{1,0:T(8,128)(2,1)S(1)}, bf16[768,256]{1,0:T(8,128)(2,1)S(1)}, bf16[768,256]{1,0:T(8,128)(2,1)S(1)}) custom-call(bf16[768,2048]{1,0:T(8,128)(2,1)S(1)} %copy-done, bf16[2048,1024]{1,0:T(8,128)(2,1)S(1)} %copy-done.2), custom_call_target="tpu_custom_call" | custom-call | flops 4000000000 | bytes 1 | tf_op jit(solution)/shard_map/partials/pallas_call | solution.py:69
  14.3 0.8 %collective-permute-done.refs_0_ = bf16[1,64,2048]{2,1,0:T(8,128)(2,1)S(1)} collective-permute-done((bf16[1,64,2048]{2,1,0:T(8,128)(2,1)S(1)}, bf16[1,64,2048]{2,1,0:T(8,128)(2,1)S(1)}, u32[]{:S(2)}, u32[]{:S(2)}) %collective-permute-start) | collective-permute-done | bytes 262176 | tf_op jit(solution)/shard_map/ppermute | solution.py:38
  15.0 1.7 %collective-permute-start.3 = (bf16[1,64,2048]{2,1,0:T(8,128)(2,1)S(1)}, bf16[1,64,2048]{2,1,0:T(8,128)(2,1)S(1)}, u32[]{:S(2)}, u32[]{:S(2)}) collective-permute-start(bf16[1,64,2048]{2,1,0:T(8,128)(2,1)S(1)} %collective-permute-done.refs_0_), channel_id=1, source_target_pairs={{0,16},{16,0},{1,17},{17,1},{2,18},{18,2},{3,19},{19,3},{4,20},{20... | collective-permute-start | bytes 786440 | tf_op jit(solution)/shard_map/ppermute | solution.py:38
  16.7 0.5 %collective-permute-start.5 = (bf16[768,256]{1,0:T(8,128)(2,1)S(1)}, bf16[768,256]{1,0:T(8,128)(2,1)S(1)}, u32[]{:S(2)}, u32[]{:S(2)}) collective-permute-start(bf16[768,256]{1,0:T(8,128)(2,1)S(1)} %get-tuple-element.31), channel_id=1, source_target_pairs={{0,1},{1,0},{2,3},{3,2},{4,5},{5,4},{6,7},{7,6},{8,9},{9,8},{10,11... | collective-permute-start | bytes 1179656 | tf_op jit(solution)/shard_map/ppermute | solution.py:38
  17.2 1.0 %partials.3.refs_0_ = bf16[768,256]{1,0:T(8,128)(2,1)S(1)} custom-call(bf16[768,2048]{1,0:T(8,128)(2,1)S(1)} %copy-done, bf16[2048,1024]{1,0:T(8,128)(2,1)S(1)} %copy-done.2, bf16[768,256]{1,0:T(8,128)(2,1)S(1)} %get-tuple-element.26.refs_0_), custom_call_target="tpu_custom_call" | custom-call | flops 1 | bytes 1 | tf_op jit(solution)/shard_map/partials/pallas_call | solution.py:69
  18.2 2.5 %collective-permute-done.2.refs_1_ = bf16[1,64,2304]{2,1,0:T(8,128)(2,1)S(1)} collective-permute-done((bf16[1,64,2304]{2,1,0:T(8,128)(2,1)S(1)}, bf16[1,64,2304]{2,1,0:T(8,128)(2,1)S(1)}, u32[]{:S(2)}, u32[]{:S(2)}) %collective-permute-start.2) | collective-permute-done | bytes 294944 | tf_op jit(solution)/shard_map/ppermute | solution.py:38
  20.7 1.3 %collective-permute-done.1.refs_4_ = bf16[2,64,256]{2,1,0:T(8,128)(2,1)S(1)} collective-permute-done((bf16[2,64,256]{2,1,0:T(8,128)(2,1)S(1)}, bf16[2,64,256]{2,1,0:T(8,128)(2,1)S(1)}, u32[]{:S(2)}, u32[]{:S(2)}) %collective-permute-start.1) | collective-permute-done | bytes 65568 | tf_op jit(solution)/shard_map/ppermute | solution.py:38
  22.0 1.3 %collective-permute-start.8 = (bf16[1,64,2304]{2,1,0:T(8,128)(2,1)S(1)}, bf16[1,64,2304]{2,1,0:T(8,128)(2,1)S(1)}, u32[]{:S(2)}, u32[]{:S(2)}) collective-permute-start(bf16[1,64,2304]{2,1,0:T(8,128)(2,1)S(1)} %collective-permute-done.2.refs_1_), channel_id=1, source_target_pairs={{0,16},{16,0},{1,17},{17,1},{2,18},{18,2},{3,19},{19,3},{4,20},{20... | collective-permute-start | bytes 884744 | tf_op jit(solution)/shard_map/ppermute | solution.py:38
  23.3 0.4 picked.1.pick_ref
  23.7 1.2 %low_rows.2.refs_2_ = f32[64,768]{1,0:T(8,128)S(1)} custom-call(s32[1,768]{1,0:T(1,128)S(1)} %bitcast.8, bf16[768,2048]{1,0:T(8,128)(2,1)S(1)} %copy-done.1, bf16[1,64,2048]{2,1,0:T(8,128)(2,1)S(1)} %collective-permute-done.refs_0_, bf16[1,64,2304]{2,1,0:T(8,128)(2,1)S(1)} %collective-permute-done.2.refs_1_, ...), custom_call_target="tpu_custom_call" | custom-call | flops 2000000000 | bytes 1 | tf_op jit(solution)/shard_map/low_rows/pallas_call | solution.py:124
  25.0 0.1 add.8
  25.1 1.7 %collective-permute-start.11 = (bf16[768,256]{1,0:T(8,128)(2,1)S(1)}, bf16[768,256]{1,0:T(8,128)(2,1)S(1)}, u32[]{:S(2)}, u32[]{:S(2)}) collective-permute-start(bf16[768,256]{1,0:T(8,128)(2,1)S(1)} %add.8), channel_id=1, source_target_pairs={{0,2},{1,3},{2,0},{3,1},{4,6},{5,7},{6,4},{7,5},{8,10},{9,11},{10,... | collective-permute-start | bytes 1179656 | tf_op jit(solution)/shard_map/ppermute | solution.py:38
  26.8 4.1 %collective-permute-done.6.refs_2_.refs_1_ = bf16[1,64,2304]{2,1,0:T(8,128)(2,1)S(1)} collective-permute-done((bf16[1,64,2304]{2,1,0:T(8,128)(2,1)S(1)}, bf16[1,64,2304]{2,1,0:T(8,128)(2,1)S(1)}, u32[]{:S(2)}, u32[]{:S(2)}) %collective-permute-start.6) | collective-permute-done | bytes 294944 | tf_op jit(solution)/shard_map/ppermute | solution.py:38
  30.9 1.1 %collective-permute-start.7 = (bf16[1,64,2304]{2,1,0:T(8,128)(2,1)S(1)}, bf16[1,64,2304]{2,1,0:T(8,128)(2,1)S(1)}, u32[]{:S(2)}, u32[]{:S(2)}) collective-permute-start(bf16[1,64,2304]{2,1,0:T(8,128)(2,1)S(1)} %collective-permute-done.6.refs_2_.refs_1_), channel_id=1, source_target_pairs={{0,16},{16,0},{1,17},{17,1},{2,18},{18,2},{3,19},{19,3},{4,20},{20... | collective-permute-start | bytes 884744 | tf_op jit(solution)/shard_map/ppermute | solution.py:38
  32.0 1.2 %low_rows.3.refs_0_ = bf16[64,768]{1,0:T(8,128)(2,1)S(1)} custom-call(s32[1,768]{1,0:T(1,128)S(1)} %bitcast.9, bf16[768,2048]{1,0:T(8,128)(2,1)S(1)} %copy-done.1, bf16[1,64,2304]{2,1,0:T(8,128)(2,1)S(1)} %collective-permute-done.8.refs_3_.refs_0_, bf16[1,64,2304]{2,1,0:T(8,128)(2,1)S(1)} %collective-permute-done.6.refs_2_.refs_1_, ...), custom_call_target="tpu_custom_call" | custom-call | flops 5000000000 | bytes 1 | tf_op jit(solution)/shard_map/low_rows/pallas_call | solution.py:124
  33.2 1.3 %collective-permute-done.9.refs_1_ = bf16[64,768]{1,0:T(8,128)(2,1)S(1)} collective-permute-done((bf16[64,768]{1,0:T(8,128)(2,1)S(1)}, bf16[64,768]{1,0:T(8,128)(2,1)S(1)}, u32[]{:S(2)}, u32[]{:S(2)}) %collective-permute-start.9) | collective-permute-done | bytes 98336 | tf_op jit(solution)/shard_map/ppermute | solution.py:38
  34.6 1.9 %collective-permute-start.10 = (bf16[64,768]{1,0:T(8,128)(2,1)S(1)}, bf16[64,768]{1,0:T(8,128)(2,1)S(1)}, u32[]{:S(2)}, u32[]{:S(2)}) collective-permute-start(bf16[64,768]{1,0:T(8,128)(2,1)S(1)} %add.7.mine_ref), channel_id=1, source_target_pairs={{0,2},{1,3},{2,0},{3,1},{4,6},{5,7},{6,4},{7,5},{8,10},{9,11},{10,... | collective-permute-start | bytes 294920 | tf_op jit(solution)/shard_map/ppermute | solution.py:38
  36.4 0.6 %rotated_ups.1 = (bf16[512,256]{1,0:T(8,128)(2,1)S(1)}, bf16[768,512]{1,0:T(8,128)(2,1)S(1)}) custom-call(s32[1,768]{1,0:T(1,128)S(1)} %bitcast.10, s32[1,128]{1,0:T(1,128)S(1)} %bitcast.11, bf16[128,128]{1,0:T(8,128)(2,1)S(1)} %copy-done.3, bf16[2,64,256]{2,1,0:T(8,128)(2,1)S(1)} %copy-done.4, bf16[1,64,2304]{2,1,0:T(8,128)(2,1)S(1)} %collective-permute-done.2.refs_1_, ...), custom_call_target="tpu_custom_call" | custom-call | flops 1 | bytes 1 | tf_op jit(solution)/shard_map/rotated_ups/pallas_call | solution.py:153
  37.0 1.9 %collective-permute-done.7.piece_ref = bf16[1,64,2304]{2,1,0:T(8,128)(2,1)S(1)} collective-permute-done((bf16[1,64,2304]{2,1,0:T(8,128)(2,1)S(1)}, bf16[1,64,2304]{2,1,0:T(8,128)(2,1)S(1)}, u32[]{:S(2)}, u32[]{:S(2)}) %collective-permute-start.7) | collective-permute-done | bytes 294944 | tf_op jit(solution)/shard_map/ppermute | solution.py:38
  38.9 1.2 %compact.1.refs_0_ = bf16[64,256]{1,0:T(8,128)(2,1)S(1)} custom-call(bf16[768,2048]{1,0:T(8,128)(2,1)S(1)} %copy-done.1, bf16[1,64,2304]{2,1,0:T(8,128)(2,1)S(1)} %collective-permute-done.7.piece_ref, bf16[768,256]{1,0:T(8,128)(2,1)S(1)} %picked.1.pick_ref), custom_call_target="tpu_custom_call" | custom-call | flops 1 | bytes 1 | tf_op jit(solution)/shard_map/compact/pallas_call | solution.py:202
  40.3 1.6 %collective-permute-start.13 = (bf16[64,256]{1,0:T(8,128)(2,1)S(1)}, bf16[64,256]{1,0:T(8,128)(2,1)S(1)}, u32[]{:S(2)}, u32[]{:S(2)}) collective-permute-start(bf16[64,256]{1,0:T(8,128)(2,1)S(1)} %compact.1.refs_0_), channel_id=1, source_target_pairs={{0,2},{1,3},{2,0},{3,1},{4,6},{5,7},{6,4},{7,5},{8,10},{9,11},{10,... | collective-permute-start | bytes 98312 | tf_op jit(solution)/shard_map/ppermute | solution.py:38
  41.8 0.3 collective-permute-start.12
  42.1 0.8 %most.1.most_ref = f32[768,256]{1,0:T(8,128)S(1)} custom-call(bf16[64,768]{1,0:T(8,128)(2,1)S(1)} %add.7.mine_ref, bf16[64,768]{1,0:T(8,128)(2,1)S(1)} %collective-permute-done.10.theirs_ref, bf16[512,256]{1,0:T(8,128)(2,1)S(1)} %get-tuple-element.38.up_ref, bf16[768,512]{1,0:T(8,128)(2,1)S(1)} %get-tuple-element.39.mask_ref, f32[1,256]{1,0:T(1,128)S(1)} %bitcast.14, ...), custom_call_target="tpu_custom_call" | custom-call | flops 1 | bytes 1 | tf_op jit(solution)/shard_map/most/pallas_call | solution.py:224
  42.9 1.0 %collective-permute-done.14.refs_3_ = bf16[64,256]{1,0:T(8,128)(2,1)S(1)} collective-permute-done((bf16[64,256]{1,0:T(8,128)(2,1)S(1)}, bf16[64,256]{1,0:T(8,128)(2,1)S(1)}, u32[]{:S(2)}, u32[]{:S(2)}) %collective-permute-start.14) | collective-permute-done | bytes 32800 | tf_op jit(solution)/shard_map/ppermute | solution.py:38
  43.9 0.4 collective-permute-done.13.refs_2_
  44.3 1.4 %final.1 = bf16[768,256]{1,0:T(8,128)(2,1)} custom-call(bf16[768,256]{1,0:T(8,128)(2,1)S(1)} %picked.1.pick_ref, bf16[1,64,2304]{2,1,0:T(8,128)(2,1)S(1)} %collective-permute-done.7.piece_ref, s32[1,128]{1,0:T(1,128)S(1)} %bitcast.13, bf16[128,128]{1,0:T(8,128)(2,1)S(1)} %copy-done.3, f32[768,256]{1,0:T(8,128)S(1)} %most.1.most_ref, ...), custom_call_target="tpu_custom_call" | custom-call | flops 1 | bytes 1 | tf_op jit(solution)/shard_map/final/pallas_call | solution.py:252
  (30 shorter events, 0.3 us)
Async XLA Ops:
  1.0 14.1 %collective-permute-start = (bf16[1,64,2048]{2,1,0:T(8,128)(2,1)S(1)}, bf16[1,64,2048]{2,1,0:T(8,128)(2,1)S(1)}, u32[]{:S(2)}, u32[]{:S(2)}) collective-permute-start(bf16[1,64,2048]{2,1,0:T(8,128)(2,1)S(1)} %dynamic-slice_bitcast_fusion), channel_id=1, source_target_pairs={{0,4},{4,0},{8,12},{12,8},{1,5},{5,1},{9,13},{13,9},{2,6},{6,2},{1... | collective-permute-start | bytes 786440 | tf_op jit(solution)/shard_map/ppermute | solution.py:38
  4.8 15.9 %collective-permute-start.2 = (bf16[1,64,2304]{2,1,0:T(8,128)(2,1)S(1)}, bf16[1,64,2304]{2,1,0:T(8,128)(2,1)S(1)}, u32[]{:S(2)}, u32[]{:S(2)}) collective-permute-start(bf16[1,64,2304]{2,1,0:T(8,128)(2,1)S(1)} %pad_maximum_fusion), channel_id=1, source_target_pairs={{0,8},{4,12},{8,0},{12,4},{1,9},{5,13},{9,1},{13,5},{2,10},{6,14},... | collective-permute-start | bytes 884744 | tf_op jit(solution)/shard_map/ppermute | solution.py:38
  7.5 1.9 %copy-start = (bf16[768,2048]{1,0:T(8,128)(2,1)S(1)}, bf16[768,2048]{1,0:T(8,128)(2,1)}, u32[]{:S(2)}) copy-start(bf16[768,2048]{1,0:T(8,128)(2,1)} %tokens_ref.9) | copy-start | bytes 9437188
  9.4 2.2 %copy-start.2 = (bf16[2048,1024]{1,0:T(8,128)(2,1)S(1)}, bf16[2048,1024]{1,0:T(8,128)(2,1)}, u32[]{:S(2)}) copy-start(bf16[2048,1024]{1,0:T(8,128)(2,1)} %weight_ref.3) | copy-start | bytes 12582916
  11.6 5.6 %copy-start.4 = (bf16[2,64,256]{2,1,0:T(8,128)(2,1)S(1)}, bf16[2,64,256]{2,1,0:T(8,128)(2,1)}, u32[]{:S(2)}) copy-start(bf16[2,64,256]{2,1,0:T(8,128)(2,1)} %refs_0_.1) | copy-start | bytes 196612
  14.2 9.1 %copy-start.6 = (s32[768,1]{0,1:T(1,128)S(1)}, s32[768,1]{0,1:T(1,128)}, u32[]{:S(2)}) copy-start(s32[768,1]{0,1:T(1,128)} %param.9) | copy-start | bytes 9220
  15.0 8.7 %collective-permute-start.3 = (bf16[1,64,2048]{2,1,0:T(8,128)(2,1)S(1)}, bf16[1,64,2048]{2,1,0:T(8,128)(2,1)S(1)}, u32[]{:S(2)}, u32[]{:S(2)}) collective-permute-start(bf16[1,64,2048]{2,1,0:T(8,128)(2,1)S(1)} %collective-permute-done.refs_0_), channel_id=1, source_target_pairs={{0,16},{16,0},{1,17},{17,1},{2,18},{18,2},{3,19},{19,3},{4,20},{20... | collective-permute-start | bytes 786440 | tf_op jit(solution)/shard_map/ppermute | solution.py:38
  16.7 8.2 %collective-permute-start.4 = (bf16[768,256]{1,0:T(8,128)(2,1)S(1)}, bf16[768,256]{1,0:T(8,128)(2,1)S(1)}, u32[]{:S(2)}, u32[]{:S(2)}) collective-permute-start(bf16[768,256]{1,0:T(8,128)(2,1)S(1)} %get-tuple-element.30), channel_id=1, source_target_pairs={{0,1},{1,0},{2,3},{3,2},{4,5},{5,4},{6,7},{7,6},{8,9},{9,8},{10,11... | collective-permute-start | bytes 1179656 | tf_op jit(solution)/shard_map/ppermute | solution.py:38
  16.7 7.0 %copy-start.1 = (bf16[768,2048]{1,0:T(8,128)(2,1)S(1)}, bf16[768,2048]{1,0:T(8,128)(2,1)}, u32[]{:S(2)}) copy-start(bf16[768,2048]{1,0:T(8,128)(2,1)} %tokens_ref.9) | copy-start | bytes 9437188
  16.7 7.0 %copy-start.5 = (bf16[2,2048,64]{1,2,0:T(8,128)(2,1)S(1)}, bf16[2,2048,64]{1,2,0:T(8,128)(2,1)}, u32[]{:S(2)}) copy-start(bf16[2,2048,64]{1,2,0:T(8,128)(2,1)} %param.12) | copy-start | bytes 1572868
  16.7 8.2 %collective-permute-start.5 = (bf16[768,256]{1,0:T(8,128)(2,1)S(1)}, bf16[768,256]{1,0:T(8,128)(2,1)S(1)}, u32[]{:S(2)}, u32[]{:S(2)}) collective-permute-start(bf16[768,256]{1,0:T(8,128)(2,1)S(1)} %get-tuple-element.31), channel_id=1, source_target_pairs={{0,1},{1,0},{2,3},{3,2},{4,5},{5,4},{6,7},{7,6},{8,9},{9,8},{10,11... | collective-permute-start | bytes 1179656 | tf_op jit(solution)/shard_map/ppermute | solution.py:38
  17.2 4.8 %collective-permute-start.1 = (bf16[2,64,256]{2,1,0:T(8,128)(2,1)S(1)}, bf16[2,64,256]{2,1,0:T(8,128)(2,1)S(1)}, u32[]{:S(2)}, u32[]{:S(2)}) collective-permute-start(bf16[2,64,256]{2,1,0:T(8,128)(2,1)S(1)} %copy-done.4), channel_id=1, source_target_pairs={{0,4},{4,0},{8,12},{12,8},{1,5},{5,1},{9,13},{13,9},{2,6},{6,2},{1... | collective-permute-start | bytes 196616 | tf_op jit(solution)/shard_map/ppermute | solution.py:38
  22.0 8.9 %collective-permute-start.6 = (bf16[1,64,2304]{2,1,0:T(8,128)(2,1)S(1)}, bf16[1,64,2304]{2,1,0:T(8,128)(2,1)S(1)}, u32[]{:S(2)}, u32[]{:S(2)}) collective-permute-start(bf16[1,64,2304]{2,1,0:T(8,128)(2,1)S(1)} %collective-permute-done.2.refs_1_), channel_id=1, source_target_pairs={{0,4},{4,0},{8,12},{12,8},{1,5},{5,1},{9,13},{13,9},{2,6},{6,2},{1... | collective-permute-start | bytes 884744 | tf_op jit(solution)/shard_map/ppermute | solution.py:38
  22.0 9.9 %collective-permute-start.8 = (bf16[1,64,2304]{2,1,0:T(8,128)(2,1)S(1)}, bf16[1,64,2304]{2,1,0:T(8,128)(2,1)S(1)}, u32[]{:S(2)}, u32[]{:S(2)}) collective-permute-start(bf16[1,64,2304]{2,1,0:T(8,128)(2,1)S(1)} %collective-permute-done.2.refs_1_), channel_id=1, source_target_pairs={{0,16},{16,0},{1,17},{17,1},{2,18},{18,2},{3,19},{19,3},{4,20},{20... | collective-permute-start | bytes 884744 | tf_op jit(solution)/shard_map/ppermute | solution.py:38
  25.1 11.4 %copy-start.3 = (bf16[128,128]{1,0:T(8,128)(2,1)S(1)}, bf16[128,128]{1,0:T(8,128)(2,1)}, u32[]{:S(2)}) copy-start(bf16[128,128]{1,0:T(8,128)(2,1)} %constant.12.clone.matrix_ref) | copy-start | bytes 98308
  25.1 11.4 %copy-start.7 = (s32[128]{0:T(128)S(1)}, s32[128]{0:T(128)}, u32[]{:S(2)}) copy-start(s32[128]{0:T(128)} %param.14) | copy-start | bytes 1540
  25.1 17.0 %collective-permute-start.11 = (bf16[768,256]{1,0:T(8,128)(2,1)S(1)}, bf16[768,256]{1,0:T(8,128)(2,1)S(1)}, u32[]{:S(2)}, u32[]{:S(2)}) collective-permute-start(bf16[768,256]{1,0:T(8,128)(2,1)S(1)} %add.8), channel_id=1, source_target_pairs={{0,2},{1,3},{2,0},{3,1},{4,6},{5,7},{6,4},{7,5},{8,10},{9,11},{10,... | collective-permute-start | bytes 1179656 | tf_op jit(solution)/shard_map/ppermute | solution.py:38
  30.9 8.0 %collective-permute-start.7 = (bf16[1,64,2304]{2,1,0:T(8,128)(2,1)S(1)}, bf16[1,64,2304]{2,1,0:T(8,128)(2,1)S(1)}, u32[]{:S(2)}, u32[]{:S(2)}) collective-permute-start(bf16[1,64,2304]{2,1,0:T(8,128)(2,1)S(1)} %collective-permute-done.6.refs_2_.refs_1_), channel_id=1, source_target_pairs={{0,16},{16,0},{1,17},{17,1},{2,18},{18,2},{3,19},{19,3},{4,20},{20... | collective-permute-start | bytes 884744 | tf_op jit(solution)/shard_map/ppermute | solution.py:38
  33.2 9.0 %copy-start.8 = (f32[256]{0:T(256)S(1)}, f32[256]{0:T(256)}, u32[]{:S(2)}) copy-start(f32[256]{0:T(256)} %param.11) | copy-start | bytes 3076
  33.2 1.4 %collective-permute-start.9 = (bf16[64,768]{1,0:T(8,128)(2,1)S(1)}, bf16[64,768]{1,0:T(8,128)(2,1)S(1)}, u32[]{:S(2)}, u32[]{:S(2)}) collective-permute-start(bf16[64,768]{1,0:T(8,128)(2,1)S(1)} %low_rows.3.refs_0_), channel_id=1, source_target_pairs={{0,1},{1,0},{2,3},{3,2},{4,5},{5,4},{6,7},{7,6},{8,9},{9,8},{10,11... | collective-permute-start | bytes 294920 | tf_op jit(solution)/shard_map/ppermute | solution.py:38
  34.6 7.6 %collective-permute-start.10 = (bf16[64,768]{1,0:T(8,128)(2,1)S(1)}, bf16[64,768]{1,0:T(8,128)(2,1)S(1)}, u32[]{:S(2)}, u32[]{:S(2)}) collective-permute-start(bf16[64,768]{1,0:T(8,128)(2,1)S(1)} %add.7.mine_ref), channel_id=1, source_target_pairs={{0,2},{1,3},{2,0},{3,1},{4,6},{5,7},{6,4},{7,5},{8,10},{9,11},{10,... | collective-permute-start | bytes 294920 | tf_op jit(solution)/shard_map/ppermute | solution.py:38
  40.2 3.7 %collective-permute-start.14 = (bf16[64,256]{1,0:T(8,128)(2,1)S(1)}, bf16[64,256]{1,0:T(8,128)(2,1)S(1)}, u32[]{:S(2)}, u32[]{:S(2)}) collective-permute-start(bf16[64,256]{1,0:T(8,128)(2,1)S(1)} %compact.1.refs_0_), channel_id=1, source_target_pairs={{0,3},{1,2},{2,1},{3,0},{4,7},{5,6},{6,5},{7,4},{8,11},{9,10},{10,... | collective-permute-start | bytes 98312 | tf_op jit(solution)/shard_map/ppermute | solution.py:38
  40.3 4.0 %collective-permute-start.13 = (bf16[64,256]{1,0:T(8,128)(2,1)S(1)}, bf16[64,256]{1,0:T(8,128)(2,1)S(1)}, u32[]{:S(2)}, u32[]{:S(2)}) collective-permute-start(bf16[64,256]{1,0:T(8,128)(2,1)S(1)} %compact.1.refs_0_), channel_id=1, source_target_pairs={{0,2},{1,3},{2,0},{3,1},{4,6},{5,7},{6,4},{7,5},{8,10},{9,11},{10,... | collective-permute-start | bytes 98312 | tf_op jit(solution)/shard_map/ppermute | solution.py:38
  41.8 2.5 %collective-permute-start.12 = (bf16[64,256]{1,0:T(8,128)(2,1)S(1)}, bf16[64,256]{1,0:T(8,128)(2,1)S(1)}, u32[]{:S(2)}, u32[]{:S(2)}) collective-permute-start(bf16[64,256]{1,0:T(8,128)(2,1)S(1)} %compact.1.refs_0_), channel_id=1, source_target_pairs={{0,1},{1,0},{2,3},{3,2},{4,5},{5,4},{6,7},{7,6},{8,9},{9,8},{10,11... | collective-permute-start | bytes 98312 | tf_op jit(solution)/shard_map/ppermute | solution.py:38

commit v16 on v13

--- a/solution.py
+++ b/solution.py
@@ -204,7 +204,7 @@
         out_specs=VMEM,
         out_shape=jax.ShapeDtypeStruct((piece.shape[1], pick.shape[1]), BF16),
         compiler_params=params(24),
-        cost_estimate=COST,
+        cost_estimate=lasting(2),
         name="compact",
     )(tokens, piece, pick)
 
@@ -238,11 +238,12 @@
     )(mine, theirs, up, mask, near, scale, bits, matrix, *terms)
 
 
-def final_kernel(mine_ref, theirs_ref, pick_ref, piece_ref, bits_ref, matrix_ref, most_ref, out_ref):
+def final_kernel(pick_ref, piece_ref, bits_ref, matrix_ref, most_ref, *refs):
+    kept_refs, out_ref = refs[:-1], refs[-1]
     share, width = piece_ref.shape[0], out_ref.shape[1]
     features, slots = piece_ref.shape[2] - width, pick_ref.shape[1] // share
     signs = (1 - 2 * bits_ref[...]).astype(F32)
-    low = (mine_ref[...].astype(F32) + theirs_ref[...].astype(F32)).astype(BF16).T
+    low = functools.reduce(jnp.add, [ref[...].astype(F32) for ref in kept_refs]).astype(BF16).T
     deltas = []
     for k in range(share):
         turned = rotate(piece_ref[k, :, features:].astype(F32), signs, matrix_ref[...])
@@ -253,16 +254,16 @@
     out_ref[...] = result.astype(BF16)
 
 
-def final(mine, theirs, pick, piece, bits, matrix, rest):
+def final(kept, pick, piece, bits, matrix, rest):
     return pl.pallas_call(
         final_kernel,
-        in_specs=[VMEM] * 7,
+        in_specs=[VMEM] * (5 + len(kept)),
         out_specs=VMEM,
         out_shape=jax.ShapeDtypeStruct(rest.shape, BF16),
         compiler_params=params(32),
         cost_estimate=COST,
         name="final",
-    )(mine, theirs, pick, piece, bits, matrix, rest)
+    )(pick, piece, bits, matrix, rest, *kept)
 
 
 def local(tokens, adapter_ids, base_weight, channel_scale, adapter_down, adapter_up, sign_bits):
@@ -344,9 +345,10 @@
     up, mask = rotated_ups(ids, bits, matrix, here, share, named, ups, arrays, width)
 
     piece, up, mask, near_up = together(last[2], up, mask, near_up)
-    kept, more_kept = both(compact(tokens, piece, pick))
+    kept = compact(tokens, piece, pick)
+    kept = [kept] + [swap(kept, "tp", offset) for offset in range(1, parts)]
     rest = most(low, other, up, mask, near_up, scale, bits, matrix, sums[0])
-    return final(kept, more_kept, pick, piece, bits, matrix, rest)
+    return final(kept, pick, piece, bits, matrix, rest)
 
 
 def solution(mesh):

time: 43.7 us -> 43.4 us (level)
  waiting for transfers between devices: 10.4 us -> 9.8 us
    ppermute x14 -> x15, waiting for transfers between devices: 10.4 us -> 9.8 us  [swap(): lax.ppermute(x, axis, [(i, i ^ bit) for i in range(lax.axis_size(axis))])]
    ppermute x14 -> x15, starting transfers between devices: 16.5 us -> 16.8 us  [swap(): lax.ppermute(x, axis, [(i, i ^ bit) for i in range(lax.axis_size(axis))])]
  transfers between devices with their start and end apart: 14 -> 15, of which waited for: 8 -> 7; matrix products, arithmetic and copies ran while one was open for 2% -> 2% of each run, Pallas kernels for 21% -> 21%
where the time goes in v16:
time: 43.4 us; the launch traced here: 43.1 us
  starting transfers between devices  16.8 us (39%)
  Pallas kernels  10.5 us (24%)
  waiting for transfers between devices  9.8 us (23%)
  local copies, waits for them, and re-layouts  5.84 us (13%)
    ppermute x15, starting transfers between devices, swap(): lax.ppermute(x, axis, [(i, i ^ bit) for i in range(lax.axis_size(axis))])  16.8 us
    ppermute x15, waiting for transfers between devices, swap(): lax.ppermute(x, axis, [(i, i ^ bit) for i in range(lax.axis_size(axis))])  9.8 us
    unnamed x18, local copies, waits for them, and re-layouts  4.11 us
    pallas_call x2, Pallas kernels, partials(): pl.pallas_call(functools.partial(partial_kernel, offsets, parts), in_spec...  3.67 us
    pallas_call x2, Pallas kernels, low_rows(): pl.pallas_call(functools.partial(low_kernel, groups, here, share, rank, b...  2.39 us
    pallas_call x1, Pallas kernels, final(): pl.pallas_call(final_kernel, in_specs=[VMEM] * (5 + len(kept)), out_specs...  1.36 us
    pallas_call x1, Pallas kernels, compact(): pl.pallas_call(compact_kernel, in_specs=[VMEM] * 3, out_specs=VMEM, out_s...  1.25 us
    dynamic_slice x1, local copies, waits for them, and re-layouts, local(): own = lax.dynamic_slice_in_dim(down, start, share, 0)  0.97 us
  transfers between devices with their start and end apart: 15, of which 7 were waited for; matrix products, arithmetic and copies ran while one was open for 2% of the time, Pallas kernels for 21%

profile of v16, /device:TPU:0, one launch (start us, length us, event | category | flops | bytes accessed | tf_op | source)
XLA Modules:
  0.0 43.1 jit_solution(4168928635004821380)
XLA Ops:
  0.0 1.0 %dynamic-slice_bitcast_fusion = bf16[1,64,2048]{2,1,0:T(8,128)(2,1)S(1)} fusion(bf16[2,2048,64]{1,2,0:T(8,128)(2,1)} %param.12, s32[]{:T(128)S(6)} %select_n.4), kind=kLoop, calls=%fused_computation.1 | loop fusion | bytes 524292 | tf_op jit(solution)/shard_map/dynamic_slice | solution.py:280
  1.0 3.1 %collective-permute-start = (bf16[1,64,2048]{2,1,0:T(8,128)(2,1)S(1)}, bf16[1,64,2048]{2,1,0:T(8,128)(2,1)S(1)}, u32[]{:S(2)}, u32[]{:S(2)}) collective-permute-start(bf16[1,64,2048]{2,1,0:T(8,128)(2,1)S(1)} %dynamic-slice_bitcast_fusion), channel_id=1, source_target_pairs={{0,4},{4,0},{8,12},{12,8},{1,5},{5,1},{9,13},{13,9},{2,6},{6,2},{1... | collective-permute-start | bytes 786440 | tf_op jit(solution)/shard_map/ppermute | solution.py:38
  4.1 0.8 %constant_dynamic-slice_fusion = bf16[1,64,256]{2,1,0:T(8,128)(2,1)S(1)} fusion(bf16[2,64,256]{2,1,0:T(8,128)(2,1)} %refs_0_.1, s32[]{:T(128)S(6)} %select_n.4), kind=kLoop, calls=%fused_computation.2 | loop fusion | bytes 65540 | tf_op jit(solution)/shard_map/dynamic_slice | solution.py:282
  4.8 2.7 %collective-permute-start.1 = (bf16[1,64,2304]{2,1,0:T(8,128)(2,1)S(1)}, bf16[1,64,2304]{2,1,0:T(8,128)(2,1)S(1)}, u32[]{:S(2)}, u32[]{:S(2)}) collective-permute-start(bf16[1,64,2304]{2,1,0:T(8,128)(2,1)S(1)} %pad_maximum_fusion), channel_id=1, source_target_pairs={{0,8},{4,12},{8,0},{12,4},{1,9},{5,13},{9,1},{13,5},{2,10},{6,14},... | collective-permute-start | bytes 884744 | tf_op jit(solution)/shard_map/ppermute | solution.py:38
  7.5 2.2 %copy-done = bf16[2048,1024]{1,0:T(8,128)(2,1)S(1)} copy-done((bf16[2048,1024]{1,0:T(8,128)(2,1)S(1)}, bf16[2048,1024]{1,0:T(8,128)(2,1)}, u32[]{:S(2)}) %copy-start) | copy-done | bytes 4194328
  9.7 1.9 %copy-done.1 = bf16[768,2048]{1,0:T(8,128)(2,1)S(1)} copy-done((bf16[768,2048]{1,0:T(8,128)(2,1)S(1)}, bf16[768,2048]{1,0:T(8,128)(2,1)}, u32[]{:S(2)}) %copy-start.1) | copy-done | bytes 3145752
  11.6 2.7 %partials.2 = (bf16[768,256]{1,0:T(8,128)(2,1)S(1)}, bf16[768,256]{1,0:T(8,128)(2,1)S(1)}, bf16[768,256]{1,0:T(8,128)(2,1)S(1)}) custom-call(bf16[768,2048]{1,0:T(8,128)(2,1)S(1)} %copy-done.1, bf16[2048,1024]{1,0:T(8,128)(2,1)S(1)} %copy-done), custom_call_target="tpu_custom_call" | custom-call | flops 4000000000 | bytes 1 | tf_op jit(solution)/shard_map/partials/pallas_call | solution.py:69
  14.3 0.8 %collective-permute-done.refs_0_ = bf16[1,64,2048]{2,1,0:T(8,128)(2,1)S(1)} collective-permute-done((bf16[1,64,2048]{2,1,0:T(8,128)(2,1)S(1)}, bf16[1,64,2048]{2,1,0:T(8,128)(2,1)S(1)}, u32[]{:S(2)}, u32[]{:S(2)}) %collective-permute-start) | collective-permute-done | bytes 262176 | tf_op jit(solution)/shard_map/ppermute | solution.py:38
  15.0 1.7 %collective-permute-start.2 = (bf16[1,64,2048]{2,1,0:T(8,128)(2,1)S(1)}, bf16[1,64,2048]{2,1,0:T(8,128)(2,1)S(1)}, u32[]{:S(2)}, u32[]{:S(2)}) collective-permute-start(bf16[1,64,2048]{2,1,0:T(8,128)(2,1)S(1)} %collective-permute-done.refs_0_), channel_id=1, source_target_pairs={{0,16},{16,0},{1,17},{17,1},{2,18},{18,2},{3,19},{19,3},{4,20},{20... | collective-permute-start | bytes 786440 | tf_op jit(solution)/shard_map/ppermute | solution.py:38
  16.7 0.5 %collective-permute-start.4 = (bf16[768,256]{1,0:T(8,128)(2,1)S(1)}, bf16[768,256]{1,0:T(8,128)(2,1)S(1)}, u32[]{:S(2)}, u32[]{:S(2)}) collective-permute-start(bf16[768,256]{1,0:T(8,128)(2,1)S(1)} %get-tuple-element.31), channel_id=1, source_target_pairs={{0,1},{1,0},{2,3},{3,2},{4,5},{5,4},{6,7},{7,6},{8,9},{9,8},{10,11... | collective-permute-start | bytes 1179656 | tf_op jit(solution)/shard_map/ppermute | solution.py:38
  17.2 1.0 %partials.3.refs_0_ = bf16[768,256]{1,0:T(8,128)(2,1)S(1)} custom-call(bf16[768,2048]{1,0:T(8,128)(2,1)S(1)} %copy-done.1, bf16[2048,1024]{1,0:T(8,128)(2,1)S(1)} %copy-done, bf16[768,256]{1,0:T(8,128)(2,1)S(1)} %get-tuple-element.27.refs_0_), custom_call_target="tpu_custom_call" | custom-call | flops 1 | bytes 1 | tf_op jit(solution)/shard_map/partials/pallas_call | solution.py:69
  18.2 2.4 %collective-permute-done.1.refs_1_ = bf16[1,64,2304]{2,1,0:T(8,128)(2,1)S(1)} collective-permute-done((bf16[1,64,2304]{2,1,0:T(8,128)(2,1)S(1)}, bf16[1,64,2304]{2,1,0:T(8,128)(2,1)S(1)}, u32[]{:S(2)}, u32[]{:S(2)}) %collective-permute-start.1) | collective-permute-done | bytes 294944 | tf_op jit(solution)/shard_map/ppermute | solution.py:38
  20.6 1.5 %collective-permute-start.7 = (bf16[1,64,2304]{2,1,0:T(8,128)(2,1)S(1)}, bf16[1,64,2304]{2,1,0:T(8,128)(2,1)S(1)}, u32[]{:S(2)}, u32[]{:S(2)}) collective-permute-start(bf16[1,64,2304]{2,1,0:T(8,128)(2,1)S(1)} %collective-permute-done.1.refs_1_), channel_id=1, source_target_pairs={{0,16},{16,0},{1,17},{17,1},{2,18},{18,2},{3,19},{19,3},{4,20},{20... | collective-permute-start | bytes 884744 | tf_op jit(solution)/shard_map/ppermute | solution.py:38
  22.2 0.4 picked.1.pick_ref
  22.5 0.5 %collective-permute-done.2.refs_2_ = bf16[1,64,2048]{2,1,0:T(8,128)(2,1)S(1)} collective-permute-done((bf16[1,64,2048]{2,1,0:T(8,128)(2,1)S(1)}, bf16[1,64,2048]{2,1,0:T(8,128)(2,1)S(1)}, u32[]{:S(2)}, u32[]{:S(2)}) %collective-permute-start.2) | collective-permute-done | bytes 262176 | tf_op jit(solution)/shard_map/ppermute | solution.py:38
  23.0 1.2 %low_rows.2.refs_2_ = f32[64,768]{1,0:T(8,128)S(1)} custom-call(s32[1,768]{1,0:T(1,128)S(1)} %bitcast.8, bf16[768,2048]{1,0:T(8,128)(2,1)S(1)} %copy-done.2, bf16[1,64,2048]{2,1,0:T(8,128)(2,1)S(1)} %collective-permute-done.refs_0_, bf16[1,64,2304]{2,1,0:T(8,128)(2,1)S(1)} %collective-permute-done.1.refs_1_, ...), custom_call_target="tpu_custom_call" | custom-call | flops 2000000000 | bytes 1 | tf_op jit(solution)/shard_map/low_rows/pallas_call | solution.py:124
  24.4 1.3 %collective-permute-start.11 = (bf16[768,256]{1,0:T(8,128)(2,1)S(1)}, bf16[768,256]{1,0:T(8,128)(2,1)S(1)}, u32[]{:S(2)}, u32[]{:S(2)}) collective-permute-start(bf16[768,256]{1,0:T(8,128)(2,1)S(1)} %add.8), channel_id=1, source_target_pairs={{0,2},{1,3},{2,0},{3,1},{4,6},{5,7},{6,4},{7,5},{8,10},{9,11},{10,... | collective-permute-start | bytes 1179656 | tf_op jit(solution)/shard_map/ppermute | solution.py:38
  25.7 2.6 %collective-permute-done.5.refs_2_.refs_1_ = bf16[1,64,2304]{2,1,0:T(8,128)(2,1)S(1)} collective-permute-done((bf16[1,64,2304]{2,1,0:T(8,128)(2,1)S(1)}, bf16[1,64,2304]{2,1,0:T(8,128)(2,1)S(1)}, u32[]{:S(2)}, u32[]{:S(2)}) %collective-permute-start.5) | collective-permute-done | bytes 294944 | tf_op jit(solution)/shard_map/ppermute | solution.py:38
  28.2 1.5 %collective-permute-start.6 = (bf16[1,64,2304]{2,1,0:T(8,128)(2,1)S(1)}, bf16[1,64,2304]{2,1,0:T(8,128)(2,1)S(1)}, u32[]{:S(2)}, u32[]{:S(2)}) collective-permute-start(bf16[1,64,2304]{2,1,0:T(8,128)(2,1)S(1)} %collective-permute-done.5.refs_2_.refs_1_), channel_id=1, source_target_pairs={{0,16},{16,0},{1,17},{17,1},{2,18},{18,2},{3,19},{19,3},{4,20},{20... | collective-permute-start | bytes 884744 | tf_op jit(solution)/shard_map/ppermute | solution.py:38
  29.8 1.2 %low_rows.3.refs_0_ = bf16[64,768]{1,0:T(8,128)(2,1)S(1)} custom-call(s32[1,768]{1,0:T(1,128)S(1)} %bitcast.9, bf16[768,2048]{1,0:T(8,128)(2,1)S(1)} %copy-done.2, bf16[1,64,2304]{2,1,0:T(8,128)(2,1)S(1)} %collective-permute-done.7.refs_3_.refs_0_, bf16[1,64,2304]{2,1,0:T(8,128)(2,1)S(1)} %collective-permute-done.5.refs_2_.refs_1_, ...), custom_call_target="tpu_custom_call" | custom-call | flops 5000000000 | bytes 1 | tf_op jit(solution)/shard_map/low_rows/pallas_call | solution.py:124
  31.0 1.0 %collective-permute-start.8 = (bf16[2,64,256]{2,1,0:T(8,128)(2,1)S(1)}, bf16[2,64,256]{2,1,0:T(8,128)(2,1)S(1)}, u32[]{:S(2)}, u32[]{:S(2)}) collective-permute-start(bf16[2,64,256]{2,1,0:T(8,128)(2,1)S(1)} %copy-done.4), channel_id=1, source_target_pairs={{0,4},{4,0},{8,12},{12,8},{1,5},{5,1},{9,13},{13,9},{2,6},{6,2},{1... | collective-permute-start | bytes 196616 | tf_op jit(solution)/shard_map/ppermute | solution.py:38
  32.1 0.5 %rotated_ups.1 = (bf16[320,256]{1,0:T(8,128)(2,1)S(1)}, bf16[768,512]{1,0:T(8,128)(2,1)S(1)}) custom-call(s32[1,768]{1,0:T(1,128)S(1)} %bitcast.10, s32[1,128]{1,0:T(1,128)S(1)} %bitcast.11, bf16[128,128]{1,0:T(8,128)(2,1)S(1)} %copy-done.3, bf16[2,64,256]{2,1,0:T(8,128)(2,1)S(1)} %copy-done.4, bf16[1,64,2304]{2,1,0:T(8,128)(2,1)S(1)} %collective-permute-done.1.refs_1_, ...), custom_call_target="tpu_custom_call" | custom-call | flops 1 | bytes 1 | tf_op jit(solution)/shard_map/rotated_ups/pallas_call | solution.py:152
  32.7 1.6 %collective-permute-start.10 = (bf16[64,768]{1,0:T(8,128)(2,1)S(1)}, bf16[64,768]{1,0:T(8,128)(2,1)S(1)}, u32[]{:S(2)}, u32[]{:S(2)}) collective-permute-start(bf16[64,768]{1,0:T(8,128)(2,1)S(1)} %add.7.mine_ref), channel_id=1, source_target_pairs={{0,2},{1,3},{2,0},{3,1},{4,6},{5,7},{6,4},{7,5},{8,10},{9,11},{10,... | collective-permute-start | bytes 294920 | tf_op jit(solution)/shard_map/ppermute | solution.py:38
  34.2 1.3 %collective-permute-done.8.near_ref = bf16[2,64,256]{2,1,0:T(8,128)(2,1)S(1)} collective-permute-done((bf16[2,64,256]{2,1,0:T(8,128)(2,1)S(1)}, bf16[2,64,256]{2,1,0:T(8,128)(2,1)S(1)}, u32[]{:S(2)}, u32[]{:S(2)}) %collective-permute-start.8) | collective-permute-done | bytes 65568 | tf_op jit(solution)/shard_map/ppermute | solution.py:38
  35.5 1.2 %compact.1.refs_0_ = bf16[64,256]{1,0:T(8,128)(2,1)S(1)} custom-call(bf16[768,2048]{1,0:T(8,128)(2,1)S(1)} %copy-done.2, bf16[1,64,2304]{2,1,0:T(8,128)(2,1)S(1)} %collective-permute-done.6.piece_ref, bf16[768,256]{1,0:T(8,128)(2,1)S(1)} %picked.1.pick_ref), custom_call_target="tpu_custom_call" | custom-call | flops 2000000000 | bytes 1 | tf_op jit(solution)/shard_map/compact/pallas_call | solution.py:201
  36.8 0.8 %collective-permute-start.14 = (bf16[64,256]{1,0:T(8,128)(2,1)S(1)}, bf16[64,256]{1,0:T(8,128)(2,1)S(1)}, u32[]{:S(2)}, u32[]{:S(2)}) collective-permute-start(bf16[64,256]{1,0:T(8,128)(2,1)S(1)} %compact.1.refs_0_), channel_id=1, source_target_pairs={{0,3},{1,2},{2,1},{3,0},{4,7},{5,6},{6,5},{7,4},{8,11},{9,10},{10,... | collective-permute-start | bytes 98312 | tf_op jit(solution)/shard_map/ppermute | solution.py:38
  37.6 0.8 %collective-permute-start.13 = (bf16[64,256]{1,0:T(8,128)(2,1)S(1)}, bf16[64,256]{1,0:T(8,128)(2,1)S(1)}, u32[]{:S(2)}, u32[]{:S(2)}) collective-permute-start(bf16[64,256]{1,0:T(8,128)(2,1)S(1)} %compact.1.refs_0_), channel_id=1, source_target_pairs={{0,2},{1,3},{2,0},{3,1},{4,6},{5,7},{6,4},{7,5},{8,10},{9,11},{10,... | collective-permute-start | bytes 98312 | tf_op jit(solution)/shard_map/ppermute | solution.py:38
  38.4 0.3 collective-permute-start.12
  38.7 0.8 %most.1.most_ref = f32[768,256]{1,0:T(8,128)S(1)} custom-call(bf16[64,768]{1,0:T(8,128)(2,1)S(1)} %add.7.mine_ref, bf16[64,768]{1,0:T(8,128)(2,1)S(1)} %collective-permute-done.10.theirs_ref, bf16[320,256]{1,0:T(8,128)(2,1)S(1)} %get-tuple-element.39.up_ref, bf16[768,512]{1,0:T(8,128)(2,1)S(1)} %get-tuple-element.40.mask_ref, ...), custom_call_target="tpu_custom_call" | custom-call | flops 1 | bytes 1 | tf_op jit(solution)/shard_map/most/pallas_call | solution.py:230
  39.5 1.0 %collective-permute-done.14.refs_3_ = bf16[64,256]{1,0:T(8,128)(2,1)S(1)} collective-permute-done((bf16[64,256]{1,0:T(8,128)(2,1)S(1)}, bf16[64,256]{1,0:T(8,128)(2,1)S(1)}, u32[]{:S(2)}, u32[]{:S(2)}) %collective-permute-start.14) | collective-permute-done | bytes 32800 | tf_op jit(solution)/shard_map/ppermute | solution.py:38
  40.5 1.3 %collective-permute-done.13.refs_2_ = bf16[64,256]{1,0:T(8,128)(2,1)S(1)} collective-permute-done((bf16[64,256]{1,0:T(8,128)(2,1)S(1)}, bf16[64,256]{1,0:T(8,128)(2,1)S(1)}, u32[]{:S(2)}, u32[]{:S(2)}) %collective-permute-start.13) | collective-permute-done | bytes 32800 | tf_op jit(solution)/shard_map/ppermute | solution.py:38
  41.8 1.4 %final.1 = bf16[768,256]{1,0:T(8,128)(2,1)} custom-call(bf16[768,256]{1,0:T(8,128)(2,1)S(1)} %picked.1.pick_ref, bf16[1,64,2304]{2,1,0:T(8,128)(2,1)S(1)} %collective-permute-done.6.piece_ref, s32[1,128]{1,0:T(1,128)S(1)} %bitcast.13, bf16[128,128]{1,0:T(8,128)(2,1)S(1)} %copy-done.3, f32[768,256]{1,0:T(8,128)S(1)} %most.1.most_ref, ...), custom_call_target="tpu_custom_call" | custom-call | flops 1 | bytes 1 | tf_op jit(solution)/shard_map/final/pallas_call | solution.py:258
  (30 shorter events, 0.3 us)
Async XLA Ops:
  1.0 14.1 %collective-permute-start = (bf16[1,64,2048]{2,1,0:T(8,128)(2,1)S(1)}, bf16[1,64,2048]{2,1,0:T(8,128)(2,1)S(1)}, u32[]{:S(2)}, u32[]{:S(2)}) collective-permute-start(bf16[1,64,2048]{2,1,0:T(8,128)(2,1)S(1)} %dynamic-slice_bitcast_fusion), channel_id=1, source_target_pairs={{0,4},{4,0},{8,12},{12,8},{1,5},{5,1},{9,13},{13,9},{2,6},{6,2},{1... | collective-permute-start | bytes 786440 | tf_op jit(solution)/shard_map/ppermute | solution.py:38
  4.8 15.8 %collective-permute-start.1 = (bf16[1,64,2304]{2,1,0:T(8,128)(2,1)S(1)}, bf16[1,64,2304]{2,1,0:T(8,128)(2,1)S(1)}, u32[]{:S(2)}, u32[]{:S(2)}) collective-permute-start(bf16[1,64,2304]{2,1,0:T(8,128)(2,1)S(1)} %pad_maximum_fusion), channel_id=1, source_target_pairs={{0,8},{4,12},{8,0},{12,4},{1,9},{5,13},{9,1},{13,5},{2,10},{6,14},... | collective-permute-start | bytes 884744 | tf_op jit(solution)/shard_map/ppermute | solution.py:38
  7.5 2.2 %copy-start = (bf16[2048,1024]{1,0:T(8,128)(2,1)S(1)}, bf16[2048,1024]{1,0:T(8,128)(2,1)}, u32[]{:S(2)}) copy-start(bf16[2048,1024]{1,0:T(8,128)(2,1)} %weight_ref.3) | copy-start | bytes 12582916
  9.7 1.9 %copy-start.1 = (bf16[768,2048]{1,0:T(8,128)(2,1)S(1)}, bf16[768,2048]{1,0:T(8,128)(2,1)}, u32[]{:S(2)}) copy-start(bf16[768,2048]{1,0:T(8,128)(2,1)} %tokens_ref.9) | copy-start | bytes 9437188
  14.2 7.9 %copy-start.6 = (s32[768,1]{0,1:T(1,128)S(1)}, s32[768,1]{0,1:T(1,128)}, u32[]{:S(2)}) copy-start(s32[768,1]{0,1:T(1,128)} %param.9) | copy-start | bytes 9220
  15.0 8.0 %collective-permute-start.2 = (bf16[1,64,2048]{2,1,0:T(8,128)(2,1)S(1)}, bf16[1,64,2048]{2,1,0:T(8,128)(2,1)S(1)}, u32[]{:S(2)}, u32[]{:S(2)}) collective-permute-start(bf16[1,64,2048]{2,1,0:T(8,128)(2,1)S(1)} %collective-permute-done.refs_0_), channel_id=1, source_target_pairs={{0,16},{16,0},{1,17},{17,1},{2,18},{18,2},{3,19},{19,3},{4,20},{20... | collective-permute-start | bytes 786440 | tf_op jit(solution)/shard_map/ppermute | solution.py:38
  16.7 7.6 %collective-permute-start.3 = (bf16[768,256]{1,0:T(8,128)(2,1)S(1)}, bf16[768,256]{1,0:T(8,128)(2,1)S(1)}, u32[]{:S(2)}, u32[]{:S(2)}) collective-permute-start(bf16[768,256]{1,0:T(8,128)(2,1)S(1)} %get-tuple-element.30), channel_id=1, source_target_pairs={{0,1},{1,0},{2,3},{3,2},{4,5},{5,4},{6,7},{7,6},{8,9},{9,8},{10,11... | collective-permute-start | bytes 1179656 | tf_op jit(solution)/shard_map/ppermute | solution.py:38
  16.7 6.3 %copy-start.2 = (bf16[768,2048]{1,0:T(8,128)(2,1)S(1)}, bf16[768,2048]{1,0:T(8,128)(2,1)}, u32[]{:S(2)}) copy-start(bf16[768,2048]{1,0:T(8,128)(2,1)} %tokens_ref.9) | copy-start | bytes 9437188
  16.7 6.3 %copy-start.5 = (bf16[2,2048,64]{1,2,0:T(8,128)(2,1)S(1)}, bf16[2,2048,64]{1,2,0:T(8,128)(2,1)}, u32[]{:S(2)}) copy-start(bf16[2,2048,64]{1,2,0:T(8,128)(2,1)} %param.12) | copy-start | bytes 1572868
  16.7 7.6 %collective-permute-start.4 = (bf16[768,256]{1,0:T(8,128)(2,1)S(1)}, bf16[768,256]{1,0:T(8,128)(2,1)S(1)}, u32[]{:S(2)}, u32[]{:S(2)}) collective-permute-start(bf16[768,256]{1,0:T(8,128)(2,1)S(1)} %get-tuple-element.31), channel_id=1, source_target_pairs={{0,1},{1,0},{2,3},{3,2},{4,5},{5,4},{6,7},{7,6},{8,9},{9,8},{10,11... | collective-permute-start | bytes 1179656 | tf_op jit(solution)/shard_map/ppermute | solution.py:38
  20.6 7.6 %collective-permute-start.5 = (bf16[1,64,2304]{2,1,0:T(8,128)(2,1)S(1)}, bf16[1,64,2304]{2,1,0:T(8,128)(2,1)S(1)}, u32[]{:S(2)}, u32[]{:S(2)}) collective-permute-start(bf16[1,64,2304]{2,1,0:T(8,128)(2,1)S(1)} %collective-permute-done.1.refs_1_), channel_id=1, source_target_pairs={{0,4},{4,0},{8,12},{12,8},{1,5},{5,1},{9,13},{13,9},{2,6},{6,2},{1... | collective-permute-start | bytes 884744 | tf_op jit(solution)/shard_map/ppermute | solution.py:38
  20.6 9.1 %collective-permute-start.7 = (bf16[1,64,2304]{2,1,0:T(8,128)(2,1)S(1)}, bf16[1,64,2304]{2,1,0:T(8,128)(2,1)S(1)}, u32[]{:S(2)}, u32[]{:S(2)}) collective-permute-start(bf16[1,64,2304]{2,1,0:T(8,128)(2,1)S(1)} %collective-permute-done.1.refs_1_), channel_id=1, source_target_pairs={{0,16},{16,0},{1,17},{17,1},{2,18},{18,2},{3,19},{19,3},{4,20},{20... | collective-permute-start | bytes 884744 | tf_op jit(solution)/shard_map/ppermute | solution.py:38
  24.4 6.6 %copy-start.4 = (bf16[2,64,256]{2,1,0:T(8,128)(2,1)S(1)}, bf16[2,64,256]{2,1,0:T(8,128)(2,1)}, u32[]{:S(2)}) copy-start(bf16[2,64,256]{2,1,0:T(8,128)(2,1)} %refs_0_.1) | copy-start | bytes 196612
  24.4 7.7 %copy-start.3 = (bf16[128,128]{1,0:T(8,128)(2,1)S(1)}, bf16[128,128]{1,0:T(8,128)(2,1)}, u32[]{:S(2)}) copy-start(bf16[128,128]{1,0:T(8,128)(2,1)} %constant.12.clone.matrix_ref) | copy-start | bytes 98308
  24.4 7.7 %copy-start.7 = (s32[128]{0:T(128)S(1)}, s32[128]{0:T(128)}, u32[]{:S(2)}) copy-start(s32[128]{0:T(128)} %param.14) | copy-start | bytes 1540
  24.4 14.3 %collective-permute-start.11 = (bf16[768,256]{1,0:T(8,128)(2,1)S(1)}, bf16[768,256]{1,0:T(8,128)(2,1)S(1)}, u32[]{:S(2)}, u32[]{:S(2)}) collective-permute-start(bf16[768,256]{1,0:T(8,128)(2,1)S(1)} %add.8), channel_id=1, source_target_pairs={{0,2},{1,3},{2,0},{3,1},{4,6},{5,7},{6,4},{7,5},{8,10},{9,11},{10,... | collective-permute-start | bytes 1179656 | tf_op jit(solution)/shard_map/ppermute | solution.py:38
  28.2 7.3 %collective-permute-start.6 = (bf16[1,64,2304]{2,1,0:T(8,128)(2,1)S(1)}, bf16[1,64,2304]{2,1,0:T(8,128)(2,1)S(1)}, u32[]{:S(2)}, u32[]{:S(2)}) collective-permute-start(bf16[1,64,2304]{2,1,0:T(8,128)(2,1)S(1)} %collective-permute-done.5.refs_2_.refs_1_), channel_id=1, source_target_pairs={{0,16},{16,0},{1,17},{17,1},{2,18},{18,2},{3,19},{19,3},{4,20},{20... | collective-permute-start | bytes 884744 | tf_op jit(solution)/shard_map/ppermute | solution.py:38
  30.9 1.7 %collective-permute-start.9 = (bf16[64,768]{1,0:T(8,128)(2,1)S(1)}, bf16[64,768]{1,0:T(8,128)(2,1)S(1)}, u32[]{:S(2)}, u32[]{:S(2)}) collective-permute-start(bf16[64,768]{1,0:T(8,128)(2,1)S(1)} %low_rows.3.refs_0_), channel_id=1, source_target_pairs={{0,1},{1,0},{2,3},{3,2},{4,5},{5,4},{6,7},{7,6},{8,9},{9,8},{10,11... | collective-permute-start | bytes 294920 | tf_op jit(solution)/shard_map/ppermute | solution.py:38
  31.0 4.5 %collective-permute-start.8 = (bf16[2,64,256]{2,1,0:T(8,128)(2,1)S(1)}, bf16[2,64,256]{2,1,0:T(8,128)(2,1)S(1)}, u32[]{:S(2)}, u32[]{:S(2)}) collective-permute-start(bf16[2,64,256]{2,1,0:T(8,128)(2,1)S(1)} %copy-done.4), channel_id=1, source_target_pairs={{0,4},{4,0},{8,12},{12,8},{1,5},{5,1},{9,13},{13,9},{2,6},{6,2},{1... | collective-permute-start | bytes 196616 | tf_op jit(solution)/shard_map/ppermute | solution.py:38
  32.1 6.6 %copy-start.8 = (f32[256]{0:T(256)S(1)}, f32[256]{0:T(256)}, u32[]{:S(2)}) copy-start(f32[256]{0:T(256)} %param.11) | copy-start | bytes 3076
  32.7 6.1 %collective-permute-start.10 = (bf16[64,768]{1,0:T(8,128)(2,1)S(1)}, bf16[64,768]{1,0:T(8,128)(2,1)S(1)}, u32[]{:S(2)}, u32[]{:S(2)}) collective-permute-start(bf16[64,768]{1,0:T(8,128)(2,1)S(1)} %add.7.mine_ref), channel_id=1, source_target_pairs={{0,2},{1,3},{2,0},{3,1},{4,6},{5,7},{6,4},{7,5},{8,10},{9,11},{10,... | collective-permute-start | bytes 294920 | tf_op jit(solution)/shard_map/ppermute | solution.py:38
  36.8 3.7 %collective-permute-start.14 = (bf16[64,256]{1,0:T(8,128)(2,1)S(1)}, bf16[64,256]{1,0:T(8,128)(2,1)S(1)}, u32[]{:S(2)}, u32[]{:S(2)}) collective-permute-start(bf16[64,256]{1,0:T(8,128)(2,1)S(1)} %compact.1.refs_0_), channel_id=1, source_target_pairs={{0,3},{1,2},{2,1},{3,0},{4,7},{5,6},{6,5},{7,4},{8,11},{9,10},{10,... | collective-permute-start | bytes 98312 | tf_op jit(solution)/shard_map/ppermute | solution.py:38
  37.6 4.2 %collective-permute-start.13 = (bf16[64,256]{1,0:T(8,128)(2,1)S(1)}, bf16[64,256]{1,0:T(8,128)(2,1)S(1)}, u32[]{:S(2)}, u32[]{:S(2)}) collective-permute-start(bf16[64,256]{1,0:T(8,128)(2,1)S(1)} %compact.1.refs_0_), channel_id=1, source_target_pairs={{0,2},{1,3},{2,0},{3,1},{4,6},{5,7},{6,4},{7,5},{8,10},{9,11},{10,... | collective-permute-start | bytes 98312 | tf_op jit(solution)/shard_map/ppermute | solution.py:38
  38.4 3.3 %collective-permute-start.12 = (bf16[64,256]{1,0:T(8,128)(2,1)S(1)}, bf16[64,256]{1,0:T(8,128)(2,1)S(1)}, u32[]{:S(2)}, u32[]{:S(2)}) collective-permute-start(bf16[64,256]{1,0:T(8,128)(2,1)S(1)} %compact.1.refs_0_), channel_id=1, source_target_pairs={{0,1},{1,0},{2,3},{3,2},{4,5},{5,4},{6,7},{7,6},{8,9},{9,8},{10,11... | collective-permute-start | bytes 98312 | tf_op jit(solution)/shard_map/ppermute | solution.py:38

commit v17 on v16

--- a/solution.py
+++ b/solution.py
@@ -314,7 +314,8 @@
     slots = -(-2 * tokens.shape[0] // (here * planes) // 128) * 128
     last = swapped[-1]
     pick = picked(ids, here, share, [(last[0], last[1], k) for k in range(share)], slots)
-    low, pick, *came = together(low, pick, *(swap(block, "tp", 1) for block in blocks[:half]))
+    low, pick = together(low, pick)
+    blocks[half], *came = together(blocks[half], *(swap(block, "tp", 1) for block in blocks[:half]))
 
     def both(low):
         bit = 1

time: 43.4 us -> 43.9 us (1.012)
  waiting for transfers between devices: 9.8 us -> 10.5 us
    ppermute x15, waiting for transfers between devices: 9.8 us -> 10.5 us  [swap(): lax.ppermute(x, axis, [(i, i ^ bit) for i in range(lax.axis_size(axis))])]
  transfers between devices with their start and end apart: 15 -> 15, of which waited for: 7 -> 8; matrix products, arithmetic and copies ran while one was open for 2% -> 2% of each run, Pallas kernels for 21% -> 21%
where the time goes in v17:
time: 43.9 us; the launch traced here: 43.6 us
  starting transfers between devices  16.6 us (38%)
  waiting for transfers between devices  10.5 us (24%)
  Pallas kernels  10.4 us (24%)
  local copies, waits for them, and re-layouts  5.84 us (13%)
    ppermute x15, starting transfers between devices, swap(): lax.ppermute(x, axis, [(i, i ^ bit) for i in range(lax.axis_size(axis))])  16.6 us
    ppermute x15, waiting for transfers between devices, swap(): lax.ppermute(x, axis, [(i, i ^ bit) for i in range(lax.axis_size(axis))])  10.5 us
    unnamed x18, local copies, waits for them, and re-layouts  4.11 us
    pallas_call x2, Pallas kernels, partials(): pl.pallas_call(functools.partial(partial_kernel, offsets, parts), in_spec...  3.65 us
    pallas_call x2, Pallas kernels, low_rows(): pl.pallas_call(functools.partial(low_kernel, groups, here, share, rank, b...  2.39 us
    pallas_call x1, Pallas kernels, final(): pl.pallas_call(final_kernel, in_specs=[VMEM] * (5 + len(kept)), out_specs...  1.36 us
    pallas_call x1, Pallas kernels, compact(): pl.pallas_call(compact_kernel, in_specs=[VMEM] * 3, out_specs=VMEM, out_s...  1.25 us
    dynamic_slice x1, local copies, waits for them, and re-layouts, local(): own = lax.dynamic_slice_in_dim(down, start, share, 0)  0.97 us
  transfers between devices with their start and end apart: 15, of which 8 were waited for; matrix products, arithmetic and copies ran while one was open for 2% of the time, Pallas kernels for 21%

profile of v17, /device:TPU:0, one launch (start us, length us, event | category | flops | bytes accessed | tf_op | source)
XLA Modules:
  0.0 43.6 jit_solution(4734877707520633591)
XLA Ops:
  0.0 1.0 %dynamic-slice_bitcast_fusion = bf16[1,64,2048]{2,1,0:T(8,128)(2,1)S(1)} fusion(bf16[2,2048,64]{1,2,0:T(8,128)(2,1)} %param.12, s32[]{:T(128)S(6)} %select_n.4), kind=kLoop, calls=%fused_computation.1 | loop fusion | bytes 524292 | tf_op jit(solution)/shard_map/dynamic_slice | solution.py:280
  1.0 3.1 %collective-permute-start = (bf16[1,64,2048]{2,1,0:T(8,128)(2,1)S(1)}, bf16[1,64,2048]{2,1,0:T(8,128)(2,1)S(1)}, u32[]{:S(2)}, u32[]{:S(2)}) collective-permute-start(bf16[1,64,2048]{2,1,0:T(8,128)(2,1)S(1)} %dynamic-slice_bitcast_fusion), channel_id=1, source_target_pairs={{0,4},{4,0},{8,12},{12,8},{1,5},{5,1},{9,13},{13,9},{2,6},{6,2},{1... | collective-permute-start | bytes 786440 | tf_op jit(solution)/shard_map/ppermute | solution.py:38
  4.1 0.8 %constant_dynamic-slice_fusion = bf16[1,64,256]{2,1,0:T(8,128)(2,1)S(1)} fusion(bf16[2,64,256]{2,1,0:T(8,128)(2,1)} %refs_0_.1, s32[]{:T(128)S(6)} %select_n.4), kind=kLoop, calls=%fused_computation.2 | loop fusion | bytes 65540 | tf_op jit(solution)/shard_map/dynamic_slice | solution.py:282
  4.8 2.7 %collective-permute-start.1 = (bf16[1,64,2304]{2,1,0:T(8,128)(2,1)S(1)}, bf16[1,64,2304]{2,1,0:T(8,128)(2,1)S(1)}, u32[]{:S(2)}, u32[]{:S(2)}) collective-permute-start(bf16[1,64,2304]{2,1,0:T(8,128)(2,1)S(1)} %pad_maximum_fusion), channel_id=1, source_target_pairs={{0,8},{4,12},{8,0},{12,4},{1,9},{5,13},{9,1},{13,5},{2,10},{6,14},... | collective-permute-start | bytes 884744 | tf_op jit(solution)/shard_map/ppermute | solution.py:38
  7.5 2.2 %copy-done = bf16[2048,1024]{1,0:T(8,128)(2,1)S(1)} copy-done((bf16[2048,1024]{1,0:T(8,128)(2,1)S(1)}, bf16[2048,1024]{1,0:T(8,128)(2,1)}, u32[]{:S(2)}) %copy-start) | copy-done | bytes 4194328
  9.7 1.9 %copy-done.1 = bf16[768,2048]{1,0:T(8,128)(2,1)S(1)} copy-done((bf16[768,2048]{1,0:T(8,128)(2,1)S(1)}, bf16[768,2048]{1,0:T(8,128)(2,1)}, u32[]{:S(2)}) %copy-start.1) | copy-done | bytes 3145752
  11.6 2.7 %partials.2 = (bf16[768,256]{1,0:T(8,128)(2,1)S(1)}, bf16[768,256]{1,0:T(8,128)(2,1)S(1)}, bf16[768,256]{1,0:T(8,128)(2,1)S(1)}) custom-call(bf16[768,2048]{1,0:T(8,128)(2,1)S(1)} %copy-done.1, bf16[2048,1024]{1,0:T(8,128)(2,1)S(1)} %copy-done), custom_call_target="tpu_custom_call" | custom-call | flops 4000000000 | bytes 1 | tf_op jit(solution)/shard_map/partials/pallas_call | solution.py:69
  14.3 0.5 %collective-permute-start.9 = (bf16[768,256]{1,0:T(8,128)(2,1)S(1)}, bf16[768,256]{1,0:T(8,128)(2,1)S(1)}, u32[]{:S(2)}, u32[]{:S(2)}) collective-permute-start(bf16[768,256]{1,0:T(8,128)(2,1)S(1)} %get-tuple-element.42), channel_id=1, source_target_pairs={{0,1},{1,0},{2,3},{3,2},{4,5},{5,4},{6,7},{7,6},{8,9},{9,8},{10,11... | collective-permute-start | bytes 1179656 | tf_op jit(solution)/shard_map/ppermute | solution.py:38
  14.8 0.2 collective-permute-done.refs_0_
  15.0 1.7 %collective-permute-start.2 = (bf16[1,64,2048]{2,1,0:T(8,128)(2,1)S(1)}, bf16[1,64,2048]{2,1,0:T(8,128)(2,1)S(1)}, u32[]{:S(2)}, u32[]{:S(2)}) collective-permute-start(bf16[1,64,2048]{2,1,0:T(8,128)(2,1)S(1)} %collective-permute-done.refs_0_), channel_id=1, source_target_pairs={{0,16},{16,0},{1,17},{17,1},{2,18},{18,2},{3,19},{19,3},{4,20},{20... | collective-permute-start | bytes 786440 | tf_op jit(solution)/shard_map/ppermute | solution.py:38
  16.7 1.0 %partials.3.refs_0_ = bf16[768,256]{1,0:T(8,128)(2,1)S(1)} custom-call(bf16[768,2048]{1,0:T(8,128)(2,1)S(1)} %copy-done.1, bf16[2048,1024]{1,0:T(8,128)(2,1)S(1)} %copy-done, bf16[768,256]{1,0:T(8,128)(2,1)S(1)} %get-tuple-element.28.refs_0_), custom_call_target="tpu_custom_call" | custom-call | flops 1 | bytes 1 | tf_op jit(solution)/shard_map/partials/pallas_call | solution.py:69
  17.7 2.9 %collective-permute-done.1.refs_1_ = bf16[1,64,2304]{2,1,0:T(8,128)(2,1)S(1)} collective-permute-done((bf16[1,64,2304]{2,1,0:T(8,128)(2,1)S(1)}, bf16[1,64,2304]{2,1,0:T(8,128)(2,1)S(1)}, u32[]{:S(2)}, u32[]{:S(2)}) %collective-permute-start.1) | collective-permute-done | bytes 294944 | tf_op jit(solution)/shard_map/ppermute | solution.py:38
  20.6 1.5 %collective-permute-start.5 = (bf16[1,64,2304]{2,1,0:T(8,128)(2,1)S(1)}, bf16[1,64,2304]{2,1,0:T(8,128)(2,1)S(1)}, u32[]{:S(2)}, u32[]{:S(2)}) collective-permute-start(bf16[1,64,2304]{2,1,0:T(8,128)(2,1)S(1)} %collective-permute-done.1.refs_1_), channel_id=1, source_target_pairs={{0,16},{16,0},{1,17},{17,1},{2,18},{18,2},{3,19},{19,3},{4,20},{20... | collective-permute-start | bytes 884744 | tf_op jit(solution)/shard_map/ppermute | solution.py:38
  22.2 0.4 picked.1.pick_ref
  22.7 1.6 %collective-permute-start.11 = (bf16[768,256]{1,0:T(8,128)(2,1)S(1)}, bf16[768,256]{1,0:T(8,128)(2,1)S(1)}, u32[]{:S(2)}, u32[]{:S(2)}) collective-permute-start(bf16[768,256]{1,0:T(8,128)(2,1)S(1)} %add.8), channel_id=1, source_target_pairs={{0,2},{1,3},{2,0},{3,1},{4,6},{5,7},{6,4},{7,5},{8,10},{9,11},{10,... | collective-permute-start | bytes 1179656 | tf_op jit(solution)/shard_map/ppermute | solution.py:38
  24.2 1.2 %low_rows.2.refs_2_ = f32[64,768]{1,0:T(8,128)S(1)} custom-call(s32[1,768]{1,0:T(1,128)S(1)} %bitcast.8, bf16[768,2048]{1,0:T(8,128)(2,1)S(1)} %copy-done.2, bf16[1,64,2048]{2,1,0:T(8,128)(2,1)S(1)} %collective-permute-done.refs_0_, bf16[1,64,2304]{2,1,0:T(8,128)(2,1)S(1)} %collective-permute-done.1.refs_1_, ...), custom_call_target="tpu_custom_call" | custom-call | flops 2000000000 | bytes 1 | tf_op jit(solution)/shard_map/low_rows/pallas_call | solution.py:124
  25.5 2.8 %collective-permute-done.3.refs_2_.refs_1_ = bf16[1,64,2304]{2,1,0:T(8,128)(2,1)S(1)} collective-permute-done((bf16[1,64,2304]{2,1,0:T(8,128)(2,1)S(1)}, bf16[1,64,2304]{2,1,0:T(8,128)(2,1)S(1)}, u32[]{:S(2)}, u32[]{:S(2)}) %collective-permute-start.3) | collective-permute-done | bytes 294944 | tf_op jit(solution)/shard_map/ppermute | solution.py:38
  28.2 1.5 %collective-permute-start.4 = (bf16[1,64,2304]{2,1,0:T(8,128)(2,1)S(1)}, bf16[1,64,2304]{2,1,0:T(8,128)(2,1)S(1)}, u32[]{:S(2)}, u32[]{:S(2)}) collective-permute-start(bf16[1,64,2304]{2,1,0:T(8,128)(2,1)S(1)} %collective-permute-done.3.refs_2_.refs_1_), channel_id=1, source_target_pairs={{0,16},{16,0},{1,17},{17,1},{2,18},{18,2},{3,19},{19,3},{4,20},{20... | collective-permute-start | bytes 884744 | tf_op jit(solution)/shard_map/ppermute | solution.py:38
  29.8 0.6 %collective-permute-done.5.refs_3_.refs_0_ = bf16[1,64,2304]{2,1,0:T(8,128)(2,1)S(1)} collective-permute-done((bf16[1,64,2304]{2,1,0:T(8,128)(2,1)S(1)}, bf16[1,64,2304]{2,1,0:T(8,128)(2,1)S(1)}, u32[]{:S(2)}, u32[]{:S(2)}) %collective-permute-start.5) | collective-permute-done | bytes 294944 | tf_op jit(solution)/shard_map/ppermute | solution.py:38
  30.3 1.2 %low_rows.3.refs_0_ = bf16[64,768]{1,0:T(8,128)(2,1)S(1)} custom-call(s32[1,768]{1,0:T(1,128)S(1)} %bitcast.9, bf16[768,2048]{1,0:T(8,128)(2,1)S(1)} %copy-done.2, bf16[1,64,2304]{2,1,0:T(8,128)(2,1)S(1)} %collective-permute-done.5.refs_3_.refs_0_, bf16[1,64,2304]{2,1,0:T(8,128)(2,1)S(1)} %collective-permute-done.3.refs_2_.refs_1_, ...), custom_call_target="tpu_custom_call" | custom-call | flops 5000000000 | bytes 1 | tf_op jit(solution)/shard_map/low_rows/pallas_call | solution.py:124
  31.6 0.5 %collective-permute-start.6 = (bf16[2,64,256]{2,1,0:T(8,128)(2,1)S(1)}, bf16[2,64,256]{2,1,0:T(8,128)(2,1)S(1)}, u32[]{:S(2)}, u32[]{:S(2)}) collective-permute-start(bf16[2,64,256]{2,1,0:T(8,128)(2,1)S(1)} %copy-done.4), channel_id=1, source_target_pairs={{0,4},{4,0},{8,12},{12,8},{1,5},{5,1},{9,13},{13,9},{2,6},{6,2},{1... | collective-permute-start | bytes 196616 | tf_op jit(solution)/shard_map/ppermute | solution.py:38
  32.1 0.5 %rotated_ups.1 = (bf16[320,256]{1,0:T(8,128)(2,1)S(1)}, bf16[768,512]{1,0:T(8,128)(2,1)S(1)}) custom-call(s32[1,768]{1,0:T(1,128)S(1)} %bitcast.10, s32[1,128]{1,0:T(1,128)S(1)} %bitcast.11, bf16[128,128]{1,0:T(8,128)(2,1)S(1)} %copy-done.3, bf16[2,64,256]{2,1,0:T(8,128)(2,1)S(1)} %copy-done.4, bf16[1,64,2304]{2,1,0:T(8,128)(2,1)S(1)} %collective-permute-done.1.refs_1_, ...), custom_call_target="tpu_custom_call" | custom-call | flops 1 | bytes 1 | tf_op jit(solution)/shard_map/rotated_ups/pallas_call | solution.py:152
  32.6 0.2 collective-permute-done.7.refs_1_
  32.9 1.5 %collective-permute-start.8 = (bf16[64,768]{1,0:T(8,128)(2,1)S(1)}, bf16[64,768]{1,0:T(8,128)(2,1)S(1)}, u32[]{:S(2)}, u32[]{:S(2)}) collective-permute-start(bf16[64,768]{1,0:T(8,128)(2,1)S(1)} %add.7.mine_ref), channel_id=1, source_target_pairs={{0,2},{1,3},{2,0},{3,1},{4,6},{5,7},{6,4},{7,5},{8,10},{9,11},{10,... | collective-permute-start | bytes 294920 | tf_op jit(solution)/shard_map/ppermute | solution.py:38
  34.4 1.7 %collective-permute-done.6.near_ref = bf16[2,64,256]{2,1,0:T(8,128)(2,1)S(1)} collective-permute-done((bf16[2,64,256]{2,1,0:T(8,128)(2,1)S(1)}, bf16[2,64,256]{2,1,0:T(8,128)(2,1)S(1)}, u32[]{:S(2)}, u32[]{:S(2)}) %collective-permute-start.6) | collective-permute-done | bytes 65568 | tf_op jit(solution)/shard_map/ppermute | solution.py:38
  36.1 1.2 %compact.1.refs_0_ = bf16[64,256]{1,0:T(8,128)(2,1)S(1)} custom-call(bf16[768,2048]{1,0:T(8,128)(2,1)S(1)} %copy-done.2, bf16[1,64,2304]{2,1,0:T(8,128)(2,1)S(1)} %collective-permute-done.4.piece_ref, bf16[768,256]{1,0:T(8,128)(2,1)S(1)} %picked.1.pick_ref), custom_call_target="tpu_custom_call" | custom-call | flops 2000000000 | bytes 1 | tf_op jit(solution)/shard_map/compact/pallas_call | solution.py:201
  37.4 1.5 %collective-permute-start.13 = (bf16[64,256]{1,0:T(8,128)(2,1)S(1)}, bf16[64,256]{1,0:T(8,128)(2,1)S(1)}, u32[]{:S(2)}, u32[]{:S(2)}) collective-permute-start(bf16[64,256]{1,0:T(8,128)(2,1)S(1)} %compact.1.refs_0_), channel_id=1, source_target_pairs={{0,2},{1,3},{2,0},{3,1},{4,6},{5,7},{6,4},{7,5},{8,10},{9,11},{10,... | collective-permute-start | bytes 98312 | tf_op jit(solution)/shard_map/ppermute | solution.py:38
  38.9 0.4 collective-permute-start.14
  39.3 0.8 %most.1.most_ref = f32[768,256]{1,0:T(8,128)S(1)} custom-call(bf16[64,768]{1,0:T(8,128)(2,1)S(1)} %add.7.mine_ref, bf16[64,768]{1,0:T(8,128)(2,1)S(1)} %collective-permute-done.8.theirs_ref, bf16[320,256]{1,0:T(8,128)(2,1)S(1)} %get-tuple-element.38.up_ref, bf16[768,512]{1,0:T(8,128)(2,1)S(1)} %get-tuple-element.39.mask_ref, ...), custom_call_target="tpu_custom_call" | custom-call | flops 1 | bytes 1 | tf_op jit(solution)/shard_map/most/pallas_call | solution.py:230
  40.1 1.3 %collective-permute-done.13.refs_2_ = bf16[64,256]{1,0:T(8,128)(2,1)S(1)} collective-permute-done((bf16[64,256]{1,0:T(8,128)(2,1)S(1)}, bf16[64,256]{1,0:T(8,128)(2,1)S(1)}, u32[]{:S(2)}, u32[]{:S(2)}) %collective-permute-start.13) | collective-permute-done | bytes 32800 | tf_op jit(solution)/shard_map/ppermute | solution.py:38
  41.4 0.9 %collective-permute-done.14.refs_3_ = bf16[64,256]{1,0:T(8,128)(2,1)S(1)} collective-permute-done((bf16[64,256]{1,0:T(8,128)(2,1)S(1)}, bf16[64,256]{1,0:T(8,128)(2,1)S(1)}, u32[]{:S(2)}, u32[]{:S(2)}) %collective-permute-start.14) | collective-permute-done | bytes 32800 | tf_op jit(solution)/shard_map/ppermute | solution.py:38
  42.3 1.4 %final.1 = bf16[768,256]{1,0:T(8,128)(2,1)} custom-call(bf16[768,256]{1,0:T(8,128)(2,1)S(1)} %picked.1.pick_ref, bf16[1,64,2304]{2,1,0:T(8,128)(2,1)S(1)} %collective-permute-done.4.piece_ref, s32[1,128]{1,0:T(1,128)S(1)} %bitcast.13, bf16[128,128]{1,0:T(8,128)(2,1)S(1)} %copy-done.3, f32[768,256]{1,0:T(8,128)S(1)} %most.1.most_ref, ...), custom_call_target="tpu_custom_call" | custom-call | flops 1 | bytes 1 | tf_op jit(solution)/shard_map/final/pallas_call | solution.py:258
  (30 shorter events, 0.4 us)
Async XLA Ops:
  1.0 14.1 %collective-permute-start = (bf16[1,64,2048]{2,1,0:T(8,128)(2,1)S(1)}, bf16[1,64,2048]{2,1,0:T(8,128)(2,1)S(1)}, u32[]{:S(2)}, u32[]{:S(2)}) collective-permute-start(bf16[1,64,2048]{2,1,0:T(8,128)(2,1)S(1)} %dynamic-slice_bitcast_fusion), channel_id=1, source_target_pairs={{0,4},{4,0},{8,12},{12,8},{1,5},{5,1},{9,13},{13,9},{2,6},{6,2},{1... | collective-permute-start | bytes 786440 | tf_op jit(solution)/shard_map/ppermute | solution.py:38
  4.8 15.8 %collective-permute-start.1 = (bf16[1,64,2304]{2,1,0:T(8,128)(2,1)S(1)}, bf16[1,64,2304]{2,1,0:T(8,128)(2,1)S(1)}, u32[]{:S(2)}, u32[]{:S(2)}) collective-permute-start(bf16[1,64,2304]{2,1,0:T(8,128)(2,1)S(1)} %pad_maximum_fusion), channel_id=1, source_target_pairs={{0,8},{4,12},{8,0},{12,4},{1,9},{5,13},{9,1},{13,5},{2,10},{6,14},... | collective-permute-start | bytes 884744 | tf_op jit(solution)/shard_map/ppermute | solution.py:38
  7.5 2.2 %copy-start = (bf16[2048,1024]{1,0:T(8,128)(2,1)S(1)}, bf16[2048,1024]{1,0:T(8,128)(2,1)}, u32[]{:S(2)}) copy-start(bf16[2048,1024]{1,0:T(8,128)(2,1)} %weight_ref.3) | copy-start | bytes 12582916
  9.7 1.9 %copy-start.1 = (bf16[768,2048]{1,0:T(8,128)(2,1)S(1)}, bf16[768,2048]{1,0:T(8,128)(2,1)}, u32[]{:S(2)}) copy-start(bf16[768,2048]{1,0:T(8,128)(2,1)} %tokens_ref.9) | copy-start | bytes 9437188
  14.2 7.9 %copy-start.6 = (s32[768,1]{0,1:T(1,128)S(1)}, s32[768,1]{0,1:T(1,128)}, u32[]{:S(2)}) copy-start(s32[768,1]{0,1:T(1,128)} %param.9) | copy-start | bytes 9220
  14.3 8.3 %collective-permute-start.10 = (bf16[768,256]{1,0:T(8,128)(2,1)S(1)}, bf16[768,256]{1,0:T(8,128)(2,1)S(1)}, u32[]{:S(2)}, u32[]{:S(2)}) collective-permute-start(bf16[768,256]{1,0:T(8,128)(2,1)S(1)} %get-tuple-element.43), channel_id=1, source_target_pairs={{0,1},{1,0},{2,3},{3,2},{4,5},{5,4},{6,7},{7,6},{8,9},{9,8},{10,11... | collective-permute-start | bytes 1179656 | tf_op jit(solution)/shard_map/ppermute | solution.py:38
  14.3 8.2 %collective-permute-start.9 = (bf16[768,256]{1,0:T(8,128)(2,1)S(1)}, bf16[768,256]{1,0:T(8,128)(2,1)S(1)}, u32[]{:S(2)}, u32[]{:S(2)}) collective-permute-start(bf16[768,256]{1,0:T(8,128)(2,1)S(1)} %get-tuple-element.42), channel_id=1, source_target_pairs={{0,1},{1,0},{2,3},{3,2},{4,5},{5,4},{6,7},{7,6},{8,9},{9,8},{10,11... | collective-permute-start | bytes 1179656 | tf_op jit(solution)/shard_map/ppermute | solution.py:38
  15.0 9.2 %copy-start.2 = (bf16[768,2048]{1,0:T(8,128)(2,1)S(1)}, bf16[768,2048]{1,0:T(8,128)(2,1)}, u32[]{:S(2)}) copy-start(bf16[768,2048]{1,0:T(8,128)(2,1)} %tokens_ref.9) | copy-start | bytes 9437188
  15.0 9.2 %copy-start.5 = (bf16[2,2048,64]{1,2,0:T(8,128)(2,1)S(1)}, bf16[2,2048,64]{1,2,0:T(8,128)(2,1)}, u32[]{:S(2)}) copy-start(bf16[2,2048,64]{1,2,0:T(8,128)(2,1)} %param.12) | copy-start | bytes 1572868
  15.0 9.2 %collective-permute-start.2 = (bf16[1,64,2048]{2,1,0:T(8,128)(2,1)S(1)}, bf16[1,64,2048]{2,1,0:T(8,128)(2,1)S(1)}, u32[]{:S(2)}, u32[]{:S(2)}) collective-permute-start(bf16[1,64,2048]{2,1,0:T(8,128)(2,1)S(1)} %collective-permute-done.refs_0_), channel_id=1, source_target_pairs={{0,16},{16,0},{1,17},{17,1},{2,18},{18,2},{3,19},{19,3},{4,20},{20... | collective-permute-start | bytes 786440 | tf_op jit(solution)/shard_map/ppermute | solution.py:38
  20.6 7.6 %collective-permute-start.3 = (bf16[1,64,2304]{2,1,0:T(8,128)(2,1)S(1)}, bf16[1,64,2304]{2,1,0:T(8,128)(2,1)S(1)}, u32[]{:S(2)}, u32[]{:S(2)}) collective-permute-start(bf16[1,64,2304]{2,1,0:T(8,128)(2,1)S(1)} %collective-permute-done.1.refs_1_), channel_id=1, source_target_pairs={{0,4},{4,0},{8,12},{12,8},{1,5},{5,1},{9,13},{13,9},{2,6},{6,2},{1... | collective-permute-start | bytes 884744 | tf_op jit(solution)/shard_map/ppermute | solution.py:38
  20.6 9.7 %collective-permute-start.5 = (bf16[1,64,2304]{2,1,0:T(8,128)(2,1)S(1)}, bf16[1,64,2304]{2,1,0:T(8,128)(2,1)S(1)}, u32[]{:S(2)}, u32[]{:S(2)}) collective-permute-start(bf16[1,64,2304]{2,1,0:T(8,128)(2,1)S(1)} %collective-permute-done.1.refs_1_), channel_id=1, source_target_pairs={{0,16},{16,0},{1,17},{17,1},{2,18},{18,2},{3,19},{19,3},{4,20},{20... | collective-permute-start | bytes 884744 | tf_op jit(solution)/shard_map/ppermute | solution.py:38
  22.7 16.6 %collective-permute-start.11 = (bf16[768,256]{1,0:T(8,128)(2,1)S(1)}, bf16[768,256]{1,0:T(8,128)(2,1)S(1)}, u32[]{:S(2)}, u32[]{:S(2)}) collective-permute-start(bf16[768,256]{1,0:T(8,128)(2,1)S(1)} %add.8), channel_id=1, source_target_pairs={{0,2},{1,3},{2,0},{3,1},{4,6},{5,7},{6,4},{7,5},{8,10},{9,11},{10,... | collective-permute-start | bytes 1179656 | tf_op jit(solution)/shard_map/ppermute | solution.py:38
  25.5 6.1 %copy-start.4 = (bf16[2,64,256]{2,1,0:T(8,128)(2,1)S(1)}, bf16[2,64,256]{2,1,0:T(8,128)(2,1)}, u32[]{:S(2)}) copy-start(bf16[2,64,256]{2,1,0:T(8,128)(2,1)} %refs_0_.1) | copy-start | bytes 196612
  25.5 6.6 %copy-start.3 = (bf16[128,128]{1,0:T(8,128)(2,1)S(1)}, bf16[128,128]{1,0:T(8,128)(2,1)}, u32[]{:S(2)}) copy-start(bf16[128,128]{1,0:T(8,128)(2,1)} %constant.12.clone.matrix_ref) | copy-start | bytes 98308
  25.5 6.6 %copy-start.7 = (s32[128]{0:T(128)S(1)}, s32[128]{0:T(128)}, u32[]{:S(2)}) copy-start(s32[128]{0:T(128)} %param.14) | copy-start | bytes 1540
  28.2 7.8 %collective-permute-start.4 = (bf16[1,64,2304]{2,1,0:T(8,128)(2,1)S(1)}, bf16[1,64,2304]{2,1,0:T(8,128)(2,1)S(1)}, u32[]{:S(2)}, u32[]{:S(2)}) collective-permute-start(bf16[1,64,2304]{2,1,0:T(8,128)(2,1)S(1)} %collective-permute-done.3.refs_2_.refs_1_), channel_id=1, source_target_pairs={{0,16},{16,0},{1,17},{17,1},{2,18},{18,2},{3,19},{19,3},{4,20},{20... | collective-permute-start | bytes 884744 | tf_op jit(solution)/shard_map/ppermute | solution.py:38
  31.5 1.4 %collective-permute-start.7 = (bf16[64,768]{1,0:T(8,128)(2,1)S(1)}, bf16[64,768]{1,0:T(8,128)(2,1)S(1)}, u32[]{:S(2)}, u32[]{:S(2)}) collective-permute-start(bf16[64,768]{1,0:T(8,128)(2,1)S(1)} %low_rows.3.refs_0_), channel_id=1, source_target_pairs={{0,1},{1,0},{2,3},{3,2},{4,5},{5,4},{6,7},{7,6},{8,9},{9,8},{10,11... | collective-permute-start | bytes 294920 | tf_op jit(solution)/shard_map/ppermute | solution.py:38
  31.6 4.5 %collective-permute-start.6 = (bf16[2,64,256]{2,1,0:T(8,128)(2,1)S(1)}, bf16[2,64,256]{2,1,0:T(8,128)(2,1)S(1)}, u32[]{:S(2)}, u32[]{:S(2)}) collective-permute-start(bf16[2,64,256]{2,1,0:T(8,128)(2,1)S(1)} %copy-done.4), channel_id=1, source_target_pairs={{0,4},{4,0},{8,12},{12,8},{1,5},{5,1},{9,13},{13,9},{2,6},{6,2},{1... | collective-permute-start | bytes 196616 | tf_op jit(solution)/shard_map/ppermute | solution.py:38
  32.1 7.2 %copy-start.8 = (f32[256]{0:T(256)S(1)}, f32[256]{0:T(256)}, u32[]{:S(2)}) copy-start(f32[256]{0:T(256)} %param.11) | copy-start | bytes 3076
  32.9 6.4 %collective-permute-start.8 = (bf16[64,768]{1,0:T(8,128)(2,1)S(1)}, bf16[64,768]{1,0:T(8,128)(2,1)S(1)}, u32[]{:S(2)}, u32[]{:S(2)}) collective-permute-start(bf16[64,768]{1,0:T(8,128)(2,1)S(1)} %add.7.mine_ref), channel_id=1, source_target_pairs={{0,2},{1,3},{2,0},{3,1},{4,6},{5,7},{6,4},{7,5},{8,10},{9,11},{10,... | collective-permute-start | bytes 294920 | tf_op jit(solution)/shard_map/ppermute | solution.py:38
  37.3 2.7 %collective-permute-start.12 = (bf16[64,256]{1,0:T(8,128)(2,1)S(1)}, bf16[64,256]{1,0:T(8,128)(2,1)S(1)}, u32[]{:S(2)}, u32[]{:S(2)}) collective-permute-start(bf16[64,256]{1,0:T(8,128)(2,1)S(1)} %compact.1.refs_0_), channel_id=1, source_target_pairs={{0,1},{1,0},{2,3},{3,2},{4,5},{5,4},{6,7},{7,6},{8,9},{9,8},{10,11... | collective-permute-start | bytes 98312 | tf_op jit(solution)/shard_map/ppermute | solution.py:38
  37.4 4.0 %collective-permute-start.13 = (bf16[64,256]{1,0:T(8,128)(2,1)S(1)}, bf16[64,256]{1,0:T(8,128)(2,1)S(1)}, u32[]{:S(2)}, u32[]{:S(2)}) collective-permute-start(bf16[64,256]{1,0:T(8,128)(2,1)S(1)} %compact.1.refs_0_), channel_id=1, source_target_pairs={{0,2},{1,3},{2,0},{3,1},{4,6},{5,7},{6,4},{7,5},{8,10},{9,11},{10,... | collective-permute-start | bytes 98312 | tf_op jit(solution)/shard_map/ppermute | solution.py:38
  38.9 3.3 %collective-permute-start.14 = (bf16[64,256]{1,0:T(8,128)(2,1)S(1)}, bf16[64,256]{1,0:T(8,128)(2,1)S(1)}, u32[]{:S(2)}, u32[]{:S(2)}) collective-permute-start(bf16[64,256]{1,0:T(8,128)(2,1)S(1)} %compact.1.refs_0_), channel_id=1, source_target_pairs={{0,3},{1,2},{2,1},{3,0},{4,7},{5,6},{6,5},{7,4},{8,11},{9,10},{10,... | collective-permute-start | bytes 98312 | tf_op jit(solution)/shard_map/ppermute | solution.py:38

commit v18 on v16

--- a/solution.py
+++ b/solution.py
@@ -344,7 +344,7 @@
     arrays = [adapter_up] + [piece for *_, piece in far]
     up, mask = rotated_ups(ids, bits, matrix, here, share, named, ups, arrays, width)
 
-    piece, up, mask, near_up = together(last[2], up, mask, near_up)
+    piece, up, mask = together(last[2], up, mask)
     kept = compact(tokens, piece, pick)
     kept = [kept] + [swap(kept, "tp", offset) for offset in range(1, parts)]
     rest = most(low, other, up, mask, near_up, scale, bits, matrix, sums[0])

time: 43.4 us -> 42.1 us (0.970)
  waiting for transfers between devices: 9.8 us -> 8.52 us
    ppermute x15, waiting for transfers between devices: 9.8 us -> 8.52 us  [swap(): lax.ppermute(x, axis, [(i, i ^ bit) for i in range(lax.axis_size(axis))])]
  transfers between devices with their start and end apart: 15 -> 15, of which waited for: 7 -> 7; matrix products, arithmetic and copies ran while one was open for 2% -> 2% of each run, Pallas kernels for 21% -> 22%
where the time goes in v18:
time: 42.1 us; the launch traced here: 41.8 us
  starting transfers between devices  16.8 us (40%)
  Pallas kernels  10.5 us (25%)
  waiting for transfers between devices  8.52 us (20%)
  local copies, waits for them, and re-layouts  5.84 us (14%)
    ppermute x15, starting transfers between devices, swap(): lax.ppermute(x, axis, [(i, i ^ bit) for i in range(lax.axis_size(axis))])  16.8 us
    ppermute x15, waiting for transfers between devices, swap(): lax.ppermute(x, axis, [(i, i ^ bit) for i in range(lax.axis_size(axis))])  8.52 us
    unnamed x18, local copies, waits for them, and re-layouts  4.11 us
    pallas_call x2, Pallas kernels, partials(): pl.pallas_call(functools.partial(partial_kernel, offsets, parts), in_spec...  3.67 us
    pallas_call x2, Pallas kernels, low_rows(): pl.pallas_call(functools.partial(low_kernel, groups, here, share, rank, b...  2.39 us
    pallas_call x1, Pallas kernels, final(): pl.pallas_call(final_kernel, in_specs=[VMEM] * (5 + len(kept)), out_specs...  1.35 us
    pallas_call x1, Pallas kernels, compact(): pl.pallas_call(compact_kernel, in_specs=[VMEM] * 3, out_specs=VMEM, out_s...  1.25 us
    dynamic_slice x1, local copies, waits for them, and re-layouts, local(): own = lax.dynamic_slice_in_dim(down, start, share, 0)  0.97 us
  transfers between devices with their start and end apart: 15, of which 7 were waited for; matrix products, arithmetic and copies ran while one was open for 2% of the time, Pallas kernels for 22%

profile of v18, /device:TPU:0, one launch (start us, length us, event | category | flops | bytes accessed | tf_op | source)
XLA Modules:
  0.0 41.8 jit_solution(16204271474940082374)
XLA Ops:
  0.0 1.0 %dynamic-slice_bitcast_fusion = bf16[1,64,2048]{2,1,0:T(8,128)(2,1)S(1)} fusion(bf16[2,2048,64]{1,2,0:T(8,128)(2,1)} %param.12, s32[]{:T(128)S(6)} %select_n.4), kind=kLoop, calls=%fused_computation.1 | loop fusion | bytes 524292 | tf_op jit(solution)/shard_map/dynamic_slice | solution.py:280
  1.0 3.1 %collective-permute-start = (bf16[1,64,2048]{2,1,0:T(8,128)(2,1)S(1)}, bf16[1,64,2048]{2,1,0:T(8,128)(2,1)S(1)}, u32[]{:S(2)}, u32[]{:S(2)}) collective-permute-start(bf16[1,64,2048]{2,1,0:T(8,128)(2,1)S(1)} %dynamic-slice_bitcast_fusion), channel_id=1, source_target_pairs={{0,4},{4,0},{8,12},{12,8},{1,5},{5,1},{9,13},{13,9},{2,6},{6,2},{1... | collective-permute-start | bytes 786440 | tf_op jit(solution)/shard_map/ppermute | solution.py:38
  4.1 0.8 %constant_dynamic-slice_fusion = bf16[1,64,256]{2,1,0:T(8,128)(2,1)S(1)} fusion(bf16[2,64,256]{2,1,0:T(8,128)(2,1)} %refs_0_.1, s32[]{:T(128)S(6)} %select_n.4), kind=kLoop, calls=%fused_computation.2 | loop fusion | bytes 65540 | tf_op jit(solution)/shard_map/dynamic_slice | solution.py:282
  4.8 2.7 %collective-permute-start.1 = (bf16[1,64,2304]{2,1,0:T(8,128)(2,1)S(1)}, bf16[1,64,2304]{2,1,0:T(8,128)(2,1)S(1)}, u32[]{:S(2)}, u32[]{:S(2)}) collective-permute-start(bf16[1,64,2304]{2,1,0:T(8,128)(2,1)S(1)} %pad_maximum_fusion), channel_id=1, source_target_pairs={{0,8},{4,12},{8,0},{12,4},{1,9},{5,13},{9,1},{13,5},{2,10},{6,14},... | collective-permute-start | bytes 884744 | tf_op jit(solution)/shard_map/ppermute | solution.py:38
  7.5 2.2 %copy-done = bf16[2048,1024]{1,0:T(8,128)(2,1)S(1)} copy-done((bf16[2048,1024]{1,0:T(8,128)(2,1)S(1)}, bf16[2048,1024]{1,0:T(8,128)(2,1)}, u32[]{:S(2)}) %copy-start) | copy-done | bytes 4194328
  9.7 1.9 %copy-done.1 = bf16[768,2048]{1,0:T(8,128)(2,1)S(1)} copy-done((bf16[768,2048]{1,0:T(8,128)(2,1)S(1)}, bf16[768,2048]{1,0:T(8,128)(2,1)}, u32[]{:S(2)}) %copy-start.1) | copy-done | bytes 3145752
  11.6 2.7 %partials.2 = (bf16[768,256]{1,0:T(8,128)(2,1)S(1)}, bf16[768,256]{1,0:T(8,128)(2,1)S(1)}, bf16[768,256]{1,0:T(8,128)(2,1)S(1)}) custom-call(bf16[768,2048]{1,0:T(8,128)(2,1)S(1)} %copy-done.1, bf16[2048,1024]{1,0:T(8,128)(2,1)S(1)} %copy-done), custom_call_target="tpu_custom_call" | custom-call | flops 4000000000 | bytes 1 | tf_op jit(solution)/shard_map/partials/pallas_call | solution.py:69
  14.3 0.8 %collective-permute-done.refs_0_ = bf16[1,64,2048]{2,1,0:T(8,128)(2,1)S(1)} collective-permute-done((bf16[1,64,2048]{2,1,0:T(8,128)(2,1)S(1)}, bf16[1,64,2048]{2,1,0:T(8,128)(2,1)S(1)}, u32[]{:S(2)}, u32[]{:S(2)}) %collective-permute-start) | collective-permute-done | bytes 262176 | tf_op jit(solution)/shard_map/ppermute | solution.py:38
  15.0 1.7 %collective-permute-start.2 = (bf16[1,64,2048]{2,1,0:T(8,128)(2,1)S(1)}, bf16[1,64,2048]{2,1,0:T(8,128)(2,1)S(1)}, u32[]{:S(2)}, u32[]{:S(2)}) collective-permute-start(bf16[1,64,2048]{2,1,0:T(8,128)(2,1)S(1)} %collective-permute-done.refs_0_), channel_id=1, source_target_pairs={{0,16},{16,0},{1,17},{17,1},{2,18},{18,2},{3,19},{19,3},{4,20},{20... | collective-permute-start | bytes 786440 | tf_op jit(solution)/shard_map/ppermute | solution.py:38
  16.7 0.5 %collective-permute-start.4 = (bf16[768,256]{1,0:T(8,128)(2,1)S(1)}, bf16[768,256]{1,0:T(8,128)(2,1)S(1)}, u32[]{:S(2)}, u32[]{:S(2)}) collective-permute-start(bf16[768,256]{1,0:T(8,128)(2,1)S(1)} %get-tuple-element.30), channel_id=1, source_target_pairs={{0,1},{1,0},{2,3},{3,2},{4,5},{5,4},{6,7},{7,6},{8,9},{9,8},{10,11... | collective-permute-start | bytes 1179656 | tf_op jit(solution)/shard_map/ppermute | solution.py:38
  17.2 1.0 %partials.3.refs_0_ = bf16[768,256]{1,0:T(8,128)(2,1)S(1)} custom-call(bf16[768,2048]{1,0:T(8,128)(2,1)S(1)} %copy-done.1, bf16[2048,1024]{1,0:T(8,128)(2,1)S(1)} %copy-done, bf16[768,256]{1,0:T(8,128)(2,1)S(1)} %get-tuple-element.26.refs_0_), custom_call_target="tpu_custom_call" | custom-call | flops 1 | bytes 1 | tf_op jit(solution)/shard_map/partials/pallas_call | solution.py:69
  18.2 2.4 %collective-permute-done.1.refs_1_ = bf16[1,64,2304]{2,1,0:T(8,128)(2,1)S(1)} collective-permute-done((bf16[1,64,2304]{2,1,0:T(8,128)(2,1)S(1)}, bf16[1,64,2304]{2,1,0:T(8,128)(2,1)S(1)}, u32[]{:S(2)}, u32[]{:S(2)}) %collective-permute-start.1) | collective-permute-done | bytes 294944 | tf_op jit(solution)/shard_map/ppermute | solution.py:38
  20.6 1.5 %collective-permute-start.7 = (bf16[1,64,2304]{2,1,0:T(8,128)(2,1)S(1)}, bf16[1,64,2304]{2,1,0:T(8,128)(2,1)S(1)}, u32[]{:S(2)}, u32[]{:S(2)}) collective-permute-start(bf16[1,64,2304]{2,1,0:T(8,128)(2,1)S(1)} %collective-permute-done.1.refs_1_), channel_id=1, source_target_pairs={{0,16},{16,0},{1,17},{17,1},{2,18},{18,2},{3,19},{19,3},{4,20},{20... | collective-permute-start | bytes 884744 | tf_op jit(solution)/shard_map/ppermute | solution.py:38
  22.2 0.4 picked.1.pick_ref
  22.5 0.5 %collective-permute-done.2.refs_2_ = bf16[1,64,2048]{2,1,0:T(8,128)(2,1)S(1)} collective-permute-done((bf16[1,64,2048]{2,1,0:T(8,128)(2,1)S(1)}, bf16[1,64,2048]{2,1,0:T(8,128)(2,1)S(1)}, u32[]{:S(2)}, u32[]{:S(2)}) %collective-permute-start.2) | collective-permute-done | bytes 262176 | tf_op jit(solution)/shard_map/ppermute | solution.py:38
  23.0 1.2 %low_rows.2.refs_2_ = f32[64,768]{1,0:T(8,128)S(1)} custom-call(s32[1,768]{1,0:T(1,128)S(1)} %bitcast.8, bf16[768,2048]{1,0:T(8,128)(2,1)S(1)} %copy-done.2, bf16[1,64,2048]{2,1,0:T(8,128)(2,1)S(1)} %collective-permute-done.refs_0_, bf16[1,64,2304]{2,1,0:T(8,128)(2,1)S(1)} %collective-permute-done.1.refs_1_, ...), custom_call_target="tpu_custom_call" | custom-call | flops 2000000000 | bytes 1 | tf_op jit(solution)/shard_map/low_rows/pallas_call | solution.py:124
  24.3 0.1 add.8
  24.4 1.3 %collective-permute-start.11 = (bf16[768,256]{1,0:T(8,128)(2,1)S(1)}, bf16[768,256]{1,0:T(8,128)(2,1)S(1)}, u32[]{:S(2)}, u32[]{:S(2)}) collective-permute-start(bf16[768,256]{1,0:T(8,128)(2,1)S(1)} %add.8), channel_id=1, source_target_pairs={{0,2},{1,3},{2,0},{3,1},{4,6},{5,7},{6,4},{7,5},{8,10},{9,11},{10,... | collective-permute-start | bytes 1179656 | tf_op jit(solution)/shard_map/ppermute | solution.py:38
  25.7 2.6 %collective-permute-done.5.refs_2_.refs_1_ = bf16[1,64,2304]{2,1,0:T(8,128)(2,1)S(1)} collective-permute-done((bf16[1,64,2304]{2,1,0:T(8,128)(2,1)S(1)}, bf16[1,64,2304]{2,1,0:T(8,128)(2,1)S(1)}, u32[]{:S(2)}, u32[]{:S(2)}) %collective-permute-start.5) | collective-permute-done | bytes 294944 | tf_op jit(solution)/shard_map/ppermute | solution.py:38
  28.2 1.5 %collective-permute-start.6 = (bf16[1,64,2304]{2,1,0:T(8,128)(2,1)S(1)}, bf16[1,64,2304]{2,1,0:T(8,128)(2,1)S(1)}, u32[]{:S(2)}, u32[]{:S(2)}) collective-permute-start(bf16[1,64,2304]{2,1,0:T(8,128)(2,1)S(1)} %collective-permute-done.5.refs_2_.refs_1_), channel_id=1, source_target_pairs={{0,16},{16,0},{1,17},{17,1},{2,18},{18,2},{3,19},{19,3},{4,20},{20... | collective-permute-start | bytes 884744 | tf_op jit(solution)/shard_map/ppermute | solution.py:38
  29.8 1.2 %low_rows.3.refs_0_ = bf16[64,768]{1,0:T(8,128)(2,1)S(1)} custom-call(s32[1,768]{1,0:T(1,128)S(1)} %bitcast.9, bf16[768,2048]{1,0:T(8,128)(2,1)S(1)} %copy-done.2, bf16[1,64,2304]{2,1,0:T(8,128)(2,1)S(1)} %collective-permute-done.7.refs_3_.refs_0_, bf16[1,64,2304]{2,1,0:T(8,128)(2,1)S(1)} %collective-permute-done.5.refs_2_.refs_1_, ...), custom_call_target="tpu_custom_call" | custom-call | flops 5000000000 | bytes 1 | tf_op jit(solution)/shard_map/low_rows/pallas_call | solution.py:124
  31.0 1.0 %collective-permute-start.10 = (bf16[2,64,256]{2,1,0:T(8,128)(2,1)S(1)}, bf16[2,64,256]{2,1,0:T(8,128)(2,1)S(1)}, u32[]{:S(2)}, u32[]{:S(2)}) collective-permute-start(bf16[2,64,256]{2,1,0:T(8,128)(2,1)S(1)} %copy-done.4), channel_id=1, source_target_pairs={{0,4},{4,0},{8,12},{12,8},{1,5},{5,1},{9,13},{13,9},{2,6},{6,2},{1... | collective-permute-start | bytes 196616 | tf_op jit(solution)/shard_map/ppermute | solution.py:38
  32.1 0.5 %rotated_ups.1 = (bf16[320,256]{1,0:T(8,128)(2,1)S(1)}, bf16[768,512]{1,0:T(8,128)(2,1)S(1)}) custom-call(s32[1,768]{1,0:T(1,128)S(1)} %bitcast.10, s32[1,128]{1,0:T(1,128)S(1)} %bitcast.11, bf16[128,128]{1,0:T(8,128)(2,1)S(1)} %copy-done.3, bf16[2,64,256]{2,1,0:T(8,128)(2,1)S(1)} %copy-done.4, bf16[1,64,2304]{2,1,0:T(8,128)(2,1)S(1)} %collective-permute-done.1.refs_1_, ...), custom_call_target="tpu_custom_call" | custom-call | flops 1 | bytes 1 | tf_op jit(solution)/shard_map/rotated_ups/pallas_call | solution.py:152
  32.7 1.6 %collective-permute-start.9 = (bf16[64,768]{1,0:T(8,128)(2,1)S(1)}, bf16[64,768]{1,0:T(8,128)(2,1)S(1)}, u32[]{:S(2)}, u32[]{:S(2)}) collective-permute-start(bf16[64,768]{1,0:T(8,128)(2,1)S(1)} %add.7.mine_ref), channel_id=1, source_target_pairs={{0,2},{1,3},{2,0},{3,1},{4,6},{5,7},{6,4},{7,5},{8,10},{9,11},{10,... | collective-permute-start | bytes 294920 | tf_op jit(solution)/shard_map/ppermute | solution.py:38
  34.2 0.9 %collective-permute-done.6.piece_ref = bf16[1,64,2304]{2,1,0:T(8,128)(2,1)S(1)} collective-permute-done((bf16[1,64,2304]{2,1,0:T(8,128)(2,1)S(1)}, bf16[1,64,2304]{2,1,0:T(8,128)(2,1)S(1)}, u32[]{:S(2)}, u32[]{:S(2)}) %collective-permute-start.6) | collective-permute-done | bytes 294944 | tf_op jit(solution)/shard_map/ppermute | solution.py:38
  35.2 1.2 %compact.1.refs_0_ = bf16[64,256]{1,0:T(8,128)(2,1)S(1)} custom-call(bf16[768,2048]{1,0:T(8,128)(2,1)S(1)} %copy-done.2, bf16[1,64,2304]{2,1,0:T(8,128)(2,1)S(1)} %collective-permute-done.6.piece_ref, bf16[768,256]{1,0:T(8,128)(2,1)S(1)} %picked.1.pick_ref), custom_call_target="tpu_custom_call" | custom-call | flops 2000000000 | bytes 1 | tf_op jit(solution)/shard_map/compact/pallas_call | solution.py:201
  36.5 1.4 %collective-permute-start.13 = (bf16[64,256]{1,0:T(8,128)(2,1)S(1)}, bf16[64,256]{1,0:T(8,128)(2,1)S(1)}, u32[]{:S(2)}, u32[]{:S(2)}) collective-permute-start(bf16[64,256]{1,0:T(8,128)(2,1)S(1)} %compact.1.refs_0_), channel_id=1, source_target_pairs={{0,2},{1,3},{2,0},{3,1},{4,6},{5,7},{6,4},{7,5},{8,10},{9,11},{10,... | collective-permute-start | bytes 98312 | tf_op jit(solution)/shard_map/ppermute | solution.py:38
  37.9 0.4 %collective-permute-start.12 = (bf16[64,256]{1,0:T(8,128)(2,1)S(1)}, bf16[64,256]{1,0:T(8,128)(2,1)S(1)}, u32[]{:S(2)}, u32[]{:S(2)}) collective-permute-start(bf16[64,256]{1,0:T(8,128)(2,1)S(1)} %compact.1.refs_0_), channel_id=1, source_target_pairs={{0,1},{1,0},{2,3},{3,2},{4,5},{5,4},{6,7},{7,6},{8,9},{9,8},{10,11... | collective-permute-start | bytes 98312 | tf_op jit(solution)/shard_map/ppermute | solution.py:38
  38.4 0.8 %most.1.most_ref = f32[768,256]{1,0:T(8,128)S(1)} custom-call(bf16[64,768]{1,0:T(8,128)(2,1)S(1)} %add.7.mine_ref, bf16[64,768]{1,0:T(8,128)(2,1)S(1)} %collective-permute-done.9.theirs_ref, bf16[320,256]{1,0:T(8,128)(2,1)S(1)} %get-tuple-element.37.up_ref, bf16[768,512]{1,0:T(8,128)(2,1)S(1)} %get-tuple-element.38.mask_ref, ...), custom_call_target="tpu_custom_call" | custom-call | flops 1 | bytes 1 | tf_op jit(solution)/shard_map/most/pallas_call | solution.py:230
  39.1 0.9 %collective-permute-done.14.refs_3_ = bf16[64,256]{1,0:T(8,128)(2,1)S(1)} collective-permute-done((bf16[64,256]{1,0:T(8,128)(2,1)S(1)}, bf16[64,256]{1,0:T(8,128)(2,1)S(1)}, u32[]{:S(2)}, u32[]{:S(2)}) %collective-permute-start.14) | collective-permute-done | bytes 32800 | tf_op jit(solution)/shard_map/ppermute | solution.py:38
  40.1 0.4 collective-permute-done.13.refs_2_
  40.5 1.4 %final.1 = bf16[768,256]{1,0:T(8,128)(2,1)} custom-call(bf16[768,256]{1,0:T(8,128)(2,1)S(1)} %picked.1.pick_ref, bf16[1,64,2304]{2,1,0:T(8,128)(2,1)S(1)} %collective-permute-done.6.piece_ref, s32[1,128]{1,0:T(1,128)S(1)} %bitcast.13, bf16[128,128]{1,0:T(8,128)(2,1)S(1)} %copy-done.3, f32[768,256]{1,0:T(8,128)S(1)} %most.1.most_ref, ...), custom_call_target="tpu_custom_call" | custom-call | flops 1 | bytes 1 | tf_op jit(solution)/shard_map/final/pallas_call | solution.py:258
  (30 shorter events, 0.3 us)
Async XLA Ops:
  1.0 14.1 %collective-permute-start = (bf16[1,64,2048]{2,1,0:T(8,128)(2,1)S(1)}, bf16[1,64,2048]{2,1,0:T(8,128)(2,1)S(1)}, u32[]{:S(2)}, u32[]{:S(2)}) collective-permute-start(bf16[1,64,2048]{2,1,0:T(8,128)(2,1)S(1)} %dynamic-slice_bitcast_fusion), channel_id=1, source_target_pairs={{0,4},{4,0},{8,12},{12,8},{1,5},{5,1},{9,13},{13,9},{2,6},{6,2},{1... | collective-permute-start | bytes 786440 | tf_op jit(solution)/shard_map/ppermute | solution.py:38
  4.8 15.8 %collective-permute-start.1 = (bf16[1,64,2304]{2,1,0:T(8,128)(2,1)S(1)}, bf16[1,64,2304]{2,1,0:T(8,128)(2,1)S(1)}, u32[]{:S(2)}, u32[]{:S(2)}) collective-permute-start(bf16[1,64,2304]{2,1,0:T(8,128)(2,1)S(1)} %pad_maximum_fusion), channel_id=1, source_target_pairs={{0,8},{4,12},{8,0},{12,4},{1,9},{5,13},{9,1},{13,5},{2,10},{6,14},... | collective-permute-start | bytes 884744 | tf_op jit(solution)/shard_map/ppermute | solution.py:38
  7.5 2.2 %copy-start = (bf16[2048,1024]{1,0:T(8,128)(2,1)S(1)}, bf16[2048,1024]{1,0:T(8,128)(2,1)}, u32[]{:S(2)}) copy-start(bf16[2048,1024]{1,0:T(8,128)(2,1)} %weight_ref.3) | copy-start | bytes 12582916
  9.7 1.9 %copy-start.1 = (bf16[768,2048]{1,0:T(8,128)(2,1)S(1)}, bf16[768,2048]{1,0:T(8,128)(2,1)}, u32[]{:S(2)}) copy-start(bf16[768,2048]{1,0:T(8,128)(2,1)} %tokens_ref.9) | copy-start | bytes 9437188
  14.2 7.9 %copy-start.6 = (s32[768,1]{0,1:T(1,128)S(1)}, s32[768,1]{0,1:T(1,128)}, u32[]{:S(2)}) copy-start(s32[768,1]{0,1:T(1,128)} %param.9) | copy-start | bytes 9220
  15.0 8.0 %collective-permute-start.2 = (bf16[1,64,2048]{2,1,0:T(8,128)(2,1)S(1)}, bf16[1,64,2048]{2,1,0:T(8,128)(2,1)S(1)}, u32[]{:S(2)}, u32[]{:S(2)}) collective-permute-start(bf16[1,64,2048]{2,1,0:T(8,128)(2,1)S(1)} %collective-permute-done.refs_0_), channel_id=1, source_target_pairs={{0,16},{16,0},{1,17},{17,1},{2,18},{18,2},{3,19},{19,3},{4,20},{20... | collective-permute-start | bytes 786440 | tf_op jit(solution)/shard_map/ppermute | solution.py:38
  16.7 7.6 %collective-permute-start.3 = (bf16[768,256]{1,0:T(8,128)(2,1)S(1)}, bf16[768,256]{1,0:T(8,128)(2,1)S(1)}, u32[]{:S(2)}, u32[]{:S(2)}) collective-permute-start(bf16[768,256]{1,0:T(8,128)(2,1)S(1)} %get-tuple-element.29), channel_id=1, source_target_pairs={{0,1},{1,0},{2,3},{3,2},{4,5},{5,4},{6,7},{7,6},{8,9},{9,8},{10,11... | collective-permute-start | bytes 1179656 | tf_op jit(solution)/shard_map/ppermute | solution.py:38
  16.7 6.3 %copy-start.2 = (bf16[768,2048]{1,0:T(8,128)(2,1)S(1)}, bf16[768,2048]{1,0:T(8,128)(2,1)}, u32[]{:S(2)}) copy-start(bf16[768,2048]{1,0:T(8,128)(2,1)} %tokens_ref.9) | copy-start | bytes 9437188
  16.7 6.3 %copy-start.5 = (bf16[2,2048,64]{1,2,0:T(8,128)(2,1)S(1)}, bf16[2,2048,64]{1,2,0:T(8,128)(2,1)}, u32[]{:S(2)}) copy-start(bf16[2,2048,64]{1,2,0:T(8,128)(2,1)} %param.12) | copy-start | bytes 1572868
  16.7 7.6 %collective-permute-start.4 = (bf16[768,256]{1,0:T(8,128)(2,1)S(1)}, bf16[768,256]{1,0:T(8,128)(2,1)S(1)}, u32[]{:S(2)}, u32[]{:S(2)}) collective-permute-start(bf16[768,256]{1,0:T(8,128)(2,1)S(1)} %get-tuple-element.30), channel_id=1, source_target_pairs={{0,1},{1,0},{2,3},{3,2},{4,5},{5,4},{6,7},{7,6},{8,9},{9,8},{10,11... | collective-permute-start | bytes 1179656 | tf_op jit(solution)/shard_map/ppermute | solution.py:38
  20.6 7.6 %collective-permute-start.5 = (bf16[1,64,2304]{2,1,0:T(8,128)(2,1)S(1)}, bf16[1,64,2304]{2,1,0:T(8,128)(2,1)S(1)}, u32[]{:S(2)}, u32[]{:S(2)}) collective-permute-start(bf16[1,64,2304]{2,1,0:T(8,128)(2,1)S(1)} %collective-permute-done.1.refs_1_), channel_id=1, source_target_pairs={{0,4},{4,0},{8,12},{12,8},{1,5},{5,1},{9,13},{13,9},{2,6},{6,2},{1... | collective-permute-start | bytes 884744 | tf_op jit(solution)/shard_map/ppermute | solution.py:38
  20.6 9.1 %collective-permute-start.7 = (bf16[1,64,2304]{2,1,0:T(8,128)(2,1)S(1)}, bf16[1,64,2304]{2,1,0:T(8,128)(2,1)S(1)}, u32[]{:S(2)}, u32[]{:S(2)}) collective-permute-start(bf16[1,64,2304]{2,1,0:T(8,128)(2,1)S(1)} %collective-permute-done.1.refs_1_), channel_id=1, source_target_pairs={{0,16},{16,0},{1,17},{17,1},{2,18},{18,2},{3,19},{19,3},{4,20},{20... | collective-permute-start | bytes 884744 | tf_op jit(solution)/shard_map/ppermute | solution.py:38
  24.4 6.6 %copy-start.4 = (bf16[2,64,256]{2,1,0:T(8,128)(2,1)S(1)}, bf16[2,64,256]{2,1,0:T(8,128)(2,1)}, u32[]{:S(2)}) copy-start(bf16[2,64,256]{2,1,0:T(8,128)(2,1)} %refs_0_.1) | copy-start | bytes 196612
  24.4 7.7 %copy-start.3 = (bf16[128,128]{1,0:T(8,128)(2,1)S(1)}, bf16[128,128]{1,0:T(8,128)(2,1)}, u32[]{:S(2)}) copy-start(bf16[128,128]{1,0:T(8,128)(2,1)} %constant.12.clone.matrix_ref) | copy-start | bytes 98308
  24.4 7.7 %copy-start.7 = (s32[128]{0:T(128)S(1)}, s32[128]{0:T(128)}, u32[]{:S(2)}) copy-start(s32[128]{0:T(128)} %param.14) | copy-start | bytes 1540
  24.4 13.9 %collective-permute-start.11 = (bf16[768,256]{1,0:T(8,128)(2,1)S(1)}, bf16[768,256]{1,0:T(8,128)(2,1)S(1)}, u32[]{:S(2)}, u32[]{:S(2)}) collective-permute-start(bf16[768,256]{1,0:T(8,128)(2,1)S(1)} %add.8), channel_id=1, source_target_pairs={{0,2},{1,3},{2,0},{3,1},{4,6},{5,7},{6,4},{7,5},{8,10},{9,11},{10,... | collective-permute-start | bytes 1179656 | tf_op jit(solution)/shard_map/ppermute | solution.py:38
  28.2 6.9 %collective-permute-start.6 = (bf16[1,64,2304]{2,1,0:T(8,128)(2,1)S(1)}, bf16[1,64,2304]{2,1,0:T(8,128)(2,1)S(1)}, u32[]{:S(2)}, u32[]{:S(2)}) collective-permute-start(bf16[1,64,2304]{2,1,0:T(8,128)(2,1)S(1)} %collective-permute-done.5.refs_2_.refs_1_), channel_id=1, source_target_pairs={{0,16},{16,0},{1,17},{17,1},{2,18},{18,2},{3,19},{19,3},{4,20},{20... | collective-permute-start | bytes 884744 | tf_op jit(solution)/shard_map/ppermute | solution.py:38
  30.9 1.7 %collective-permute-start.8 = (bf16[64,768]{1,0:T(8,128)(2,1)S(1)}, bf16[64,768]{1,0:T(8,128)(2,1)S(1)}, u32[]{:S(2)}, u32[]{:S(2)}) collective-permute-start(bf16[64,768]{1,0:T(8,128)(2,1)S(1)} %low_rows.3.refs_0_), channel_id=1, source_target_pairs={{0,1},{1,0},{2,3},{3,2},{4,5},{5,4},{6,7},{7,6},{8,9},{9,8},{10,11... | collective-permute-start | bytes 294920 | tf_op jit(solution)/shard_map/ppermute | solution.py:38
  31.0 6.9 %collective-permute-start.10 = (bf16[2,64,256]{2,1,0:T(8,128)(2,1)S(1)}, bf16[2,64,256]{2,1,0:T(8,128)(2,1)S(1)}, u32[]{:S(2)}, u32[]{:S(2)}) collective-permute-start(bf16[2,64,256]{2,1,0:T(8,128)(2,1)S(1)} %copy-done.4), channel_id=1, source_target_pairs={{0,4},{4,0},{8,12},{12,8},{1,5},{5,1},{9,13},{13,9},{2,6},{6,2},{1... | collective-permute-start | bytes 196616 | tf_op jit(solution)/shard_map/ppermute | solution.py:38
  32.1 6.3 %copy-start.8 = (f32[256]{0:T(256)S(1)}, f32[256]{0:T(256)}, u32[]{:S(2)}) copy-start(f32[256]{0:T(256)} %param.11) | copy-start | bytes 3076
  32.7 5.7 %collective-permute-start.9 = (bf16[64,768]{1,0:T(8,128)(2,1)S(1)}, bf16[64,768]{1,0:T(8,128)(2,1)S(1)}, u32[]{:S(2)}, u32[]{:S(2)}) collective-permute-start(bf16[64,768]{1,0:T(8,128)(2,1)S(1)} %add.7.mine_ref), channel_id=1, source_target_pairs={{0,2},{1,3},{2,0},{3,1},{4,6},{5,7},{6,4},{7,5},{8,10},{9,11},{10,... | collective-permute-start | bytes 294920 | tf_op jit(solution)/shard_map/ppermute | solution.py:38
  36.4 3.6 %collective-permute-start.14 = (bf16[64,256]{1,0:T(8,128)(2,1)S(1)}, bf16[64,256]{1,0:T(8,128)(2,1)S(1)}, u32[]{:S(2)}, u32[]{:S(2)}) collective-permute-start(bf16[64,256]{1,0:T(8,128)(2,1)S(1)} %compact.1.refs_0_), channel_id=1, source_target_pairs={{0,3},{1,2},{2,1},{3,0},{4,7},{5,6},{6,5},{7,4},{8,11},{9,10},{10,... | collective-permute-start | bytes 98312 | tf_op jit(solution)/shard_map/ppermute | solution.py:38
  36.5 4.0 %collective-permute-start.13 = (bf16[64,256]{1,0:T(8,128)(2,1)S(1)}, bf16[64,256]{1,0:T(8,128)(2,1)S(1)}, u32[]{:S(2)}, u32[]{:S(2)}) collective-permute-start(bf16[64,256]{1,0:T(8,128)(2,1)S(1)} %compact.1.refs_0_), channel_id=1, source_target_pairs={{0,2},{1,3},{2,0},{3,1},{4,6},{5,7},{6,4},{7,5},{8,10},{9,11},{10,... | collective-permute-start | bytes 98312 | tf_op jit(solution)/shard_map/ppermute | solution.py:38
  37.9 2.6 %collective-permute-start.12 = (bf16[64,256]{1,0:T(8,128)(2,1)S(1)}, bf16[64,256]{1,0:T(8,128)(2,1)S(1)}, u32[]{:S(2)}, u32[]{:S(2)}) collective-permute-start(bf16[64,256]{1,0:T(8,128)(2,1)S(1)} %compact.1.refs_0_), channel_id=1, source_target_pairs={{0,1},{1,0},{2,3},{3,2},{4,5},{5,4},{6,7},{7,6},{8,9},{9,8},{10,11... | collective-permute-start | bytes 98312 | tf_op jit(solution)/shard_map/ppermute | solution.py:38

commit v19 on v18

--- a/solution.py
+++ b/solution.py
@@ -12,6 +12,7 @@
 SMEM = pl.BlockSpec(memory_space=pltpu.SMEM)
 F32, BF16 = jnp.float32, jnp.bfloat16
 LAST = (((1,), (1,)), ((), ()))
+FIRST = (((0,), (0,)), ((), ()))
 
 
 def params(mib):
@@ -160,7 +161,7 @@
     )(ids, bits, matrix, *arrays)
 
 
-def pick_kernel(named, here, share, ids_ref, pick_ref):
+def pick_kernel(named, here, share, ids_ref, tokens_ref, pick_ref, chosen_ref):
     rows, slots = pick_ref.shape[0], pick_ref.shape[1] // len(named)
     earlier = lax.broadcasted_iota(jnp.int32, (rows, rows), 0) < lax.broadcasted_iota(jnp.int32, (rows, rows), 1)
     earlier = jnp.where(earlier, 1.0, 0.0).astype(BF16)
@@ -173,40 +174,45 @@
         for at in range(0, slots, 128):
             slot = (lax.broadcasted_iota(jnp.int32, (rows, 128), 1) + at).astype(F32)
             pick_ref[:, k * slots + at : k * slots + at + 128] = jnp.where(rank == slot, 1.0, 0.0).astype(BF16)
-
-
-def picked(ids, here, share, named, slots):
+    rows = lax.dot_general(pick_ref[...], tokens_ref[...], FIRST, preferred_element_type=F32)
+    chosen_ref[...] = rows.astype(BF16)
+
+
+def picked(ids, tokens, here, share, named, slots):
+    rows, features = tokens.shape
+    columns = len(named) * slots
     return pl.pallas_call(
         functools.partial(pick_kernel, named, here, share),
-        in_specs=[VMEM],
+        in_specs=[VMEM] * 2,
+        out_specs=[VMEM] * 2,
+        out_shape=[jax.ShapeDtypeStruct((rows, columns), BF16), jax.ShapeDtypeStruct((columns, features), BF16)],
+        compiler_params=params(24),
+        cost_estimate=COST,
+        name="picked",
+    )(ids, tokens)
+
+
+def compact_kernel(chosen_ref, piece_ref, out_ref):
+    share, features = piece_ref.shape[0], chosen_ref.shape[1]
+    slots = chosen_ref.shape[0] // share
+    for k in range(share):
+        mine = slice(k * slots, (k + 1) * slots)
+        product = lax.dot_general(
+            piece_ref[k, :, :features], chosen_ref[mine], LAST, preferred_element_type=F32
+        )
+        out_ref[:, mine] = product.astype(BF16)
+
+
+def compact(chosen, piece):
+    return pl.pallas_call(
+        compact_kernel,
+        in_specs=[VMEM] * 2,
         out_specs=VMEM,
-        out_shape=jax.ShapeDtypeStruct((ids.shape[1], len(named) * slots), BF16),
-        compiler_params=params(24),
-        cost_estimate=COST,
-        name="picked",
-    )(ids)
-
-
-def compact_kernel(tokens_ref, piece_ref, pick_ref, out_ref):
-    share, features = piece_ref.shape[0], tokens_ref.shape[1]
-    slots = pick_ref.shape[1] // share
-    for k in range(share):
-        product = lax.dot_general(piece_ref[k, :, :features], tokens_ref[...], LAST, preferred_element_type=F32)
-        columns = slice(k * slots, (k + 1) * slots)
-        kept = jnp.dot(product.astype(BF16), pick_ref[:, columns], preferred_element_type=F32)
-        out_ref[:, columns] = kept.astype(BF16)
-
-
-def compact(tokens, piece, pick):
-    return pl.pallas_call(
-        compact_kernel,
-        in_specs=[VMEM] * 3,
-        out_specs=VMEM,
-        out_shape=jax.ShapeDtypeStruct((piece.shape[1], pick.shape[1]), BF16),
+        out_shape=jax.ShapeDtypeStruct((piece.shape[1], chosen.shape[0]), BF16),
         compiler_params=params(24),
         cost_estimate=lasting(2),
         name="compact",
-    )(tokens, piece, pick)
+    )(chosen, piece)
 
 
 def most_kernel(mine_ref, theirs_ref, up_ref, mask_ref, near_ref, scale_ref, bits_ref, matrix_ref, *refs):
@@ -239,7 +245,7 @@
 
 
 def final_kernel(pick_ref, piece_ref, bits_ref, matrix_ref, most_ref, *refs):
-    kept_refs, out_ref = refs[:-1], refs[-1]
+    kept_refs, (out_ref, half_ref, sems) = refs[:-3], refs[-3:]
     share, width = piece_ref.shape[0], out_ref.shape[1]
     features, slots = piece_ref.shape[2] - width, pick_ref.shape[1] // share
     signs = (1 - 2 * bits_ref[...]).astype(F32)
@@ -250,16 +256,25 @@
         up = jnp.concatenate(turned, axis=1).astype(BF16)
         deltas.append(jnp.dot(low[k * slots : (k + 1) * slots], up, preferred_element_type=F32).astype(BF16))
     delta = deltas[0] if share == 1 else jnp.concatenate(deltas, axis=0)
-    result = most_ref[...] + jnp.dot(pick_ref[...], delta, preferred_element_type=F32)
-    out_ref[...] = result.astype(BF16)
+    count, rows, _ = half_ref.shape
+    copies = []
+    for n in range(count):
+        part = slice(n * rows, (n + 1) * rows)
+        result = most_ref[part] + jnp.dot(pick_ref[part], delta, preferred_element_type=F32)
+        half_ref[n] = result.astype(BF16)
+        copies.append(pltpu.make_async_copy(half_ref.at[n], out_ref.at[pl.ds(n * rows, rows)], sems.at[n]))
+        copies[-1].start()
+    for copy in copies:
+        copy.wait()
 
 
 def final(kept, pick, piece, bits, matrix, rest):
     return pl.pallas_call(
         final_kernel,
         in_specs=[VMEM] * (5 + len(kept)),
-        out_specs=VMEM,
+        out_specs=pl.BlockSpec(memory_space=pl.ANY),
         out_shape=jax.ShapeDtypeStruct(rest.shape, BF16),
+        scratch_shapes=[pltpu.VMEM((2, rest.shape[0] // 2, rest.shape[1]), BF16), pltpu.SemaphoreType.DMA((2,))],
         compiler_params=params(32),
         cost_estimate=COST,
         name="final",
@@ -289,7 +304,10 @@
     blocks = list(partials(tokens, base_weight, parts, offsets, lasting(4)))
     near, blocks[-1] = together(near, blocks[-1])
     (block,) = partials(tokens, base_weight, parts, (0,), COST, blocks[-1])
-    close, block, *far = together(near, block, *(piece for _, piece in mine[1:]))
+    slots = -(-2 * tokens.shape[0] // (here * planes) // 128) * 128
+    lasts = [(planes - 1, groups - 1, k) for k in range(share)]
+    pick, chosen = picked(ids, tokens, here, share, lasts, slots)
+    close, block, pick, chosen, *far = together(near, block, pick, chosen, *(piece for _, piece in mine[1:]))
     blocks = blocks[:half] + [block] + blocks[half:]
     mine = mine[:1] + [(plane, piece) for (plane, _), piece in zip(mine[1:], far)]
     odd = [(1, near)] + [(plane | 1, swap(piece, "adp", 1)) for plane, piece in mine[1:]]
@@ -311,10 +329,7 @@
         return low_rows(ids, tokens, here, share, [((0, features), every)], arrays, low, dtype, cost)
 
     low = more(None, held[: len(mine)] + swapped[:1], F32, lasting(2))
-    slots = -(-2 * tokens.shape[0] // (here * planes) // 128) * 128
-    last = swapped[-1]
-    pick = picked(ids, here, share, [(last[0], last[1], k) for k in range(share)], slots)
-    low, pick, *came = together(low, pick, *(swap(block, "tp", 1) for block in blocks[:half]))
+    low, *came = together(low, *(swap(block, "tp", 1) for block in blocks[:half]))
 
     def both(low):
         bit = 1
@@ -344,8 +359,8 @@
     arrays = [adapter_up] + [piece for *_, piece in far]
     up, mask = rotated_ups(ids, bits, matrix, here, share, named, ups, arrays, width)
 
-    piece, up, mask = together(last[2], up, mask)
-    kept = compact(tokens, piece, pick)
+    piece, up, mask = together(swapped[-1][2], up, mask)
+    kept = compact(chosen, piece)
     kept = [kept] + [swap(kept, "tp", offset) for offset in range(1, parts)]
     rest = most(low, other, up, mask, near_up, scale, bits, matrix, sums[0])
     return final(kept, pick, piece, bits, matrix, rest)

time: 42.1 us -> 41.8 us (level)
    pallas_call x1, Pallas kernels: 0.36 us -> 1.33 us  [picked(): pl.pallas_call(functools.partial(pick_kernel, named, here, share), in_spe...]
    pallas_call x1, Pallas kernels: 1.25 us -> 0.45 us  [compact(): pl.pallas_call(compact_kernel, in_specs=[VMEM] * 2, out_specs=VMEM, out_s...]
    unnamed x18 -> x20, local copies, waits for them, and re-layouts: 4.11 us -> 4.12 us
where the time goes in v19:
time: 41.8 us; the launch traced here: 41.6 us
  starting transfers between devices  16.5 us (39%)
  Pallas kernels  10.7 us (26%)
  waiting for transfers between devices  8.32 us (20%)
  local copies, waits for them, and re-layouts  5.84 us (14%)
    ppermute x15, starting transfers between devices, swap(): lax.ppermute(x, axis, [(i, i ^ bit) for i in range(lax.axis_size(axis))])  16.5 us
    ppermute x15, waiting for transfers between devices, swap(): lax.ppermute(x, axis, [(i, i ^ bit) for i in range(lax.axis_size(axis))])  8.32 us
    unnamed x20, local copies, waits for them, and re-layouts  4.12 us
    pallas_call x2, Pallas kernels, partials(): pl.pallas_call(functools.partial(partial_kernel, offsets, parts), in_spec...  3.66 us
    pallas_call x2, Pallas kernels, low_rows(): pl.pallas_call(functools.partial(low_kernel, groups, here, share, rank, b...  2.45 us
    pallas_call x1, Pallas kernels, final(): pl.pallas_call(final_kernel, in_specs=[VMEM] * (5 + len(kept)), out_specs...  1.34 us
    pallas_call x1, Pallas kernels, picked(): pl.pallas_call(functools.partial(pick_kernel, named, here, share), in_spe...  1.33 us
    dynamic_slice x1, local copies, waits for them, and re-layouts, local(): own = lax.dynamic_slice_in_dim(down, start, share, 0)  0.97 us
  transfers between devices with their start and end apart: 15, of which 7 were waited for; matrix products, arithmetic and copies ran while one was open for 2% of the time, Pallas kernels for 22%

profile of v19, /device:TPU:0, one launch (start us, length us, event | category | flops | bytes accessed | tf_op | source)
XLA Modules:
  0.0 41.6 jit_solution(16826921637855755744)
XLA Ops:
  0.0 1.0 %dynamic-slice_bitcast_fusion = bf16[1,64,2048]{2,1,0:T(8,128)(2,1)S(1)} fusion(bf16[2,2048,64]{1,2,0:T(8,128)(2,1)} %param.12, s32[]{:T(128)S(6)} %select_n.4), kind=kLoop, calls=%fused_computation.1 | loop fusion | bytes 524292 | tf_op jit(solution)/shard_map/dynamic_slice | solution.py:295
  1.0 3.1 %collective-permute-start = (bf16[1,64,2048]{2,1,0:T(8,128)(2,1)S(1)}, bf16[1,64,2048]{2,1,0:T(8,128)(2,1)S(1)}, u32[]{:S(2)}, u32[]{:S(2)}) collective-permute-start(bf16[1,64,2048]{2,1,0:T(8,128)(2,1)S(1)} %dynamic-slice_bitcast_fusion), channel_id=1, source_target_pairs={{0,4},{4,0},{8,12},{12,8},{1,5},{5,1},{9,13},{13,9},{2,6},{6,2},{1... | collective-permute-start | bytes 786440 | tf_op jit(solution)/shard_map/ppermute | solution.py:39
  4.1 0.8 %constant_dynamic-slice_fusion = bf16[1,64,256]{2,1,0:T(8,128)(2,1)S(1)} fusion(bf16[2,64,256]{2,1,0:T(8,128)(2,1)} %refs_0_.1, s32[]{:T(128)S(6)} %select_n.4), kind=kLoop, calls=%fused_computation.2 | loop fusion | bytes 65540 | tf_op jit(solution)/shard_map/dynamic_slice | solution.py:297
  4.8 2.7 %collective-permute-start.1 = (bf16[1,64,2304]{2,1,0:T(8,128)(2,1)S(1)}, bf16[1,64,2304]{2,1,0:T(8,128)(2,1)S(1)}, u32[]{:S(2)}, u32[]{:S(2)}) collective-permute-start(bf16[1,64,2304]{2,1,0:T(8,128)(2,1)S(1)} %pad_maximum_fusion), channel_id=1, source_target_pairs={{0,8},{4,12},{8,0},{12,4},{1,9},{5,13},{9,1},{13,5},{2,10},{6,14},... | collective-permute-start | bytes 884744 | tf_op jit(solution)/shard_map/ppermute | solution.py:39
  7.5 1.9 %copy-done = bf16[768,2048]{1,0:T(8,128)(2,1)S(1)} copy-done((bf16[768,2048]{1,0:T(8,128)(2,1)S(1)}, bf16[768,2048]{1,0:T(8,128)(2,1)}, u32[]{:S(2)}) %copy-start) | copy-done | bytes 3145752
  9.4 2.2 %copy-done.2 = bf16[2048,1024]{1,0:T(8,128)(2,1)S(1)} copy-done((bf16[2048,1024]{1,0:T(8,128)(2,1)S(1)}, bf16[2048,1024]{1,0:T(8,128)(2,1)}, u32[]{:S(2)}) %copy-start.2) | copy-done | bytes 4194328
  11.6 2.7 %partials.2 = (bf16[768,256]{1,0:T(8,128)(2,1)S(1)}, bf16[768,256]{1,0:T(8,128)(2,1)S(1)}, bf16[768,256]{1,0:T(8,128)(2,1)S(1)}) custom-call(bf16[768,2048]{1,0:T(8,128)(2,1)S(1)} %copy-done, bf16[2048,1024]{1,0:T(8,128)(2,1)S(1)} %copy-done.2), custom_call_target="tpu_custom_call" | custom-call | flops 4000000000 | bytes 1 | tf_op jit(solution)/shard_map/partials/pallas_call | solution.py:70
  14.3 0.8 %collective-permute-done.refs_0_ = bf16[1,64,2048]{2,1,0:T(8,128)(2,1)S(1)} collective-permute-done((bf16[1,64,2048]{2,1,0:T(8,128)(2,1)S(1)}, bf16[1,64,2048]{2,1,0:T(8,128)(2,1)S(1)}, u32[]{:S(2)}, u32[]{:S(2)}) %collective-permute-start) | collective-permute-done | bytes 262176 | tf_op jit(solution)/shard_map/ppermute | solution.py:39
  15.0 1.7 %collective-permute-start.5 = (bf16[1,64,2048]{2,1,0:T(8,128)(2,1)S(1)}, bf16[1,64,2048]{2,1,0:T(8,128)(2,1)S(1)}, u32[]{:S(2)}, u32[]{:S(2)}) collective-permute-start(bf16[1,64,2048]{2,1,0:T(8,128)(2,1)S(1)} %collective-permute-done.refs_0_), channel_id=1, source_target_pairs={{0,16},{16,0},{1,17},{17,1},{2,18},{18,2},{3,19},{19,3},{4,20},{20... | collective-permute-start | bytes 786440 | tf_op jit(solution)/shard_map/ppermute | solution.py:39
  16.7 0.5 %collective-permute-start.7 = (bf16[768,256]{1,0:T(8,128)(2,1)S(1)}, bf16[768,256]{1,0:T(8,128)(2,1)S(1)}, u32[]{:S(2)}, u32[]{:S(2)}) collective-permute-start(bf16[768,256]{1,0:T(8,128)(2,1)S(1)} %get-tuple-element.39), channel_id=1, source_target_pairs={{0,1},{1,0},{2,3},{3,2},{4,5},{5,4},{6,7},{7,6},{8,9},{9,8},{10,11... | collective-permute-start | bytes 1179656 | tf_op jit(solution)/shard_map/ppermute | solution.py:39
  17.2 1.3 %picked.1 = (bf16[768,256]{1,0:T(8,128)(2,1)S(1)}, bf16[256,2048]{1,0:T(8,128)(2,1)S(1)}) custom-call(s32[1,768]{1,0:T(1,128)S(1)} %bitcast.7, bf16[768,2048]{1,0:T(8,128)(2,1)S(1)} %copy-done.1), custom_call_target="tpu_custom_call" | custom-call | flops 1 | bytes 1 | tf_op jit(solution)/shard_map/picked/pallas_call | solution.py:184
  18.6 1.0 %partials.3.refs_0_ = bf16[768,256]{1,0:T(8,128)(2,1)S(1)} custom-call(bf16[768,2048]{1,0:T(8,128)(2,1)S(1)} %copy-done.1, bf16[2048,1024]{1,0:T(8,128)(2,1)S(1)} %copy-done.3, bf16[768,256]{1,0:T(8,128)(2,1)S(1)} %get-tuple-element.29.refs_0_), custom_call_target="tpu_custom_call" | custom-call | flops 1 | bytes 1 | tf_op jit(solution)/shard_map/partials/pallas_call | solution.py:70
  19.6 1.0 %collective-permute-done.1.refs_1_ = bf16[1,64,2304]{2,1,0:T(8,128)(2,1)S(1)} collective-permute-done((bf16[1,64,2304]{2,1,0:T(8,128)(2,1)S(1)}, bf16[1,64,2304]{2,1,0:T(8,128)(2,1)S(1)}, u32[]{:S(2)}, u32[]{:S(2)}) %collective-permute-start.1) | collective-permute-done | bytes 294944 | tf_op jit(solution)/shard_map/ppermute | solution.py:39
  20.6 1.5 %collective-permute-start.4 = (bf16[1,64,2304]{2,1,0:T(8,128)(2,1)S(1)}, bf16[1,64,2304]{2,1,0:T(8,128)(2,1)S(1)}, u32[]{:S(2)}, u32[]{:S(2)}) collective-permute-start(bf16[1,64,2304]{2,1,0:T(8,128)(2,1)S(1)} %collective-permute-done.1.refs_1_), channel_id=1, source_target_pairs={{0,16},{16,0},{1,17},{17,1},{2,18},{18,2},{3,19},{19,3},{4,20},{20... | collective-permute-start | bytes 884744 | tf_op jit(solution)/shard_map/ppermute | solution.py:39
  22.2 0.4 %collective-permute-done.5.refs_2_ = bf16[1,64,2048]{2,1,0:T(8,128)(2,1)S(1)} collective-permute-done((bf16[1,64,2048]{2,1,0:T(8,128)(2,1)S(1)}, bf16[1,64,2048]{2,1,0:T(8,128)(2,1)S(1)}, u32[]{:S(2)}, u32[]{:S(2)}) %collective-permute-start.5) | collective-permute-done | bytes 262176 | tf_op jit(solution)/shard_map/ppermute | solution.py:39
  22.6 1.2 %low_rows.2.refs_2_ = f32[64,768]{1,0:T(8,128)S(1)} custom-call(s32[1,768]{1,0:T(1,128)S(1)} %bitcast.8, bf16[768,2048]{1,0:T(8,128)(2,1)S(1)} %copy-done.1, bf16[1,64,2048]{2,1,0:T(8,128)(2,1)S(1)} %collective-permute-done.refs_0_, bf16[1,64,2304]{2,1,0:T(8,128)(2,1)S(1)} %collective-permute-done.1.refs_1_, ...), custom_call_target="tpu_custom_call" | custom-call | flops 2000000000 | bytes 1 | tf_op jit(solution)/shard_map/low_rows/pallas_call | solution.py:125
  23.9 0.1 add.8
  24.0 1.3 %collective-permute-start.11 = (bf16[768,256]{1,0:T(8,128)(2,1)S(1)}, bf16[768,256]{1,0:T(8,128)(2,1)S(1)}, u32[]{:S(2)}, u32[]{:S(2)}) collective-permute-start(bf16[768,256]{1,0:T(8,128)(2,1)S(1)} %add.8), channel_id=1, source_target_pairs={{0,2},{1,3},{2,0},{3,1},{4,6},{5,7},{6,4},{7,5},{8,10},{9,11},{10,... | collective-permute-start | bytes 1179656 | tf_op jit(solution)/shard_map/ppermute | solution.py:39
  25.3 3.3 %collective-permute-done.2.refs_2_.refs_1_ = bf16[1,64,2304]{2,1,0:T(8,128)(2,1)S(1)} collective-permute-done((bf16[1,64,2304]{2,1,0:T(8,128)(2,1)S(1)}, bf16[1,64,2304]{2,1,0:T(8,128)(2,1)S(1)}, u32[]{:S(2)}, u32[]{:S(2)}) %collective-permute-start.2) | collective-permute-done | bytes 294944 | tf_op jit(solution)/shard_map/ppermute | solution.py:39
  28.6 1.1 %collective-permute-start.3 = (bf16[1,64,2304]{2,1,0:T(8,128)(2,1)S(1)}, bf16[1,64,2304]{2,1,0:T(8,128)(2,1)S(1)}, u32[]{:S(2)}, u32[]{:S(2)}) collective-permute-start(bf16[1,64,2304]{2,1,0:T(8,128)(2,1)S(1)} %collective-permute-done.2.refs_2_.refs_1_), channel_id=1, source_target_pairs={{0,16},{16,0},{1,17},{17,1},{2,18},{18,2},{3,19},{19,3},{4,20},{20... | collective-permute-start | bytes 884744 | tf_op jit(solution)/shard_map/ppermute | solution.py:39
  29.8 1.2 %low_rows.3.refs_0_ = bf16[64,768]{1,0:T(8,128)(2,1)S(1)} custom-call(s32[1,768]{1,0:T(1,128)S(1)} %bitcast.9, bf16[768,2048]{1,0:T(8,128)(2,1)S(1)} %copy-done.1, bf16[1,64,2304]{2,1,0:T(8,128)(2,1)S(1)} %collective-permute-done.4.refs_3_.refs_0_, bf16[1,64,2304]{2,1,0:T(8,128)(2,1)S(1)} %collective-permute-done.2.refs_2_.refs_1_, ...), custom_call_target="tpu_custom_call" | custom-call | flops 5000000000 | bytes 1 | tf_op jit(solution)/shard_map/low_rows/pallas_call | solution.py:125
  31.1 1.0 %collective-permute-start.10 = (bf16[2,64,256]{2,1,0:T(8,128)(2,1)S(1)}, bf16[2,64,256]{2,1,0:T(8,128)(2,1)S(1)}, u32[]{:S(2)}, u32[]{:S(2)}) collective-permute-start(bf16[2,64,256]{2,1,0:T(8,128)(2,1)S(1)} %copy-done.5), channel_id=1, source_target_pairs={{0,4},{4,0},{8,12},{12,8},{1,5},{5,1},{9,13},{13,9},{2,6},{6,2},{1... | collective-permute-start | bytes 196616 | tf_op jit(solution)/shard_map/ppermute | solution.py:39
  32.1 0.5 %rotated_ups.1 = (bf16[320,256]{1,0:T(8,128)(2,1)S(1)}, bf16[768,512]{1,0:T(8,128)(2,1)S(1)}) custom-call(s32[1,768]{1,0:T(1,128)S(1)} %bitcast.10, s32[1,128]{1,0:T(1,128)S(1)} %bitcast.11, bf16[128,128]{1,0:T(8,128)(2,1)S(1)} %copy-done.4, bf16[2,64,256]{2,1,0:T(8,128)(2,1)S(1)} %copy-done.5, bf16[1,64,2304]{2,1,0:T(8,128)(2,1)S(1)} %collective-permute-done.1.refs_1_, ...), custom_call_target="tpu_custom_call" | custom-call | flops 1 | bytes 1 | tf_op jit(solution)/shard_map/rotated_ups/pallas_call | solution.py:153
  32.7 1.6 %collective-permute-start.9 = (bf16[64,768]{1,0:T(8,128)(2,1)S(1)}, bf16[64,768]{1,0:T(8,128)(2,1)S(1)}, u32[]{:S(2)}, u32[]{:S(2)}) collective-permute-start(bf16[64,768]{1,0:T(8,128)(2,1)S(1)} %add.7.mine_ref), channel_id=1, source_target_pairs={{0,2},{1,3},{2,0},{3,1},{4,6},{5,7},{6,4},{7,5},{8,10},{9,11},{10,... | collective-permute-start | bytes 294920 | tf_op jit(solution)/shard_map/ppermute | solution.py:39
  34.2 1.4 %collective-permute-done.3.piece_ref = bf16[1,64,2304]{2,1,0:T(8,128)(2,1)S(1)} collective-permute-done((bf16[1,64,2304]{2,1,0:T(8,128)(2,1)S(1)}, bf16[1,64,2304]{2,1,0:T(8,128)(2,1)S(1)}, u32[]{:S(2)}, u32[]{:S(2)}) %collective-permute-start.3) | collective-permute-done | bytes 294944 | tf_op jit(solution)/shard_map/ppermute | solution.py:39
  35.7 0.4 %compact.1.refs_0_ = bf16[64,256]{1,0:T(8,128)(2,1)S(1)} custom-call(bf16[256,2048]{1,0:T(8,128)(2,1)S(1)} %get-tuple-element.48.chosen_ref, bf16[1,64,2304]{2,1,0:T(8,128)(2,1)S(1)} %collective-permute-done.3.piece_ref), custom_call_target="tpu_custom_call" | custom-call | flops 2000000000 | bytes 1 | tf_op jit(solution)/shard_map/compact/pallas_call | solution.py:207
  36.2 1.5 %collective-permute-start.13 = (bf16[64,256]{1,0:T(8,128)(2,1)S(1)}, bf16[64,256]{1,0:T(8,128)(2,1)S(1)}, u32[]{:S(2)}, u32[]{:S(2)}) collective-permute-start(bf16[64,256]{1,0:T(8,128)(2,1)S(1)} %compact.1.refs_0_), channel_id=1, source_target_pairs={{0,2},{1,3},{2,0},{3,1},{4,6},{5,7},{6,4},{7,5},{8,10},{9,11},{10,... | collective-permute-start | bytes 98312 | tf_op jit(solution)/shard_map/ppermute | solution.py:39
  37.7 0.3 collective-permute-start.12
  38.1 0.8 %most.1.most_ref = f32[768,256]{1,0:T(8,128)S(1)} custom-call(bf16[64,768]{1,0:T(8,128)(2,1)S(1)} %add.7.mine_ref, bf16[64,768]{1,0:T(8,128)(2,1)S(1)} %collective-permute-done.9.theirs_ref, bf16[320,256]{1,0:T(8,128)(2,1)S(1)} %get-tuple-element.42.up_ref, bf16[768,512]{1,0:T(8,128)(2,1)S(1)} %get-tuple-element.43.mask_ref, ...), custom_call_target="tpu_custom_call" | custom-call | flops 1 | bytes 1 | tf_op jit(solution)/shard_map/most/pallas_call | solution.py:236
  38.9 1.0 %collective-permute-done.14.refs_3_ = bf16[64,256]{1,0:T(8,128)(2,1)S(1)} collective-permute-done((bf16[64,256]{1,0:T(8,128)(2,1)S(1)}, bf16[64,256]{1,0:T(8,128)(2,1)S(1)}, u32[]{:S(2)}, u32[]{:S(2)}) %collective-permute-start.14) | collective-permute-done | bytes 32800 | tf_op jit(solution)/shard_map/ppermute | solution.py:39
  39.9 0.4 collective-permute-done.13.refs_2_
  40.2 1.3 %final.1 = bf16[768,256]{1,0:T(8,128)(2,1)} custom-call(bf16[768,256]{1,0:T(8,128)(2,1)S(1)} %get-tuple-element.32.pick_ref, bf16[1,64,2304]{2,1,0:T(8,128)(2,1)S(1)} %collective-permute-done.3.piece_ref, s32[1,128]{1,0:T(1,128)S(1)} %bitcast.13, bf16[128,128]{1,0:T(8,128)(2,1)S(1)} %copy-done.4, f32[768,256]{1,0:T(8,128)S(1)} %most.1.most_ref, ...), custom_call_target="tpu_custom_call" | custom-call | flops 1 | bytes 1 | tf_op jit(solution)/shard_map/final/pallas_call | solution.py:272
  (32 shorter events, 0.3 us)
Async XLA Ops:
  1.0 14.1 %collective-permute-start = (bf16[1,64,2048]{2,1,0:T(8,128)(2,1)S(1)}, bf16[1,64,2048]{2,1,0:T(8,128)(2,1)S(1)}, u32[]{:S(2)}, u32[]{:S(2)}) collective-permute-start(bf16[1,64,2048]{2,1,0:T(8,128)(2,1)S(1)} %dynamic-slice_bitcast_fusion), channel_id=1, source_target_pairs={{0,4},{4,0},{8,12},{12,8},{1,5},{5,1},{9,13},{13,9},{2,6},{6,2},{1... | collective-permute-start | bytes 786440 | tf_op jit(solution)/shard_map/ppermute | solution.py:39
  4.8 15.8 %collective-permute-start.1 = (bf16[1,64,2304]{2,1,0:T(8,128)(2,1)S(1)}, bf16[1,64,2304]{2,1,0:T(8,128)(2,1)S(1)}, u32[]{:S(2)}, u32[]{:S(2)}) collective-permute-start(bf16[1,64,2304]{2,1,0:T(8,128)(2,1)S(1)} %pad_maximum_fusion), channel_id=1, source_target_pairs={{0,8},{4,12},{8,0},{12,4},{1,9},{5,13},{9,1},{13,5},{2,10},{6,14},... | collective-permute-start | bytes 884744 | tf_op jit(solution)/shard_map/ppermute | solution.py:39
  7.5 1.9 %copy-start = (bf16[768,2048]{1,0:T(8,128)(2,1)S(1)}, bf16[768,2048]{1,0:T(8,128)(2,1)}, u32[]{:S(2)}) copy-start(bf16[768,2048]{1,0:T(8,128)(2,1)} %tokens_ref.9) | copy-start | bytes 9437188
  9.4 2.2 %copy-start.2 = (bf16[2048,1024]{1,0:T(8,128)(2,1)S(1)}, bf16[2048,1024]{1,0:T(8,128)(2,1)}, u32[]{:S(2)}) copy-start(bf16[2048,1024]{1,0:T(8,128)(2,1)} %weight_ref.3) | copy-start | bytes 12582916
  11.6 5.6 %copy-start.1 = (bf16[768,2048]{1,0:T(8,128)(2,1)S(1)}, bf16[768,2048]{1,0:T(8,128)(2,1)}, u32[]{:S(2)}) copy-start(bf16[768,2048]{1,0:T(8,128)(2,1)} %tokens_ref.9) | copy-start | bytes 9437188
  11.6 5.6 %copy-start.7 = (s32[768,1]{0,1:T(1,128)S(1)}, s32[768,1]{0,1:T(1,128)}, u32[]{:S(2)}) copy-start(s32[768,1]{0,1:T(1,128)} %param.9) | copy-start | bytes 9220
  11.6 7.0 %copy-start.3 = (bf16[2048,1024]{1,0:T(8,128)(2,1)S(1)}, bf16[2048,1024]{1,0:T(8,128)(2,1)}, u32[]{:S(2)}) copy-start(bf16[2048,1024]{1,0:T(8,128)(2,1)} %weight_ref.3) | copy-start | bytes 12582916
  15.0 7.6 %collective-permute-start.5 = (bf16[1,64,2048]{2,1,0:T(8,128)(2,1)S(1)}, bf16[1,64,2048]{2,1,0:T(8,128)(2,1)S(1)}, u32[]{:S(2)}, u32[]{:S(2)}) collective-permute-start(bf16[1,64,2048]{2,1,0:T(8,128)(2,1)S(1)} %collective-permute-done.refs_0_), channel_id=1, source_target_pairs={{0,16},{16,0},{1,17},{17,1},{2,18},{18,2},{3,19},{19,3},{4,20},{20... | collective-permute-start | bytes 786440 | tf_op jit(solution)/shard_map/ppermute | solution.py:39
  16.7 7.1 %collective-permute-start.6 = (bf16[768,256]{1,0:T(8,128)(2,1)S(1)}, bf16[768,256]{1,0:T(8,128)(2,1)S(1)}, u32[]{:S(2)}, u32[]{:S(2)}) collective-permute-start(bf16[768,256]{1,0:T(8,128)(2,1)S(1)} %get-tuple-element.38), channel_id=1, source_target_pairs={{0,1},{1,0},{2,3},{3,2},{4,5},{5,4},{6,7},{7,6},{8,9},{9,8},{10,11... | collective-permute-start | bytes 1179656 | tf_op jit(solution)/shard_map/ppermute | solution.py:39
  16.7 7.1 %collective-permute-start.7 = (bf16[768,256]{1,0:T(8,128)(2,1)S(1)}, bf16[768,256]{1,0:T(8,128)(2,1)S(1)}, u32[]{:S(2)}, u32[]{:S(2)}) collective-permute-start(bf16[768,256]{1,0:T(8,128)(2,1)S(1)} %get-tuple-element.39), channel_id=1, source_target_pairs={{0,1},{1,0},{2,3},{3,2},{4,5},{5,4},{6,7},{7,6},{8,9},{9,8},{10,11... | collective-permute-start | bytes 1179656 | tf_op jit(solution)/shard_map/ppermute | solution.py:39
  18.6 4.0 %copy-start.6 = (bf16[2,2048,64]{1,2,0:T(8,128)(2,1)S(1)}, bf16[2,2048,64]{1,2,0:T(8,128)(2,1)}, u32[]{:S(2)}) copy-start(bf16[2,2048,64]{1,2,0:T(8,128)(2,1)} %param.12) | copy-start | bytes 1572868
  20.6 8.0 %collective-permute-start.2 = (bf16[1,64,2304]{2,1,0:T(8,128)(2,1)S(1)}, bf16[1,64,2304]{2,1,0:T(8,128)(2,1)S(1)}, u32[]{:S(2)}, u32[]{:S(2)}) collective-permute-start(bf16[1,64,2304]{2,1,0:T(8,128)(2,1)S(1)} %collective-permute-done.1.refs_1_), channel_id=1, source_target_pairs={{0,4},{4,0},{8,12},{12,8},{1,5},{5,1},{9,13},{13,9},{2,6},{6,2},{1... | collective-permute-start | bytes 884744 | tf_op jit(solution)/shard_map/ppermute | solution.py:39
  20.6 9.1 %collective-permute-start.4 = (bf16[1,64,2304]{2,1,0:T(8,128)(2,1)S(1)}, bf16[1,64,2304]{2,1,0:T(8,128)(2,1)S(1)}, u32[]{:S(2)}, u32[]{:S(2)}) collective-permute-start(bf16[1,64,2304]{2,1,0:T(8,128)(2,1)S(1)} %collective-permute-done.1.refs_1_), channel_id=1, source_target_pairs={{0,16},{16,0},{1,17},{17,1},{2,18},{18,2},{3,19},{19,3},{4,20},{20... | collective-permute-start | bytes 884744 | tf_op jit(solution)/shard_map/ppermute | solution.py:39
  24.0 7.1 %copy-start.5 = (bf16[2,64,256]{2,1,0:T(8,128)(2,1)S(1)}, bf16[2,64,256]{2,1,0:T(8,128)(2,1)}, u32[]{:S(2)}) copy-start(bf16[2,64,256]{2,1,0:T(8,128)(2,1)} %refs_0_.1) | copy-start | bytes 196612
  24.0 8.1 %copy-start.4 = (bf16[128,128]{1,0:T(8,128)(2,1)S(1)}, bf16[128,128]{1,0:T(8,128)(2,1)}, u32[]{:S(2)}) copy-start(bf16[128,128]{1,0:T(8,128)(2,1)} %constant.12.clone.matrix_ref) | copy-start | bytes 98308
  24.0 8.1 %copy-start.8 = (s32[128]{0:T(128)S(1)}, s32[128]{0:T(128)}, u32[]{:S(2)}) copy-start(s32[128]{0:T(128)} %param.14) | copy-start | bytes 1540
  24.0 14.0 %collective-permute-start.11 = (bf16[768,256]{1,0:T(8,128)(2,1)S(1)}, bf16[768,256]{1,0:T(8,128)(2,1)S(1)}, u32[]{:S(2)}, u32[]{:S(2)}) collective-permute-start(bf16[768,256]{1,0:T(8,128)(2,1)S(1)} %add.8), channel_id=1, source_target_pairs={{0,2},{1,3},{2,0},{3,1},{4,6},{5,7},{6,4},{7,5},{8,10},{9,11},{10,... | collective-permute-start | bytes 1179656 | tf_op jit(solution)/shard_map/ppermute | solution.py:39
  28.6 7.1 %collective-permute-start.3 = (bf16[1,64,2304]{2,1,0:T(8,128)(2,1)S(1)}, bf16[1,64,2304]{2,1,0:T(8,128)(2,1)S(1)}, u32[]{:S(2)}, u32[]{:S(2)}) collective-permute-start(bf16[1,64,2304]{2,1,0:T(8,128)(2,1)S(1)} %collective-permute-done.2.refs_2_.refs_1_), channel_id=1, source_target_pairs={{0,16},{16,0},{1,17},{17,1},{2,18},{18,2},{3,19},{19,3},{4,20},{20... | collective-permute-start | bytes 884744 | tf_op jit(solution)/shard_map/ppermute | solution.py:39
  31.0 1.7 %collective-permute-start.8 = (bf16[64,768]{1,0:T(8,128)(2,1)S(1)}, bf16[64,768]{1,0:T(8,128)(2,1)S(1)}, u32[]{:S(2)}, u32[]{:S(2)}) collective-permute-start(bf16[64,768]{1,0:T(8,128)(2,1)S(1)} %low_rows.3.refs_0_), channel_id=1, source_target_pairs={{0,1},{1,0},{2,3},{3,2},{4,5},{5,4},{6,7},{7,6},{8,9},{9,8},{10,11... | collective-permute-start | bytes 294920 | tf_op jit(solution)/shard_map/ppermute | solution.py:39
  31.1 6.7 %collective-permute-start.10 = (bf16[2,64,256]{2,1,0:T(8,128)(2,1)S(1)}, bf16[2,64,256]{2,1,0:T(8,128)(2,1)S(1)}, u32[]{:S(2)}, u32[]{:S(2)}) collective-permute-start(bf16[2,64,256]{2,1,0:T(8,128)(2,1)S(1)} %copy-done.5), channel_id=1, source_target_pairs={{0,4},{4,0},{8,12},{12,8},{1,5},{5,1},{9,13},{13,9},{2,6},{6,2},{1... | collective-permute-start | bytes 196616 | tf_op jit(solution)/shard_map/ppermute | solution.py:39
  32.1 5.9 %copy-start.9 = (f32[256]{0:T(256)S(1)}, f32[256]{0:T(256)}, u32[]{:S(2)}) copy-start(f32[256]{0:T(256)} %param.11) | copy-start | bytes 3076
  32.7 5.4 %collective-permute-start.9 = (bf16[64,768]{1,0:T(8,128)(2,1)S(1)}, bf16[64,768]{1,0:T(8,128)(2,1)S(1)}, u32[]{:S(2)}, u32[]{:S(2)}) collective-permute-start(bf16[64,768]{1,0:T(8,128)(2,1)S(1)} %add.7.mine_ref), channel_id=1, source_target_pairs={{0,2},{1,3},{2,0},{3,1},{4,6},{5,7},{6,4},{7,5},{8,10},{9,11},{10,... | collective-permute-start | bytes 294920 | tf_op jit(solution)/shard_map/ppermute | solution.py:39
  36.1 3.7 %collective-permute-start.14 = (bf16[64,256]{1,0:T(8,128)(2,1)S(1)}, bf16[64,256]{1,0:T(8,128)(2,1)S(1)}, u32[]{:S(2)}, u32[]{:S(2)}) collective-permute-start(bf16[64,256]{1,0:T(8,128)(2,1)S(1)} %compact.1.refs_0_), channel_id=1, source_target_pairs={{0,3},{1,2},{2,1},{3,0},{4,7},{5,6},{6,5},{7,4},{8,11},{9,10},{10,... | collective-permute-start | bytes 98312 | tf_op jit(solution)/shard_map/ppermute | solution.py:39
  36.2 4.0 %collective-permute-start.13 = (bf16[64,256]{1,0:T(8,128)(2,1)S(1)}, bf16[64,256]{1,0:T(8,128)(2,1)S(1)}, u32[]{:S(2)}, u32[]{:S(2)}) collective-permute-start(bf16[64,256]{1,0:T(8,128)(2,1)S(1)} %compact.1.refs_0_), channel_id=1, source_target_pairs={{0,2},{1,3},{2,0},{3,1},{4,6},{5,7},{6,4},{7,5},{8,10},{9,11},{10,... | collective-permute-start | bytes 98312 | tf_op jit(solution)/shard_map/ppermute | solution.py:39
  37.7 2.5 %collective-permute-start.12 = (bf16[64,256]{1,0:T(8,128)(2,1)S(1)}, bf16[64,256]{1,0:T(8,128)(2,1)S(1)}, u32[]{:S(2)}, u32[]{:S(2)}) collective-permute-start(bf16[64,256]{1,0:T(8,128)(2,1)S(1)} %compact.1.refs_0_), channel_id=1, source_target_pairs={{0,1},{1,0},{2,3},{3,2},{4,5},{5,4},{6,7},{7,6},{8,9},{9,8},{10,11... | collective-permute-start | bytes 98312 | tf_op jit(solution)/shard_map/ppermute | solution.py:39

commit v20 on v19

--- a/solution.py
+++ b/solution.py
@@ -215,9 +215,11 @@
     )(chosen, piece)
 
 
-def most_kernel(mine_ref, theirs_ref, up_ref, mask_ref, near_ref, scale_ref, bits_ref, matrix_ref, *refs):
+def most_kernel(mine_ref, theirs_ref, up_ref, mask_ref, near_ref, piece_ref, scale_ref, bits_ref, matrix_ref, *refs):
+    terms, (last_ref, out_ref) = refs[:-2], refs[-2:]
+    rank, width = piece_ref.shape[1], out_ref.shape[1]
     low = (mine_ref[...].astype(F32) + theirs_ref[...].astype(F32)).astype(BF16).T
-    rank, columns = low.shape[1], mask_ref.shape[1]
+    columns = mask_ref.shape[1]
     signs = (1 - 2 * bits_ref[...]).astype(F32)
     ups = [up_ref[...]]
     for k in range(near_ref.shape[0]):
@@ -228,32 +230,37 @@
         ups.append(jnp.zeros((missing, up_ref.shape[1]), BF16))
     spread = jnp.concatenate([low] * (columns // rank), axis=1) * mask_ref[...]
     delta = jnp.dot(spread, jnp.concatenate(ups, axis=0), preferred_element_type=F32)
-    value = functools.reduce(jnp.add, [ref[...].astype(F32) for ref in refs[:-1]]) * scale_ref[...]
-    refs[-1][...] = jnp.concatenate(rotate(value, signs, matrix_ref[...]), axis=1) + delta
-
-
-def most(mine, theirs, up, mask, near, scale, bits, matrix, terms):
+    value = functools.reduce(jnp.add, [ref[...].astype(F32) for ref in terms]) * scale_ref[...]
+    out_ref[...] = jnp.concatenate(rotate(value, signs, matrix_ref[...]), axis=1) + delta
+    for k in range(piece_ref.shape[0]):
+        turned = rotate(piece_ref[k, :, piece_ref.shape[2] - width :].astype(F32), signs, matrix_ref[...])
+        last_ref[k * rank : (k + 1) * rank] = jnp.concatenate(turned, axis=1).astype(BF16)
+
+
+def most(mine, theirs, up, mask, near, piece, scale, bits, matrix, terms):
     return pl.pallas_call(
         most_kernel,
-        in_specs=[VMEM] * (8 + len(terms)),
-        out_specs=VMEM,
-        out_shape=jax.ShapeDtypeStruct(terms[0].shape, F32),
+        in_specs=[VMEM] * (9 + len(terms)),
+        out_specs=[VMEM] * 2,
+        out_shape=[
+            jax.ShapeDtypeStruct((piece.shape[0] * piece.shape[1], terms[0].shape[1]), BF16),
+            jax.ShapeDtypeStruct(terms[0].shape, F32),
+        ],
         compiler_params=params(32),
         cost_estimate=COST,
         name="most",
-    )(mine, theirs, up, mask, near, scale, bits, matrix, *terms)
-
-
-def final_kernel(pick_ref, piece_ref, bits_ref, matrix_ref, most_ref, *refs):
+    )(mine, theirs, up, mask, near, piece, scale, bits, matrix, *terms)
+
+
+def final_kernel(pick_ref, last_ref, most_ref, *refs):
     kept_refs, (out_ref, half_ref, sems) = refs[:-3], refs[-3:]
-    share, width = piece_ref.shape[0], out_ref.shape[1]
-    features, slots = piece_ref.shape[2] - width, pick_ref.shape[1] // share
-    signs = (1 - 2 * bits_ref[...]).astype(F32)
+    rank, slots = kept_refs[0].shape
+    share = last_ref.shape[0] // rank
+    slots = slots // share
     low = functools.reduce(jnp.add, [ref[...].astype(F32) for ref in kept_refs]).astype(BF16).T
     deltas = []
     for k in range(share):
-        turned = rotate(piece_ref[k, :, features:].astype(F32), signs, matrix_ref[...])
-        up = jnp.concatenate(turned, axis=1).astype(BF16)
+        up = last_ref[k * rank : (k + 1) * rank]
         deltas.append(jnp.dot(low[k * slots : (k + 1) * slots], up, preferred_element_type=F32).astype(BF16))
     delta = deltas[0] if share == 1 else jnp.concatenate(deltas, axis=0)
     count, rows, _ = half_ref.shape
@@ -268,17 +275,17 @@
         copy.wait()
 
 
-def final(kept, pick, piece, bits, matrix, rest):
+def final(kept, pick, last, rest):
     return pl.pallas_call(
         final_kernel,
-        in_specs=[VMEM] * (5 + len(kept)),
+        in_specs=[VMEM] * (3 + len(kept)),
         out_specs=pl.BlockSpec(memory_space=pl.ANY),
         out_shape=jax.ShapeDtypeStruct(rest.shape, BF16),
         scratch_shapes=[pltpu.VMEM((2, rest.shape[0] // 2, rest.shape[1]), BF16), pltpu.SemaphoreType.DMA((2,))],
         compiler_params=params(32),
         cost_estimate=COST,
         name="final",
-    )(pick, piece, bits, matrix, rest, *kept)
+    )(pick, last, rest, *kept)
 
 
 def local(tokens, adapter_ids, base_weight, channel_scale, adapter_down, adapter_up, sign_bits):
@@ -362,8 +369,8 @@
     piece, up, mask = together(swapped[-1][2], up, mask)
     kept = compact(chosen, piece)
     kept = [kept] + [swap(kept, "tp", offset) for offset in range(1, parts)]
-    rest = most(low, other, up, mask, near_up, scale, bits, matrix, sums[0])
-    return final(kept, pick, piece, bits, matrix, rest)
+    last, rest = most(low, other, up, mask, near_up, piece, scale, bits, matrix, sums[0])
+    return final(kept, pick, last, rest)
 
 
 def solution(mesh):

time: 41.8 us -> 41.7 us (level)
  transfers between devices with their start and end apart: 15 -> 15, of which waited for: 7 -> 7; matrix products, arithmetic and copies ran while one was open for 2% -> 2% of each run, Pallas kernels for 22% -> 23%
where the time goes in v20:
time: 41.7 us; the launch traced here: 41.5 us
  starting transfers between devices  16.5 us (40%)
  Pallas kernels  10.6 us (25%)
  waiting for transfers between devices  8.29 us (20%)
  local copies, waits for them, and re-layouts  5.84 us (14%)
    ppermute x15, starting transfers between devices, swap(): lax.ppermute(x, axis, [(i, i ^ bit) for i in range(lax.axis_size(axis))])  16.5 us
    ppermute x15, waiting for transfers between devices, swap(): lax.ppermute(x, axis, [(i, i ^ bit) for i in range(lax.axis_size(axis))])  8.29 us
    unnamed x20, local copies, waits for them, and re-layouts  4.12 us
    pallas_call x2, Pallas kernels, partials(): pl.pallas_call(functools.partial(partial_kernel, offsets, parts), in_spec...  3.66 us
    pallas_call x2, Pallas kernels, low_rows(): pl.pallas_call(functools.partial(low_kernel, groups, here, share, rank, b...  2.45 us
    pallas_call x1, Pallas kernels, picked(): pl.pallas_call(functools.partial(pick_kernel, named, here, share), in_spe...  1.33 us
    pallas_call x1, Pallas kernels, final(): pl.pallas_call(final_kernel, in_specs=[VMEM] * (3 + len(kept)), out_specs...  1.23 us
    dynamic_slice x1, local copies, waits for them, and re-layouts, local(): own = lax.dynamic_slice_in_dim(down, start, share, 0)  0.97 us
  transfers between devices with their start and end apart: 15, of which 7 were waited for; matrix products, arithmetic and copies ran while one was open for 2% of the time, Pallas kernels for 23%

profile of v20, /device:TPU:0, one launch (start us, length us, event | category | flops | bytes accessed | tf_op | source)
XLA Modules:
  0.0 41.5 jit_solution(2156942703437997542)
XLA Ops:
  0.0 1.0 %dynamic-slice_bitcast_fusion = bf16[1,64,2048]{2,1,0:T(8,128)(2,1)S(1)} fusion(bf16[2,2048,64]{1,2,0:T(8,128)(2,1)} %param.12, s32[]{:T(128)S(6)} %select_n.4), kind=kLoop, calls=%fused_computation.1 | loop fusion | bytes 524292 | tf_op jit(solution)/shard_map/dynamic_slice | solution.py:302
  1.0 3.1 %collective-permute-start = (bf16[1,64,2048]{2,1,0:T(8,128)(2,1)S(1)}, bf16[1,64,2048]{2,1,0:T(8,128)(2,1)S(1)}, u32[]{:S(2)}, u32[]{:S(2)}) collective-permute-start(bf16[1,64,2048]{2,1,0:T(8,128)(2,1)S(1)} %dynamic-slice_bitcast_fusion), channel_id=1, source_target_pairs={{0,4},{4,0},{8,12},{12,8},{1,5},{5,1},{9,13},{13,9},{2,6},{6,2},{1... | collective-permute-start | bytes 786440 | tf_op jit(solution)/shard_map/ppermute | solution.py:39
  4.1 0.8 %constant_dynamic-slice_fusion = bf16[1,64,256]{2,1,0:T(8,128)(2,1)S(1)} fusion(bf16[2,64,256]{2,1,0:T(8,128)(2,1)} %refs_0_.1, s32[]{:T(128)S(6)} %select_n.4), kind=kLoop, calls=%fused_computation.2 | loop fusion | bytes 65540 | tf_op jit(solution)/shard_map/dynamic_slice | solution.py:304
  4.8 2.7 %collective-permute-start.1 = (bf16[1,64,2304]{2,1,0:T(8,128)(2,1)S(1)}, bf16[1,64,2304]{2,1,0:T(8,128)(2,1)S(1)}, u32[]{:S(2)}, u32[]{:S(2)}) collective-permute-start(bf16[1,64,2304]{2,1,0:T(8,128)(2,1)S(1)} %pad_maximum_fusion), channel_id=1, source_target_pairs={{0,8},{4,12},{8,0},{12,4},{1,9},{5,13},{9,1},{13,5},{2,10},{6,14},... | collective-permute-start | bytes 884744 | tf_op jit(solution)/shard_map/ppermute | solution.py:39
  7.5 1.9 %copy-done = bf16[768,2048]{1,0:T(8,128)(2,1)S(1)} copy-done((bf16[768,2048]{1,0:T(8,128)(2,1)S(1)}, bf16[768,2048]{1,0:T(8,128)(2,1)}, u32[]{:S(2)}) %copy-start) | copy-done | bytes 3145752
  9.4 2.2 %copy-done.2 = bf16[2048,1024]{1,0:T(8,128)(2,1)S(1)} copy-done((bf16[2048,1024]{1,0:T(8,128)(2,1)S(1)}, bf16[2048,1024]{1,0:T(8,128)(2,1)}, u32[]{:S(2)}) %copy-start.2) | copy-done | bytes 4194328
  11.6 2.7 %partials.2 = (bf16[768,256]{1,0:T(8,128)(2,1)S(1)}, bf16[768,256]{1,0:T(8,128)(2,1)S(1)}, bf16[768,256]{1,0:T(8,128)(2,1)S(1)}) custom-call(bf16[768,2048]{1,0:T(8,128)(2,1)S(1)} %copy-done, bf16[2048,1024]{1,0:T(8,128)(2,1)S(1)} %copy-done.2), custom_call_target="tpu_custom_call" | custom-call | flops 4000000000 | bytes 1 | tf_op jit(solution)/shard_map/partials/pallas_call | solution.py:70
  14.3 0.8 %collective-permute-done.refs_0_ = bf16[1,64,2048]{2,1,0:T(8,128)(2,1)S(1)} collective-permute-done((bf16[1,64,2048]{2,1,0:T(8,128)(2,1)S(1)}, bf16[1,64,2048]{2,1,0:T(8,128)(2,1)S(1)}, u32[]{:S(2)}, u32[]{:S(2)}) %collective-permute-start) | collective-permute-done | bytes 262176 | tf_op jit(solution)/shard_map/ppermute | solution.py:39
  15.0 1.7 %collective-permute-start.4 = (bf16[1,64,2048]{2,1,0:T(8,128)(2,1)S(1)}, bf16[1,64,2048]{2,1,0:T(8,128)(2,1)S(1)}, u32[]{:S(2)}, u32[]{:S(2)}) collective-permute-start(bf16[1,64,2048]{2,1,0:T(8,128)(2,1)S(1)} %collective-permute-done.refs_0_), channel_id=1, source_target_pairs={{0,16},{16,0},{1,17},{17,1},{2,18},{18,2},{3,19},{19,3},{4,20},{20... | collective-permute-start | bytes 786440 | tf_op jit(solution)/shard_map/ppermute | solution.py:39
  16.7 0.5 %collective-permute-start.6 = (bf16[768,256]{1,0:T(8,128)(2,1)S(1)}, bf16[768,256]{1,0:T(8,128)(2,1)S(1)}, u32[]{:S(2)}, u32[]{:S(2)}) collective-permute-start(bf16[768,256]{1,0:T(8,128)(2,1)S(1)} %get-tuple-element.38), channel_id=1, source_target_pairs={{0,1},{1,0},{2,3},{3,2},{4,5},{5,4},{6,7},{7,6},{8,9},{9,8},{10,11... | collective-permute-start | bytes 1179656 | tf_op jit(solution)/shard_map/ppermute | solution.py:39
  17.2 1.3 %picked.1 = (bf16[768,256]{1,0:T(8,128)(2,1)S(1)}, bf16[256,2048]{1,0:T(8,128)(2,1)S(1)}) custom-call(s32[1,768]{1,0:T(1,128)S(1)} %bitcast.7, bf16[768,2048]{1,0:T(8,128)(2,1)S(1)} %copy-done.1), custom_call_target="tpu_custom_call" | custom-call | flops 1 | bytes 1 | tf_op jit(solution)/shard_map/picked/pallas_call | solution.py:184
  18.6 1.0 %partials.3.refs_0_ = bf16[768,256]{1,0:T(8,128)(2,1)S(1)} custom-call(bf16[768,2048]{1,0:T(8,128)(2,1)S(1)} %copy-done.1, bf16[2048,1024]{1,0:T(8,128)(2,1)S(1)} %copy-done.3, bf16[768,256]{1,0:T(8,128)(2,1)S(1)} %get-tuple-element.31.refs_0_), custom_call_target="tpu_custom_call" | custom-call | flops 1 | bytes 1 | tf_op jit(solution)/shard_map/partials/pallas_call | solution.py:70
  19.6 1.0 %collective-permute-done.1.refs_1_ = bf16[1,64,2304]{2,1,0:T(8,128)(2,1)S(1)} collective-permute-done((bf16[1,64,2304]{2,1,0:T(8,128)(2,1)S(1)}, bf16[1,64,2304]{2,1,0:T(8,128)(2,1)S(1)}, u32[]{:S(2)}, u32[]{:S(2)}) %collective-permute-start.1) | collective-permute-done | bytes 294944 | tf_op jit(solution)/shard_map/ppermute | solution.py:39
  20.6 1.5 %collective-permute-start.2 = (bf16[1,64,2304]{2,1,0:T(8,128)(2,1)S(1)}, bf16[1,64,2304]{2,1,0:T(8,128)(2,1)S(1)}, u32[]{:S(2)}, u32[]{:S(2)}) collective-permute-start(bf16[1,64,2304]{2,1,0:T(8,128)(2,1)S(1)} %collective-permute-done.1.refs_1_), channel_id=1, source_target_pairs={{0,16},{16,0},{1,17},{17,1},{2,18},{18,2},{3,19},{19,3},{4,20},{20... | collective-permute-start | bytes 884744 | tf_op jit(solution)/shard_map/ppermute | solution.py:39
  22.2 0.4 %collective-permute-done.4.refs_2_ = bf16[1,64,2048]{2,1,0:T(8,128)(2,1)S(1)} collective-permute-done((bf16[1,64,2048]{2,1,0:T(8,128)(2,1)S(1)}, bf16[1,64,2048]{2,1,0:T(8,128)(2,1)S(1)}, u32[]{:S(2)}, u32[]{:S(2)}) %collective-permute-start.4) | collective-permute-done | bytes 262176 | tf_op jit(solution)/shard_map/ppermute | solution.py:39
  22.6 1.2 %low_rows.2.refs_2_ = f32[64,768]{1,0:T(8,128)S(1)} custom-call(s32[1,768]{1,0:T(1,128)S(1)} %bitcast.8, bf16[768,2048]{1,0:T(8,128)(2,1)S(1)} %copy-done.1, bf16[1,64,2048]{2,1,0:T(8,128)(2,1)S(1)} %collective-permute-done.refs_0_, bf16[1,64,2304]{2,1,0:T(8,128)(2,1)S(1)} %collective-permute-done.1.refs_1_, ...), custom_call_target="tpu_custom_call" | custom-call | flops 2000000000 | bytes 1 | tf_op jit(solution)/shard_map/low_rows/pallas_call | solution.py:125
  23.9 0.1 add.8
  24.0 1.3 %collective-permute-start.11 = (bf16[768,256]{1,0:T(8,128)(2,1)S(1)}, bf16[768,256]{1,0:T(8,128)(2,1)S(1)}, u32[]{:S(2)}, u32[]{:S(2)}) collective-permute-start(bf16[768,256]{1,0:T(8,128)(2,1)S(1)} %add.8), channel_id=1, source_target_pairs={{0,2},{1,3},{2,0},{3,1},{4,6},{5,7},{6,4},{7,5},{8,10},{9,11},{10,... | collective-permute-start | bytes 1179656 | tf_op jit(solution)/shard_map/ppermute | solution.py:39
  25.3 3.3 %collective-permute-done.3.refs_1_.refs_2_ = bf16[1,64,2304]{2,1,0:T(8,128)(2,1)S(1)} collective-permute-done((bf16[1,64,2304]{2,1,0:T(8,128)(2,1)S(1)}, bf16[1,64,2304]{2,1,0:T(8,128)(2,1)S(1)}, u32[]{:S(2)}, u32[]{:S(2)}) %collective-permute-start.3) | collective-permute-done | bytes 294944 | tf_op jit(solution)/shard_map/ppermute | solution.py:39
  28.6 1.1 %collective-permute-start.9 = (bf16[1,64,2304]{2,1,0:T(8,128)(2,1)S(1)}, bf16[1,64,2304]{2,1,0:T(8,128)(2,1)S(1)}, u32[]{:S(2)}, u32[]{:S(2)}) collective-permute-start(bf16[1,64,2304]{2,1,0:T(8,128)(2,1)S(1)} %collective-permute-done.3.refs_1_.refs_2_), channel_id=1, source_target_pairs={{0,16},{16,0},{1,17},{17,1},{2,18},{18,2},{3,19},{19,3},{4,20},{20... | collective-permute-start | bytes 884744 | tf_op jit(solution)/shard_map/ppermute | solution.py:39
  29.8 1.2 %low_rows.3.refs_0_ = bf16[64,768]{1,0:T(8,128)(2,1)S(1)} custom-call(s32[1,768]{1,0:T(1,128)S(1)} %bitcast.9, bf16[768,2048]{1,0:T(8,128)(2,1)S(1)} %copy-done.1, bf16[1,64,2304]{2,1,0:T(8,128)(2,1)S(1)} %collective-permute-done.2.refs_0_.refs_3_, bf16[1,64,2304]{2,1,0:T(8,128)(2,1)S(1)} %collective-permute-done.3.refs_1_.refs_2_, ...), custom_call_target="tpu_custom_call" | custom-call | flops 5000000000 | bytes 1 | tf_op jit(solution)/shard_map/low_rows/pallas_call | solution.py:125
  31.1 1.0 %collective-permute-start.10 = (bf16[2,64,256]{2,1,0:T(8,128)(2,1)S(1)}, bf16[2,64,256]{2,1,0:T(8,128)(2,1)S(1)}, u32[]{:S(2)}, u32[]{:S(2)}) collective-permute-start(bf16[2,64,256]{2,1,0:T(8,128)(2,1)S(1)} %copy-done.4), channel_id=1, source_target_pairs={{0,4},{4,0},{8,12},{12,8},{1,5},{5,1},{9,13},{13,9},{2,6},{6,2},{1... | collective-permute-start | bytes 196616 | tf_op jit(solution)/shard_map/ppermute | solution.py:39
  32.1 0.5 %rotated_ups.1 = (bf16[320,256]{1,0:T(8,128)(2,1)S(1)}, bf16[768,512]{1,0:T(8,128)(2,1)S(1)}) custom-call(s32[1,768]{1,0:T(1,128)S(1)} %bitcast.10, s32[1,128]{1,0:T(1,128)S(1)} %bitcast.11, bf16[128,128]{1,0:T(8,128)(2,1)S(1)} %copy-done.5, bf16[2,64,256]{2,1,0:T(8,128)(2,1)S(1)} %copy-done.4, bf16[1,64,2304]{2,1,0:T(8,128)(2,1)S(1)} %collective-permute-done.1.refs_1_, ...), custom_call_target="tpu_custom_call" | custom-call | flops 1 | bytes 1 | tf_op jit(solution)/shard_map/rotated_ups/pallas_call | solution.py:153
  32.7 1.6 %collective-permute-start.8 = (bf16[64,768]{1,0:T(8,128)(2,1)S(1)}, bf16[64,768]{1,0:T(8,128)(2,1)S(1)}, u32[]{:S(2)}, u32[]{:S(2)}) collective-permute-start(bf16[64,768]{1,0:T(8,128)(2,1)S(1)} %add.7.mine_ref), channel_id=1, source_target_pairs={{0,2},{1,3},{2,0},{3,1},{4,6},{5,7},{6,4},{7,5},{8,10},{9,11},{10,... | collective-permute-start | bytes 294920 | tf_op jit(solution)/shard_map/ppermute | solution.py:39
  34.2 1.4 %collective-permute-done.9.piece_ref = bf16[1,64,2304]{2,1,0:T(8,128)(2,1)S(1)} collective-permute-done((bf16[1,64,2304]{2,1,0:T(8,128)(2,1)S(1)}, bf16[1,64,2304]{2,1,0:T(8,128)(2,1)S(1)}, u32[]{:S(2)}, u32[]{:S(2)}) %collective-permute-start.9) | collective-permute-done | bytes 294944 | tf_op jit(solution)/shard_map/ppermute | solution.py:39
  35.7 0.4 %compact.1.refs_0_ = bf16[64,256]{1,0:T(8,128)(2,1)S(1)} custom-call(bf16[256,2048]{1,0:T(8,128)(2,1)S(1)} %get-tuple-element.52.chosen_ref, bf16[1,64,2304]{2,1,0:T(8,128)(2,1)S(1)} %collective-permute-done.9.piece_ref), custom_call_target="tpu_custom_call" | custom-call | flops 2000000000 | bytes 1 | tf_op jit(solution)/shard_map/compact/pallas_call | solution.py:207
  36.2 1.5 %collective-permute-start.13 = (bf16[64,256]{1,0:T(8,128)(2,1)S(1)}, bf16[64,256]{1,0:T(8,128)(2,1)S(1)}, u32[]{:S(2)}, u32[]{:S(2)}) collective-permute-start(bf16[64,256]{1,0:T(8,128)(2,1)S(1)} %compact.1.refs_0_), channel_id=1, source_target_pairs={{0,2},{1,3},{2,0},{3,1},{4,6},{5,7},{6,4},{7,5},{8,10},{9,11},{10,... | collective-permute-start | bytes 98312 | tf_op jit(solution)/shard_map/ppermute | solution.py:39
  37.7 0.3 collective-permute-start.12
  38.1 0.8 %most.1 = (bf16[64,256]{1,0:T(8,128)(2,1)S(1)}, f32[768,256]{1,0:T(8,128)S(1)}) custom-call(bf16[64,768]{1,0:T(8,128)(2,1)S(1)} %add.7.mine_ref, bf16[64,768]{1,0:T(8,128)(2,1)S(1)} %collective-permute-done.8.theirs_ref, bf16[320,256]{1,0:T(8,128)(2,1)S(1)} %get-tuple-element.43.up_ref, bf16[768,512]{1,0:T(8,128)(2,1)S(1)} %get-tuple-element.44.mask_ref, ...), custom_call_target="tpu_custom_call" | custom-call | flops 1 | bytes 1 | tf_op jit(solution)/shard_map/most/pallas_call | solution.py:241
  38.9 1.0 %collective-permute-done.14.refs_3_ = bf16[64,256]{1,0:T(8,128)(2,1)S(1)} collective-permute-done((bf16[64,256]{1,0:T(8,128)(2,1)S(1)}, bf16[64,256]{1,0:T(8,128)(2,1)S(1)}, u32[]{:S(2)}, u32[]{:S(2)}) %collective-permute-start.14) | collective-permute-done | bytes 32800 | tf_op jit(solution)/shard_map/ppermute | solution.py:39
  39.9 0.4 collective-permute-done.13.refs_2_
  40.2 1.2 %final.1 = bf16[768,256]{1,0:T(8,128)(2,1)} custom-call(bf16[768,256]{1,0:T(8,128)(2,1)S(1)} %get-tuple-element.34.pick_ref, bf16[64,256]{1,0:T(8,128)(2,1)S(1)} %get-tuple-element.50.last_ref, f32[768,256]{1,0:T(8,128)S(1)} %get-tuple-element.51.most_ref, bf16[64,256]{1,0:T(8,128)(2,1)S(1)} %compact.1.refs_0_, ...), custom_call_target="tpu_custom_call" | custom-call | flops 1 | bytes 1 | tf_op jit(solution)/shard_map/final/pallas_call | solution.py:279
  (32 shorter events, 0.3 us)
Async XLA Ops:
  1.0 14.1 %collective-permute-start = (bf16[1,64,2048]{2,1,0:T(8,128)(2,1)S(1)}, bf16[1,64,2048]{2,1,0:T(8,128)(2,1)S(1)}, u32[]{:S(2)}, u32[]{:S(2)}) collective-permute-start(bf16[1,64,2048]{2,1,0:T(8,128)(2,1)S(1)} %dynamic-slice_bitcast_fusion), channel_id=1, source_target_pairs={{0,4},{4,0},{8,12},{12,8},{1,5},{5,1},{9,13},{13,9},{2,6},{6,2},{1... | collective-permute-start | bytes 786440 | tf_op jit(solution)/shard_map/ppermute | solution.py:39
  4.8 15.8 %collective-permute-start.1 = (bf16[1,64,2304]{2,1,0:T(8,128)(2,1)S(1)}, bf16[1,64,2304]{2,1,0:T(8,128)(2,1)S(1)}, u32[]{:S(2)}, u32[]{:S(2)}) collective-permute-start(bf16[1,64,2304]{2,1,0:T(8,128)(2,1)S(1)} %pad_maximum_fusion), channel_id=1, source_target_pairs={{0,8},{4,12},{8,0},{12,4},{1,9},{5,13},{9,1},{13,5},{2,10},{6,14},... | collective-permute-start | bytes 884744 | tf_op jit(solution)/shard_map/ppermute | solution.py:39
  7.5 1.9 %copy-start = (bf16[768,2048]{1,0:T(8,128)(2,1)S(1)}, bf16[768,2048]{1,0:T(8,128)(2,1)}, u32[]{:S(2)}) copy-start(bf16[768,2048]{1,0:T(8,128)(2,1)} %tokens_ref.9) | copy-start | bytes 9437188
  9.4 2.2 %copy-start.2 = (bf16[2048,1024]{1,0:T(8,128)(2,1)S(1)}, bf16[2048,1024]{1,0:T(8,128)(2,1)}, u32[]{:S(2)}) copy-start(bf16[2048,1024]{1,0:T(8,128)(2,1)} %weight_ref.3) | copy-start | bytes 12582916
  11.6 5.6 %copy-start.1 = (bf16[768,2048]{1,0:T(8,128)(2,1)S(1)}, bf16[768,2048]{1,0:T(8,128)(2,1)}, u32[]{:S(2)}) copy-start(bf16[768,2048]{1,0:T(8,128)(2,1)} %tokens_ref.9) | copy-start | bytes 9437188
  11.6 5.6 %copy-start.7 = (s32[768,1]{0,1:T(1,128)S(1)}, s32[768,1]{0,1:T(1,128)}, u32[]{:S(2)}) copy-start(s32[768,1]{0,1:T(1,128)} %param.9) | copy-start | bytes 9220
  11.6 7.0 %copy-start.3 = (bf16[2048,1024]{1,0:T(8,128)(2,1)S(1)}, bf16[2048,1024]{1,0:T(8,128)(2,1)}, u32[]{:S(2)}) copy-start(bf16[2048,1024]{1,0:T(8,128)(2,1)} %weight_ref.3) | copy-start | bytes 12582916
  15.0 7.6 %collective-permute-start.4 = (bf16[1,64,2048]{2,1,0:T(8,128)(2,1)S(1)}, bf16[1,64,2048]{2,1,0:T(8,128)(2,1)S(1)}, u32[]{:S(2)}, u32[]{:S(2)}) collective-permute-start(bf16[1,64,2048]{2,1,0:T(8,128)(2,1)S(1)} %collective-permute-done.refs_0_), channel_id=1, source_target_pairs={{0,16},{16,0},{1,17},{17,1},{2,18},{18,2},{3,19},{19,3},{4,20},{20... | collective-permute-start | bytes 786440 | tf_op jit(solution)/shard_map/ppermute | solution.py:39
  16.7 7.1 %collective-permute-start.5 = (bf16[768,256]{1,0:T(8,128)(2,1)S(1)}, bf16[768,256]{1,0:T(8,128)(2,1)S(1)}, u32[]{:S(2)}, u32[]{:S(2)}) collective-permute-start(bf16[768,256]{1,0:T(8,128)(2,1)S(1)} %get-tuple-element.37), channel_id=1, source_target_pairs={{0,1},{1,0},{2,3},{3,2},{4,5},{5,4},{6,7},{7,6},{8,9},{9,8},{10,11... | collective-permute-start | bytes 1179656 | tf_op jit(solution)/shard_map/ppermute | solution.py:39
  16.7 7.1 %collective-permute-start.6 = (bf16[768,256]{1,0:T(8,128)(2,1)S(1)}, bf16[768,256]{1,0:T(8,128)(2,1)S(1)}, u32[]{:S(2)}, u32[]{:S(2)}) collective-permute-start(bf16[768,256]{1,0:T(8,128)(2,1)S(1)} %get-tuple-element.38), channel_id=1, source_target_pairs={{0,1},{1,0},{2,3},{3,2},{4,5},{5,4},{6,7},{7,6},{8,9},{9,8},{10,11... | collective-permute-start | bytes 1179656 | tf_op jit(solution)/shard_map/ppermute | solution.py:39
  18.6 4.0 %copy-start.6 = (bf16[2,2048,64]{1,2,0:T(8,128)(2,1)S(1)}, bf16[2,2048,64]{1,2,0:T(8,128)(2,1)}, u32[]{:S(2)}) copy-start(bf16[2,2048,64]{1,2,0:T(8,128)(2,1)} %param.12) | copy-start | bytes 1572868
  20.6 8.0 %collective-permute-start.3 = (bf16[1,64,2304]{2,1,0:T(8,128)(2,1)S(1)}, bf16[1,64,2304]{2,1,0:T(8,128)(2,1)S(1)}, u32[]{:S(2)}, u32[]{:S(2)}) collective-permute-start(bf16[1,64,2304]{2,1,0:T(8,128)(2,1)S(1)} %collective-permute-done.1.refs_1_), channel_id=1, source_target_pairs={{0,4},{4,0},{8,12},{12,8},{1,5},{5,1},{9,13},{13,9},{2,6},{6,2},{1... | collective-permute-start | bytes 884744 | tf_op jit(solution)/shard_map/ppermute | solution.py:39
  20.6 9.1 %collective-permute-start.2 = (bf16[1,64,2304]{2,1,0:T(8,128)(2,1)S(1)}, bf16[1,64,2304]{2,1,0:T(8,128)(2,1)S(1)}, u32[]{:S(2)}, u32[]{:S(2)}) collective-permute-start(bf16[1,64,2304]{2,1,0:T(8,128)(2,1)S(1)} %collective-permute-done.1.refs_1_), channel_id=1, source_target_pairs={{0,16},{16,0},{1,17},{17,1},{2,18},{18,2},{3,19},{19,3},{4,20},{20... | collective-permute-start | bytes 884744 | tf_op jit(solution)/shard_map/ppermute | solution.py:39
  24.0 7.1 %copy-start.4 = (bf16[2,64,256]{2,1,0:T(8,128)(2,1)S(1)}, bf16[2,64,256]{2,1,0:T(8,128)(2,1)}, u32[]{:S(2)}) copy-start(bf16[2,64,256]{2,1,0:T(8,128)(2,1)} %refs_0_.1) | copy-start | bytes 196612
  24.0 8.1 %copy-start.5 = (bf16[128,128]{1,0:T(8,128)(2,1)S(1)}, bf16[128,128]{1,0:T(8,128)(2,1)}, u32[]{:S(2)}) copy-start(bf16[128,128]{1,0:T(8,128)(2,1)} %constant.12.clone.matrix_ref) | copy-start | bytes 98308
  24.0 8.1 %copy-start.8 = (s32[128]{0:T(128)S(1)}, s32[128]{0:T(128)}, u32[]{:S(2)}) copy-start(s32[128]{0:T(128)} %param.14) | copy-start | bytes 1540
  24.0 14.0 %collective-permute-start.11 = (bf16[768,256]{1,0:T(8,128)(2,1)S(1)}, bf16[768,256]{1,0:T(8,128)(2,1)S(1)}, u32[]{:S(2)}, u32[]{:S(2)}) collective-permute-start(bf16[768,256]{1,0:T(8,128)(2,1)S(1)} %add.8), channel_id=1, source_target_pairs={{0,2},{1,3},{2,0},{3,1},{4,6},{5,7},{6,4},{7,5},{8,10},{9,11},{10,... | collective-permute-start | bytes 1179656 | tf_op jit(solution)/shard_map/ppermute | solution.py:39
  28.6 7.1 %collective-permute-start.9 = (bf16[1,64,2304]{2,1,0:T(8,128)(2,1)S(1)}, bf16[1,64,2304]{2,1,0:T(8,128)(2,1)S(1)}, u32[]{:S(2)}, u32[]{:S(2)}) collective-permute-start(bf16[1,64,2304]{2,1,0:T(8,128)(2,1)S(1)} %collective-permute-done.3.refs_1_.refs_2_), channel_id=1, source_target_pairs={{0,16},{16,0},{1,17},{17,1},{2,18},{18,2},{3,19},{19,3},{4,20},{20... | collective-permute-start | bytes 884744 | tf_op jit(solution)/shard_map/ppermute | solution.py:39
  31.0 1.7 %collective-permute-start.7 = (bf16[64,768]{1,0:T(8,128)(2,1)S(1)}, bf16[64,768]{1,0:T(8,128)(2,1)S(1)}, u32[]{:S(2)}, u32[]{:S(2)}) collective-permute-start(bf16[64,768]{1,0:T(8,128)(2,1)S(1)} %low_rows.3.refs_0_), channel_id=1, source_target_pairs={{0,1},{1,0},{2,3},{3,2},{4,5},{5,4},{6,7},{7,6},{8,9},{9,8},{10,11... | collective-permute-start | bytes 294920 | tf_op jit(solution)/shard_map/ppermute | solution.py:39
  31.1 6.7 %collective-permute-start.10 = (bf16[2,64,256]{2,1,0:T(8,128)(2,1)S(1)}, bf16[2,64,256]{2,1,0:T(8,128)(2,1)S(1)}, u32[]{:S(2)}, u32[]{:S(2)}) collective-permute-start(bf16[2,64,256]{2,1,0:T(8,128)(2,1)S(1)} %copy-done.4), channel_id=1, source_target_pairs={{0,4},{4,0},{8,12},{12,8},{1,5},{5,1},{9,13},{13,9},{2,6},{6,2},{1... | collective-permute-start | bytes 196616 | tf_op jit(solution)/shard_map/ppermute | solution.py:39
  32.1 5.9 %copy-start.9 = (f32[256]{0:T(256)S(1)}, f32[256]{0:T(256)}, u32[]{:S(2)}) copy-start(f32[256]{0:T(256)} %param.11) | copy-start | bytes 3076
  32.7 5.4 %collective-permute-start.8 = (bf16[64,768]{1,0:T(8,128)(2,1)S(1)}, bf16[64,768]{1,0:T(8,128)(2,1)S(1)}, u32[]{:S(2)}, u32[]{:S(2)}) collective-permute-start(bf16[64,768]{1,0:T(8,128)(2,1)S(1)} %add.7.mine_ref), channel_id=1, source_target_pairs={{0,2},{1,3},{2,0},{3,1},{4,6},{5,7},{6,4},{7,5},{8,10},{9,11},{10,... | collective-permute-start | bytes 294920 | tf_op jit(solution)/shard_map/ppermute | solution.py:39
  36.1 3.7 %collective-permute-start.14 = (bf16[64,256]{1,0:T(8,128)(2,1)S(1)}, bf16[64,256]{1,0:T(8,128)(2,1)S(1)}, u32[]{:S(2)}, u32[]{:S(2)}) collective-permute-start(bf16[64,256]{1,0:T(8,128)(2,1)S(1)} %compact.1.refs_0_), channel_id=1, source_target_pairs={{0,3},{1,2},{2,1},{3,0},{4,7},{5,6},{6,5},{7,4},{8,11},{9,10},{10,... | collective-permute-start | bytes 98312 | tf_op jit(solution)/shard_map/ppermute | solution.py:39
  36.2 4.0 %collective-permute-start.13 = (bf16[64,256]{1,0:T(8,128)(2,1)S(1)}, bf16[64,256]{1,0:T(8,128)(2,1)S(1)}, u32[]{:S(2)}, u32[]{:S(2)}) collective-permute-start(bf16[64,256]{1,0:T(8,128)(2,1)S(1)} %compact.1.refs_0_), channel_id=1, source_target_pairs={{0,2},{1,3},{2,0},{3,1},{4,6},{5,7},{6,4},{7,5},{8,10},{9,11},{10,... | collective-permute-start | bytes 98312 | tf_op jit(solution)/shard_map/ppermute | solution.py:39
  37.7 2.5 %collective-permute-start.12 = (bf16[64,256]{1,0:T(8,128)(2,1)S(1)}, bf16[64,256]{1,0:T(8,128)(2,1)S(1)}, u32[]{:S(2)}, u32[]{:S(2)}) collective-permute-start(bf16[64,256]{1,0:T(8,128)(2,1)S(1)} %compact.1.refs_0_), channel_id=1, source_target_pairs={{0,1},{1,0},{2,3},{3,2},{4,5},{5,4},{6,7},{7,6},{8,9},{9,8},{10,11... | collective-permute-start | bytes 98312 | tf_op jit(solution)/shard_map/ppermute | solution.py:39

commit v21 on v20

--- a/solution.py
+++ b/solution.py
@@ -133,32 +133,48 @@
     )(ids, tokens, *arrays, *more)
 
 
-def ups_kernel(named, terms, here, share, rank, ids_ref, bits_ref, matrix_ref, *refs):
-    up_ref, mask_ref = refs[-2:]
-    width = up_ref.shape[1]
+def join_kernel(first_ref, second_ref, out_ref):
+    out_ref[: first_ref.shape[0]] = first_ref[...]
+    out_ref[first_ref.shape[0] :] = second_ref[...]
+
+
+def joined(first, second):
+    return pl.pallas_call(
+        join_kernel,
+        in_specs=[VMEM] * 2,
+        out_specs=VMEM,
+        out_shape=jax.ShapeDtypeStruct((2 * first.shape[0], *first.shape[1:]), BF16),
+        compiler_params=params(16),
+        cost_estimate=COST,
+        name="joined",
+    )(first, second)
+
+
+def ups_kernel(here, share, named, ids_ref, bits_ref, matrix_ref, first_ref, second_ref, up_ref, mask_ref):
+    half, rank, _ = first_ref.shape
     signs = (1 - 2 * bits_ref[...]).astype(F32)
-    for n, (i, k, cut) in enumerate(terms):
-        turned = rotate(refs[i][k, :, cut : cut + width].astype(F32), signs, matrix_ref[...])
+    ids = jnp.broadcast_to(ids_ref[...], (rank, ids_ref.shape[1])).T
+    for n, name in enumerate(named):
+        turned = rotate((first_ref if n < half else second_ref)[n % half].astype(F32), signs, matrix_ref[...])
         up_ref[n * rank : (n + 1) * rank, :] = jnp.concatenate(turned, axis=1).astype(BF16)
-    ids = jnp.broadcast_to(ids_ref[...], (rank, ids_ref.shape[1])).T
-    mask_ref[...] = jnp.zeros_like(mask_ref)
-    for n, name in enumerate(named):
         mine = ids == adapter(here, share, name)
         mask_ref[:, n * rank : (n + 1) * rank] = jnp.where(mine, 1.0, 0.0).astype(BF16)
 
 
-def rotated_ups(ids, bits, matrix, here, share, named, terms, arrays, width):
-    rank, rows = arrays[0].shape[1], ids.shape[1]
-    columns = -(-len(named) * rank // 128) * 128
-    return pl.pallas_call(
-        functools.partial(ups_kernel, named, terms, here, share, rank),
-        in_specs=[VMEM] * (3 + len(arrays)),
+def rotated_ups(ids, bits, matrix, here, share, named, first, second):
+    _, rank, width = first.shape
+    return pl.pallas_call(
+        functools.partial(ups_kernel, here, share, named),
+        in_specs=[VMEM] * 5,
         out_specs=[VMEM, VMEM],
-        out_shape=[jax.ShapeDtypeStruct((len(terms) * rank, width), BF16), jax.ShapeDtypeStruct((rows, columns), BF16)],
+        out_shape=[
+            jax.ShapeDtypeStruct((len(named) * rank, width), BF16),
+            jax.ShapeDtypeStruct((ids.shape[1], len(named) * rank), BF16),
+        ],
         compiler_params=params(32),
         cost_estimate=COST,
         name="rotated_ups",
-    )(ids, bits, matrix, *arrays)
+    )(ids, bits, matrix, first, second)
 
 
 def pick_kernel(named, here, share, ids_ref, tokens_ref, pick_ref, chosen_ref):
@@ -215,41 +231,35 @@
     )(chosen, piece)
 
 
-def most_kernel(mine_ref, theirs_ref, up_ref, mask_ref, near_ref, piece_ref, scale_ref, bits_ref, matrix_ref, *refs):
+def most_kernel(share, spots, mine_ref, theirs_ref, up_ref, mask_ref, scale_ref, bits_ref, matrix_ref, *refs):
     terms, (last_ref, out_ref) = refs[:-2], refs[-2:]
-    rank, width = piece_ref.shape[1], out_ref.shape[1]
     low = (mine_ref[...].astype(F32) + theirs_ref[...].astype(F32)).astype(BF16).T
-    columns = mask_ref.shape[1]
+    rank, columns = low.shape[1], mask_ref.shape[1]
     signs = (1 - 2 * bits_ref[...]).astype(F32)
-    ups = [up_ref[...]]
-    for k in range(near_ref.shape[0]):
-        turned = rotate(near_ref[k].astype(F32), signs, matrix_ref[...])
-        ups.append(jnp.concatenate(turned, axis=1).astype(BF16))
-    missing = columns - sum(up.shape[0] for up in ups)
-    if missing:
-        ups.append(jnp.zeros((missing, up_ref.shape[1]), BF16))
     spread = jnp.concatenate([low] * (columns // rank), axis=1) * mask_ref[...]
-    delta = jnp.dot(spread, jnp.concatenate(ups, axis=0), preferred_element_type=F32)
+    delta = jnp.dot(spread, up_ref[...], preferred_element_type=F32)
     value = functools.reduce(jnp.add, [ref[...].astype(F32) for ref in terms]) * scale_ref[...]
     out_ref[...] = jnp.concatenate(rotate(value, signs, matrix_ref[...]), axis=1) + delta
-    for k in range(piece_ref.shape[0]):
-        turned = rotate(piece_ref[k, :, piece_ref.shape[2] - width :].astype(F32), signs, matrix_ref[...])
-        last_ref[k * rank : (k + 1) * rank] = jnp.concatenate(turned, axis=1).astype(BF16)
-
-
-def most(mine, theirs, up, mask, near, piece, scale, bits, matrix, terms):
-    return pl.pallas_call(
-        most_kernel,
-        in_specs=[VMEM] * (9 + len(terms)),
+    off = jnp.bitwise_xor(lax.axis_index("grp"), lax.axis_size("grp") - 1) * share
+    for k, spot in enumerate(spots):
+        at = pl.multiple_of((spot + off) * rank, rank)
+        last_ref[k * rank : (k + 1) * rank] = up_ref[pl.ds(at, rank)]
+
+
+def most(mine, theirs, up, mask, scale, bits, matrix, terms, here, share, spots):
+    width = up.shape[1]
+    return pl.pallas_call(
+        functools.partial(most_kernel, share, spots),
+        in_specs=[VMEM] * (7 + len(terms)),
         out_specs=[VMEM] * 2,
         out_shape=[
-            jax.ShapeDtypeStruct((piece.shape[0] * piece.shape[1], terms[0].shape[1]), BF16),
+            jax.ShapeDtypeStruct((share * mine.shape[0], width), BF16),
             jax.ShapeDtypeStruct(terms[0].shape, F32),
         ],
         compiler_params=params(32),
         cost_estimate=COST,
         name="most",
-    )(mine, theirs, up, mask, near, piece, scale, bits, matrix, *terms)
+    )(mine, theirs, up, mask, scale, bits, matrix, *terms)
 
 
 def final_kernel(pick_ref, last_ref, most_ref, *refs):
@@ -298,10 +308,9 @@
     bits, scale, ids = sign_bits[None, :], channel_scale[None, :], adapter_ids.T
     down = jnp.swapaxes(adapter_down, 1, 2)
 
-    start = lax.axis_index("grp") * share
-    own = lax.dynamic_slice_in_dim(down, start, share, 0)
+    own = lax.dynamic_slice_in_dim(down, lax.axis_index("grp") * share, share, 0)
     near = swap(own, "adp", 1)
-    mine = [(0, jnp.concatenate([own, lax.dynamic_slice_in_dim(adapter_up, start, share, 0)], axis=2))]
+    mine = [(0, own)]
     bit = planes // 2
     while bit > 1:
         mine += [(plane | bit, swap(piece, "adp", bit)) for plane, piece in mine]
@@ -336,7 +345,7 @@
         return low_rows(ids, tokens, here, share, [((0, features), every)], arrays, low, dtype, cost)
 
     low = more(None, held[: len(mine)] + swapped[:1], F32, lasting(2))
-    low, *came = together(low, *(swap(block, "tp", 1) for block in blocks[:half]))
+    low, ups, *came = together(low, adapter_up, *(swap(block, "tp", 1) for block in blocks[:half]))
 
     def both(low):
         bit = 1
@@ -346,9 +355,16 @@
         return low, swap(low, "tp", bit)
 
     rest = held[len(mine) :]
+    order = [0]
+    bit = planes // 2
+    while bit > 1:
+        (plane, off, piece), other = rest[0], swap(ups, "adp", bit)
+        piece, other = together(piece, other)
+        rest[0], ups = (plane, off, piece), joined(ups, other)
+        order += [plane | bit for plane in order]
+        bit //= 2
     low = more(low, swapped[1:-1] + rest, BF16, lasting(5))
-    low, up = together(low, adapter_up)
-    near_up = swap(up, "adp", 1)
+    more_ups = swap(ups, "adp", 1)
     low, other = both(low)
 
     sums = [[block, pair] for block, pair in zip(blocks[half:], came)]
@@ -358,18 +374,12 @@
         sums = [terms + [pair] for terms, pair in zip(sums[0::2], came)]
         bit *= 2
 
-    far = [one for one in held + swapped[:-1] if one[0] > 1]
-    named = [("plane", 0, k) for k in range(here)]
-    named += [(plane, off, k) for plane, off, _ in far for k in range(share)]
-    ups = [(0, k, 0) for k in range(here)] + [(1 + i, k, features) for i in range(len(far)) for k in range(share)]
-    named += [("plane", 1, k) for k in range(here)]
-    arrays = [adapter_up] + [piece for *_, piece in far]
-    up, mask = rotated_ups(ids, bits, matrix, here, share, named, ups, arrays, width)
-
-    piece, up, mask = together(swapped[-1][2], up, mask)
+    named = [("plane", plane | side, k) for side in (0, 1) for plane in order for k in range(here)]
+    piece = swapped[-1][2]
     kept = compact(chosen, piece)
     kept = [kept] + [swap(kept, "tp", offset) for offset in range(1, parts)]
-    last, rest = most(low, other, up, mask, near_up, piece, scale, bits, matrix, sums[0])
+    up, mask = rotated_ups(ids, bits, matrix, here, share, named, ups, more_ups)
+    last, rest = most(low, other, up, mask, scale, bits, matrix, sums[0], here, share, [named.index(("plane", planes - 1, k)) for k in range(share)])
     return final(kept, pick, last, rest)
 
 

time: 41.7 us -> 44.7 us (1.072)
  starting transfers between devices: 16.5 us -> 18.4 us
  waiting for transfers between devices: 8.29 us -> 10.1 us
  local copies, waits for them, and re-layouts: 5.84 us -> 5.1 us
    ppermute x15 -> x16, starting transfers between devices: 16.5 us -> 18.4 us  [swap(): lax.ppermute(x, axis, [(i, i ^ bit) for i in range(lax.axis_size(axis))])]
    ppermute x15 -> x16, waiting for transfers between devices: 8.29 us -> 10.1 us  [swap(): lax.ppermute(x, axis, [(i, i ^ bit) for i in range(lax.axis_size(axis))])]
    dynamic_slice x2 -> x1, local copies, waits for them, and re-layouts: 1.73 us -> 0.98 us  [local(): lax.dynamic_slice_in_dim(down, lax.axis_index('grp') * share, share, 0)]
    pallas_call x2 -> x3, Pallas kernels: 1.36 us -> 1.45 us  [the longest x1 0.77 us: most(): pl.pallas_call(functools.partial(most_kernel, share, spots), in_specs=[VM...]
  transfers between devices with their start and end apart: 15 -> 16, of which waited for: 7 -> 5; matrix products, arithmetic and copies ran while one was open for 2% -> 0% of each run, Pallas kernels for 23% -> 21%
where the time goes in v21:
time: 44.7 us; the launch traced here: 44.5 us
  starting transfers between devices  18.4 us (41%)
  Pallas kernels  10.7 us (24%)
  waiting for transfers between devices  10.1 us (23%)
  local copies, waits for them, and re-layouts  5.1 us (11%)
    ppermute x16, starting transfers between devices, swap(): lax.ppermute(x, axis, [(i, i ^ bit) for i in range(lax.axis_size(axis))])  18.4 us
    ppermute x16, waiting for transfers between devices, swap(): lax.ppermute(x, axis, [(i, i ^ bit) for i in range(lax.axis_size(axis))])  10.1 us
    unnamed x20, local copies, waits for them, and re-layouts  4.12 us
    pallas_call x2, Pallas kernels, partials(): pl.pallas_call(functools.partial(partial_kernel, offsets, parts), in_spec...  3.66 us
    pallas_call x2, Pallas kernels, low_rows(): pl.pallas_call(functools.partial(low_kernel, groups, here, share, rank, b...  2.42 us
    pallas_call x1, Pallas kernels, picked(): pl.pallas_call(functools.partial(pick_kernel, named, here, share), in_spe...  1.33 us
    pallas_call x1, Pallas kernels, final(): pl.pallas_call(final_kernel, in_specs=[VMEM] * (3 + len(kept)), out_specs...  1.24 us
    dynamic_slice x1, local copies, waits for them, and re-layouts, local(): lax.dynamic_slice_in_dim(down, lax.axis_index('grp') * share, share, 0)  0.98 us
  transfers between devices with their start and end apart: 16, of which 5 were waited for; matrix products, arithmetic and copies ran while one was open for 0% of the time, Pallas kernels for 21%

profile of v21, /device:TPU:0, one launch (start us, length us, event | category | flops | bytes accessed | tf_op | source)
XLA Modules:
  0.0 44.5 jit_solution(16105225012603476489)
XLA Ops:
  0.0 1.0 %dynamic-slice_bitcast_fusion = bf16[1,64,2048]{2,1,0:T(8,128)(2,1)S(1)} fusion(bf16[2,2048,64]{1,2,0:T(8,128)(2,1)} %param.12, s32[]{:T(128)S(6)} %select_n.3), kind=kLoop, calls=%fused_computation | loop fusion | bytes 524292 | tf_op jit(solution)/shard_map/dynamic_slice | solution.py:311
  1.0 4.1 %collective-permute-start.1 = (bf16[1,64,2048]{2,1,0:T(8,128)(2,1)S(1)}, bf16[1,64,2048]{2,1,0:T(8,128)(2,1)S(1)}, u32[]{:S(2)}, u32[]{:S(2)}) collective-permute-start(bf16[1,64,2048]{2,1,0:T(8,128)(2,1)S(1)} %dynamic-slice_bitcast_fusion), channel_id=1, source_target_pairs={{0,8},{4,12},{8,0},{12,4},{1,9},{5,13},{9,1},{13,5},{2,10},{6,14},... | collective-permute-start | bytes 786440 | tf_op jit(solution)/shard_map/ppermute | solution.py:39
  5.1 1.6 %collective-permute-start = (bf16[1,64,2048]{2,1,0:T(8,128)(2,1)S(1)}, bf16[1,64,2048]{2,1,0:T(8,128)(2,1)S(1)}, u32[]{:S(2)}, u32[]{:S(2)}) collective-permute-start(bf16[1,64,2048]{2,1,0:T(8,128)(2,1)S(1)} %dynamic-slice_bitcast_fusion), channel_id=1, source_target_pairs={{0,4},{4,0},{8,12},{12,8},{1,5},{5,1},{9,13},{13,9},{2,6},{6,2},{1... | collective-permute-start | bytes 786440 | tf_op jit(solution)/shard_map/ppermute | solution.py:39
  6.7 1.9 %copy-done = bf16[768,2048]{1,0:T(8,128)(2,1)S(1)} copy-done((bf16[768,2048]{1,0:T(8,128)(2,1)S(1)}, bf16[768,2048]{1,0:T(8,128)(2,1)}, u32[]{:S(2)}) %copy-start) | copy-done | bytes 3145752
  8.6 2.2 %copy-done.2 = bf16[2048,1024]{1,0:T(8,128)(2,1)S(1)} copy-done((bf16[2048,1024]{1,0:T(8,128)(2,1)S(1)}, bf16[2048,1024]{1,0:T(8,128)(2,1)}, u32[]{:S(2)}) %copy-start.2) | copy-done | bytes 4194328
  10.7 2.7 %partials.2 = (bf16[768,256]{1,0:T(8,128)(2,1)S(1)}, bf16[768,256]{1,0:T(8,128)(2,1)S(1)}, bf16[768,256]{1,0:T(8,128)(2,1)S(1)}) custom-call(bf16[768,2048]{1,0:T(8,128)(2,1)S(1)} %copy-done, bf16[2048,1024]{1,0:T(8,128)(2,1)S(1)} %copy-done.2), custom_call_target="tpu_custom_call" | custom-call | flops 4000000000 | bytes 1 | tf_op jit(solution)/shard_map/partials/pallas_call | solution.py:70
  13.4 3.9 %collective-permute-done.refs_0_ = bf16[1,64,2048]{2,1,0:T(8,128)(2,1)S(1)} collective-permute-done((bf16[1,64,2048]{2,1,0:T(8,128)(2,1)S(1)}, bf16[1,64,2048]{2,1,0:T(8,128)(2,1)S(1)}, u32[]{:S(2)}, u32[]{:S(2)}) %collective-permute-start) | collective-permute-done | bytes 262176 | tf_op jit(solution)/shard_map/ppermute | solution.py:39
  17.3 1.6 %collective-permute-start.4 = (bf16[1,64,2048]{2,1,0:T(8,128)(2,1)S(1)}, bf16[1,64,2048]{2,1,0:T(8,128)(2,1)S(1)}, u32[]{:S(2)}, u32[]{:S(2)}) collective-permute-start(bf16[1,64,2048]{2,1,0:T(8,128)(2,1)S(1)} %collective-permute-done.refs_0_), channel_id=1, source_target_pairs={{0,16},{16,0},{1,17},{17,1},{2,18},{18,2},{3,19},{19,3},{4,20},{20... | collective-permute-start | bytes 786440 | tf_op jit(solution)/shard_map/ppermute | solution.py:39
  18.9 0.5 %collective-permute-start.6 = (bf16[768,256]{1,0:T(8,128)(2,1)S(1)}, bf16[768,256]{1,0:T(8,128)(2,1)S(1)}, u32[]{:S(2)}, u32[]{:S(2)}) collective-permute-start(bf16[768,256]{1,0:T(8,128)(2,1)S(1)} %get-tuple-element.36), channel_id=1, source_target_pairs={{0,1},{1,0},{2,3},{3,2},{4,5},{5,4},{6,7},{7,6},{8,9},{9,8},{10,11... | collective-permute-start | bytes 1179656 | tf_op jit(solution)/shard_map/ppermute | solution.py:39
  19.4 1.3 %picked.1 = (bf16[768,256]{1,0:T(8,128)(2,1)S(1)}, bf16[256,2048]{1,0:T(8,128)(2,1)S(1)}) custom-call(s32[1,768]{1,0:T(1,128)S(1)} %bitcast.7, bf16[768,2048]{1,0:T(8,128)(2,1)S(1)} %copy-done.1), custom_call_target="tpu_custom_call" | custom-call | flops 1 | bytes 1 | tf_op jit(solution)/shard_map/picked/pallas_call | solution.py:200
  20.8 1.0 %partials.3.refs_0_ = bf16[768,256]{1,0:T(8,128)(2,1)S(1)} custom-call(bf16[768,2048]{1,0:T(8,128)(2,1)S(1)} %copy-done.1, bf16[2048,1024]{1,0:T(8,128)(2,1)S(1)} %copy-done.3, bf16[768,256]{1,0:T(8,128)(2,1)S(1)} %get-tuple-element.29.refs_0_), custom_call_target="tpu_custom_call" | custom-call | flops 1 | bytes 1 | tf_op jit(solution)/shard_map/partials/pallas_call | solution.py:70
  21.8 1.5 %collective-permute-start.3 = (bf16[1,64,2048]{2,1,0:T(8,128)(2,1)S(1)}, bf16[1,64,2048]{2,1,0:T(8,128)(2,1)S(1)}, u32[]{:S(2)}, u32[]{:S(2)}) collective-permute-start(bf16[1,64,2048]{2,1,0:T(8,128)(2,1)S(1)} %collective-permute-done.1.refs_1_), channel_id=1, source_target_pairs={{0,4},{4,0},{8,12},{12,8},{1,5},{5,1},{9,13},{13,9},{2,6},{6,2},{1... | collective-permute-start | bytes 786440 | tf_op jit(solution)/shard_map/ppermute | solution.py:39
  23.3 0.5 %collective-permute-start.2 = (bf16[1,64,2048]{2,1,0:T(8,128)(2,1)S(1)}, bf16[1,64,2048]{2,1,0:T(8,128)(2,1)S(1)}, u32[]{:S(2)}, u32[]{:S(2)}) collective-permute-start(bf16[1,64,2048]{2,1,0:T(8,128)(2,1)S(1)} %collective-permute-done.1.refs_1_), channel_id=1, source_target_pairs={{0,16},{16,0},{1,17},{17,1},{2,18},{18,2},{3,19},{19,3},{4,20},{20... | collective-permute-start | bytes 786440 | tf_op jit(solution)/shard_map/ppermute | solution.py:39
  23.8 1.3 %low_rows.2.refs_2_ = f32[64,768]{1,0:T(8,128)S(1)} custom-call(s32[1,768]{1,0:T(1,128)S(1)} %bitcast.8, bf16[768,2048]{1,0:T(8,128)(2,1)S(1)} %copy-done.1, bf16[1,64,2048]{2,1,0:T(8,128)(2,1)S(1)} %collective-permute-done.refs_0_, bf16[1,64,2048]{2,1,0:T(8,128)(2,1)S(1)} %collective-permute-done.1.refs_1_, ...), custom_call_target="tpu_custom_call" | custom-call | flops 2000000000 | bytes 1 | tf_op jit(solution)/shard_map/low_rows/pallas_call | solution.py:125
  25.1 2.2 %collective-permute-start.7 = (bf16[2,64,256]{2,1,0:T(8,128)(2,1)S(1)}, bf16[2,64,256]{2,1,0:T(8,128)(2,1)S(1)}, u32[]{:S(2)}, u32[]{:S(2)}) collective-permute-start(bf16[2,64,256]{2,1,0:T(8,128)(2,1)S(1)} %copy-done.6), channel_id=1, source_target_pairs={{0,8},{4,12},{8,0},{12,4},{1,9},{5,13},{9,1},{13,5},{2,10},{6,14},... | collective-permute-start | bytes 196616 | tf_op jit(solution)/shard_map/ppermute | solution.py:39
  27.3 0.1 add.7
  27.4 1.6 %collective-permute-start.11 = (bf16[768,256]{1,0:T(8,128)(2,1)S(1)}, bf16[768,256]{1,0:T(8,128)(2,1)S(1)}, u32[]{:S(2)}, u32[]{:S(2)}) collective-permute-start(bf16[768,256]{1,0:T(8,128)(2,1)S(1)} %add.7), channel_id=1, source_target_pairs={{0,2},{1,3},{2,0},{3,1},{4,6},{5,7},{6,4},{7,5},{8,10},{9,11},{10,... | collective-permute-start | bytes 1179656 | tf_op jit(solution)/shard_map/ppermute | solution.py:39
  28.9 2.6 %collective-permute-done.3.refs_1_ = bf16[1,64,2048]{2,1,0:T(8,128)(2,1)S(1)} collective-permute-done((bf16[1,64,2048]{2,1,0:T(8,128)(2,1)S(1)}, bf16[1,64,2048]{2,1,0:T(8,128)(2,1)S(1)}, u32[]{:S(2)}, u32[]{:S(2)}) %collective-permute-start.3) | collective-permute-done | bytes 262176 | tf_op jit(solution)/shard_map/ppermute | solution.py:39
  31.5 1.2 %low_rows.3.refs_0_ = bf16[64,768]{1,0:T(8,128)(2,1)S(1)} custom-call(s32[1,768]{1,0:T(1,128)S(1)} %bitcast.9, bf16[768,2048]{1,0:T(8,128)(2,1)S(1)} %copy-done.1, bf16[1,64,2048]{2,1,0:T(8,128)(2,1)S(1)} %collective-permute-done.2.refs_0_, bf16[1,64,2048]{2,1,0:T(8,128)(2,1)S(1)} %collective-permute-done.3.refs_1_, f32[64,768]{1,0:T(8,128)S(1)} %low_rows.2.refs_2_), custom_call_target="tpu_custom_call" | custom-call | flops 5000000000 | bytes 1 | tf_op jit(solution)/shard_map/low_rows/pallas_call | solution.py:125
  32.7 0.1 collective-permute-start.8
  32.8 1.4 %collective-permute-start.10 = (bf16[4,64,256]{2,1,0:T(8,128)(2,1)S(1)}, bf16[4,64,256]{2,1,0:T(8,128)(2,1)S(1)}, u32[]{:S(2)}, u32[]{:S(2)}) collective-permute-start(bf16[4,64,256]{2,1,0:T(8,128)(2,1)S(1)} %joined.1.first_ref), channel_id=1, source_target_pairs={{0,4},{4,0},{8,12},{12,8},{1,5},{5,1},{9,13},{13,9},{2,6},{6,2},{1... | collective-permute-start | bytes 393224 | tf_op jit(solution)/shard_map/ppermute | solution.py:39
  34.2 1.5 %collective-permute-start.9 = (bf16[64,768]{1,0:T(8,128)(2,1)S(1)}, bf16[64,768]{1,0:T(8,128)(2,1)S(1)}, u32[]{:S(2)}, u32[]{:S(2)}) collective-permute-start(bf16[64,768]{1,0:T(8,128)(2,1)S(1)} %add.6.mine_ref), channel_id=1, source_target_pairs={{0,2},{1,3},{2,0},{3,1},{4,6},{5,7},{6,4},{7,5},{8,10},{9,11},{10,... | collective-permute-start | bytes 294920 | tf_op jit(solution)/shard_map/ppermute | solution.py:39
  35.8 3.0 %collective-permute-done.12.piece_ref = bf16[1,64,2048]{2,1,0:T(8,128)(2,1)S(1)} collective-permute-done((bf16[1,64,2048]{2,1,0:T(8,128)(2,1)S(1)}, bf16[1,64,2048]{2,1,0:T(8,128)(2,1)S(1)}, u32[]{:S(2)}, u32[]{:S(2)}) %collective-permute-start.12) | collective-permute-done | bytes 262176 | tf_op jit(solution)/shard_map/ppermute | solution.py:39
  38.7 0.4 compact.1.refs_0_
  39.2 0.1 collective-permute-start.15
  39.2 1.3 %collective-permute-start.14 = (bf16[64,256]{1,0:T(8,128)(2,1)S(1)}, bf16[64,256]{1,0:T(8,128)(2,1)S(1)}, u32[]{:S(2)}, u32[]{:S(2)}) collective-permute-start(bf16[64,256]{1,0:T(8,128)(2,1)S(1)} %compact.1.refs_0_), channel_id=1, source_target_pairs={{0,2},{1,3},{2,0},{3,1},{4,6},{5,7},{6,4},{7,5},{8,10},{9,11},{10,... | collective-permute-start | bytes 98312 | tf_op jit(solution)/shard_map/ppermute | solution.py:39
  40.5 0.6 %collective-permute-start.13 = (bf16[64,256]{1,0:T(8,128)(2,1)S(1)}, bf16[64,256]{1,0:T(8,128)(2,1)S(1)}, u32[]{:S(2)}, u32[]{:S(2)}) collective-permute-start(bf16[64,256]{1,0:T(8,128)(2,1)S(1)} %compact.1.refs_0_), channel_id=1, source_target_pairs={{0,1},{1,0},{2,3},{3,2},{4,5},{5,4},{6,7},{7,6},{8,9},{9,8},{10,11... | collective-permute-start | bytes 98312 | tf_op jit(solution)/shard_map/ppermute | solution.py:39
  41.1 0.7 %rotated_ups.1 = (bf16[512,256]{1,0:T(8,128)(2,1)S(1)}, bf16[768,512]{1,0:T(8,128)(2,1)S(1)}) custom-call(s32[1,768]{1,0:T(1,128)S(1)} %bitcast.10, s32[1,128]{1,0:T(1,128)S(1)} %bitcast.11, bf16[128,128]{1,0:T(8,128)(2,1)S(1)} %copy-done.4, bf16[4,64,256]{2,1,0:T(8,128)(2,1)S(1)} %joined.1.first_ref, bf16[4,64,256]{2,1,0:T(8,128)(2,1)S(1)} %collective-permute-done.10.second_ref), custom_call_target="tpu_custom_call" | custom-call | flops 1 | bytes 1 | tf_op jit(solution)/shard_map/rotated_ups/pallas_call | solution.py:166
  41.8 0.8 %most.1 = (bf16[64,256]{1,0:T(8,128)(2,1)S(1)}, f32[768,256]{1,0:T(8,128)S(1)}) custom-call(bf16[64,768]{1,0:T(8,128)(2,1)S(1)} %add.6.mine_ref, bf16[64,768]{1,0:T(8,128)(2,1)S(1)} %collective-permute-done.9.theirs_ref, bf16[512,256]{1,0:T(8,128)(2,1)S(1)} %get-tuple-element.41.up_ref, bf16[768,512]{1,0:T(8,128)(2,1)S(1)} %get-tuple-element.42.mask_ref, ...), custom_call_target="tpu_custom_call" | custom-call | flops 1 | bytes 1 | tf_op jit(solution)/shard_map/most/pallas_call | solution.py:251
  42.6 0.1 collective-permute-done.15.refs_3_
  42.7 0.6 %collective-permute-done.14.refs_2_ = bf16[64,256]{1,0:T(8,128)(2,1)S(1)} collective-permute-done((bf16[64,256]{1,0:T(8,128)(2,1)S(1)}, bf16[64,256]{1,0:T(8,128)(2,1)S(1)}, u32[]{:S(2)}, u32[]{:S(2)}) %collective-permute-start.14) | collective-permute-done | bytes 32800 | tf_op jit(solution)/shard_map/ppermute | solution.py:39
  43.3 1.2 %final.1 = bf16[768,256]{1,0:T(8,128)(2,1)} custom-call(bf16[768,256]{1,0:T(8,128)(2,1)S(1)} %get-tuple-element.32.pick_ref, bf16[64,256]{1,0:T(8,128)(2,1)S(1)} %get-tuple-element.46.last_ref, f32[768,256]{1,0:T(8,128)S(1)} %get-tuple-element.47.most_ref, bf16[64,256]{1,0:T(8,128)(2,1)S(1)} %compact.1.refs_0_, ...), custom_call_target="tpu_custom_call" | custom-call | flops 1 | bytes 1 | tf_op jit(solution)/shard_map/final/pallas_call | solution.py:289
  (33 shorter events, 0.1 us)
Async XLA Ops:
  0.0 19.4 %copy-start.7 = (s32[768,1]{0,1:T(1,128)S(1)}, s32[768,1]{0,1:T(1,128)}, u32[]{:S(2)}) copy-start(s32[768,1]{0,1:T(1,128)} %param.9) | copy-start | bytes 9220
  1.0 20.8 %collective-permute-start.1 = (bf16[1,64,2048]{2,1,0:T(8,128)(2,1)S(1)}, bf16[1,64,2048]{2,1,0:T(8,128)(2,1)S(1)}, u32[]{:S(2)}, u32[]{:S(2)}) collective-permute-start(bf16[1,64,2048]{2,1,0:T(8,128)(2,1)S(1)} %dynamic-slice_bitcast_fusion), channel_id=1, source_target_pairs={{0,8},{4,12},{8,0},{12,4},{1,9},{5,13},{9,1},{13,5},{2,10},{6,14},... | collective-permute-start | bytes 786440 | tf_op jit(solution)/shard_map/ppermute | solution.py:39
  5.1 12.2 %collective-permute-start = (bf16[1,64,2048]{2,1,0:T(8,128)(2,1)S(1)}, bf16[1,64,2048]{2,1,0:T(8,128)(2,1)S(1)}, u32[]{:S(2)}, u32[]{:S(2)}) collective-permute-start(bf16[1,64,2048]{2,1,0:T(8,128)(2,1)S(1)} %dynamic-slice_bitcast_fusion), channel_id=1, source_target_pairs={{0,4},{4,0},{8,12},{12,8},{1,5},{5,1},{9,13},{13,9},{2,6},{6,2},{1... | collective-permute-start | bytes 786440 | tf_op jit(solution)/shard_map/ppermute | solution.py:39
  6.7 1.9 %copy-start = (bf16[768,2048]{1,0:T(8,128)(2,1)S(1)}, bf16[768,2048]{1,0:T(8,128)(2,1)}, u32[]{:S(2)}) copy-start(bf16[768,2048]{1,0:T(8,128)(2,1)} %tokens_ref.9) | copy-start | bytes 9437188
  8.6 2.2 %copy-start.2 = (bf16[2048,1024]{1,0:T(8,128)(2,1)S(1)}, bf16[2048,1024]{1,0:T(8,128)(2,1)}, u32[]{:S(2)}) copy-start(bf16[2048,1024]{1,0:T(8,128)(2,1)} %weight_ref.3) | copy-start | bytes 12582916
  10.7 8.7 %copy-start.1 = (bf16[768,2048]{1,0:T(8,128)(2,1)S(1)}, bf16[768,2048]{1,0:T(8,128)(2,1)}, u32[]{:S(2)}) copy-start(bf16[768,2048]{1,0:T(8,128)(2,1)} %tokens_ref.9) | copy-start | bytes 9437188
  10.7 10.0 %copy-start.3 = (bf16[2048,1024]{1,0:T(8,128)(2,1)S(1)}, bf16[2048,1024]{1,0:T(8,128)(2,1)}, u32[]{:S(2)}) copy-start(bf16[2048,1024]{1,0:T(8,128)(2,1)} %weight_ref.3) | copy-start | bytes 12582916
  17.3 6.5 %collective-permute-start.4 = (bf16[1,64,2048]{2,1,0:T(8,128)(2,1)S(1)}, bf16[1,64,2048]{2,1,0:T(8,128)(2,1)S(1)}, u32[]{:S(2)}, u32[]{:S(2)}) collective-permute-start(bf16[1,64,2048]{2,1,0:T(8,128)(2,1)S(1)} %collective-permute-done.refs_0_), channel_id=1, source_target_pairs={{0,16},{16,0},{1,17},{17,1},{2,18},{18,2},{3,19},{19,3},{4,20},{20... | collective-permute-start | bytes 786440 | tf_op jit(solution)/shard_map/ppermute | solution.py:39
  18.9 6.2 %collective-permute-start.5 = (bf16[768,256]{1,0:T(8,128)(2,1)S(1)}, bf16[768,256]{1,0:T(8,128)(2,1)S(1)}, u32[]{:S(2)}, u32[]{:S(2)}) collective-permute-start(bf16[768,256]{1,0:T(8,128)(2,1)S(1)} %get-tuple-element.35), channel_id=1, source_target_pairs={{0,1},{1,0},{2,3},{3,2},{4,5},{5,4},{6,7},{7,6},{8,9},{9,8},{10,11... | collective-permute-start | bytes 1179656 | tf_op jit(solution)/shard_map/ppermute | solution.py:39
  18.9 6.2 %collective-permute-start.6 = (bf16[768,256]{1,0:T(8,128)(2,1)S(1)}, bf16[768,256]{1,0:T(8,128)(2,1)S(1)}, u32[]{:S(2)}, u32[]{:S(2)}) collective-permute-start(bf16[768,256]{1,0:T(8,128)(2,1)S(1)} %get-tuple-element.36), channel_id=1, source_target_pairs={{0,1},{1,0},{2,3},{3,2},{4,5},{5,4},{6,7},{7,6},{8,9},{9,8},{10,11... | collective-permute-start | bytes 1179656 | tf_op jit(solution)/shard_map/ppermute | solution.py:39
  20.7 3.1 %copy-start.5 = (bf16[2,2048,64]{1,2,0:T(8,128)(2,1)S(1)}, bf16[2,2048,64]{1,2,0:T(8,128)(2,1)}, u32[]{:S(2)}) copy-start(bf16[2,2048,64]{1,2,0:T(8,128)(2,1)} %param.12) | copy-start | bytes 1572868
  21.8 3.3 %copy-start.6 = (bf16[2,64,256]{2,1,0:T(8,128)(2,1)S(1)}, bf16[2,64,256]{2,1,0:T(8,128)(2,1)}, u32[]{:S(2)}) copy-start(bf16[2,64,256]{2,1,0:T(8,128)(2,1)} %first_ref) | copy-start | bytes 196612
  21.8 9.7 %collective-permute-start.3 = (bf16[1,64,2048]{2,1,0:T(8,128)(2,1)S(1)}, bf16[1,64,2048]{2,1,0:T(8,128)(2,1)S(1)}, u32[]{:S(2)}, u32[]{:S(2)}) collective-permute-start(bf16[1,64,2048]{2,1,0:T(8,128)(2,1)S(1)} %collective-permute-done.1.refs_1_), channel_id=1, source_target_pairs={{0,4},{4,0},{8,12},{12,8},{1,5},{5,1},{9,13},{13,9},{2,6},{6,2},{1... | collective-permute-start | bytes 786440 | tf_op jit(solution)/shard_map/ppermute | solution.py:39
  23.3 8.2 %collective-permute-start.2 = (bf16[1,64,2048]{2,1,0:T(8,128)(2,1)S(1)}, bf16[1,64,2048]{2,1,0:T(8,128)(2,1)S(1)}, u32[]{:S(2)}, u32[]{:S(2)}) collective-permute-start(bf16[1,64,2048]{2,1,0:T(8,128)(2,1)S(1)} %collective-permute-done.1.refs_1_), channel_id=1, source_target_pairs={{0,16},{16,0},{1,17},{17,1},{2,18},{18,2},{3,19},{19,3},{4,20},{20... | collective-permute-start | bytes 786440 | tf_op jit(solution)/shard_map/ppermute | solution.py:39
  25.1 6.4 %collective-permute-start.7 = (bf16[2,64,256]{2,1,0:T(8,128)(2,1)S(1)}, bf16[2,64,256]{2,1,0:T(8,128)(2,1)S(1)}, u32[]{:S(2)}, u32[]{:S(2)}) collective-permute-start(bf16[2,64,256]{2,1,0:T(8,128)(2,1)S(1)} %copy-done.6), channel_id=1, source_target_pairs={{0,8},{4,12},{8,0},{12,4},{1,9},{5,13},{9,1},{13,5},{2,10},{6,14},... | collective-permute-start | bytes 196616 | tf_op jit(solution)/shard_map/ppermute | solution.py:39
  27.4 14.4 %collective-permute-start.11 = (bf16[768,256]{1,0:T(8,128)(2,1)S(1)}, bf16[768,256]{1,0:T(8,128)(2,1)S(1)}, u32[]{:S(2)}, u32[]{:S(2)}) collective-permute-start(bf16[768,256]{1,0:T(8,128)(2,1)S(1)} %add.7), channel_id=1, source_target_pairs={{0,2},{1,3},{2,0},{3,1},{4,6},{5,7},{6,4},{7,5},{8,10},{9,11},{10,... | collective-permute-start | bytes 1179656 | tf_op jit(solution)/shard_map/ppermute | solution.py:39
  31.5 7.2 %collective-permute-start.12 = (bf16[1,64,2048]{2,1,0:T(8,128)(2,1)S(1)}, bf16[1,64,2048]{2,1,0:T(8,128)(2,1)S(1)}, u32[]{:S(2)}, u32[]{:S(2)}) collective-permute-start(bf16[1,64,2048]{2,1,0:T(8,128)(2,1)S(1)} %collective-permute-done.3.refs_1_), channel_id=1, source_target_pairs={{0,16},{16,0},{1,17},{17,1},{2,18},{18,2},{3,19},{19,3},{4,20},{20... | collective-permute-start | bytes 786440 | tf_op jit(solution)/shard_map/ppermute | solution.py:39
  32.7 8.4 %copy-start.4 = (bf16[128,128]{1,0:T(8,128)(2,1)S(1)}, bf16[128,128]{1,0:T(8,128)(2,1)}, u32[]{:S(2)}) copy-start(bf16[128,128]{1,0:T(8,128)(2,1)} %constant.12.clone.matrix_ref) | copy-start | bytes 98308
  32.7 8.4 %copy-start.8 = (s32[128]{0:T(128)S(1)}, s32[128]{0:T(128)}, u32[]{:S(2)}) copy-start(s32[128]{0:T(128)} %param.14) | copy-start | bytes 1540
  32.7 9.1 %copy-start.9 = (f32[256]{0:T(256)S(1)}, f32[256]{0:T(256)}, u32[]{:S(2)}) copy-start(f32[256]{0:T(256)} %param.11) | copy-start | bytes 3076
  32.7 1.5 %collective-permute-start.8 = (bf16[64,768]{1,0:T(8,128)(2,1)S(1)}, bf16[64,768]{1,0:T(8,128)(2,1)S(1)}, u32[]{:S(2)}, u32[]{:S(2)}) collective-permute-start(bf16[64,768]{1,0:T(8,128)(2,1)S(1)} %low_rows.3.refs_0_), channel_id=1, source_target_pairs={{0,1},{1,0},{2,3},{3,2},{4,5},{5,4},{6,7},{7,6},{8,9},{9,8},{10,11... | collective-permute-start | bytes 294920 | tf_op jit(solution)/shard_map/ppermute | solution.py:39
  32.8 7.7 %collective-permute-start.10 = (bf16[4,64,256]{2,1,0:T(8,128)(2,1)S(1)}, bf16[4,64,256]{2,1,0:T(8,128)(2,1)S(1)}, u32[]{:S(2)}, u32[]{:S(2)}) collective-permute-start(bf16[4,64,256]{2,1,0:T(8,128)(2,1)S(1)} %joined.1.first_ref), channel_id=1, source_target_pairs={{0,4},{4,0},{8,12},{12,8},{1,5},{5,1},{9,13},{13,9},{2,6},{6,2},{1... | collective-permute-start | bytes 393224 | tf_op jit(solution)/shard_map/ppermute | solution.py:39
  34.2 7.6 %collective-permute-start.9 = (bf16[64,768]{1,0:T(8,128)(2,1)S(1)}, bf16[64,768]{1,0:T(8,128)(2,1)S(1)}, u32[]{:S(2)}, u32[]{:S(2)}) collective-permute-start(bf16[64,768]{1,0:T(8,128)(2,1)S(1)} %add.6.mine_ref), channel_id=1, source_target_pairs={{0,2},{1,3},{2,0},{3,1},{4,6},{5,7},{6,4},{7,5},{8,10},{9,11},{10,... | collective-permute-start | bytes 294920 | tf_op jit(solution)/shard_map/ppermute | solution.py:39
  39.2 3.5 %collective-permute-start.15 = (bf16[64,256]{1,0:T(8,128)(2,1)S(1)}, bf16[64,256]{1,0:T(8,128)(2,1)S(1)}, u32[]{:S(2)}, u32[]{:S(2)}) collective-permute-start(bf16[64,256]{1,0:T(8,128)(2,1)S(1)} %compact.1.refs_0_), channel_id=1, source_target_pairs={{0,3},{1,2},{2,1},{3,0},{4,7},{5,6},{6,5},{7,4},{8,11},{9,10},{10,... | collective-permute-start | bytes 98312 | tf_op jit(solution)/shard_map/ppermute | solution.py:39
  39.2 4.0 %collective-permute-start.14 = (bf16[64,256]{1,0:T(8,128)(2,1)S(1)}, bf16[64,256]{1,0:T(8,128)(2,1)S(1)}, u32[]{:S(2)}, u32[]{:S(2)}) collective-permute-start(bf16[64,256]{1,0:T(8,128)(2,1)S(1)} %compact.1.refs_0_), channel_id=1, source_target_pairs={{0,2},{1,3},{2,0},{3,1},{4,6},{5,7},{6,4},{7,5},{8,10},{9,11},{10,... | collective-permute-start | bytes 98312 | tf_op jit(solution)/shard_map/ppermute | solution.py:39
  40.5 2.8 %collective-permute-start.13 = (bf16[64,256]{1,0:T(8,128)(2,1)S(1)}, bf16[64,256]{1,0:T(8,128)(2,1)S(1)}, u32[]{:S(2)}, u32[]{:S(2)}) collective-permute-start(bf16[64,256]{1,0:T(8,128)(2,1)S(1)} %compact.1.refs_0_), channel_id=1, source_target_pairs={{0,1},{1,0},{2,3},{3,2},{4,5},{5,4},{6,7},{7,6},{8,9},{9,8},{10,11... | collective-permute-start | bytes 98312 | tf_op jit(solution)/shard_map/ppermute | solution.py:39

commit v22 on v21

--- a/solution.py
+++ b/solution.py
@@ -131,6 +131,22 @@
         cost_estimate=cost,
         name="low_rows",
     )(ids, tokens, *arrays, *more)
+
+
+def copy_kernel(in_ref, out_ref):
+    out_ref[...] = in_ref[...]
+
+
+def copied(value):
+    return pl.pallas_call(
+        copy_kernel,
+        in_specs=[VMEM],
+        out_specs=VMEM,
+        out_shape=jax.ShapeDtypeStruct(value.shape, value.dtype),
+        compiler_params=params(16),
+        cost_estimate=COST,
+        name="copied",
+    )(value)
 
 
 def join_kernel(first_ref, second_ref, out_ref):
@@ -310,7 +326,7 @@
 
     own = lax.dynamic_slice_in_dim(down, lax.axis_index("grp") * share, share, 0)
     near = swap(own, "adp", 1)
-    mine = [(0, own)]
+    mine = [(0, copied(own))]
     bit = planes // 2
     while bit > 1:
         mine += [(plane | bit, swap(piece, "adp", bit)) for plane, piece in mine]

time: 44.7 us -> 42.7 us (0.955)
  starting transfers between devices: 18.4 us -> 14.9 us
  waiting for transfers between devices: 10.1 us -> 11.7 us
    ppermute x16, starting transfers between devices: 18.4 us -> 14.9 us  [swap(): lax.ppermute(x, axis, [(i, i ^ bit) for i in range(lax.axis_size(axis))])]
    ppermute x16, waiting for transfers between devices: 10.1 us -> 11.7 us  [swap(): lax.ppermute(x, axis, [(i, i ^ bit) for i in range(lax.axis_size(axis))])]
  transfers between devices with their start and end apart: 16 -> 16, of which waited for: 5 -> 8; matrix products, arithmetic and copies ran while one was open for 0% -> 0% of each run, Pallas kernels for 21% -> 22%
where the time goes in v22:
time: 42.7 us; the launch traced here: 42.5 us
  starting transfers between devices  14.9 us (35%)
  waiting for transfers between devices  11.7 us (27%)
  Pallas kernels  10.7 us (25%)
  local copies, waits for them, and re-layouts  5.09 us (12%)
    ppermute x16, starting transfers between devices, swap(): lax.ppermute(x, axis, [(i, i ^ bit) for i in range(lax.axis_size(axis))])  14.9 us
    ppermute x16, waiting for transfers between devices, swap(): lax.ppermute(x, axis, [(i, i ^ bit) for i in range(lax.axis_size(axis))])  11.7 us
    unnamed x20, local copies, waits for them, and re-layouts  4.12 us
    pallas_call x2, Pallas kernels, partials(): pl.pallas_call(functools.partial(partial_kernel, offsets, parts), in_spec...  3.66 us
    pallas_call x2, Pallas kernels, low_rows(): pl.pallas_call(functools.partial(low_kernel, groups, here, share, rank, b...  2.43 us
    pallas_call x1, Pallas kernels, picked(): pl.pallas_call(functools.partial(pick_kernel, named, here, share), in_spe...  1.33 us
    pallas_call x1, Pallas kernels, final(): pl.pallas_call(final_kernel, in_specs=[VMEM] * (3 + len(kept)), out_specs...  1.22 us
    dynamic_slice x1, local copies, waits for them, and re-layouts, local(): lax.dynamic_slice_in_dim(down, lax.axis_index('grp') * share, share, 0)  0.97 us
  transfers between devices with their start and end apart: 16, of which 8 were waited for; matrix products, arithmetic and copies ran while one was open for 0% of the time, Pallas kernels for 22%

profile of v22, /device:TPU:0, one launch (start us, length us, event | category | flops | bytes accessed | tf_op | source)
XLA Modules:
  0.0 42.5 jit_solution(13441897603005023789)
XLA Ops:
  0.0 1.0 %dynamic-slice_bitcast_fusion.in_ref = bf16[1,64,2048]{2,1,0:T(8,128)(2,1)S(1)} fusion(bf16[2,2048,64]{1,2,0:T(8,128)(2,1)} %param.12, s32[]{:T(128)S(6)} %select_n.3), kind=kLoop, calls=%fused_computation | loop fusion | bytes 524292 | tf_op jit(solution)/shard_map/dynamic_slice | solution.py:327
  1.0 3.1 %collective-permute-start = (bf16[1,64,2048]{2,1,0:T(8,128)(2,1)S(1)}, bf16[1,64,2048]{2,1,0:T(8,128)(2,1)S(1)}, u32[]{:S(2)}, u32[]{:S(2)}) collective-permute-start(bf16[1,64,2048]{2,1,0:T(8,128)(2,1)S(1)} %dynamic-slice_bitcast_fusion.in_ref), channel_id=1, source_target_pairs={{0,4},{4,0},{8,12},{12,8},{1,5},{5,1},{9,13},{13,9},{2,6},{6,2},{1... | collective-permute-start | bytes 786440 | tf_op jit(solution)/shard_map/ppermute | solution.py:39
  4.1 2.7 %collective-permute-start.1 = (bf16[1,64,2048]{2,1,0:T(8,128)(2,1)S(1)}, bf16[1,64,2048]{2,1,0:T(8,128)(2,1)S(1)}, u32[]{:S(2)}, u32[]{:S(2)}) collective-permute-start(bf16[1,64,2048]{2,1,0:T(8,128)(2,1)S(1)} %copied.1), channel_id=1, source_target_pairs={{0,8},{4,12},{8,0},{12,4},{1,9},{5,13},{9,1},{13,5},{2,10},{6,14},... | collective-permute-start | bytes 786440 | tf_op jit(solution)/shard_map/ppermute | solution.py:39
  6.7 1.9 %copy-done = bf16[768,2048]{1,0:T(8,128)(2,1)S(1)} copy-done((bf16[768,2048]{1,0:T(8,128)(2,1)S(1)}, bf16[768,2048]{1,0:T(8,128)(2,1)}, u32[]{:S(2)}) %copy-start) | copy-done | bytes 3145752
  8.6 2.2 %copy-done.2 = bf16[2048,1024]{1,0:T(8,128)(2,1)S(1)} copy-done((bf16[2048,1024]{1,0:T(8,128)(2,1)S(1)}, bf16[2048,1024]{1,0:T(8,128)(2,1)}, u32[]{:S(2)}) %copy-start.2) | copy-done | bytes 4194328
  10.8 2.7 %partials.2 = (bf16[768,256]{1,0:T(8,128)(2,1)S(1)}, bf16[768,256]{1,0:T(8,128)(2,1)S(1)}, bf16[768,256]{1,0:T(8,128)(2,1)S(1)}) custom-call(bf16[768,2048]{1,0:T(8,128)(2,1)S(1)} %copy-done, bf16[2048,1024]{1,0:T(8,128)(2,1)S(1)} %copy-done.2), custom_call_target="tpu_custom_call" | custom-call | flops 4000000000 | bytes 1 | tf_op jit(solution)/shard_map/partials/pallas_call | solution.py:70
  13.5 2.3 %collective-permute-done.refs_0_ = bf16[1,64,2048]{2,1,0:T(8,128)(2,1)S(1)} collective-permute-done((bf16[1,64,2048]{2,1,0:T(8,128)(2,1)S(1)}, bf16[1,64,2048]{2,1,0:T(8,128)(2,1)S(1)}, u32[]{:S(2)}, u32[]{:S(2)}) %collective-permute-start) | collective-permute-done | bytes 262176 | tf_op jit(solution)/shard_map/ppermute | solution.py:39
  15.8 1.7 %collective-permute-start.4 = (bf16[1,64,2048]{2,1,0:T(8,128)(2,1)S(1)}, bf16[1,64,2048]{2,1,0:T(8,128)(2,1)S(1)}, u32[]{:S(2)}, u32[]{:S(2)}) collective-permute-start(bf16[1,64,2048]{2,1,0:T(8,128)(2,1)S(1)} %collective-permute-done.refs_0_), channel_id=1, source_target_pairs={{0,16},{16,0},{1,17},{17,1},{2,18},{18,2},{3,19},{19,3},{4,20},{20... | collective-permute-start | bytes 786440 | tf_op jit(solution)/shard_map/ppermute | solution.py:39
  17.5 0.5 %collective-permute-start.6 = (bf16[768,256]{1,0:T(8,128)(2,1)S(1)}, bf16[768,256]{1,0:T(8,128)(2,1)S(1)}, u32[]{:S(2)}, u32[]{:S(2)}) collective-permute-start(bf16[768,256]{1,0:T(8,128)(2,1)S(1)} %get-tuple-element.36), channel_id=1, source_target_pairs={{0,1},{1,0},{2,3},{3,2},{4,5},{5,4},{6,7},{7,6},{8,9},{9,8},{10,11... | collective-permute-start | bytes 1179656 | tf_op jit(solution)/shard_map/ppermute | solution.py:39
  18.0 1.3 %picked.1 = (bf16[768,256]{1,0:T(8,128)(2,1)S(1)}, bf16[256,2048]{1,0:T(8,128)(2,1)S(1)}) custom-call(s32[1,768]{1,0:T(1,128)S(1)} %bitcast.7, bf16[768,2048]{1,0:T(8,128)(2,1)S(1)} %copy-done.1), custom_call_target="tpu_custom_call" | custom-call | flops 1 | bytes 1 | tf_op jit(solution)/shard_map/picked/pallas_call | solution.py:216
  19.3 1.0 %partials.3.refs_0_ = bf16[768,256]{1,0:T(8,128)(2,1)S(1)} custom-call(bf16[768,2048]{1,0:T(8,128)(2,1)S(1)} %copy-done.1, bf16[2048,1024]{1,0:T(8,128)(2,1)S(1)} %copy-done.3, bf16[768,256]{1,0:T(8,128)(2,1)S(1)} %get-tuple-element.29.refs_0_), custom_call_target="tpu_custom_call" | custom-call | flops 1 | bytes 1 | tf_op jit(solution)/shard_map/partials/pallas_call | solution.py:70
  20.5 0.4 collective-permute-start.2
  20.9 2.5 %collective-permute-done.4.refs_2_ = bf16[1,64,2048]{2,1,0:T(8,128)(2,1)S(1)} collective-permute-done((bf16[1,64,2048]{2,1,0:T(8,128)(2,1)S(1)}, bf16[1,64,2048]{2,1,0:T(8,128)(2,1)S(1)}, u32[]{:S(2)}, u32[]{:S(2)}) %collective-permute-start.4) | collective-permute-done | bytes 262176 | tf_op jit(solution)/shard_map/ppermute | solution.py:39
  23.3 1.3 %low_rows.2.refs_2_ = f32[64,768]{1,0:T(8,128)S(1)} custom-call(s32[1,768]{1,0:T(1,128)S(1)} %bitcast.8, bf16[768,2048]{1,0:T(8,128)(2,1)S(1)} %copy-done.1, bf16[1,64,2048]{2,1,0:T(8,128)(2,1)S(1)} %collective-permute-done.refs_0_, bf16[1,64,2048]{2,1,0:T(8,128)(2,1)S(1)} %collective-permute-done.1.refs_1_, ...), custom_call_target="tpu_custom_call" | custom-call | flops 2000000000 | bytes 1 | tf_op jit(solution)/shard_map/low_rows/pallas_call | solution.py:125
  24.7 0.7 %collective-permute-start.7 = (bf16[2,64,256]{2,1,0:T(8,128)(2,1)S(1)}, bf16[2,64,256]{2,1,0:T(8,128)(2,1)S(1)}, u32[]{:S(2)}, u32[]{:S(2)}) collective-permute-start(bf16[2,64,256]{2,1,0:T(8,128)(2,1)S(1)} %copy-done.6), channel_id=1, source_target_pairs={{0,8},{4,12},{8,0},{12,4},{1,9},{5,13},{9,1},{13,5},{2,10},{6,14},... | collective-permute-start | bytes 196616 | tf_op jit(solution)/shard_map/ppermute | solution.py:39
  25.5 1.6 %collective-permute-start.11 = (bf16[768,256]{1,0:T(8,128)(2,1)S(1)}, bf16[768,256]{1,0:T(8,128)(2,1)S(1)}, u32[]{:S(2)}, u32[]{:S(2)}) collective-permute-start(bf16[768,256]{1,0:T(8,128)(2,1)S(1)} %add.7), channel_id=1, source_target_pairs={{0,2},{1,3},{2,0},{3,1},{4,6},{5,7},{6,4},{7,5},{8,10},{9,11},{10,... | collective-permute-start | bytes 1179656 | tf_op jit(solution)/shard_map/ppermute | solution.py:39
  27.1 2.5 %collective-permute-done.3.refs_1_ = bf16[1,64,2048]{2,1,0:T(8,128)(2,1)S(1)} collective-permute-done((bf16[1,64,2048]{2,1,0:T(8,128)(2,1)S(1)}, bf16[1,64,2048]{2,1,0:T(8,128)(2,1)S(1)}, u32[]{:S(2)}, u32[]{:S(2)}) %collective-permute-start.3) | collective-permute-done | bytes 262176 | tf_op jit(solution)/shard_map/ppermute | solution.py:39
  29.6 0.1 collective-permute-start.12
  29.7 1.4 %collective-permute-done.7.second_ref = bf16[2,64,256]{2,1,0:T(8,128)(2,1)S(1)} collective-permute-done((bf16[2,64,256]{2,1,0:T(8,128)(2,1)S(1)}, bf16[2,64,256]{2,1,0:T(8,128)(2,1)S(1)}, u32[]{:S(2)}, u32[]{:S(2)}) %collective-permute-start.7) | collective-permute-done | bytes 65568 | tf_op jit(solution)/shard_map/ppermute | solution.py:39
  31.1 1.2 %low_rows.3.refs_0_ = bf16[64,768]{1,0:T(8,128)(2,1)S(1)} custom-call(s32[1,768]{1,0:T(1,128)S(1)} %bitcast.9, bf16[768,2048]{1,0:T(8,128)(2,1)S(1)} %copy-done.1, bf16[1,64,2048]{2,1,0:T(8,128)(2,1)S(1)} %collective-permute-done.2.refs_0_, bf16[1,64,2048]{2,1,0:T(8,128)(2,1)S(1)} %collective-permute-done.3.refs_1_, f32[64,768]{1,0:T(8,128)S(1)} %low_rows.2.refs_2_), custom_call_target="tpu_custom_call" | custom-call | flops 5000000000 | bytes 1 | tf_op jit(solution)/shard_map/low_rows/pallas_call | solution.py:125
  32.4 0.6 %collective-permute-start.10 = (bf16[4,64,256]{2,1,0:T(8,128)(2,1)S(1)}, bf16[4,64,256]{2,1,0:T(8,128)(2,1)S(1)}, u32[]{:S(2)}, u32[]{:S(2)}) collective-permute-start(bf16[4,64,256]{2,1,0:T(8,128)(2,1)S(1)} %joined.1.first_ref), channel_id=1, source_target_pairs={{0,4},{4,0},{8,12},{12,8},{1,5},{5,1},{9,13},{13,9},{2,6},{6,2},{1... | collective-permute-start | bytes 393224 | tf_op jit(solution)/shard_map/ppermute | solution.py:39
  33.0 0.6 %collective-permute-done.8.refs_1_ = bf16[64,768]{1,0:T(8,128)(2,1)S(1)} collective-permute-done((bf16[64,768]{1,0:T(8,128)(2,1)S(1)}, bf16[64,768]{1,0:T(8,128)(2,1)S(1)}, u32[]{:S(2)}, u32[]{:S(2)}) %collective-permute-start.8) | collective-permute-done | bytes 98336 | tf_op jit(solution)/shard_map/ppermute | solution.py:39
  33.7 1.4 %collective-permute-start.9 = (bf16[64,768]{1,0:T(8,128)(2,1)S(1)}, bf16[64,768]{1,0:T(8,128)(2,1)S(1)}, u32[]{:S(2)}, u32[]{:S(2)}) collective-permute-start(bf16[64,768]{1,0:T(8,128)(2,1)S(1)} %add.6.mine_ref), channel_id=1, source_target_pairs={{0,2},{1,3},{2,0},{3,1},{4,6},{5,7},{6,4},{7,5},{8,10},{9,11},{10,... | collective-permute-start | bytes 294920 | tf_op jit(solution)/shard_map/ppermute | solution.py:39
  35.1 1.7 %collective-permute-done.12.piece_ref = bf16[1,64,2048]{2,1,0:T(8,128)(2,1)S(1)} collective-permute-done((bf16[1,64,2048]{2,1,0:T(8,128)(2,1)S(1)}, bf16[1,64,2048]{2,1,0:T(8,128)(2,1)S(1)}, u32[]{:S(2)}, u32[]{:S(2)}) %collective-permute-start.12) | collective-permute-done | bytes 262176 | tf_op jit(solution)/shard_map/ppermute | solution.py:39
  36.8 0.4 %compact.1.refs_0_ = bf16[64,256]{1,0:T(8,128)(2,1)S(1)} custom-call(bf16[256,2048]{1,0:T(8,128)(2,1)S(1)} %get-tuple-element.48.chosen_ref, bf16[1,64,2048]{2,1,0:T(8,128)(2,1)S(1)} %collective-permute-done.12.piece_ref), custom_call_target="tpu_custom_call" | custom-call | flops 2000000000 | bytes 1 | tf_op jit(solution)/shard_map/compact/pallas_call | solution.py:239
  37.3 1.5 %collective-permute-start.14 = (bf16[64,256]{1,0:T(8,128)(2,1)S(1)}, bf16[64,256]{1,0:T(8,128)(2,1)S(1)}, u32[]{:S(2)}, u32[]{:S(2)}) collective-permute-start(bf16[64,256]{1,0:T(8,128)(2,1)S(1)} %compact.1.refs_0_), channel_id=1, source_target_pairs={{0,2},{1,3},{2,0},{3,1},{4,6},{5,7},{6,4},{7,5},{8,10},{9,11},{10,... | collective-permute-start | bytes 98312 | tf_op jit(solution)/shard_map/ppermute | solution.py:39
  38.8 0.4 collective-permute-start.13
  39.2 0.7 %rotated_ups.1 = (bf16[512,256]{1,0:T(8,128)(2,1)S(1)}, bf16[768,512]{1,0:T(8,128)(2,1)S(1)}) custom-call(s32[1,768]{1,0:T(1,128)S(1)} %bitcast.10, s32[1,128]{1,0:T(1,128)S(1)} %bitcast.11, bf16[128,128]{1,0:T(8,128)(2,1)S(1)} %copy-done.4, bf16[4,64,256]{2,1,0:T(8,128)(2,1)S(1)} %joined.1.first_ref, bf16[4,64,256]{2,1,0:T(8,128)(2,1)S(1)} %collective-permute-done.10.second_ref), custom_call_target="tpu_custom_call" | custom-call | flops 1 | bytes 1 | tf_op jit(solution)/shard_map/rotated_ups/pallas_call | solution.py:182
  39.9 0.8 %most.1 = (bf16[64,256]{1,0:T(8,128)(2,1)S(1)}, f32[768,256]{1,0:T(8,128)S(1)}) custom-call(bf16[64,768]{1,0:T(8,128)(2,1)S(1)} %add.6.mine_ref, bf16[64,768]{1,0:T(8,128)(2,1)S(1)} %collective-permute-done.9.theirs_ref, bf16[512,256]{1,0:T(8,128)(2,1)S(1)} %get-tuple-element.41.up_ref, bf16[768,512]{1,0:T(8,128)(2,1)S(1)} %get-tuple-element.42.mask_ref, ...), custom_call_target="tpu_custom_call" | custom-call | flops 1 | bytes 1 | tf_op jit(solution)/shard_map/most/pallas_call | solution.py:267
  40.6 0.3 collective-permute-done.15.refs_3_
  41.0 0.3 collective-permute-done.14.refs_2_
  41.3 1.2 %final.1 = bf16[768,256]{1,0:T(8,128)(2,1)} custom-call(bf16[768,256]{1,0:T(8,128)(2,1)S(1)} %get-tuple-element.32.pick_ref, bf16[64,256]{1,0:T(8,128)(2,1)S(1)} %get-tuple-element.46.last_ref, f32[768,256]{1,0:T(8,128)S(1)} %get-tuple-element.47.most_ref, bf16[64,256]{1,0:T(8,128)(2,1)S(1)} %compact.1.refs_0_, ...), custom_call_target="tpu_custom_call" | custom-call | flops 1 | bytes 1 | tf_op jit(solution)/shard_map/final/pallas_call | solution.py:305
  (34 shorter events, 0.4 us)
Async XLA Ops:
  1.0 14.8 %collective-permute-start = (bf16[1,64,2048]{2,1,0:T(8,128)(2,1)S(1)}, bf16[1,64,2048]{2,1,0:T(8,128)(2,1)S(1)}, u32[]{:S(2)}, u32[]{:S(2)}) collective-permute-start(bf16[1,64,2048]{2,1,0:T(8,128)(2,1)S(1)} %dynamic-slice_bitcast_fusion.in_ref), channel_id=1, source_target_pairs={{0,4},{4,0},{8,12},{12,8},{1,5},{5,1},{9,13},{13,9},{2,6},{6,2},{1... | collective-permute-start | bytes 786440 | tf_op jit(solution)/shard_map/ppermute | solution.py:39
  4.1 16.3 %collective-permute-start.1 = (bf16[1,64,2048]{2,1,0:T(8,128)(2,1)S(1)}, bf16[1,64,2048]{2,1,0:T(8,128)(2,1)S(1)}, u32[]{:S(2)}, u32[]{:S(2)}) collective-permute-start(bf16[1,64,2048]{2,1,0:T(8,128)(2,1)S(1)} %copied.1), channel_id=1, source_target_pairs={{0,8},{4,12},{8,0},{12,4},{1,9},{5,13},{9,1},{13,5},{2,10},{6,14},... | collective-permute-start | bytes 786440 | tf_op jit(solution)/shard_map/ppermute | solution.py:39
  6.7 1.9 %copy-start = (bf16[768,2048]{1,0:T(8,128)(2,1)S(1)}, bf16[768,2048]{1,0:T(8,128)(2,1)}, u32[]{:S(2)}) copy-start(bf16[768,2048]{1,0:T(8,128)(2,1)} %tokens_ref.9) | copy-start | bytes 9437188
  8.6 2.2 %copy-start.2 = (bf16[2048,1024]{1,0:T(8,128)(2,1)S(1)}, bf16[2048,1024]{1,0:T(8,128)(2,1)}, u32[]{:S(2)}) copy-start(bf16[2048,1024]{1,0:T(8,128)(2,1)} %weight_ref.3) | copy-start | bytes 12582916
  10.8 7.2 %copy-start.1 = (bf16[768,2048]{1,0:T(8,128)(2,1)S(1)}, bf16[768,2048]{1,0:T(8,128)(2,1)}, u32[]{:S(2)}) copy-start(bf16[768,2048]{1,0:T(8,128)(2,1)} %tokens_ref.9) | copy-start | bytes 9437188
  10.8 7.2 %copy-start.7 = (s32[768,1]{0,1:T(1,128)S(1)}, s32[768,1]{0,1:T(1,128)}, u32[]{:S(2)}) copy-start(s32[768,1]{0,1:T(1,128)} %param.9) | copy-start | bytes 9220
  10.8 8.5 %copy-start.3 = (bf16[2048,1024]{1,0:T(8,128)(2,1)S(1)}, bf16[2048,1024]{1,0:T(8,128)(2,1)}, u32[]{:S(2)}) copy-start(bf16[2048,1024]{1,0:T(8,128)(2,1)} %weight_ref.3) | copy-start | bytes 12582916
  15.8 7.6 %collective-permute-start.4 = (bf16[1,64,2048]{2,1,0:T(8,128)(2,1)S(1)}, bf16[1,64,2048]{2,1,0:T(8,128)(2,1)S(1)}, u32[]{:S(2)}, u32[]{:S(2)}) collective-permute-start(bf16[1,64,2048]{2,1,0:T(8,128)(2,1)S(1)} %collective-permute-done.refs_0_), channel_id=1, source_target_pairs={{0,16},{16,0},{1,17},{17,1},{2,18},{18,2},{3,19},{19,3},{4,20},{20... | collective-permute-start | bytes 786440 | tf_op jit(solution)/shard_map/ppermute | solution.py:39
  17.5 7.2 %collective-permute-start.5 = (bf16[768,256]{1,0:T(8,128)(2,1)S(1)}, bf16[768,256]{1,0:T(8,128)(2,1)S(1)}, u32[]{:S(2)}, u32[]{:S(2)}) collective-permute-start(bf16[768,256]{1,0:T(8,128)(2,1)S(1)} %get-tuple-element.35), channel_id=1, source_target_pairs={{0,1},{1,0},{2,3},{3,2},{4,5},{5,4},{6,7},{7,6},{8,9},{9,8},{10,11... | collective-permute-start | bytes 1179656 | tf_op jit(solution)/shard_map/ppermute | solution.py:39
  17.5 7.2 %collective-permute-start.6 = (bf16[768,256]{1,0:T(8,128)(2,1)S(1)}, bf16[768,256]{1,0:T(8,128)(2,1)S(1)}, u32[]{:S(2)}, u32[]{:S(2)}) collective-permute-start(bf16[768,256]{1,0:T(8,128)(2,1)S(1)} %get-tuple-element.36), channel_id=1, source_target_pairs={{0,1},{1,0},{2,3},{3,2},{4,5},{5,4},{6,7},{7,6},{8,9},{9,8},{10,11... | collective-permute-start | bytes 1179656 | tf_op jit(solution)/shard_map/ppermute | solution.py:39
  19.3 4.0 %copy-start.5 = (bf16[2,2048,64]{1,2,0:T(8,128)(2,1)S(1)}, bf16[2,2048,64]{1,2,0:T(8,128)(2,1)}, u32[]{:S(2)}) copy-start(bf16[2,2048,64]{1,2,0:T(8,128)(2,1)} %param.12) | copy-start | bytes 1572868
  20.4 4.3 %copy-start.6 = (bf16[2,64,256]{2,1,0:T(8,128)(2,1)S(1)}, bf16[2,64,256]{2,1,0:T(8,128)(2,1)}, u32[]{:S(2)}) copy-start(bf16[2,64,256]{2,1,0:T(8,128)(2,1)} %first_ref) | copy-start | bytes 196612
  20.4 9.2 %collective-permute-start.3 = (bf16[1,64,2048]{2,1,0:T(8,128)(2,1)S(1)}, bf16[1,64,2048]{2,1,0:T(8,128)(2,1)S(1)}, u32[]{:S(2)}, u32[]{:S(2)}) collective-permute-start(bf16[1,64,2048]{2,1,0:T(8,128)(2,1)S(1)} %collective-permute-done.1.refs_1_), channel_id=1, source_target_pairs={{0,4},{4,0},{8,12},{12,8},{1,5},{5,1},{9,13},{13,9},{2,6},{6,2},{1... | collective-permute-start | bytes 786440 | tf_op jit(solution)/shard_map/ppermute | solution.py:39
  20.5 10.6 %collective-permute-start.2 = (bf16[1,64,2048]{2,1,0:T(8,128)(2,1)S(1)}, bf16[1,64,2048]{2,1,0:T(8,128)(2,1)S(1)}, u32[]{:S(2)}, u32[]{:S(2)}) collective-permute-start(bf16[1,64,2048]{2,1,0:T(8,128)(2,1)S(1)} %collective-permute-done.1.refs_1_), channel_id=1, source_target_pairs={{0,16},{16,0},{1,17},{17,1},{2,18},{18,2},{3,19},{19,3},{4,20},{20... | collective-permute-start | bytes 786440 | tf_op jit(solution)/shard_map/ppermute | solution.py:39
  24.7 6.4 %collective-permute-start.7 = (bf16[2,64,256]{2,1,0:T(8,128)(2,1)S(1)}, bf16[2,64,256]{2,1,0:T(8,128)(2,1)S(1)}, u32[]{:S(2)}, u32[]{:S(2)}) collective-permute-start(bf16[2,64,256]{2,1,0:T(8,128)(2,1)S(1)} %copy-done.6), channel_id=1, source_target_pairs={{0,8},{4,12},{8,0},{12,4},{1,9},{5,13},{9,1},{13,5},{2,10},{6,14},... | collective-permute-start | bytes 196616 | tf_op jit(solution)/shard_map/ppermute | solution.py:39
  25.5 14.4 %collective-permute-start.11 = (bf16[768,256]{1,0:T(8,128)(2,1)S(1)}, bf16[768,256]{1,0:T(8,128)(2,1)S(1)}, u32[]{:S(2)}, u32[]{:S(2)}) collective-permute-start(bf16[768,256]{1,0:T(8,128)(2,1)S(1)} %add.7), channel_id=1, source_target_pairs={{0,2},{1,3},{2,0},{3,1},{4,6},{5,7},{6,4},{7,5},{8,10},{9,11},{10,... | collective-permute-start | bytes 1179656 | tf_op jit(solution)/shard_map/ppermute | solution.py:39
  29.6 7.2 %collective-permute-start.12 = (bf16[1,64,2048]{2,1,0:T(8,128)(2,1)S(1)}, bf16[1,64,2048]{2,1,0:T(8,128)(2,1)S(1)}, u32[]{:S(2)}, u32[]{:S(2)}) collective-permute-start(bf16[1,64,2048]{2,1,0:T(8,128)(2,1)S(1)} %collective-permute-done.3.refs_1_), channel_id=1, source_target_pairs={{0,16},{16,0},{1,17},{17,1},{2,18},{18,2},{3,19},{19,3},{4,20},{20... | collective-permute-start | bytes 786440 | tf_op jit(solution)/shard_map/ppermute | solution.py:39
  32.3 6.9 %copy-start.4 = (bf16[128,128]{1,0:T(8,128)(2,1)S(1)}, bf16[128,128]{1,0:T(8,128)(2,1)}, u32[]{:S(2)}) copy-start(bf16[128,128]{1,0:T(8,128)(2,1)} %constant.12.clone.matrix_ref) | copy-start | bytes 98308
  32.3 6.9 %copy-start.8 = (s32[128]{0:T(128)S(1)}, s32[128]{0:T(128)}, u32[]{:S(2)}) copy-start(s32[128]{0:T(128)} %param.14) | copy-start | bytes 1540
  32.3 7.6 %copy-start.9 = (f32[256]{0:T(256)S(1)}, f32[256]{0:T(256)}, u32[]{:S(2)}) copy-start(f32[256]{0:T(256)} %param.11) | copy-start | bytes 3076
  32.3 1.4 %collective-permute-start.8 = (bf16[64,768]{1,0:T(8,128)(2,1)S(1)}, bf16[64,768]{1,0:T(8,128)(2,1)S(1)}, u32[]{:S(2)}, u32[]{:S(2)}) collective-permute-start(bf16[64,768]{1,0:T(8,128)(2,1)S(1)} %low_rows.3.refs_0_), channel_id=1, source_target_pairs={{0,1},{1,0},{2,3},{3,2},{4,5},{5,4},{6,7},{7,6},{8,9},{9,8},{10,11... | collective-permute-start | bytes 294920 | tf_op jit(solution)/shard_map/ppermute | solution.py:39
  32.4 6.4 %collective-permute-start.10 = (bf16[4,64,256]{2,1,0:T(8,128)(2,1)S(1)}, bf16[4,64,256]{2,1,0:T(8,128)(2,1)S(1)}, u32[]{:S(2)}, u32[]{:S(2)}) collective-permute-start(bf16[4,64,256]{2,1,0:T(8,128)(2,1)S(1)} %joined.1.first_ref), channel_id=1, source_target_pairs={{0,4},{4,0},{8,12},{12,8},{1,5},{5,1},{9,13},{13,9},{2,6},{6,2},{1... | collective-permute-start | bytes 393224 | tf_op jit(solution)/shard_map/ppermute | solution.py:39
  33.7 6.1 %collective-permute-start.9 = (bf16[64,768]{1,0:T(8,128)(2,1)S(1)}, bf16[64,768]{1,0:T(8,128)(2,1)S(1)}, u32[]{:S(2)}, u32[]{:S(2)}) collective-permute-start(bf16[64,768]{1,0:T(8,128)(2,1)S(1)} %add.6.mine_ref), channel_id=1, source_target_pairs={{0,2},{1,3},{2,0},{3,1},{4,6},{5,7},{6,4},{7,5},{8,10},{9,11},{10,... | collective-permute-start | bytes 294920 | tf_op jit(solution)/shard_map/ppermute | solution.py:39
  37.2 3.8 %collective-permute-start.15 = (bf16[64,256]{1,0:T(8,128)(2,1)S(1)}, bf16[64,256]{1,0:T(8,128)(2,1)S(1)}, u32[]{:S(2)}, u32[]{:S(2)}) collective-permute-start(bf16[64,256]{1,0:T(8,128)(2,1)S(1)} %compact.1.refs_0_), channel_id=1, source_target_pairs={{0,3},{1,2},{2,1},{3,0},{4,7},{5,6},{6,5},{7,4},{8,11},{9,10},{10,... | collective-permute-start | bytes 98312 | tf_op jit(solution)/shard_map/ppermute | solution.py:39
  37.3 4.0 %collective-permute-start.14 = (bf16[64,256]{1,0:T(8,128)(2,1)S(1)}, bf16[64,256]{1,0:T(8,128)(2,1)S(1)}, u32[]{:S(2)}, u32[]{:S(2)}) collective-permute-start(bf16[64,256]{1,0:T(8,128)(2,1)S(1)} %compact.1.refs_0_), channel_id=1, source_target_pairs={{0,2},{1,3},{2,0},{3,1},{4,6},{5,7},{6,4},{7,5},{8,10},{9,11},{10,... | collective-permute-start | bytes 98312 | tf_op jit(solution)/shard_map/ppermute | solution.py:39
  38.8 2.5 %collective-permute-start.13 = (bf16[64,256]{1,0:T(8,128)(2,1)S(1)}, bf16[64,256]{1,0:T(8,128)(2,1)S(1)}, u32[]{:S(2)}, u32[]{:S(2)}) collective-permute-start(bf16[64,256]{1,0:T(8,128)(2,1)S(1)} %compact.1.refs_0_), channel_id=1, source_target_pairs={{0,1},{1,0},{2,3},{3,2},{4,5},{5,4},{6,7},{7,6},{8,9},{9,8},{10,11... | collective-permute-start | bytes 98312 | tf_op jit(solution)/shard_map/ppermute | solution.py:39

commit v23 on v22

--- a/solution.py
+++ b/solution.py
@@ -332,15 +332,13 @@
         mine += [(plane | bit, swap(piece, "adp", bit)) for plane, piece in mine]
         bit //= 2
     half = parts // 2
-    offsets = (*range(1, parts, 2), *range(2, parts, 2))
+    offsets = (*range(1, parts, 2), *range(0, parts, 2))
     blocks = list(partials(tokens, base_weight, parts, offsets, lasting(4)))
-    near, blocks[-1] = together(near, blocks[-1])
-    (block,) = partials(tokens, base_weight, parts, (0,), COST, blocks[-1])
     slots = -(-2 * tokens.shape[0] // (here * planes) // 128) * 128
     lasts = [(planes - 1, groups - 1, k) for k in range(share)]
     pick, chosen = picked(ids, tokens, here, share, lasts, slots)
-    close, block, pick, chosen, *far = together(near, block, pick, chosen, *(piece for _, piece in mine[1:]))
-    blocks = blocks[:half] + [block] + blocks[half:]
+    near, blocks[-1], pick, chosen = together(near, blocks[-1], pick, chosen)
+    close, *far = together(near, *(piece for _, piece in mine[1:]))
     mine = mine[:1] + [(plane, piece) for (plane, _), piece in zip(mine[1:], far)]
     odd = [(1, near)] + [(plane | 1, swap(piece, "adp", 1)) for plane, piece in mine[1:]]
 

time: 42.7 us -> 42.5 us (level)
  waiting for transfers between devices: 11.7 us -> 9.34 us
  starting transfers between devices: 14.9 us -> 17.2 us
    ppermute x16, waiting for transfers between devices: 11.7 us -> 9.34 us  [swap(): lax.ppermute(x, axis, [(i, i ^ bit) for i in range(lax.axis_size(axis))])]
    ppermute x16, starting transfers between devices: 14.9 us -> 17.2 us  [swap(): lax.ppermute(x, axis, [(i, i ^ bit) for i in range(lax.axis_size(axis))])]
    pallas_call x2 -> x1, Pallas kernels: 3.66 us -> 3.43 us  [partials(): pl.pallas_call(functools.partial(partial_kernel, offsets, parts), in_spec...]
    unnamed x20 -> x18, local copies, waits for them, and re-layouts: 4.12 us -> 4.11 us
  transfers between devices with their start and end apart: 16 -> 16, of which waited for: 8 -> 7; matrix products, arithmetic and copies ran while one was open for 0% -> 0% of each run, Pallas kernels for 22% -> 22%
where the time goes in v23:
time: 42.5 us; the launch traced here: 42.2 us
  starting transfers between devices  17.2 us (40%)
  Pallas kernels  10.4 us (24%)
  waiting for transfers between devices  9.34 us (22%)
  local copies, waits for them, and re-layouts  5.08 us (12%)
    ppermute x16, starting transfers between devices, swap(): lax.ppermute(x, axis, [(i, i ^ bit) for i in range(lax.axis_size(axis))])  17.2 us
    ppermute x16, waiting for transfers between devices, swap(): lax.ppermute(x, axis, [(i, i ^ bit) for i in range(lax.axis_size(axis))])  9.34 us
    unnamed x18, local copies, waits for them, and re-layouts  4.11 us
    pallas_call x1, Pallas kernels, partials(): pl.pallas_call(functools.partial(partial_kernel, offsets, parts), in_spec...  3.43 us
    pallas_call x2, Pallas kernels, low_rows(): pl.pallas_call(functools.partial(low_kernel, groups, here, share, rank, b...  2.38 us
    pallas_call x1, Pallas kernels, picked(): pl.pallas_call(functools.partial(pick_kernel, named, here, share), in_spe...  1.34 us
    pallas_call x1, Pallas kernels, final(): pl.pallas_call(final_kernel, in_specs=[VMEM] * (3 + len(kept)), out_specs...  1.24 us
    dynamic_slice x1, local copies, waits for them, and re-layouts, local(): lax.dynamic_slice_in_dim(down, lax.axis_index('grp') * share, share, 0)  0.97 us
  transfers between devices with their start and end apart: 16, of which 7 were waited for; matrix products, arithmetic and copies ran while one was open for 0% of the time, Pallas kernels for 22%

profile of v23, /device:TPU:0, one launch (start us, length us, event | category | flops | bytes accessed | tf_op | source)
XLA Modules:
  0.0 42.2 jit_solution(11475070642861965728)
XLA Ops:
  0.0 1.0 %dynamic-slice_bitcast_fusion.in_ref = bf16[1,64,2048]{2,1,0:T(8,128)(2,1)S(1)} fusion(bf16[2,2048,64]{1,2,0:T(8,128)(2,1)} %param.12, s32[]{:T(128)S(6)} %select_n.3), kind=kLoop, calls=%fused_computation | loop fusion | bytes 524292 | tf_op jit(solution)/shard_map/dynamic_slice | solution.py:327
  1.0 3.1 %collective-permute-start = (bf16[1,64,2048]{2,1,0:T(8,128)(2,1)S(1)}, bf16[1,64,2048]{2,1,0:T(8,128)(2,1)S(1)}, u32[]{:S(2)}, u32[]{:S(2)}) collective-permute-start(bf16[1,64,2048]{2,1,0:T(8,128)(2,1)S(1)} %dynamic-slice_bitcast_fusion.in_ref), channel_id=1, source_target_pairs={{0,4},{4,0},{8,12},{12,8},{1,5},{5,1},{9,13},{13,9},{2,6},{6,2},{1... | collective-permute-start | bytes 786440 | tf_op jit(solution)/shard_map/ppermute | solution.py:39
  4.1 2.7 %collective-permute-start.1 = (bf16[1,64,2048]{2,1,0:T(8,128)(2,1)S(1)}, bf16[1,64,2048]{2,1,0:T(8,128)(2,1)S(1)}, u32[]{:S(2)}, u32[]{:S(2)}) collective-permute-start(bf16[1,64,2048]{2,1,0:T(8,128)(2,1)S(1)} %copied.1), channel_id=1, source_target_pairs={{0,8},{4,12},{8,0},{12,4},{1,9},{5,13},{9,1},{13,5},{2,10},{6,14},... | collective-permute-start | bytes 786440 | tf_op jit(solution)/shard_map/ppermute | solution.py:39
  6.7 1.9 %copy-done = bf16[768,2048]{1,0:T(8,128)(2,1)S(1)} copy-done((bf16[768,2048]{1,0:T(8,128)(2,1)S(1)}, bf16[768,2048]{1,0:T(8,128)(2,1)}, u32[]{:S(2)}) %copy-start) | copy-done | bytes 3145752
  8.6 2.2 %copy-done.8 = bf16[2048,1024]{1,0:T(8,128)(2,1)S(1)} copy-done((bf16[2048,1024]{1,0:T(8,128)(2,1)S(1)}, bf16[2048,1024]{1,0:T(8,128)(2,1)}, u32[]{:S(2)}) %copy-start.8) | copy-done | bytes 4194328
  10.8 3.4 %partials.1 = (bf16[768,256]{1,0:T(8,128)(2,1)S(1)}, bf16[768,256]{1,0:T(8,128)(2,1)S(1)}, bf16[768,256]{1,0:T(8,128)(2,1)S(1)}, bf16[768,256]{1,0:T(8,128)(2,1)S(1)}) custom-call(bf16[768,2048]{1,0:T(8,128)(2,1)S(1)} %copy-done, bf16[2048,1024]{1,0:T(8,128)(2,1)S(1)} %copy-done.8), custom_call_target="tpu_custom_call" | custom-call | flops 4000000000 | bytes 1 | tf_op jit(solution)/shard_map/partials/pallas_call | solution.py:70
  14.3 1.3 %picked.1 = (bf16[768,256]{1,0:T(8,128)(2,1)S(1)}, bf16[256,2048]{1,0:T(8,128)(2,1)S(1)}) custom-call(s32[1,768]{1,0:T(1,128)S(1)} %bitcast.7, bf16[768,2048]{1,0:T(8,128)(2,1)S(1)} %copy-done.1), custom_call_target="tpu_custom_call" | custom-call | flops 1 | bytes 1 | tf_op jit(solution)/shard_map/picked/pallas_call | solution.py:216
  15.6 0.2 collective-permute-done.refs_0_
  15.8 1.7 %collective-permute-start.4 = (bf16[1,64,2048]{2,1,0:T(8,128)(2,1)S(1)}, bf16[1,64,2048]{2,1,0:T(8,128)(2,1)S(1)}, u32[]{:S(2)}, u32[]{:S(2)}) collective-permute-start(bf16[1,64,2048]{2,1,0:T(8,128)(2,1)S(1)} %collective-permute-done.refs_0_), channel_id=1, source_target_pairs={{0,16},{16,0},{1,17},{17,1},{2,18},{18,2},{3,19},{19,3},{4,20},{20... | collective-permute-start | bytes 786440 | tf_op jit(solution)/shard_map/ppermute | solution.py:39
  17.5 0.5 %collective-permute-start.6 = (bf16[768,256]{1,0:T(8,128)(2,1)S(1)}, bf16[768,256]{1,0:T(8,128)(2,1)S(1)}, u32[]{:S(2)}, u32[]{:S(2)}) collective-permute-start(bf16[768,256]{1,0:T(8,128)(2,1)S(1)} %get-tuple-element.35), channel_id=1, source_target_pairs={{0,1},{1,0},{2,3},{3,2},{4,5},{5,4},{6,7},{7,6},{8,9},{9,8},{10,11... | collective-permute-start | bytes 1179656 | tf_op jit(solution)/shard_map/ppermute | solution.py:39
  18.0 0.5 %collective-permute-done.1.refs_1_ = bf16[1,64,2048]{2,1,0:T(8,128)(2,1)S(1)} collective-permute-done((bf16[1,64,2048]{2,1,0:T(8,128)(2,1)S(1)}, bf16[1,64,2048]{2,1,0:T(8,128)(2,1)S(1)}, u32[]{:S(2)}, u32[]{:S(2)}) %collective-permute-start.1) | collective-permute-done | bytes 262176 | tf_op jit(solution)/shard_map/ppermute | solution.py:39
  18.5 0.4 collective-permute-start.3
  18.8 1.5 %collective-permute-start.2 = (bf16[1,64,2048]{2,1,0:T(8,128)(2,1)S(1)}, bf16[1,64,2048]{2,1,0:T(8,128)(2,1)S(1)}, u32[]{:S(2)}, u32[]{:S(2)}) collective-permute-start(bf16[1,64,2048]{2,1,0:T(8,128)(2,1)S(1)} %collective-permute-done.1.refs_1_), channel_id=1, source_target_pairs={{0,16},{16,0},{1,17},{17,1},{2,18},{18,2},{3,19},{19,3},{4,20},{20... | collective-permute-start | bytes 786440 | tf_op jit(solution)/shard_map/ppermute | solution.py:39
  20.4 4.7 %collective-permute-done.4.refs_2_ = bf16[1,64,2048]{2,1,0:T(8,128)(2,1)S(1)} collective-permute-done((bf16[1,64,2048]{2,1,0:T(8,128)(2,1)S(1)}, bf16[1,64,2048]{2,1,0:T(8,128)(2,1)S(1)}, u32[]{:S(2)}, u32[]{:S(2)}) %collective-permute-start.4) | collective-permute-done | bytes 262176 | tf_op jit(solution)/shard_map/ppermute | solution.py:39
  25.0 1.2 %low_rows.2.refs_2_ = f32[64,768]{1,0:T(8,128)S(1)} custom-call(s32[1,768]{1,0:T(1,128)S(1)} %bitcast.8, bf16[768,2048]{1,0:T(8,128)(2,1)S(1)} %copy-done.1, bf16[1,64,2048]{2,1,0:T(8,128)(2,1)S(1)} %collective-permute-done.refs_0_, bf16[1,64,2048]{2,1,0:T(8,128)(2,1)S(1)} %collective-permute-done.1.refs_1_, ...), custom_call_target="tpu_custom_call" | custom-call | flops 2000000000 | bytes 1 | tf_op jit(solution)/shard_map/low_rows/pallas_call | solution.py:125
  26.3 0.1 collective-permute-start.7
  26.4 0.1 add.7
  26.5 1.7 %collective-permute-start.11 = (bf16[768,256]{1,0:T(8,128)(2,1)S(1)}, bf16[768,256]{1,0:T(8,128)(2,1)S(1)}, u32[]{:S(2)}, u32[]{:S(2)}) collective-permute-start(bf16[768,256]{1,0:T(8,128)(2,1)S(1)} %add.7), channel_id=1, source_target_pairs={{0,2},{1,3},{2,0},{3,1},{4,6},{5,7},{6,4},{7,5},{8,10},{9,11},{10,... | collective-permute-start | bytes 1179656 | tf_op jit(solution)/shard_map/ppermute | solution.py:39
  28.2 1.5 %collective-permute-start.12 = (bf16[1,64,2048]{2,1,0:T(8,128)(2,1)S(1)}, bf16[1,64,2048]{2,1,0:T(8,128)(2,1)S(1)}, u32[]{:S(2)}, u32[]{:S(2)}) collective-permute-start(bf16[1,64,2048]{2,1,0:T(8,128)(2,1)S(1)} %collective-permute-done.3.refs_1_), channel_id=1, source_target_pairs={{0,16},{16,0},{1,17},{17,1},{2,18},{18,2},{3,19},{19,3},{4,20},{20... | collective-permute-start | bytes 786440 | tf_op jit(solution)/shard_map/ppermute | solution.py:39
  29.7 2.2 %collective-permute-done.7.second_ref = bf16[2,64,256]{2,1,0:T(8,128)(2,1)S(1)} collective-permute-done((bf16[2,64,256]{2,1,0:T(8,128)(2,1)S(1)}, bf16[2,64,256]{2,1,0:T(8,128)(2,1)S(1)}, u32[]{:S(2)}, u32[]{:S(2)}) %collective-permute-start.7) | collective-permute-done | bytes 65568 | tf_op jit(solution)/shard_map/ppermute | solution.py:39
  31.9 1.2 %low_rows.3.refs_0_ = bf16[64,768]{1,0:T(8,128)(2,1)S(1)} custom-call(s32[1,768]{1,0:T(1,128)S(1)} %bitcast.9, bf16[768,2048]{1,0:T(8,128)(2,1)S(1)} %copy-done.1, bf16[1,64,2048]{2,1,0:T(8,128)(2,1)S(1)} %collective-permute-done.2.refs_0_, bf16[1,64,2048]{2,1,0:T(8,128)(2,1)S(1)} %collective-permute-done.3.refs_1_, f32[64,768]{1,0:T(8,128)S(1)} %low_rows.2.refs_2_), custom_call_target="tpu_custom_call" | custom-call | flops 5000000000 | bytes 1 | tf_op jit(solution)/shard_map/low_rows/pallas_call | solution.py:125
  33.1 0.1 collective-permute-start.8
  33.2 0.9 %collective-permute-start.10 = (bf16[4,64,256]{2,1,0:T(8,128)(2,1)S(1)}, bf16[4,64,256]{2,1,0:T(8,128)(2,1)S(1)}, u32[]{:S(2)}, u32[]{:S(2)}) collective-permute-start(bf16[4,64,256]{2,1,0:T(8,128)(2,1)S(1)} %joined.1.first_ref), channel_id=1, source_target_pairs={{0,4},{4,0},{8,12},{12,8},{1,5},{5,1},{9,13},{13,9},{2,6},{6,2},{1... | collective-permute-start | bytes 393224 | tf_op jit(solution)/shard_map/ppermute | solution.py:39
  34.1 0.4 collective-permute-done.8.refs_1_
  34.5 1.6 %collective-permute-start.9 = (bf16[64,768]{1,0:T(8,128)(2,1)S(1)}, bf16[64,768]{1,0:T(8,128)(2,1)S(1)}, u32[]{:S(2)}, u32[]{:S(2)}) collective-permute-start(bf16[64,768]{1,0:T(8,128)(2,1)S(1)} %add.6.mine_ref), channel_id=1, source_target_pairs={{0,2},{1,3},{2,0},{3,1},{4,6},{5,7},{6,4},{7,5},{8,10},{9,11},{10,... | collective-permute-start | bytes 294920 | tf_op jit(solution)/shard_map/ppermute | solution.py:39
  36.1 0.4 %compact.1.refs_0_ = bf16[64,256]{1,0:T(8,128)(2,1)S(1)} custom-call(bf16[256,2048]{1,0:T(8,128)(2,1)S(1)} %get-tuple-element.48.chosen_ref, bf16[1,64,2048]{2,1,0:T(8,128)(2,1)S(1)} %collective-permute-done.12.piece_ref), custom_call_target="tpu_custom_call" | custom-call | flops 2000000000 | bytes 1 | tf_op jit(solution)/shard_map/compact/pallas_call | solution.py:239
  36.6 1.5 %collective-permute-start.14 = (bf16[64,256]{1,0:T(8,128)(2,1)S(1)}, bf16[64,256]{1,0:T(8,128)(2,1)S(1)}, u32[]{:S(2)}, u32[]{:S(2)}) collective-permute-start(bf16[64,256]{1,0:T(8,128)(2,1)S(1)} %compact.1.refs_0_), channel_id=1, source_target_pairs={{0,2},{1,3},{2,0},{3,1},{4,6},{5,7},{6,4},{7,5},{8,10},{9,11},{10,... | collective-permute-start | bytes 98312 | tf_op jit(solution)/shard_map/ppermute | solution.py:39
  38.1 1.1 %collective-permute-done.10.second_ref = bf16[4,64,256]{2,1,0:T(8,128)(2,1)S(1)} collective-permute-done((bf16[4,64,256]{2,1,0:T(8,128)(2,1)S(1)}, bf16[4,64,256]{2,1,0:T(8,128)(2,1)S(1)}, u32[]{:S(2)}, u32[]{:S(2)}) %collective-permute-start.10) | collective-permute-done | bytes 131104 | tf_op jit(solution)/shard_map/ppermute | solution.py:39
  39.2 0.7 %rotated_ups.1 = (bf16[512,256]{1,0:T(8,128)(2,1)S(1)}, bf16[768,512]{1,0:T(8,128)(2,1)S(1)}) custom-call(s32[1,768]{1,0:T(1,128)S(1)} %bitcast.10, s32[1,128]{1,0:T(1,128)S(1)} %bitcast.11, bf16[128,128]{1,0:T(8,128)(2,1)S(1)} %copy-done.2, bf16[4,64,256]{2,1,0:T(8,128)(2,1)S(1)} %joined.1.first_ref, bf16[4,64,256]{2,1,0:T(8,128)(2,1)S(1)} %collective-permute-done.10.second_ref), custom_call_target="tpu_custom_call" | custom-call | flops 1 | bytes 1 | tf_op jit(solution)/shard_map/rotated_ups/pallas_call | solution.py:182
  39.9 0.8 %most.1 = (bf16[64,256]{1,0:T(8,128)(2,1)S(1)}, f32[768,256]{1,0:T(8,128)S(1)}) custom-call(bf16[64,768]{1,0:T(8,128)(2,1)S(1)} %add.6.mine_ref, bf16[64,768]{1,0:T(8,128)(2,1)S(1)} %collective-permute-done.9.theirs_ref, bf16[512,256]{1,0:T(8,128)(2,1)S(1)} %get-tuple-element.40.up_ref, bf16[768,512]{1,0:T(8,128)(2,1)S(1)} %get-tuple-element.41.mask_ref, ...), custom_call_target="tpu_custom_call" | custom-call | flops 1 | bytes 1 | tf_op jit(solution)/shard_map/most/pallas_call | solution.py:267
  40.7 0.3 collective-permute-done.14.refs_2_
  41.0 1.2 %final.1 = bf16[768,256]{1,0:T(8,128)(2,1)} custom-call(bf16[768,256]{1,0:T(8,128)(2,1)S(1)} %get-tuple-element.30.pick_ref, bf16[64,256]{1,0:T(8,128)(2,1)S(1)} %get-tuple-element.46.last_ref, f32[768,256]{1,0:T(8,128)S(1)} %get-tuple-element.47.most_ref, bf16[64,256]{1,0:T(8,128)(2,1)S(1)} %compact.1.refs_0_, ...), custom_call_target="tpu_custom_call" | custom-call | flops 1 | bytes 1 | tf_op jit(solution)/shard_map/final/pallas_call | solution.py:305
  (31 shorter events, 0.2 us)
Async XLA Ops:
  1.0 14.8 %collective-permute-start = (bf16[1,64,2048]{2,1,0:T(8,128)(2,1)S(1)}, bf16[1,64,2048]{2,1,0:T(8,128)(2,1)S(1)}, u32[]{:S(2)}, u32[]{:S(2)}) collective-permute-start(bf16[1,64,2048]{2,1,0:T(8,128)(2,1)S(1)} %dynamic-slice_bitcast_fusion.in_ref), channel_id=1, source_target_pairs={{0,4},{4,0},{8,12},{12,8},{1,5},{5,1},{9,13},{13,9},{2,6},{6,2},{1... | collective-permute-start | bytes 786440 | tf_op jit(solution)/shard_map/ppermute | solution.py:39
  4.1 14.4 %collective-permute-start.1 = (bf16[1,64,2048]{2,1,0:T(8,128)(2,1)S(1)}, bf16[1,64,2048]{2,1,0:T(8,128)(2,1)S(1)}, u32[]{:S(2)}, u32[]{:S(2)}) collective-permute-start(bf16[1,64,2048]{2,1,0:T(8,128)(2,1)S(1)} %copied.1), channel_id=1, source_target_pairs={{0,8},{4,12},{8,0},{12,4},{1,9},{5,13},{9,1},{13,5},{2,10},{6,14},... | collective-permute-start | bytes 786440 | tf_op jit(solution)/shard_map/ppermute | solution.py:39
  6.7 1.9 %copy-start = (bf16[768,2048]{1,0:T(8,128)(2,1)S(1)}, bf16[768,2048]{1,0:T(8,128)(2,1)}, u32[]{:S(2)}) copy-start(bf16[768,2048]{1,0:T(8,128)(2,1)} %tokens_ref.7) | copy-start | bytes 9437188
  8.6 2.2 %copy-start.8 = (bf16[2048,1024]{1,0:T(8,128)(2,1)S(1)}, bf16[2048,1024]{1,0:T(8,128)(2,1)}, u32[]{:S(2)}) copy-start(bf16[2048,1024]{1,0:T(8,128)(2,1)} %weight_ref.1) | copy-start | bytes 12582916
  10.8 3.4 %copy-start.1 = (bf16[768,2048]{1,0:T(8,128)(2,1)S(1)}, bf16[768,2048]{1,0:T(8,128)(2,1)}, u32[]{:S(2)}) copy-start(bf16[768,2048]{1,0:T(8,128)(2,1)} %tokens_ref.7) | copy-start | bytes 9437188
  10.8 3.5 %copy-start.5 = (s32[768,1]{0,1:T(1,128)S(1)}, s32[768,1]{0,1:T(1,128)}, u32[]{:S(2)}) copy-start(s32[768,1]{0,1:T(1,128)} %param.9) | copy-start | bytes 9220
  10.8 14.2 %copy-start.3 = (bf16[2,2048,64]{1,2,0:T(8,128)(2,1)S(1)}, bf16[2,2048,64]{1,2,0:T(8,128)(2,1)}, u32[]{:S(2)}) copy-start(bf16[2,2048,64]{1,2,0:T(8,128)(2,1)} %param.12) | copy-start | bytes 1572868
  15.6 10.7 %copy-start.4 = (bf16[2,64,256]{2,1,0:T(8,128)(2,1)S(1)}, bf16[2,64,256]{2,1,0:T(8,128)(2,1)}, u32[]{:S(2)}) copy-start(bf16[2,64,256]{2,1,0:T(8,128)(2,1)} %first_ref) | copy-start | bytes 196612
  15.8 9.2 %collective-permute-start.4 = (bf16[1,64,2048]{2,1,0:T(8,128)(2,1)S(1)}, bf16[1,64,2048]{2,1,0:T(8,128)(2,1)S(1)}, u32[]{:S(2)}, u32[]{:S(2)}) collective-permute-start(bf16[1,64,2048]{2,1,0:T(8,128)(2,1)S(1)} %collective-permute-done.refs_0_), channel_id=1, source_target_pairs={{0,16},{16,0},{1,17},{17,1},{2,18},{18,2},{3,19},{19,3},{4,20},{20... | collective-permute-start | bytes 786440 | tf_op jit(solution)/shard_map/ppermute | solution.py:39
  17.5 8.8 %collective-permute-start.5 = (bf16[768,256]{1,0:T(8,128)(2,1)S(1)}, bf16[768,256]{1,0:T(8,128)(2,1)S(1)}, u32[]{:S(2)}, u32[]{:S(2)}) collective-permute-start(bf16[768,256]{1,0:T(8,128)(2,1)S(1)} %get-tuple-element.34), channel_id=1, source_target_pairs={{0,1},{1,0},{2,3},{3,2},{4,5},{5,4},{6,7},{7,6},{8,9},{9,8},{10,11... | collective-permute-start | bytes 1179656 | tf_op jit(solution)/shard_map/ppermute | solution.py:39
  17.5 8.8 %collective-permute-start.6 = (bf16[768,256]{1,0:T(8,128)(2,1)S(1)}, bf16[768,256]{1,0:T(8,128)(2,1)S(1)}, u32[]{:S(2)}, u32[]{:S(2)}) collective-permute-start(bf16[768,256]{1,0:T(8,128)(2,1)S(1)} %get-tuple-element.35), channel_id=1, source_target_pairs={{0,1},{1,0},{2,3},{3,2},{4,5},{5,4},{6,7},{7,6},{8,9},{9,8},{10,11... | collective-permute-start | bytes 1179656 | tf_op jit(solution)/shard_map/ppermute | solution.py:39
  18.5 9.7 %collective-permute-start.3 = (bf16[1,64,2048]{2,1,0:T(8,128)(2,1)S(1)}, bf16[1,64,2048]{2,1,0:T(8,128)(2,1)S(1)}, u32[]{:S(2)}, u32[]{:S(2)}) collective-permute-start(bf16[1,64,2048]{2,1,0:T(8,128)(2,1)S(1)} %collective-permute-done.1.refs_1_), channel_id=1, source_target_pairs={{0,4},{4,0},{8,12},{12,8},{1,5},{5,1},{9,13},{13,9},{2,6},{6,2},{1... | collective-permute-start | bytes 786440 | tf_op jit(solution)/shard_map/ppermute | solution.py:39
  18.8 13.1 %collective-permute-start.2 = (bf16[1,64,2048]{2,1,0:T(8,128)(2,1)S(1)}, bf16[1,64,2048]{2,1,0:T(8,128)(2,1)S(1)}, u32[]{:S(2)}, u32[]{:S(2)}) collective-permute-start(bf16[1,64,2048]{2,1,0:T(8,128)(2,1)S(1)} %collective-permute-done.1.refs_1_), channel_id=1, source_target_pairs={{0,16},{16,0},{1,17},{17,1},{2,18},{18,2},{3,19},{19,3},{4,20},{20... | collective-permute-start | bytes 786440 | tf_op jit(solution)/shard_map/ppermute | solution.py:39
  26.3 5.6 %collective-permute-start.7 = (bf16[2,64,256]{2,1,0:T(8,128)(2,1)S(1)}, bf16[2,64,256]{2,1,0:T(8,128)(2,1)S(1)}, u32[]{:S(2)}, u32[]{:S(2)}) collective-permute-start(bf16[2,64,256]{2,1,0:T(8,128)(2,1)S(1)} %copy-done.4), channel_id=1, source_target_pairs={{0,8},{4,12},{8,0},{12,4},{1,9},{5,13},{9,1},{13,5},{2,10},{6,14},... | collective-permute-start | bytes 196616 | tf_op jit(solution)/shard_map/ppermute | solution.py:39
  26.5 13.4 %collective-permute-start.11 = (bf16[768,256]{1,0:T(8,128)(2,1)S(1)}, bf16[768,256]{1,0:T(8,128)(2,1)S(1)}, u32[]{:S(2)}, u32[]{:S(2)}) collective-permute-start(bf16[768,256]{1,0:T(8,128)(2,1)S(1)} %add.7), channel_id=1, source_target_pairs={{0,2},{1,3},{2,0},{3,1},{4,6},{5,7},{6,4},{7,5},{8,10},{9,11},{10,... | collective-permute-start | bytes 1179656 | tf_op jit(solution)/shard_map/ppermute | solution.py:39
  28.2 7.9 %collective-permute-start.12 = (bf16[1,64,2048]{2,1,0:T(8,128)(2,1)S(1)}, bf16[1,64,2048]{2,1,0:T(8,128)(2,1)S(1)}, u32[]{:S(2)}, u32[]{:S(2)}) collective-permute-start(bf16[1,64,2048]{2,1,0:T(8,128)(2,1)S(1)} %collective-permute-done.3.refs_1_), channel_id=1, source_target_pairs={{0,16},{16,0},{1,17},{17,1},{2,18},{18,2},{3,19},{19,3},{4,20},{20... | collective-permute-start | bytes 786440 | tf_op jit(solution)/shard_map/ppermute | solution.py:39
  33.1 6.1 %copy-start.2 = (bf16[128,128]{1,0:T(8,128)(2,1)S(1)}, bf16[128,128]{1,0:T(8,128)(2,1)}, u32[]{:S(2)}) copy-start(bf16[128,128]{1,0:T(8,128)(2,1)} %constant.12.clone.matrix_ref) | copy-start | bytes 98308
  33.1 6.1 %copy-start.6 = (s32[128]{0:T(128)S(1)}, s32[128]{0:T(128)}, u32[]{:S(2)}) copy-start(s32[128]{0:T(128)} %param.14) | copy-start | bytes 1540
  33.1 6.8 %copy-start.7 = (f32[256]{0:T(256)S(1)}, f32[256]{0:T(256)}, u32[]{:S(2)}) copy-start(f32[256]{0:T(256)} %param.11) | copy-start | bytes 3076
  33.1 1.4 %collective-permute-start.8 = (bf16[64,768]{1,0:T(8,128)(2,1)S(1)}, bf16[64,768]{1,0:T(8,128)(2,1)S(1)}, u32[]{:S(2)}, u32[]{:S(2)}) collective-permute-start(bf16[64,768]{1,0:T(8,128)(2,1)S(1)} %low_rows.3.refs_0_), channel_id=1, source_target_pairs={{0,1},{1,0},{2,3},{3,2},{4,5},{5,4},{6,7},{7,6},{8,9},{9,8},{10,11... | collective-permute-start | bytes 294920 | tf_op jit(solution)/shard_map/ppermute | solution.py:39
  33.2 6.0 %collective-permute-start.10 = (bf16[4,64,256]{2,1,0:T(8,128)(2,1)S(1)}, bf16[4,64,256]{2,1,0:T(8,128)(2,1)S(1)}, u32[]{:S(2)}, u32[]{:S(2)}) collective-permute-start(bf16[4,64,256]{2,1,0:T(8,128)(2,1)S(1)} %joined.1.first_ref), channel_id=1, source_target_pairs={{0,4},{4,0},{8,12},{12,8},{1,5},{5,1},{9,13},{13,9},{2,6},{6,2},{1... | collective-permute-start | bytes 393224 | tf_op jit(solution)/shard_map/ppermute | solution.py:39
  34.5 5.3 %collective-permute-start.9 = (bf16[64,768]{1,0:T(8,128)(2,1)S(1)}, bf16[64,768]{1,0:T(8,128)(2,1)S(1)}, u32[]{:S(2)}, u32[]{:S(2)}) collective-permute-start(bf16[64,768]{1,0:T(8,128)(2,1)S(1)} %add.6.mine_ref), channel_id=1, source_target_pairs={{0,2},{1,3},{2,0},{3,1},{4,6},{5,7},{6,4},{7,5},{8,10},{9,11},{10,... | collective-permute-start | bytes 294920 | tf_op jit(solution)/shard_map/ppermute | solution.py:39
  36.5 4.1 %collective-permute-start.15 = (bf16[64,256]{1,0:T(8,128)(2,1)S(1)}, bf16[64,256]{1,0:T(8,128)(2,1)S(1)}, u32[]{:S(2)}, u32[]{:S(2)}) collective-permute-start(bf16[64,256]{1,0:T(8,128)(2,1)S(1)} %compact.1.refs_0_), channel_id=1, source_target_pairs={{0,3},{1,2},{2,1},{3,0},{4,7},{5,6},{6,5},{7,4},{8,11},{9,10},{10,... | collective-permute-start | bytes 98312 | tf_op jit(solution)/shard_map/ppermute | solution.py:39
  36.6 4.4 %collective-permute-start.14 = (bf16[64,256]{1,0:T(8,128)(2,1)S(1)}, bf16[64,256]{1,0:T(8,128)(2,1)S(1)}, u32[]{:S(2)}, u32[]{:S(2)}) collective-permute-start(bf16[64,256]{1,0:T(8,128)(2,1)S(1)} %compact.1.refs_0_), channel_id=1, source_target_pairs={{0,2},{1,3},{2,0},{3,1},{4,6},{5,7},{6,4},{7,5},{8,10},{9,11},{10,... | collective-permute-start | bytes 98312 | tf_op jit(solution)/shard_map/ppermute | solution.py:39
  39.2 1.8 %collective-permute-start.13 = (bf16[64,256]{1,0:T(8,128)(2,1)S(1)}, bf16[64,256]{1,0:T(8,128)(2,1)S(1)}, u32[]{:S(2)}, u32[]{:S(2)}) collective-permute-start(bf16[64,256]{1,0:T(8,128)(2,1)S(1)} %compact.1.refs_0_), channel_id=1, source_target_pairs={{0,1},{1,0},{2,3},{3,2},{4,5},{5,4},{6,7},{7,6},{8,9},{9,8},{10,11... | collective-permute-start | bytes 98312 | tf_op jit(solution)/shard_map/ppermute | solution.py:39

commit v24 on v23

--- a/solution.py
+++ b/solution.py
@@ -358,7 +358,7 @@
             arrays = arrays + [down]
         return low_rows(ids, tokens, here, share, [((0, features), every)], arrays, low, dtype, cost)
 
-    low = more(None, held[: len(mine)] + swapped[:1], F32, lasting(2))
+    low = more(None, held[: len(mine)], F32, lasting(5))
     low, ups, *came = together(low, adapter_up, *(swap(block, "tp", 1) for block in blocks[:half]))
 
     def both(low):
@@ -377,6 +377,7 @@
         rest[0], ups = (plane, off, piece), joined(ups, other)
         order += [plane | bit for plane in order]
         bit //= 2
+    low = more(low, swapped[:1], F32, lasting(5))
     low = more(low, swapped[1:-1] + rest, BF16, lasting(5))
     more_ups = swap(ups, "adp", 1)
     low, other = both(low)

time: 42.5 us -> 42.2 us (level)
  waiting for transfers between devices: 9.34 us -> 7.41 us
  Pallas kernels: 10.4 us -> 11.3 us
  starting transfers between devices: 17.2 us -> 18 us
    ppermute x16, waiting for transfers between devices: 9.34 us -> 7.41 us  [swap(): lax.ppermute(x, axis, [(i, i ^ bit) for i in range(lax.axis_size(axis))])]
    pallas_call x2 -> x3, Pallas kernels: 2.38 us -> 3.26 us  [low_rows(): pl.pallas_call(functools.partial(low_kernel, groups, here, share, rank, b...]
    ppermute x16, starting transfers between devices: 17.2 us -> 18 us  [swap(): lax.ppermute(x, axis, [(i, i ^ bit) for i in range(lax.axis_size(axis))])]
  transfers between devices with their start and end apart: 16 -> 16, of which waited for: 7 -> 6; matrix products, arithmetic and copies ran while one was open for 0% -> 0% of each run, Pallas kernels for 22% -> 24%
where the time goes in v24:
time: 42.2 us; the launch traced here: 42 us
  starting transfers between devices  18 us (43%)
  Pallas kernels  11.3 us (27%)
  waiting for transfers between devices  7.41 us (18%)
  local copies, waits for them, and re-layouts  5.08 us (12%)
    ppermute x16, starting transfers between devices, swap(): lax.ppermute(x, axis, [(i, i ^ bit) for i in range(lax.axis_size(axis))])  18 us
    ppermute x16, waiting for transfers between devices, swap(): lax.ppermute(x, axis, [(i, i ^ bit) for i in range(lax.axis_size(axis))])  7.41 us
    unnamed x18, local copies, waits for them, and re-layouts  4.11 us
    pallas_call x1, Pallas kernels, partials(): pl.pallas_call(functools.partial(partial_kernel, offsets, parts), in_spec...  3.43 us
    pallas_call x3, Pallas kernels, low_rows(): pl.pallas_call(functools.partial(low_kernel, groups, here, share, rank, b...  3.26 us
    pallas_call x1, Pallas kernels, picked(): pl.pallas_call(functools.partial(pick_kernel, named, here, share), in_spe...  1.33 us
    pallas_call x1, Pallas kernels, final(): pl.pallas_call(final_kernel, in_specs=[VMEM] * (3 + len(kept)), out_specs...  1.24 us
    dynamic_slice x1, local copies, waits for them, and re-layouts, local(): lax.dynamic_slice_in_dim(down, lax.axis_index('grp') * share, share, 0)  0.97 us
  transfers between devices with their start and end apart: 16, of which 6 were waited for; matrix products, arithmetic and copies ran while one was open for 0% of the time, Pallas kernels for 24%

profile of v24, /device:TPU:0, one launch (start us, length us, event | category | flops | bytes accessed | tf_op | source)
XLA Modules:
  0.0 42.0 jit_solution(16472440653419249177)
XLA Ops:
  0.0 1.0 %dynamic-slice_bitcast_fusion.in_ref = bf16[1,64,2048]{2,1,0:T(8,128)(2,1)S(1)} fusion(bf16[2,2048,64]{1,2,0:T(8,128)(2,1)} %param.12, s32[]{:T(128)S(6)} %select_n.3), kind=kLoop, calls=%fused_computation | loop fusion | bytes 524292 | tf_op jit(solution)/shard_map/dynamic_slice | solution.py:327
  1.0 3.1 %collective-permute-start = (bf16[1,64,2048]{2,1,0:T(8,128)(2,1)S(1)}, bf16[1,64,2048]{2,1,0:T(8,128)(2,1)S(1)}, u32[]{:S(2)}, u32[]{:S(2)}) collective-permute-start(bf16[1,64,2048]{2,1,0:T(8,128)(2,1)S(1)} %dynamic-slice_bitcast_fusion.in_ref), channel_id=1, source_target_pairs={{0,4},{4,0},{8,12},{12,8},{1,5},{5,1},{9,13},{13,9},{2,6},{6,2},{1... | collective-permute-start | bytes 786440 | tf_op jit(solution)/shard_map/ppermute | solution.py:39
  4.1 2.7 %collective-permute-start.1 = (bf16[1,64,2048]{2,1,0:T(8,128)(2,1)S(1)}, bf16[1,64,2048]{2,1,0:T(8,128)(2,1)S(1)}, u32[]{:S(2)}, u32[]{:S(2)}) collective-permute-start(bf16[1,64,2048]{2,1,0:T(8,128)(2,1)S(1)} %copied.1), channel_id=1, source_target_pairs={{0,8},{4,12},{8,0},{12,4},{1,9},{5,13},{9,1},{13,5},{2,10},{6,14},... | collective-permute-start | bytes 786440 | tf_op jit(solution)/shard_map/ppermute | solution.py:39
  6.7 1.9 %copy-done = bf16[768,2048]{1,0:T(8,128)(2,1)S(1)} copy-done((bf16[768,2048]{1,0:T(8,128)(2,1)S(1)}, bf16[768,2048]{1,0:T(8,128)(2,1)}, u32[]{:S(2)}) %copy-start) | copy-done | bytes 3145752
  8.6 2.2 %copy-done.8 = bf16[2048,1024]{1,0:T(8,128)(2,1)S(1)} copy-done((bf16[2048,1024]{1,0:T(8,128)(2,1)S(1)}, bf16[2048,1024]{1,0:T(8,128)(2,1)}, u32[]{:S(2)}) %copy-start.8) | copy-done | bytes 4194328
  10.8 3.4 %partials.1 = (bf16[768,256]{1,0:T(8,128)(2,1)S(1)}, bf16[768,256]{1,0:T(8,128)(2,1)S(1)}, bf16[768,256]{1,0:T(8,128)(2,1)S(1)}, bf16[768,256]{1,0:T(8,128)(2,1)S(1)}) custom-call(bf16[768,2048]{1,0:T(8,128)(2,1)S(1)} %copy-done, bf16[2048,1024]{1,0:T(8,128)(2,1)S(1)} %copy-done.8), custom_call_target="tpu_custom_call" | custom-call | flops 4000000000 | bytes 1 | tf_op jit(solution)/shard_map/partials/pallas_call | solution.py:70
  14.3 0.1 collective-permute-start.4
  14.3 0.5 %collective-permute-start.5 = (bf16[768,256]{1,0:T(8,128)(2,1)S(1)}, bf16[768,256]{1,0:T(8,128)(2,1)S(1)}, u32[]{:S(2)}, u32[]{:S(2)}) collective-permute-start(bf16[768,256]{1,0:T(8,128)(2,1)S(1)} %get-tuple-element.35), channel_id=1, source_target_pairs={{0,1},{1,0},{2,3},{3,2},{4,5},{5,4},{6,7},{7,6},{8,9},{9,8},{10,11... | collective-permute-start | bytes 1179656 | tf_op jit(solution)/shard_map/ppermute | solution.py:39
  14.8 1.3 %picked.1 = (bf16[768,256]{1,0:T(8,128)(2,1)S(1)}, bf16[256,2048]{1,0:T(8,128)(2,1)S(1)}) custom-call(s32[1,768]{1,0:T(1,128)S(1)} %bitcast.7, bf16[768,2048]{1,0:T(8,128)(2,1)S(1)} %copy-done.1), custom_call_target="tpu_custom_call" | custom-call | flops 1 | bytes 1 | tf_op jit(solution)/shard_map/picked/pallas_call | solution.py:216
  16.2 1.6 %collective-permute-start.7 = (bf16[1,64,2048]{2,1,0:T(8,128)(2,1)S(1)}, bf16[1,64,2048]{2,1,0:T(8,128)(2,1)S(1)}, u32[]{:S(2)}, u32[]{:S(2)}) collective-permute-start(bf16[1,64,2048]{2,1,0:T(8,128)(2,1)S(1)} %collective-permute-done.refs_0_), channel_id=1, source_target_pairs={{0,16},{16,0},{1,17},{17,1},{2,18},{18,2},{3,19},{19,3},{4,20},{20... | collective-permute-start | bytes 786440 | tf_op jit(solution)/shard_map/ppermute | solution.py:39
  17.8 0.7 %collective-permute-done.1.refs_1_ = bf16[1,64,2048]{2,1,0:T(8,128)(2,1)S(1)} collective-permute-done((bf16[1,64,2048]{2,1,0:T(8,128)(2,1)S(1)}, bf16[1,64,2048]{2,1,0:T(8,128)(2,1)S(1)}, u32[]{:S(2)}, u32[]{:S(2)}) %collective-permute-start.1) | collective-permute-done | bytes 262176 | tf_op jit(solution)/shard_map/ppermute | solution.py:39
  18.5 0.4 collective-permute-start.3
  18.8 1.0 %low_rows.3.refs_1_ = f32[64,768]{1,0:T(8,128)S(1)} custom-call(s32[1,768]{1,0:T(1,128)S(1)} %bitcast.8, bf16[768,2048]{1,0:T(8,128)(2,1)S(1)} %copy-done.1, bf16[1,64,2048]{2,1,0:T(8,128)(2,1)S(1)} %collective-permute-done.refs_0_, bf16[1,64,2048]{2,1,0:T(8,128)(2,1)S(1)} %collective-permute-done.1.refs_1_, bf16[2,64,2048]{2,1,0:T(8,128)(2,1)S(1)} %bitcast.6), custom_call_target="tpu_custom_call" | custom-call | flops 5000000000 | bytes 1 | tf_op jit(solution)/shard_map/low_rows/pallas_call | solution.py:125
  19.9 2.7 %collective-permute-start.6 = (bf16[2,64,256]{2,1,0:T(8,128)(2,1)S(1)}, bf16[2,64,256]{2,1,0:T(8,128)(2,1)S(1)}, u32[]{:S(2)}, u32[]{:S(2)}) collective-permute-start(bf16[2,64,256]{2,1,0:T(8,128)(2,1)S(1)} %copy-done.4), channel_id=1, source_target_pairs={{0,8},{4,12},{8,0},{12,4},{1,9},{5,13},{9,1},{13,5},{2,10},{6,14},... | collective-permute-start | bytes 196616 | tf_op jit(solution)/shard_map/ppermute | solution.py:39
  22.6 1.6 %collective-permute-start.2 = (bf16[1,64,2048]{2,1,0:T(8,128)(2,1)S(1)}, bf16[1,64,2048]{2,1,0:T(8,128)(2,1)S(1)}, u32[]{:S(2)}, u32[]{:S(2)}) collective-permute-start(bf16[1,64,2048]{2,1,0:T(8,128)(2,1)S(1)} %collective-permute-done.1.refs_1_), channel_id=1, source_target_pairs={{0,16},{16,0},{1,17},{17,1},{2,18},{18,2},{3,19},{19,3},{4,20},{20... | collective-permute-start | bytes 786440 | tf_op jit(solution)/shard_map/ppermute | solution.py:39
  24.2 0.1 add.7
  24.3 1.6 %collective-permute-start.11 = (bf16[768,256]{1,0:T(8,128)(2,1)S(1)}, bf16[768,256]{1,0:T(8,128)(2,1)S(1)}, u32[]{:S(2)}, u32[]{:S(2)}) collective-permute-start(bf16[768,256]{1,0:T(8,128)(2,1)S(1)} %add.7), channel_id=1, source_target_pairs={{0,2},{1,3},{2,0},{3,1},{4,6},{5,7},{6,4},{7,5},{8,10},{9,11},{10,... | collective-permute-start | bytes 1179656 | tf_op jit(solution)/shard_map/ppermute | solution.py:39
  25.9 1.3 %collective-permute-done.3.refs_1_ = bf16[1,64,2048]{2,1,0:T(8,128)(2,1)S(1)} collective-permute-done((bf16[1,64,2048]{2,1,0:T(8,128)(2,1)S(1)}, bf16[1,64,2048]{2,1,0:T(8,128)(2,1)S(1)}, u32[]{:S(2)}, u32[]{:S(2)}) %collective-permute-start.3) | collective-permute-done | bytes 262176 | tf_op jit(solution)/shard_map/ppermute | solution.py:39
  27.2 0.6 %collective-permute-start.12 = (bf16[1,64,2048]{2,1,0:T(8,128)(2,1)S(1)}, bf16[1,64,2048]{2,1,0:T(8,128)(2,1)S(1)}, u32[]{:S(2)}, u32[]{:S(2)}) collective-permute-start(bf16[1,64,2048]{2,1,0:T(8,128)(2,1)S(1)} %collective-permute-done.3.refs_1_), channel_id=1, source_target_pairs={{0,16},{16,0},{1,17},{17,1},{2,18},{18,2},{3,19},{19,3},{4,20},{20... | collective-permute-start | bytes 786440 | tf_op jit(solution)/shard_map/ppermute | solution.py:39
  27.8 1.1 %low_rows.4.refs_2_ = f32[64,768]{1,0:T(8,128)S(1)} custom-call(s32[1,768]{1,0:T(1,128)S(1)} %bitcast.9, bf16[768,2048]{1,0:T(8,128)(2,1)S(1)} %copy-done.1, bf16[1,64,2048]{2,1,0:T(8,128)(2,1)S(1)} %collective-permute-done.7.refs_0_, f32[64,768]{1,0:T(8,128)S(1)} %low_rows.3.refs_1_), custom_call_target="tpu_custom_call" | custom-call | flops 5000000000 | bytes 1 | tf_op jit(solution)/shard_map/low_rows/pallas_call | solution.py:125
  28.8 3.0 %collective-permute-done.2.refs_0_ = bf16[1,64,2048]{2,1,0:T(8,128)(2,1)S(1)} collective-permute-done((bf16[1,64,2048]{2,1,0:T(8,128)(2,1)S(1)}, bf16[1,64,2048]{2,1,0:T(8,128)(2,1)S(1)}, u32[]{:S(2)}, u32[]{:S(2)}) %collective-permute-start.2) | collective-permute-done | bytes 262176 | tf_op jit(solution)/shard_map/ppermute | solution.py:39
  31.9 1.2 %low_rows.5.refs_0_ = bf16[64,768]{1,0:T(8,128)(2,1)S(1)} custom-call(s32[1,768]{1,0:T(1,128)S(1)} %bitcast.10, bf16[768,2048]{1,0:T(8,128)(2,1)S(1)} %copy-done.1, bf16[1,64,2048]{2,1,0:T(8,128)(2,1)S(1)} %collective-permute-done.2.refs_0_, bf16[1,64,2048]{2,1,0:T(8,128)(2,1)S(1)} %collective-permute-done.3.refs_1_, f32[64,768]{1,0:T(8,128)S(1)} %low_rows.4.refs_2_), custom_call_target="tpu_custom_call" | custom-call | flops 5000000000 | bytes 1 | tf_op jit(solution)/shard_map/low_rows/pallas_call | solution.py:125
  33.3 1.2 %collective-permute-done.8.refs_1_ = bf16[64,768]{1,0:T(8,128)(2,1)S(1)} collective-permute-done((bf16[64,768]{1,0:T(8,128)(2,1)S(1)}, bf16[64,768]{1,0:T(8,128)(2,1)S(1)}, u32[]{:S(2)}, u32[]{:S(2)}) %collective-permute-start.8) | collective-permute-done | bytes 98336 | tf_op jit(solution)/shard_map/ppermute | solution.py:39
  34.5 1.6 %collective-permute-start.9 = (bf16[64,768]{1,0:T(8,128)(2,1)S(1)}, bf16[64,768]{1,0:T(8,128)(2,1)S(1)}, u32[]{:S(2)}, u32[]{:S(2)}) collective-permute-start(bf16[64,768]{1,0:T(8,128)(2,1)S(1)} %add.6.mine_ref), channel_id=1, source_target_pairs={{0,2},{1,3},{2,0},{3,1},{4,6},{5,7},{6,4},{7,5},{8,10},{9,11},{10,... | collective-permute-start | bytes 294920 | tf_op jit(solution)/shard_map/ppermute | solution.py:39
  36.1 0.4 %compact.1.refs_0_ = bf16[64,256]{1,0:T(8,128)(2,1)S(1)} custom-call(bf16[256,2048]{1,0:T(8,128)(2,1)S(1)} %get-tuple-element.48.chosen_ref, bf16[1,64,2048]{2,1,0:T(8,128)(2,1)S(1)} %collective-permute-done.12.piece_ref), custom_call_target="tpu_custom_call" | custom-call | flops 2000000000 | bytes 1 | tf_op jit(solution)/shard_map/compact/pallas_call | solution.py:239
  36.5 0.1 collective-permute-start.15
  36.6 1.5 %collective-permute-start.14 = (bf16[64,256]{1,0:T(8,128)(2,1)S(1)}, bf16[64,256]{1,0:T(8,128)(2,1)S(1)}, u32[]{:S(2)}, u32[]{:S(2)}) collective-permute-start(bf16[64,256]{1,0:T(8,128)(2,1)S(1)} %compact.1.refs_0_), channel_id=1, source_target_pairs={{0,2},{1,3},{2,0},{3,1},{4,6},{5,7},{6,4},{7,5},{8,10},{9,11},{10,... | collective-permute-start | bytes 98312 | tf_op jit(solution)/shard_map/ppermute | solution.py:39
  38.1 1.1 %collective-permute-done.10.second_ref = bf16[4,64,256]{2,1,0:T(8,128)(2,1)S(1)} collective-permute-done((bf16[4,64,256]{2,1,0:T(8,128)(2,1)S(1)}, bf16[4,64,256]{2,1,0:T(8,128)(2,1)S(1)}, u32[]{:S(2)}, u32[]{:S(2)}) %collective-permute-start.10) | collective-permute-done | bytes 131104 | tf_op jit(solution)/shard_map/ppermute | solution.py:39
  39.2 0.7 %rotated_ups.1 = (bf16[512,256]{1,0:T(8,128)(2,1)S(1)}, bf16[768,512]{1,0:T(8,128)(2,1)S(1)}) custom-call(s32[1,768]{1,0:T(1,128)S(1)} %bitcast.11, s32[1,128]{1,0:T(1,128)S(1)} %bitcast.12, bf16[128,128]{1,0:T(8,128)(2,1)S(1)} %copy-done.2, bf16[4,64,256]{2,1,0:T(8,128)(2,1)S(1)} %joined.1.first_ref, bf16[4,64,256]{2,1,0:T(8,128)(2,1)S(1)} %collective-permute-done.10.second_ref), custom_call_target="tpu_custom_call" | custom-call | flops 1 | bytes 1 | tf_op jit(solution)/shard_map/rotated_ups/pallas_call | solution.py:182
  39.9 0.8 %most.1 = (bf16[64,256]{1,0:T(8,128)(2,1)S(1)}, f32[768,256]{1,0:T(8,128)S(1)}) custom-call(bf16[64,768]{1,0:T(8,128)(2,1)S(1)} %add.6.mine_ref, bf16[64,768]{1,0:T(8,128)(2,1)S(1)} %collective-permute-done.9.theirs_ref, bf16[512,256]{1,0:T(8,128)(2,1)S(1)} %get-tuple-element.40.up_ref, bf16[768,512]{1,0:T(8,128)(2,1)S(1)} %get-tuple-element.41.mask_ref, ...), custom_call_target="tpu_custom_call" | custom-call | flops 1 | bytes 1 | tf_op jit(solution)/shard_map/most/pallas_call | solution.py:267
  40.7 0.1 collective-permute-done.14.refs_2_
  40.7 1.2 %final.1 = bf16[768,256]{1,0:T(8,128)(2,1)} custom-call(bf16[768,256]{1,0:T(8,128)(2,1)S(1)} %get-tuple-element.30.pick_ref, bf16[64,256]{1,0:T(8,128)(2,1)S(1)} %get-tuple-element.46.last_ref, f32[768,256]{1,0:T(8,128)S(1)} %get-tuple-element.47.most_ref, bf16[64,256]{1,0:T(8,128)(2,1)S(1)} %compact.1.refs_0_, ...), custom_call_target="tpu_custom_call" | custom-call | flops 1 | bytes 1 | tf_op jit(solution)/shard_map/final/pallas_call | solution.py:305
  (32 shorter events, 0.3 us)
Async XLA Ops:
  1.0 15.2 %collective-permute-start = (bf16[1,64,2048]{2,1,0:T(8,128)(2,1)S(1)}, bf16[1,64,2048]{2,1,0:T(8,128)(2,1)S(1)}, u32[]{:S(2)}, u32[]{:S(2)}) collective-permute-start(bf16[1,64,2048]{2,1,0:T(8,128)(2,1)S(1)} %dynamic-slice_bitcast_fusion.in_ref), channel_id=1, source_target_pairs={{0,4},{4,0},{8,12},{12,8},{1,5},{5,1},{9,13},{13,9},{2,6},{6,2},{1... | collective-permute-start | bytes 786440 | tf_op jit(solution)/shard_map/ppermute | solution.py:39
  4.1 14.4 %collective-permute-start.1 = (bf16[1,64,2048]{2,1,0:T(8,128)(2,1)S(1)}, bf16[1,64,2048]{2,1,0:T(8,128)(2,1)S(1)}, u32[]{:S(2)}, u32[]{:S(2)}) collective-permute-start(bf16[1,64,2048]{2,1,0:T(8,128)(2,1)S(1)} %copied.1), channel_id=1, source_target_pairs={{0,8},{4,12},{8,0},{12,4},{1,9},{5,13},{9,1},{13,5},{2,10},{6,14},... | collective-permute-start | bytes 786440 | tf_op jit(solution)/shard_map/ppermute | solution.py:39
  6.7 1.9 %copy-start = (bf16[768,2048]{1,0:T(8,128)(2,1)S(1)}, bf16[768,2048]{1,0:T(8,128)(2,1)}, u32[]{:S(2)}) copy-start(bf16[768,2048]{1,0:T(8,128)(2,1)} %tokens_ref.9) | copy-start | bytes 9437188
  8.6 2.2 %copy-start.8 = (bf16[2048,1024]{1,0:T(8,128)(2,1)S(1)}, bf16[2048,1024]{1,0:T(8,128)(2,1)}, u32[]{:S(2)}) copy-start(bf16[2048,1024]{1,0:T(8,128)(2,1)} %weight_ref.1) | copy-start | bytes 12582916
  10.8 4.0 %copy-start.1 = (bf16[768,2048]{1,0:T(8,128)(2,1)S(1)}, bf16[768,2048]{1,0:T(8,128)(2,1)}, u32[]{:S(2)}) copy-start(bf16[768,2048]{1,0:T(8,128)(2,1)} %tokens_ref.9) | copy-start | bytes 9437188
  10.8 4.0 %copy-start.5 = (s32[768,1]{0,1:T(1,128)S(1)}, s32[768,1]{0,1:T(1,128)}, u32[]{:S(2)}) copy-start(s32[768,1]{0,1:T(1,128)} %param.9) | copy-start | bytes 9220
  10.8 8.0 %copy-start.3 = (bf16[2,2048,64]{1,2,0:T(8,128)(2,1)S(1)}, bf16[2,2048,64]{1,2,0:T(8,128)(2,1)}, u32[]{:S(2)}) copy-start(bf16[2,2048,64]{1,2,0:T(8,128)(2,1)} %param.12) | copy-start | bytes 1572868
  14.3 5.6 %collective-permute-start.4 = (bf16[768,256]{1,0:T(8,128)(2,1)S(1)}, bf16[768,256]{1,0:T(8,128)(2,1)S(1)}, u32[]{:S(2)}, u32[]{:S(2)}) collective-permute-start(bf16[768,256]{1,0:T(8,128)(2,1)S(1)} %get-tuple-element.34), channel_id=1, source_target_pairs={{0,1},{1,0},{2,3},{3,2},{4,5},{5,4},{6,7},{7,6},{8,9},{9,8},{10,11... | collective-permute-start | bytes 1179656 | tf_op jit(solution)/shard_map/ppermute | solution.py:39
  14.3 5.5 %collective-permute-start.5 = (bf16[768,256]{1,0:T(8,128)(2,1)S(1)}, bf16[768,256]{1,0:T(8,128)(2,1)S(1)}, u32[]{:S(2)}, u32[]{:S(2)}) collective-permute-start(bf16[768,256]{1,0:T(8,128)(2,1)S(1)} %get-tuple-element.35), channel_id=1, source_target_pairs={{0,1},{1,0},{2,3},{3,2},{4,5},{5,4},{6,7},{7,6},{8,9},{9,8},{10,11... | collective-permute-start | bytes 1179656 | tf_op jit(solution)/shard_map/ppermute | solution.py:39
  16.2 11.6 %collective-permute-start.7 = (bf16[1,64,2048]{2,1,0:T(8,128)(2,1)S(1)}, bf16[1,64,2048]{2,1,0:T(8,128)(2,1)S(1)}, u32[]{:S(2)}, u32[]{:S(2)}) collective-permute-start(bf16[1,64,2048]{2,1,0:T(8,128)(2,1)S(1)} %collective-permute-done.refs_0_), channel_id=1, source_target_pairs={{0,16},{16,0},{1,17},{17,1},{2,18},{18,2},{3,19},{19,3},{4,20},{20... | collective-permute-start | bytes 786440 | tf_op jit(solution)/shard_map/ppermute | solution.py:39
  18.5 8.7 %collective-permute-start.3 = (bf16[1,64,2048]{2,1,0:T(8,128)(2,1)S(1)}, bf16[1,64,2048]{2,1,0:T(8,128)(2,1)S(1)}, u32[]{:S(2)}, u32[]{:S(2)}) collective-permute-start(bf16[1,64,2048]{2,1,0:T(8,128)(2,1)S(1)} %collective-permute-done.1.refs_1_), channel_id=1, source_target_pairs={{0,4},{4,0},{8,12},{12,8},{1,5},{5,1},{9,13},{13,9},{2,6},{6,2},{1... | collective-permute-start | bytes 786440 | tf_op jit(solution)/shard_map/ppermute | solution.py:39
  18.8 1.0 %copy-start.4 = (bf16[2,64,256]{2,1,0:T(8,128)(2,1)S(1)}, bf16[2,64,256]{2,1,0:T(8,128)(2,1)}, u32[]{:S(2)}) copy-start(bf16[2,64,256]{2,1,0:T(8,128)(2,1)} %first_ref) | copy-start | bytes 196612
  19.9 6.0 %collective-permute-start.6 = (bf16[2,64,256]{2,1,0:T(8,128)(2,1)S(1)}, bf16[2,64,256]{2,1,0:T(8,128)(2,1)S(1)}, u32[]{:S(2)}, u32[]{:S(2)}) collective-permute-start(bf16[2,64,256]{2,1,0:T(8,128)(2,1)S(1)} %copy-done.4), channel_id=1, source_target_pairs={{0,8},{4,12},{8,0},{12,4},{1,9},{5,13},{9,1},{13,5},{2,10},{6,14},... | collective-permute-start | bytes 196616 | tf_op jit(solution)/shard_map/ppermute | solution.py:39
  22.6 9.2 %collective-permute-start.2 = (bf16[1,64,2048]{2,1,0:T(8,128)(2,1)S(1)}, bf16[1,64,2048]{2,1,0:T(8,128)(2,1)S(1)}, u32[]{:S(2)}, u32[]{:S(2)}) collective-permute-start(bf16[1,64,2048]{2,1,0:T(8,128)(2,1)S(1)} %collective-permute-done.1.refs_1_), channel_id=1, source_target_pairs={{0,16},{16,0},{1,17},{17,1},{2,18},{18,2},{3,19},{19,3},{4,20},{20... | collective-permute-start | bytes 786440 | tf_op jit(solution)/shard_map/ppermute | solution.py:39
  24.3 15.5 %collective-permute-start.11 = (bf16[768,256]{1,0:T(8,128)(2,1)S(1)}, bf16[768,256]{1,0:T(8,128)(2,1)S(1)}, u32[]{:S(2)}, u32[]{:S(2)}) collective-permute-start(bf16[768,256]{1,0:T(8,128)(2,1)S(1)} %add.7), channel_id=1, source_target_pairs={{0,2},{1,3},{2,0},{3,1},{4,6},{5,7},{6,4},{7,5},{8,10},{9,11},{10,... | collective-permute-start | bytes 1179656 | tf_op jit(solution)/shard_map/ppermute | solution.py:39
  27.2 8.9 %collective-permute-start.12 = (bf16[1,64,2048]{2,1,0:T(8,128)(2,1)S(1)}, bf16[1,64,2048]{2,1,0:T(8,128)(2,1)S(1)}, u32[]{:S(2)}, u32[]{:S(2)}) collective-permute-start(bf16[1,64,2048]{2,1,0:T(8,128)(2,1)S(1)} %collective-permute-done.3.refs_1_), channel_id=1, source_target_pairs={{0,16},{16,0},{1,17},{17,1},{2,18},{18,2},{3,19},{19,3},{4,20},{20... | collective-permute-start | bytes 786440 | tf_op jit(solution)/shard_map/ppermute | solution.py:39
  33.1 6.1 %copy-start.2 = (bf16[128,128]{1,0:T(8,128)(2,1)S(1)}, bf16[128,128]{1,0:T(8,128)(2,1)}, u32[]{:S(2)}) copy-start(bf16[128,128]{1,0:T(8,128)(2,1)} %constant.12.clone.matrix_ref) | copy-start | bytes 98308
  33.1 6.1 %copy-start.6 = (s32[128]{0:T(128)S(1)}, s32[128]{0:T(128)}, u32[]{:S(2)}) copy-start(s32[128]{0:T(128)} %param.14) | copy-start | bytes 1540
  33.1 6.8 %copy-start.7 = (f32[256]{0:T(256)S(1)}, f32[256]{0:T(256)}, u32[]{:S(2)}) copy-start(f32[256]{0:T(256)} %param.11) | copy-start | bytes 3076
  33.1 1.4 %collective-permute-start.8 = (bf16[64,768]{1,0:T(8,128)(2,1)S(1)}, bf16[64,768]{1,0:T(8,128)(2,1)S(1)}, u32[]{:S(2)}, u32[]{:S(2)}) collective-permute-start(bf16[64,768]{1,0:T(8,128)(2,1)S(1)} %low_rows.5.refs_0_), channel_id=1, source_target_pairs={{0,1},{1,0},{2,3},{3,2},{4,5},{5,4},{6,7},{7,6},{8,9},{9,8},{10,11... | collective-permute-start | bytes 294920 | tf_op jit(solution)/shard_map/ppermute | solution.py:39
  33.2 6.0 %collective-permute-start.10 = (bf16[4,64,256]{2,1,0:T(8,128)(2,1)S(1)}, bf16[4,64,256]{2,1,0:T(8,128)(2,1)S(1)}, u32[]{:S(2)}, u32[]{:S(2)}) collective-permute-start(bf16[4,64,256]{2,1,0:T(8,128)(2,1)S(1)} %joined.1.first_ref), channel_id=1, source_target_pairs={{0,4},{4,0},{8,12},{12,8},{1,5},{5,1},{9,13},{13,9},{2,6},{6,2},{1... | collective-permute-start | bytes 393224 | tf_op jit(solution)/shard_map/ppermute | solution.py:39
  34.5 5.3 %collective-permute-start.9 = (bf16[64,768]{1,0:T(8,128)(2,1)S(1)}, bf16[64,768]{1,0:T(8,128)(2,1)S(1)}, u32[]{:S(2)}, u32[]{:S(2)}) collective-permute-start(bf16[64,768]{1,0:T(8,128)(2,1)S(1)} %add.6.mine_ref), channel_id=1, source_target_pairs={{0,2},{1,3},{2,0},{3,1},{4,6},{5,7},{6,4},{7,5},{8,10},{9,11},{10,... | collective-permute-start | bytes 294920 | tf_op jit(solution)/shard_map/ppermute | solution.py:39
  36.5 4.1 %collective-permute-start.15 = (bf16[64,256]{1,0:T(8,128)(2,1)S(1)}, bf16[64,256]{1,0:T(8,128)(2,1)S(1)}, u32[]{:S(2)}, u32[]{:S(2)}) collective-permute-start(bf16[64,256]{1,0:T(8,128)(2,1)S(1)} %compact.1.refs_0_), channel_id=1, source_target_pairs={{0,3},{1,2},{2,1},{3,0},{4,7},{5,6},{6,5},{7,4},{8,11},{9,10},{10,... | collective-permute-start | bytes 98312 | tf_op jit(solution)/shard_map/ppermute | solution.py:39
  36.6 4.2 %collective-permute-start.14 = (bf16[64,256]{1,0:T(8,128)(2,1)S(1)}, bf16[64,256]{1,0:T(8,128)(2,1)S(1)}, u32[]{:S(2)}, u32[]{:S(2)}) collective-permute-start(bf16[64,256]{1,0:T(8,128)(2,1)S(1)} %compact.1.refs_0_), channel_id=1, source_target_pairs={{0,2},{1,3},{2,0},{3,1},{4,6},{5,7},{6,4},{7,5},{8,10},{9,11},{10,... | collective-permute-start | bytes 98312 | tf_op jit(solution)/shard_map/ppermute | solution.py:39
  39.2 1.6 %collective-permute-start.13 = (bf16[64,256]{1,0:T(8,128)(2,1)S(1)}, bf16[64,256]{1,0:T(8,128)(2,1)S(1)}, u32[]{:S(2)}, u32[]{:S(2)}) collective-permute-start(bf16[64,256]{1,0:T(8,128)(2,1)S(1)} %compact.1.refs_0_), channel_id=1, source_target_pairs={{0,1},{1,0},{2,3},{3,2},{4,5},{5,4},{6,7},{7,6},{8,9},{9,8},{10,11... | collective-permute-start | bytes 98312 | tf_op jit(solution)/shard_map/ppermute | solution.py:39

commit v25 on v20

--- a/solution.py
+++ b/solution.py
@@ -336,7 +336,7 @@
         return low_rows(ids, tokens, here, share, [((0, features), every)], arrays, low, dtype, cost)
 
     low = more(None, held[: len(mine)] + swapped[:1], F32, lasting(2))
-    low, *came = together(low, *(swap(block, "tp", 1) for block in blocks[:half]))
+    blocks[half], *came = together(blocks[half], *(swap(block, "tp", 1) for block in blocks[:half]))
 
     def both(low):
         bit = 1

time: 41.7 us -> 41.8 us (level)
  transfers between devices with their start and end apart: 15 -> 15, of which waited for: 7 -> 9; matrix products, arithmetic and copies ran while one was open for 2% -> 2% of each run, Pallas kernels for 23% -> 23%
where the time goes in v25:
time: 41.8 us; the launch traced here: 41.5 us
  starting transfers between devices  16.7 us (40%)
  Pallas kernels  10.6 us (25%)
  waiting for transfers between devices  8.23 us (20%)
  local copies, waits for them, and re-layouts  5.84 us (14%)
    ppermute x15, starting transfers between devices, swap(): lax.ppermute(x, axis, [(i, i ^ bit) for i in range(lax.axis_size(axis))])  16.7 us
    ppermute x15, waiting for transfers between devices, swap(): lax.ppermute(x, axis, [(i, i ^ bit) for i in range(lax.axis_size(axis))])  8.23 us
    unnamed x20, local copies, waits for them, and re-layouts  4.12 us
    pallas_call x2, Pallas kernels, partials(): pl.pallas_call(functools.partial(partial_kernel, offsets, parts), in_spec...  3.66 us
    pallas_call x2, Pallas kernels, low_rows(): pl.pallas_call(functools.partial(low_kernel, groups, here, share, rank, b...  2.45 us
    pallas_call x1, Pallas kernels, picked(): pl.pallas_call(functools.partial(pick_kernel, named, here, share), in_spe...  1.33 us
    pallas_call x1, Pallas kernels, final(): pl.pallas_call(final_kernel, in_specs=[VMEM] * (3 + len(kept)), out_specs...  1.22 us
    dynamic_slice x1, local copies, waits for them, and re-layouts, local(): own = lax.dynamic_slice_in_dim(down, start, share, 0)  0.97 us
  transfers between devices with their start and end apart: 15, of which 9 were waited for; matrix products, arithmetic and copies ran while one was open for 2% of the time, Pallas kernels for 23%

profile of v25, /device:TPU:0, one launch (start us, length us, event | category | flops | bytes accessed | tf_op | source)
XLA Modules:
  0.0 41.5 jit_solution(12813524311402736982)
XLA Ops:
  0.0 1.0 %dynamic-slice_bitcast_fusion = bf16[1,64,2048]{2,1,0:T(8,128)(2,1)S(1)} fusion(bf16[2,2048,64]{1,2,0:T(8,128)(2,1)} %param.12, s32[]{:T(128)S(6)} %select_n.4), kind=kLoop, calls=%fused_computation.1 | loop fusion | bytes 524292 | tf_op jit(solution)/shard_map/dynamic_slice | solution.py:302
  1.0 3.1 %collective-permute-start = (bf16[1,64,2048]{2,1,0:T(8,128)(2,1)S(1)}, bf16[1,64,2048]{2,1,0:T(8,128)(2,1)S(1)}, u32[]{:S(2)}, u32[]{:S(2)}) collective-permute-start(bf16[1,64,2048]{2,1,0:T(8,128)(2,1)S(1)} %dynamic-slice_bitcast_fusion), channel_id=1, source_target_pairs={{0,4},{4,0},{8,12},{12,8},{1,5},{5,1},{9,13},{13,9},{2,6},{6,2},{1... | collective-permute-start | bytes 786440 | tf_op jit(solution)/shard_map/ppermute | solution.py:39
  4.1 0.8 %constant_dynamic-slice_fusion = bf16[1,64,256]{2,1,0:T(8,128)(2,1)S(1)} fusion(bf16[2,64,256]{2,1,0:T(8,128)(2,1)} %refs_0_.1, s32[]{:T(128)S(6)} %select_n.4), kind=kLoop, calls=%fused_computation.2 | loop fusion | bytes 65540 | tf_op jit(solution)/shard_map/dynamic_slice | solution.py:304
  4.8 2.7 %collective-permute-start.1 = (bf16[1,64,2304]{2,1,0:T(8,128)(2,1)S(1)}, bf16[1,64,2304]{2,1,0:T(8,128)(2,1)S(1)}, u32[]{:S(2)}, u32[]{:S(2)}) collective-permute-start(bf16[1,64,2304]{2,1,0:T(8,128)(2,1)S(1)} %pad_maximum_fusion), channel_id=1, source_target_pairs={{0,8},{4,12},{8,0},{12,4},{1,9},{5,13},{9,1},{13,5},{2,10},{6,14},... | collective-permute-start | bytes 884744 | tf_op jit(solution)/shard_map/ppermute | solution.py:39
  7.5 1.9 %copy-done = bf16[768,2048]{1,0:T(8,128)(2,1)S(1)} copy-done((bf16[768,2048]{1,0:T(8,128)(2,1)S(1)}, bf16[768,2048]{1,0:T(8,128)(2,1)}, u32[]{:S(2)}) %copy-start) | copy-done | bytes 3145752
  9.4 2.2 %copy-done.2 = bf16[2048,1024]{1,0:T(8,128)(2,1)S(1)} copy-done((bf16[2048,1024]{1,0:T(8,128)(2,1)S(1)}, bf16[2048,1024]{1,0:T(8,128)(2,1)}, u32[]{:S(2)}) %copy-start.2) | copy-done | bytes 4194328
  11.6 2.7 %partials.2 = (bf16[768,256]{1,0:T(8,128)(2,1)S(1)}, bf16[768,256]{1,0:T(8,128)(2,1)S(1)}, bf16[768,256]{1,0:T(8,128)(2,1)S(1)}) custom-call(bf16[768,2048]{1,0:T(8,128)(2,1)S(1)} %copy-done, bf16[2048,1024]{1,0:T(8,128)(2,1)S(1)} %copy-done.2), custom_call_target="tpu_custom_call" | custom-call | flops 4000000000 | bytes 1 | tf_op jit(solution)/shard_map/partials/pallas_call | solution.py:70
  14.3 0.5 %collective-permute-start.10 = (bf16[768,256]{1,0:T(8,128)(2,1)S(1)}, bf16[768,256]{1,0:T(8,128)(2,1)S(1)}, u32[]{:S(2)}, u32[]{:S(2)}) collective-permute-start(bf16[768,256]{1,0:T(8,128)(2,1)S(1)} %get-tuple-element.46), channel_id=1, source_target_pairs={{0,1},{1,0},{2,3},{3,2},{4,5},{5,4},{6,7},{7,6},{8,9},{9,8},{10,11... | collective-permute-start | bytes 1179656 | tf_op jit(solution)/shard_map/ppermute | solution.py:39
  14.8 0.2 collective-permute-done.refs_0_
  15.0 1.7 %collective-permute-start.4 = (bf16[1,64,2048]{2,1,0:T(8,128)(2,1)S(1)}, bf16[1,64,2048]{2,1,0:T(8,128)(2,1)S(1)}, u32[]{:S(2)}, u32[]{:S(2)}) collective-permute-start(bf16[1,64,2048]{2,1,0:T(8,128)(2,1)S(1)} %collective-permute-done.refs_0_), channel_id=1, source_target_pairs={{0,16},{16,0},{1,17},{17,1},{2,18},{18,2},{3,19},{19,3},{4,20},{20... | collective-permute-start | bytes 786440 | tf_op jit(solution)/shard_map/ppermute | solution.py:39
  16.7 1.3 %picked.1 = (bf16[768,256]{1,0:T(8,128)(2,1)S(1)}, bf16[256,2048]{1,0:T(8,128)(2,1)S(1)}) custom-call(s32[1,768]{1,0:T(1,128)S(1)} %bitcast.7, bf16[768,2048]{1,0:T(8,128)(2,1)S(1)} %copy-done.1), custom_call_target="tpu_custom_call" | custom-call | flops 1 | bytes 1 | tf_op jit(solution)/shard_map/picked/pallas_call | solution.py:184
  18.1 1.0 %partials.3.refs_0_ = bf16[768,256]{1,0:T(8,128)(2,1)S(1)} custom-call(bf16[768,2048]{1,0:T(8,128)(2,1)S(1)} %copy-done.1, bf16[2048,1024]{1,0:T(8,128)(2,1)S(1)} %copy-done.3, bf16[768,256]{1,0:T(8,128)(2,1)S(1)} %get-tuple-element.31.refs_0_), custom_call_target="tpu_custom_call" | custom-call | flops 1 | bytes 1 | tf_op jit(solution)/shard_map/partials/pallas_call | solution.py:70
  19.1 1.6 %collective-permute-done.1.refs_1_ = bf16[1,64,2304]{2,1,0:T(8,128)(2,1)S(1)} collective-permute-done((bf16[1,64,2304]{2,1,0:T(8,128)(2,1)S(1)}, bf16[1,64,2304]{2,1,0:T(8,128)(2,1)S(1)}, u32[]{:S(2)}, u32[]{:S(2)}) %collective-permute-start.1) | collective-permute-done | bytes 294944 | tf_op jit(solution)/shard_map/ppermute | solution.py:39
  20.6 1.5 %collective-permute-start.2 = (bf16[1,64,2304]{2,1,0:T(8,128)(2,1)S(1)}, bf16[1,64,2304]{2,1,0:T(8,128)(2,1)S(1)}, u32[]{:S(2)}, u32[]{:S(2)}) collective-permute-start(bf16[1,64,2304]{2,1,0:T(8,128)(2,1)S(1)} %collective-permute-done.1.refs_1_), channel_id=1, source_target_pairs={{0,16},{16,0},{1,17},{17,1},{2,18},{18,2},{3,19},{19,3},{4,20},{20... | collective-permute-start | bytes 884744 | tf_op jit(solution)/shard_map/ppermute | solution.py:39
  22.3 1.6 %collective-permute-start.11 = (bf16[768,256]{1,0:T(8,128)(2,1)S(1)}, bf16[768,256]{1,0:T(8,128)(2,1)S(1)}, u32[]{:S(2)}, u32[]{:S(2)}) collective-permute-start(bf16[768,256]{1,0:T(8,128)(2,1)S(1)} %add.8), channel_id=1, source_target_pairs={{0,2},{1,3},{2,0},{3,1},{4,6},{5,7},{6,4},{7,5},{8,10},{9,11},{10,... | collective-permute-start | bytes 1179656 | tf_op jit(solution)/shard_map/ppermute | solution.py:39
  23.8 0.4 collective-permute-done.4.refs_2_
  24.2 1.2 %low_rows.2.refs_2_ = f32[64,768]{1,0:T(8,128)S(1)} custom-call(s32[1,768]{1,0:T(1,128)S(1)} %bitcast.8, bf16[768,2048]{1,0:T(8,128)(2,1)S(1)} %copy-done.1, bf16[1,64,2048]{2,1,0:T(8,128)(2,1)S(1)} %collective-permute-done.refs_0_, bf16[1,64,2304]{2,1,0:T(8,128)(2,1)S(1)} %collective-permute-done.1.refs_1_, ...), custom_call_target="tpu_custom_call" | custom-call | flops 2000000000 | bytes 1 | tf_op jit(solution)/shard_map/low_rows/pallas_call | solution.py:125
  25.5 2.7 %collective-permute-done.3.refs_1_.refs_2_ = bf16[1,64,2304]{2,1,0:T(8,128)(2,1)S(1)} collective-permute-done((bf16[1,64,2304]{2,1,0:T(8,128)(2,1)S(1)}, bf16[1,64,2304]{2,1,0:T(8,128)(2,1)S(1)}, u32[]{:S(2)}, u32[]{:S(2)}) %collective-permute-start.3) | collective-permute-done | bytes 294944 | tf_op jit(solution)/shard_map/ppermute | solution.py:39
  28.2 1.5 %collective-permute-start.7 = (bf16[1,64,2304]{2,1,0:T(8,128)(2,1)S(1)}, bf16[1,64,2304]{2,1,0:T(8,128)(2,1)S(1)}, u32[]{:S(2)}, u32[]{:S(2)}) collective-permute-start(bf16[1,64,2304]{2,1,0:T(8,128)(2,1)S(1)} %collective-permute-done.3.refs_1_.refs_2_), channel_id=1, source_target_pairs={{0,16},{16,0},{1,17},{17,1},{2,18},{18,2},{3,19},{19,3},{4,20},{20... | collective-permute-start | bytes 884744 | tf_op jit(solution)/shard_map/ppermute | solution.py:39
  29.8 0.4 %collective-permute-done.2.refs_0_.refs_3_ = bf16[1,64,2304]{2,1,0:T(8,128)(2,1)S(1)} collective-permute-done((bf16[1,64,2304]{2,1,0:T(8,128)(2,1)S(1)}, bf16[1,64,2304]{2,1,0:T(8,128)(2,1)S(1)}, u32[]{:S(2)}, u32[]{:S(2)}) %collective-permute-start.2) | collective-permute-done | bytes 294944 | tf_op jit(solution)/shard_map/ppermute | solution.py:39
  30.2 1.2 %low_rows.3.refs_0_ = bf16[64,768]{1,0:T(8,128)(2,1)S(1)} custom-call(s32[1,768]{1,0:T(1,128)S(1)} %bitcast.9, bf16[768,2048]{1,0:T(8,128)(2,1)S(1)} %copy-done.1, bf16[1,64,2304]{2,1,0:T(8,128)(2,1)S(1)} %collective-permute-done.2.refs_0_.refs_3_, bf16[1,64,2304]{2,1,0:T(8,128)(2,1)S(1)} %collective-permute-done.3.refs_1_.refs_2_, ...), custom_call_target="tpu_custom_call" | custom-call | flops 5000000000 | bytes 1 | tf_op jit(solution)/shard_map/low_rows/pallas_call | solution.py:125
  31.5 0.6 %collective-permute-start.8 = (bf16[2,64,256]{2,1,0:T(8,128)(2,1)S(1)}, bf16[2,64,256]{2,1,0:T(8,128)(2,1)S(1)}, u32[]{:S(2)}, u32[]{:S(2)}) collective-permute-start(bf16[2,64,256]{2,1,0:T(8,128)(2,1)S(1)} %copy-done.4), channel_id=1, source_target_pairs={{0,4},{4,0},{8,12},{12,8},{1,5},{5,1},{9,13},{13,9},{2,6},{6,2},{1... | collective-permute-start | bytes 196616 | tf_op jit(solution)/shard_map/ppermute | solution.py:39
  32.1 0.5 %rotated_ups.1 = (bf16[320,256]{1,0:T(8,128)(2,1)S(1)}, bf16[768,512]{1,0:T(8,128)(2,1)S(1)}) custom-call(s32[1,768]{1,0:T(1,128)S(1)} %bitcast.10, s32[1,128]{1,0:T(1,128)S(1)} %bitcast.11, bf16[128,128]{1,0:T(8,128)(2,1)S(1)} %copy-done.5, bf16[2,64,256]{2,1,0:T(8,128)(2,1)S(1)} %copy-done.4, bf16[1,64,2304]{2,1,0:T(8,128)(2,1)S(1)} %collective-permute-done.1.refs_1_, ...), custom_call_target="tpu_custom_call" | custom-call | flops 1 | bytes 1 | tf_op jit(solution)/shard_map/rotated_ups/pallas_call | solution.py:153
  32.8 1.5 %collective-permute-start.6 = (bf16[64,768]{1,0:T(8,128)(2,1)S(1)}, bf16[64,768]{1,0:T(8,128)(2,1)S(1)}, u32[]{:S(2)}, u32[]{:S(2)}) collective-permute-start(bf16[64,768]{1,0:T(8,128)(2,1)S(1)} %add.7.mine_ref), channel_id=1, source_target_pairs={{0,2},{1,3},{2,0},{3,1},{4,6},{5,7},{6,4},{7,5},{8,10},{9,11},{10,... | collective-permute-start | bytes 294920 | tf_op jit(solution)/shard_map/ppermute | solution.py:39
  34.3 1.4 %collective-permute-done.7.piece_ref = bf16[1,64,2304]{2,1,0:T(8,128)(2,1)S(1)} collective-permute-done((bf16[1,64,2304]{2,1,0:T(8,128)(2,1)S(1)}, bf16[1,64,2304]{2,1,0:T(8,128)(2,1)S(1)}, u32[]{:S(2)}, u32[]{:S(2)}) %collective-permute-start.7) | collective-permute-done | bytes 294944 | tf_op jit(solution)/shard_map/ppermute | solution.py:39
  35.8 0.4 %compact.1.refs_0_ = bf16[64,256]{1,0:T(8,128)(2,1)S(1)} custom-call(bf16[256,2048]{1,0:T(8,128)(2,1)S(1)} %get-tuple-element.52.chosen_ref, bf16[1,64,2304]{2,1,0:T(8,128)(2,1)S(1)} %collective-permute-done.7.piece_ref), custom_call_target="tpu_custom_call" | custom-call | flops 2000000000 | bytes 1 | tf_op jit(solution)/shard_map/compact/pallas_call | solution.py:207
  36.3 1.5 %collective-permute-start.13 = (bf16[64,256]{1,0:T(8,128)(2,1)S(1)}, bf16[64,256]{1,0:T(8,128)(2,1)S(1)}, u32[]{:S(2)}, u32[]{:S(2)}) collective-permute-start(bf16[64,256]{1,0:T(8,128)(2,1)S(1)} %compact.1.refs_0_), channel_id=1, source_target_pairs={{0,2},{1,3},{2,0},{3,1},{4,6},{5,7},{6,4},{7,5},{8,10},{9,11},{10,... | collective-permute-start | bytes 98312 | tf_op jit(solution)/shard_map/ppermute | solution.py:39
  37.8 0.3 collective-permute-start.12
  38.1 0.8 %most.1 = (bf16[64,256]{1,0:T(8,128)(2,1)S(1)}, f32[768,256]{1,0:T(8,128)S(1)}) custom-call(bf16[64,768]{1,0:T(8,128)(2,1)S(1)} %add.7.mine_ref, bf16[64,768]{1,0:T(8,128)(2,1)S(1)} %collective-permute-done.6.theirs_ref, bf16[320,256]{1,0:T(8,128)(2,1)S(1)} %get-tuple-element.40.up_ref, bf16[768,512]{1,0:T(8,128)(2,1)S(1)} %get-tuple-element.41.mask_ref, ...), custom_call_target="tpu_custom_call" | custom-call | flops 1 | bytes 1 | tf_op jit(solution)/shard_map/most/pallas_call | solution.py:241
  39.0 1.0 %collective-permute-done.14.refs_3_ = bf16[64,256]{1,0:T(8,128)(2,1)S(1)} collective-permute-done((bf16[64,256]{1,0:T(8,128)(2,1)S(1)}, bf16[64,256]{1,0:T(8,128)(2,1)S(1)}, u32[]{:S(2)}, u32[]{:S(2)}) %collective-permute-start.14) | collective-permute-done | bytes 32800 | tf_op jit(solution)/shard_map/ppermute | solution.py:39
  39.9 0.4 collective-permute-done.13.refs_2_
  40.3 1.2 %final.1 = bf16[768,256]{1,0:T(8,128)(2,1)} custom-call(bf16[768,256]{1,0:T(8,128)(2,1)S(1)} %get-tuple-element.34.pick_ref, bf16[64,256]{1,0:T(8,128)(2,1)S(1)} %get-tuple-element.50.last_ref, f32[768,256]{1,0:T(8,128)S(1)} %get-tuple-element.51.most_ref, bf16[64,256]{1,0:T(8,128)(2,1)S(1)} %compact.1.refs_0_, ...), custom_call_target="tpu_custom_call" | custom-call | flops 1 | bytes 1 | tf_op jit(solution)/shard_map/final/pallas_call | solution.py:279
  (32 shorter events, 0.5 us)
Async XLA Ops:
  1.0 14.1 %collective-permute-start = (bf16[1,64,2048]{2,1,0:T(8,128)(2,1)S(1)}, bf16[1,64,2048]{2,1,0:T(8,128)(2,1)S(1)}, u32[]{:S(2)}, u32[]{:S(2)}) collective-permute-start(bf16[1,64,2048]{2,1,0:T(8,128)(2,1)S(1)} %dynamic-slice_bitcast_fusion), channel_id=1, source_target_pairs={{0,4},{4,0},{8,12},{12,8},{1,5},{5,1},{9,13},{13,9},{2,6},{6,2},{1... | collective-permute-start | bytes 786440 | tf_op jit(solution)/shard_map/ppermute | solution.py:39
  4.8 15.8 %collective-permute-start.1 = (bf16[1,64,2304]{2,1,0:T(8,128)(2,1)S(1)}, bf16[1,64,2304]{2,1,0:T(8,128)(2,1)S(1)}, u32[]{:S(2)}, u32[]{:S(2)}) collective-permute-start(bf16[1,64,2304]{2,1,0:T(8,128)(2,1)S(1)} %pad_maximum_fusion), channel_id=1, source_target_pairs={{0,8},{4,12},{8,0},{12,4},{1,9},{5,13},{9,1},{13,5},{2,10},{6,14},... | collective-permute-start | bytes 884744 | tf_op jit(solution)/shard_map/ppermute | solution.py:39
  7.5 1.9 %copy-start = (bf16[768,2048]{1,0:T(8,128)(2,1)S(1)}, bf16[768,2048]{1,0:T(8,128)(2,1)}, u32[]{:S(2)}) copy-start(bf16[768,2048]{1,0:T(8,128)(2,1)} %tokens_ref.9) | copy-start | bytes 9437188
  9.4 2.2 %copy-start.2 = (bf16[2048,1024]{1,0:T(8,128)(2,1)S(1)}, bf16[2048,1024]{1,0:T(8,128)(2,1)}, u32[]{:S(2)}) copy-start(bf16[2048,1024]{1,0:T(8,128)(2,1)} %weight_ref.3) | copy-start | bytes 12582916
  11.6 5.1 %copy-start.1 = (bf16[768,2048]{1,0:T(8,128)(2,1)S(1)}, bf16[768,2048]{1,0:T(8,128)(2,1)}, u32[]{:S(2)}) copy-start(bf16[768,2048]{1,0:T(8,128)(2,1)} %tokens_ref.9) | copy-start | bytes 9437188
  11.6 5.1 %copy-start.7 = (s32[768,1]{0,1:T(1,128)S(1)}, s32[768,1]{0,1:T(1,128)}, u32[]{:S(2)}) copy-start(s32[768,1]{0,1:T(1,128)} %param.9) | copy-start | bytes 9220
  11.6 6.5 %copy-start.3 = (bf16[2048,1024]{1,0:T(8,128)(2,1)S(1)}, bf16[2048,1024]{1,0:T(8,128)(2,1)}, u32[]{:S(2)}) copy-start(bf16[2048,1024]{1,0:T(8,128)(2,1)} %weight_ref.3) | copy-start | bytes 12582916
  14.2 7.9 %collective-permute-start.9 = (bf16[768,256]{1,0:T(8,128)(2,1)S(1)}, bf16[768,256]{1,0:T(8,128)(2,1)S(1)}, u32[]{:S(2)}, u32[]{:S(2)}) collective-permute-start(bf16[768,256]{1,0:T(8,128)(2,1)S(1)} %get-tuple-element.45), channel_id=1, source_target_pairs={{0,1},{1,0},{2,3},{3,2},{4,5},{5,4},{6,7},{7,6},{8,9},{9,8},{10,11... | collective-permute-start | bytes 1179656 | tf_op jit(solution)/shard_map/ppermute | solution.py:39
  14.3 7.8 %collective-permute-start.10 = (bf16[768,256]{1,0:T(8,128)(2,1)S(1)}, bf16[768,256]{1,0:T(8,128)(2,1)S(1)}, u32[]{:S(2)}, u32[]{:S(2)}) collective-permute-start(bf16[768,256]{1,0:T(8,128)(2,1)S(1)} %get-tuple-element.46), channel_id=1, source_target_pairs={{0,1},{1,0},{2,3},{3,2},{4,5},{5,4},{6,7},{7,6},{8,9},{9,8},{10,11... | collective-permute-start | bytes 1179656 | tf_op jit(solution)/shard_map/ppermute | solution.py:39
  15.0 9.2 %collective-permute-start.4 = (bf16[1,64,2048]{2,1,0:T(8,128)(2,1)S(1)}, bf16[1,64,2048]{2,1,0:T(8,128)(2,1)S(1)}, u32[]{:S(2)}, u32[]{:S(2)}) collective-permute-start(bf16[1,64,2048]{2,1,0:T(8,128)(2,1)S(1)} %collective-permute-done.refs_0_), channel_id=1, source_target_pairs={{0,16},{16,0},{1,17},{17,1},{2,18},{18,2},{3,19},{19,3},{4,20},{20... | collective-permute-start | bytes 786440 | tf_op jit(solution)/shard_map/ppermute | solution.py:39
  18.1 6.2 %copy-start.6 = (bf16[2,2048,64]{1,2,0:T(8,128)(2,1)S(1)}, bf16[2,2048,64]{1,2,0:T(8,128)(2,1)}, u32[]{:S(2)}) copy-start(bf16[2,2048,64]{1,2,0:T(8,128)(2,1)} %param.12) | copy-start | bytes 1572868
  20.6 7.6 %collective-permute-start.3 = (bf16[1,64,2304]{2,1,0:T(8,128)(2,1)S(1)}, bf16[1,64,2304]{2,1,0:T(8,128)(2,1)S(1)}, u32[]{:S(2)}, u32[]{:S(2)}) collective-permute-start(bf16[1,64,2304]{2,1,0:T(8,128)(2,1)S(1)} %collective-permute-done.1.refs_1_), channel_id=1, source_target_pairs={{0,4},{4,0},{8,12},{12,8},{1,5},{5,1},{9,13},{13,9},{2,6},{6,2},{1... | collective-permute-start | bytes 884744 | tf_op jit(solution)/shard_map/ppermute | solution.py:39
  20.6 9.6 %collective-permute-start.2 = (bf16[1,64,2304]{2,1,0:T(8,128)(2,1)S(1)}, bf16[1,64,2304]{2,1,0:T(8,128)(2,1)S(1)}, u32[]{:S(2)}, u32[]{:S(2)}) collective-permute-start(bf16[1,64,2304]{2,1,0:T(8,128)(2,1)S(1)} %collective-permute-done.1.refs_1_), channel_id=1, source_target_pairs={{0,16},{16,0},{1,17},{17,1},{2,18},{18,2},{3,19},{19,3},{4,20},{20... | collective-permute-start | bytes 884744 | tf_op jit(solution)/shard_map/ppermute | solution.py:39
  22.3 15.9 %collective-permute-start.11 = (bf16[768,256]{1,0:T(8,128)(2,1)S(1)}, bf16[768,256]{1,0:T(8,128)(2,1)S(1)}, u32[]{:S(2)}, u32[]{:S(2)}) collective-permute-start(bf16[768,256]{1,0:T(8,128)(2,1)S(1)} %add.8), channel_id=1, source_target_pairs={{0,2},{1,3},{2,0},{3,1},{4,6},{5,7},{6,4},{7,5},{8,10},{9,11},{10,... | collective-permute-start | bytes 1179656 | tf_op jit(solution)/shard_map/ppermute | solution.py:39
  25.5 6.0 %copy-start.4 = (bf16[2,64,256]{2,1,0:T(8,128)(2,1)S(1)}, bf16[2,64,256]{2,1,0:T(8,128)(2,1)}, u32[]{:S(2)}) copy-start(bf16[2,64,256]{2,1,0:T(8,128)(2,1)} %refs_0_.1) | copy-start | bytes 196612
  25.5 6.6 %copy-start.5 = (bf16[128,128]{1,0:T(8,128)(2,1)S(1)}, bf16[128,128]{1,0:T(8,128)(2,1)}, u32[]{:S(2)}) copy-start(bf16[128,128]{1,0:T(8,128)(2,1)} %constant.12.clone.matrix_ref) | copy-start | bytes 98308
  25.5 6.6 %copy-start.8 = (s32[128]{0:T(128)S(1)}, s32[128]{0:T(128)}, u32[]{:S(2)}) copy-start(s32[128]{0:T(128)} %param.14) | copy-start | bytes 1540
  28.2 7.5 %collective-permute-start.7 = (bf16[1,64,2304]{2,1,0:T(8,128)(2,1)S(1)}, bf16[1,64,2304]{2,1,0:T(8,128)(2,1)S(1)}, u32[]{:S(2)}, u32[]{:S(2)}) collective-permute-start(bf16[1,64,2304]{2,1,0:T(8,128)(2,1)S(1)} %collective-permute-done.3.refs_1_.refs_2_), channel_id=1, source_target_pairs={{0,16},{16,0},{1,17},{17,1},{2,18},{18,2},{3,19},{19,3},{4,20},{20... | collective-permute-start | bytes 884744 | tf_op jit(solution)/shard_map/ppermute | solution.py:39
  31.4 1.4 %collective-permute-start.5 = (bf16[64,768]{1,0:T(8,128)(2,1)S(1)}, bf16[64,768]{1,0:T(8,128)(2,1)S(1)}, u32[]{:S(2)}, u32[]{:S(2)}) collective-permute-start(bf16[64,768]{1,0:T(8,128)(2,1)S(1)} %low_rows.3.refs_0_), channel_id=1, source_target_pairs={{0,1},{1,0},{2,3},{3,2},{4,5},{5,4},{6,7},{7,6},{8,9},{9,8},{10,11... | collective-permute-start | bytes 294920 | tf_op jit(solution)/shard_map/ppermute | solution.py:39
  31.5 6.3 %collective-permute-start.8 = (bf16[2,64,256]{2,1,0:T(8,128)(2,1)S(1)}, bf16[2,64,256]{2,1,0:T(8,128)(2,1)S(1)}, u32[]{:S(2)}, u32[]{:S(2)}) collective-permute-start(bf16[2,64,256]{2,1,0:T(8,128)(2,1)S(1)} %copy-done.4), channel_id=1, source_target_pairs={{0,4},{4,0},{8,12},{12,8},{1,5},{5,1},{9,13},{13,9},{2,6},{6,2},{1... | collective-permute-start | bytes 196616 | tf_op jit(solution)/shard_map/ppermute | solution.py:39
  32.1 6.0 %copy-start.9 = (f32[256]{0:T(256)S(1)}, f32[256]{0:T(256)}, u32[]{:S(2)}) copy-start(f32[256]{0:T(256)} %param.11) | copy-start | bytes 3076
  32.8 5.3 %collective-permute-start.6 = (bf16[64,768]{1,0:T(8,128)(2,1)S(1)}, bf16[64,768]{1,0:T(8,128)(2,1)S(1)}, u32[]{:S(2)}, u32[]{:S(2)}) collective-permute-start(bf16[64,768]{1,0:T(8,128)(2,1)S(1)} %add.7.mine_ref), channel_id=1, source_target_pairs={{0,2},{1,3},{2,0},{3,1},{4,6},{5,7},{6,4},{7,5},{8,10},{9,11},{10,... | collective-permute-start | bytes 294920 | tf_op jit(solution)/shard_map/ppermute | solution.py:39
  36.2 3.7 %collective-permute-start.14 = (bf16[64,256]{1,0:T(8,128)(2,1)S(1)}, bf16[64,256]{1,0:T(8,128)(2,1)S(1)}, u32[]{:S(2)}, u32[]{:S(2)}) collective-permute-start(bf16[64,256]{1,0:T(8,128)(2,1)S(1)} %compact.1.refs_0_), channel_id=1, source_target_pairs={{0,3},{1,2},{2,1},{3,0},{4,7},{5,6},{6,5},{7,4},{8,11},{9,10},{10,... | collective-permute-start | bytes 98312 | tf_op jit(solution)/shard_map/ppermute | solution.py:39
  36.3 4.0 %collective-permute-start.13 = (bf16[64,256]{1,0:T(8,128)(2,1)S(1)}, bf16[64,256]{1,0:T(8,128)(2,1)S(1)}, u32[]{:S(2)}, u32[]{:S(2)}) collective-permute-start(bf16[64,256]{1,0:T(8,128)(2,1)S(1)} %compact.1.refs_0_), channel_id=1, source_target_pairs={{0,2},{1,3},{2,0},{3,1},{4,6},{5,7},{6,4},{7,5},{8,10},{9,11},{10,... | collective-permute-start | bytes 98312 | tf_op jit(solution)/shard_map/ppermute | solution.py:39
  37.8 2.5 %collective-permute-start.12 = (bf16[64,256]{1,0:T(8,128)(2,1)S(1)}, bf16[64,256]{1,0:T(8,128)(2,1)S(1)}, u32[]{:S(2)}, u32[]{:S(2)}) collective-permute-start(bf16[64,256]{1,0:T(8,128)(2,1)S(1)} %compact.1.refs_0_), channel_id=1, source_target_pairs={{0,1},{1,0},{2,3},{3,2},{4,5},{5,4},{6,7},{7,6},{8,9},{9,8},{10,11... | collective-permute-start | bytes 98312 | tf_op jit(solution)/shard_map/ppermute | solution.py:39
